TPU v7x, 32 devices: a whole 2x2x4 slice. The times are simulated.
32 devices in a mesh: dp: 4 (over y, x), ctx: 8 (over z, core).
Axes of the slice: x: 2, y: 2, z: 4, core: 2. Of those that a mesh axis runs over, the one named last changes fastest.
Arguments:
- hidden_in: bfloat16 [4, 1536, 16384], P('dp', 'ctx'), may hold values from -8 to 8
- queries: bfloat16 [4, 1536, 1024], P('dp', 'ctx'), may hold values from -14 to 14
- grad_out: bfloat16 [4, 1536, 1024], P('dp', 'ctx'), may hold values from -6 to 6
- w_key: bfloat16 [16384, 128], P('dp'), may hold values from -1 to 1
- w_value: bfloat16 [16384, 128], P('dp'), may hold values from -0.046875 to 0.046875
- stretch_order: int32 [16], replicated, may hold values from 0 to 15, each once
- doc_lengths: int32 [4, 8], P('dp'), may hold values from 1 to 768, 1536 in all within a row
Outputs:
- query_grad: bfloat16 [4, 1536, 1024], P('dp', 'ctx')
- key_weight_grad: float32 [16384, 128], P('dp')
- value_weight_grad: float32 [16384, 128], P('dp')
Inputs may be any that keep to these rules, and one draw needn't show every extreme that they name: `stretch_order`: every block number appears exactly once. `doc_lengths`: each sequence's lengths sum to 1536, and one of them is 768.
All inputs are finite; a program needn't handle non-finite values.
Results may differ from a plain program's by a relative error of at most 0.03.
Values may be sent and summed in bfloat16 or wider, within the bound.
No kernel may reach another device: no remote copies, remote signals or barrier semaphores. Data moves between devices by JAX's collectives and lax.ppermute only.
A program may use at most 128 MiB of HBM per device.

v0:
```python
import math

import jax
import jax.numpy as jnp
from jax import lax
from jax.sharding import PartitionSpec as P


def table_lookup(slots, table):
    choices_all = jnp.arange(table.shape[0], dtype=jnp.int32)
    return jnp.sum(jnp.where(slots[:, None] == choices_all[None, :], table[None, :], 0), axis=1)


def place_and_doc(stored, stretch_order, stretch_rows, doc_ends):
    place = (
        table_lookup(stored // stretch_rows, stretch_order) * stretch_rows + stored % stretch_rows
    )
    documents = jnp.sum((place[:, None] >= doc_ends[None, :]).astype(jnp.int32), axis=1)
    return (place, documents)


def attention_grads(query_rows, key_rows, value_rows, cotangent, allowed, head_count, head_dim):
    row_count = query_rows.shape[0]
    score_scale = 1.0 / math.sqrt(head_dim)
    query_heads = jnp.transpose(query_rows.reshape(row_count, head_count, head_dim), (1, 0, 2))
    cot_heads = jnp.transpose(cotangent.reshape(row_count, head_count, head_dim), (1, 0, 2))

    def one_head(running, items):
        query_one, cot_one = items
        scores = (
            jnp.dot(query_one, jnp.transpose(key_rows), preferred_element_type=jnp.float32)
            * score_scale
        )
        masked = jnp.where(allowed, scores, -jnp.inf)
        row_max = jnp.max(masked, axis=-1, keepdims=True)
        expsum = jnp.where(allowed, jnp.exp(masked - row_max), 0.0)
        probabilities = expsum / jnp.sum(expsum, axis=-1, keepdims=True)
        probs_low = probabilities.astype(jnp.bfloat16)
        attended = jnp.dot(probs_low, value_rows, preferred_element_type=jnp.float32)
        delta_rows = jnp.sum(cot_one.astype(jnp.float32) * attended, axis=-1)
        dprob = jnp.dot(cot_one, jnp.transpose(value_rows), preferred_element_type=jnp.float32)
        dscore = (probabilities * (dprob - delta_rows[:, None])).astype(jnp.bfloat16)
        query_grad = (
            jnp.dot(dscore, key_rows, preferred_element_type=jnp.float32) * score_scale
        ).astype(jnp.bfloat16)
        key_grad = (
            lax.dot_general(
                dscore, query_one, (((0,), (0,)), ((), ())), preferred_element_type=jnp.float32
            )
            * score_scale
        )
        value_grad = lax.dot_general(
            probs_low, cot_one, (((0,), (0,)), ((), ())), preferred_element_type=jnp.float32
        )
        return (running + jnp.concatenate([key_grad, value_grad], axis=1), query_grad)

    start_sum = jnp.zeros((key_rows.shape[0], 2 * head_dim), jnp.float32)
    kv_grads, query_grad = lax.scan(one_head, start_sum, (query_heads, cot_heads))
    return (
        jnp.transpose(query_grad, (1, 0, 2)).reshape(row_count, head_count * head_dim),
        kv_grads,
    )


def on_device(hidden_in, queries, grad_out, w_key, w_value, stretch_order, doc_lengths):
    inputs = hidden_in[0]
    row_count = inputs.shape[0]
    stretch_rows = row_count // 2
    head_dim = w_key.shape[1]
    head_count = queries.shape[2] // head_dim
    ctx_count = lax.axis_size("ctx")
    seq_rows = row_count * ctx_count
    stacked = jnp.concatenate([w_key, w_value], axis=1)
    columns = inputs
    projected = jnp.dot(
        columns,
        lax.all_gather(stacked, "dp", axis=0, tiled=True),
        preferred_element_type=jnp.float32,
    ).astype(jnp.bfloat16)
    gathered = lax.all_gather(projected, "ctx", axis=0, tiled=True)
    doc_ends = jnp.cumsum(doc_lengths[0])
    every_row = jnp.arange(seq_rows, dtype=jnp.int32)
    own_rows = lax.axis_index("ctx") * row_count + jnp.arange(row_count, dtype=jnp.int32)
    key_place, key_docs = place_and_doc(every_row, stretch_order, stretch_rows, doc_ends)
    query_place, query_docs = place_and_doc(own_rows, stretch_order, stretch_rows, doc_ends)
    allowed = (key_place[None, :] <= query_place[:, None]) & (
        key_docs[None, :] == query_docs[:, None]
    )
    query_grad, kv_partial = attention_grads(
        queries[0],
        gathered[:, :head_dim],
        gathered[:, head_dim:],
        grad_out[0],
        allowed,
        head_count,
        head_dim,
    )
    kv_grads = lax.psum_scatter(
        kv_partial.astype(jnp.bfloat16), "ctx", scatter_dimension=0, tiled=True
    )
    columns = inputs
    partial_rows = lax.psum_scatter(
        lax.dot_general(
            columns, kv_grads, (((0,), (0,)), ((), ())), preferred_element_type=jnp.float32
        ).astype(jnp.bfloat16),
        "dp",
        scatter_dimension=0,
        tiled=True,
    )
    weight_grads = lax.psum(partial_rows, "ctx").astype(jnp.float32)
    return (
        query_grad.reshape(1, row_count, head_count * head_dim),
        weight_grads[:, :head_dim],
        weight_grads[:, head_dim:],
    )


def solution(mesh):
    return jax.shard_map(
        on_device,
        mesh=mesh,
        in_specs=(
            P("dp", "ctx", None),
            P("dp", "ctx", None),
            P("dp", "ctx", None),
            P("dp", None),
            P("dp", None),
            P(),
            P("dp", None),
        ),
        out_specs=(P("dp", "ctx", None), P("dp", None), P("dp", None)),
        check_vma=False,
    )
```

profile of v0, /device:TPU:0, one launch (start us, length us, event | category | flops | bytes accessed | tf_op | source)
XLA Modules:
  0.0 396.2 jit_solution(4296075789398332422)
XLA Ops:
  7.2 3.1 pad_maximum_fusion
  12.8 88.0 %all-gather.2.cloned.1.call-done = bf16[16384,256]{1,0:T(8,128)(2,1)} async-done(((bf16[4096,256]{1,0:T(8,128)(2,1)}), bf16[16384,256]{1,0:T(8,128)(2,1)}) %all-gather.2.cloned.1.call-update) | async-done | bytes 8388624 | tf_op jit(solution)/shard_map/all_gather | solution.py:77
  100.8 7.0 %fusion.33 = bf16[192,256]{1,0:T(8,128)(2,1)S(1)} fusion(bf16[16384,256]{1,0:T(8,128)(2,1)} %all-gather.2.cloned.1.call-done, bf16[1,192,16384]{2,1,0:T(8,128)(2,1)} %param.9), kind=kOutput, calls=%fused_computation.40 | convolution fusion | flops 1610661888 | bytes 14778368 | tf_op jit(solution)/shard_map/dot_general | solution.py:75
  107.8 15.5 %all_gather.7 = bf16[1536,256]{1,0:T(8,128)(2,1)S(1)} all-gather(bf16[192,256]{1,0:T(8,128)(2,1)S(1)} %fusion.33), channel_id=1, replica_groups=mesh['dp'=4,'ctx'=8] {'ctx'}, dimensions={0}, use_global_device_ids=true | all-gather | bytes 884736 | tf_op jit(solution)/shard_map/all_gather | solution.py:80
  123.4 63.3 %while.13 = (s32[]{:T(128)}, f32[1536,256]{0,1:T(8,128)}, bf16[8,192,128]{2,1,0:T(8,128)(2,1)}, bf16[8,192,128]{2,1,0:T(8,128)(2,1)}, bf16[1536,128]{1,0:T(8,128...) while((s32[]{:T(128)}, f32[1536,256]{0,1:T(8,128)}, ...), condition=%wide.region_9.10_spmd.clone, body=%wide.region_5.9_spmd.clone.sunk | while | flops 461266368 | bytes 18235028 | solution.py:58
  123.4 1.3 fusion.87
  126.3 1.1 convolution_multiply_fusion.5
  127.8 1.4 maximum_add_fusion.2
  129.1 0.9 fusion.93
  130.1 1.3 fusion.87
  133.0 1.1 convolution_multiply_fusion.5
  134.4 2.8 maximum_add_fusion.2
  137.2 0.9 fusion.93
  138.1 1.3 fusion.87
  141.1 1.1 convolution_multiply_fusion.5
  142.5 2.8 maximum_add_fusion.2
  145.3 0.9 fusion.93
  146.2 1.3 fusion.87
  149.2 1.1 convolution_multiply_fusion.5
  150.6 2.8 maximum_add_fusion.2
  153.4 0.9 fusion.93
  154.3 1.3 fusion.87
  157.2 1.1 convolution_multiply_fusion.5
  158.7 2.8 maximum_add_fusion.2
  161.5 0.9 fusion.93
  162.4 1.3 fusion.87
  165.3 1.1 convolution_multiply_fusion.5
  166.8 2.8 maximum_add_fusion.2
  169.6 0.9 fusion.93
  170.5 1.3 fusion.87
  173.4 1.1 convolution_multiply_fusion.5
  174.9 2.8 maximum_add_fusion.2
  177.6 0.9 fusion.93
  178.6 1.3 fusion.87
  181.5 1.1 convolution_multiply_fusion.5
  182.9 2.8 maximum_add_fusion.2
  185.7 0.9 fusion.93
  186.7 1.5 convert_element_type.40
  188.1 1.2 copy.28
  189.4 32.0 %reduce-scatter.7.cloned.1.call-done = bf16[192,256]{1,0:T(8,128)(2,1)} async-done(((bf16[1536,256]{1,0:T(8,128)(2,1)}), bf16[192,256]{1,0:T(8,128)(2,1)}) %reduce-scatter.7.cloned.1.call-update) | async-done | bytes 98320
  221.4 8.4 %fusion.26 = bf16[16384,256]{0,1:T(8,128)(2,1)} fusion(bf16[192,256]{1,0:T(8,128)(2,1)} %reduce-scatter.7.cloned.1.call-done, bf16[1,192,16384]{2,1,0:T(8,128)(2,1)} %param.9), kind=kOutput, calls=%fused_computation.34 | convolution fusion | flops 1614807040 | bytes 14778368 | tf_op jit(solution)/shard_map/dot_general | solution.py:103
  229.9 84.6 %reduce-scatter.5.cloned.1.call-done = bf16[4096,256]{0,1:T(8,128)(2,1)} async-done(((bf16[16384,256]{0,1:T(8,128)(2,1)}), bf16[4096,256]{0,1:T(8,128)(2,1)}) %reduce-scatter.5.cloned.1.call-update) | async-done | bytes 2097168 | tf_op jit(solution)/shard_map/reduce_scatter | solution.py:102
  314.5 1.3 copy.25
  315.8 0.9 reshape_reshape.3
  316.7 65.0 %all-reduce.2.cloned.1.call-done = bf16[4096,256]{0,1:T(8,128)(2,1)} async-done(((bf16[4096,256]{0,1:T(8,128)(2,1)}), bf16[4096,256]{0,1:T(8,128)(2,1)}) %all-reduce.2.cloned.1.call-update) | async-done | bytes 2097168 | tf_op jit(solution)/shard_map/psum | solution.py:110
  381.6 3.3 fusion.48
  385.0 2.9 copy.26
  387.9 1.8 copy.27
  (72 shorter events, 18.2 us)
Async XLA Ops:
  7.2 93.6 %all-gather.2.cloned.1.call-start = ((), (), s32[]{:S(2)}) async-start(), calls=%async_computation.2 | async-start | bytes 10485760 | tf_op jit(solution)/shard_map/all_gather | solution.py:77
  10.3 0.7 copy-start.3
  10.3 1.0 copy-start
  10.3 1.9 copy-start.1
  10.3 211.1 %reduce-scatter.7.cloned.1.call-start = ((), (), s32[]{:S(2)}) async-start(), calls=%async_computation.5 | async-start | bytes 884736
  11.3 1.1 copy-start.2
  189.3 125.2 %reduce-scatter.5.cloned.1.call-start = ((), (), s32[]{:S(2)}) async-start(), calls=%async_computation.3 | async-start | bytes 10485760 | tf_op jit(solution)/shard_map/reduce_scatter | solution.py:102
  229.9 151.8 %all-reduce.2.cloned.1.call-start = ((), (), s32[]{:S(2)}) async-start(), calls=%async_computation.4 | async-start | bytes 4194304 | tf_op jit(solution)/shard_map/psum | solution.py:110
Sparse Core Ops, SparseCore 0:
  10.4 90.2 all-gather.1
  189.4 31.9 reduce-scatter.6
  230.0 84.4 reduce-scatter.4
  316.7 64.8 all-reduce.1
where the time goes:
time: 398 us; the launch traced here: 396 us
  waiting for transfers between devices  270 us (68%)
  matrix products  50.3 us (13%)
  other arithmetic  33.2 us (8%)
  blocking collectives  15.5 us (4%)
  between operations  13.9 us (3%)
  local copies, waits for them, and re-layouts  13.2 us (3%)
    all_gather x1, waiting for transfers between devices, on_device(): lax.all_gather(stacked, 'dp', axis=0, tiled=True)  88 us
    reduce_scatter x1, waiting for transfers between devices, on_device(): lax.psum_scatter(lax.dot_general(columns, kv_grads, (((0,), (0,)), ((), (...  84.6 us
    psum x1, waiting for transfers between devices, on_device(): weight_grads = lax.psum(partial_rows, 'ctx').astype(jnp.float32)  65 us
    unnamed x5, waiting for transfers between devices  32.1 us
    add x8, other arithmetic, one_head(): running + jnp.concatenate([key_grad, value_grad], axis=1)  20.9 us
    all_gather x1, blocking collectives, on_device(): gathered = lax.all_gather(projected, 'ctx', axis=0, tiled=True)  15.5 us
    dot_general x8, matrix products, one_head(): jnp.dot(query_one, jnp.transpose(key_rows), preferred_element_type=jnp.fl...  10.3 us
    dot_general x8, matrix products, one_head(): lax.dot_general(dscore, query_one, (((0,), (0,)), ((), ())), preferred_el...  8.9 us
  transfers between devices with their start and end apart: 4, of which 4 were waited for; matrix products, arithmetic and copies ran while one was open for 1% of the time, Pallas kernels for 0%

commit v1 on v0

v1 whole, which is shorter than its diff:
```python
import functools
import math

import jax
import jax.numpy as jnp
from jax import lax
from jax.experimental import pallas as pl
from jax.experimental.pallas import tpu as pltpu
from jax.sharding import PartitionSpec as P

VMEM_LIMIT = 48 * 1024 * 1024


def swap(array, axis, distance):
    count = lax.axis_size(axis)
    return lax.ppermute(array, axis, [(i, i ^ distance) for i in range(count)])


def after(arrays, *earlier):
    tied = lax.optimization_barrier((tuple(arrays), tuple(earlier)))
    return list(tied[0]), list(tied[1])


def attention_kernel(
    shape, ids, order, lengths, q_ref, g_ref, *refs
):
    ctx_count, stretch_rows, head_count, head_dim, window, chunk = shape
    kv_refs = refs[:ctx_count]
    qgrad_ref, keep_ref, send_ref, keys, values, total, qs, gs, dqs = refs[ctx_count:]
    me = ids[0]
    row_count = 2 * stretch_rows
    stretch_count = 2 * ctx_count
    score_scale = 1.0 / math.sqrt(head_dim)

    def place(device, half):
        return pl.multiple_of(order[2 * device + half] * stretch_rows, stretch_rows)

    for index in range(ctx_count):
        for half in range(2):
            rows = pl.ds(place(me ^ index, half), stretch_rows)
            block = kv_refs[index][half * stretch_rows : (half + 1) * stretch_rows, :]
            keys[rows, :] = block[:, :head_dim]
            values[rows, :] = block[:, head_dim:]
    total[...] = jnp.zeros_like(total)
    for half in range(2):
        for head in range(head_count):
            to = slice((half * head_count + head) * stretch_rows, (half * head_count + head + 1) * stretch_rows)
            rows = slice(half * stretch_rows, (half + 1) * stretch_rows)
            columns = slice(head * head_dim, (head + 1) * head_dim)
            qs[to, :] = q_ref[rows, columns]
            gs[to, :] = g_ref[rows, columns]
    ends = []
    running = 0
    for at in range(lengths.shape[0]):
        running = running + lengths[at]
        ends.append(running)
    chunks_half = head_count * stretch_rows // chunk

    def step(at, carry):
        half = at // chunks_half
        block = order[2 * me + half]
        first = jnp.maximum(block - stretch_count // 2, 0) * stretch_rows
        first = pl.multiple_of(first, stretch_rows)
        part = pl.ds(pl.multiple_of(at * chunk, chunk), chunk)
        inside = (at - half * chunks_half) * chunk + lax.broadcasted_iota(jnp.int32, (1, chunk), 1)
        at_query = block * stretch_rows + lax.rem(inside, stretch_rows)
        begin = jnp.zeros_like(at_query)
        for end in ends:
            begin = jnp.where(at_query >= end, end, begin)
        at_key = first + lax.broadcasted_iota(jnp.int32, (window, chunk), 0)
        allowed = (at_key >= begin) & (at_key <= at_query)
        k = keys[pl.ds(first, window), :]
        v = values[pl.ds(first, window), :]
        q = qs[part, :]
        g = gs[part, :]
        last = (((1,), (1,)), ((), ()))
        scores = lax.dot_general(k, q, last, preferred_element_type=jnp.float32) * score_scale
        masked = jnp.where(allowed, scores, -jnp.inf)
        expsum = jnp.exp(masked - jnp.max(masked, axis=0, keepdims=True))
        probs = expsum * (1.0 / jnp.sum(expsum, axis=0, keepdims=True))
        probs_low = probs.astype(jnp.bfloat16)
        dprob = lax.dot_general(v, g, last, preferred_element_type=jnp.float32)
        delta = jnp.sum(probs_low.astype(jnp.float32) * dprob, axis=0, keepdims=True)
        dscore = (probs * (dprob - delta)).astype(jnp.bfloat16)
        dq = lax.dot_general(
            k, dscore, (((0,), (0,)), ((), ())), preferred_element_type=jnp.float32
        )
        dqs[part, :] = (jnp.transpose(dq) * score_scale).astype(jnp.bfloat16)
        dk = jnp.dot(dscore, q, preferred_element_type=jnp.float32) * score_scale
        dv = jnp.dot(probs_low, g, preferred_element_type=jnp.float32)
        total[pl.ds(first, window), :head_dim] += dk
        total[pl.ds(first, window), head_dim:] += dv
        return carry

    lax.fori_loop(0, 2 * chunks_half, step, 0)
    for half in range(2):
        for head in range(head_count):
            origin = slice((half * head_count + head) * stretch_rows, (half * head_count + head + 1) * stretch_rows)
            rows = slice(half * stretch_rows, (half + 1) * stretch_rows)
            columns = slice(head * head_dim, (head + 1) * head_dim)
            qgrad_ref[rows, columns] = dqs[origin, :]
    for index in range(ctx_count):
        for half in range(2):
            rows = pl.ds(place(me ^ index, half), stretch_rows)
            start = (index // 2) * row_count + half * stretch_rows
            if index % 2:
                send_ref[start : start + stretch_rows, :] = total[rows, :].astype(jnp.bfloat16)
            else:
                keep_ref[start : start + stretch_rows, :] = total[rows, :]


def attention(me, order, lengths, queries, cotangent, kv_blocks, head_dim):
    row_count, width = queries.shape
    ctx_count = len(kv_blocks)
    stretch_rows = row_count // 2
    head_count = width // head_dim
    seq_rows = row_count * ctx_count
    window = seq_rows // 2 + stretch_rows
    stacked = head_count * stretch_rows
    chunk = 256 if stacked % 256 == 0 else 128
    shape = (ctx_count, stretch_rows, head_count, head_dim, window, chunk)
    smem = pl.BlockSpec(memory_space=pltpu.SMEM)
    vmem = pl.BlockSpec(memory_space=pltpu.VMEM)
    half_rows = seq_rows // 2
    return pl.pallas_call(
        functools.partial(attention_kernel, shape),
        out_shape=(
            jax.ShapeDtypeStruct((row_count, width), jnp.bfloat16),
            jax.ShapeDtypeStruct((half_rows, 2 * head_dim), jnp.float32),
            jax.ShapeDtypeStruct((half_rows, 2 * head_dim), jnp.bfloat16),
        ),
        in_specs=[smem] * 3 + [vmem] * (2 + ctx_count),
        out_specs=(vmem,) * 3,
        scratch_shapes=[
            pltpu.VMEM((seq_rows, head_dim), jnp.bfloat16),
            pltpu.VMEM((seq_rows, head_dim), jnp.bfloat16),
            pltpu.VMEM((seq_rows, 2 * head_dim), jnp.float32),
            pltpu.VMEM((2 * stacked, head_dim), jnp.bfloat16),
            pltpu.VMEM((2 * stacked, head_dim), jnp.bfloat16),
            pltpu.VMEM((2 * stacked, head_dim), jnp.bfloat16),
        ],
        compiler_params=pltpu.CompilerParams(vmem_limit_bytes=VMEM_LIMIT),
        cost_estimate=pl.CostEstimate(
            flops=10 * window * 2 * stacked * head_dim,
            bytes_accessed=8 * row_count * width + 10 * seq_rows * head_dim,
            transcendentals=window * 2 * stacked,
        ),
        name="attention",
    )(me, order, lengths, queries, cotangent, *kv_blocks)


def weight_kernel(dp_count, z_count, z, *refs):
    hidden, grads, out_ref = refs[:dp_count], refs[dp_count : 2 * dp_count], refs[-1]
    columns = hidden[0].shape[1]
    share = columns // z_count
    tile = max(share, 128)
    for start in range(0, columns, tile):
        product = None
        for one, grad in zip(hidden, grads):
            term = lax.dot_general(
                one[:, start : start + tile],
                grad[...],
                (((0,), (0,)), ((), ())),
                preferred_element_type=jnp.float32,
            )
            product = term if product is None else product + term
        for inner in range(0, tile, share):
            to = pl.multiple_of((z[0] ^ ((start + inner) // share)) * share, share)
            out_ref[pl.ds(to, share), :] = product[inner : inner + share, :].astype(out_ref.dtype)


def weight_rows(z, hidden, grads, z_count, kind):
    columns, width = hidden[0].shape[1], grads[0].shape[1]
    rows = sum(one.shape[0] for one in hidden)
    smem = pl.BlockSpec(memory_space=pltpu.SMEM)
    vmem = pl.BlockSpec(memory_space=pltpu.VMEM)
    return pl.pallas_call(
        functools.partial(weight_kernel, len(hidden), z_count),
        out_shape=jax.ShapeDtypeStruct((columns, width), kind),
        in_specs=[smem] + [vmem] * (2 * len(hidden)),
        out_specs=vmem,
        compiler_params=pltpu.CompilerParams(vmem_limit_bytes=VMEM_LIMIT),
        cost_estimate=pl.CostEstimate(
            flops=2 * rows * columns * width,
            bytes_accessed=2 * rows * (columns + width) + 4 * columns * width,
            transcendentals=0,
        ),
        name="weight_rows",
    )(z, *hidden, *grads)


def assemble_kernel(z_count, ids, *refs):
    blocks, key_ref, value_ref = refs[:-2], refs[-2], refs[-1]
    share, width = blocks[0].shape
    for side in range(2):
        for m in range(z_count):
            to = ((ids[1] ^ side) * z_count + (ids[0] ^ m)) * share
            to = pl.multiple_of(to, share)
            block = blocks[side * z_count + m][...].astype(jnp.float32)
            key_ref[pl.ds(to, share), :] = block[:, : width // 2]
            value_ref[pl.ds(to, share), :] = block[:, width // 2 :]


def assemble(ids, blocks, z_count):
    share, width = blocks[0].shape
    shape = jax.ShapeDtypeStruct((2 * z_count * share, width // 2), jnp.float32)
    smem = pl.BlockSpec(memory_space=pltpu.SMEM)
    vmem = pl.BlockSpec(memory_space=pltpu.VMEM)
    return pl.pallas_call(
        functools.partial(assemble_kernel, z_count),
        out_shape=(shape, shape),
        in_specs=[smem] + [vmem] * len(blocks),
        out_specs=(vmem, vmem),
        compiler_params=pltpu.CompilerParams(vmem_limit_bytes=VMEM_LIMIT),
        name="assemble",
    )(ids, *blocks)


def dot32(left, right):
    return jnp.dot(left, right, preferred_element_type=jnp.float32)


def on_device(hidden_in, queries, grad_out, w_key, w_value, stretch_order, doc_lengths):
    inputs = hidden_in[0]
    row_count = inputs.shape[0]
    head_dim = w_key.shape[1]
    dp_count = lax.axis_size("dp")
    ctx_count = lax.axis_size("ctx")
    z_count = ctx_count // 2
    dp, ctx = lax.axis_index("dp"), lax.axis_index("ctx")
    z, core = ctx // 2, ctx % 2
    block_rows = w_key.shape[0]
    half_rows = block_rows // 2

    bits = [1 << at for at in range(dp_count.bit_length() - 1)]

    def gather(weight, order):
        mine = {0: lax.dynamic_slice_in_dim(weight, core * half_rows, half_rows, 0)}
        for bit in order:
            mine.update({j | bit: swap(piece, "dp", bit) for j, piece in list(mine.items())})
        other = {0: lax.dynamic_slice_in_dim(weight, (1 - core) * half_rows, half_rows, 0)}
        other.update({j: swap(mine[j], "ctx", 1) for j in mine if j})
        return mine, other

    key_pieces = gather(w_key, bits)
    value_pieces = gather(w_value, bits[::-1])

    def columns(j, side):
        start = (dp ^ j) * block_rows + (core ^ side) * half_rows
        return lax.dynamic_slice_in_dim(inputs, start, half_rows, 1)

    hidden = {(j, side): columns(j, side) for j in range(dp_count) for side in range(2)}

    landed = [pieces[0][j] for pieces in (key_pieces, value_pieces) for j in range(1, dp_count)]
    names = [name for name in hidden if name[0]]
    sent, landed = after([hidden[name] for name in names], *landed)
    landed = iter(landed)
    for pieces in (key_pieces, value_pieces):
        for j in range(1, dp_count):
            pieces[0][j] = next(landed)
    swapped = {name: swap(one, "dp", name[0]) for name, one in zip(names, sent)}
    for side in range(2):
        swapped[0, side] = hidden[0, side]

    keys = sum(dot32(hidden[j, side], key_pieces[side][j]) for j in range(dp_count) for side in range(2))
    values = sum(dot32(hidden[j, side], value_pieces[side][j]) for j in range(dp_count) for side in range(2))
    own = jnp.concatenate([keys.astype(jnp.bfloat16), values.astype(jnp.bfloat16)], axis=1)

    along = [own] + [swap(own, "ctx", 2 * m) for m in range(1, z_count)]
    kv_blocks = []
    for one in along:
        kv_blocks += [one, swap(one, "ctx", 1)]

    me = jnp.reshape(ctx, (1,)).astype(jnp.int32)
    query_grad, keep, send = attention(
        me, stretch_order, doc_lengths[0], queries[0], grad_out[0], kv_blocks, head_dim
    )

    chip = keep + swap(send, "ctx", 1).astype(jnp.float32)
    chip = chip.reshape(z_count, row_count, 2 * head_dim)
    kv_grad = chip[0]
    for m in range(1, z_count):
        kv_grad = kv_grad + swap(chip[m].astype(jnp.bfloat16), "ctx", 2 * m).astype(jnp.float32)
    kv_grad = kv_grad.astype(jnp.bfloat16)
    grads = [kv_grad] + [swap(kv_grad, "dp", j) for j in range(1, dp_count)]

    z_id = jnp.reshape(z, (1,)).astype(jnp.int32)
    theirs = weight_rows(
        z_id, [swapped[j, 1] for j in range(dp_count)], grads, z_count, jnp.bfloat16
    )
    from_core = swap(theirs, "ctx", 1)
    ours = weight_rows(
        z_id, [swapped[j, 0] for j in range(dp_count)], grads, z_count, jnp.float32
    )
    share = half_rows // z_count
    partial = (ours + from_core.astype(jnp.float32)).reshape(z_count, share, 2 * head_dim)
    final = partial[0]
    for m in range(1, z_count):
        final = final + swap(partial[m].astype(jnp.bfloat16), "ctx", 2 * m).astype(jnp.float32)
    final = final.astype(jnp.bfloat16)
    rows = [final] + [swap(final, "ctx", 2 * m) for m in range(1, z_count)]
    blocks = rows + [swap(one, "ctx", 1) for one in rows]
    ids = jnp.stack([z, core]).astype(jnp.int32)
    key_rows, value_rows = assemble(ids, blocks, z_count)
    return query_grad[None], key_rows, value_rows


def solution(mesh):
    return jax.shard_map(
        on_device,
        mesh=mesh,
        in_specs=(
            P("dp", "ctx", None),
            P("dp", "ctx", None),
            P("dp", "ctx", None),
            P("dp", None),
            P("dp", None),
            P(),
            P("dp", None),
        ),
        out_specs=(P("dp", "ctx", None), P("dp", None), P("dp", None)),
        check_vma=False,
    )
```

time: 398 us -> 220 us (0.55)
  waiting for transfers between devices: 270 us -> 134 us
  starting transfers between devices: 0.16 us -> 41.6 us
  matrix products: 50.3 us -> 15.5 us
  other arithmetic: 33.2 us -> 0.72 us
  Pallas kernels: 0 us -> 17.8 us
  blocking collectives: 15.5 us -> 0 us
  between operations: 13.9 us -> 1.03 us
  local copies, waits for them, and re-layouts: 13.2 us -> 8.21 us
    ppermute x0 -> x43, waiting for transfers between devices: none -> 134 us  [swap(): return lax.ppermute(array, axis, [(i, i ^ distance) for i in range(count)])]
    all_gather x1 -> x0, waiting for transfers between devices: 88 us -> none  [on_device(): lax.all_gather(stacked, 'dp', axis=0, tiled=True)]
    reduce_scatter x1 -> x0, waiting for transfers between devices: 84.6 us -> none  [on_device(): lax.psum_scatter(lax.dot_general(columns, kv_grads, (((0,), (0,)), ((), (...]
    psum x1 -> x0, waiting for transfers between devices: 65 us -> none  [on_device(): weight_grads = lax.psum(partial_rows, 'ctx').astype(jnp.float32)]
    ppermute x0 -> x43, starting transfers between devices: none -> 41.6 us  [swap(): return lax.ppermute(array, axis, [(i, i ^ distance) for i in range(count)])]
    dot_general x50 -> x16, matrix products: 50.3 us -> 15.5 us  [dot32(): return jnp.dot(left, right, preferred_element_type=jnp.float32)]
    unnamed x5 -> x0, waiting for transfers between devices: 32.1 us -> none
    add x10 -> x0, other arithmetic: 20.9 us -> none  [the longest x8 20.9 us: one_head(): running + jnp.concatenate([key_grad, value_grad], axis=1)]
  transfers between devices with their start and end apart: 4 -> 43, of which waited for: 4 -> 25; matrix products, arithmetic and copies ran while one was open for 1% -> 10% of each run, Pallas kernels for 0% -> 1%
where the time goes in v1:
time: 220 us; the launch traced here: 218 us
  waiting for transfers between devices  134 us (61%)
  starting transfers between devices  41.6 us (19%)
  Pallas kernels  17.8 us (8%)
  matrix products  15.5 us (7%)
  local copies, waits for them, and re-layouts  8.21 us (4%)
    ppermute x43, waiting for transfers between devices, swap(): return lax.ppermute(array, axis, [(i, i ^ distance) for i in range(count)])  134 us
    ppermute x43, starting transfers between devices, swap(): return lax.ppermute(array, axis, [(i, i ^ distance) for i in range(count)])  41.6 us
    dot_general x16, matrix products, dot32(): return jnp.dot(left, right, preferred_element_type=jnp.float32)  15.5 us
    pallas_call x1, Pallas kernels, attention(): pl.pallas_call(functools.partial(attention_kernel, shape), out_shape=(jax...  9.59 us
    pallas_call x2, Pallas kernels, weight_rows(): pl.pallas_call(functools.partial(weight_kernel, len(hidden), z_count), ou...  5.37 us
    dynamic_slice x1, local copies, waits for them, and re-layouts, columns(): return lax.dynamic_slice_in_dim(inputs, start, half_rows, 1)  4.93 us
  transfers between devices with their start and end apart: 43, of which 25 were waited for; matrix products, arithmetic and copies ran while one was open for 10% of the time, Pallas kernels for 1%

profile of v1, /device:TPU:0, one launch (start us, length us, event | category | flops | bytes accessed | tf_op | source)
XLA Modules:
  0.0 218.5 jit_solution(2478302654126602505)
XLA Ops:
  1.9 3.0 %collective-permute-start = (bf16[2048,128]{1,0:T(8,128)(2,1)S(1)}, bf16[2048,128]{1,0:T(8,128)(2,1)}, u32[]{:S(2)}, u32[]{:S(2)}) collective-permute-start(bf16[2048,128]{1,0:T(8,128)(2,1)S(1)} %constant_dynamic-slice_fusion.1), channel_id=1, source_target_pairs={{0,8},{8,0},{16,24},{24,16},{1,9},{9,1},{17,25},{25,17},{2,10},{10... | collective-permute-start | bytes 1572872 | tf_op jit(solution)/shard_map/ppermute | solution.py:16
  4.9 1.5 collective-permute-start.1
  6.4 1.9 constant_dynamic-slice_fusion
  8.9 4.9 %dynamic-slice_bitcast_fusion.6 = (bf16[192,2048]{1,0:T(8,128)(2,1)S(1)}, bf16[192,2048]{1,0:T(8,128)(2,1)}, bf16[192,2048]{1,0:T(8,128)(2,1)S(1)}, bf16[192,204...) fusion(bf16[1,192,16384]{2,1,0:T(8,128)(2,1)} %param.7, ...), kind=kLoop, calls=%fused_computation.24 | loop fusion | bytes 12582944 | tf_op jit(solution)/shard_map/dynamic_slice | solution.py:250
  14.2 3.5 %collective-permute-done = bf16[2048,128]{1,0:T(8,128)(2,1)} collective-permute-done((bf16[2048,128]{1,0:T(8,128)(2,1)S(1)}, bf16[2048,128]{1,0:T(8,128)(2,1)}, u32[]{:S(2)}, u32[]{:S(2)}) %collective-permute-start) | collective-permute-done | bytes 524320 | tf_op jit(solution)/shard_map/ppermute | solution.py:16
  17.8 2.1 collective-permute-start.2
  19.8 11.2 %collective-permute-done.4 = bf16[2048,128]{1,0:T(8,128)(2,1)} collective-permute-done((bf16[2048,128]{1,0:T(8,128)(2,1)}, bf16[2048,128]{1,0:T(8,128)(2,1)}, u32[]{:S(2)}, u32[]{:S(2)}) %collective-permute-start.4) | collective-permute-done | bytes 524320 | tf_op jit(solution)/shard_map/ppermute | solution.py:16
  31.5 1.4 fusion.29
  33.9 6.8 %collective-permute-done.2 = bf16[2048,128]{1,0:T(8,128)(2,1)S(1)} collective-permute-done((bf16[2048,128]{1,0:T(8,128)(2,1)}, bf16[2048,128]{1,0:T(8,128)(2,1)S(1)}, u32[]{:S(2)}, u32[]{:S(2)}) %collective-permute-start.2) | collective-permute-done | bytes 524320 | tf_op jit(solution)/shard_map/ppermute | solution.py:16
  40.8 1.6 collective-permute-done.5
  42.3 1.4 fusion.26
  44.1 1.4 fusion.31
  46.8 1.5 fusion.27
  48.7 1.4 fusion.7
  50.1 1.5 fusion.32
  51.6 1.5 fusion.3
  53.1 1.5 fusion.8
  54.6 1.5 fusion.9
  56.1 1.7 collective-permute-start.13
  57.8 2.6 %collective-permute-start.15 = (bf16[192,256]{1,0:T(8,128)(2,1)S(1)}, bf16[192,256]{1,0:T(8,128)(2,1)S(1)}, u32[]{:S(2)}, u32[]{:S(2)}) collective-permute-start(bf16[192,256]{1,0:T(8,128)(2,1)S(1)} %pad_maximum_fusion.refs_0_), channel_id=1, source_target_pairs={{0,4},{1,5},{2,6},{3,7},{4,0},{5,1},{6,2},{7,3},{8,12},{9,13},{10,... | collective-permute-start | bytes 294920 | tf_op jit(solution)/shard_map/ppermute | solution.py:16
  61.1 7.3 %collective-permute-done.15.refs_4_ = bf16[192,256]{1,0:T(8,128)(2,1)S(1)} collective-permute-done((bf16[192,256]{1,0:T(8,128)(2,1)S(1)}, bf16[192,256]{1,0:T(8,128)(2,1)S(1)}, u32[]{:S(2)}, u32[]{:S(2)}) %collective-permute-start.15) | collective-permute-done | bytes 98336 | tf_op jit(solution)/shard_map/ppermute | solution.py:16
  69.9 9.6 %attention.1 = (bf16[192,1024]{1,0:T(8,128)(2,1)}, f32[768,256]{1,0:T(8,128)S(1)}, bf16[768,256]{1,0:T(8,128)(2,1)S(1)}) custom-call(s32[1]{0:T(128)} %bitcast.ids, s32[16]{0:T(128)S(1)} %copy-done.3, s32[8]{0:T(128)S(1)} %bitcast.55, bf16[192,1024]{1,0:T(8,128)(2,1)S(1)} %bitcast.53, bf16[192,1024]{1,0:T(8,128)(2,1)S(1)} %bitcast.54, ...), custom_call_target="tpu_custom_call" | custom-call | flops 1698693120 | bytes 3538944 | tf_op jit(solution)/shard_map/attention/pallas_call | solution.py:125
  80.4 1.5 collective-permute-start.30
  81.9 1.4 collective-permute-start.31
  83.5 1.4 collective-permute-start.23
  84.9 1.8 collective-permute-start.24
  86.7 2.5 %collective-permute-done.23 = bf16[192,256]{1,0:T(8,128)(2,1)S(1)} collective-permute-done((bf16[192,256]{1,0:T(8,128)(2,1)S(1)}, bf16[192,256]{1,0:T(8,128)(2,1)S(1)}, u32[]{:S(2)}, u32[]{:S(2)}) %collective-permute-start.23) | collective-permute-done | bytes 98336 | tf_op jit(solution)/shard_map/ppermute | solution.py:16
  89.2 2.0 collective-permute-start.25
  91.2 2.2 %collective-permute-done.24 = bf16[192,256]{1,0:T(8,128)(2,1)S(1)} collective-permute-done((bf16[192,256]{1,0:T(8,128)(2,1)S(1)}, bf16[192,256]{1,0:T(8,128)(2,1)S(1)}, u32[]{:S(2)}, u32[]{:S(2)}) %collective-permute-start.24) | collective-permute-done | bytes 98336 | tf_op jit(solution)/shard_map/ppermute | solution.py:16
  93.4 2.3 %collective-permute-done.25 = bf16[192,256]{1,0:T(8,128)(2,1)S(1)} collective-permute-done((bf16[192,256]{1,0:T(8,128)(2,1)S(1)}, bf16[192,256]{1,0:T(8,128)(2,1)S(1)}, u32[]{:S(2)}, u32[]{:S(2)}) %collective-permute-start.25) | collective-permute-done | bytes 98336 | tf_op jit(solution)/shard_map/ppermute | solution.py:16
  96.4 1.5 collective-permute-start.27
  97.9 2.4 %collective-permute-done.29.refs_1_ = bf16[192,2048]{1,0:T(8,128)(2,1)S(1)} collective-permute-done((bf16[192,2048]{1,0:T(8,128)(2,1)S(1)}, bf16[192,2048]{1,0:T(8,128)(2,1)S(1)}, u32[]{:S(2)}, u32[]{:S(2)}) %collective-permute-start.29) | collective-permute-done | bytes 786464 | tf_op jit(solution)/shard_map/ppermute | solution.py:16
  100.3 1.5 collective-permute-start.28
  101.8 15.9 %collective-permute-done.30.refs_2_ = bf16[192,2048]{1,0:T(8,128)(2,1)} collective-permute-done((bf16[192,2048]{1,0:T(8,128)(2,1)}, bf16[192,2048]{1,0:T(8,128)(2,1)}, u32[]{:S(2)}, u32[]{:S(2)}) %collective-permute-start.30) | collective-permute-done | bytes 786464 | tf_op jit(solution)/shard_map/ppermute | solution.py:16
  120.1 1.6 collective-permute-done.28.refs_7_
  121.6 3.0 %weight_rows.3 = bf16[2048,256]{1,0:T(8,128)(2,1)S(1)} custom-call(s32[1]{0:T(128)} %bitcast.13.z, bf16[192,2048]{1,0:T(8,128)(2,1)S(1)} %get-tuple-element.41.refs_0_, bf16[192,2048]{1,0:T(8,128)(2,1)S(1)} %collective-permute-done.29.refs_1_, bf16[192,2048]{1,0:T(8,128)(2,1)} %collective-permute-done.30.refs_2_, ...), custom_call_target="tpu_custom_call" | custom-call | flops 805306368 | bytes 5636096 | tf_op jit(solution)/shard_map/weight_rows/pallas_call | solution.py:177
  125.7 1.5 collective-permute-start.20
  128.2 16.9 %collective-permute-done.19.refs_1_ = bf16[192,2048]{1,0:T(8,128)(2,1)S(1)} collective-permute-done((bf16[192,2048]{1,0:T(8,128)(2,1)S(1)}, bf16[192,2048]{1,0:T(8,128)(2,1)S(1)}, u32[]{:S(2)}, u32[]{:S(2)}) %collective-permute-start.19) | collective-permute-done | bytes 786464 | tf_op jit(solution)/shard_map/ppermute | solution.py:16
  145.1 17.1 %collective-permute-done.20.refs_2_ = bf16[192,2048]{1,0:T(8,128)(2,1)S(1)} collective-permute-done((bf16[192,2048]{1,0:T(8,128)(2,1)S(1)}, bf16[192,2048]{1,0:T(8,128)(2,1)S(1)}, u32[]{:S(2)}, u32[]{:S(2)}) %collective-permute-start.20) | collective-permute-done | bytes 786464 | tf_op jit(solution)/shard_map/ppermute | solution.py:16
  162.2 2.4 %weight_rows.2 = f32[2048,256]{1,0:T(8,128)S(1)} custom-call(s32[1]{0:T(128)} %bitcast.13.z, bf16[192,2048]{1,0:T(8,128)(2,1)S(1)} %get-tuple-element.46.refs_0_, bf16[192,2048]{1,0:T(8,128)(2,1)S(1)} %collective-permute-done.19.refs_1_, bf16[192,2048]{1,0:T(8,128)(2,1)S(1)} %collective-permute-done.20.refs_2_, ...), custom_call_target="tpu_custom_call" | custom-call | flops 805306368 | bytes 5636096 | tf_op jit(solution)/shard_map/weight_rows/pallas_call | solution.py:177
  165.0 1.6 collective-permute-start.33
  166.6 1.6 collective-permute-start.34
  169.4 7.9 %collective-permute-done.33 = bf16[512,256]{1,0:T(8,128)(2,1)S(1)} collective-permute-done((bf16[512,256]{1,0:T(8,128)(2,1)S(1)}, bf16[512,256]{1,0:T(8,128)(2,1)S(1)}, u32[]{:S(2)}, u32[]{:S(2)}) %collective-permute-start.33) | collective-permute-done | bytes 262176 | tf_op jit(solution)/shard_map/ppermute | solution.py:16
  177.3 10.6 %collective-permute-done.34 = bf16[512,256]{1,0:T(8,128)(2,1)S(1)} collective-permute-done((bf16[512,256]{1,0:T(8,128)(2,1)S(1)}, bf16[512,256]{1,0:T(8,128)(2,1)S(1)}, u32[]{:S(2)}, u32[]{:S(2)}) %collective-permute-start.34) | collective-permute-done | bytes 262176 | tf_op jit(solution)/shard_map/ppermute | solution.py:16
  188.1 4.4 %collective-permute-start.36 = (bf16[512,256]{1,0:T(8,128)(2,1)S(1)}, bf16[512,256]{1,0:T(8,128)(2,1)S(1)}, u32[]{:S(2)}, u32[]{:S(2)}) collective-permute-start(bf16[512,256]{1,0:T(8,128)(2,1)S(1)} %fusion.12.refs_0_), channel_id=1, source_target_pairs={{0,2},{1,3},{2,0},{3,1},{4,6},{5,7},{6,4},{7,5},{8,10},{9,11},{10,... | collective-permute-start | bytes 786440 | tf_op jit(solution)/shard_map/ppermute | solution.py:16
  195.0 6.1 %collective-permute-done.36.refs_1_ = bf16[512,256]{1,0:T(8,128)(2,1)S(1)} collective-permute-done((bf16[512,256]{1,0:T(8,128)(2,1)S(1)}, bf16[512,256]{1,0:T(8,128)(2,1)S(1)}, u32[]{:S(2)}, u32[]{:S(2)}) %collective-permute-start.36) | collective-permute-done | bytes 262176 | tf_op jit(solution)/shard_map/ppermute | solution.py:16
  201.1 12.7 %collective-permute-done.37.refs_2_ = bf16[512,256]{1,0:T(8,128)(2,1)S(1)} collective-permute-done((bf16[512,256]{1,0:T(8,128)(2,1)S(1)}, bf16[512,256]{1,0:T(8,128)(2,1)S(1)}, u32[]{:S(2)}, u32[]{:S(2)}) %collective-permute-start.37) | collective-permute-done | bytes 262176 | tf_op jit(solution)/shard_map/ppermute | solution.py:16
  215.6 2.8 %assemble.1 = (f32[4096,128]{1,0:T(8,128)}, f32[4096,128]{1,0:T(8,128)}) custom-call(s32[2]{0:T(128)S(1)} %pad_add_fusion.ids, bf16[512,256]{1,0:T(8,128)(2,1)S(1)} %fusion.12.refs_0_, bf16[512,256]{1,0:T(8,128)(2,1)S(1)} %collective-permute-done.36.refs_1_, bf16[512,256]{1,0:T(8,128)(2,1)S(1)} %collective-permute-done.37.refs_2_, ...), custom_call_target="tpu_custom_call" | custom-call | tf_op jit(solution)/shard_map/assemble/pallas_call | solution.py:209
  (93 shorter events, 20.2 us)
Async XLA Ops:
  1.9 15.9 %collective-permute-start = (bf16[2048,128]{1,0:T(8,128)(2,1)S(1)}, bf16[2048,128]{1,0:T(8,128)(2,1)}, u32[]{:S(2)}, u32[]{:S(2)}) collective-permute-start(bf16[2048,128]{1,0:T(8,128)(2,1)S(1)} %constant_dynamic-slice_fusion.1), channel_id=1, source_target_pairs={{0,8},{8,0},{16,24},{24,16},{1,9},{9,1},{17,25},{25,17},{2,10},{10... | collective-permute-start | bytes 1572872 | tf_op jit(solution)/shard_map/ppermute | solution.py:16
  4.9 28.5 %collective-permute-start.1 = (bf16[2048,128]{1,0:T(8,128)(2,1)S(1)}, bf16[2048,128]{1,0:T(8,128)(2,1)}, u32[]{:S(2)}, u32[]{:S(2)}) collective-permute-start(bf16[2048,128]{1,0:T(8,128)(2,1)S(1)} %constant_dynamic-slice_fusion.1), channel_id=1, source_target_pairs={{0,16},{8,24},{16,0},{24,8},{1,17},{9,25},{17,1},{25,9},{2,18},{10... | collective-permute-start | bytes 1572872 | tf_op jit(solution)/shard_map/ppermute | solution.py:16
  8.3 22.8 %collective-permute-start.4 = (bf16[2048,128]{1,0:T(8,128)(2,1)}, bf16[2048,128]{1,0:T(8,128)(2,1)}, u32[]{:S(2)}, u32[]{:S(2)}) collective-permute-start(bf16[2048,128]{1,0:T(8,128)(2,1)} %constant_dynamic-slice_fusion), channel_id=1, source_target_pairs={{0,16},{8,24},{16,0},{24,8},{1,17},{9,25},{17,1},{25,9},{2,18},{10... | collective-permute-start | bytes 1572872 | tf_op jit(solution)/shard_map/ppermute | solution.py:16
  8.8 25.0 %collective-permute-start.3 = (bf16[2048,128]{1,0:T(8,128)(2,1)}, bf16[2048,128]{1,0:T(8,128)(2,1)}, u32[]{:S(2)}, u32[]{:S(2)}) collective-permute-start(bf16[2048,128]{1,0:T(8,128)(2,1)} %constant_dynamic-slice_fusion), channel_id=1, source_target_pairs={{0,8},{8,0},{16,24},{24,16},{1,9},{9,1},{17,25},{25,17},{2,10},{10... | collective-permute-start | bytes 1572872 | tf_op jit(solution)/shard_map/ppermute | solution.py:16
  13.9 30.2 %copy-start.7 = (bf16[192,2048]{1,0:T(8,128)(2,1)}, bf16[192,2048]{1,0:T(8,128)(2,1)S(1)}, u32[]{:S(2)}) copy-start(bf16[192,2048]{1,0:T(8,128)(2,1)S(1)} %get-tuple-element.28) | copy-start | bytes 2359300
  13.9 31.6 %copy-start.5 = (bf16[192,2048]{1,0:T(8,128)(2,1)}, bf16[192,2048]{1,0:T(8,128)(2,1)S(1)}, u32[]{:S(2)}) copy-start(bf16[192,2048]{1,0:T(8,128)(2,1)S(1)} %get-tuple-element.29) | copy-start | bytes 2359300
  13.9 37.7 %copy-start.9 = (bf16[192,2048]{1,0:T(8,128)(2,1)}, bf16[192,2048]{1,0:T(8,128)(2,1)S(1)}, u32[]{:S(2)}) copy-start(bf16[192,2048]{1,0:T(8,128)(2,1)S(1)} %get-tuple-element.27) | copy-start | bytes 2359300
  13.9 19.0 %copy-start.11 = (bf16[4096,128]{1,0:T(8,128)(2,1)S(1)}, bf16[4096,128]{1,0:T(8,128)(2,1)}, u32[]{:S(2)}) copy-start(bf16[4096,128]{1,0:T(8,128)(2,1)} %param.11) | copy-start | bytes 3145732
  17.8 23.0 %collective-permute-start.2 = (bf16[2048,128]{1,0:T(8,128)(2,1)}, bf16[2048,128]{1,0:T(8,128)(2,1)S(1)}, u32[]{:S(2)}, u32[]{:S(2)}) collective-permute-start(bf16[2048,128]{1,0:T(8,128)(2,1)} %collective-permute-done), channel_id=1, source_target_pairs={{0,16},{8,24},{16,0},{24,8},{1,17},{9,25},{17,1},{25,9},{2,18},{10... | collective-permute-start | bytes 1572872 | tf_op jit(solution)/shard_map/ppermute | solution.py:16
  31.1 11.2 %collective-permute-start.5 = (bf16[2048,128]{1,0:T(8,128)(2,1)}, bf16[2048,128]{1,0:T(8,128)(2,1)S(1)}, u32[]{:S(2)}, u32[]{:S(2)}) collective-permute-start(bf16[2048,128]{1,0:T(8,128)(2,1)} %collective-permute-done.4), channel_id=1, source_target_pairs={{0,8},{8,0},{16,24},{24,16},{1,9},{9,1},{17,25},{25,17},{2,10},{10... | collective-permute-start | bytes 1572872 | tf_op jit(solution)/shard_map/ppermute | solution.py:16
  33.3 12.7 %collective-permute-start.6 = (bf16[2048,128]{1,0:T(8,128)(2,1)}, bf16[2048,128]{1,0:T(8,128)(2,1)S(1)}, u32[]{:S(2)}, u32[]{:S(2)}) collective-permute-start(bf16[2048,128]{1,0:T(8,128)(2,1)} %collective-permute-done), channel_id=1, source_target_pairs={{0,1},{1,0},{2,3},{3,2},{4,5},{5,4},{6,7},{7,6},{8,9},{9,8},{10,11... | collective-permute-start | bytes 1572872 | tf_op jit(solution)/shard_map/ppermute | solution.py:16
  33.4 16.7 %collective-permute-start.10 = (bf16[2048,128]{1,0:T(8,128)(2,1)}, bf16[2048,128]{1,0:T(8,128)(2,1)S(1)}, u32[]{:S(2)}, u32[]{:S(2)}) collective-permute-start(bf16[2048,128]{1,0:T(8,128)(2,1)} %collective-permute-done.4), channel_id=1, source_target_pairs={{0,1},{1,0},{2,3},{3,2},{4,5},{5,4},{6,7},{7,6},{8,9},{9,8},{10,11... | collective-permute-start | bytes 1572872 | tf_op jit(solution)/shard_map/ppermute | solution.py:16
  33.9 12.9 %collective-permute-start.7 = (bf16[2048,128]{1,0:T(8,128)(2,1)}, bf16[2048,128]{1,0:T(8,128)(2,1)S(1)}, u32[]{:S(2)}, u32[]{:S(2)}) collective-permute-start(bf16[2048,128]{1,0:T(8,128)(2,1)} %collective-permute-done.1), channel_id=1, source_target_pairs={{0,1},{1,0},{2,3},{3,2},{4,5},{5,4},{6,7},{7,6},{8,9},{9,8},{10,11... | collective-permute-start | bytes 1572872 | tf_op jit(solution)/shard_map/ppermute | solution.py:16
  40.8 7.5 %collective-permute-start.9 = (bf16[2048,128]{1,0:T(8,128)(2,1)}, bf16[2048,128]{1,0:T(8,128)(2,1)S(1)}, u32[]{:S(2)}, u32[]{:S(2)}) collective-permute-start(bf16[2048,128]{1,0:T(8,128)(2,1)} %collective-permute-done.3), channel_id=1, source_target_pairs={{0,1},{1,0},{2,3},{3,2},{4,5},{5,4},{6,7},{7,6},{8,9},{9,8},{10,11... | collective-permute-start | bytes 1572872 | tf_op jit(solution)/shard_map/ppermute | solution.py:16
  45.8 7.2 %collective-permute-start.8 = (bf16[2048,128]{1,0:T(8,128)(2,1)S(1)}, bf16[2048,128]{1,0:T(8,128)(2,1)S(1)}, u32[]{:S(2)}, u32[]{:S(2)}) collective-permute-start(bf16[2048,128]{1,0:T(8,128)(2,1)S(1)} %collective-permute-done.2), channel_id=1, source_target_pairs={{0,1},{1,0},{2,3},{3,2},{4,5},{5,4},{6,7},{7,6},{8,9},{9,8},{10,11... | collective-permute-start | bytes 1572872 | tf_op jit(solution)/shard_map/ppermute | solution.py:16
  45.9 8.7 %collective-permute-start.11 = (bf16[2048,128]{1,0:T(8,128)(2,1)S(1)}, bf16[2048,128]{1,0:T(8,128)(2,1)S(1)}, u32[]{:S(2)}, u32[]{:S(2)}) collective-permute-start(bf16[2048,128]{1,0:T(8,128)(2,1)S(1)} %collective-permute-done.5), channel_id=1, source_target_pairs={{0,1},{1,0},{2,3},{3,2},{4,5},{5,4},{6,7},{7,6},{8,9},{9,8},{10,11... | collective-permute-start | bytes 1572872 | tf_op jit(solution)/shard_map/ppermute | solution.py:16
  51.6 18.3 %copy-start.1 = (bf16[1,192,1024]{2,1,0:T(8,128)(2,1)S(1)}, bf16[1,192,1024]{2,1,0:T(8,128)(2,1)}, u32[]{:S(2)}) copy-start(bf16[1,192,1024]{2,1,0:T(8,128)(2,1)} %param.8) | copy-start | bytes 1179652
  56.1 4.9 %collective-permute-start.13 = (bf16[192,256]{1,0:T(8,128)(2,1)S(1)}, bf16[192,256]{1,0:T(8,128)(2,1)S(1)}, u32[]{:S(2)}, u32[]{:S(2)}) collective-permute-start(bf16[192,256]{1,0:T(8,128)(2,1)S(1)} %pad_maximum_fusion.refs_0_), channel_id=1, source_target_pairs={{0,2},{1,3},{2,0},{3,1},{4,6},{5,7},{6,4},{7,5},{8,10},{9,11},{10,... | collective-permute-start | bytes 294920 | tf_op jit(solution)/shard_map/ppermute | solution.py:16
  57.8 10.7 %collective-permute-start.15 = (bf16[192,256]{1,0:T(8,128)(2,1)S(1)}, bf16[192,256]{1,0:T(8,128)(2,1)S(1)}, u32[]{:S(2)}, u32[]{:S(2)}) collective-permute-start(bf16[192,256]{1,0:T(8,128)(2,1)S(1)} %pad_maximum_fusion.refs_0_), channel_id=1, source_target_pairs={{0,4},{1,5},{2,6},{3,7},{4,0},{5,1},{6,2},{7,3},{8,12},{9,13},{10,... | collective-permute-start | bytes 294920 | tf_op jit(solution)/shard_map/ppermute | solution.py:16
  60.4 8.1 %collective-permute-start.17 = (bf16[192,256]{1,0:T(8,128)(2,1)S(1)}, bf16[192,256]{1,0:T(8,128)(2,1)S(1)}, u32[]{:S(2)}, u32[]{:S(2)}) collective-permute-start(bf16[192,256]{1,0:T(8,128)(2,1)S(1)} %pad_maximum_fusion.refs_0_), channel_id=1, source_target_pairs={{0,6},{1,7},{2,4},{3,5},{4,2},{5,3},{6,0},{7,1},{8,14},{9,15},{10,... | collective-permute-start | bytes 294920 | tf_op jit(solution)/shard_map/ppermute | solution.py:16
  60.6 8.4 %collective-permute-start.12 = (bf16[192,256]{1,0:T(8,128)(2,1)S(1)}, bf16[192,256]{1,0:T(8,128)(2,1)S(1)}, u32[]{:S(2)}, u32[]{:S(2)}) collective-permute-start(bf16[192,256]{1,0:T(8,128)(2,1)S(1)} %pad_maximum_fusion.refs_0_), channel_id=1, source_target_pairs={{0,1},{1,0},{2,3},{3,2},{4,5},{5,4},{6,7},{7,6},{8,9},{9,8},{10,11... | collective-permute-start | bytes 294920 | tf_op jit(solution)/shard_map/ppermute | solution.py:16
  61.0 8.0 %collective-permute-start.14 = (bf16[192,256]{1,0:T(8,128)(2,1)S(1)}, bf16[192,256]{1,0:T(8,128)(2,1)S(1)}, u32[]{:S(2)}, u32[]{:S(2)}) collective-permute-start(bf16[192,256]{1,0:T(8,128)(2,1)S(1)} %collective-permute-done.13.refs_2_), channel_id=1, source_target_pairs={{0,1},{1,0},{2,3},{3,2},{4,5},{5,4},{6,7},{7,6},{8,9},{9,8},{10,11... | collective-permute-start | bytes 294920 | tf_op jit(solution)/shard_map/ppermute | solution.py:16
  68.4 1.3 collective-permute-start.16
  68.4 1.5 collective-permute-start.18
  79.5 3.9 %collective-permute-start.22 = (bf16[768,256]{1,0:T(8,128)(2,1)S(1)}, bf16[768,256]{1,0:T(8,128)(2,1)S(1)}, u32[]{:S(2)}, u32[]{:S(2)}) collective-permute-start(bf16[768,256]{1,0:T(8,128)(2,1)S(1)} %get-tuple-element.31), channel_id=1, source_target_pairs={{0,1},{1,0},{2,3},{3,2},{4,5},{5,4},{6,7},{7,6},{8,9},{9,8},{10,11... | collective-permute-start | bytes 1179656 | tf_op jit(solution)/shard_map/ppermute | solution.py:16
  79.9 20.4 %collective-permute-start.29 = (bf16[192,2048]{1,0:T(8,128)(2,1)S(1)}, bf16[192,2048]{1,0:T(8,128)(2,1)S(1)}, u32[]{:S(2)}, u32[]{:S(2)}) collective-permute-start(bf16[192,2048]{1,0:T(8,128)(2,1)S(1)} %get-tuple-element.32), channel_id=1, source_target_pairs={{0,8},{8,0},{16,24},{24,16},{1,9},{9,1},{17,25},{25,17},{2,10},{10... | collective-permute-start | bytes 2359304 | tf_op jit(solution)/shard_map/ppermute | solution.py:16
  80.4 37.3 %collective-permute-start.30 = (bf16[192,2048]{1,0:T(8,128)(2,1)}, bf16[192,2048]{1,0:T(8,128)(2,1)}, u32[]{:S(2)}, u32[]{:S(2)}) collective-permute-start(bf16[192,2048]{1,0:T(8,128)(2,1)} %get-tuple-element.33), channel_id=1, source_target_pairs={{0,16},{8,24},{16,0},{24,8},{1,17},{9,25},{17,1},{25,9},{2,18},{10... | collective-permute-start | bytes 2359304 | tf_op jit(solution)/shard_map/ppermute | solution.py:16
  81.9 36.3 %collective-permute-start.31 = (bf16[192,2048]{1,0:T(8,128)(2,1)}, bf16[192,2048]{1,0:T(8,128)(2,1)}, u32[]{:S(2)}, u32[]{:S(2)}) collective-permute-start(bf16[192,2048]{1,0:T(8,128)(2,1)} %get-tuple-element.34), channel_id=1, source_target_pairs={{0,24},{8,16},{16,8},{24,0},{1,25},{9,17},{17,9},{25,1},{2,26},{10... | collective-permute-start | bytes 2359304 | tf_op jit(solution)/shard_map/ppermute | solution.py:16
  83.5 5.7 %collective-permute-start.23 = (bf16[192,256]{1,0:T(8,128)(2,1)S(1)}, bf16[192,256]{1,0:T(8,128)(2,1)S(1)}, u32[]{:S(2)}, u32[]{:S(2)}) collective-permute-start(bf16[192,256]{1,0:T(8,128)(2,1)S(1)} %get-tuple-element.52), channel_id=1, source_target_pairs={{0,2},{1,3},{2,0},{3,1},{4,6},{5,7},{6,4},{7,5},{8,10},{9,11},{10,... | collective-permute-start | bytes 294920 | tf_op jit(solution)/shard_map/ppermute | solution.py:16
  84.9 8.5 %collective-permute-start.24 = (bf16[192,256]{1,0:T(8,128)(2,1)S(1)}, bf16[192,256]{1,0:T(8,128)(2,1)S(1)}, u32[]{:S(2)}, u32[]{:S(2)}) collective-permute-start(bf16[192,256]{1,0:T(8,128)(2,1)S(1)} %get-tuple-element.54), channel_id=1, source_target_pairs={{0,4},{1,5},{2,6},{3,7},{4,0},{5,1},{6,2},{7,3},{8,12},{9,13},{10,... | collective-permute-start | bytes 294920 | tf_op jit(solution)/shard_map/ppermute | solution.py:16
  89.2 6.5 %collective-permute-start.25 = (bf16[192,256]{1,0:T(8,128)(2,1)S(1)}, bf16[192,256]{1,0:T(8,128)(2,1)S(1)}, u32[]{:S(2)}, u32[]{:S(2)}) collective-permute-start(bf16[192,256]{1,0:T(8,128)(2,1)S(1)} %get-tuple-element.53), channel_id=1, source_target_pairs={{0,6},{1,7},{2,4},{3,5},{4,2},{5,3},{6,0},{7,1},{8,14},{9,15},{10,... | collective-permute-start | bytes 294920 | tf_op jit(solution)/shard_map/ppermute | solution.py:16
  95.8 23.6 %collective-permute-start.26 = (bf16[192,256]{1,0:T(8,128)(2,1)S(1)}, bf16[192,256]{1,0:T(8,128)(2,1)}, u32[]{:S(2)}, u32[]{:S(2)}) collective-permute-start(bf16[192,256]{1,0:T(8,128)(2,1)S(1)} %fusion.17.refs_4_), channel_id=1, source_target_pairs={{0,8},{8,0},{16,24},{24,16},{1,9},{9,1},{17,25},{25,17},{2,10},{10... | collective-permute-start | bytes 294920 | tf_op jit(solution)/shard_map/ppermute | solution.py:16
  96.4 23.7 %collective-permute-start.27 = (bf16[192,256]{1,0:T(8,128)(2,1)S(1)}, bf16[192,256]{1,0:T(8,128)(2,1)}, u32[]{:S(2)}, u32[]{:S(2)}) collective-permute-start(bf16[192,256]{1,0:T(8,128)(2,1)S(1)} %fusion.17.refs_4_), channel_id=1, source_target_pairs={{0,16},{8,24},{16,0},{24,8},{1,17},{9,25},{17,1},{25,9},{2,18},{10... | collective-permute-start | bytes 294920 | tf_op jit(solution)/shard_map/ppermute | solution.py:16
  100.3 21.4 %collective-permute-start.28 = (bf16[192,256]{1,0:T(8,128)(2,1)S(1)}, bf16[192,256]{1,0:T(8,128)(2,1)}, u32[]{:S(2)}, u32[]{:S(2)}) collective-permute-start(bf16[192,256]{1,0:T(8,128)(2,1)S(1)} %fusion.17.refs_4_), channel_id=1, source_target_pairs={{0,24},{8,16},{16,8},{24,0},{1,25},{9,17},{17,9},{25,1},{2,26},{10... | collective-permute-start | bytes 294920 | tf_op jit(solution)/shard_map/ppermute | solution.py:16
  124.6 40.0 %collective-permute-start.32 = (bf16[2048,256]{1,0:T(8,128)(2,1)S(1)}, bf16[2048,256]{1,0:T(8,128)(2,1)S(1)}, u32[]{:S(2)}, u32[]{:S(2)}) collective-permute-start(bf16[2048,256]{1,0:T(8,128)(2,1)S(1)} %weight_rows.3), channel_id=1, source_target_pairs={{0,1},{1,0},{2,3},{3,2},{4,5},{5,4},{6,7},{7,6},{8,9},{9,8},{10,11... | collective-permute-start | bytes 3145736 | tf_op jit(solution)/shard_map/ppermute | solution.py:16
  124.7 20.4 %collective-permute-start.19 = (bf16[192,2048]{1,0:T(8,128)(2,1)S(1)}, bf16[192,2048]{1,0:T(8,128)(2,1)S(1)}, u32[]{:S(2)}, u32[]{:S(2)}) collective-permute-start(bf16[192,2048]{1,0:T(8,128)(2,1)S(1)} %copy-done.10), channel_id=1, source_target_pairs={{0,8},{8,0},{16,24},{24,16},{1,9},{9,1},{17,25},{25,17},{2,10},{10... | collective-permute-start | bytes 2359304 | tf_op jit(solution)/shard_map/ppermute | solution.py:16
  125.7 36.5 %collective-permute-start.20 = (bf16[192,2048]{1,0:T(8,128)(2,1)S(1)}, bf16[192,2048]{1,0:T(8,128)(2,1)S(1)}, u32[]{:S(2)}, u32[]{:S(2)}) collective-permute-start(bf16[192,2048]{1,0:T(8,128)(2,1)S(1)} %copy-done.8), channel_id=1, source_target_pairs={{0,16},{8,24},{16,0},{24,8},{1,17},{9,25},{17,1},{25,9},{2,18},{10... | collective-permute-start | bytes 2359304 | tf_op jit(solution)/shard_map/ppermute | solution.py:16
  127.2 34.9 %collective-permute-start.21 = (bf16[192,2048]{1,0:T(8,128)(2,1)S(1)}, bf16[192,2048]{1,0:T(8,128)(2,1)S(1)}, u32[]{:S(2)}, u32[]{:S(2)}) collective-permute-start(bf16[192,2048]{1,0:T(8,128)(2,1)S(1)} %copy-done.6), channel_id=1, source_target_pairs={{0,24},{8,16},{16,8},{24,0},{1,25},{9,17},{17,9},{25,1},{2,26},{10... | collective-permute-start | bytes 2359304 | tf_op jit(solution)/shard_map/ppermute | solution.py:16
  165.0 12.3 %collective-permute-start.33 = (bf16[512,256]{1,0:T(8,128)(2,1)S(1)}, bf16[512,256]{1,0:T(8,128)(2,1)S(1)}, u32[]{:S(2)}, u32[]{:S(2)}) collective-permute-start(bf16[512,256]{1,0:T(8,128)(2,1)S(1)} %get-tuple-element.49), channel_id=1, source_target_pairs={{0,2},{1,3},{2,0},{3,1},{4,6},{5,7},{6,4},{7,5},{8,10},{9,11},{10,... | collective-permute-start | bytes 786440 | tf_op jit(solution)/shard_map/ppermute | solution.py:16
  166.6 21.4 %collective-permute-start.34 = (bf16[512,256]{1,0:T(8,128)(2,1)S(1)}, bf16[512,256]{1,0:T(8,128)(2,1)S(1)}, u32[]{:S(2)}, u32[]{:S(2)}) collective-permute-start(bf16[512,256]{1,0:T(8,128)(2,1)S(1)} %get-tuple-element.51), channel_id=1, source_target_pairs={{0,4},{1,5},{2,6},{3,7},{4,0},{5,1},{6,2},{7,3},{8,12},{9,13},{10,... | collective-permute-start | bytes 786440 | tf_op jit(solution)/shard_map/ppermute | solution.py:16
  168.1 19.8 %collective-permute-start.35 = (bf16[512,256]{1,0:T(8,128)(2,1)S(1)}, bf16[512,256]{1,0:T(8,128)(2,1)S(1)}, u32[]{:S(2)}, u32[]{:S(2)}) collective-permute-start(bf16[512,256]{1,0:T(8,128)(2,1)S(1)} %get-tuple-element.50), channel_id=1, source_target_pairs={{0,6},{1,7},{2,4},{3,5},{4,2},{5,3},{6,0},{7,1},{8,14},{9,15},{10,... | collective-permute-start | bytes 786440 | tf_op jit(solution)/shard_map/ppermute | solution.py:16
  188.1 12.9 %collective-permute-start.36 = (bf16[512,256]{1,0:T(8,128)(2,1)S(1)}, bf16[512,256]{1,0:T(8,128)(2,1)S(1)}, u32[]{:S(2)}, u32[]{:S(2)}) collective-permute-start(bf16[512,256]{1,0:T(8,128)(2,1)S(1)} %fusion.12.refs_0_), channel_id=1, source_target_pairs={{0,2},{1,3},{2,0},{3,1},{4,6},{5,7},{6,4},{7,5},{8,10},{9,11},{10,... | collective-permute-start | bytes 786440 | tf_op jit(solution)/shard_map/ppermute | solution.py:16
  192.5 21.2 %collective-permute-start.37 = (bf16[512,256]{1,0:T(8,128)(2,1)S(1)}, bf16[512,256]{1,0:T(8,128)(2,1)S(1)}, u32[]{:S(2)}, u32[]{:S(2)}) collective-permute-start(bf16[512,256]{1,0:T(8,128)(2,1)S(1)} %fusion.12.refs_0_), channel_id=1, source_target_pairs={{0,4},{1,5},{2,6},{3,7},{4,0},{5,1},{6,2},{7,3},{8,12},{9,13},{10,... | collective-permute-start | bytes 786440 | tf_op jit(solution)/shard_map/ppermute | solution.py:16
  193.6 20.1 %collective-permute-start.38 = (bf16[512,256]{1,0:T(8,128)(2,1)S(1)}, bf16[512,256]{1,0:T(8,128)(2,1)S(1)}, u32[]{:S(2)}, u32[]{:S(2)}) collective-permute-start(bf16[512,256]{1,0:T(8,128)(2,1)S(1)} %fusion.12.refs_0_), channel_id=1, source_target_pairs={{0,6},{1,7},{2,4},{3,5},{4,2},{5,3},{6,0},{7,1},{8,14},{9,15},{10,... | collective-permute-start | bytes 786440 | tf_op jit(solution)/shard_map/ppermute | solution.py:16
  195.0 19.3 %collective-permute-start.39 = (bf16[512,256]{1,0:T(8,128)(2,1)S(1)}, bf16[512,256]{1,0:T(8,128)(2,1)S(1)}, u32[]{:S(2)}, u32[]{:S(2)}) collective-permute-start(bf16[512,256]{1,0:T(8,128)(2,1)S(1)} %fusion.12.refs_0_), channel_id=1, source_target_pairs={{0,1},{1,0},{2,3},{3,2},{4,5},{5,4},{6,7},{7,6},{8,9},{9,8},{10,11... | collective-permute-start | bytes 786440 | tf_op jit(solution)/shard_map/ppermute | solution.py:16
  201.1 13.3 %collective-permute-start.40 = (bf16[512,256]{1,0:T(8,128)(2,1)S(1)}, bf16[512,256]{1,0:T(8,128)(2,1)S(1)}, u32[]{:S(2)}, u32[]{:S(2)}) collective-permute-start(bf16[512,256]{1,0:T(8,128)(2,1)S(1)} %collective-permute-done.36.refs_1_), channel_id=1, source_target_pairs={{0,1},{1,0},{2,3},{3,2},{4,5},{5,4},{6,7},{7,6},{8,9},{9,8},{10,11... | collective-permute-start | bytes 786440 | tf_op jit(solution)/shard_map/ppermute | solution.py:16
  213.7 1.5 collective-permute-start.41
  213.7 1.9 collective-permute-start.42
  (7 other events, 69.0 us)

commit v2 on v1

--- a/solution.py
+++ b/solution.py
@@ -9,6 +9,11 @@
 from jax.sharding import PartitionSpec as P
 
 VMEM_LIMIT = 48 * 1024 * 1024
+NO_COST = pl.CostEstimate(flops=0, bytes_accessed=0, transcendentals=0)
+
+
+def moved_rows(block_rows):
+    return block_rows * 4 // 8 // 256 * 256
 
 
 def swap(array, axis, distance):
@@ -140,84 +145,176 @@
             pltpu.VMEM((2 * stacked, head_dim), jnp.bfloat16),
         ],
         compiler_params=pltpu.CompilerParams(vmem_limit_bytes=VMEM_LIMIT),
-        cost_estimate=pl.CostEstimate(
-            flops=10 * window * 2 * stacked * head_dim,
-            bytes_accessed=8 * row_count * width + 10 * seq_rows * head_dim,
-            transcendentals=window * 2 * stacked,
-        ),
+        cost_estimate=NO_COST,
         name="attention",
     )(me, order, lengths, queries, cotangent, *kv_blocks)
 
 
-def weight_kernel(dp_count, z_count, z, *refs):
-    hidden, grads, out_ref = refs[:dp_count], refs[dp_count : 2 * dp_count], refs[-1]
-    columns = hidden[0].shape[1]
-    share = columns // z_count
-    tile = max(share, 128)
-    for start in range(0, columns, tile):
-        product = None
-        for one, grad in zip(hidden, grads):
-            term = lax.dot_general(
-                one[:, start : start + tile],
-                grad[...],
-                (((0,), (0,)), ((), ())),
-                preferred_element_type=jnp.float32,
-            )
-            product = term if product is None else product + term
-        for inner in range(0, tile, share):
-            to = pl.multiple_of((z[0] ^ ((start + inner) // share)) * share, share)
-            out_ref[pl.ds(to, share), :] = product[inner : inner + share, :].astype(out_ref.dtype)
-
-
-def weight_rows(z, hidden, grads, z_count, kind):
-    columns, width = hidden[0].shape[1], grads[0].shape[1]
-    rows = sum(one.shape[0] for one in hidden)
+def project_kernel(plan, side_rows, core, *refs):
+    start_ref, out_ref = refs[0], refs[-1]
+    hidden = refs[1 : 1 + plan.hidden]
+    weights = refs[1 + plan.hidden : -1]
+    width = weights[0].shape[1]
+    total = [start_ref[:, :width], start_ref[:, width:]] if plan.start else [None, None]
+    for (which, block, side), weight in zip(plan.terms, weights):
+        from_column = pl.multiple_of((core[0] ^ side) * side_rows, side_rows)
+        left = hidden[block][:, pl.ds(from_column, side_rows)]
+        term = jnp.dot(left, weight[...], preferred_element_type=jnp.float32)
+        total[which] = term if total[which] is None else total[which] + term
+    out_ref[:, :width] = total[0].astype(out_ref.dtype)
+    out_ref[:, width:] = total[1].astype(out_ref.dtype)
+
+
+class Plan:
+    def __init__(self, **fields):
+        self.__dict__.update(fields)
+
+
+def project(core, start, hidden, terms, kind):
+    row_count = hidden[0].shape[0]
+    side_rows, width = terms[0][3].shape
+    plan = Plan(hidden=len(hidden), terms=[term[:3] for term in terms], start=start is not None)
+    if start is None:
+        start = core
     smem = pl.BlockSpec(memory_space=pltpu.SMEM)
     vmem = pl.BlockSpec(memory_space=pltpu.VMEM)
     return pl.pallas_call(
-        functools.partial(weight_kernel, len(hidden), z_count),
-        out_shape=jax.ShapeDtypeStruct((columns, width), kind),
-        in_specs=[smem] + [vmem] * (2 * len(hidden)),
+        functools.partial(project_kernel, plan, side_rows),
+        out_shape=jax.ShapeDtypeStruct((row_count, 2 * width), kind),
+        in_specs=[smem, vmem if plan.start else smem] + [vmem] * (len(hidden) + len(terms)),
         out_specs=vmem,
         compiler_params=pltpu.CompilerParams(vmem_limit_bytes=VMEM_LIMIT),
-        cost_estimate=pl.CostEstimate(
-            flops=2 * rows * columns * width,
-            bytes_accessed=2 * rows * (columns + width) + 4 * columns * width,
-            transcendentals=0,
-        ),
+        cost_estimate=NO_COST,
+        name="project",
+    )(core, start, *hidden, *[term[3] for term in terms])
+
+
+def weight_kernel(plan, ids, *refs):
+    hidden = refs[: plan.hidden]
+    grads = refs[plan.hidden : plan.hidden + plan.grads]
+    theirs_ref, key_ref, value_ref = refs[plan.hidden + plan.grads :]
+    z, core = ids[0] % plan.sub_count, ids[1]
+    rows, width = plan.rows, grads[0].shape[1] // 2
+    share = rows // plan.sub_count
+    tile = next(size for size in (512, 256, 128) if rows % size == 0)
+    step = math.gcd(share, tile)
+    for side in (1, 0):
+        origin = plan.origin + (core ^ side) * rows
+        for at, group in enumerate(plan.groups):
+            for start in range(0, rows, tile):
+                product = None
+                for block, grad in group:
+                    columns = pl.ds(pl.multiple_of(origin + start, 128), tile)
+                    term = lax.dot_general(
+                        hidden[block][:, columns],
+                        grads[grad][...],
+                        (((0,), (0,)), ((), ())),
+                        preferred_element_type=jnp.float32,
+                    )
+                    product = term if product is None else product + term
+                for inner in range(0, tile, step):
+                    part, offset = divmod(start + inner, share)
+                    to = pl.multiple_of(at * rows + (z ^ part) * share + offset, step)
+                    piece = product[inner : inner + step, :]
+                    if side:
+                        theirs_ref[pl.ds(to, step), :] = piece.astype(theirs_ref.dtype)
+                    else:
+                        key_ref[pl.ds(to, step), :] = piece[:, :width]
+                        value_ref[pl.ds(to, step), :] = piece[:, width:]
+
+
+def weight_rows(ids, hidden, grads, groups, origin, rows, sub_count):
+    width = grads[0].shape[1]
+    total_rows = rows * len(groups)
+    smem = pl.BlockSpec(memory_space=pltpu.SMEM)
+    vmem = pl.BlockSpec(memory_space=pltpu.VMEM)
+    plan = Plan(
+        hidden=len(hidden),
+        grads=len(grads),
+        groups=groups,
+        origin=origin,
+        rows=rows,
+        sub_count=sub_count,
+    )
+    half = jax.ShapeDtypeStruct((total_rows, width // 2), jnp.float32)
+    return pl.pallas_call(
+        functools.partial(weight_kernel, plan),
+        out_shape=(jax.ShapeDtypeStruct((total_rows, width), jnp.bfloat16), half, half),
+        in_specs=[smem] + [vmem] * (len(hidden) + len(grads)),
+        out_specs=(vmem, vmem, vmem),
+        compiler_params=pltpu.CompilerParams(vmem_limit_bytes=VMEM_LIMIT),
+        cost_estimate=NO_COST,
         name="weight_rows",
-    )(z, *hidden, *grads)
-
-
-def assemble_kernel(z_count, ids, *refs):
+    )(ids, *hidden, *grads)
+
+
+def assemble_kernel(sub_count, regions, ids, *refs):
     blocks, key_ref, value_ref = refs[:-2], refs[-2], refs[-1]
-    share, width = blocks[0].shape
-    for side in range(2):
-        for m in range(z_count):
-            to = ((ids[1] ^ side) * z_count + (ids[0] ^ m)) * share
-            to = pl.multiple_of(to, share)
-            block = blocks[side * z_count + m][...].astype(jnp.float32)
-            key_ref[pl.ds(to, share), :] = block[:, : width // 2]
-            value_ref[pl.ds(to, share), :] = block[:, width // 2 :]
-
-
-def assemble(ids, blocks, z_count):
-    share, width = blocks[0].shape
-    shape = jax.ShapeDtypeStruct((2 * z_count * share, width // 2), jnp.float32)
+    z, core = ids[0] % sub_count, ids[1]
+    blocks = iter(blocks)
+    for origin, rows in regions:
+        share = rows // sub_count
+        for side in range(2):
+            for m in range(sub_count):
+                to = origin + (core ^ side) * rows + (z ^ m) * share
+                to = pl.multiple_of(to, share)
+                block_ref = next(blocks)
+                width = block_ref.shape[1] // 2
+                key_ref[pl.ds(to, share), :] = block_ref[:, :width].astype(jnp.float32)
+                value_ref[pl.ds(to, share), :] = block_ref[:, width:].astype(jnp.float32)
+
+
+def assemble(ids, blocks, sub_count, regions):
+    rows = sum(block.shape[0] for block in blocks)
+    shape = jax.ShapeDtypeStruct((rows, blocks[0].shape[1] // 2), jnp.float32)
     smem = pl.BlockSpec(memory_space=pltpu.SMEM)
     vmem = pl.BlockSpec(memory_space=pltpu.VMEM)
     return pl.pallas_call(
-        functools.partial(assemble_kernel, z_count),
+        functools.partial(assemble_kernel, sub_count, regions),
         out_shape=(shape, shape),
         in_specs=[smem] + [vmem] * len(blocks),
         out_specs=(vmem, vmem),
         compiler_params=pltpu.CompilerParams(vmem_limit_bytes=VMEM_LIMIT),
+        cost_estimate=NO_COST,
         name="assemble",
     )(ids, *blocks)
 
 
-def dot32(left, right):
-    return jnp.dot(left, right, preferred_element_type=jnp.float32)
+def add_cores(theirs, keys, values):
+    width = keys.shape[1]
+    came = swap(theirs, "ctx", 1).astype(jnp.float32)
+    return keys + came[:, :width], values + came[:, width:]
+
+
+def sum_over_dp(array, order):
+    count = lax.axis_size("dp")
+    rows = array.shape[0] // count
+    parts = {j: array[j * rows : (j + 1) * rows] for j in range(count)}
+    for bit in order:
+        leaving = [j for j in parts if j & bit]
+        stacked = jnp.concatenate([parts.pop(j).astype(jnp.bfloat16) for j in leaving], axis=0)
+        came = swap(stacked, "dp", bit).astype(jnp.float32)
+        for at, j in enumerate(leaving):
+            parts[j ^ bit] = parts[j ^ bit] + came[at * rows : (at + 1) * rows]
+    return parts[0]
+
+
+def sum_along_z(full, sub_count):
+    share = full.shape[0] // sub_count
+    parts = {m: full[m * share : (m + 1) * share] for m in range(sub_count)}
+    bits = [1 << at for at in range(sub_count.bit_length() - 1)]
+    for bit in bits:
+        for m in list(parts):
+            if m & bit:
+                came = swap(parts.pop(m).astype(jnp.bfloat16), "ctx", 2 * bit)
+                parts[m ^ bit] = parts[m ^ bit] + came.astype(jnp.float32)
+    low = parts[0].astype(jnp.bfloat16)
+    final = (parts[0] + swap(low, "ctx", 2 * sub_count).astype(jnp.float32)).astype(jnp.bfloat16)
+    rows = {0: final}
+    for bit in bits[::-1]:
+        rows.update({m | bit: swap(one, "ctx", 2 * bit) for m, one in list(rows.items())})
+    own = [rows[m] for m in range(sub_count)]
+    return own + [swap(one, "ctx", 1) for one in own]
 
 
 def on_device(hidden_in, queries, grad_out, w_key, w_value, stretch_order, doc_lengths):
@@ -245,31 +342,42 @@
     key_pieces = gather(w_key, bits)
     value_pieces = gather(w_value, bits[::-1])
 
-    def columns(j, side):
-        start = (dp ^ j) * block_rows + (core ^ side) * half_rows
-        return lax.dynamic_slice_in_dim(inputs, start, half_rows, 1)
-
-    hidden = {(j, side): columns(j, side) for j in range(dp_count) for side in range(2)}
+    hidden = [
+        lax.dynamic_slice_in_dim(inputs, (dp ^ j) * block_rows, block_rows, 1)
+        for j in range(dp_count)
+    ]
 
     landed = [pieces[0][j] for pieces in (key_pieces, value_pieces) for j in range(1, dp_count)]
-    names = [name for name in hidden if name[0]]
-    sent, landed = after([hidden[name] for name in names], *landed)
+    first_rows = moved_rows(block_rows)
+    sent, landed = after([one[:, :first_rows] for one in hidden[1:]], *landed)
     landed = iter(landed)
     for pieces in (key_pieces, value_pieces):
         for j in range(1, dp_count):
             pieces[0][j] = next(landed)
-    swapped = {name: swap(one, "dp", name[0]) for name, one in zip(names, sent)}
-    for side in range(2):
-        swapped[0, side] = hidden[0, side]
-
-    keys = sum(dot32(hidden[j, side], key_pieces[side][j]) for j in range(dp_count) for side in range(2))
-    values = sum(dot32(hidden[j, side], value_pieces[side][j]) for j in range(dp_count) for side in range(2))
-    own = jnp.concatenate([keys.astype(jnp.bfloat16), values.astype(jnp.bfloat16)], axis=1)
+    near = [j for j in range(1, dp_count) if j in bits]
+    far = [j for j in range(1, dp_count) if j not in bits]
+    swapped = {0: hidden[0][:, :first_rows]}
+    swapped.update({j: swap(sent[j - 1], "dp", j) for j in near})
+
+    core_id = jnp.reshape(core, (1,)).astype(jnp.int32)
+    early, late = [], []
+    for which, (pieces, first) in enumerate(((key_pieces, bits[0]), (value_pieces, bits[-1]))):
+        for j in range(dp_count):
+            for side in range(2):
+                (early if j in (0, first) else late).append((which, j, side, pieces[side][j]))
+    partial = project(core_id, None, hidden, early, jnp.float32)
+    own = project(core_id, partial, hidden, late, jnp.bfloat16)
 
     along = [own] + [swap(own, "ctx", 2 * m) for m in range(1, z_count)]
     kv_blocks = []
     for one in along:
         kv_blocks += [one, swap(one, "ctx", 1)]
+
+    ready = kv_blocks + [sent[j - 1] for j in far]
+    ready, ended = after(ready, *[swapped[j] for j in near])
+    kv_blocks = ready[:ctx_count]
+    swapped.update(zip(near, ended))
+    swapped.update({j: swap(one, "dp", j) for j, one in zip(far, ready[ctx_count:])})
 
     me = jnp.reshape(ctx, (1,)).astype(jnp.int32)
     query_grad, keep, send = attention(
@@ -282,26 +390,27 @@
     for m in range(1, z_count):
         kv_grad = kv_grad + swap(chip[m].astype(jnp.bfloat16), "ctx", 2 * m).astype(jnp.float32)
     kv_grad = kv_grad.astype(jnp.bfloat16)
+    (kv_grad,), ended = after([kv_grad], *[swapped[j] for j in far])
+    swapped.update(zip(far, ended))
     grads = [kv_grad] + [swap(kv_grad, "dp", j) for j in range(1, dp_count)]
 
-    z_id = jnp.reshape(z, (1,)).astype(jnp.int32)
-    theirs = weight_rows(
-        z_id, [swapped[j, 1] for j in range(dp_count)], grads, z_count, jnp.bfloat16
-    )
-    from_core = swap(theirs, "ctx", 1)
-    ours = weight_rows(
-        z_id, [swapped[j, 0] for j in range(dp_count)], grads, z_count, jnp.float32
-    )
-    share = half_rows // z_count
-    partial = (ours + from_core.astype(jnp.float32)).reshape(z_count, share, 2 * head_dim)
-    final = partial[0]
-    for m in range(1, z_count):
-        final = final + swap(partial[m].astype(jnp.bfloat16), "ctx", 2 * m).astype(jnp.float32)
-    final = final.astype(jnp.bfloat16)
-    rows = [final] + [swap(final, "ctx", 2 * m) for m in range(1, z_count)]
-    blocks = rows + [swap(one, "ctx", 1) for one in rows]
     ids = jnp.stack([z, core]).astype(jnp.int32)
-    key_rows, value_rows = assemble(ids, blocks, z_count)
+    sub_count = z_count // 2
+    first_half, last_half = first_rows // 2, (block_rows - first_rows) // 2
+    regions = ((0, first_half), (first_rows, last_half))
+
+    groups = [[(j, 0)] for j in range(dp_count)]
+    parts = weight_rows(ids, hidden, [kv_grad], groups, first_rows, last_half, sub_count)
+    key_part, value_part = add_cores(*parts)
+    last = [sum_over_dp(key_part, bits), sum_over_dp(value_part, bits[::-1])]
+
+    moved = [swapped[j] for j in range(dp_count)]
+
+    groups = [[(j, j) for j in range(dp_count)]]
+    first = add_cores(*weight_rows(ids, moved, grads, groups, 0, first_half, sub_count))
+    blocks = sum_along_z(jnp.concatenate(first, axis=1), sub_count)
+    blocks += sum_along_z(jnp.concatenate(last, axis=1), sub_count)
+    key_rows, value_rows = assemble(ids, blocks, sub_count, regions)
     return query_grad[None], key_rows, value_rows
 
 

time: 220 us -> 188 us (0.85)
  waiting for transfers between devices: 134 us -> 105 us
  matrix products: 15.5 us -> 0 us
  Pallas kernels: 17.8 us -> 28.7 us
  starting transfers between devices: 41.6 us -> 36.9 us
  local copies, waits for them, and re-layouts: 8.21 us -> 12.9 us
  other arithmetic: 0.72 us -> 3.17 us
    ppermute x43 -> x45, waiting for transfers between devices: 134 us -> 105 us  [swap(): return lax.ppermute(array, axis, [(i, i ^ distance) for i in range(count)])]
    dot_general x16 -> x0, matrix products: 15.5 us -> none  [dot32(): return jnp.dot(left, right, preferred_element_type=jnp.float32)]
    pallas_call x3 -> x5, Pallas kernels: 8.2 us -> 19.1 us  [the longest x2 8.92 us: project(): pl.pallas_call(functools.partial(project_kernel, plan, side_rows), out_sh...]
    ppermute x43 -> x45, starting transfers between devices: 41.6 us -> 36.9 us  [swap(): return lax.ppermute(array, axis, [(i, i ^ distance) for i in range(count)])]
    unnamed x24 -> x46, local copies, waits for them, and re-layouts: 1.26 us -> 5.04 us
  transfers between devices with their start and end apart: 43 -> 45, of which waited for: 25 -> 23; matrix products, arithmetic and copies ran while one was open for 10% -> 4% of each run, Pallas kernels for 1% -> 6%
where the time goes in v2:
time: 188 us
  waiting for transfers between devices  105 us (56%)
  starting transfers between devices  36.9 us (20%)
  Pallas kernels  28.7 us (15%)
  local copies, waits for them, and re-layouts  12.9 us (7%)
  other arithmetic  3.17 us (2%)
    ppermute x45, waiting for transfers between devices, swap(): return lax.ppermute(array, axis, [(i, i ^ distance) for i in range(count)])  105 us
    ppermute x45, starting transfers between devices, swap(): return lax.ppermute(array, axis, [(i, i ^ distance) for i in range(count)])  36.9 us
    pallas_call x1, Pallas kernels, attention(): pl.pallas_call(functools.partial(attention_kernel, shape), out_shape=(jax...  9.59 us
    pallas_call x2, Pallas kernels, project(): pl.pallas_call(functools.partial(project_kernel, plan, side_rows), out_sh...  8.92 us
    pallas_call x2, Pallas kernels, weight_rows(): pl.pallas_call(functools.partial(weight_kernel, plan), out_shape=(jax.Sha...  7.32 us
    unnamed x46, local copies, waits for them, and re-layouts  5.04 us
  transfers between devices with their start and end apart: 45, of which 23 were waited for; matrix products, arithmetic and copies ran while one was open for 4% of the time, Pallas kernels for 6%

profile of v2, /device:TPU:0, one launch (start us, length us, event | category | flops | bytes accessed | tf_op | source)
XLA Modules:
  0.0 187.6 jit_solution(8140143565784631505)
XLA Ops:
  0.7 2.2 %constant_dynamic-slice_fusion.2 = (bf16[2048,128]{1,0:T(8,128)(2,1)}, bf16[2048,128]{1,0:T(8,128)(2,1)S(1)}) fusion(bf16[4096,128]{1,0:T(8,128)(2,1)} %param.10, s32[]{:T(128)S(6)} %select_n.37, s32[]{:T(128)S(6)} %select_n.36), kind=kLoop, calls=%fused_computation.39 | loop fusion | bytes 2097160 | tf_op jit(solution)/shard_map/dynamic_slice | solution.py:338
  2.8 2.9 %collective-permute-start = (bf16[2048,128]{1,0:T(8,128)(2,1)S(1)}, bf16[2048,128]{1,0:T(8,128)(2,1)S(1)}, u32[]{:S(2)}, u32[]{:S(2)}) collective-permute-start(bf16[2048,128]{1,0:T(8,128)(2,1)S(1)} %get-tuple-element.85.refs_5_), channel_id=1, source_target_pairs={{0,8},{8,0},{16,24},{24,16},{1,9},{9,1},{17,25},{25,17},{2,10},{10... | collective-permute-start | bytes 1572872 | tf_op jit(solution)/shard_map/ppermute | solution.py:21
  6.6 1.5 collective-permute-start.4
  9.6 8.9 %collective-permute-done.refs_7_ = bf16[2048,128]{1,0:T(8,128)(2,1)S(1)} collective-permute-done((bf16[2048,128]{1,0:T(8,128)(2,1)S(1)}, bf16[2048,128]{1,0:T(8,128)(2,1)S(1)}, u32[]{:S(2)}, u32[]{:S(2)}) %collective-permute-start) | collective-permute-done | bytes 524320 | tf_op jit(solution)/shard_map/ppermute | solution.py:21
  18.5 2.1 %collective-permute-start.2 = (bf16[2048,128]{1,0:T(8,128)(2,1)S(1)}, bf16[2048,128]{1,0:T(8,128)(2,1)}, u32[]{:S(2)}, u32[]{:S(2)}) collective-permute-start(bf16[2048,128]{1,0:T(8,128)(2,1)S(1)} %collective-permute-done.refs_7_), channel_id=1, source_target_pairs={{0,16},{8,24},{16,0},{24,8},{1,17},{9,25},{17,1},{25,9},{2,18},{10... | collective-permute-start | bytes 1572872 | tf_op jit(solution)/shard_map/ppermute | solution.py:21
  20.6 0.9 collective-permute-done.4.refs_11_
  22.1 10.7 %collective-permute-done.1.refs_5_ = bf16[2048,128]{1,0:T(8,128)(2,1)} collective-permute-done((bf16[2048,128]{1,0:T(8,128)(2,1)S(1)}, bf16[2048,128]{1,0:T(8,128)(2,1)}, u32[]{:S(2)}, u32[]{:S(2)}) %collective-permute-start.1) | collective-permute-done | bytes 524320 | tf_op jit(solution)/shard_map/ppermute | solution.py:21
  33.3 9.3 %collective-permute-done.2.refs_7_ = bf16[2048,128]{1,0:T(8,128)(2,1)} collective-permute-done((bf16[2048,128]{1,0:T(8,128)(2,1)S(1)}, bf16[2048,128]{1,0:T(8,128)(2,1)}, u32[]{:S(2)}, u32[]{:S(2)}) %collective-permute-start.2) | collective-permute-done | bytes 524320 | tf_op jit(solution)/shard_map/ppermute | solution.py:21
  43.2 3.5 %dynamic-slice_bitcast_fusion = (bf16[192,4096]{1,0:T(8,128)(2,1)S(1)}, bf16[192,4096]{1,0:T(8,128)(2,1)S(1)}, bf16[192,4096]{1,0:T(8,128)(2,1)S(1)}, bf16[192,4096]{1,0:T(8,128)(2,1)S(1)}) fusion(bf16[1,192,16384]{2,1,0:T(8,128)(2,1)} %param.7, s32[]{:T(128)S(6)} %select_n.35, s32[]{:T(128)S(6)} %select_n.33, s32[]{:T(128)S(6)} %select_n.32, s32[]{:T(128)S(6)} %select_n.34), kind=kLoop, calls=%fused_computation.2 | loop fusion | bytes 12582928 | tf_op jit(solution)/shard_map/dynamic_slice | solution.py:346
  47.0 1.0 slice.128
  49.7 1.6 collective-permute-start.20
  51.4 4.2 %project.2.refs_0_ = f32[192,256]{1,0:T(8,128)S(1)} custom-call(s32[1]{0:T(128)} %bitcast.4.core.refs_0_, s32[1]{0:T(128)} %bitcast.4.core.refs_0_, bf16[192,4096]{1,0:T(8,128)(2,1)S(1)} %get-tuple-element.75.refs_1_.refs_0_, bf16[192,4096]{1,0:T(8,128)(2,1)} %copy-done, bf16[192,4096]{1,0:T(8,128)(2,1)} %copy-done.2, bf16[192,4096]{1,0:T(8,128)(2,1)} %copy-done.19, ...), custom_call_target="tpu_custom_call" | custom-call | tf_op jit(solution)/shard_map/project/pallas_call | solution.py:181
  55.6 4.8 %project.3.refs_0_ = bf16[192,256]{1,0:T(8,128)(2,1)S(1)} custom-call(s32[1]{0:T(128)} %bitcast.4.core.refs_0_, f32[192,256]{1,0:T(8,128)S(1)} %project.2.refs_0_, bf16[192,4096]{1,0:T(8,128)(2,1)S(1)} %get-tuple-element.75.refs_1_.refs_0_, bf16[192,4096]{1,0:T(8,128)(2,1)} %copy-done, bf16[192,4096]{1,0:T(8,128)(2,1)} %copy-done.2, ...), custom_call_target="tpu_custom_call" | custom-call | tf_op jit(solution)/shard_map/project/pallas_call | solution.py:181
  60.5 1.6 collective-permute-start.13
  62.1 2.6 %collective-permute-start.15 = (bf16[192,256]{1,0:T(8,128)(2,1)S(1)}, bf16[192,256]{1,0:T(8,128)(2,1)S(1)}, u32[]{:S(2)}, u32[]{:S(2)}) collective-permute-start(bf16[192,256]{1,0:T(8,128)(2,1)S(1)} %project.3.refs_0_), channel_id=1, source_target_pairs={{0,4},{1,5},{2,6},{3,7},{4,0},{5,1},{6,2},{7,3},{8,12},{9,13},{10,... | collective-permute-start | bytes 294920 | tf_op jit(solution)/shard_map/ppermute | solution.py:21
  65.7 7.2 %collective-permute-done.15.refs_4_ = bf16[192,256]{1,0:T(8,128)(2,1)S(1)} collective-permute-done((bf16[192,256]{1,0:T(8,128)(2,1)S(1)}, bf16[192,256]{1,0:T(8,128)(2,1)S(1)}, u32[]{:S(2)}, u32[]{:S(2)}) %collective-permute-start.15) | collective-permute-done | bytes 98336 | tf_op jit(solution)/shard_map/ppermute | solution.py:21
  74.4 9.6 %attention.1 = (bf16[192,1024]{1,0:T(8,128)(2,1)}, f32[768,256]{1,0:T(8,128)S(1)}, bf16[768,256]{1,0:T(8,128)(2,1)S(1)}) custom-call(s32[1]{0:T(128)} %bitcast.ids, s32[16]{0:T(128)S(1)} %copy-done.17, s32[8]{0:T(128)S(1)} %bitcast.17, bf16[192,1024]{1,0:T(8,128)(2,1)S(1)} %bitcast.15, bf16[192,1024]{1,0:T(8,128)(2,1)S(1)} %bitcast.16, ...), custom_call_target="tpu_custom_call" | custom-call | tf_op jit(solution)/shard_map/attention/pallas_call | solution.py:130
  84.0 0.9 copy-done.10
  85.3 1.4 collective-permute-start.25
  86.8 1.3 fusion.16
  88.1 2.6 %collective-permute-start.24 = (bf16[192,256]{1,0:T(8,128)(2,1)S(1)}, bf16[192,256]{1,0:T(8,128)(2,1)S(1)}, u32[]{:S(2)}, u32[]{:S(2)}) collective-permute-start(bf16[192,256]{1,0:T(8,128)(2,1)S(1)} %get-tuple-element.87), channel_id=1, source_target_pairs={{0,6},{1,7},{2,4},{3,5},{4,2},{5,3},{6,0},{7,1},{8,14},{9,15},{10,... | collective-permute-start | bytes 294920 | tf_op jit(solution)/shard_map/ppermute | solution.py:21
  91.4 1.2 collective-permute-start.22
  92.7 3.0 %collective-permute-done.24 = bf16[192,256]{1,0:T(8,128)(2,1)S(1)} collective-permute-done((bf16[192,256]{1,0:T(8,128)(2,1)S(1)}, bf16[192,256]{1,0:T(8,128)(2,1)S(1)}, u32[]{:S(2)}, u32[]{:S(2)}) %collective-permute-start.24) | collective-permute-done | bytes 98336 | tf_op jit(solution)/shard_map/ppermute | solution.py:21
  95.7 4.8 %collective-permute-done.23 = bf16[192,256]{1,0:T(8,128)(2,1)S(1)} collective-permute-done((bf16[192,256]{1,0:T(8,128)(2,1)S(1)}, bf16[192,256]{1,0:T(8,128)(2,1)S(1)}, u32[]{:S(2)}, u32[]{:S(2)}) %collective-permute-start.23) | collective-permute-done | bytes 98336 | tf_op jit(solution)/shard_map/ppermute | solution.py:21
  100.6 5.4 %collective-permute-done.25.refs_3_ = bf16[192,2048]{1,0:T(8,128)(2,1)S(1)} collective-permute-done((bf16[192,2048]{1,0:T(8,128)(2,1)}, bf16[192,2048]{1,0:T(8,128)(2,1)S(1)}, u32[]{:S(2)}, u32[]{:S(2)}) %collective-permute-start.25) | collective-permute-done | bytes 786464 | tf_op jit(solution)/shard_map/ppermute | solution.py:21
  106.0 5.4 %weight_rows.3 = (bf16[4096,256]{1,0:T(8,128)(2,1)}, f32[4096,128]{1,0:T(8,128)}, f32[4096,128]{1,0:T(8,128)}) custom-call(s32[2]{0:T(128)S(1)} %pad_add_fusion.ids, bf16[192,4096]{1,0:T(8,128)(2,1)S(1)} %get-tuple-element.75.refs_1_.refs_0_, bf16[192,4096]{1,0:T(8,128)(2,1)S(1)} %copy-done.1, bf16[192,4096]{1,0:T(8,128)(2,1)S(1)} %copy-done.3, ...), custom_call_target="tpu_custom_call" | custom-call | tf_op jit(solution)/shard_map/weight_rows/pallas_call | solution.py:240
  111.3 1.6 collective-permute-start.26
  113.4 1.5 collective-permute-start.28
  115.0 1.6 collective-permute-done.26.refs_5_
  116.6 3.3 %collective-permute-done.27.refs_6_ = bf16[192,256]{1,0:T(8,128)(2,1)S(1)} collective-permute-done((bf16[192,256]{1,0:T(8,128)(2,1)S(1)}, bf16[192,256]{1,0:T(8,128)(2,1)S(1)}, u32[]{:S(2)}, u32[]{:S(2)}) %collective-permute-start.27) | collective-permute-done | bytes 98336 | tf_op jit(solution)/shard_map/ppermute | solution.py:21
  119.9 2.0 %weight_rows.2 = (bf16[1024,256]{1,0:T(8,128)(2,1)S(1)}, f32[1024,128]{1,0:T(8,128)S(1)}, f32[1024,128]{1,0:T(8,128)S(1)}) custom-call(s32[2]{0:T(128)S(1)} %pad_add_fusion.ids, bf16[192,2048]{1,0:T(8,128)(2,1)S(1)} %slice.129.refs_0_, bf16[192,2048]{1,0:T(8,128)(2,1)S(1)} %copy-done.12, bf16[192,2048]{1,0:T(8,128)(2,1)S(1)} %copy-done.14, ...), custom_call_target="tpu_custom_call" | custom-call | tf_op jit(solution)/shard_map/weight_rows/pallas_call | solution.py:240
  121.9 1.9 %collective-permute-done.29 = bf16[1024,256]{1,0:T(8,128)(2,1)S(1)} collective-permute-done((bf16[1024,256]{1,0:T(8,128)(2,1)S(1)}, bf16[1024,256]{1,0:T(8,128)(2,1)S(1)}, u32[]{:S(2)}, u32[]{:S(2)}) %collective-permute-start.29) | collective-permute-done | bytes 524320 | tf_op jit(solution)/shard_map/ppermute | solution.py:21
  124.3 1.2 copy-done.20
  127.4 1.2 collective-permute-start.36
  128.7 12.0 %collective-permute-done.38 = bf16[2048,128]{1,0:T(8,128)(2,1)S(1)} collective-permute-done((bf16[2048,128]{1,0:T(8,128)(2,1)S(1)}, bf16[2048,128]{1,0:T(8,128)(2,1)S(1)}, u32[]{:S(2)}, u32[]{:S(2)}) %collective-permute-start.38) | collective-permute-done | bytes 524320 | tf_op jit(solution)/shard_map/ppermute | solution.py:21
  141.5 1.8 collective-permute-start.30
  143.4 1.3 collective-permute-start.37
  144.7 3.7 %collective-permute-done.39 = bf16[1024,128]{1,0:T(8,128)(2,1)S(1)} collective-permute-done((bf16[1024,128]{1,0:T(8,128)(2,1)S(1)}, bf16[1024,128]{1,0:T(8,128)(2,1)S(1)}, u32[]{:S(2)}, u32[]{:S(2)}) %collective-permute-start.39) | collective-permute-done | bytes 262176 | tf_op jit(solution)/shard_map/ppermute | solution.py:21
  148.5 1.9 %collective-permute-done.37 = bf16[1024,128]{1,0:T(8,128)(2,1)S(1)} collective-permute-done((bf16[1024,128]{1,0:T(8,128)(2,1)S(1)}, bf16[1024,128]{1,0:T(8,128)(2,1)S(1)}, u32[]{:S(2)}, u32[]{:S(2)}) %collective-permute-start.37) | collective-permute-done | bytes 262176 | tf_op jit(solution)/shard_map/ppermute | solution.py:21
  151.0 2.8 %collective-permute-start.31 = (bf16[512,256]{1,0:T(8,128)(2,1)S(1)}, bf16[512,256]{1,0:T(8,128)(2,1)S(1)}, u32[]{:S(2)}, u32[]{:S(2)}) collective-permute-start(bf16[512,256]{1,0:T(8,128)(2,1)S(1)} %fusion.13), channel_id=1, source_target_pairs={{0,4},{1,5},{2,6},{3,7},{4,0},{5,1},{6,2},{7,3},{8,12},{9,13},{10,... | collective-permute-start | bytes 786440 | tf_op jit(solution)/shard_map/ppermute | solution.py:21
  153.8 8.1 %collective-permute-done.40 = bf16[512,256]{1,0:T(8,128)(2,1)S(1)} collective-permute-done((bf16[512,256]{1,0:T(8,128)(2,1)S(1)}, bf16[512,256]{1,0:T(8,128)(2,1)S(1)}, u32[]{:S(2)}, u32[]{:S(2)}) %collective-permute-start.40) | collective-permute-done | bytes 262176 | tf_op jit(solution)/shard_map/ppermute | solution.py:21
  162.1 5.6 %collective-permute-done.31 = bf16[512,256]{1,0:T(8,128)(2,1)S(1)} collective-permute-done((bf16[512,256]{1,0:T(8,128)(2,1)S(1)}, bf16[512,256]{1,0:T(8,128)(2,1)S(1)}, u32[]{:S(2)}, u32[]{:S(2)}) %collective-permute-start.31) | collective-permute-done | bytes 262176 | tf_op jit(solution)/shard_map/ppermute | solution.py:21
  167.8 1.1 collective-permute-start.32
  168.9 5.9 %collective-permute-done.41 = bf16[512,256]{1,0:T(8,128)(2,1)S(1)} collective-permute-done((bf16[512,256]{1,0:T(8,128)(2,1)S(1)}, bf16[512,256]{1,0:T(8,128)(2,1)S(1)}, u32[]{:S(2)}, u32[]{:S(2)}) %collective-permute-start.41) | collective-permute-done | bytes 262176 | tf_op jit(solution)/shard_map/ppermute | solution.py:21
  175.1 2.6 %collective-permute-done.32.refs_1_ = bf16[512,256]{1,0:T(8,128)(2,1)S(1)} collective-permute-done((bf16[512,256]{1,0:T(8,128)(2,1)S(1)}, bf16[512,256]{1,0:T(8,128)(2,1)S(1)}, u32[]{:S(2)}, u32[]{:S(2)}) %collective-permute-start.32) | collective-permute-done | bytes 262176 | tf_op jit(solution)/shard_map/ppermute | solution.py:21
  178.2 5.0 %collective-permute-done.42.refs_5_ = bf16[512,256]{1,0:T(8,128)(2,1)S(1)} collective-permute-done((bf16[512,256]{1,0:T(8,128)(2,1)S(1)}, bf16[512,256]{1,0:T(8,128)(2,1)S(1)}, u32[]{:S(2)}, u32[]{:S(2)}) %collective-permute-start.42) | collective-permute-done | bytes 262176 | tf_op jit(solution)/shard_map/ppermute | solution.py:21
  183.2 1.5 collective-permute-done.44.refs_7_
  184.7 2.8 %assemble.1 = (f32[4096,128]{1,0:T(8,128)}, f32[4096,128]{1,0:T(8,128)}) custom-call(s32[2]{0:T(128)S(1)} %pad_add_fusion.ids, bf16[512,256]{1,0:T(8,128)(2,1)S(1)} %add_convert_fusion.1.refs_0_, bf16[512,256]{1,0:T(8,128)(2,1)S(1)} %collective-permute-done.32.refs_1_, bf16[512,256]{1,0:T(8,128)(2,1)S(1)} %collective-permute-done.33.refs_2_, ...), custom_call_target="tpu_custom_call" | custom-call | tf_op jit(solution)/shard_map/assemble/pallas_call | solution.py:272
  (124 shorter events, 15.2 us)
Async XLA Ops:
  2.8 40.3 %copy-start.5 = (bf16[2048,128]{1,0:T(8,128)(2,1)}, bf16[2048,128]{1,0:T(8,128)(2,1)S(1)}, u32[]{:S(2)}) copy-start(bf16[2048,128]{1,0:T(8,128)(2,1)S(1)} %get-tuple-element.85.refs_5_) | copy-start | bytes 1572868
  2.8 15.7 %collective-permute-start = (bf16[2048,128]{1,0:T(8,128)(2,1)S(1)}, bf16[2048,128]{1,0:T(8,128)(2,1)S(1)}, u32[]{:S(2)}, u32[]{:S(2)}) collective-permute-start(bf16[2048,128]{1,0:T(8,128)(2,1)S(1)} %get-tuple-element.85.refs_5_), channel_id=1, source_target_pairs={{0,8},{8,0},{16,24},{24,16},{1,9},{9,1},{17,25},{25,17},{2,10},{10... | collective-permute-start | bytes 1572872 | tf_op jit(solution)/shard_map/ppermute | solution.py:21
  6.6 14.8 %collective-permute-start.4 = (bf16[2048,128]{1,0:T(8,128)(2,1)S(1)}, bf16[2048,128]{1,0:T(8,128)(2,1)S(1)}, u32[]{:S(2)}, u32[]{:S(2)}) collective-permute-start(bf16[2048,128]{1,0:T(8,128)(2,1)S(1)} %get-tuple-element.83.refs_9_), channel_id=1, source_target_pairs={{0,16},{8,24},{16,0},{24,8},{1,17},{9,25},{17,1},{25,9},{2,18},{10... | collective-permute-start | bytes 1572872 | tf_op jit(solution)/shard_map/ppermute | solution.py:21
  8.2 24.7 %collective-permute-start.1 = (bf16[2048,128]{1,0:T(8,128)(2,1)S(1)}, bf16[2048,128]{1,0:T(8,128)(2,1)}, u32[]{:S(2)}, u32[]{:S(2)}) collective-permute-start(bf16[2048,128]{1,0:T(8,128)(2,1)S(1)} %get-tuple-element.85.refs_5_), channel_id=1, source_target_pairs={{0,16},{8,24},{16,0},{24,8},{1,17},{9,25},{17,1},{25,9},{2,18},{10... | collective-permute-start | bytes 1572872 | tf_op jit(solution)/shard_map/ppermute | solution.py:21
  8.7 24.2 %collective-permute-start.3 = (bf16[2048,128]{1,0:T(8,128)(2,1)S(1)}, bf16[2048,128]{1,0:T(8,128)(2,1)}, u32[]{:S(2)}, u32[]{:S(2)}) collective-permute-start(bf16[2048,128]{1,0:T(8,128)(2,1)S(1)} %get-tuple-element.83.refs_9_), channel_id=1, source_target_pairs={{0,8},{8,0},{16,24},{24,16},{1,9},{9,1},{17,25},{25,17},{2,10},{10... | collective-permute-start | bytes 1572872 | tf_op jit(solution)/shard_map/ppermute | solution.py:21
  18.5 24.1 %collective-permute-start.2 = (bf16[2048,128]{1,0:T(8,128)(2,1)S(1)}, bf16[2048,128]{1,0:T(8,128)(2,1)}, u32[]{:S(2)}, u32[]{:S(2)}) collective-permute-start(bf16[2048,128]{1,0:T(8,128)(2,1)S(1)} %collective-permute-done.refs_7_), channel_id=1, source_target_pairs={{0,16},{8,24},{16,0},{24,8},{1,17},{9,25},{17,1},{25,9},{2,18},{10... | collective-permute-start | bytes 1572872 | tf_op jit(solution)/shard_map/ppermute | solution.py:21
  21.5 21.1 %collective-permute-start.5 = (bf16[2048,128]{1,0:T(8,128)(2,1)S(1)}, bf16[2048,128]{1,0:T(8,128)(2,1)}, u32[]{:S(2)}, u32[]{:S(2)}) collective-permute-start(bf16[2048,128]{1,0:T(8,128)(2,1)S(1)} %collective-permute-done.4.refs_11_), channel_id=1, source_target_pairs={{0,8},{8,0},{16,24},{24,16},{1,9},{9,1},{17,25},{25,17},{2,10},{10... | collective-permute-start | bytes 1572872 | tf_op jit(solution)/shard_map/ppermute | solution.py:21
  22.1 21.0 %collective-permute-start.6 = (bf16[2048,128]{1,0:T(8,128)(2,1)S(1)}, bf16[2048,128]{1,0:T(8,128)(2,1)S(1)}, u32[]{:S(2)}, u32[]{:S(2)}) collective-permute-start(bf16[2048,128]{1,0:T(8,128)(2,1)S(1)} %collective-permute-done.refs_7_), channel_id=1, source_target_pairs={{0,1},{1,0},{2,3},{3,2},{4,5},{5,4},{6,7},{7,6},{8,9},{9,8},{10,11... | collective-permute-start | bytes 1572872 | tf_op jit(solution)/shard_map/ppermute | solution.py:21
  32.8 16.5 %collective-permute-start.7 = (bf16[2048,128]{1,0:T(8,128)(2,1)S(1)}, bf16[2048,128]{1,0:T(8,128)(2,1)S(1)}, u32[]{:S(2)}, u32[]{:S(2)}) collective-permute-start(bf16[2048,128]{1,0:T(8,128)(2,1)S(1)} %collective-permute-done.4.refs_11_), channel_id=1, source_target_pairs={{0,1},{1,0},{2,3},{3,2},{4,5},{5,4},{6,7},{7,6},{8,9},{9,8},{10,11... | collective-permute-start | bytes 1572872 | tf_op jit(solution)/shard_map/ppermute | solution.py:21
  32.8 16.9 %collective-permute-start.8 = (bf16[2048,128]{1,0:T(8,128)(2,1)}, bf16[2048,128]{1,0:T(8,128)(2,1)S(1)}, u32[]{:S(2)}, u32[]{:S(2)}) collective-permute-start(bf16[2048,128]{1,0:T(8,128)(2,1)} %collective-permute-done.1.refs_5_), channel_id=1, source_target_pairs={{0,1},{1,0},{2,3},{3,2},{4,5},{5,4},{6,7},{7,6},{8,9},{9,8},{10,11... | collective-permute-start | bytes 1572872 | tf_op jit(solution)/shard_map/ppermute | solution.py:21
  42.6 13.0 %collective-permute-start.10 = (bf16[2048,128]{1,0:T(8,128)(2,1)}, bf16[2048,128]{1,0:T(8,128)(2,1)S(1)}, u32[]{:S(2)}, u32[]{:S(2)}) collective-permute-start(bf16[2048,128]{1,0:T(8,128)(2,1)} %collective-permute-done.3.refs_9_), channel_id=1, source_target_pairs={{0,1},{1,0},{2,3},{3,2},{4,5},{5,4},{6,7},{7,6},{8,9},{9,8},{10,11... | collective-permute-start | bytes 1572872 | tf_op jit(solution)/shard_map/ppermute | solution.py:21
  42.6 13.0 %collective-permute-start.9 = (bf16[2048,128]{1,0:T(8,128)(2,1)}, bf16[2048,128]{1,0:T(8,128)(2,1)S(1)}, u32[]{:S(2)}, u32[]{:S(2)}) collective-permute-start(bf16[2048,128]{1,0:T(8,128)(2,1)} %collective-permute-done.2.refs_7_), channel_id=1, source_target_pairs={{0,1},{1,0},{2,3},{3,2},{4,5},{5,4},{6,7},{7,6},{8,9},{9,8},{10,11... | collective-permute-start | bytes 1572872 | tf_op jit(solution)/shard_map/ppermute | solution.py:21
  43.1 12.5 %collective-permute-start.11 = (bf16[2048,128]{1,0:T(8,128)(2,1)}, bf16[2048,128]{1,0:T(8,128)(2,1)S(1)}, u32[]{:S(2)}, u32[]{:S(2)}) collective-permute-start(bf16[2048,128]{1,0:T(8,128)(2,1)} %collective-permute-done.5.refs_11_), channel_id=1, source_target_pairs={{0,1},{1,0},{2,3},{3,2},{4,5},{5,4},{6,7},{7,6},{8,9},{9,8},{10,11... | collective-permute-start | bytes 1572872 | tf_op jit(solution)/shard_map/ppermute | solution.py:21
  49.3 25.0 %collective-permute-start.19 = (bf16[192,2048]{1,0:T(8,128)(2,1)S(1)}, bf16[192,2048]{1,0:T(8,128)(2,1)S(1)}, u32[]{:S(2)}, u32[]{:S(2)}) collective-permute-start(bf16[192,2048]{1,0:T(8,128)(2,1)S(1)} %slice.126), channel_id=1, source_target_pairs={{0,8},{8,0},{16,24},{24,16},{1,9},{9,1},{17,25},{25,17},{2,10},{10... | collective-permute-start | bytes 2359304 | tf_op jit(solution)/shard_map/ppermute | solution.py:21
  49.7 24.6 %collective-permute-start.20 = (bf16[192,2048]{1,0:T(8,128)(2,1)S(1)}, bf16[192,2048]{1,0:T(8,128)(2,1)S(1)}, u32[]{:S(2)}, u32[]{:S(2)}) collective-permute-start(bf16[192,2048]{1,0:T(8,128)(2,1)S(1)} %slice.127), channel_id=1, source_target_pairs={{0,16},{8,24},{16,0},{24,8},{1,17},{9,25},{17,1},{25,9},{2,18},{10... | collective-permute-start | bytes 2359304 | tf_op jit(solution)/shard_map/ppermute | solution.py:21
  60.4 4.3 %collective-permute-start.12 = (bf16[192,256]{1,0:T(8,128)(2,1)S(1)}, bf16[192,256]{1,0:T(8,128)(2,1)S(1)}, u32[]{:S(2)}, u32[]{:S(2)}) collective-permute-start(bf16[192,256]{1,0:T(8,128)(2,1)S(1)} %project.3.refs_0_), channel_id=1, source_target_pairs={{0,1},{1,0},{2,3},{3,2},{4,5},{5,4},{6,7},{7,6},{8,9},{9,8},{10,11... | collective-permute-start | bytes 294920 | tf_op jit(solution)/shard_map/ppermute | solution.py:21
  60.5 5.2 %collective-permute-start.13 = (bf16[192,256]{1,0:T(8,128)(2,1)S(1)}, bf16[192,256]{1,0:T(8,128)(2,1)S(1)}, u32[]{:S(2)}, u32[]{:S(2)}) collective-permute-start(bf16[192,256]{1,0:T(8,128)(2,1)S(1)} %project.3.refs_0_), channel_id=1, source_target_pairs={{0,2},{1,3},{2,0},{3,1},{4,6},{5,7},{6,4},{7,5},{8,10},{9,11},{10,... | collective-permute-start | bytes 294920 | tf_op jit(solution)/shard_map/ppermute | solution.py:21
  62.1 10.8 %collective-permute-start.15 = (bf16[192,256]{1,0:T(8,128)(2,1)S(1)}, bf16[192,256]{1,0:T(8,128)(2,1)S(1)}, u32[]{:S(2)}, u32[]{:S(2)}) collective-permute-start(bf16[192,256]{1,0:T(8,128)(2,1)S(1)} %project.3.refs_0_), channel_id=1, source_target_pairs={{0,4},{1,5},{2,6},{3,7},{4,0},{5,1},{6,2},{7,3},{8,12},{9,13},{10,... | collective-permute-start | bytes 294920 | tf_op jit(solution)/shard_map/ppermute | solution.py:21
  64.7 8.2 %collective-permute-start.17 = (bf16[192,256]{1,0:T(8,128)(2,1)S(1)}, bf16[192,256]{1,0:T(8,128)(2,1)S(1)}, u32[]{:S(2)}, u32[]{:S(2)}) collective-permute-start(bf16[192,256]{1,0:T(8,128)(2,1)S(1)} %project.3.refs_0_), channel_id=1, source_target_pairs={{0,6},{1,7},{2,4},{3,5},{4,2},{5,3},{6,0},{7,1},{8,14},{9,15},{10,... | collective-permute-start | bytes 294920 | tf_op jit(solution)/shard_map/ppermute | solution.py:21
  65.7 7.7 %collective-permute-start.14 = (bf16[192,256]{1,0:T(8,128)(2,1)S(1)}, bf16[192,256]{1,0:T(8,128)(2,1)S(1)}, u32[]{:S(2)}, u32[]{:S(2)}) collective-permute-start(bf16[192,256]{1,0:T(8,128)(2,1)S(1)} %collective-permute-done.13.refs_2_), channel_id=1, source_target_pairs={{0,1},{1,0},{2,3},{3,2},{4,5},{5,4},{6,7},{7,6},{8,9},{9,8},{10,11... | collective-permute-start | bytes 294920 | tf_op jit(solution)/shard_map/ppermute | solution.py:21
  72.9 1.3 collective-permute-start.16
  72.9 1.5 collective-permute-start.18
  84.9 21.1 %copy-start.1 = (bf16[192,4096]{1,0:T(8,128)(2,1)S(1)}, bf16[192,4096]{1,0:T(8,128)(2,1)}, u32[]{:S(2)}) copy-start(bf16[192,4096]{1,0:T(8,128)(2,1)} %copy-done) | copy-start | bytes 4718596
  84.9 1.9 collective-permute-start.21
  85.3 20.7 %copy-start.3 = (bf16[192,4096]{1,0:T(8,128)(2,1)S(1)}, bf16[192,4096]{1,0:T(8,128)(2,1)}, u32[]{:S(2)}) copy-start(bf16[192,4096]{1,0:T(8,128)(2,1)} %copy-done.2) | copy-start | bytes 4718596
  85.3 20.7 %collective-permute-start.25 = (bf16[192,2048]{1,0:T(8,128)(2,1)}, bf16[192,2048]{1,0:T(8,128)(2,1)S(1)}, u32[]{:S(2)}, u32[]{:S(2)}) collective-permute-start(bf16[192,2048]{1,0:T(8,128)(2,1)} %slice.128), channel_id=1, source_target_pairs={{0,24},{8,16},{16,8},{24,0},{1,25},{9,17},{17,9},{25,1},{2,26},{10... | collective-permute-start | bytes 2359304 | tf_op jit(solution)/shard_map/ppermute | solution.py:21
  88.1 7.6 %collective-permute-start.24 = (bf16[192,256]{1,0:T(8,128)(2,1)S(1)}, bf16[192,256]{1,0:T(8,128)(2,1)S(1)}, u32[]{:S(2)}, u32[]{:S(2)}) collective-permute-start(bf16[192,256]{1,0:T(8,128)(2,1)S(1)} %get-tuple-element.87), channel_id=1, source_target_pairs={{0,6},{1,7},{2,4},{3,5},{4,2},{5,3},{6,0},{7,1},{8,14},{9,15},{10,... | collective-permute-start | bytes 294920 | tf_op jit(solution)/shard_map/ppermute | solution.py:21
  90.7 9.8 %collective-permute-start.23 = (bf16[192,256]{1,0:T(8,128)(2,1)S(1)}, bf16[192,256]{1,0:T(8,128)(2,1)S(1)}, u32[]{:S(2)}, u32[]{:S(2)}) collective-permute-start(bf16[192,256]{1,0:T(8,128)(2,1)S(1)} %get-tuple-element.88), channel_id=1, source_target_pairs={{0,4},{1,5},{2,6},{3,7},{4,0},{5,1},{6,2},{7,3},{8,12},{9,13},{10,... | collective-permute-start | bytes 294920 | tf_op jit(solution)/shard_map/ppermute | solution.py:21
  91.4 9.1 %collective-permute-start.22 = (bf16[192,256]{1,0:T(8,128)(2,1)S(1)}, bf16[192,256]{1,0:T(8,128)(2,1)S(1)}, u32[]{:S(2)}, u32[]{:S(2)}) collective-permute-start(bf16[192,256]{1,0:T(8,128)(2,1)S(1)} %get-tuple-element.86), channel_id=1, source_target_pairs={{0,2},{1,3},{2,0},{3,1},{4,6},{5,7},{6,4},{7,5},{8,10},{9,11},{10,... | collective-permute-start | bytes 294920 | tf_op jit(solution)/shard_map/ppermute | solution.py:21
  111.3 12.6 %collective-permute-start.35 = (bf16[4096,256]{1,0:T(8,128)(2,1)}, bf16[4096,256]{1,0:T(8,128)(2,1)S(1)}, u32[]{:S(2)}, u32[]{:S(2)}) collective-permute-start(bf16[4096,256]{1,0:T(8,128)(2,1)} %get-tuple-element.65), channel_id=1, source_target_pairs={{0,1},{1,0},{2,3},{3,2},{4,5},{5,4},{6,7},{7,6},{8,9},{9,8},{10,11... | collective-permute-start | bytes 6291464 | tf_op jit(solution)/shard_map/ppermute | solution.py:21
  111.3 5.2 %collective-permute-start.26 = (bf16[192,256]{1,0:T(8,128)(2,1)S(1)}, bf16[192,256]{1,0:T(8,128)(2,1)S(1)}, u32[]{:S(2)}, u32[]{:S(2)}) collective-permute-start(bf16[192,256]{1,0:T(8,128)(2,1)S(1)} %fusion.12.refs_4_), channel_id=1, source_target_pairs={{0,8},{8,0},{16,24},{24,16},{1,9},{9,1},{17,25},{25,17},{2,10},{10... | collective-permute-start | bytes 294920 | tf_op jit(solution)/shard_map/ppermute | solution.py:21
  112.9 7.0 %collective-permute-start.27 = (bf16[192,256]{1,0:T(8,128)(2,1)S(1)}, bf16[192,256]{1,0:T(8,128)(2,1)S(1)}, u32[]{:S(2)}, u32[]{:S(2)}) collective-permute-start(bf16[192,256]{1,0:T(8,128)(2,1)S(1)} %fusion.12.refs_4_), channel_id=1, source_target_pairs={{0,16},{8,24},{16,0},{24,8},{1,17},{9,25},{17,1},{25,9},{2,18},{10... | collective-permute-start | bytes 294920 | tf_op jit(solution)/shard_map/ppermute | solution.py:21
  113.4 6.5 %collective-permute-start.28 = (bf16[192,256]{1,0:T(8,128)(2,1)S(1)}, bf16[192,256]{1,0:T(8,128)(2,1)S(1)}, u32[]{:S(2)}, u32[]{:S(2)}) collective-permute-start(bf16[192,256]{1,0:T(8,128)(2,1)S(1)} %fusion.12.refs_4_), channel_id=1, source_target_pairs={{0,24},{8,16},{16,8},{24,0},{1,25},{9,17},{17,9},{25,1},{2,26},{10... | collective-permute-start | bytes 294920 | tf_op jit(solution)/shard_map/ppermute | solution.py:21
  121.9 2.0 %collective-permute-start.29 = (bf16[1024,256]{1,0:T(8,128)(2,1)S(1)}, bf16[1024,256]{1,0:T(8,128)(2,1)S(1)}, u32[]{:S(2)}, u32[]{:S(2)}) collective-permute-start(bf16[1024,256]{1,0:T(8,128)(2,1)S(1)} %get-tuple-element.62), channel_id=1, source_target_pairs={{0,1},{1,0},{2,3},{3,2},{4,5},{5,4},{6,7},{7,6},{8,9},{9,8},{10,11... | collective-permute-start | bytes 1572872 | tf_op jit(solution)/shard_map/ppermute | solution.py:21
  126.7 14.0 %collective-permute-start.38 = (bf16[2048,128]{1,0:T(8,128)(2,1)S(1)}, bf16[2048,128]{1,0:T(8,128)(2,1)S(1)}, u32[]{:S(2)}, u32[]{:S(2)}) collective-permute-start(bf16[2048,128]{1,0:T(8,128)(2,1)S(1)} %slice.213), channel_id=1, source_target_pairs={{0,16},{8,24},{16,0},{24,8},{1,17},{9,25},{17,1},{25,9},{2,18},{10... | collective-permute-start | bytes 1572872 | tf_op jit(solution)/shard_map/ppermute | solution.py:21
  127.4 15.9 %collective-permute-start.36 = (bf16[2048,128]{1,0:T(8,128)(2,1)S(1)}, bf16[2048,128]{1,0:T(8,128)(2,1)S(1)}, u32[]{:S(2)}, u32[]{:S(2)}) collective-permute-start(bf16[2048,128]{1,0:T(8,128)(2,1)S(1)} %pad_maximum_fusion.2), channel_id=1, source_target_pairs={{0,8},{8,0},{16,24},{24,16},{1,9},{9,1},{17,25},{25,17},{2,10},{10... | collective-permute-start | bytes 1572872 | tf_op jit(solution)/shard_map/ppermute | solution.py:21
  140.9 7.6 %collective-permute-start.39 = (bf16[1024,128]{1,0:T(8,128)(2,1)S(1)}, bf16[1024,128]{1,0:T(8,128)(2,1)S(1)}, u32[]{:S(2)}, u32[]{:S(2)}) collective-permute-start(bf16[1024,128]{1,0:T(8,128)(2,1)S(1)} %fusion.5), channel_id=1, source_target_pairs={{0,8},{8,0},{16,24},{24,16},{1,9},{9,1},{17,25},{25,17},{2,10},{10... | collective-permute-start | bytes 786440 | tf_op jit(solution)/shard_map/ppermute | solution.py:21
  141.5 9.5 %collective-permute-start.30 = (bf16[512,256]{1,0:T(8,128)(2,1)S(1)}, bf16[512,256]{1,0:T(8,128)(2,1)S(1)}, u32[]{:S(2)}, u32[]{:S(2)}) collective-permute-start(bf16[512,256]{1,0:T(8,128)(2,1)S(1)} %fusion.9), channel_id=1, source_target_pairs={{0,2},{1,3},{2,0},{3,1},{4,6},{5,7},{6,4},{7,5},{8,10},{9,11},{10,... | collective-permute-start | bytes 786440 | tf_op jit(solution)/shard_map/ppermute | solution.py:21
  143.4 7.0 %collective-permute-start.37 = (bf16[1024,128]{1,0:T(8,128)(2,1)S(1)}, bf16[1024,128]{1,0:T(8,128)(2,1)S(1)}, u32[]{:S(2)}, u32[]{:S(2)}) collective-permute-start(bf16[1024,128]{1,0:T(8,128)(2,1)S(1)} %fusion.7), channel_id=1, source_target_pairs={{0,16},{8,24},{16,0},{24,8},{1,17},{9,25},{17,1},{25,9},{2,18},{10... | collective-permute-start | bytes 786440 | tf_op jit(solution)/shard_map/ppermute | solution.py:21
  150.6 11.4 %collective-permute-start.40 = (bf16[512,256]{1,0:T(8,128)(2,1)S(1)}, bf16[512,256]{1,0:T(8,128)(2,1)S(1)}, u32[]{:S(2)}, u32[]{:S(2)}) collective-permute-start(bf16[512,256]{1,0:T(8,128)(2,1)S(1)} %fusion.4), channel_id=1, source_target_pairs={{0,2},{1,3},{2,0},{3,1},{4,6},{5,7},{6,4},{7,5},{8,10},{9,11},{10,... | collective-permute-start | bytes 786440 | tf_op jit(solution)/shard_map/ppermute | solution.py:21
  151.0 16.7 %collective-permute-start.31 = (bf16[512,256]{1,0:T(8,128)(2,1)S(1)}, bf16[512,256]{1,0:T(8,128)(2,1)S(1)}, u32[]{:S(2)}, u32[]{:S(2)}) collective-permute-start(bf16[512,256]{1,0:T(8,128)(2,1)S(1)} %fusion.13), channel_id=1, source_target_pairs={{0,4},{1,5},{2,6},{3,7},{4,0},{5,1},{6,2},{7,3},{8,12},{9,13},{10,... | collective-permute-start | bytes 786440 | tf_op jit(solution)/shard_map/ppermute | solution.py:21
  162.0 12.9 %collective-permute-start.41 = (bf16[512,256]{1,0:T(8,128)(2,1)S(1)}, bf16[512,256]{1,0:T(8,128)(2,1)S(1)}, u32[]{:S(2)}, u32[]{:S(2)}) collective-permute-start(bf16[512,256]{1,0:T(8,128)(2,1)S(1)} %fusion.14), channel_id=1, source_target_pairs={{0,4},{1,5},{2,6},{3,7},{4,0},{5,1},{6,2},{7,3},{8,12},{9,13},{10,... | collective-permute-start | bytes 786440 | tf_op jit(solution)/shard_map/ppermute | solution.py:21
  167.8 9.9 %collective-permute-start.32 = (bf16[512,256]{1,0:T(8,128)(2,1)S(1)}, bf16[512,256]{1,0:T(8,128)(2,1)S(1)}, u32[]{:S(2)}, u32[]{:S(2)}) collective-permute-start(bf16[512,256]{1,0:T(8,128)(2,1)S(1)} %add_convert_fusion.1.refs_0_), channel_id=1, source_target_pairs={{0,2},{1,3},{2,0},{3,1},{4,6},{5,7},{6,4},{7,5},{8,10},{9,11},{10,... | collective-permute-start | bytes 786440 | tf_op jit(solution)/shard_map/ppermute | solution.py:21
  174.9 8.2 %collective-permute-start.42 = (bf16[512,256]{1,0:T(8,128)(2,1)S(1)}, bf16[512,256]{1,0:T(8,128)(2,1)S(1)}, u32[]{:S(2)}, u32[]{:S(2)}) collective-permute-start(bf16[512,256]{1,0:T(8,128)(2,1)S(1)} %add_convert_fusion.refs_4_), channel_id=1, source_target_pairs={{0,2},{1,3},{2,0},{3,1},{4,6},{5,7},{6,4},{7,5},{8,10},{9,11},{10,... | collective-permute-start | bytes 786440 | tf_op jit(solution)/shard_map/ppermute | solution.py:21
  175.0 8.2 %collective-permute-start.33 = (bf16[512,256]{1,0:T(8,128)(2,1)S(1)}, bf16[512,256]{1,0:T(8,128)(2,1)S(1)}, u32[]{:S(2)}, u32[]{:S(2)}) collective-permute-start(bf16[512,256]{1,0:T(8,128)(2,1)S(1)} %add_convert_fusion.1.refs_0_), channel_id=1, source_target_pairs={{0,1},{1,0},{2,3},{3,2},{4,5},{5,4},{6,7},{7,6},{8,9},{9,8},{10,11... | collective-permute-start | bytes 786440 | tf_op jit(solution)/shard_map/ppermute | solution.py:21
  177.7 5.5 %collective-permute-start.34 = (bf16[512,256]{1,0:T(8,128)(2,1)S(1)}, bf16[512,256]{1,0:T(8,128)(2,1)S(1)}, u32[]{:S(2)}, u32[]{:S(2)}) collective-permute-start(bf16[512,256]{1,0:T(8,128)(2,1)S(1)} %collective-permute-done.32.refs_1_), channel_id=1, source_target_pairs={{0,1},{1,0},{2,3},{3,2},{4,5},{5,4},{6,7},{7,6},{8,9},{9,8},{10,11... | collective-permute-start | bytes 786440 | tf_op jit(solution)/shard_map/ppermute | solution.py:21
  177.7 5.5 %collective-permute-start.43 = (bf16[512,256]{1,0:T(8,128)(2,1)S(1)}, bf16[512,256]{1,0:T(8,128)(2,1)S(1)}, u32[]{:S(2)}, u32[]{:S(2)}) collective-permute-start(bf16[512,256]{1,0:T(8,128)(2,1)S(1)} %add_convert_fusion.refs_4_), channel_id=1, source_target_pairs={{0,1},{1,0},{2,3},{3,2},{4,5},{5,4},{6,7},{7,6},{8,9},{9,8},{10,11... | collective-permute-start | bytes 786440 | tf_op jit(solution)/shard_map/ppermute | solution.py:21
  183.2 1.5 collective-permute-start.44
  (20 other events, 147.4 us)

commit v3 on v0

v3 whole, which is shorter than its diff:
```python
import functools
import math

import jax
import jax.numpy as jnp
from jax import lax
from jax.experimental import pallas as pl
from jax.experimental.pallas import tpu as pltpu
from jax.sharding import PartitionSpec as P

VMEM_LIMIT = 28 * 1024 * 1024
NO_COST = pl.CostEstimate(flops=0, bytes_accessed=0, transcendentals=0)


def moved_rows(block_rows):
    return block_rows * 4 // 8 // 256 * 256


class Plan:
    def __init__(self, **fields):
        self.__dict__.update(fields)


def swap(array, axis, distance):
    count = lax.axis_size(axis)
    return lax.ppermute(array, axis, [(i, i ^ distance) for i in range(count)])


def after(arrays, *earlier):
    tied = lax.optimization_barrier((tuple(arrays), tuple(earlier)))
    return list(tied[0]), list(tied[1])


def kernel_call(kernel, name, outs, scalars, arrays, scratch=(), cost=NO_COST):
    smem = pl.BlockSpec(memory_space=pltpu.SMEM)
    vmem = pl.BlockSpec(memory_space=pltpu.VMEM)
    single = not isinstance(outs, tuple)
    return pl.pallas_call(
        kernel,
        out_shape=outs,
        in_specs=[smem] * len(scalars) + [vmem] * len(arrays),
        out_specs=vmem if single else (vmem,) * len(outs),
        scratch_shapes=list(scratch),
        compiler_params=pltpu.CompilerParams(vmem_limit_bytes=VMEM_LIMIT),
        cost_estimate=cost,
        name=name,
    )(*scalars, *arrays)


def bytes_cost(amount):
    return pl.CostEstimate(flops=0, bytes_accessed=amount, transcendentals=0)


def first_key(order, me, half, plan):
    block = order[2 * me + half]
    first = jnp.maximum(block - plan.stretch_count // 2, 0) * plan.stretch_rows
    return block, pl.multiple_of(first, plan.stretch_rows)


def sort_rows(plan, me, order, block_refs, sorted_ref):
    rows = plan.stretch_rows
    for index, block in enumerate(block_refs):
        for half in range(2):
            to = pl.multiple_of(order[2 * (me ^ index) + half] * rows, rows)
            sorted_ref[pl.ds(to, rows), :] = block[half * rows : (half + 1) * rows, :]


def unsort_rows(plan, me, order, total, keep_ref, send_ref):
    rows = plan.stretch_rows
    for index in range(plan.ctx_count):
        for half in range(2):
            origin = pl.multiple_of(order[2 * (me ^ index) + half] * rows, rows)
            start = (index // 2) * 2 * rows + half * rows
            to_ref = send_ref if index % 2 else keep_ref
            to_ref[start : start + rows, :] = total[pl.ds(origin, rows), :].astype(to_ref.dtype)


def stack_heads(plan, array_ref, stacked_ref):
    rows, width = plan.stretch_rows, plan.head_dim
    for half in range(2):
        for head in range(plan.head_count):
            start = (half * plan.head_count + head) * rows
            stacked_ref[start : start + rows, :] = array_ref[
                half * rows : (half + 1) * rows, head * width : (head + 1) * width
            ]


def unstack_heads(plan, stacked_ref, array_ref):
    rows, width = plan.stretch_rows, plan.head_dim
    for half in range(2):
        for head in range(plan.head_count):
            start = (half * plan.head_count + head) * rows
            array_ref[half * rows : (half + 1) * rows, head * width : (head + 1) * width] = (
                stacked_ref[start : start + rows, :]
            )


NT = (((1,), (1,)), ((), ()))
TN = (((0,), (0,)), ((), ()))


def probs_kernel(plan, ids, order, lengths, q_ref, g_ref, *refs):
    key_refs = refs[: plan.ctx_count]
    probs_ref, keys, qs, gs, keep_ref, send_ref, total = refs[plan.ctx_count :]
    me = ids[0]
    sort_rows(plan, me, order, key_refs, keys)
    stack_heads(plan, q_ref, qs)
    stack_heads(plan, g_ref, gs)
    total[...] = jnp.zeros_like(total)
    ends = []
    running = 0
    for at in range(lengths.shape[0]):
        running = running + lengths[at]
        ends.append(running)

    def step(at, carry):
        half = at // plan.steps
        block, first = first_key(order, me, half, plan)
        part = pl.ds(pl.multiple_of(at * plan.chunk, plan.chunk), plan.chunk)
        inside = (at - half * plan.steps) * plan.chunk
        inside = inside + lax.broadcasted_iota(jnp.int32, (1, plan.chunk), 1)
        at_query = block * plan.stretch_rows + lax.rem(inside, plan.stretch_rows)
        begin = jnp.zeros_like(at_query)
        for end in ends:
            begin = jnp.where(at_query >= end, end, begin)
        at_key = first + lax.broadcasted_iota(jnp.int32, (plan.window, plan.chunk), 0)
        allowed = (at_key >= begin) & (at_key <= at_query)
        k = keys[pl.ds(first, plan.window), :]
        scores = lax.dot_general(k, qs[part, :], NT, preferred_element_type=jnp.float32)
        masked = jnp.where(allowed, scores * plan.score_scale, -jnp.inf)
        expsum = jnp.exp(masked - jnp.max(masked, axis=0, keepdims=True))
        probs = expsum * (1.0 / jnp.sum(expsum, axis=0, keepdims=True))
        probs_low = probs.astype(jnp.bfloat16)
        probs_ref[at] = probs_low
        dv = jnp.dot(probs_low, gs[part, :], preferred_element_type=jnp.float32)
        total[pl.ds(first, plan.window), :] += dv
        return carry

    lax.fori_loop(0, 2 * plan.steps, step, 0)
    unsort_rows(plan, me, order, total, keep_ref, send_ref)


def scores_kernel(plan, ids, order, probs_ref, keys, qs, gs, *refs):
    value_refs = refs[: plan.ctx_count]
    qgrad_ref, keep_ref, send_ref, values, total, dqs = refs[plan.ctx_count :]
    me = ids[0]
    sort_rows(plan, me, order, value_refs, values)
    total[...] = jnp.zeros_like(total)

    def step(at, carry):
        half = at // plan.steps
        block, first = first_key(order, me, half, plan)
        part = pl.ds(pl.multiple_of(at * plan.chunk, plan.chunk), plan.chunk)
        k = keys[pl.ds(first, plan.window), :]
        v = values[pl.ds(first, plan.window), :]
        probs = probs_ref[at].astype(jnp.float32)
        dprob = lax.dot_general(v, gs[part, :], NT, preferred_element_type=jnp.float32)
        delta = jnp.sum(probs * dprob, axis=0, keepdims=True)
        dscore = (probs * (dprob - delta)).astype(jnp.bfloat16)
        dq = lax.dot_general(k, dscore, TN, preferred_element_type=jnp.float32)
        dqs[part, :] = (jnp.transpose(dq) * plan.score_scale).astype(jnp.bfloat16)
        dk = jnp.dot(dscore, qs[part, :], preferred_element_type=jnp.float32) * plan.score_scale
        total[pl.ds(first, plan.window), :] += dk
        return carry

    lax.fori_loop(0, 2 * plan.steps, step, 0)
    unsort_rows(plan, me, order, total, keep_ref, send_ref)
    unstack_heads(plan, dqs, qgrad_ref)


def attention_plan(queries, head_dim, ctx_count):
    row_count, width = queries.shape
    stretch_rows = row_count // 2
    head_count = width // head_dim
    stacked = head_count * stretch_rows
    chunk = 256 if stacked % 256 == 0 else 128
    return Plan(
        ctx_count=ctx_count,
        stretch_rows=stretch_rows,
        stretch_count=2 * ctx_count,
        head_count=head_count,
        head_dim=head_dim,
        chunk=chunk,
        steps=stacked // chunk,
        stacked=2 * stacked,
        seq_rows=row_count * ctx_count,
        window=row_count * ctx_count // 2 + stretch_rows,
        score_scale=1.0 / math.sqrt(head_dim),
    )


def shape_of(rows, width, kind=jnp.bfloat16):
    return jax.ShapeDtypeStruct((rows, width), kind)


def probs_and_value_grad(plan, me, order, lengths, queries, cotangent, key_blocks):
    width = plan.head_dim
    outs = (
        jax.ShapeDtypeStruct((2 * plan.steps, plan.window, plan.chunk), jnp.bfloat16),
        shape_of(plan.seq_rows, width),
        shape_of(plan.stacked, width),
        shape_of(plan.stacked, width),
        shape_of(plan.seq_rows // 2, width, jnp.float32),
        shape_of(plan.seq_rows // 2, width),
    )
    return kernel_call(
        functools.partial(probs_kernel, plan),
        "probs",
        outs,
        (me, order, lengths),
        (queries, cotangent, *key_blocks),
        [pltpu.VMEM((plan.seq_rows, width), jnp.float32)],
        cost=bytes_cost(18 * plan.window * plan.stacked),
    )


def query_and_key_grad(plan, me, order, saved, value_blocks):
    width = plan.head_dim
    outs = (
        shape_of(2 * plan.stretch_rows, plan.head_count * width),
        shape_of(plan.seq_rows // 2, width, jnp.float32),
        shape_of(plan.seq_rows // 2, width),
    )
    return kernel_call(
        functools.partial(scores_kernel, plan),
        "scores",
        outs,
        (me, order),
        (*saved, *value_blocks),
        [
            pltpu.VMEM((plan.seq_rows, width), jnp.bfloat16),
            pltpu.VMEM((plan.seq_rows, width), jnp.float32),
            pltpu.VMEM((plan.stacked, width), jnp.bfloat16),
        ],
        cost=bytes_cost(14 * plan.window * plan.stacked),
    )


def project_kernel(plan, ids, hidden, *refs):
    out_ref = refs[-1]
    dp, core = ids[2], ids[1]
    total = refs[0][...] if plan.start else None
    for (block, side, offset), weight in zip(plan.terms, refs[plan.start : -1]):
        from_column = (dp ^ block) * plan.block_rows + (core ^ side) * plan.side_rows + offset
        columns = pl.ds(pl.multiple_of(from_column, 128), weight.shape[0])
        term = jnp.dot(hidden[:, columns], weight[...], preferred_element_type=jnp.float32)
        total = term if total is None else total + term
    out_ref[...] = total.astype(out_ref.dtype)


def project(ids, start, inputs, block_rows, pieces, kind):
    names = sorted(pieces)
    weights = [pieces[name] for name in names]
    started = [] if start is None else [start]
    plan = Plan(terms=names, start=len(started), block_rows=block_rows, side_rows=block_rows // 2)
    rows = inputs.shape[0]
    amount = sum(2 * weight.size + 2 * rows * weight.shape[0] for weight in weights)
    return kernel_call(
        functools.partial(project_kernel, plan),
        "project",
        shape_of(rows, weights[0].shape[1], kind),
        (ids,),
        (inputs, *started, *weights),
        cost=bytes_cost(amount),
    )


def weight_kernel(plan, ids, *refs):
    hidden = refs[: plan.hidden]
    grads = refs[plan.hidden : -2]
    z, core, dp = ids[0] % plan.sub_count, ids[1], ids[2]
    rows = plan.rows
    share = rows // plan.sub_count
    tile = next(size for size in (512, 256, 128) if rows % size == 0)
    step = math.gcd(share, tile)
    for side, out_ref in ((1, refs[-2]), (0, refs[-1])):
        for at, group in enumerate(plan.groups):
            for start in range(0, rows, tile):
                product = None
                for array, block, grad in group:
                    origin = plan.origin + (core ^ side) * rows + start
                    if block is not None:
                        origin = origin + (dp ^ block) * plan.block_rows
                    columns = pl.ds(pl.multiple_of(origin, 128), tile)
                    term = lax.dot_general(
                        hidden[array][:, columns],
                        grads[grad][...],
                        TN,
                        preferred_element_type=jnp.float32,
                    )
                    product = term if product is None else product + term
                for inner in range(0, tile, step):
                    part, offset = divmod(start + inner, share)
                    to = pl.multiple_of(at * rows + (z ^ part) * share + offset, step)
                    piece = product[inner : inner + step, :]
                    out_ref[pl.ds(to, step), :] = piece.astype(out_ref.dtype)


def weight_rows(ids, hidden, grads, groups, origin, rows, block_rows, sub_count):
    plan = Plan(
        hidden=len(hidden),
        groups=groups,
        origin=origin,
        rows=rows,
        block_rows=block_rows,
        sub_count=sub_count,
    )
    out = shape_of(rows * len(groups), grads[0].shape[1])
    amount = 2 * sum(len(group) for group in groups) * rows * 2 * hidden[0].shape[0] + 4 * out.size
    theirs, ours = kernel_call(
        functools.partial(weight_kernel, plan),
        "weight_rows",
        (out, out),
        (ids,),
        (*hidden, *grads),
        cost=bytes_cost(amount),
    )
    return ours.astype(jnp.float32) + swap(theirs, "ctx", 1).astype(jnp.float32)


def sum_over_dp(array):
    count = lax.axis_size("dp")
    rows = array.shape[0] // count
    total = array[:rows]
    for j in range(1, count):
        leaving = array[j * rows : (j + 1) * rows].astype(jnp.bfloat16)
        total = total + swap(leaving, "dp", j).astype(jnp.float32)
    return total


def sum_along_z(full, sub_count):
    share = full.shape[0] // sub_count
    parts = {m: full[m * share : (m + 1) * share] for m in range(sub_count)}
    bits = [1 << at for at in range(sub_count.bit_length() - 1)]
    for bit in bits:
        for m in list(parts):
            if m & bit:
                came = swap(parts.pop(m).astype(jnp.bfloat16), "ctx", 2 * bit)
                parts[m ^ bit] = parts[m ^ bit] + came.astype(jnp.float32)
    low = parts[0].astype(jnp.bfloat16)
    final = (parts[0] + swap(low, "ctx", 2 * sub_count).astype(jnp.float32)).astype(jnp.bfloat16)
    rows = {0: final}
    for bit in bits[::-1]:
        rows.update({m | bit: swap(one, "ctx", 2 * bit) for m, one in list(rows.items())})
    own = [rows[m] for m in range(sub_count)]
    return own + [swap(one, "ctx", 1) for one in own]


def assemble_kernel(sub_count, regions, ids, *refs):
    out_ref = refs[-1]
    blocks = iter(refs[:-1])
    z, core = ids[0] % sub_count, ids[1]
    for origin, rows in regions:
        share = rows // sub_count
        for side in range(2):
            for m in range(sub_count):
                to = origin + (core ^ side) * rows + (z ^ m) * share
                to = pl.multiple_of(to, share)
                out_ref[pl.ds(to, share), :] = next(blocks)[...].astype(jnp.float32)


def assemble(ids, blocks, sub_count, regions):
    rows = sum(block.shape[0] for block in blocks)
    return kernel_call(
        functools.partial(assemble_kernel, sub_count, regions),
        "assemble",
        shape_of(rows, blocks[0].shape[1], jnp.float32),
        (ids,),
        blocks,
    )


def on_device(hidden_in, queries, grad_out, w_key, w_value, stretch_order, doc_lengths):
    inputs = hidden_in[0]
    head_dim = w_key.shape[1]
    dp_count = lax.axis_size("dp")
    ctx_count = lax.axis_size("ctx")
    z_count = ctx_count // 2
    sub_count = z_count // 2
    dp, ctx = lax.axis_index("dp"), lax.axis_index("ctx")
    z, core = ctx // 2, ctx % 2
    ids = jnp.stack([z, core, dp]).astype(jnp.int32)
    me = jnp.reshape(ctx, (1,)).astype(jnp.int32)
    block_rows = w_key.shape[0]
    half_rows = block_rows // 2
    quarter = half_rows // 2
    bits = [1 << at for at in range(dp_count.bit_length() - 1)]

    def own_pieces(weight):
        return {
            (0, side, offset): lax.dynamic_slice_in_dim(
                weight, (core ^ side) * half_rows + offset, quarter, 0
            )
            for side in range(2)
            for offset in (0, quarter)
        }

    def gather(pieces, steps):
        for step in steps:
            for offset, order in ((0, bits), (quarter, bits[::-1])):
                bit = order[step]
                have = [name for name in pieces if name[1] == 0 and name[2] == offset]
                for j, _, _ in have:
                    pieces[j | bit, 0, offset] = swap(pieces[j, 0, offset], "dp", bit)

    def from_other_core(pieces, names):
        pieces.update({(j, 1, offset): swap(pieces[j, 0, offset], "ctx", 1) for j, _, offset in names})

    def last_step(name):
        return name[0] not in [0] + bits

    key_pieces = own_pieces(w_key)
    gather(key_pieces, range(len(bits)))
    landing = [(j, 0, offset) for j in range(1, dp_count) for offset in (0, quarter)]
    from_other_core(key_pieces, landing)
    first = [(bits[0], 0, 0), (bits[-1], 0, quarter)]
    leaving = [(0, 0, 0), (0, 0, quarter)]
    value_pieces = own_pieces(w_value)
    tied, ended = after(
        [value_pieces[name] for name in leaving], *[key_pieces[name] for name in first]
    )
    value_pieces.update(zip(leaving, tied))
    gather(value_pieces, range(1))

    def project_all(pieces):
        early = {name: one for name, one in pieces.items() if not last_step(name)}
        late = {name: one for name, one in pieces.items() if last_step(name)}
        partial = project(ids, None, inputs, block_rows, early, jnp.float32)
        return project(ids, partial, inputs, block_rows, late, jnp.bfloat16)

    def gather_along_z(own):
        return [swap(own, "ctx", 2 * m) if m else own for m in range(z_count)]

    def both_cores(along):
        return [block for one in along for block in (one, swap(one, "ctx", 1))]

    def over_cores(keep, send):
        return keep + swap(send, "ctx", 1).astype(jnp.float32)

    def to_owner(chip):
        rows = chip.shape[0] // z_count
        total = chip[:rows]
        for m in range(1, z_count):
            leaving = chip[m * rows : (m + 1) * rows].astype(jnp.bfloat16)
            total = total + swap(leaving, "ctx", 2 * m).astype(jnp.float32)
        return total.astype(jnp.bfloat16)

    first_rows = moved_rows(block_rows)
    first_half, last_half = first_rows // 2, (block_rows - first_rows) // 2
    regions = ((0, first_half), (first_rows, last_half))
    moving = [
        lax.dynamic_slice_in_dim(inputs, (dp ^ j) * block_rows, first_rows, 1)
        for j in range(dp_count)
    ]
    def hold(arrays, names):
        tied, ended = after(arrays, *[value_pieces[name] for name in names])
        value_pieces.update(zip(names, ended))
        return tied

    plan = attention_plan(queries[0], head_dim, ctx_count)
    own, *moving[1:] = hold([project_all(key_pieces), *moving[1:]], first)
    gather(value_pieces, range(1, len(bits)))
    from_other_core(value_pieces, first)
    along = gather_along_z(own)
    second = [name for name in landing if name not in first and not last_step(name)]
    along = hold(along, second)
    from_other_core(value_pieces, [name for name in landing if name not in first])
    key_blocks = both_cores(along)
    moving[1:] = hold(moving[1:], landing)
    near = [j for j in range(1, dp_count) if j in bits]
    far = [j for j in range(1, dp_count) if j not in bits]
    moved = {0: moving[0]}
    moved.update({j: swap(moving[j], "dp", j) for j in near})
    key_blocks, (own,) = after(key_blocks, project_all(value_pieces))
    along = gather_along_z(own)
    *saved, keep_v, send_v = probs_and_value_grad(
        plan, me, stretch_order, doc_lengths[0], queries[0], grad_out[0], key_blocks
    )
    along, (send_v,) = after(along, send_v)
    value_blocks = both_cores(along)
    (send_v,), ended = after([send_v], *value_blocks, *[moved[j] for j in near])
    value_blocks = ended[:ctx_count]
    moved.update(zip(near, ended[ctx_count:]))

    ready, ended = after([moving[j] for j in far], *[moved[j] for j in near])
    moved.update(zip(near, ended))
    moved.update({j: swap(one, "dp", j) for j, one in zip(far, ready)})
    query_grad, keep_k, send_k = query_and_key_grad(plan, me, stretch_order, saved, value_blocks)
    chip_v = over_cores(keep_v, send_v)
    chip_k = over_cores(keep_k, send_k)
    value_grad = to_owner(chip_v)
    (value_grad,), (chip_k,) = after([value_grad], chip_k)
    key_grad = to_owner(chip_k)
    (key_grad,), ended = after([key_grad], *[moved[j] for j in far])
    moved.update(zip(far, ended))

    def weight_grad(grad):
        grads = [grad] + [swap(grad, "dp", j) for j in range(1, dp_count)]
        groups = [[(0, j, 0)] for j in range(dp_count)]
        last = weight_rows(
            ids, [inputs], [grad], groups, first_rows, last_half, block_rows, sub_count
        )
        last = sum_along_z(sum_over_dp(last), sub_count)
        groups = [[(j, None, j) for j in range(dp_count)]]
        arrays = [moved[j] for j in range(dp_count)]
        first = weight_rows(ids, arrays, grads, groups, 0, first_half, block_rows, sub_count)
        first = sum_along_z(first, sub_count)
        return assemble(ids, first + last, sub_count, regions)

    value_rows = weight_grad(value_grad)
    key_rows = weight_grad(key_grad)
    return query_grad[None], key_rows, value_rows


def solution(mesh):
    return jax.shard_map(
        on_device,
        mesh=mesh,
        in_specs=(
            P("dp", "ctx", None),
            P("dp", "ctx", None),
            P("dp", "ctx", None),
            P("dp", None),
            P("dp", None),
            P(),
            P("dp", None),
        ),
        out_specs=(P("dp", "ctx", None), P("dp", None), P("dp", None)),
        check_vma=False,
    )
```

time: 398 us -> 192 us (0.48)
  waiting for transfers between devices: 270 us -> 79 us
  starting transfers between devices: 0.16 us -> 63.4 us
  matrix products: 50.3 us -> 0 us
  Pallas kernels: 0 us -> 33.1 us
  other arithmetic: 33.2 us -> 1.43 us
  blocking collectives: 15.5 us -> 0 us
  between operations: 13.9 us -> 1.28 us
    all_gather x1 -> x0, waiting for transfers between devices: 88 us -> none  [on_device(): lax.all_gather(stacked, 'dp', axis=0, tiled=True)]
    reduce_scatter x1 -> x0, waiting for transfers between devices: 84.6 us -> none  [on_device(): lax.psum_scatter(lax.dot_general(columns, kv_grads, (((0,), (0,)), ((), (...]
    ppermute x0 -> x85, waiting for transfers between devices: none -> 79 us  [swap(): return lax.ppermute(array, axis, [(i, i ^ distance) for i in range(count)])]
    psum x1 -> x0, waiting for transfers between devices: 65 us -> none  [on_device(): weight_grads = lax.psum(partial_rows, 'ctx').astype(jnp.float32)]
    ppermute x0 -> x85, starting transfers between devices: none -> 63.4 us  [swap(): return lax.ppermute(array, axis, [(i, i ^ distance) for i in range(count)])]
    dot_general x50 -> x0, matrix products: 50.3 us -> none  [the longest x8 10.3 us: one_head(): jnp.dot(query_one, jnp.transpose(key_rows), preferred_element_type=jnp.fl...]
    pallas_call x0 -> x12, Pallas kernels: none -> 33.1 us  [kernel_call(): pl.pallas_call(kernel, out_shape=outs, in_specs=[smem] * len(scalars) + [...]
    unnamed x5 -> x0, waiting for transfers between devices: 32.1 us -> none
  transfers between devices with their start and end apart: 4 -> 85, of which waited for: 4 -> 40; matrix products, arithmetic and copies ran while one was open for 1% -> 3% of each run, Pallas kernels for 0% -> 15%
where the time goes in v3:
time: 192 us
  waiting for transfers between devices  79 us (41%)
  starting transfers between devices  63.4 us (33%)
  Pallas kernels  33.1 us (17%)
  local copies, waits for them, and re-layouts  13.5 us (7%)
    ppermute x85, waiting for transfers between devices, swap(): return lax.ppermute(array, axis, [(i, i ^ distance) for i in range(count)])  79 us
    ppermute x85, starting transfers between devices, swap(): return lax.ppermute(array, axis, [(i, i ^ distance) for i in range(count)])  63.4 us
    pallas_call x12, Pallas kernels, kernel_call(): pl.pallas_call(kernel, out_shape=outs, in_specs=[smem] * len(scalars) + [...  33.1 us
    unnamed x36, local copies, waits for them, and re-layouts  7.37 us
  transfers between devices with their start and end apart: 85, of which 40 were waited for; matrix products, arithmetic and copies ran while one was open for 3% of the time, Pallas kernels for 15%

profile of v3, /device:TPU:0, one launch (start us, length us, event | category | flops | bytes accessed | tf_op | source)
XLA Modules:
  0.0 191.6 jit_solution(14250051995638799360)
XLA Ops:
  1.9 3.0 %collective-permute-start.5 = (bf16[1024,128]{1,0:T(8,128)(2,1)S(1)}, bf16[1024,128]{1,0:T(8,128)(2,1)S(1)}, u32[]{:S(2)}, u32[]{:S(2)}) collective-permute-start(bf16[1024,128]{1,0:T(8,128)(2,1)S(1)} %get-tuple-element.168.refs_1_), channel_id=1, source_target_pairs={{0,16},{8,24},{16,0},{24,8},{1,17},{9,25},{17,1},{25,9},{2,18},{10... | collective-permute-start | bytes 786440 | tf_op jit(solution)/shard_map/ppermute | solution.py:26
  7.1 5.0 %collective-permute-done.5.refs_9_ = bf16[1024,128]{1,0:T(8,128)(2,1)S(1)} collective-permute-done((bf16[1024,128]{1,0:T(8,128)(2,1)S(1)}, bf16[1024,128]{1,0:T(8,128)(2,1)S(1)}, u32[]{:S(2)}, u32[]{:S(2)}) %collective-permute-start.5) | collective-permute-done | bytes 262176 | tf_op jit(solution)/shard_map/ppermute | solution.py:26
  12.1 2.0 %collective-permute-start.9 = (bf16[1024,128]{1,0:T(8,128)(2,1)S(1)}, bf16[1024,128]{1,0:T(8,128)(2,1)}, u32[]{:S(2)}, u32[]{:S(2)}) collective-permute-start(bf16[1024,128]{1,0:T(8,128)(2,1)S(1)} %collective-permute-done.5.refs_9_), channel_id=1, source_target_pairs={{0,8},{8,0},{16,24},{24,16},{1,9},{9,1},{17,25},{25,17},{2,10},{10... | collective-permute-start | bytes 786440 | tf_op jit(solution)/shard_map/ppermute | solution.py:26
  14.7 2.2 %collective-permute-done.4.refs_8_ = bf16[1024,128]{1,0:T(8,128)(2,1)S(1)} collective-permute-done((bf16[1024,128]{1,0:T(8,128)(2,1)S(1)}, bf16[1024,128]{1,0:T(8,128)(2,1)S(1)}, u32[]{:S(2)}, u32[]{:S(2)}) %collective-permute-start.4) | collective-permute-done | bytes 262176 | tf_op jit(solution)/shard_map/ppermute | solution.py:26
  16.9 3.0 %collective-permute-done.refs_4_ = bf16[1024,128]{1,0:T(8,128)(2,1)} collective-permute-done((bf16[1024,128]{1,0:T(8,128)(2,1)S(1)}, bf16[1024,128]{1,0:T(8,128)(2,1)}, u32[]{:S(2)}, u32[]{:S(2)}) %collective-permute-start) | collective-permute-done | bytes 262176 | tf_op jit(solution)/shard_map/ppermute | solution.py:26
  21.2 2.8 %collective-permute-done.9.refs_2_ = bf16[1024,128]{1,0:T(8,128)(2,1)} collective-permute-done((bf16[1024,128]{1,0:T(8,128)(2,1)S(1)}, bf16[1024,128]{1,0:T(8,128)(2,1)}, u32[]{:S(2)}, u32[]{:S(2)}) %collective-permute-start.9) | collective-permute-done | bytes 262176 | tf_op jit(solution)/shard_map/ppermute | solution.py:26
  27.5 3.4 %dynamic-slice_bitcast_fusion = (bf16[192,2048]{1,0:T(8,128)(2,1)S(1)}, bf16[192,2048]{1,0:T(8,128)(2,1)}, bf16[192,2048]{1,0:T(8,128)(2,1)}, bf16[192,2048]{1,0:T(8,128)(2,1)}) fusion(bf16[1,192,16384]{2,1,0:T(8,128)(2,1)} %param.7, s32[]{:T(128)S(6)} %select_n.48, s32[]{:T(128)S(6)} %select_n.46, s32[]{:T(128)S(6)} %select_n.45, s32[]{:T(128)S(6)} %select_n.47), kind=kLoop, calls=%fused_computation.2 | loop fusion | bytes 6291472 | tf_op jit(solution)/shard_map/dynamic_slice | solution.py:452
  30.9 1.5 collective-permute-start.18
  33.3 2.8 %copy-done = bf16[1,192,16384]{2,1,0:T(8,128)(2,1)S(1)} copy-done((bf16[1,192,16384]{2,1,0:T(8,128)(2,1)S(1)}, bf16[1,192,16384]{2,1,0:T(8,128)(2,1)}, u32[]{:S(2)}) %copy-start) | copy-done | bytes 6291480
  39.9 2.6 %project.4.refs_0_ = f32[192,128]{1,0:T(8,128)S(1)} custom-call(s32[3]{0:T(128)S(1)} %pad_add_fusion.ids, bf16[192,16384]{1,0:T(8,128)(2,1)S(1)} %bitcast.17, bf16[1024,128]{1,0:T(8,128)(2,1)S(1)} %get-tuple-element.169.refs_0_, bf16[1024,128]{1,0:T(8,128)(2,1)S(1)} %get-tuple-element.168.refs_1_, bf16[1024,128]{1,0:T(8,128)(2,1)S(1)} %get-tuple-element.170.refs_2_, ...), custom_call_target="tpu_custom_call" | custom-call | bytes 7864320 | tf_op jit(solution)/shard_map/project/pallas_call | solution.py:38
  42.5 1.9 project.5.refs_0_
  46.2 3.6 %collective-permute-start.16 = (bf16[192,128]{1,0:T(8,128)(2,1)S(1)}, bf16[192,128]{1,0:T(8,128)(2,1)S(1)}, u32[]{:S(2)}, u32[]{:S(2)}) collective-permute-start(bf16[192,128]{1,0:T(8,128)(2,1)S(1)} %project.5.refs_0_), channel_id=1, source_target_pairs={{0,6},{1,7},{2,4},{3,5},{4,2},{5,3},{6,0},{7,1},{8,14},{9,15},{10,... | collective-permute-start | bytes 147464 | tf_op jit(solution)/shard_map/ppermute | solution.py:26
  50.6 1.9 collective-permute-done.16.refs_6_
  52.5 2.3 %collective-permute-done.15.refs_4_ = bf16[192,128]{1,0:T(8,128)(2,1)S(1)} collective-permute-done((bf16[192,128]{1,0:T(8,128)(2,1)S(1)}, bf16[192,128]{1,0:T(8,128)(2,1)S(1)}, u32[]{:S(2)}, u32[]{:S(2)}) %collective-permute-start.15) | collective-permute-done | bytes 49184 | tf_op jit(solution)/shard_map/ppermute | solution.py:26
  55.8 1.6 collective-permute-start.39
  61.8 1.9 %project.6.refs_0_ = f32[192,128]{1,0:T(8,128)S(1)} custom-call(s32[3]{0:T(128)S(1)} %pad_add_fusion.ids, bf16[192,16384]{1,0:T(8,128)(2,1)S(1)} %bitcast.19, bf16[1024,128]{1,0:T(8,128)(2,1)S(1)} %get-tuple-element.75.refs_0_, bf16[1024,128]{1,0:T(8,128)(2,1)S(1)} %get-tuple-element.76.refs_1_, bf16[1024,128]{1,0:T(8,128)(2,1)S(1)} %get-tuple-element.166.refs_2_, ...), custom_call_target="tpu_custom_call" | custom-call | bytes 7864320 | tf_op jit(solution)/shard_map/project/pallas_call | solution.py:38
  65.0 1.8 collective-permute-start.33
  67.1 2.3 %collective-permute-start.31 = (bf16[192,128]{1,0:T(8,128)(2,1)S(1)}, bf16[192,128]{1,0:T(8,128)(2,1)S(1)}, u32[]{:S(2)}, u32[]{:S(2)}) collective-permute-start(bf16[192,128]{1,0:T(8,128)(2,1)S(1)} %project.7.refs_0_), channel_id=1, source_target_pairs={{0,2},{1,3},{2,0},{3,1},{4,6},{5,7},{6,4},{7,5},{8,10},{9,11},{10,... | collective-permute-start | bytes 147464 | tf_op jit(solution)/shard_map/ppermute | solution.py:26
  69.4 6.5 %probs.1 = (bf16[6,864,256]{2,1,0:T(8,128)(2,1)S(1)}, bf16[1536,128]{1,0:T(8,128)(2,1)S(1)}, bf16[1536,128]{1,0:T(8,128)(2,1)S(1)}, bf16[1536,128]{1,0:T(8,128)(...) custom-call(s32[1]{0:T(128)} %bitcast.ids, s32[16]{0:T(128)S(1)} %copy-done.11, s32[8]{0:T(128)S(1)} %bitcast.27, ...), custom_call_target="tpu_custom_call" | custom-call | bytes 23887872 | tf_op jit(solution)/shard_map/probs/pallas_call | solution.py:38
  78.7 7.4 %scores.1 = (bf16[192,1024]{1,0:T(8,128)(2,1)}, f32[768,128]{1,0:T(8,128)S(1)}, bf16[768,128]{1,0:T(8,128)(2,1)S(1)}) custom-call(s32[1]{0:T(128)} %bitcast.ids, s32[16]{0:T(128)S(1)} %copy-done.11, bf16[6,864,256]{2,1,0:T(8,128)(2,1)S(1)} %get-tuple-element.103.probs_ref, bf16[1536,128]{1,0:T(8,128)(2,1)S(1)} %get-tuple-element.104.keys, ...), custom_call_target="tpu_custom_call" | custom-call | bytes 18579456 | tf_op jit(solution)/shard_map/scores/pallas_call | solution.py:38
  87.6 2.6 %collective-permute-start.43 = (bf16[192,128]{1,0:T(8,128)(2,1)S(1)}, bf16[192,128]{1,0:T(8,128)(2,1)S(1)}, u32[]{:S(2)}, u32[]{:S(2)}) collective-permute-start(bf16[192,128]{1,0:T(8,128)(2,1)S(1)} %get-tuple-element.175), channel_id=1, source_target_pairs={{0,6},{1,7},{2,4},{3,5},{4,2},{5,3},{6,0},{7,1},{8,14},{9,15},{10,... | collective-permute-start | bytes 147464 | tf_op jit(solution)/shard_map/ppermute | solution.py:26
  91.7 2.2 %collective-permute-done.43 = bf16[192,128]{1,0:T(8,128)(2,1)S(1)} collective-permute-done((bf16[192,128]{1,0:T(8,128)(2,1)S(1)}, bf16[192,128]{1,0:T(8,128)(2,1)S(1)}, u32[]{:S(2)}, u32[]{:S(2)}) %collective-permute-start.43) | collective-permute-done | bytes 49184 | tf_op jit(solution)/shard_map/ppermute | solution.py:26
  94.0 2.0 %collective-permute-done.42 = bf16[192,128]{1,0:T(8,128)(2,1)S(1)} collective-permute-done((bf16[192,128]{1,0:T(8,128)(2,1)S(1)}, bf16[192,128]{1,0:T(8,128)(2,1)S(1)}, u32[]{:S(2)}, u32[]{:S(2)}) %collective-permute-start.42) | collective-permute-done | bytes 49184 | tf_op jit(solution)/shard_map/ppermute | solution.py:26
  96.1 2.0 %collective-permute-start.47 = (bf16[192,128]{1,0:T(8,128)(2,1)S(1)}, bf16[192,128]{1,0:T(8,128)(2,1)S(1)}, u32[]{:S(2)}, u32[]{:S(2)}) collective-permute-start(bf16[192,128]{1,0:T(8,128)(2,1)S(1)} %get-tuple-element.172), channel_id=1, source_target_pairs={{0,6},{1,7},{2,4},{3,5},{4,2},{5,3},{6,0},{7,1},{8,14},{9,15},{10,... | collective-permute-start | bytes 147464 | tf_op jit(solution)/shard_map/ppermute | solution.py:26
  99.6 1.9 collective-permute-start.69
  104.1 3.6 %collective-permute-done.48.refs_3_ = bf16[192,2048]{1,0:T(8,128)(2,1)S(1)} collective-permute-done((bf16[192,2048]{1,0:T(8,128)(2,1)S(1)}, bf16[192,2048]{1,0:T(8,128)(2,1)S(1)}, u32[]{:S(2)}, u32[]{:S(2)}) %collective-permute-start.48) | collective-permute-done | bytes 786464 | tf_op jit(solution)/shard_map/ppermute | solution.py:26
  109.1 1.9 weight_rows.6
  111.1 1.9 weight_rows.7
  117.0 1.8 collective-permute-done.51.refs_7_
  120.2 1.9 weight_rows.4
  122.2 1.9 weight_rows.5
  124.9 2.1 %collective-permute-start.53 = (bf16[512,128]{1,0:T(8,128)(2,1)S(1)}, bf16[512,128]{1,0:T(8,128)(2,1)S(1)}, u32[]{:S(2)}, u32[]{:S(2)}) collective-permute-start(bf16[512,128]{1,0:T(8,128)(2,1)S(1)} %slice.180), channel_id=1, source_target_pairs={{0,2},{1,3},{2,0},{3,1},{4,6},{5,7},{6,4},{7,5},{8,10},{9,11},{10,... | collective-permute-start | bytes 393224 | tf_op jit(solution)/shard_map/ppermute | solution.py:26
  127.0 4.2 %collective-permute-done.71 = bf16[512,128]{1,0:T(8,128)(2,1)S(1)} collective-permute-done((bf16[512,128]{1,0:T(8,128)(2,1)S(1)}, bf16[512,128]{1,0:T(8,128)(2,1)S(1)}, u32[]{:S(2)}, u32[]{:S(2)}) %collective-permute-start.71) | collective-permute-done | bytes 131104 | tf_op jit(solution)/shard_map/ppermute | solution.py:26
  133.1 1.7 collective-permute-start.54
  137.2 5.0 %collective-permute-done.72 = bf16[512,128]{1,0:T(8,128)(2,1)S(1)} collective-permute-done((bf16[512,128]{1,0:T(8,128)(2,1)S(1)}, bf16[512,128]{1,0:T(8,128)(2,1)S(1)}, u32[]{:S(2)}, u32[]{:S(2)}) %collective-permute-start.72) | collective-permute-done | bytes 131104 | tf_op jit(solution)/shard_map/ppermute | solution.py:26
  145.7 1.8 collective-permute-done.79
  147.5 1.8 collective-permute-start.61
  149.3 3.1 %collective-permute-done.78 = bf16[1024,128]{1,0:T(8,128)(2,1)S(1)} collective-permute-done((bf16[1024,128]{1,0:T(8,128)(2,1)S(1)}, bf16[1024,128]{1,0:T(8,128)(2,1)S(1)}, u32[]{:S(2)}, u32[]{:S(2)}) %collective-permute-start.78) | collective-permute-done | bytes 262176 | tf_op jit(solution)/shard_map/ppermute | solution.py:26
  153.9 5.4 %collective-permute-done.61 = bf16[1024,128]{1,0:T(8,128)(2,1)S(1)} collective-permute-done((bf16[1024,128]{1,0:T(8,128)(2,1)S(1)}, bf16[1024,128]{1,0:T(8,128)(2,1)S(1)}, u32[]{:S(2)}, u32[]{:S(2)}) %collective-permute-start.61) | collective-permute-done | bytes 262176 | tf_op jit(solution)/shard_map/ppermute | solution.py:26
  159.3 1.7 collective-permute-start.80
  161.0 3.8 %collective-permute-done.60 = bf16[1024,128]{1,0:T(8,128)(2,1)S(1)} collective-permute-done((bf16[1024,128]{1,0:T(8,128)(2,1)S(1)}, bf16[1024,128]{1,0:T(8,128)(2,1)S(1)}, u32[]{:S(2)}, u32[]{:S(2)}) %collective-permute-start.60) | collective-permute-done | bytes 262176 | tf_op jit(solution)/shard_map/ppermute | solution.py:26
  166.4 6.0 %collective-permute-done.62 = bf16[512,128]{1,0:T(8,128)(2,1)S(1)} collective-permute-done((bf16[512,128]{1,0:T(8,128)(2,1)S(1)}, bf16[512,128]{1,0:T(8,128)(2,1)S(1)}, u32[]{:S(2)}, u32[]{:S(2)}) %collective-permute-start.62) | collective-permute-done | bytes 131104 | tf_op jit(solution)/shard_map/ppermute | solution.py:26
  172.5 5.2 %collective-permute-done.81 = bf16[512,128]{1,0:T(8,128)(2,1)S(1)} collective-permute-done((bf16[512,128]{1,0:T(8,128)(2,1)S(1)}, bf16[512,128]{1,0:T(8,128)(2,1)S(1)}, u32[]{:S(2)}, u32[]{:S(2)}) %collective-permute-start.81) | collective-permute-done | bytes 131104 | tf_op jit(solution)/shard_map/ppermute | solution.py:26
  177.8 2.1 %collective-permute-done.63 = bf16[512,128]{1,0:T(8,128)(2,1)S(1)} collective-permute-done((bf16[512,128]{1,0:T(8,128)(2,1)S(1)}, bf16[512,128]{1,0:T(8,128)(2,1)S(1)}, u32[]{:S(2)}, u32[]{:S(2)}) %collective-permute-start.63) | collective-permute-done | bytes 131104 | tf_op jit(solution)/shard_map/ppermute | solution.py:26
  180.0 2.1 %collective-permute-start.64 = (bf16[512,128]{1,0:T(8,128)(2,1)S(1)}, bf16[512,128]{1,0:T(8,128)(2,1)S(1)}, u32[]{:S(2)}, u32[]{:S(2)}) collective-permute-start(bf16[512,128]{1,0:T(8,128)(2,1)S(1)} %add_convert_fusion.2.refs_4_), channel_id=1, source_target_pairs={{0,2},{1,3},{2,0},{3,1},{4,6},{5,7},{6,4},{7,5},{8,10},{9,11},{10,... | collective-permute-start | bytes 393224 | tf_op jit(solution)/shard_map/ppermute | solution.py:26
  182.1 4.1 %collective-permute-done.82.refs_5_ = bf16[512,128]{1,0:T(8,128)(2,1)S(1)} collective-permute-done((bf16[512,128]{1,0:T(8,128)(2,1)S(1)}, bf16[512,128]{1,0:T(8,128)(2,1)S(1)}, u32[]{:S(2)}, u32[]{:S(2)}) %collective-permute-start.82) | collective-permute-done | bytes 131104 | tf_op jit(solution)/shard_map/ppermute | solution.py:26
  187.6 2.0 %assemble.3 = f32[4096,128]{1,0:T(8,128)} custom-call(s32[3]{0:T(128)S(1)} %pad_add_fusion.ids, bf16[512,128]{1,0:T(8,128)(2,1)S(1)} %add_convert_fusion.1.refs_0_, bf16[512,128]{1,0:T(8,128)(2,1)S(1)} %collective-permute-done.73.refs_1_, bf16[512,128]{1,0:T(8,128)(2,1)S(1)} %collective-permute-done.74.refs_2_, ...), custom_call_target="tpu_custom_call" | custom-call | tf_op jit(solution)/shard_map/assemble/pallas_call | solution.py:38
  189.6 2.0 %assemble.2 = f32[4096,128]{1,0:T(8,128)} custom-call(s32[3]{0:T(128)S(1)} %pad_add_fusion.ids, bf16[512,128]{1,0:T(8,128)(2,1)S(1)} %add_convert_fusion.3.refs_0_, bf16[512,128]{1,0:T(8,128)(2,1)S(1)} %collective-permute-done.55.refs_1_, bf16[512,128]{1,0:T(8,128)(2,1)S(1)} %collective-permute-done.56.refs_2_, ...), custom_call_target="tpu_custom_call" | custom-call | tf_op jit(solution)/shard_map/assemble/pallas_call | solution.py:38
  (202 shorter events, 52.8 us)
Async XLA Ops:
  1.9 10.2 %collective-permute-start.5 = (bf16[1024,128]{1,0:T(8,128)(2,1)S(1)}, bf16[1024,128]{1,0:T(8,128)(2,1)S(1)}, u32[]{:S(2)}, u32[]{:S(2)}) collective-permute-start(bf16[1024,128]{1,0:T(8,128)(2,1)S(1)} %get-tuple-element.168.refs_1_), channel_id=1, source_target_pairs={{0,16},{8,24},{16,0},{24,8},{1,17},{9,25},{17,1},{25,9},{2,18},{10... | collective-permute-start | bytes 786440 | tf_op jit(solution)/shard_map/ppermute | solution.py:26
  5.0 9.2 %collective-permute-start.1 = (bf16[1024,128]{1,0:T(8,128)(2,1)S(1)}, bf16[1024,128]{1,0:T(8,128)(2,1)S(1)}, u32[]{:S(2)}, u32[]{:S(2)}) collective-permute-start(bf16[1024,128]{1,0:T(8,128)(2,1)S(1)} %get-tuple-element.168.refs_1_), channel_id=1, source_target_pairs={{0,8},{8,0},{16,24},{24,16},{1,9},{9,1},{17,25},{25,17},{2,10},{10... | collective-permute-start | bytes 786440 | tf_op jit(solution)/shard_map/ppermute | solution.py:26
  6.5 10.4 %collective-permute-start.4 = (bf16[1024,128]{1,0:T(8,128)(2,1)S(1)}, bf16[1024,128]{1,0:T(8,128)(2,1)S(1)}, u32[]{:S(2)}, u32[]{:S(2)}) collective-permute-start(bf16[1024,128]{1,0:T(8,128)(2,1)S(1)} %get-tuple-element.169.refs_0_), channel_id=1, source_target_pairs={{0,16},{8,24},{16,0},{24,8},{1,17},{9,25},{17,1},{25,9},{2,18},{10... | collective-permute-start | bytes 786440 | tf_op jit(solution)/shard_map/ppermute | solution.py:26
  7.0 13.0 %collective-permute-start = (bf16[1024,128]{1,0:T(8,128)(2,1)S(1)}, bf16[1024,128]{1,0:T(8,128)(2,1)}, u32[]{:S(2)}, u32[]{:S(2)}) collective-permute-start(bf16[1024,128]{1,0:T(8,128)(2,1)S(1)} %get-tuple-element.169.refs_0_), channel_id=1, source_target_pairs={{0,8},{8,0},{16,24},{24,16},{1,9},{9,1},{17,25},{25,17},{2,10},{10... | collective-permute-start | bytes 786440 | tf_op jit(solution)/shard_map/ppermute | solution.py:26
  12.1 12.0 %collective-permute-start.9 = (bf16[1024,128]{1,0:T(8,128)(2,1)S(1)}, bf16[1024,128]{1,0:T(8,128)(2,1)}, u32[]{:S(2)}, u32[]{:S(2)}) collective-permute-start(bf16[1024,128]{1,0:T(8,128)(2,1)S(1)} %collective-permute-done.5.refs_9_), channel_id=1, source_target_pairs={{0,8},{8,0},{16,24},{24,16},{1,9},{9,1},{17,25},{25,17},{2,10},{10... | collective-permute-start | bytes 786440 | tf_op jit(solution)/shard_map/ppermute | solution.py:26
  14.1 11.4 %collective-permute-start.7 = (bf16[1024,128]{1,0:T(8,128)(2,1)S(1)}, bf16[1024,128]{1,0:T(8,128)(2,1)S(1)}, u32[]{:S(2)}, u32[]{:S(2)}) collective-permute-start(bf16[1024,128]{1,0:T(8,128)(2,1)S(1)} %collective-permute-done.5.refs_9_), channel_id=1, source_target_pairs={{0,1},{1,0},{2,3},{3,2},{4,5},{5,4},{6,7},{7,6},{8,9},{9,8},{10,11... | collective-permute-start | bytes 786440 | tf_op jit(solution)/shard_map/ppermute | solution.py:26
  14.2 12.6 %collective-permute-start.3 = (bf16[1024,128]{1,0:T(8,128)(2,1)S(1)}, bf16[1024,128]{1,0:T(8,128)(2,1)}, u32[]{:S(2)}, u32[]{:S(2)}) collective-permute-start(bf16[1024,128]{1,0:T(8,128)(2,1)S(1)} %collective-permute-done.1.refs_5_), channel_id=1, source_target_pairs={{0,1},{1,0},{2,3},{3,2},{4,5},{5,4},{6,7},{7,6},{8,9},{9,8},{10,11... | collective-permute-start | bytes 786440 | tf_op jit(solution)/shard_map/ppermute | solution.py:26
  16.9 9.9 %collective-permute-start.6 = (bf16[1024,128]{1,0:T(8,128)(2,1)S(1)}, bf16[1024,128]{1,0:T(8,128)(2,1)}, u32[]{:S(2)}, u32[]{:S(2)}) collective-permute-start(bf16[1024,128]{1,0:T(8,128)(2,1)S(1)} %collective-permute-done.4.refs_8_), channel_id=1, source_target_pairs={{0,1},{1,0},{2,3},{3,2},{4,5},{5,4},{6,7},{7,6},{8,9},{9,8},{10,11... | collective-permute-start | bytes 786440 | tf_op jit(solution)/shard_map/ppermute | solution.py:26
  19.9 7.4 %collective-permute-start.8 = (bf16[1024,128]{1,0:T(8,128)(2,1)}, bf16[1024,128]{1,0:T(8,128)(2,1)}, u32[]{:S(2)}, u32[]{:S(2)}) collective-permute-start(bf16[1024,128]{1,0:T(8,128)(2,1)} %collective-permute-done.refs_4_), channel_id=1, source_target_pairs={{0,16},{8,24},{16,0},{24,8},{1,17},{9,25},{17,1},{25,9},{2,18},{10... | collective-permute-start | bytes 786440 | tf_op jit(solution)/shard_map/ppermute | solution.py:26
  24.1 20.3 %collective-permute-start.12 = (bf16[1024,128]{1,0:T(8,128)(2,1)S(1)}, bf16[1024,128]{1,0:T(8,128)(2,1)S(1)}, u32[]{:S(2)}, u32[]{:S(2)}) collective-permute-start(bf16[1024,128]{1,0:T(8,128)(2,1)S(1)} %get-tuple-element.75.refs_0_), channel_id=1, source_target_pairs={{0,8},{8,0},{16,24},{24,16},{1,9},{9,1},{17,25},{25,17},{2,10},{10... | collective-permute-start | bytes 786440 | tf_op jit(solution)/shard_map/ppermute | solution.py:26
  26.3 18.1 %collective-permute-start.13 = (bf16[1024,128]{1,0:T(8,128)(2,1)S(1)}, bf16[1024,128]{1,0:T(8,128)(2,1)S(1)}, u32[]{:S(2)}, u32[]{:S(2)}) collective-permute-start(bf16[1024,128]{1,0:T(8,128)(2,1)S(1)} %get-tuple-element.76.refs_1_), channel_id=1, source_target_pairs={{0,16},{8,24},{16,0},{24,8},{1,17},{9,25},{17,1},{25,9},{2,18},{10... | collective-permute-start | bytes 786440 | tf_op jit(solution)/shard_map/ppermute | solution.py:26
  27.4 15.1 %collective-permute-start.10 = (bf16[1024,128]{1,0:T(8,128)(2,1)}, bf16[1024,128]{1,0:T(8,128)(2,1)}, u32[]{:S(2)}, u32[]{:S(2)}) collective-permute-start(bf16[1024,128]{1,0:T(8,128)(2,1)} %collective-permute-done.8.refs_1_), channel_id=1, source_target_pairs={{0,1},{1,0},{2,3},{3,2},{4,5},{5,4},{6,7},{7,6},{8,9},{9,8},{10,11... | collective-permute-start | bytes 786440 | tf_op jit(solution)/shard_map/ppermute | solution.py:26
  30.9 18.9 %collective-permute-start.18 = (bf16[1024,128]{1,0:T(8,128)(2,1)S(1)}, bf16[1024,128]{1,0:T(8,128)(2,1)S(1)}, u32[]{:S(2)}, u32[]{:S(2)}) collective-permute-start(bf16[1024,128]{1,0:T(8,128)(2,1)S(1)} %get-tuple-element.75.refs_0_), channel_id=1, source_target_pairs={{0,16},{8,24},{16,0},{24,8},{1,17},{9,25},{17,1},{25,9},{2,18},{10... | collective-permute-start | bytes 786440 | tf_op jit(solution)/shard_map/ppermute | solution.py:26
  32.4 17.4 %collective-permute-start.17 = (bf16[1024,128]{1,0:T(8,128)(2,1)S(1)}, bf16[1024,128]{1,0:T(8,128)(2,1)S(1)}, u32[]{:S(2)}, u32[]{:S(2)}) collective-permute-start(bf16[1024,128]{1,0:T(8,128)(2,1)S(1)} %get-tuple-element.76.refs_1_), channel_id=1, source_target_pairs={{0,8},{8,0},{16,24},{24,16},{1,9},{9,1},{17,25},{25,17},{2,10},{10... | collective-permute-start | bytes 786440 | tf_op jit(solution)/shard_map/ppermute | solution.py:26
  44.4 10.4 %collective-permute-start.23 = (bf16[1024,128]{1,0:T(8,128)(2,1)S(1)}, bf16[1024,128]{1,0:T(8,128)(2,1)S(1)}, u32[]{:S(2)}, u32[]{:S(2)}) collective-permute-start(bf16[1024,128]{1,0:T(8,128)(2,1)S(1)} %collective-permute-done.12.refs_4_), channel_id=1, source_target_pairs={{0,16},{8,24},{16,0},{24,8},{1,17},{9,25},{17,1},{25,9},{2,18},{10... | collective-permute-start | bytes 786440 | tf_op jit(solution)/shard_map/ppermute | solution.py:26
  45.0 9.8 %collective-permute-start.24 = (bf16[1024,128]{1,0:T(8,128)(2,1)S(1)}, bf16[1024,128]{1,0:T(8,128)(2,1)S(1)}, u32[]{:S(2)}, u32[]{:S(2)}) collective-permute-start(bf16[1024,128]{1,0:T(8,128)(2,1)S(1)} %collective-permute-done.13.refs_9_), channel_id=1, source_target_pairs={{0,8},{8,0},{16,24},{24,16},{1,9},{9,1},{17,25},{25,17},{2,10},{10... | collective-permute-start | bytes 786440 | tf_op jit(solution)/shard_map/ppermute | solution.py:26
  54.8 23.7 %collective-permute-start.38 = (bf16[192,2048]{1,0:T(8,128)(2,1)S(1)}, bf16[192,2048]{1,0:T(8,128)(2,1)S(1)}, u32[]{:S(2)}, u32[]{:S(2)}) collective-permute-start(bf16[192,2048]{1,0:T(8,128)(2,1)S(1)} %copy-done.15), channel_id=1, source_target_pairs={{0,8},{8,0},{16,24},{24,16},{1,9},{9,1},{17,25},{25,17},{2,10},{10... | collective-permute-start | bytes 2359304 | tf_op jit(solution)/shard_map/ppermute | solution.py:26
  55.8 22.8 %collective-permute-start.39 = (bf16[192,2048]{1,0:T(8,128)(2,1)S(1)}, bf16[192,2048]{1,0:T(8,128)(2,1)S(1)}, u32[]{:S(2)}, u32[]{:S(2)}) collective-permute-start(bf16[192,2048]{1,0:T(8,128)(2,1)S(1)} %copy-done.14), channel_id=1, source_target_pairs={{0,16},{8,24},{16,0},{24,8},{1,17},{9,25},{17,1},{25,9},{2,18},{10... | collective-permute-start | bytes 2359304 | tf_op jit(solution)/shard_map/ppermute | solution.py:26
  65.0 11.0 %collective-permute-start.33 = (bf16[192,128]{1,0:T(8,128)(2,1)S(1)}, bf16[192,128]{1,0:T(8,128)(2,1)S(1)}, u32[]{:S(2)}, u32[]{:S(2)}) collective-permute-start(bf16[192,128]{1,0:T(8,128)(2,1)S(1)} %project.7.refs_0_), channel_id=1, source_target_pairs={{0,6},{1,7},{2,4},{3,5},{4,2},{5,3},{6,0},{7,1},{8,14},{9,15},{10,... | collective-permute-start | bytes 147464 | tf_op jit(solution)/shard_map/ppermute | solution.py:26
  66.8 9.2 %collective-permute-start.32 = (bf16[192,128]{1,0:T(8,128)(2,1)S(1)}, bf16[192,128]{1,0:T(8,128)(2,1)S(1)}, u32[]{:S(2)}, u32[]{:S(2)}) collective-permute-start(bf16[192,128]{1,0:T(8,128)(2,1)S(1)} %project.7.refs_0_), channel_id=1, source_target_pairs={{0,4},{1,5},{2,6},{3,7},{4,0},{5,1},{6,2},{7,3},{8,12},{9,13},{10,... | collective-permute-start | bytes 147464 | tf_op jit(solution)/shard_map/ppermute | solution.py:26
  67.1 8.9 %collective-permute-start.31 = (bf16[192,128]{1,0:T(8,128)(2,1)S(1)}, bf16[192,128]{1,0:T(8,128)(2,1)S(1)}, u32[]{:S(2)}, u32[]{:S(2)}) collective-permute-start(bf16[192,128]{1,0:T(8,128)(2,1)S(1)} %project.7.refs_0_), channel_id=1, source_target_pairs={{0,2},{1,3},{2,0},{3,1},{4,6},{5,7},{6,4},{7,5},{8,10},{9,11},{10,... | collective-permute-start | bytes 147464 | tf_op jit(solution)/shard_map/ppermute | solution.py:26
  78.5 9.0 %collective-permute-start.40 = (bf16[768,128]{1,0:T(8,128)(2,1)S(1)}, bf16[768,128]{1,0:T(8,128)(2,1)S(1)}, u32[]{:S(2)}, u32[]{:S(2)}) collective-permute-start(bf16[768,128]{1,0:T(8,128)(2,1)S(1)} %get-tuple-element.131), channel_id=1, source_target_pairs={{0,1},{1,0},{2,3},{3,2},{4,5},{5,4},{6,7},{7,6},{8,9},{9,8},{10,11... | collective-permute-start | bytes 589832 | tf_op jit(solution)/shard_map/ppermute | solution.py:26
  86.5 21.3 %collective-permute-start.48 = (bf16[192,2048]{1,0:T(8,128)(2,1)S(1)}, bf16[192,2048]{1,0:T(8,128)(2,1)S(1)}, u32[]{:S(2)}, u32[]{:S(2)}) collective-permute-start(bf16[192,2048]{1,0:T(8,128)(2,1)S(1)} %copy-done.13), channel_id=1, source_target_pairs={{0,24},{8,16},{16,8},{24,0},{1,25},{9,17},{17,9},{25,1},{2,26},{10... | collective-permute-start | bytes 2359304 | tf_op jit(solution)/shard_map/ppermute | solution.py:26
  99.6 9.0 %collective-permute-start.69 = (bf16[192,128]{1,0:T(8,128)(2,1)S(1)}, bf16[192,128]{1,0:T(8,128)(2,1)S(1)}, u32[]{:S(2)}, u32[]{:S(2)}) collective-permute-start(bf16[192,128]{1,0:T(8,128)(2,1)S(1)} %fusion.10.refs_4_.refs_1_), channel_id=1, source_target_pairs={{0,24},{8,16},{16,8},{24,0},{1,25},{9,17},{17,9},{25,1},{2,26},{10... | collective-permute-start | bytes 147464 | tf_op jit(solution)/shard_map/ppermute | solution.py:26
  101.5 7.6 %collective-permute-start.68 = (bf16[192,128]{1,0:T(8,128)(2,1)S(1)}, bf16[192,128]{1,0:T(8,128)(2,1)S(1)}, u32[]{:S(2)}, u32[]{:S(2)}) collective-permute-start(bf16[192,128]{1,0:T(8,128)(2,1)S(1)} %fusion.10.refs_4_.refs_1_), channel_id=1, source_target_pairs={{0,16},{8,24},{16,0},{24,8},{1,17},{9,25},{17,1},{25,9},{2,18},{10... | collective-permute-start | bytes 147464 | tf_op jit(solution)/shard_map/ppermute | solution.py:26
  102.3 6.8 %collective-permute-start.67 = (bf16[192,128]{1,0:T(8,128)(2,1)S(1)}, bf16[192,128]{1,0:T(8,128)(2,1)S(1)}, u32[]{:S(2)}, u32[]{:S(2)}) collective-permute-start(bf16[192,128]{1,0:T(8,128)(2,1)S(1)} %fusion.10.refs_4_.refs_1_), channel_id=1, source_target_pairs={{0,8},{8,0},{16,24},{24,16},{1,9},{9,1},{17,25},{25,17},{2,10},{10... | collective-permute-start | bytes 147464 | tf_op jit(solution)/shard_map/ppermute | solution.py:26
  111.0 13.7 %collective-permute-start.70 = (bf16[1024,128]{1,0:T(8,128)(2,1)S(1)}, bf16[1024,128]{1,0:T(8,128)(2,1)S(1)}, u32[]{:S(2)}, u32[]{:S(2)}) collective-permute-start(bf16[1024,128]{1,0:T(8,128)(2,1)S(1)} %get-tuple-element.144), channel_id=1, source_target_pairs={{0,1},{1,0},{2,3},{3,2},{4,5},{5,4},{6,7},{7,6},{8,9},{9,8},{10,11... | collective-permute-start | bytes 786440 | tf_op jit(solution)/shard_map/ppermute | solution.py:26
  113.0 21.7 %collective-permute-start.76 = (bf16[4096,128]{1,0:T(8,128)(2,1)S(1)}, bf16[4096,128]{1,0:T(8,128)(2,1)S(1)}, u32[]{:S(2)}, u32[]{:S(2)}) collective-permute-start(bf16[4096,128]{1,0:T(8,128)(2,1)S(1)} %get-tuple-element.146), channel_id=1, source_target_pairs={{0,1},{1,0},{2,3},{3,2},{4,5},{5,4},{6,7},{7,6},{8,9},{9,8},{10,11... | collective-permute-start | bytes 3145736 | tf_op jit(solution)/shard_map/ppermute | solution.py:26
  124.1 20.2 %collective-permute-start.58 = (bf16[4096,128]{1,0:T(8,128)(2,1)S(1)}, bf16[4096,128]{1,0:T(8,128)(2,1)S(1)}, u32[]{:S(2)}, u32[]{:S(2)}) collective-permute-start(bf16[4096,128]{1,0:T(8,128)(2,1)S(1)} %get-tuple-element.141), channel_id=1, source_target_pairs={{0,1},{1,0},{2,3},{3,2},{4,5},{5,4},{6,7},{7,6},{8,9},{9,8},{10,11... | collective-permute-start | bytes 3145736 | tf_op jit(solution)/shard_map/ppermute | solution.py:26
  124.9 8.1 %collective-permute-start.53 = (bf16[512,128]{1,0:T(8,128)(2,1)S(1)}, bf16[512,128]{1,0:T(8,128)(2,1)S(1)}, u32[]{:S(2)}, u32[]{:S(2)}) collective-permute-start(bf16[512,128]{1,0:T(8,128)(2,1)S(1)} %slice.180), channel_id=1, source_target_pairs={{0,2},{1,3},{2,0},{3,1},{4,6},{5,7},{6,4},{7,5},{8,10},{9,11},{10,... | collective-permute-start | bytes 393224 | tf_op jit(solution)/shard_map/ppermute | solution.py:26
  131.2 11.0 %collective-permute-start.72 = (bf16[512,128]{1,0:T(8,128)(2,1)S(1)}, bf16[512,128]{1,0:T(8,128)(2,1)S(1)}, u32[]{:S(2)}, u32[]{:S(2)}) collective-permute-start(bf16[512,128]{1,0:T(8,128)(2,1)S(1)} %fusion.6), channel_id=1, source_target_pairs={{0,4},{1,5},{2,6},{3,7},{4,0},{5,1},{6,2},{7,3},{8,12},{9,13},{10,... | collective-permute-start | bytes 393224 | tf_op jit(solution)/shard_map/ppermute | solution.py:26
  133.1 11.2 %collective-permute-start.54 = (bf16[512,128]{1,0:T(8,128)(2,1)S(1)}, bf16[512,128]{1,0:T(8,128)(2,1)S(1)}, u32[]{:S(2)}, u32[]{:S(2)}) collective-permute-start(bf16[512,128]{1,0:T(8,128)(2,1)S(1)} %fusion.4), channel_id=1, source_target_pairs={{0,4},{1,5},{2,6},{3,7},{4,0},{5,1},{6,2},{7,3},{8,12},{9,13},{10,... | collective-permute-start | bytes 393224 | tf_op jit(solution)/shard_map/ppermute | solution.py:26
  135.1 9.6 %collective-permute-start.77 = (bf16[1024,128]{1,0:T(8,128)(2,1)S(1)}, bf16[1024,128]{1,0:T(8,128)(2,1)S(1)}, u32[]{:S(2)}, u32[]{:S(2)}) collective-permute-start(bf16[1024,128]{1,0:T(8,128)(2,1)S(1)} %get-tuple-element.157), channel_id=1, source_target_pairs={{0,8},{8,0},{16,24},{24,16},{1,9},{9,1},{17,25},{25,17},{2,10},{10... | collective-permute-start | bytes 786440 | tf_op jit(solution)/shard_map/ppermute | solution.py:26
  136.1 11.4 %collective-permute-start.79 = (bf16[1024,128]{1,0:T(8,128)(2,1)S(1)}, bf16[1024,128]{1,0:T(8,128)(2,1)S(1)}, u32[]{:S(2)}, u32[]{:S(2)}) collective-permute-start(bf16[1024,128]{1,0:T(8,128)(2,1)S(1)} %get-tuple-element.158), channel_id=1, source_target_pairs={{0,24},{8,16},{16,8},{24,0},{1,25},{9,17},{17,9},{25,1},{2,26},{10... | collective-permute-start | bytes 786440 | tf_op jit(solution)/shard_map/ppermute | solution.py:26
  142.2 10.3 %collective-permute-start.78 = (bf16[1024,128]{1,0:T(8,128)(2,1)S(1)}, bf16[1024,128]{1,0:T(8,128)(2,1)S(1)}, u32[]{:S(2)}, u32[]{:S(2)}) collective-permute-start(bf16[1024,128]{1,0:T(8,128)(2,1)S(1)} %get-tuple-element.159), channel_id=1, source_target_pairs={{0,16},{8,24},{16,0},{24,8},{1,17},{9,25},{17,1},{25,9},{2,18},{10... | collective-permute-start | bytes 786440 | tf_op jit(solution)/shard_map/ppermute | solution.py:26
  144.2 35.7 %collective-permute-start.74 = (bf16[512,128]{1,0:T(8,128)(2,1)S(1)}, bf16[512,128]{1,0:T(8,128)(2,1)S(1)}, u32[]{:S(2)}, u32[]{:S(2)}) collective-permute-start(bf16[512,128]{1,0:T(8,128)(2,1)S(1)} %add_convert_fusion.1.refs_0_), channel_id=1, source_target_pairs={{0,1},{1,0},{2,3},{3,2},{4,5},{5,4},{6,7},{7,6},{8,9},{9,8},{10,11... | collective-permute-start | bytes 393224 | tf_op jit(solution)/shard_map/ppermute | solution.py:26
  144.3 9.3 %collective-permute-start.73 = (bf16[512,128]{1,0:T(8,128)(2,1)S(1)}, bf16[512,128]{1,0:T(8,128)(2,1)S(1)}, u32[]{:S(2)}, u32[]{:S(2)}) collective-permute-start(bf16[512,128]{1,0:T(8,128)(2,1)S(1)} %add_convert_fusion.1.refs_0_), channel_id=1, source_target_pairs={{0,2},{1,3},{2,0},{3,1},{4,6},{5,7},{6,4},{7,5},{8,10},{9,11},{10,... | collective-permute-start | bytes 393224 | tf_op jit(solution)/shard_map/ppermute | solution.py:26
  144.7 9.2 %collective-permute-start.59 = (bf16[1024,128]{1,0:T(8,128)(2,1)S(1)}, bf16[1024,128]{1,0:T(8,128)(2,1)S(1)}, u32[]{:S(2)}, u32[]{:S(2)}) collective-permute-start(bf16[1024,128]{1,0:T(8,128)(2,1)S(1)} %get-tuple-element.160), channel_id=1, source_target_pairs={{0,8},{8,0},{16,24},{24,16},{1,9},{9,1},{17,25},{25,17},{2,10},{10... | collective-permute-start | bytes 786440 | tf_op jit(solution)/shard_map/ppermute | solution.py:26
  147.5 11.7 %collective-permute-start.61 = (bf16[1024,128]{1,0:T(8,128)(2,1)S(1)}, bf16[1024,128]{1,0:T(8,128)(2,1)S(1)}, u32[]{:S(2)}, u32[]{:S(2)}) collective-permute-start(bf16[1024,128]{1,0:T(8,128)(2,1)S(1)} %get-tuple-element.161), channel_id=1, source_target_pairs={{0,24},{8,16},{16,8},{24,0},{1,25},{9,17},{17,9},{25,1},{2,26},{10... | collective-permute-start | bytes 786440 | tf_op jit(solution)/shard_map/ppermute | solution.py:26
  152.5 12.3 %collective-permute-start.60 = (bf16[1024,128]{1,0:T(8,128)(2,1)S(1)}, bf16[1024,128]{1,0:T(8,128)(2,1)S(1)}, u32[]{:S(2)}, u32[]{:S(2)}) collective-permute-start(bf16[1024,128]{1,0:T(8,128)(2,1)S(1)} %get-tuple-element.162), channel_id=1, source_target_pairs={{0,16},{8,24},{16,0},{24,8},{1,17},{9,25},{17,1},{25,9},{2,18},{10... | collective-permute-start | bytes 786440 | tf_op jit(solution)/shard_map/ppermute | solution.py:26
  153.6 28.4 %collective-permute-start.55 = (bf16[512,128]{1,0:T(8,128)(2,1)S(1)}, bf16[512,128]{1,0:T(8,128)(2,1)S(1)}, u32[]{:S(2)}, u32[]{:S(2)}) collective-permute-start(bf16[512,128]{1,0:T(8,128)(2,1)S(1)} %add_convert_fusion.3.refs_0_), channel_id=1, source_target_pairs={{0,2},{1,3},{2,0},{3,1},{4,6},{5,7},{6,4},{7,5},{8,10},{9,11},{10,... | collective-permute-start | bytes 393224 | tf_op jit(solution)/shard_map/ppermute | solution.py:26
  153.9 32.3 %collective-permute-start.75 = (bf16[512,128]{1,0:T(8,128)(2,1)S(1)}, bf16[512,128]{1,0:T(8,128)(2,1)S(1)}, u32[]{:S(2)}, u32[]{:S(2)}) collective-permute-start(bf16[512,128]{1,0:T(8,128)(2,1)S(1)} %collective-permute-done.73.refs_1_), channel_id=1, source_target_pairs={{0,1},{1,0},{2,3},{3,2},{4,5},{5,4},{6,7},{7,6},{8,9},{9,8},{10,11... | collective-permute-start | bytes 393224 | tf_op jit(solution)/shard_map/ppermute | solution.py:26
  164.9 7.5 %collective-permute-start.62 = (bf16[512,128]{1,0:T(8,128)(2,1)S(1)}, bf16[512,128]{1,0:T(8,128)(2,1)S(1)}, u32[]{:S(2)}, u32[]{:S(2)}) collective-permute-start(bf16[512,128]{1,0:T(8,128)(2,1)S(1)} %slice.179), channel_id=1, source_target_pairs={{0,2},{1,3},{2,0},{3,1},{4,6},{5,7},{6,4},{7,5},{8,10},{9,11},{10,... | collective-permute-start | bytes 393224 | tf_op jit(solution)/shard_map/ppermute | solution.py:26
  165.0 12.7 %collective-permute-start.81 = (bf16[512,128]{1,0:T(8,128)(2,1)S(1)}, bf16[512,128]{1,0:T(8,128)(2,1)S(1)}, u32[]{:S(2)}, u32[]{:S(2)}) collective-permute-start(bf16[512,128]{1,0:T(8,128)(2,1)S(1)} %fusion.7), channel_id=1, source_target_pairs={{0,4},{1,5},{2,6},{3,7},{4,0},{5,1},{6,2},{7,3},{8,12},{9,13},{10,... | collective-permute-start | bytes 393224 | tf_op jit(solution)/shard_map/ppermute | solution.py:26
  172.4 7.5 %collective-permute-start.63 = (bf16[512,128]{1,0:T(8,128)(2,1)S(1)}, bf16[512,128]{1,0:T(8,128)(2,1)S(1)}, u32[]{:S(2)}, u32[]{:S(2)}) collective-permute-start(bf16[512,128]{1,0:T(8,128)(2,1)S(1)} %fusion.5), channel_id=1, source_target_pairs={{0,4},{1,5},{2,6},{3,7},{4,0},{5,1},{6,2},{7,3},{8,12},{9,13},{10,... | collective-permute-start | bytes 393224 | tf_op jit(solution)/shard_map/ppermute | solution.py:26
  177.8 8.9 %collective-permute-start.83 = (bf16[512,128]{1,0:T(8,128)(2,1)S(1)}, bf16[512,128]{1,0:T(8,128)(2,1)S(1)}, u32[]{:S(2)}, u32[]{:S(2)}) collective-permute-start(bf16[512,128]{1,0:T(8,128)(2,1)S(1)} %add_convert_fusion.refs_4_), channel_id=1, source_target_pairs={{0,1},{1,0},{2,3},{3,2},{4,5},{5,4},{6,7},{7,6},{8,9},{9,8},{10,11... | collective-permute-start | bytes 393224 | tf_op jit(solution)/shard_map/ppermute | solution.py:26
  180.0 7.6 %collective-permute-start.64 = (bf16[512,128]{1,0:T(8,128)(2,1)S(1)}, bf16[512,128]{1,0:T(8,128)(2,1)S(1)}, u32[]{:S(2)}, u32[]{:S(2)}) collective-permute-start(bf16[512,128]{1,0:T(8,128)(2,1)S(1)} %add_convert_fusion.2.refs_4_), channel_id=1, source_target_pairs={{0,2},{1,3},{2,0},{3,1},{4,6},{5,7},{6,4},{7,5},{8,10},{9,11},{10,... | collective-permute-start | bytes 393224 | tf_op jit(solution)/shard_map/ppermute | solution.py:26
  182.1 7.6 %collective-permute-start.56 = (bf16[512,128]{1,0:T(8,128)(2,1)S(1)}, bf16[512,128]{1,0:T(8,128)(2,1)S(1)}, u32[]{:S(2)}, u32[]{:S(2)}) collective-permute-start(bf16[512,128]{1,0:T(8,128)(2,1)S(1)} %add_convert_fusion.3.refs_0_), channel_id=1, source_target_pairs={{0,1},{1,0},{2,3},{3,2},{4,5},{5,4},{6,7},{7,6},{8,9},{9,8},{10,11... | collective-permute-start | bytes 393224 | tf_op jit(solution)/shard_map/ppermute | solution.py:26
  (55 other events, 318.6 us)

commit v4 on v1

v4 whole, which is shorter than its diff:
```python
import functools
import math

import jax
import jax.numpy as jnp
from jax import lax
from jax.experimental import pallas as pl
from jax.experimental.pallas import tpu as pltpu
from jax.sharding import PartitionSpec as P

VMEM_LIMIT = 28 * 1024 * 1024
NO_COST = pl.CostEstimate(flops=0, bytes_accessed=0, transcendentals=0)


def moved_rows(block_rows):
    return block_rows * 10 // 16 // 256 * 256


class Plan:
    def __init__(self, **fields):
        self.__dict__.update(fields)


def swap(array, axis, distance):
    count = lax.axis_size(axis)
    return lax.ppermute(array, axis, [(i, i ^ distance) for i in range(count)])


def after(arrays, *earlier):
    tied = lax.optimization_barrier((tuple(arrays), tuple(earlier)))
    return list(tied[0]), list(tied[1])


def shape_of(rows, width, kind=jnp.bfloat16):
    return jax.ShapeDtypeStruct((rows, width), kind)


def kernel_call(kernel, name, outs, scalars, arrays, scratch=(), cost=NO_COST):
    smem = pl.BlockSpec(memory_space=pltpu.SMEM)
    vmem = pl.BlockSpec(memory_space=pltpu.VMEM)
    single = not isinstance(outs, tuple)
    return pl.pallas_call(
        kernel,
        out_shape=outs,
        in_specs=[smem] * len(scalars) + [vmem] * len(arrays),
        out_specs=vmem if single else (vmem,) * len(outs),
        scratch_shapes=list(scratch),
        compiler_params=pltpu.CompilerParams(vmem_limit_bytes=VMEM_LIMIT),
        cost_estimate=cost,
        name=name,
    )(*scalars, *arrays)


def bytes_cost(amount):
    return pl.CostEstimate(flops=0, bytes_accessed=amount, transcendentals=0)


TN = (((0,), (0,)), ((), ()))


def attention_kernel(
    shape, ids, order, lengths, q_ref, g_ref, *refs
):
    ctx_count, stretch_rows, head_count, head_dim, window, chunk = shape
    kv_refs = refs[:ctx_count]
    qgrad_ref, keep_ref, send_ref, keys, values, total, qs, gs, dqs = refs[ctx_count:]
    me = ids[0]
    row_count = 2 * stretch_rows
    stretch_count = 2 * ctx_count
    score_scale = 1.0 / math.sqrt(head_dim)

    def place(device, half):
        return pl.multiple_of(order[2 * device + half] * stretch_rows, stretch_rows)

    for index in range(ctx_count):
        for half in range(2):
            rows = pl.ds(place(me ^ index, half), stretch_rows)
            block = kv_refs[index][half * stretch_rows : (half + 1) * stretch_rows, :]
            keys[rows, :] = block[:, :head_dim]
            values[rows, :] = block[:, head_dim:]
    total[...] = jnp.zeros_like(total)
    for half in range(2):
        for head in range(head_count):
            to = slice((half * head_count + head) * stretch_rows, (half * head_count + head + 1) * stretch_rows)
            rows = slice(half * stretch_rows, (half + 1) * stretch_rows)
            columns = slice(head * head_dim, (head + 1) * head_dim)
            qs[to, :] = q_ref[rows, columns]
            gs[to, :] = g_ref[rows, columns]
    ends = []
    running = 0
    for at in range(lengths.shape[0]):
        running = running + lengths[at]
        ends.append(running)
    chunks_half = head_count * stretch_rows // chunk

    def step(at, carry):
        half = at // chunks_half
        block = order[2 * me + half]
        first = jnp.maximum(block - stretch_count // 2, 0) * stretch_rows
        first = pl.multiple_of(first, stretch_rows)
        part = pl.ds(pl.multiple_of(at * chunk, chunk), chunk)
        inside = (at - half * chunks_half) * chunk + lax.broadcasted_iota(jnp.int32, (1, chunk), 1)
        at_query = block * stretch_rows + lax.rem(inside, stretch_rows)
        begin = jnp.zeros_like(at_query)
        for end in ends:
            begin = jnp.where(at_query >= end, end, begin)
        at_key = first + lax.broadcasted_iota(jnp.int32, (window, chunk), 0)
        allowed = (at_key >= begin) & (at_key <= at_query)
        k = keys[pl.ds(first, window), :]
        v = values[pl.ds(first, window), :]
        q = qs[part, :]
        g = gs[part, :]
        last = (((1,), (1,)), ((), ()))
        scores = lax.dot_general(k, q, last, preferred_element_type=jnp.float32) * score_scale
        masked = jnp.where(allowed, scores, -jnp.inf)
        expsum = jnp.exp(masked - jnp.max(masked, axis=0, keepdims=True))
        probs = expsum * (1.0 / jnp.sum(expsum, axis=0, keepdims=True))
        probs_low = probs.astype(jnp.bfloat16)
        dprob = lax.dot_general(v, g, last, preferred_element_type=jnp.float32)
        delta = jnp.sum(probs_low.astype(jnp.float32) * dprob, axis=0, keepdims=True)
        dscore = (probs * (dprob - delta)).astype(jnp.bfloat16)
        dq = lax.dot_general(
            k, dscore, (((0,), (0,)), ((), ())), preferred_element_type=jnp.float32
        )
        dqs[part, :] = (jnp.transpose(dq) * score_scale).astype(jnp.bfloat16)
        dk = jnp.dot(dscore, q, preferred_element_type=jnp.float32) * score_scale
        dv = jnp.dot(probs_low, g, preferred_element_type=jnp.float32)
        total[pl.ds(first, window), :head_dim] += dk
        total[pl.ds(first, window), head_dim:] += dv
        return carry

    lax.fori_loop(0, 2 * chunks_half, step, 0)
    for half in range(2):
        for head in range(head_count):
            origin = slice((half * head_count + head) * stretch_rows, (half * head_count + head + 1) * stretch_rows)
            rows = slice(half * stretch_rows, (half + 1) * stretch_rows)
            columns = slice(head * head_dim, (head + 1) * head_dim)
            qgrad_ref[rows, columns] = dqs[origin, :]
    for index in range(ctx_count):
        for half in range(2):
            rows = pl.ds(place(me ^ index, half), stretch_rows)
            start = (index // 2) * row_count + half * stretch_rows
            if index % 2:
                send_ref[start : start + stretch_rows, :] = total[rows, :].astype(jnp.bfloat16)
            else:
                keep_ref[start : start + stretch_rows, :] = total[rows, :]


def attention(me, order, lengths, queries, cotangent, kv_blocks, head_dim):
    row_count, width = queries.shape
    ctx_count = len(kv_blocks)
    stretch_rows = row_count // 2
    head_count = width // head_dim
    seq_rows = row_count * ctx_count
    window = seq_rows // 2 + stretch_rows
    stacked = head_count * stretch_rows
    chunk = 256 if stacked % 256 == 0 else 128
    shape = (ctx_count, stretch_rows, head_count, head_dim, window, chunk)
    smem = pl.BlockSpec(memory_space=pltpu.SMEM)
    vmem = pl.BlockSpec(memory_space=pltpu.VMEM)
    half_rows = seq_rows // 2
    return pl.pallas_call(
        functools.partial(attention_kernel, shape),
        out_shape=(
            jax.ShapeDtypeStruct((row_count, width), jnp.bfloat16),
            jax.ShapeDtypeStruct((half_rows, 2 * head_dim), jnp.float32),
            jax.ShapeDtypeStruct((half_rows, 2 * head_dim), jnp.bfloat16),
        ),
        in_specs=[smem] * 3 + [vmem] * (2 + ctx_count),
        out_specs=(vmem,) * 3,
        scratch_shapes=[
            pltpu.VMEM((seq_rows, head_dim), jnp.bfloat16),
            pltpu.VMEM((seq_rows, head_dim), jnp.bfloat16),
            pltpu.VMEM((seq_rows, 2 * head_dim), jnp.float32),
            pltpu.VMEM((2 * stacked, head_dim), jnp.bfloat16),
            pltpu.VMEM((2 * stacked, head_dim), jnp.bfloat16),
            pltpu.VMEM((2 * stacked, head_dim), jnp.bfloat16),
        ],
        compiler_params=pltpu.CompilerParams(vmem_limit_bytes=VMEM_LIMIT),
        cost_estimate=NO_COST,
        name="attention",
    )(me, order, lengths, queries, cotangent, *kv_blocks)


def project_kernel(plan, ids, hidden, *refs):
    out_ref = refs[-1]
    dp, core = ids[2], ids[1]
    if plan.start:
        total = refs[0][...]
    else:
        columns = pl.ds(pl.multiple_of(dp * plan.block_rows, plan.block_rows), plan.block_rows)
        total = jnp.concatenate(
            [
                jnp.dot(hidden[:, columns], own[...], preferred_element_type=jnp.float32)
                for own in refs[:2]
            ],
            axis=1,
        )
    for (block, side, offset), weight in zip(plan.terms, refs[1 if plan.start else 2 : -1]):
        from_column = (dp ^ block) * plan.block_rows + (core ^ side) * plan.side_rows + offset
        columns = pl.ds(pl.multiple_of(from_column, 128), weight.shape[0])
        total += jnp.dot(hidden[:, columns], weight[...], preferred_element_type=jnp.float32)
    out_ref[...] = total.astype(out_ref.dtype)


def project(ids, begin, inputs, block_rows, pieces, kind, cost=NO_COST):
    names = sorted(pieces)
    weights = [pieces[name] for name in names]
    plan = Plan(
        terms=names, start=len(begin) == 1, block_rows=block_rows, side_rows=block_rows // 2
    )
    return kernel_call(
        functools.partial(project_kernel, plan),
        "project",
        shape_of(inputs.shape[0], weights[0].shape[1], kind),
        (ids,),
        (inputs, *begin, *weights),
        cost=cost,
    )


def weight_kernel(plan, ids, *refs):
    hidden = refs[: plan.hidden]
    grads = refs[plan.hidden : -2]
    z, core, dp = ids[0] % plan.sub_count, ids[1], ids[2]
    rows = plan.rows
    share = rows // plan.sub_count
    tile = next(size for size in (512, 256, 128) if rows % size == 0)
    step = math.gcd(share, tile)
    for side, out_ref in ((1, refs[-2]), (0, refs[-1])):
        for at, group in enumerate(plan.groups):
            for start in range(0, rows, tile):
                product = None
                for array, block, grad in group:
                    origin = plan.origin + (core ^ side) * rows + start
                    if block is not None:
                        origin = origin + (dp ^ block) * plan.block_rows
                    columns = pl.ds(pl.multiple_of(origin, 128), tile)
                    term = lax.dot_general(
                        hidden[array][:, columns],
                        grads[grad][...],
                        TN,
                        preferred_element_type=jnp.float32,
                    )
                    product = term if product is None else product + term
                for inner in range(0, tile, step):
                    part, offset = divmod(start + inner, share)
                    to = pl.multiple_of(at * rows + (z ^ part) * share + offset, step)
                    piece = product[inner : inner + step, :]
                    out_ref[pl.ds(to, step), :] = piece.astype(out_ref.dtype)


def weight_rows(ids, hidden, grads, groups, origin, rows, block_rows, sub_count):
    plan = Plan(
        hidden=len(hidden),
        groups=groups,
        origin=origin,
        rows=rows,
        block_rows=block_rows,
        sub_count=sub_count,
    )
    out = shape_of(rows * len(groups), grads[0].shape[1])
    theirs, ours = kernel_call(
        functools.partial(weight_kernel, plan),
        "weight_rows",
        (out, out),
        (ids,),
        (*hidden, *grads),
        cost=bytes_cost(1 << 23),
    )
    return ours.astype(jnp.float32) + swap(theirs, "ctx", 1).astype(jnp.float32)


def send_over_dp(array):
    count = lax.axis_size("dp")
    rows = array.shape[0] // count
    leaving = [array[j * rows : (j + 1) * rows] for j in range(count)]
    return leaving[:1] + [
        swap(one.astype(jnp.bfloat16), "dp", j) for j, one in enumerate(leaving) if j
    ]


def sum_of(arrays):
    total = arrays[0]
    for one in arrays[1:]:
        total = total + one.astype(jnp.float32)
    return total


def z_bits(sub_count):
    return [1 << at for at in range(sub_count.bit_length() - 1)]


def scatter_along_z(full, sub_count):
    share = full.shape[0] // sub_count
    parts = {m: full[m * share : (m + 1) * share] for m in range(sub_count)}
    for bit in z_bits(sub_count):
        for m in list(parts):
            if m & bit:
                came = swap(parts.pop(m).astype(jnp.bfloat16), "ctx", 2 * bit)
                parts[m ^ bit] = parts[m ^ bit] + came.astype(jnp.float32)
    return parts[0]


def sum_of_halves(part, sub_count):
    low = swap(part.astype(jnp.bfloat16), "ctx", 2 * sub_count)
    return (part + low.astype(jnp.float32)).astype(jnp.bfloat16)


def gather_parts(part, sub_count):
    rows = {0: part}
    for bit in z_bits(sub_count)[::-1]:
        rows.update({m | bit: swap(one, "ctx", 2 * bit) for m, one in list(rows.items())})
    own = [rows[m] for m in range(sub_count)]
    return own + [swap(one, "ctx", 1) for one in own]


def assemble_kernel(sub_count, regions, ids, *refs):
    key_ref, value_ref = refs[-2:]
    blocks = iter(refs[:-2])
    z, core = ids[0] % sub_count, ids[1]
    for origin, rows in regions:
        share = rows // sub_count
        for side in range(2):
            for m in range(sub_count):
                to = origin + (core ^ side) * rows + (z ^ m) * share
                to = pl.multiple_of(to, share)
                block_ref = next(blocks)
                width = block_ref.shape[1] // 2
                key_ref[pl.ds(to, share), :] = block_ref[:, :width].astype(jnp.float32)
                value_ref[pl.ds(to, share), :] = block_ref[:, width:].astype(jnp.float32)


def assemble(ids, blocks, sub_count, regions):
    rows = sum(block.shape[0] for block in blocks)
    out = shape_of(rows, blocks[0].shape[1] // 2, jnp.float32)
    return kernel_call(
        functools.partial(assemble_kernel, sub_count, regions),
        "assemble",
        (out, out),
        (ids,),
        blocks,
    )


def on_device(hidden_in, queries, grad_out, w_key, w_value, stretch_order, doc_lengths):
    inputs = hidden_in[0]
    head_dim = w_key.shape[1]
    dp_count = lax.axis_size("dp")
    ctx_count = lax.axis_size("ctx")
    z_count = ctx_count // 2
    sub_count = z_count // 2
    dp, ctx = lax.axis_index("dp"), lax.axis_index("ctx")
    z, core = ctx // 2, ctx % 2
    ids = jnp.stack([z, core, dp]).astype(jnp.int32)
    me = jnp.reshape(ctx, (1,)).astype(jnp.int32)
    block_rows = w_key.shape[0]
    half_rows = block_rows // 2
    quarter = half_rows // 2
    bits = [1 << at for at in range(dp_count.bit_length() - 1)]
    near = [j for j in range(1, dp_count) if j in bits]
    far = [j for j in range(1, dp_count) if j not in bits]

    def gather_near(*weights):
        halves = [
            lax.dynamic_slice_in_dim(weight, core * half_rows, half_rows, 0) for weight in weights
        ]
        mine = jnp.concatenate(halves, axis=1)
        return {(j, 0, 0): swap(mine, "dp", j) for j in near}

    def gather_far(landed):
        pieces = {}
        for j in far:
            for offset, bit in ((0, 1 << (j.bit_length() - 1)), (quarter, j & -j)):
                if (j ^ bit) in near:
                    origin = landed[j ^ bit, 0, 0][offset : offset + quarter]
                else:
                    origin = pieces[j ^ bit, 0, offset]
                pieces[j, 0, offset] = swap(origin, "dp", bit)
        return pieces

    def from_other_core(pieces):
        return {(j, 1, offset): swap(one, "ctx", 1) for (j, _, offset), one in pieces.items()}

    def hold(arrays, pieces):
        names = list(pieces)
        tied, ended = after(arrays, *[pieces[name] for name in names])
        pieces.update(zip(names, ended))
        return tied

    def gather_along_z(own):
        return [swap(own, "ctx", 2 * m) if m else own for m in range(z_count)]

    def both_cores(along):
        return [block for one in along for block in (one, swap(one, "ctx", 1))]

    first_rows = moved_rows(block_rows)
    first_half, last_half = first_rows // 2, (block_rows - first_rows) // 2
    regions = ((0, first_half), (first_rows, last_half))
    moving = {
        j: lax.dynamic_slice_in_dim(inputs, (dp ^ j) * block_rows, first_rows, 1)
        for j in range(dp_count)
    }

    near_pieces = gather_near(w_key, w_value)
    far_pieces = gather_far(near_pieces)
    near_pieces.update(from_other_core(near_pieces))
    early = project(
        ids, (w_key, w_value), inputs, block_rows, near_pieces, jnp.float32, bytes_cost(1 << 24)
    )
    others = near + far
    early, *tied = hold([early] + [moving[j] for j in others], far_pieces)
    moving.update(zip(others, tied))
    far_pieces.update(from_other_core(far_pieces))
    own = project(ids, (early,), inputs, block_rows, far_pieces, jnp.bfloat16)
    moved = {0: moving[0]}
    moved.update({j: swap(moving[j], "dp", j) for j in near})
    along = gather_along_z(own)
    along, _ = after(along)
    kv_blocks = both_cores(along)

    query_grad, keep, send = attention(
        me, stretch_order, doc_lengths[0], queries[0], grad_out[0], kv_blocks, head_dim
    )
    ready, ended = after([send] + [moving[j] for j in far], *[moved[j] for j in near])
    send = ready[0]
    moved.update(zip(near, ended))
    moved.update({j: swap(one, "dp", j) for j, one in zip(far, ready[1:])})

    chip = keep + swap(send, "ctx", 1).astype(jnp.float32)
    rows = chip.shape[0] // z_count
    grad = chip[:rows]
    for m in range(1, z_count):
        leaving = chip[m * rows : (m + 1) * rows].astype(jnp.bfloat16)
        grad = grad + swap(leaving, "ctx", 2 * m).astype(jnp.float32)
    grad = grad.astype(jnp.bfloat16)
    grads = [grad] + [swap(grad, "dp", j) for j in range(1, dp_count)]

    (grad,), ended = after([grad], *grads[1:], *[moved[j] for j in far])
    grads[1:] = ended[: dp_count - 1]
    moved.update(zip(far, ended[dp_count - 1 :]))
    groups = [[(0, j, 0)] for j in range(dp_count)]
    last = weight_rows(
        ids, [inputs], [grad], groups, first_rows, last_half, block_rows, sub_count
    )
    last = send_over_dp(last)
    groups = [[(j, None, j) for j in range(dp_count)]]
    arrays = [moved[j] for j in range(dp_count)]
    first = weight_rows(ids, arrays, grads, groups, 0, first_half, block_rows, sub_count)
    first = scatter_along_z(first, sub_count)
    first = sum_of_halves(first, sub_count)
    last, _ = after(last, first)
    last = sum_of_halves(scatter_along_z(sum_of(last), sub_count), sub_count)
    blocks = gather_parts(first, sub_count) + gather_parts(last, sub_count)
    key_rows, value_rows = assemble(ids, blocks, sub_count, regions)
    return query_grad[None], key_rows, value_rows


def solution(mesh):
    return jax.shard_map(
        on_device,
        mesh=mesh,
        in_specs=(
            P("dp", "ctx", None),
            P("dp", "ctx", None),
            P("dp", "ctx", None),
            P("dp", None),
            P("dp", None),
            P(),
            P("dp", None),
        ),
        out_specs=(P("dp", "ctx", None), P("dp", None), P("dp", None)),
        check_vma=False,
    )
```

time: 220 us -> 171 us (0.78)
  waiting for transfers between devices: 134 us -> 108 us
  matrix products: 15.5 us -> 0 us
  starting transfers between devices: 41.6 us -> 33.3 us
  Pallas kernels: 17.8 us -> 21 us
    ppermute x43 -> x40, waiting for transfers between devices: 134 us -> 108 us  [swap(): return lax.ppermute(array, axis, [(i, i ^ distance) for i in range(count)])]
    dot_general x16 -> x0, matrix products: 15.5 us -> none  [dot32(): return jnp.dot(left, right, preferred_element_type=jnp.float32)]
    ppermute x43 -> x40, starting transfers between devices: 41.6 us -> 33.3 us  [swap(): return lax.ppermute(array, axis, [(i, i ^ distance) for i in range(count)])]
    pallas_call x3 -> x5, Pallas kernels: 8.2 us -> 11.5 us  [kernel_call(): pl.pallas_call(kernel, out_shape=outs, in_specs=[smem] * len(scalars) + [...]
    dynamic_slice x3 -> x2, local copies, waits for them, and re-layouts: 6.88 us -> 3.77 us  [the longest x1 2.49 us: on_device(): lax.dynamic_slice_in_dim(inputs, (dp ^ j) * block_rows, first_rows, 1)]
  transfers between devices with their start and end apart: 43 -> 40, of which waited for: 25 -> 25; matrix products, arithmetic and copies ran while one was open for 10% -> 3% of each run, Pallas kernels for 1% -> 9%
where the time goes in v4:
time: 171 us
  waiting for transfers between devices  108 us (63%)
  starting transfers between devices  33.3 us (19%)
  Pallas kernels  21 us (12%)
  local copies, waits for them, and re-layouts  6.56 us (4%)
    ppermute x40, waiting for transfers between devices, swap(): return lax.ppermute(array, axis, [(i, i ^ distance) for i in range(count)])  108 us
    ppermute x40, starting transfers between devices, swap(): return lax.ppermute(array, axis, [(i, i ^ distance) for i in range(count)])  33.3 us
    pallas_call x5, Pallas kernels, kernel_call(): pl.pallas_call(kernel, out_shape=outs, in_specs=[smem] * len(scalars) + [...  11.5 us
    pallas_call x1, Pallas kernels, attention(): pl.pallas_call(functools.partial(attention_kernel, shape), out_shape=(jax...  9.59 us
  transfers between devices with their start and end apart: 40, of which 25 were waited for; matrix products, arithmetic and copies ran while one was open for 3% of the time, Pallas kernels for 9%

profile of v4, /device:TPU:0, one launch (start us, length us, event | category | flops | bytes accessed | tf_op | source)
XLA Modules:
  0.0 171.1 jit_solution(7260294049105026455)
XLA Ops:
  0.6 1.3 constant_dynamic-slice_fusion
  2.1 3.0 %collective-permute-start.2 = (bf16[2048,256]{1,0:T(8,128)(2,1)S(1)}, bf16[2048,256]{1,0:T(8,128)(2,1)S(1)}, u32[]{:S(2)}, u32[]{:S(2)}) collective-permute-start(bf16[2048,256]{1,0:T(8,128)(2,1)S(1)} %pad_maximum_fusion), channel_id=1, source_target_pairs={{0,16},{8,24},{16,0},{24,8},{1,17},{9,25},{17,1},{25,9},{2,18},{10... | collective-permute-start | bytes 3145736 | tf_op jit(solution)/shard_map/ppermute | solution.py:26
  5.1 1.5 collective-permute-start
  6.6 21.7 %collective-permute-done.2.refs_4_ = bf16[2048,256]{1,0:T(8,128)(2,1)S(1)} collective-permute-done((bf16[2048,256]{1,0:T(8,128)(2,1)S(1)}, bf16[2048,256]{1,0:T(8,128)(2,1)S(1)}, u32[]{:S(2)}, u32[]{:S(2)}) %collective-permute-start.2) | collective-permute-done | bytes 1048608 | tf_op jit(solution)/shard_map/ppermute | solution.py:26
  28.3 1.6 collective-permute-done.refs_2_
  29.9 1.6 collective-permute-start.5
  31.4 1.1 slice.64
  32.5 0.8 collective-permute-start.4
  33.3 2.5 %dynamic-slice_bitcast_fusion = (bf16[192,2560]{1,0:T(8,128)(2,1)S(1)}, bf16[192,2560]{1,0:T(8,128)(2,1)S(1)}, bf16[192,2560]{1,0:T(8,128)(2,1)S(1)}, bf16[192,2560]{1,0:T(8,128)(2,1)S(1)}) fusion(bf16[1,192,16384]{2,1,0:T(8,128)(2,1)} %param.7, s32[]{:T(128)S(6)} %select_n.33, s32[]{:T(128)S(6)} %select_n.31, s32[]{:T(128)S(6)} %select_n.30, s32[]{:T(128)S(6)} %select_n.32), kind=kLoop, calls=%fused_computation.3 | loop fusion | bytes 7864336 | tf_op jit(solution)/shard_map/dynamic_slice | solution.py:401
  35.9 0.8 slice-done.1
  37.3 3.7 %project.2.refs_0_ = f32[192,256]{1,0:T(8,128)S(1)} custom-call(s32[3]{0:T(128)S(1)} %pad_add_fusion.ids, bf16[192,16384]{1,0:T(8,128)(2,1)S(1)} %bitcast.19, bf16[4096,128]{1,0:T(8,128)(2,1)S(1)} %copy-done, bf16[4096,128]{1,0:T(8,128)(2,1)S(1)} %copy-done.1, bf16[2048,256]{1,0:T(8,128)(2,1)} %collective-permute-done.refs_2_, ...), custom_call_target="tpu_custom_call" | custom-call | bytes 16777216 | tf_op jit(solution)/shard_map/project/pallas_call | solution.py:42
  41.0 3.3 %collective-permute-done.5.refs_2_ = bf16[1024,256]{1,0:T(8,128)(2,1)S(1)} collective-permute-done((bf16[1024,256]{1,0:T(8,128)(2,1)S(1)}, bf16[1024,256]{1,0:T(8,128)(2,1)S(1)}, u32[]{:S(2)}, u32[]{:S(2)}) %collective-permute-start.5) | collective-permute-done | bytes 524320 | tf_op jit(solution)/shard_map/ppermute | solution.py:26
  44.3 2.4 %collective-permute-done.4.refs_1_ = bf16[1024,256]{1,0:T(8,128)(2,1)S(1)} collective-permute-done((bf16[1024,256]{1,0:T(8,128)(2,1)S(1)}, bf16[1024,256]{1,0:T(8,128)(2,1)S(1)}, u32[]{:S(2)}, u32[]{:S(2)}) %collective-permute-start.4) | collective-permute-done | bytes 524320 | tf_op jit(solution)/shard_map/ppermute | solution.py:26
  48.1 1.4 collective-permute-done.6.refs_3_
  49.5 0.7 collective-permute-done.7.refs_4_
  50.2 1.1 project.3.refs_0_
  51.4 3.8 %collective-permute-start.10 = (bf16[192,256]{1,0:T(8,128)(2,1)S(1)}, bf16[192,256]{1,0:T(8,128)(2,1)S(1)}, u32[]{:S(2)}, u32[]{:S(2)}) collective-permute-start(bf16[192,256]{1,0:T(8,128)(2,1)S(1)} %project.3.refs_0_), channel_id=1, source_target_pairs={{0,6},{1,7},{2,4},{3,5},{4,2},{5,3},{6,0},{7,1},{8,14},{9,15},{10,... | collective-permute-start | bytes 294920 | tf_op jit(solution)/shard_map/ppermute | solution.py:26
  55.2 0.6 collective-permute-start.8
  55.9 3.1 %collective-permute-done.10.refs_6_ = bf16[192,256]{1,0:T(8,128)(2,1)S(1)} collective-permute-done((bf16[192,256]{1,0:T(8,128)(2,1)S(1)}, bf16[192,256]{1,0:T(8,128)(2,1)S(1)}, u32[]{:S(2)}, u32[]{:S(2)}) %collective-permute-start.10) | collective-permute-done | bytes 98336 | tf_op jit(solution)/shard_map/ppermute | solution.py:26
  59.0 4.8 %collective-permute-done.9.refs_4_ = bf16[192,256]{1,0:T(8,128)(2,1)S(1)} collective-permute-done((bf16[192,256]{1,0:T(8,128)(2,1)S(1)}, bf16[192,256]{1,0:T(8,128)(2,1)S(1)}, u32[]{:S(2)}, u32[]{:S(2)}) %collective-permute-start.9) | collective-permute-done | bytes 98336 | tf_op jit(solution)/shard_map/ppermute | solution.py:26
  64.3 0.8 collective-permute-done.11.refs_1_
  65.6 0.8 collective-permute-done.14.refs_7_
  66.4 9.6 %attention.1 = (bf16[192,1024]{1,0:T(8,128)(2,1)}, f32[768,256]{1,0:T(8,128)S(1)}, bf16[768,256]{1,0:T(8,128)(2,1)S(1)}) custom-call(s32[1]{0:T(128)} %bitcast.ids, s32[16]{0:T(128)S(1)} %copy-done.4, s32[8]{0:T(128)S(1)} %bitcast.24, bf16[192,1024]{1,0:T(8,128)(2,1)S(1)} %bitcast.22, bf16[192,1024]{1,0:T(8,128)(2,1)S(1)} %bitcast.23, ...), custom_call_target="tpu_custom_call" | custom-call | tf_op jit(solution)/shard_map/attention/pallas_call | solution.py:162
  76.2 2.5 %collective-permute-start.24 = (bf16[192,2560]{1,0:T(8,128)(2,1)S(1)}, bf16[192,2560]{1,0:T(8,128)(2,1)S(1)}, u32[]{:S(2)}, u32[]{:S(2)}) collective-permute-start(bf16[192,2560]{1,0:T(8,128)(2,1)S(1)} %get-tuple-element.51), channel_id=1, source_target_pairs={{0,24},{8,16},{16,8},{24,0},{1,25},{9,17},{17,9},{25,1},{2,26},{10... | collective-permute-start | bytes 2949128 | tf_op jit(solution)/shard_map/ppermute | solution.py:26
  79.3 2.0 %collective-permute-start.20 = (bf16[192,256]{1,0:T(8,128)(2,1)S(1)}, bf16[192,256]{1,0:T(8,128)(2,1)S(1)}, u32[]{:S(2)}, u32[]{:S(2)}) collective-permute-start(bf16[192,256]{1,0:T(8,128)(2,1)S(1)} %get-tuple-element.79), channel_id=1, source_target_pairs={{0,6},{1,7},{2,4},{3,5},{4,2},{5,3},{6,0},{7,1},{8,14},{9,15},{10,... | collective-permute-start | bytes 294920 | tf_op jit(solution)/shard_map/ppermute | solution.py:26
  81.4 0.9 collective-permute-start.19
  82.3 1.3 collective-permute-done.18
  83.6 3.5 %collective-permute-done.20 = bf16[192,256]{1,0:T(8,128)(2,1)S(1)} collective-permute-done((bf16[192,256]{1,0:T(8,128)(2,1)S(1)}, bf16[192,256]{1,0:T(8,128)(2,1)S(1)}, u32[]{:S(2)}, u32[]{:S(2)}) %collective-permute-start.20) | collective-permute-done | bytes 98336 | tf_op jit(solution)/shard_map/ppermute | solution.py:26
  87.1 4.1 %collective-permute-done.19 = bf16[192,256]{1,0:T(8,128)(2,1)S(1)} collective-permute-done((bf16[192,256]{1,0:T(8,128)(2,1)S(1)}, bf16[192,256]{1,0:T(8,128)(2,1)S(1)}, u32[]{:S(2)}, u32[]{:S(2)}) %collective-permute-start.19) | collective-permute-done | bytes 98336 | tf_op jit(solution)/shard_map/ppermute | solution.py:26
  91.2 1.7 collective-permute-start.23
  93.4 1.4 collective-permute-start.21
  94.8 9.0 %collective-permute-done.23.refs_7_ = bf16[192,256]{1,0:T(8,128)(2,1)S(1)} collective-permute-done((bf16[192,256]{1,0:T(8,128)(2,1)S(1)}, bf16[192,256]{1,0:T(8,128)(2,1)S(1)}, u32[]{:S(2)}, u32[]{:S(2)}) %collective-permute-start.23) | collective-permute-done | bytes 98336 | tf_op jit(solution)/shard_map/ppermute | solution.py:26
  103.8 1.5 collective-permute-done.22.refs_6_
  105.4 2.2 %weight_rows.2 = (bf16[1280,256]{1,0:T(8,128)(2,1)S(1)}, bf16[1280,256]{1,0:T(8,128)(2,1)S(1)}) custom-call(s32[3]{0:T(128)S(1)} %pad_add_fusion.ids, bf16[192,2560]{1,0:T(8,128)(2,1)S(1)} %get-tuple-element.69.refs_0_, bf16[192,2560]{1,0:T(8,128)(2,1)S(1)} %collective-permute-done.15.refs_1_, bf16[192,2560]{1,0:T(8,128)(2,1)S(1)} %collective-permute-done.16.refs_2_, ...), custom_call_target="tpu_custom_call" | custom-call | bytes 8388608 | tf_op jit(solution)/shard_map/weight_rows/pallas_call | solution.py:42
  107.6 1.7 weight_rows.3
  110.7 9.1 %collective-permute-done.26 = bf16[640,256]{1,0:T(8,128)(2,1)S(1)} collective-permute-done((bf16[640,256]{1,0:T(8,128)(2,1)S(1)}, bf16[640,256]{1,0:T(8,128)(2,1)S(1)}, u32[]{:S(2)}, u32[]{:S(2)}) %collective-permute-start.26) | collective-permute-done | bytes 327712 | tf_op jit(solution)/shard_map/ppermute | solution.py:26
  119.9 1.4 collective-permute-start.27
  121.8 2.4 %collective-permute-start.34 = (bf16[768,256]{1,0:T(8,128)(2,1)S(1)}, bf16[768,256]{1,0:T(8,128)(2,1)S(1)}, u32[]{:S(2)}, u32[]{:S(2)}) collective-permute-start(bf16[768,256]{1,0:T(8,128)(2,1)S(1)} %get-tuple-element.75), channel_id=1, source_target_pairs={{0,24},{8,16},{16,8},{24,0},{1,25},{9,17},{17,9},{25,1},{2,26},{10... | collective-permute-start | bytes 1179656 | tf_op jit(solution)/shard_map/ppermute | solution.py:26
  125.4 11.2 %collective-permute-done.27 = bf16[640,256]{1,0:T(8,128)(2,1)S(1)} collective-permute-done((bf16[640,256]{1,0:T(8,128)(2,1)S(1)}, bf16[640,256]{1,0:T(8,128)(2,1)S(1)}, u32[]{:S(2)}, u32[]{:S(2)}) %collective-permute-start.27) | collective-permute-done | bytes 327712 | tf_op jit(solution)/shard_map/ppermute | solution.py:26
  136.8 4.7 %collective-permute-done.33 = bf16[768,256]{1,0:T(8,128)(2,1)S(1)} collective-permute-done((bf16[768,256]{1,0:T(8,128)(2,1)S(1)}, bf16[768,256]{1,0:T(8,128)(2,1)S(1)}, u32[]{:S(2)}, u32[]{:S(2)}) %collective-permute-start.33) | collective-permute-done | bytes 393248 | tf_op jit(solution)/shard_map/ppermute | solution.py:26
  141.7 1.5 collective-permute-start.35
  143.2 5.4 %collective-permute-done.35 = bf16[384,256]{1,0:T(8,128)(2,1)S(1)} collective-permute-done((bf16[384,256]{1,0:T(8,128)(2,1)S(1)}, bf16[384,256]{1,0:T(8,128)(2,1)S(1)}, u32[]{:S(2)}, u32[]{:S(2)}) %collective-permute-start.35) | collective-permute-done | bytes 196640 | tf_op jit(solution)/shard_map/ppermute | solution.py:26
  148.6 1.4 collective-permute-start.36
  150.5 9.4 %collective-permute-done.36 = bf16[384,256]{1,0:T(8,128)(2,1)S(1)} collective-permute-done((bf16[384,256]{1,0:T(8,128)(2,1)S(1)}, bf16[384,256]{1,0:T(8,128)(2,1)S(1)}, u32[]{:S(2)}, u32[]{:S(2)}) %collective-permute-start.36) | collective-permute-done | bytes 196640 | tf_op jit(solution)/shard_map/ppermute | solution.py:26
  160.1 3.4 %collective-permute-done.28.refs_1_ = bf16[640,256]{1,0:T(8,128)(2,1)S(1)} collective-permute-done((bf16[640,256]{1,0:T(8,128)(2,1)S(1)}, bf16[640,256]{1,0:T(8,128)(2,1)S(1)}, u32[]{:S(2)}, u32[]{:S(2)}) %collective-permute-start.28) | collective-permute-done | bytes 327712 | tf_op jit(solution)/shard_map/ppermute | solution.py:26
  164.0 2.8 %collective-permute-done.37.refs_5_ = bf16[384,256]{1,0:T(8,128)(2,1)S(1)} collective-permute-done((bf16[384,256]{1,0:T(8,128)(2,1)S(1)}, bf16[384,256]{1,0:T(8,128)(2,1)S(1)}, u32[]{:S(2)}, u32[]{:S(2)}) %collective-permute-start.37) | collective-permute-done | bytes 196640 | tf_op jit(solution)/shard_map/ppermute | solution.py:26
  166.8 1.4 collective-permute-done.39.refs_7_
  168.2 2.8 %assemble.1 = (f32[4096,128]{1,0:T(8,128)}, f32[4096,128]{1,0:T(8,128)}) custom-call(s32[3]{0:T(128)S(1)} %pad_add_fusion.ids, bf16[640,256]{1,0:T(8,128)(2,1)S(1)} %add_convert_fusion.refs_0_, bf16[640,256]{1,0:T(8,128)(2,1)S(1)} %collective-permute-done.28.refs_1_, bf16[640,256]{1,0:T(8,128)(2,1)S(1)} %collective-permute-done.29.refs_2_, ...), custom_call_target="tpu_custom_call" | custom-call | tf_op jit(solution)/shard_map/assemble/pallas_call | solution.py:42
  (75 shorter events, 9.8 us)
Async XLA Ops:
  1.9 33.9 %slice-start = ((s8[6291456]{0:T(1024)(128)(4,1)}), s8[2097152]{0:T(1024)(128)(4,1)S(1)}, s32[]{:S(2)}) async-start(s8[6291456]{0:T(1024)(128)(4,1)} %bitcast.17), calls=%async_computation | async-start | bytes 4194304
  2.1 26.2 %collective-permute-start.2 = (bf16[2048,256]{1,0:T(8,128)(2,1)S(1)}, bf16[2048,256]{1,0:T(8,128)(2,1)S(1)}, u32[]{:S(2)}, u32[]{:S(2)}) collective-permute-start(bf16[2048,256]{1,0:T(8,128)(2,1)S(1)} %pad_maximum_fusion), channel_id=1, source_target_pairs={{0,16},{8,24},{16,0},{24,8},{1,17},{9,25},{17,1},{25,9},{2,18},{10... | collective-permute-start | bytes 3145736 | tf_op jit(solution)/shard_map/ppermute | solution.py:26
  5.1 24.7 %collective-permute-start = (bf16[2048,256]{1,0:T(8,128)(2,1)S(1)}, bf16[2048,256]{1,0:T(8,128)(2,1)}, u32[]{:S(2)}, u32[]{:S(2)}) collective-permute-start(bf16[2048,256]{1,0:T(8,128)(2,1)S(1)} %pad_maximum_fusion), channel_id=1, source_target_pairs={{0,8},{8,0},{16,24},{24,16},{1,9},{9,1},{17,25},{25,17},{2,10},{10... | collective-permute-start | bytes 3145736 | tf_op jit(solution)/shard_map/ppermute | solution.py:26
  28.3 7.6 %collective-permute-start.3 = (bf16[2048,256]{1,0:T(8,128)(2,1)S(1)}, bf16[2048,256]{1,0:T(8,128)(2,1)}, u32[]{:S(2)}, u32[]{:S(2)}) collective-permute-start(bf16[2048,256]{1,0:T(8,128)(2,1)S(1)} %collective-permute-done.2.refs_4_), channel_id=1, source_target_pairs={{0,1},{1,0},{2,3},{3,2},{4,5},{5,4},{6,7},{7,6},{8,9},{9,8},{10,11... | collective-permute-start | bytes 3145736 | tf_op jit(solution)/shard_map/ppermute | solution.py:26
  29.8 6.0 %collective-permute-start.1 = (bf16[2048,256]{1,0:T(8,128)(2,1)}, bf16[2048,256]{1,0:T(8,128)(2,1)}, u32[]{:S(2)}, u32[]{:S(2)}) collective-permute-start(bf16[2048,256]{1,0:T(8,128)(2,1)} %collective-permute-done.refs_2_), channel_id=1, source_target_pairs={{0,1},{1,0},{2,3},{3,2},{4,5},{5,4},{6,7},{7,6},{8,9},{9,8},{10,11... | collective-permute-start | bytes 3145736 | tf_op jit(solution)/shard_map/ppermute | solution.py:26
  29.9 14.4 %collective-permute-start.5 = (bf16[1024,256]{1,0:T(8,128)(2,1)S(1)}, bf16[1024,256]{1,0:T(8,128)(2,1)S(1)}, u32[]{:S(2)}, u32[]{:S(2)}) collective-permute-start(bf16[1024,256]{1,0:T(8,128)(2,1)S(1)} %slice.65), channel_id=1, source_target_pairs={{0,8},{8,0},{16,24},{24,16},{1,9},{9,1},{17,25},{25,17},{2,10},{10... | collective-permute-start | bytes 1572872 | tf_op jit(solution)/shard_map/ppermute | solution.py:26
  32.5 14.1 %collective-permute-start.4 = (bf16[1024,256]{1,0:T(8,128)(2,1)S(1)}, bf16[1024,256]{1,0:T(8,128)(2,1)S(1)}, u32[]{:S(2)}, u32[]{:S(2)}) collective-permute-start(bf16[1024,256]{1,0:T(8,128)(2,1)S(1)} %slice.64), channel_id=1, source_target_pairs={{0,16},{8,24},{16,0},{24,8},{1,17},{9,25},{17,1},{25,9},{2,18},{10... | collective-permute-start | bytes 1572872 | tf_op jit(solution)/shard_map/ppermute | solution.py:26
  33.3 3.4 %slice-start.1 = ((s8[6291456]{0:T(1024)(128)(4,1)}), s8[4194304]{0:T(1024)(128)(4,1)S(1)}, s32[]{:S(2)}) async-start(s8[6291456]{0:T(1024)(128)(4,1)} %bitcast.17), calls=%async_computation.1 | async-start | bytes 8388608
  33.3 3.7 %copy-start = (bf16[4096,128]{1,0:T(8,128)(2,1)S(1)}, bf16[4096,128]{1,0:T(8,128)(2,1)}, u32[]{:S(2)}) copy-start(bf16[4096,128]{1,0:T(8,128)(2,1)} %refs_0_.1) | copy-start | bytes 3145732
  33.3 4.0 %copy-start.1 = (bf16[4096,128]{1,0:T(8,128)(2,1)S(1)}, bf16[4096,128]{1,0:T(8,128)(2,1)}, u32[]{:S(2)}) copy-start(bf16[4096,128]{1,0:T(8,128)(2,1)} %refs_1_.1) | copy-start | bytes 3145732
  46.6 19.8 %copy-start.2 = (bf16[1,192,1024]{2,1,0:T(8,128)(2,1)S(1)}, bf16[1,192,1024]{2,1,0:T(8,128)(2,1)}, u32[]{:S(2)}) copy-start(bf16[1,192,1024]{2,1,0:T(8,128)(2,1)} %param.8) | copy-start | bytes 1179652
  46.6 19.8 %copy-start.3 = (bf16[1,192,1024]{2,1,0:T(8,128)(2,1)S(1)}, bf16[1,192,1024]{2,1,0:T(8,128)(2,1)}, u32[]{:S(2)}) copy-start(bf16[1,192,1024]{2,1,0:T(8,128)(2,1)} %param.9) | copy-start | bytes 1179652
  46.6 19.8 %copy-start.4 = (s32[16]{0:T(128)S(1)}, s32[16]{0:T(128)}, u32[]{:S(2)}) copy-start(s32[16]{0:T(128)} %order.1) | copy-start | bytes 196
  46.6 19.8 %copy-start.5 = (s32[1,8]{1,0:T(1,128)S(1)}, s32[1,8]{1,0:T(1,128)}, u32[]{:S(2)}) copy-start(s32[1,8]{1,0:T(1,128)} %param.13) | copy-start | bytes 100
  46.6 29.4 %collective-permute-start.15 = (bf16[192,2560]{1,0:T(8,128)(2,1)S(1)}, bf16[192,2560]{1,0:T(8,128)(2,1)S(1)}, u32[]{:S(2)}, u32[]{:S(2)}) collective-permute-start(bf16[192,2560]{1,0:T(8,128)(2,1)S(1)} %get-tuple-element.45), channel_id=1, source_target_pairs={{0,8},{8,0},{16,24},{24,16},{1,9},{9,1},{17,25},{25,17},{2,10},{10... | collective-permute-start | bytes 2949128 | tf_op jit(solution)/shard_map/ppermute | solution.py:26
  47.2 28.8 %collective-permute-start.16 = (bf16[192,2560]{1,0:T(8,128)(2,1)S(1)}, bf16[192,2560]{1,0:T(8,128)(2,1)S(1)}, u32[]{:S(2)}, u32[]{:S(2)}) collective-permute-start(bf16[192,2560]{1,0:T(8,128)(2,1)S(1)} %get-tuple-element.46), channel_id=1, source_target_pairs={{0,16},{8,24},{16,0},{24,8},{1,17},{9,25},{17,1},{25,9},{2,18},{10... | collective-permute-start | bytes 2949128 | tf_op jit(solution)/shard_map/ppermute | solution.py:26
  47.6 1.9 %collective-permute-start.6 = (bf16[1024,256]{1,0:T(8,128)(2,1)S(1)}, bf16[1024,256]{1,0:T(8,128)(2,1)S(1)}, u32[]{:S(2)}, u32[]{:S(2)}) collective-permute-start(bf16[1024,256]{1,0:T(8,128)(2,1)S(1)} %collective-permute-done.4.refs_1_), channel_id=1, source_target_pairs={{0,1},{1,0},{2,3},{3,2},{4,5},{5,4},{6,7},{7,6},{8,9},{9,8},{10,11... | collective-permute-start | bytes 1572872 | tf_op jit(solution)/shard_map/ppermute | solution.py:26
  47.6 2.7 %collective-permute-start.7 = (bf16[1024,256]{1,0:T(8,128)(2,1)S(1)}, bf16[1024,256]{1,0:T(8,128)(2,1)S(1)}, u32[]{:S(2)}, u32[]{:S(2)}) collective-permute-start(bf16[1024,256]{1,0:T(8,128)(2,1)S(1)} %collective-permute-done.5.refs_2_), channel_id=1, source_target_pairs={{0,1},{1,0},{2,3},{3,2},{4,5},{5,4},{6,7},{7,6},{8,9},{9,8},{10,11... | collective-permute-start | bytes 1572872 | tf_op jit(solution)/shard_map/ppermute | solution.py:26
  51.4 7.6 %collective-permute-start.10 = (bf16[192,256]{1,0:T(8,128)(2,1)S(1)}, bf16[192,256]{1,0:T(8,128)(2,1)S(1)}, u32[]{:S(2)}, u32[]{:S(2)}) collective-permute-start(bf16[192,256]{1,0:T(8,128)(2,1)S(1)} %project.3.refs_0_), channel_id=1, source_target_pairs={{0,6},{1,7},{2,4},{3,5},{4,2},{5,3},{6,0},{7,1},{8,14},{9,15},{10,... | collective-permute-start | bytes 294920 | tf_op jit(solution)/shard_map/ppermute | solution.py:26
  55.2 8.6 %collective-permute-start.9 = (bf16[192,256]{1,0:T(8,128)(2,1)S(1)}, bf16[192,256]{1,0:T(8,128)(2,1)S(1)}, u32[]{:S(2)}, u32[]{:S(2)}) collective-permute-start(bf16[192,256]{1,0:T(8,128)(2,1)S(1)} %project.3.refs_0_), channel_id=1, source_target_pairs={{0,4},{1,5},{2,6},{3,7},{4,0},{5,1},{6,2},{7,3},{8,12},{9,13},{10,... | collective-permute-start | bytes 294920 | tf_op jit(solution)/shard_map/ppermute | solution.py:26
  55.2 8.6 %collective-permute-start.8 = (bf16[192,256]{1,0:T(8,128)(2,1)S(1)}, bf16[192,256]{1,0:T(8,128)(2,1)S(1)}, u32[]{:S(2)}, u32[]{:S(2)}) collective-permute-start(bf16[192,256]{1,0:T(8,128)(2,1)S(1)} %project.3.refs_0_), channel_id=1, source_target_pairs={{0,2},{1,3},{2,0},{3,1},{4,6},{5,7},{6,4},{7,5},{8,10},{9,11},{10,... | collective-permute-start | bytes 294920 | tf_op jit(solution)/shard_map/ppermute | solution.py:26
  63.8 1.3 collective-permute-start.11
  63.8 1.5 collective-permute-start.12
  64.3 1.3 collective-permute-start.13
  65.1 1.3 collective-permute-start.14
  76.0 2.6 %collective-permute-start.17 = (bf16[768,256]{1,0:T(8,128)(2,1)S(1)}, bf16[768,256]{1,0:T(8,128)(2,1)S(1)}, u32[]{:S(2)}, u32[]{:S(2)}) collective-permute-start(bf16[768,256]{1,0:T(8,128)(2,1)S(1)} %get-tuple-element.50), channel_id=1, source_target_pairs={{0,1},{1,0},{2,3},{3,2},{4,5},{5,4},{6,7},{7,6},{8,9},{9,8},{10,11... | collective-permute-start | bytes 1179656 | tf_op jit(solution)/shard_map/ppermute | solution.py:26
  76.2 29.2 %collective-permute-start.24 = (bf16[192,2560]{1,0:T(8,128)(2,1)S(1)}, bf16[192,2560]{1,0:T(8,128)(2,1)S(1)}, u32[]{:S(2)}, u32[]{:S(2)}) collective-permute-start(bf16[192,2560]{1,0:T(8,128)(2,1)S(1)} %get-tuple-element.51), channel_id=1, source_target_pairs={{0,24},{8,16},{16,8},{24,0},{1,25},{9,17},{17,9},{25,1},{2,26},{10... | collective-permute-start | bytes 2949128 | tf_op jit(solution)/shard_map/ppermute | solution.py:26
  78.8 4.8 %collective-permute-start.18 = (bf16[192,256]{1,0:T(8,128)(2,1)S(1)}, bf16[192,256]{1,0:T(8,128)(2,1)S(1)}, u32[]{:S(2)}, u32[]{:S(2)}) collective-permute-start(bf16[192,256]{1,0:T(8,128)(2,1)S(1)} %get-tuple-element.78), channel_id=1, source_target_pairs={{0,2},{1,3},{2,0},{3,1},{4,6},{5,7},{6,4},{7,5},{8,10},{9,11},{10,... | collective-permute-start | bytes 294920 | tf_op jit(solution)/shard_map/ppermute | solution.py:26
  79.3 7.7 %collective-permute-start.20 = (bf16[192,256]{1,0:T(8,128)(2,1)S(1)}, bf16[192,256]{1,0:T(8,128)(2,1)S(1)}, u32[]{:S(2)}, u32[]{:S(2)}) collective-permute-start(bf16[192,256]{1,0:T(8,128)(2,1)S(1)} %get-tuple-element.79), channel_id=1, source_target_pairs={{0,6},{1,7},{2,4},{3,5},{4,2},{5,3},{6,0},{7,1},{8,14},{9,15},{10,... | collective-permute-start | bytes 294920 | tf_op jit(solution)/shard_map/ppermute | solution.py:26
  81.4 9.8 %collective-permute-start.19 = (bf16[192,256]{1,0:T(8,128)(2,1)S(1)}, bf16[192,256]{1,0:T(8,128)(2,1)S(1)}, u32[]{:S(2)}, u32[]{:S(2)}) collective-permute-start(bf16[192,256]{1,0:T(8,128)(2,1)S(1)} %get-tuple-element.80), channel_id=1, source_target_pairs={{0,4},{1,5},{2,6},{3,7},{4,0},{5,1},{6,2},{7,3},{8,12},{9,13},{10,... | collective-permute-start | bytes 294920 | tf_op jit(solution)/shard_map/ppermute | solution.py:26
  91.2 12.6 %collective-permute-start.23 = (bf16[192,256]{1,0:T(8,128)(2,1)S(1)}, bf16[192,256]{1,0:T(8,128)(2,1)S(1)}, u32[]{:S(2)}, u32[]{:S(2)}) collective-permute-start(bf16[192,256]{1,0:T(8,128)(2,1)S(1)} %fusion.4.refs_4_.refs_1_), channel_id=1, source_target_pairs={{0,24},{8,16},{16,8},{24,0},{1,25},{9,17},{17,9},{25,1},{2,26},{10... | collective-permute-start | bytes 294920 | tf_op jit(solution)/shard_map/ppermute | solution.py:26
  92.9 12.4 %collective-permute-start.22 = (bf16[192,256]{1,0:T(8,128)(2,1)S(1)}, bf16[192,256]{1,0:T(8,128)(2,1)S(1)}, u32[]{:S(2)}, u32[]{:S(2)}) collective-permute-start(bf16[192,256]{1,0:T(8,128)(2,1)S(1)} %fusion.4.refs_4_.refs_1_), channel_id=1, source_target_pairs={{0,16},{8,24},{16,0},{24,8},{1,17},{9,25},{17,1},{25,9},{2,18},{10... | collective-permute-start | bytes 294920 | tf_op jit(solution)/shard_map/ppermute | solution.py:26
  93.4 12.0 %collective-permute-start.21 = (bf16[192,256]{1,0:T(8,128)(2,1)S(1)}, bf16[192,256]{1,0:T(8,128)(2,1)S(1)}, u32[]{:S(2)}, u32[]{:S(2)}) collective-permute-start(bf16[192,256]{1,0:T(8,128)(2,1)S(1)} %fusion.4.refs_4_.refs_1_), channel_id=1, source_target_pairs={{0,8},{8,0},{16,24},{24,16},{1,9},{9,1},{17,25},{25,17},{2,10},{10... | collective-permute-start | bytes 294920 | tf_op jit(solution)/shard_map/ppermute | solution.py:26
  107.6 2.3 %collective-permute-start.25 = (bf16[1280,256]{1,0:T(8,128)(2,1)S(1)}, bf16[1280,256]{1,0:T(8,128)(2,1)S(1)}, u32[]{:S(2)}, u32[]{:S(2)}) collective-permute-start(bf16[1280,256]{1,0:T(8,128)(2,1)S(1)} %get-tuple-element.57), channel_id=1, source_target_pairs={{0,1},{1,0},{2,3},{3,2},{4,5},{5,4},{6,7},{7,6},{8,9},{9,8},{10,11... | collective-permute-start | bytes 1966088 | tf_op jit(solution)/shard_map/ppermute | solution.py:26
  109.3 11.9 %collective-permute-start.31 = (bf16[3072,256]{1,0:T(8,128)(2,1)S(1)}, bf16[3072,256]{1,0:T(8,128)(2,1)S(1)}, u32[]{:S(2)}, u32[]{:S(2)}) collective-permute-start(bf16[3072,256]{1,0:T(8,128)(2,1)S(1)} %get-tuple-element.60), channel_id=1, source_target_pairs={{0,1},{1,0},{2,3},{3,2},{4,5},{5,4},{6,7},{7,6},{8,9},{9,8},{10,11... | collective-permute-start | bytes 4718600 | tf_op jit(solution)/shard_map/ppermute | solution.py:26
  110.1 9.7 %collective-permute-start.26 = (bf16[640,256]{1,0:T(8,128)(2,1)S(1)}, bf16[640,256]{1,0:T(8,128)(2,1)S(1)}, u32[]{:S(2)}, u32[]{:S(2)}) collective-permute-start(bf16[640,256]{1,0:T(8,128)(2,1)S(1)} %slice.97), channel_id=1, source_target_pairs={{0,2},{1,3},{2,0},{3,1},{4,6},{5,7},{6,4},{7,5},{8,10},{9,11},{10,... | collective-permute-start | bytes 983048 | tf_op jit(solution)/shard_map/ppermute | solution.py:26
  119.9 16.7 %collective-permute-start.27 = (bf16[640,256]{1,0:T(8,128)(2,1)S(1)}, bf16[640,256]{1,0:T(8,128)(2,1)S(1)}, u32[]{:S(2)}, u32[]{:S(2)}) collective-permute-start(bf16[640,256]{1,0:T(8,128)(2,1)S(1)} %fusion), channel_id=1, source_target_pairs={{0,4},{1,5},{2,6},{3,7},{4,0},{5,1},{6,2},{7,3},{8,12},{9,13},{10,... | collective-permute-start | bytes 983048 | tf_op jit(solution)/shard_map/ppermute | solution.py:26
  121.8 14.9 %collective-permute-start.34 = (bf16[768,256]{1,0:T(8,128)(2,1)S(1)}, bf16[768,256]{1,0:T(8,128)(2,1)S(1)}, u32[]{:S(2)}, u32[]{:S(2)}) collective-permute-start(bf16[768,256]{1,0:T(8,128)(2,1)S(1)} %get-tuple-element.75), channel_id=1, source_target_pairs={{0,24},{8,16},{16,8},{24,0},{1,25},{9,17},{17,9},{25,1},{2,26},{10... | collective-permute-start | bytes 1179656 | tf_op jit(solution)/shard_map/ppermute | solution.py:26
  124.2 17.2 %collective-permute-start.33 = (bf16[768,256]{1,0:T(8,128)(2,1)S(1)}, bf16[768,256]{1,0:T(8,128)(2,1)S(1)}, u32[]{:S(2)}, u32[]{:S(2)}) collective-permute-start(bf16[768,256]{1,0:T(8,128)(2,1)S(1)} %get-tuple-element.76), channel_id=1, source_target_pairs={{0,16},{8,24},{16,0},{24,8},{1,17},{9,25},{17,1},{25,9},{2,18},{10... | collective-permute-start | bytes 1179656 | tf_op jit(solution)/shard_map/ppermute | solution.py:26
  124.8 16.6 %collective-permute-start.32 = (bf16[768,256]{1,0:T(8,128)(2,1)S(1)}, bf16[768,256]{1,0:T(8,128)(2,1)S(1)}, u32[]{:S(2)}, u32[]{:S(2)}) collective-permute-start(bf16[768,256]{1,0:T(8,128)(2,1)S(1)} %get-tuple-element.77), channel_id=1, source_target_pairs={{0,8},{8,0},{16,24},{24,16},{1,9},{9,1},{17,25},{25,17},{2,10},{10... | collective-permute-start | bytes 1179656 | tf_op jit(solution)/shard_map/ppermute | solution.py:26
  141.7 6.9 %collective-permute-start.35 = (bf16[384,256]{1,0:T(8,128)(2,1)S(1)}, bf16[384,256]{1,0:T(8,128)(2,1)S(1)}, u32[]{:S(2)}, u32[]{:S(2)}) collective-permute-start(bf16[384,256]{1,0:T(8,128)(2,1)S(1)} %slice.98), channel_id=1, source_target_pairs={{0,2},{1,3},{2,0},{3,1},{4,6},{5,7},{6,4},{7,5},{8,10},{9,11},{10,... | collective-permute-start | bytes 589832 | tf_op jit(solution)/shard_map/ppermute | solution.py:26
  148.6 11.3 %collective-permute-start.36 = (bf16[384,256]{1,0:T(8,128)(2,1)S(1)}, bf16[384,256]{1,0:T(8,128)(2,1)S(1)}, u32[]{:S(2)}, u32[]{:S(2)}) collective-permute-start(bf16[384,256]{1,0:T(8,128)(2,1)S(1)} %fusion.1), channel_id=1, source_target_pairs={{0,4},{1,5},{2,6},{3,7},{4,0},{5,1},{6,2},{7,3},{8,12},{9,13},{10,... | collective-permute-start | bytes 589832 | tf_op jit(solution)/shard_map/ppermute | solution.py:26
  150.0 13.5 %collective-permute-start.28 = (bf16[640,256]{1,0:T(8,128)(2,1)S(1)}, bf16[640,256]{1,0:T(8,128)(2,1)S(1)}, u32[]{:S(2)}, u32[]{:S(2)}) collective-permute-start(bf16[640,256]{1,0:T(8,128)(2,1)S(1)} %add_convert_fusion.refs_0_), channel_id=1, source_target_pairs={{0,2},{1,3},{2,0},{3,1},{4,6},{5,7},{6,4},{7,5},{8,10},{9,11},{10,... | collective-permute-start | bytes 983048 | tf_op jit(solution)/shard_map/ppermute | solution.py:26
  159.9 6.9 %collective-permute-start.37 = (bf16[384,256]{1,0:T(8,128)(2,1)S(1)}, bf16[384,256]{1,0:T(8,128)(2,1)S(1)}, u32[]{:S(2)}, u32[]{:S(2)}) collective-permute-start(bf16[384,256]{1,0:T(8,128)(2,1)S(1)} %add_convert_fusion.1.refs_4_), channel_id=1, source_target_pairs={{0,2},{1,3},{2,0},{3,1},{4,6},{5,7},{6,4},{7,5},{8,10},{9,11},{10,... | collective-permute-start | bytes 589832 | tf_op jit(solution)/shard_map/ppermute | solution.py:26
  160.0 6.8 %collective-permute-start.29 = (bf16[640,256]{1,0:T(8,128)(2,1)S(1)}, bf16[640,256]{1,0:T(8,128)(2,1)S(1)}, u32[]{:S(2)}, u32[]{:S(2)}) collective-permute-start(bf16[640,256]{1,0:T(8,128)(2,1)S(1)} %add_convert_fusion.refs_0_), channel_id=1, source_target_pairs={{0,1},{1,0},{2,3},{3,2},{4,5},{5,4},{6,7},{7,6},{8,9},{9,8},{10,11... | collective-permute-start | bytes 983048 | tf_op jit(solution)/shard_map/ppermute | solution.py:26
  163.5 3.3 %collective-permute-start.30 = (bf16[640,256]{1,0:T(8,128)(2,1)S(1)}, bf16[640,256]{1,0:T(8,128)(2,1)S(1)}, u32[]{:S(2)}, u32[]{:S(2)}) collective-permute-start(bf16[640,256]{1,0:T(8,128)(2,1)S(1)} %collective-permute-done.28.refs_1_), channel_id=1, source_target_pairs={{0,1},{1,0},{2,3},{3,2},{4,5},{5,4},{6,7},{7,6},{8,9},{9,8},{10,11... | collective-permute-start | bytes 983048 | tf_op jit(solution)/shard_map/ppermute | solution.py:26
  163.5 3.3 %collective-permute-start.38 = (bf16[384,256]{1,0:T(8,128)(2,1)S(1)}, bf16[384,256]{1,0:T(8,128)(2,1)S(1)}, u32[]{:S(2)}, u32[]{:S(2)}) collective-permute-start(bf16[384,256]{1,0:T(8,128)(2,1)S(1)} %add_convert_fusion.1.refs_4_), channel_id=1, source_target_pairs={{0,1},{1,0},{2,3},{3,2},{4,5},{5,4},{6,7},{7,6},{8,9},{9,8},{10,11... | collective-permute-start | bytes 589832 | tf_op jit(solution)/shard_map/ppermute | solution.py:26
  166.8 1.4 collective-permute-start.39

commit v5 on v4

--- a/solution.py
+++ b/solution.py
@@ -219,6 +219,31 @@
     )
 
 
+def split_kernel(rows, keep, came, own_ref, *leaving_refs):
+    own_ref[...] = keep[:rows, :] + came[:rows, :].astype(jnp.float32)
+    for m, leaving in enumerate(leaving_refs, 1):
+        block = slice(m * rows, (m + 1) * rows)
+        leaving[...] = (keep[block, :] + came[block, :].astype(jnp.float32)).astype(leaving.dtype)
+
+
+def add_and_split(keep, came, count):
+    rows, width = keep.shape[0] // count, keep.shape[1]
+    outs = (shape_of(rows, width, jnp.float32),) + (shape_of(rows, width),) * (count - 1)
+    return kernel_call(functools.partial(split_kernel, rows), "split", outs, (), (keep, came))
+
+
+def total_kernel(*refs):
+    total = refs[0][...]
+    for one in refs[1:-1]:
+        total = total + one[...].astype(jnp.float32)
+    refs[-1][...] = total.astype(refs[-1].dtype)
+
+
+def add_all(arrays):
+    out = jax.ShapeDtypeStruct(arrays[0].shape, jnp.bfloat16)
+    return kernel_call(total_kernel, "total", out, (), arrays)
+
+
 def weight_kernel(plan, ids, *refs):
     hidden = refs[: plan.hidden]
     grads = refs[plan.hidden : -2]
@@ -291,13 +316,14 @@
     return [1 << at for at in range(sub_count.bit_length() - 1)]
 
 
-def scatter_along_z(full, sub_count):
+def scatter_along_z(full, sub_count, earlier=()):
     share = full.shape[0] // sub_count
     parts = {m: full[m * share : (m + 1) * share] for m in range(sub_count)}
     for bit in z_bits(sub_count):
         for m in list(parts):
             if m & bit:
                 came = swap(parts.pop(m).astype(jnp.bfloat16), "ctx", 2 * bit)
+                (came,), _ = after([came], *earlier)
                 parts[m ^ bit] = parts[m ^ bit] + came.astype(jnp.float32)
     return parts[0]
 
@@ -362,20 +388,20 @@
     far = [j for j in range(1, dp_count) if j not in bits]
 
     def gather_near(*weights):
-        halves = [
-            lax.dynamic_slice_in_dim(weight, core * half_rows, half_rows, 0) for weight in weights
-        ]
-        mine = jnp.concatenate(halves, axis=1)
-        return {(j, 0, 0): swap(mine, "dp", j) for j in near}
+        pieces = {}
+        for turn in range(2):
+            for at, j in enumerate(near):
+                offset = ((at + turn) % 2) * quarter
+                start = core * half_rows + offset
+                rows = [lax.dynamic_slice_in_dim(weight, start, quarter, 0) for weight in weights]
+                pieces[j, 0, offset] = swap(jnp.concatenate(rows, axis=1), "dp", j)
+        return pieces
 
     def gather_far(landed):
         pieces = {}
         for j in far:
             for offset, bit in ((0, 1 << (j.bit_length() - 1)), (quarter, j & -j)):
-                if (j ^ bit) in near:
-                    origin = landed[j ^ bit, 0, 0][offset : offset + quarter]
-                else:
-                    origin = pieces[j ^ bit, 0, offset]
+                origin = landed.get((j ^ bit, 0, offset), pieces.get((j ^ bit, 0, offset)))
                 pieces[j, 0, offset] = swap(origin, "dp", bit)
         return pieces
 
@@ -416,24 +442,19 @@
     moved = {0: moving[0]}
     moved.update({j: swap(moving[j], "dp", j) for j in near})
     along = gather_along_z(own)
-    along, _ = after(along)
+    along, tied = after(along, *[moving[j] for j in far])
+    moving.update(zip(far, tied))
     kv_blocks = both_cores(along)
 
     query_grad, keep, send = attention(
         me, stretch_order, doc_lengths[0], queries[0], grad_out[0], kv_blocks, head_dim
     )
-    ready, ended = after([send] + [moving[j] for j in far], *[moved[j] for j in near])
-    send = ready[0]
+    (send,), ended = after([send], *[moved[j] for j in near])
     moved.update(zip(near, ended))
-    moved.update({j: swap(one, "dp", j) for j, one in zip(far, ready[1:])})
-
-    chip = keep + swap(send, "ctx", 1).astype(jnp.float32)
-    rows = chip.shape[0] // z_count
-    grad = chip[:rows]
-    for m in range(1, z_count):
-        leaving = chip[m * rows : (m + 1) * rows].astype(jnp.bfloat16)
-        grad = grad + swap(leaving, "ctx", 2 * m).astype(jnp.float32)
-    grad = grad.astype(jnp.bfloat16)
+    moved.update({j: swap(moving[j], "dp", j) for j in far})
+
+    own, *leaving = add_and_split(keep, swap(send, "ctx", 1), z_count)
+    grad = add_all([own] + [swap(one, "ctx", 2 * m) for m, one in enumerate(leaving, 1)])
     grads = [grad] + [swap(grad, "dp", j) for j in range(1, dp_count)]
 
     (grad,), ended = after([grad], *grads[1:], *[moved[j] for j in far])
@@ -449,8 +470,7 @@
     first = weight_rows(ids, arrays, grads, groups, 0, first_half, block_rows, sub_count)
     first = scatter_along_z(first, sub_count)
     first = sum_of_halves(first, sub_count)
-    last, _ = after(last, first)
-    last = sum_of_halves(scatter_along_z(sum_of(last), sub_count), sub_count)
+    last = sum_of_halves(scatter_along_z(sum_of(last), sub_count, [first]), sub_count)
     blocks = gather_parts(first, sub_count) + gather_parts(last, sub_count)
     key_rows, value_rows = assemble(ids, blocks, sub_count, regions)
     return query_grad[None], key_rows, value_rows

time: 171 us -> 171 us (level)
  starting transfers between devices: 33.3 us -> 39.7 us
  waiting for transfers between devices: 108 us -> 102 us
    ppermute x40 -> x44, starting transfers between devices: 33.3 us -> 39.7 us  [swap(): return lax.ppermute(array, axis, [(i, i ^ distance) for i in range(count)])]
    ppermute x40 -> x44, waiting for transfers between devices: 108 us -> 102 us  [swap(): return lax.ppermute(array, axis, [(i, i ^ distance) for i in range(count)])]
    pallas_call x5 -> x7, Pallas kernels: 11.5 us -> 11.2 us  [kernel_call(): pl.pallas_call(kernel, out_shape=outs, in_specs=[smem] * len(scalars) + [...]
  transfers between devices with their start and end apart: 40 -> 44, of which waited for: 25 -> 28; matrix products, arithmetic and copies ran while one was open for 3% -> 3% of each run, Pallas kernels for 9% -> 9%
where the time goes in v5:
time: 171 us
  waiting for transfers between devices  102 us (60%)
  starting transfers between devices  39.7 us (23%)
  Pallas kernels  20.8 us (12%)
  local copies, waits for them, and re-layouts  5.5 us (3%)
  other arithmetic  2.81 us (2%)
    ppermute x44, waiting for transfers between devices, swap(): return lax.ppermute(array, axis, [(i, i ^ distance) for i in range(count)])  102 us
    ppermute x44, starting transfers between devices, swap(): return lax.ppermute(array, axis, [(i, i ^ distance) for i in range(count)])  39.7 us
    pallas_call x7, Pallas kernels, kernel_call(): pl.pallas_call(kernel, out_shape=outs, in_specs=[smem] * len(scalars) + [...  11.2 us
    pallas_call x1, Pallas kernels, attention(): pl.pallas_call(functools.partial(attention_kernel, shape), out_shape=(jax...  9.59 us
  transfers between devices with their start and end apart: 44, of which 28 were waited for; matrix products, arithmetic and copies ran while one was open for 3% of the time, Pallas kernels for 9%

profile of v5, /device:TPU:0, one launch (start us, length us, event | category | flops | bytes accessed | tf_op | source)
XLA Modules:
  0.0 171.2 jit_solution(13713640857840853673)
XLA Ops:
  0.7 1.4 constant_dynamic-slice_fusion
  2.1 0.9 pad_maximum_fusion
  2.9 3.0 %collective-permute-start.4 = (bf16[1024,256]{1,0:T(8,128)(2,1)}, bf16[1024,256]{1,0:T(8,128)(2,1)S(1)}, u32[]{:S(2)}, u32[]{:S(2)}) collective-permute-start(bf16[1024,256]{1,0:T(8,128)(2,1)} %pad_maximum_fusion), channel_id=1, source_target_pairs={{0,16},{8,24},{16,0},{24,8},{1,17},{9,25},{17,1},{25,9},{2,18},{10... | collective-permute-start | bytes 1572872 | tf_op jit(solution)/shard_map/ppermute | solution.py:26
  5.9 1.5 collective-permute-start
  8.8 10.1 %collective-permute-done.4.refs_6_ = bf16[1024,256]{1,0:T(8,128)(2,1)S(1)} collective-permute-done((bf16[1024,256]{1,0:T(8,128)(2,1)}, bf16[1024,256]{1,0:T(8,128)(2,1)S(1)}, u32[]{:S(2)}, u32[]{:S(2)}) %collective-permute-start.4) | collective-permute-done | bytes 524320 | tf_op jit(solution)/shard_map/ppermute | solution.py:26
  18.9 2.1 %collective-permute-done.refs_2_ = bf16[1024,256]{1,0:T(8,128)(2,1)S(1)} collective-permute-done((bf16[1024,256]{1,0:T(8,128)(2,1)}, bf16[1024,256]{1,0:T(8,128)(2,1)S(1)}, u32[]{:S(2)}, u32[]{:S(2)}) %collective-permute-start) | collective-permute-done | bytes 524320 | tf_op jit(solution)/shard_map/ppermute | solution.py:26
  21.2 9.0 %collective-permute-done.5.refs_7_ = bf16[1024,256]{1,0:T(8,128)(2,1)} collective-permute-done((bf16[1024,256]{1,0:T(8,128)(2,1)}, bf16[1024,256]{1,0:T(8,128)(2,1)}, u32[]{:S(2)}, u32[]{:S(2)}) %collective-permute-start.5) | collective-permute-done | bytes 524320 | tf_op jit(solution)/shard_map/ppermute | solution.py:26
  30.2 2.0 %collective-permute-start.9 = (bf16[1024,256]{1,0:T(8,128)(2,1)}, bf16[1024,256]{1,0:T(8,128)(2,1)S(1)}, u32[]{:S(2)}, u32[]{:S(2)}) collective-permute-start(bf16[1024,256]{1,0:T(8,128)(2,1)} %collective-permute-done.5.refs_7_), channel_id=1, source_target_pairs={{0,8},{8,0},{16,24},{24,16},{1,9},{9,1},{17,25},{25,17},{2,10},{10... | collective-permute-start | bytes 1572872 | tf_op jit(solution)/shard_map/ppermute | solution.py:26
  32.8 2.5 %dynamic-slice_bitcast_fusion = (bf16[192,2560]{1,0:T(8,128)(2,1)S(1)}, bf16[192,2560]{1,0:T(8,128)(2,1)S(1)}, bf16[192,2560]{1,0:T(8,128)(2,1)S(1)}, bf16[192,2560]{1,0:T(8,128)(2,1)S(1)}) fusion(bf16[1,192,16384]{2,1,0:T(8,128)(2,1)} %param.7, s32[]{:T(128)S(6)} %select_n.42, s32[]{:T(128)S(6)} %select_n.40, s32[]{:T(128)S(6)} %select_n.39, s32[]{:T(128)S(6)} %select_n.41), kind=kLoop, calls=%fused_computation.2 | loop fusion | bytes 7864336 | tf_op jit(solution)/shard_map/dynamic_slice | solution.py:427
  36.8 3.2 %project.2.refs_0_ = f32[192,256]{1,0:T(8,128)S(1)} custom-call(s32[3]{0:T(128)S(1)} %pad_add_fusion.ids, bf16[192,16384]{1,0:T(8,128)(2,1)S(1)} %bitcast.19, bf16[4096,128]{1,0:T(8,128)(2,1)S(1)} %copy-done, bf16[4096,128]{1,0:T(8,128)(2,1)S(1)} %copy-done.1, bf16[1024,256]{1,0:T(8,128)(2,1)S(1)} %collective-permute-done.refs_2_, ...), custom_call_target="tpu_custom_call" | custom-call | bytes 16777216 | tf_op jit(solution)/shard_map/project/pallas_call | solution.py:42
  40.5 2.2 %collective-permute-done.9.refs_2_ = bf16[1024,256]{1,0:T(8,128)(2,1)S(1)} collective-permute-done((bf16[1024,256]{1,0:T(8,128)(2,1)}, bf16[1024,256]{1,0:T(8,128)(2,1)S(1)}, u32[]{:S(2)}, u32[]{:S(2)}) %collective-permute-start.9) | collective-permute-done | bytes 524320 | tf_op jit(solution)/shard_map/ppermute | solution.py:26
  43.3 1.4 collective-permute-start.19
  44.7 1.5 collective-permute-start.20
  46.2 1.1 project.3.refs_0_
  47.4 3.7 %collective-permute-start.14 = (bf16[192,256]{1,0:T(8,128)(2,1)S(1)}, bf16[192,256]{1,0:T(8,128)(2,1)S(1)}, u32[]{:S(2)}, u32[]{:S(2)}) collective-permute-start(bf16[192,256]{1,0:T(8,128)(2,1)S(1)} %project.3.refs_0_), channel_id=1, source_target_pairs={{0,6},{1,7},{2,4},{3,5},{4,2},{5,3},{6,0},{7,1},{8,14},{9,15},{10,... | collective-permute-start | bytes 294920 | tf_op jit(solution)/shard_map/ppermute | solution.py:26
  51.8 3.2 %collective-permute-done.14.refs_6_ = bf16[192,256]{1,0:T(8,128)(2,1)S(1)} collective-permute-done((bf16[192,256]{1,0:T(8,128)(2,1)S(1)}, bf16[192,256]{1,0:T(8,128)(2,1)S(1)}, u32[]{:S(2)}, u32[]{:S(2)}) %collective-permute-start.14) | collective-permute-done | bytes 98336 | tf_op jit(solution)/shard_map/ppermute | solution.py:26
  55.0 4.0 %collective-permute-done.13.refs_4_ = bf16[192,256]{1,0:T(8,128)(2,1)S(1)} collective-permute-done((bf16[192,256]{1,0:T(8,128)(2,1)S(1)}, bf16[192,256]{1,0:T(8,128)(2,1)S(1)}, u32[]{:S(2)}, u32[]{:S(2)}) %collective-permute-start.13) | collective-permute-done | bytes 98336 | tf_op jit(solution)/shard_map/ppermute | solution.py:26
  59.0 2.2 %collective-permute-start.28 = (bf16[192,2560]{1,0:T(8,128)(2,1)S(1)}, bf16[192,2560]{1,0:T(8,128)(2,1)S(1)}, u32[]{:S(2)}, u32[]{:S(2)}) collective-permute-start(bf16[192,2560]{1,0:T(8,128)(2,1)S(1)} %get-tuple-element.56), channel_id=1, source_target_pairs={{0,24},{8,16},{16,8},{24,0},{1,25},{9,17},{17,9},{25,1},{2,26},{10... | collective-permute-start | bytes 2949128 | tf_op jit(solution)/shard_map/ppermute | solution.py:26
  63.9 9.6 %attention.1 = (bf16[192,1024]{1,0:T(8,128)(2,1)}, f32[768,256]{1,0:T(8,128)S(1)}, bf16[768,256]{1,0:T(8,128)(2,1)S(1)}) custom-call(s32[1]{0:T(128)} %bitcast.ids, s32[16]{0:T(128)S(1)} %copy-done.4, s32[8]{0:T(128)S(1)} %bitcast.24, bf16[192,1024]{1,0:T(8,128)(2,1)S(1)} %bitcast.22, bf16[192,1024]{1,0:T(8,128)(2,1)S(1)} %bitcast.23, ...), custom_call_target="tpu_custom_call" | custom-call | tf_op jit(solution)/shard_map/attention/pallas_call | solution.py:162
  73.5 15.7 %collective-permute-done.20.refs_2_ = bf16[192,2560]{1,0:T(8,128)(2,1)S(1)} collective-permute-done((bf16[192,2560]{1,0:T(8,128)(2,1)S(1)}, bf16[192,2560]{1,0:T(8,128)(2,1)S(1)}, u32[]{:S(2)}, u32[]{:S(2)}) %collective-permute-start.20) | collective-permute-done | bytes 983072 | tf_op jit(solution)/shard_map/ppermute | solution.py:26
  89.2 1.7 %collective-permute-done.21.came = bf16[768,256]{1,0:T(8,128)(2,1)S(1)} collective-permute-done((bf16[768,256]{1,0:T(8,128)(2,1)S(1)}, bf16[768,256]{1,0:T(8,128)(2,1)S(1)}, u32[]{:S(2)}, u32[]{:S(2)}) %collective-permute-start.21) | collective-permute-done | bytes 393248 | tf_op jit(solution)/shard_map/ppermute | solution.py:26
  91.0 1.6 collective-permute-start.22
  92.7 2.6 %collective-permute-start.23 = (bf16[192,256]{1,0:T(8,128)(2,1)S(1)}, bf16[192,256]{1,0:T(8,128)(2,1)S(1)}, u32[]{:S(2)}, u32[]{:S(2)}) collective-permute-start(bf16[192,256]{1,0:T(8,128)(2,1)S(1)} %get-tuple-element.54), channel_id=1, source_target_pairs={{0,4},{1,5},{2,6},{3,7},{4,0},{5,1},{6,2},{7,3},{8,12},{9,13},{10,... | collective-permute-start | bytes 294920 | tf_op jit(solution)/shard_map/ppermute | solution.py:26
  95.9 7.4 %collective-permute-done.23.refs_2_ = bf16[192,256]{1,0:T(8,128)(2,1)S(1)} collective-permute-done((bf16[192,256]{1,0:T(8,128)(2,1)S(1)}, bf16[192,256]{1,0:T(8,128)(2,1)S(1)}, u32[]{:S(2)}, u32[]{:S(2)}) %collective-permute-start.23) | collective-permute-done | bytes 98336 | tf_op jit(solution)/shard_map/ppermute | solution.py:26
  103.4 1.6 collective-permute-start.27
  105.1 1.9 %collective-permute-start.25 = (bf16[192,256]{1,0:T(8,128)(2,1)S(1)}, bf16[192,256]{1,0:T(8,128)(2,1)S(1)}, u32[]{:S(2)}, u32[]{:S(2)}) collective-permute-start(bf16[192,256]{1,0:T(8,128)(2,1)S(1)} %total.1.refs_4_.refs_1_), channel_id=1, source_target_pairs={{0,8},{8,0},{16,24},{24,16},{1,9},{9,1},{17,25},{25,17},{2,10},{10... | collective-permute-start | bytes 294920 | tf_op jit(solution)/shard_map/ppermute | solution.py:26
  107.0 2.1 %collective-permute-done.27.refs_7_ = bf16[192,256]{1,0:T(8,128)(2,1)S(1)} collective-permute-done((bf16[192,256]{1,0:T(8,128)(2,1)S(1)}, bf16[192,256]{1,0:T(8,128)(2,1)S(1)}, u32[]{:S(2)}, u32[]{:S(2)}) %collective-permute-start.27) | collective-permute-done | bytes 98336 | tf_op jit(solution)/shard_map/ppermute | solution.py:26
  109.0 1.0 collective-permute-done.26.refs_6_
  110.1 1.7 weight_rows.3
  111.9 2.2 %weight_rows.2 = (bf16[1280,256]{1,0:T(8,128)(2,1)S(1)}, bf16[1280,256]{1,0:T(8,128)(2,1)S(1)}) custom-call(s32[3]{0:T(128)S(1)} %pad_add_fusion.ids, bf16[192,2560]{1,0:T(8,128)(2,1)S(1)} %get-tuple-element.69.refs_0_, bf16[192,2560]{1,0:T(8,128)(2,1)S(1)} %collective-permute-done.19.refs_1_, bf16[192,2560]{1,0:T(8,128)(2,1)S(1)} %collective-permute-done.20.refs_2_, ...), custom_call_target="tpu_custom_call" | custom-call | bytes 8388608 | tf_op jit(solution)/shard_map/weight_rows/pallas_call | solution.py:42
  114.6 1.7 %collective-permute-done.29 = bf16[1280,256]{1,0:T(8,128)(2,1)S(1)} collective-permute-done((bf16[1280,256]{1,0:T(8,128)(2,1)S(1)}, bf16[1280,256]{1,0:T(8,128)(2,1)S(1)}, u32[]{:S(2)}, u32[]{:S(2)}) %collective-permute-start.29) | collective-permute-done | bytes 655392 | tf_op jit(solution)/shard_map/ppermute | solution.py:26
  116.5 2.1 %collective-permute-start.30 = (bf16[640,256]{1,0:T(8,128)(2,1)S(1)}, bf16[640,256]{1,0:T(8,128)(2,1)S(1)}, u32[]{:S(2)}, u32[]{:S(2)}) collective-permute-start(bf16[640,256]{1,0:T(8,128)(2,1)S(1)} %slice.62), channel_id=1, source_target_pairs={{0,2},{1,3},{2,0},{3,1},{4,6},{5,7},{6,4},{7,5},{8,10},{9,11},{10,... | collective-permute-start | bytes 983048 | tf_op jit(solution)/shard_map/ppermute | solution.py:26
  119.2 1.2 collective-permute-start.36
  120.4 1.5 collective-permute-start.38
  121.8 0.9 collective-permute-start.37
  122.7 4.2 %collective-permute-done.30 = bf16[640,256]{1,0:T(8,128)(2,1)S(1)} collective-permute-done((bf16[640,256]{1,0:T(8,128)(2,1)S(1)}, bf16[640,256]{1,0:T(8,128)(2,1)S(1)}, u32[]{:S(2)}, u32[]{:S(2)}) %collective-permute-start.30) | collective-permute-done | bytes 327712 | tf_op jit(solution)/shard_map/ppermute | solution.py:26
  126.9 2.7 %collective-permute-start.31 = (bf16[640,256]{1,0:T(8,128)(2,1)S(1)}, bf16[640,256]{1,0:T(8,128)(2,1)S(1)}, u32[]{:S(2)}, u32[]{:S(2)}) collective-permute-start(bf16[640,256]{1,0:T(8,128)(2,1)S(1)} %fusion.2), channel_id=1, source_target_pairs={{0,4},{1,5},{2,6},{3,7},{4,0},{5,1},{6,2},{7,3},{8,12},{9,13},{10,... | collective-permute-start | bytes 983048 | tf_op jit(solution)/shard_map/ppermute | solution.py:26
  129.6 1.6 collective-permute-done.36
  131.2 8.3 %collective-permute-done.38 = bf16[768,256]{1,0:T(8,128)(2,1)S(1)} collective-permute-done((bf16[768,256]{1,0:T(8,128)(2,1)S(1)}, bf16[768,256]{1,0:T(8,128)(2,1)S(1)}, u32[]{:S(2)}, u32[]{:S(2)}) %collective-permute-start.38) | collective-permute-done | bytes 393248 | tf_op jit(solution)/shard_map/ppermute | solution.py:26
  139.5 1.4 collective-permute-done.37
  141.4 3.0 %collective-permute-done.31 = bf16[640,256]{1,0:T(8,128)(2,1)S(1)} collective-permute-done((bf16[640,256]{1,0:T(8,128)(2,1)S(1)}, bf16[640,256]{1,0:T(8,128)(2,1)S(1)}, u32[]{:S(2)}, u32[]{:S(2)}) %collective-permute-start.31) | collective-permute-done | bytes 327712 | tf_op jit(solution)/shard_map/ppermute | solution.py:26
  144.5 4.0 %collective-permute-done.39 = bf16[384,256]{1,0:T(8,128)(2,1)S(1)} collective-permute-done((bf16[384,256]{1,0:T(8,128)(2,1)S(1)}, bf16[384,256]{1,0:T(8,128)(2,1)S(1)}, u32[]{:S(2)}, u32[]{:S(2)}) %collective-permute-start.39) | collective-permute-done | bytes 196640 | tf_op jit(solution)/shard_map/ppermute | solution.py:26
  148.9 2.5 %collective-permute-start.32 = (bf16[640,256]{1,0:T(8,128)(2,1)S(1)}, bf16[640,256]{1,0:T(8,128)(2,1)S(1)}, u32[]{:S(2)}, u32[]{:S(2)}) collective-permute-start(bf16[640,256]{1,0:T(8,128)(2,1)S(1)} %add_convert_fusion.refs_0_), channel_id=1, source_target_pairs={{0,2},{1,3},{2,0},{3,1},{4,6},{5,7},{6,4},{7,5},{8,10},{9,11},{10,... | collective-permute-start | bytes 983048 | tf_op jit(solution)/shard_map/ppermute | solution.py:26
  151.4 8.3 %collective-permute-done.40 = bf16[384,256]{1,0:T(8,128)(2,1)S(1)} collective-permute-done((bf16[384,256]{1,0:T(8,128)(2,1)S(1)}, bf16[384,256]{1,0:T(8,128)(2,1)S(1)}, u32[]{:S(2)}, u32[]{:S(2)}) %collective-permute-start.40) | collective-permute-done | bytes 196640 | tf_op jit(solution)/shard_map/ppermute | solution.py:26
  159.9 3.0 %collective-permute-done.32.refs_1_ = bf16[640,256]{1,0:T(8,128)(2,1)S(1)} collective-permute-done((bf16[640,256]{1,0:T(8,128)(2,1)S(1)}, bf16[640,256]{1,0:T(8,128)(2,1)S(1)}, u32[]{:S(2)}, u32[]{:S(2)}) %collective-permute-start.32) | collective-permute-done | bytes 327712 | tf_op jit(solution)/shard_map/ppermute | solution.py:26
  163.4 3.5 %collective-permute-done.41.refs_5_ = bf16[384,256]{1,0:T(8,128)(2,1)S(1)} collective-permute-done((bf16[384,256]{1,0:T(8,128)(2,1)S(1)}, bf16[384,256]{1,0:T(8,128)(2,1)S(1)}, u32[]{:S(2)}, u32[]{:S(2)}) %collective-permute-start.41) | collective-permute-done | bytes 196640 | tf_op jit(solution)/shard_map/ppermute | solution.py:26
  166.9 1.4 collective-permute-done.43.refs_7_
  168.3 2.8 %assemble.1 = (f32[4096,128]{1,0:T(8,128)}, f32[4096,128]{1,0:T(8,128)}) custom-call(s32[3]{0:T(128)S(1)} %pad_add_fusion.ids, bf16[640,256]{1,0:T(8,128)(2,1)S(1)} %add_convert_fusion.refs_0_, bf16[640,256]{1,0:T(8,128)(2,1)S(1)} %collective-permute-done.32.refs_1_, bf16[640,256]{1,0:T(8,128)(2,1)S(1)} %collective-permute-done.33.refs_2_, ...), custom_call_target="tpu_custom_call" | custom-call | tf_op jit(solution)/shard_map/assemble/pallas_call | solution.py:42
  (80 shorter events, 12.4 us)
Async XLA Ops:
  0.7 34.7 %slice-start = ((s8[6291456]{0:T(1024)(128)(4,1)}), s8[2097152]{0:T(1024)(128)(4,1)S(1)}, s32[]{:S(2)}) async-start(s8[6291456]{0:T(1024)(128)(4,1)} %bitcast.17), calls=%async_computation | async-start | bytes 4194304
  2.9 15.9 %collective-permute-start.4 = (bf16[1024,256]{1,0:T(8,128)(2,1)}, bf16[1024,256]{1,0:T(8,128)(2,1)S(1)}, u32[]{:S(2)}, u32[]{:S(2)}) collective-permute-start(bf16[1024,256]{1,0:T(8,128)(2,1)} %pad_maximum_fusion), channel_id=1, source_target_pairs={{0,16},{8,24},{16,0},{24,8},{1,17},{9,25},{17,1},{25,9},{2,18},{10... | collective-permute-start | bytes 1572872 | tf_op jit(solution)/shard_map/ppermute | solution.py:26
  5.9 15.1 %collective-permute-start = (bf16[1024,256]{1,0:T(8,128)(2,1)}, bf16[1024,256]{1,0:T(8,128)(2,1)S(1)}, u32[]{:S(2)}, u32[]{:S(2)}) collective-permute-start(bf16[1024,256]{1,0:T(8,128)(2,1)} %pad_maximum_fusion), channel_id=1, source_target_pairs={{0,8},{8,0},{16,24},{24,16},{1,9},{9,1},{17,25},{25,17},{2,10},{10... | collective-permute-start | bytes 1572872 | tf_op jit(solution)/shard_map/ppermute | solution.py:26
  8.2 22.0 %collective-permute-start.5 = (bf16[1024,256]{1,0:T(8,128)(2,1)}, bf16[1024,256]{1,0:T(8,128)(2,1)}, u32[]{:S(2)}, u32[]{:S(2)}) collective-permute-start(bf16[1024,256]{1,0:T(8,128)(2,1)} %pad_maximum_fusion.1), channel_id=1, source_target_pairs={{0,16},{8,24},{16,0},{24,8},{1,17},{9,25},{17,1},{25,9},{2,18},{10... | collective-permute-start | bytes 1572872 | tf_op jit(solution)/shard_map/ppermute | solution.py:26
  8.7 23.5 %collective-permute-start.1 = (bf16[1024,256]{1,0:T(8,128)(2,1)}, bf16[1024,256]{1,0:T(8,128)(2,1)}, u32[]{:S(2)}, u32[]{:S(2)}) collective-permute-start(bf16[1024,256]{1,0:T(8,128)(2,1)} %pad_maximum_fusion.1), channel_id=1, source_target_pairs={{0,8},{8,0},{16,24},{24,16},{1,9},{9,1},{17,25},{25,17},{2,10},{10... | collective-permute-start | bytes 1572872 | tf_op jit(solution)/shard_map/ppermute | solution.py:26
  18.9 13.4 %collective-permute-start.6 = (bf16[1024,256]{1,0:T(8,128)(2,1)S(1)}, bf16[1024,256]{1,0:T(8,128)(2,1)}, u32[]{:S(2)}, u32[]{:S(2)}) collective-permute-start(bf16[1024,256]{1,0:T(8,128)(2,1)S(1)} %collective-permute-done.4.refs_6_), channel_id=1, source_target_pairs={{0,1},{1,0},{2,3},{3,2},{4,5},{5,4},{6,7},{7,6},{8,9},{9,8},{10,11... | collective-permute-start | bytes 1572872 | tf_op jit(solution)/shard_map/ppermute | solution.py:26
  21.0 19.5 %collective-permute-start.8 = (bf16[1024,256]{1,0:T(8,128)(2,1)S(1)}, bf16[1024,256]{1,0:T(8,128)(2,1)S(1)}, u32[]{:S(2)}, u32[]{:S(2)}) collective-permute-start(bf16[1024,256]{1,0:T(8,128)(2,1)S(1)} %collective-permute-done.refs_2_), channel_id=1, source_target_pairs={{0,16},{8,24},{16,0},{24,8},{1,17},{9,25},{17,1},{25,9},{2,18},{10... | collective-permute-start | bytes 1572872 | tf_op jit(solution)/shard_map/ppermute | solution.py:26
  21.0 14.4 %collective-permute-start.2 = (bf16[1024,256]{1,0:T(8,128)(2,1)S(1)}, bf16[1024,256]{1,0:T(8,128)(2,1)S(1)}, u32[]{:S(2)}, u32[]{:S(2)}) collective-permute-start(bf16[1024,256]{1,0:T(8,128)(2,1)S(1)} %collective-permute-done.refs_2_), channel_id=1, source_target_pairs={{0,1},{1,0},{2,3},{3,2},{4,5},{5,4},{6,7},{7,6},{8,9},{9,8},{10,11... | collective-permute-start | bytes 1572872 | tf_op jit(solution)/shard_map/ppermute | solution.py:26
  30.2 12.5 %collective-permute-start.9 = (bf16[1024,256]{1,0:T(8,128)(2,1)}, bf16[1024,256]{1,0:T(8,128)(2,1)S(1)}, u32[]{:S(2)}, u32[]{:S(2)}) collective-permute-start(bf16[1024,256]{1,0:T(8,128)(2,1)} %collective-permute-done.5.refs_7_), channel_id=1, source_target_pairs={{0,8},{8,0},{16,24},{24,16},{1,9},{9,1},{17,25},{25,17},{2,10},{10... | collective-permute-start | bytes 1572872 | tf_op jit(solution)/shard_map/ppermute | solution.py:26
  32.2 3.1 %collective-permute-start.7 = (bf16[1024,256]{1,0:T(8,128)(2,1)}, bf16[1024,256]{1,0:T(8,128)(2,1)S(1)}, u32[]{:S(2)}, u32[]{:S(2)}) collective-permute-start(bf16[1024,256]{1,0:T(8,128)(2,1)} %collective-permute-done.5.refs_7_), channel_id=1, source_target_pairs={{0,1},{1,0},{2,3},{3,2},{4,5},{5,4},{6,7},{7,6},{8,9},{9,8},{10,11... | collective-permute-start | bytes 1572872 | tf_op jit(solution)/shard_map/ppermute | solution.py:26
  32.2 3.1 %collective-permute-start.3 = (bf16[1024,256]{1,0:T(8,128)(2,1)}, bf16[1024,256]{1,0:T(8,128)(2,1)S(1)}, u32[]{:S(2)}, u32[]{:S(2)}) collective-permute-start(bf16[1024,256]{1,0:T(8,128)(2,1)} %collective-permute-done.1.refs_3_), channel_id=1, source_target_pairs={{0,1},{1,0},{2,3},{3,2},{4,5},{5,4},{6,7},{7,6},{8,9},{9,8},{10,11... | collective-permute-start | bytes 1572872 | tf_op jit(solution)/shard_map/ppermute | solution.py:26
  42.7 21.2 %copy-start.3 = (bf16[1,192,1024]{2,1,0:T(8,128)(2,1)S(1)}, bf16[1,192,1024]{2,1,0:T(8,128)(2,1)}, u32[]{:S(2)}) copy-start(bf16[1,192,1024]{2,1,0:T(8,128)(2,1)} %param.9) | copy-start | bytes 1179652
  42.7 21.2 %copy-start.4 = (s32[16]{0:T(128)S(1)}, s32[16]{0:T(128)}, u32[]{:S(2)}) copy-start(s32[16]{0:T(128)} %order.1) | copy-start | bytes 196
  42.7 21.2 %copy-start.5 = (s32[1,8]{1,0:T(1,128)S(1)}, s32[1,8]{1,0:T(1,128)}, u32[]{:S(2)}) copy-start(s32[1,8]{1,0:T(1,128)} %param.13) | copy-start | bytes 100
  42.7 3.5 %collective-permute-start.10 = (bf16[1024,256]{1,0:T(8,128)(2,1)S(1)}, bf16[1024,256]{1,0:T(8,128)(2,1)S(1)}, u32[]{:S(2)}, u32[]{:S(2)}) collective-permute-start(bf16[1024,256]{1,0:T(8,128)(2,1)S(1)} %collective-permute-done.8.refs_1_), channel_id=1, source_target_pairs={{0,1},{1,0},{2,3},{3,2},{4,5},{5,4},{6,7},{7,6},{8,9},{9,8},{10,11... | collective-permute-start | bytes 1572872 | tf_op jit(solution)/shard_map/ppermute | solution.py:26
  42.8 3.4 %collective-permute-start.11 = (bf16[1024,256]{1,0:T(8,128)(2,1)S(1)}, bf16[1024,256]{1,0:T(8,128)(2,1)S(1)}, u32[]{:S(2)}, u32[]{:S(2)}) collective-permute-start(bf16[1024,256]{1,0:T(8,128)(2,1)S(1)} %collective-permute-done.9.refs_2_), channel_id=1, source_target_pairs={{0,1},{1,0},{2,3},{3,2},{4,5},{5,4},{6,7},{7,6},{8,9},{9,8},{10,11... | collective-permute-start | bytes 1572872 | tf_op jit(solution)/shard_map/ppermute | solution.py:26
  43.3 30.3 %collective-permute-start.19 = (bf16[192,2560]{1,0:T(8,128)(2,1)S(1)}, bf16[192,2560]{1,0:T(8,128)(2,1)S(1)}, u32[]{:S(2)}, u32[]{:S(2)}) collective-permute-start(bf16[192,2560]{1,0:T(8,128)(2,1)S(1)} %get-tuple-element.46), channel_id=1, source_target_pairs={{0,8},{8,0},{16,24},{24,16},{1,9},{9,1},{17,25},{25,17},{2,10},{10... | collective-permute-start | bytes 2949128 | tf_op jit(solution)/shard_map/ppermute | solution.py:26
  44.7 44.5 %collective-permute-start.20 = (bf16[192,2560]{1,0:T(8,128)(2,1)S(1)}, bf16[192,2560]{1,0:T(8,128)(2,1)S(1)}, u32[]{:S(2)}, u32[]{:S(2)}) collective-permute-start(bf16[192,2560]{1,0:T(8,128)(2,1)S(1)} %get-tuple-element.47), channel_id=1, source_target_pairs={{0,16},{8,24},{16,0},{24,8},{1,17},{9,25},{17,1},{25,9},{2,18},{10... | collective-permute-start | bytes 2949128 | tf_op jit(solution)/shard_map/ppermute | solution.py:26
  47.4 7.6 %collective-permute-start.14 = (bf16[192,256]{1,0:T(8,128)(2,1)S(1)}, bf16[192,256]{1,0:T(8,128)(2,1)S(1)}, u32[]{:S(2)}, u32[]{:S(2)}) collective-permute-start(bf16[192,256]{1,0:T(8,128)(2,1)S(1)} %project.3.refs_0_), channel_id=1, source_target_pairs={{0,6},{1,7},{2,4},{3,5},{4,2},{5,3},{6,0},{7,1},{8,14},{9,15},{10,... | collective-permute-start | bytes 294920 | tf_op jit(solution)/shard_map/ppermute | solution.py:26
  51.0 8.0 %collective-permute-start.13 = (bf16[192,256]{1,0:T(8,128)(2,1)S(1)}, bf16[192,256]{1,0:T(8,128)(2,1)S(1)}, u32[]{:S(2)}, u32[]{:S(2)}) collective-permute-start(bf16[192,256]{1,0:T(8,128)(2,1)S(1)} %project.3.refs_0_), channel_id=1, source_target_pairs={{0,4},{1,5},{2,6},{3,7},{4,0},{5,1},{6,2},{7,3},{8,12},{9,13},{10,... | collective-permute-start | bytes 294920 | tf_op jit(solution)/shard_map/ppermute | solution.py:26
  51.0 8.0 %collective-permute-start.12 = (bf16[192,256]{1,0:T(8,128)(2,1)S(1)}, bf16[192,256]{1,0:T(8,128)(2,1)S(1)}, u32[]{:S(2)}, u32[]{:S(2)}) collective-permute-start(bf16[192,256]{1,0:T(8,128)(2,1)S(1)} %project.3.refs_0_), channel_id=1, source_target_pairs={{0,2},{1,3},{2,0},{3,1},{4,6},{5,7},{6,4},{7,5},{8,10},{9,11},{10,... | collective-permute-start | bytes 294920 | tf_op jit(solution)/shard_map/ppermute | solution.py:26
  59.0 51.2 %collective-permute-start.28 = (bf16[192,2560]{1,0:T(8,128)(2,1)S(1)}, bf16[192,2560]{1,0:T(8,128)(2,1)S(1)}, u32[]{:S(2)}, u32[]{:S(2)}) collective-permute-start(bf16[192,2560]{1,0:T(8,128)(2,1)S(1)} %get-tuple-element.56), channel_id=1, source_target_pairs={{0,24},{8,16},{16,8},{24,0},{1,25},{9,17},{17,9},{25,1},{2,26},{10... | collective-permute-start | bytes 2949128 | tf_op jit(solution)/shard_map/ppermute | solution.py:26
  61.2 1.3 collective-permute-start.15
  61.2 1.5 collective-permute-start.16
  62.5 1.3 collective-permute-start.17
  62.6 1.3 collective-permute-start.18
  89.2 1.7 %collective-permute-start.21 = (bf16[768,256]{1,0:T(8,128)(2,1)S(1)}, bf16[768,256]{1,0:T(8,128)(2,1)S(1)}, u32[]{:S(2)}, u32[]{:S(2)}) collective-permute-start(bf16[768,256]{1,0:T(8,128)(2,1)S(1)} %get-tuple-element.51), channel_id=1, source_target_pairs={{0,1},{1,0},{2,3},{3,2},{4,5},{5,4},{6,7},{7,6},{8,9},{9,8},{10,11... | collective-permute-start | bytes 1179656 | tf_op jit(solution)/shard_map/ppermute | solution.py:26
  91.0 4.9 %collective-permute-start.22 = (bf16[192,256]{1,0:T(8,128)(2,1)S(1)}, bf16[192,256]{1,0:T(8,128)(2,1)S(1)}, u32[]{:S(2)}, u32[]{:S(2)}) collective-permute-start(bf16[192,256]{1,0:T(8,128)(2,1)S(1)} %get-tuple-element.53), channel_id=1, source_target_pairs={{0,2},{1,3},{2,0},{3,1},{4,6},{5,7},{6,4},{7,5},{8,10},{9,11},{10,... | collective-permute-start | bytes 294920 | tf_op jit(solution)/shard_map/ppermute | solution.py:26
  92.7 10.7 %collective-permute-start.23 = (bf16[192,256]{1,0:T(8,128)(2,1)S(1)}, bf16[192,256]{1,0:T(8,128)(2,1)S(1)}, u32[]{:S(2)}, u32[]{:S(2)}) collective-permute-start(bf16[192,256]{1,0:T(8,128)(2,1)S(1)} %get-tuple-element.54), channel_id=1, source_target_pairs={{0,4},{1,5},{2,6},{3,7},{4,0},{5,1},{6,2},{7,3},{8,12},{9,13},{10,... | collective-permute-start | bytes 294920 | tf_op jit(solution)/shard_map/ppermute | solution.py:26
  95.3 8.1 %collective-permute-start.24 = (bf16[192,256]{1,0:T(8,128)(2,1)S(1)}, bf16[192,256]{1,0:T(8,128)(2,1)S(1)}, u32[]{:S(2)}, u32[]{:S(2)}) collective-permute-start(bf16[192,256]{1,0:T(8,128)(2,1)S(1)} %get-tuple-element.55), channel_id=1, source_target_pairs={{0,6},{1,7},{2,4},{3,5},{4,2},{5,3},{6,0},{7,1},{8,14},{9,15},{10,... | collective-permute-start | bytes 294920 | tf_op jit(solution)/shard_map/ppermute | solution.py:26
  103.4 5.6 %collective-permute-start.27 = (bf16[192,256]{1,0:T(8,128)(2,1)S(1)}, bf16[192,256]{1,0:T(8,128)(2,1)S(1)}, u32[]{:S(2)}, u32[]{:S(2)}) collective-permute-start(bf16[192,256]{1,0:T(8,128)(2,1)S(1)} %total.1.refs_4_.refs_1_), channel_id=1, source_target_pairs={{0,24},{8,16},{16,8},{24,0},{1,25},{9,17},{17,9},{25,1},{2,26},{10... | collective-permute-start | bytes 294920 | tf_op jit(solution)/shard_map/ppermute | solution.py:26
  105.0 5.1 %collective-permute-start.26 = (bf16[192,256]{1,0:T(8,128)(2,1)S(1)}, bf16[192,256]{1,0:T(8,128)(2,1)S(1)}, u32[]{:S(2)}, u32[]{:S(2)}) collective-permute-start(bf16[192,256]{1,0:T(8,128)(2,1)S(1)} %total.1.refs_4_.refs_1_), channel_id=1, source_target_pairs={{0,16},{8,24},{16,0},{24,8},{1,17},{9,25},{17,1},{25,9},{2,18},{10... | collective-permute-start | bytes 294920 | tf_op jit(solution)/shard_map/ppermute | solution.py:26
  105.1 5.1 %collective-permute-start.25 = (bf16[192,256]{1,0:T(8,128)(2,1)S(1)}, bf16[192,256]{1,0:T(8,128)(2,1)S(1)}, u32[]{:S(2)}, u32[]{:S(2)}) collective-permute-start(bf16[192,256]{1,0:T(8,128)(2,1)S(1)} %total.1.refs_4_.refs_1_), channel_id=1, source_target_pairs={{0,8},{8,0},{16,24},{24,16},{1,9},{9,1},{17,25},{25,17},{2,10},{10... | collective-permute-start | bytes 294920 | tf_op jit(solution)/shard_map/ppermute | solution.py:26
  111.8 6.8 %collective-permute-start.35 = (bf16[3072,256]{1,0:T(8,128)(2,1)S(1)}, bf16[3072,256]{1,0:T(8,128)(2,1)S(1)}, u32[]{:S(2)}, u32[]{:S(2)}) collective-permute-start(bf16[3072,256]{1,0:T(8,128)(2,1)S(1)} %get-tuple-element.65), channel_id=1, source_target_pairs={{0,1},{1,0},{2,3},{3,2},{4,5},{5,4},{6,7},{7,6},{8,9},{9,8},{10,11... | collective-permute-start | bytes 4718600 | tf_op jit(solution)/shard_map/ppermute | solution.py:26
  114.1 2.3 %collective-permute-start.29 = (bf16[1280,256]{1,0:T(8,128)(2,1)S(1)}, bf16[1280,256]{1,0:T(8,128)(2,1)S(1)}, u32[]{:S(2)}, u32[]{:S(2)}) collective-permute-start(bf16[1280,256]{1,0:T(8,128)(2,1)S(1)} %get-tuple-element.62), channel_id=1, source_target_pairs={{0,1},{1,0},{2,3},{3,2},{4,5},{5,4},{6,7},{7,6},{8,9},{9,8},{10,11... | collective-permute-start | bytes 1966088 | tf_op jit(solution)/shard_map/ppermute | solution.py:26
  116.5 10.3 %collective-permute-start.30 = (bf16[640,256]{1,0:T(8,128)(2,1)S(1)}, bf16[640,256]{1,0:T(8,128)(2,1)S(1)}, u32[]{:S(2)}, u32[]{:S(2)}) collective-permute-start(bf16[640,256]{1,0:T(8,128)(2,1)S(1)} %slice.62), channel_id=1, source_target_pairs={{0,2},{1,3},{2,0},{3,1},{4,6},{5,7},{6,4},{7,5},{8,10},{9,11},{10,... | collective-permute-start | bytes 983048 | tf_op jit(solution)/shard_map/ppermute | solution.py:26
  119.2 12.0 %collective-permute-start.36 = (bf16[768,256]{1,0:T(8,128)(2,1)S(1)}, bf16[768,256]{1,0:T(8,128)(2,1)S(1)}, u32[]{:S(2)}, u32[]{:S(2)}) collective-permute-start(bf16[768,256]{1,0:T(8,128)(2,1)S(1)} %get-tuple-element.75), channel_id=1, source_target_pairs={{0,8},{8,0},{16,24},{24,16},{1,9},{9,1},{17,25},{25,17},{2,10},{10... | collective-permute-start | bytes 1179656 | tf_op jit(solution)/shard_map/ppermute | solution.py:26
  120.4 19.1 %collective-permute-start.38 = (bf16[768,256]{1,0:T(8,128)(2,1)S(1)}, bf16[768,256]{1,0:T(8,128)(2,1)S(1)}, u32[]{:S(2)}, u32[]{:S(2)}) collective-permute-start(bf16[768,256]{1,0:T(8,128)(2,1)S(1)} %get-tuple-element.76), channel_id=1, source_target_pairs={{0,24},{8,16},{16,8},{24,0},{1,25},{9,17},{17,9},{25,1},{2,26},{10... | collective-permute-start | bytes 1179656 | tf_op jit(solution)/shard_map/ppermute | solution.py:26
  121.8 19.0 %collective-permute-start.37 = (bf16[768,256]{1,0:T(8,128)(2,1)S(1)}, bf16[768,256]{1,0:T(8,128)(2,1)S(1)}, u32[]{:S(2)}, u32[]{:S(2)}) collective-permute-start(bf16[768,256]{1,0:T(8,128)(2,1)S(1)} %get-tuple-element.77), channel_id=1, source_target_pairs={{0,16},{8,24},{16,0},{24,8},{1,17},{9,25},{17,1},{25,9},{2,18},{10... | collective-permute-start | bytes 1179656 | tf_op jit(solution)/shard_map/ppermute | solution.py:26
  126.9 17.5 %collective-permute-start.31 = (bf16[640,256]{1,0:T(8,128)(2,1)S(1)}, bf16[640,256]{1,0:T(8,128)(2,1)S(1)}, u32[]{:S(2)}, u32[]{:S(2)}) collective-permute-start(bf16[640,256]{1,0:T(8,128)(2,1)S(1)} %fusion.2), channel_id=1, source_target_pairs={{0,4},{1,5},{2,6},{3,7},{4,0},{5,1},{6,2},{7,3},{8,12},{9,13},{10,... | collective-permute-start | bytes 983048 | tf_op jit(solution)/shard_map/ppermute | solution.py:26
  141.0 7.5 %collective-permute-start.39 = (bf16[384,256]{1,0:T(8,128)(2,1)S(1)}, bf16[384,256]{1,0:T(8,128)(2,1)S(1)}, u32[]{:S(2)}, u32[]{:S(2)}) collective-permute-start(bf16[384,256]{1,0:T(8,128)(2,1)S(1)} %slice.63), channel_id=1, source_target_pairs={{0,2},{1,3},{2,0},{3,1},{4,6},{5,7},{6,4},{7,5},{8,10},{9,11},{10,... | collective-permute-start | bytes 589832 | tf_op jit(solution)/shard_map/ppermute | solution.py:26
  148.6 11.1 %collective-permute-start.40 = (bf16[384,256]{1,0:T(8,128)(2,1)S(1)}, bf16[384,256]{1,0:T(8,128)(2,1)S(1)}, u32[]{:S(2)}, u32[]{:S(2)}) collective-permute-start(bf16[384,256]{1,0:T(8,128)(2,1)S(1)} %fusion.3), channel_id=1, source_target_pairs={{0,4},{1,5},{2,6},{3,7},{4,0},{5,1},{6,2},{7,3},{8,12},{9,13},{10,... | collective-permute-start | bytes 589832 | tf_op jit(solution)/shard_map/ppermute | solution.py:26
  148.9 14.0 %collective-permute-start.32 = (bf16[640,256]{1,0:T(8,128)(2,1)S(1)}, bf16[640,256]{1,0:T(8,128)(2,1)S(1)}, u32[]{:S(2)}, u32[]{:S(2)}) collective-permute-start(bf16[640,256]{1,0:T(8,128)(2,1)S(1)} %add_convert_fusion.refs_0_), channel_id=1, source_target_pairs={{0,2},{1,3},{2,0},{3,1},{4,6},{5,7},{6,4},{7,5},{8,10},{9,11},{10,... | collective-permute-start | bytes 983048 | tf_op jit(solution)/shard_map/ppermute | solution.py:26
  159.7 7.1 %collective-permute-start.41 = (bf16[384,256]{1,0:T(8,128)(2,1)S(1)}, bf16[384,256]{1,0:T(8,128)(2,1)S(1)}, u32[]{:S(2)}, u32[]{:S(2)}) collective-permute-start(bf16[384,256]{1,0:T(8,128)(2,1)S(1)} %add_convert_fusion.1.refs_4_), channel_id=1, source_target_pairs={{0,2},{1,3},{2,0},{3,1},{4,6},{5,7},{6,4},{7,5},{8,10},{9,11},{10,... | collective-permute-start | bytes 589832 | tf_op jit(solution)/shard_map/ppermute | solution.py:26
  159.8 7.1 %collective-permute-start.33 = (bf16[640,256]{1,0:T(8,128)(2,1)S(1)}, bf16[640,256]{1,0:T(8,128)(2,1)S(1)}, u32[]{:S(2)}, u32[]{:S(2)}) collective-permute-start(bf16[640,256]{1,0:T(8,128)(2,1)S(1)} %add_convert_fusion.refs_0_), channel_id=1, source_target_pairs={{0,1},{1,0},{2,3},{3,2},{4,5},{5,4},{6,7},{7,6},{8,9},{9,8},{10,11... | collective-permute-start | bytes 983048 | tf_op jit(solution)/shard_map/ppermute | solution.py:26
  162.9 4.0 %collective-permute-start.34 = (bf16[640,256]{1,0:T(8,128)(2,1)S(1)}, bf16[640,256]{1,0:T(8,128)(2,1)S(1)}, u32[]{:S(2)}, u32[]{:S(2)}) collective-permute-start(bf16[640,256]{1,0:T(8,128)(2,1)S(1)} %collective-permute-done.32.refs_1_), channel_id=1, source_target_pairs={{0,1},{1,0},{2,3},{3,2},{4,5},{5,4},{6,7},{7,6},{8,9},{9,8},{10,11... | collective-permute-start | bytes 983048 | tf_op jit(solution)/shard_map/ppermute | solution.py:26
  162.9 4.0 %collective-permute-start.42 = (bf16[384,256]{1,0:T(8,128)(2,1)S(1)}, bf16[384,256]{1,0:T(8,128)(2,1)S(1)}, u32[]{:S(2)}, u32[]{:S(2)}) collective-permute-start(bf16[384,256]{1,0:T(8,128)(2,1)S(1)} %add_convert_fusion.1.refs_4_), channel_id=1, source_target_pairs={{0,1},{1,0},{2,3},{3,2},{4,5},{5,4},{6,7},{7,6},{8,9},{9,8},{10,11... | collective-permute-start | bytes 589832 | tf_op jit(solution)/shard_map/ppermute | solution.py:26
  166.9 1.4 collective-permute-start.43
  (4 other events, 32.2 us)

commit v6 on v5

--- a/solution.py
+++ b/solution.py
@@ -12,8 +12,14 @@
 NO_COST = pl.CostEstimate(flops=0, bytes_accessed=0, transcendentals=0)
 
 
-def moved_rows(block_rows):
-    return block_rows * 10 // 16 // 256 * 256
+MOVED = (6, 5)
+TIED = 1
+
+
+def region_sizes(block_rows):
+    units = block_rows // 256
+    sizes = [256 * (units * share // 16) for share in MOVED]
+    return sizes + [block_rows - sum(sizes)]
 
 
 class Plan:
@@ -420,9 +426,9 @@
     def both_cores(along):
         return [block for one in along for block in (one, swap(one, "ctx", 1))]
 
-    first_rows = moved_rows(block_rows)
-    first_half, last_half = first_rows // 2, (block_rows - first_rows) // 2
-    regions = ((0, first_half), (first_rows, last_half))
+    sizes = region_sizes(block_rows)
+    regions = [(sum(sizes[:at]), size // 2) for at, size in enumerate(sizes)]
+    first_rows = sum(sizes[:-1])
     moving = {
         j: lax.dynamic_slice_in_dim(inputs, (dp ^ j) * block_rows, first_rows, 1)
         for j in range(dp_count)
@@ -449,29 +455,28 @@
     query_grad, keep, send = attention(
         me, stretch_order, doc_lengths[0], queries[0], grad_out[0], kv_blocks, head_dim
     )
-    (send,), ended = after([send], *[moved[j] for j in near])
-    moved.update(zip(near, ended))
     moved.update({j: swap(moving[j], "dp", j) for j in far})
 
     own, *leaving = add_and_split(keep, swap(send, "ctx", 1), z_count)
     grad = add_all([own] + [swap(one, "ctx", 2 * m) for m, one in enumerate(leaving, 1)])
     grads = [grad] + [swap(grad, "dp", j) for j in range(1, dp_count)]
 
-    (grad,), ended = after([grad], *grads[1:], *[moved[j] for j in far])
+    (grad,), ended = after([grad], *grads[1:], *[moved[j] for j in others])
     grads[1:] = ended[: dp_count - 1]
-    moved.update(zip(far, ended[dp_count - 1 :]))
+    moved.update(zip(others, ended[dp_count - 1 :]))
     groups = [[(0, j, 0)] for j in range(dp_count)]
-    last = weight_rows(
-        ids, [inputs], [grad], groups, first_rows, last_half, block_rows, sub_count
-    )
-    last = send_over_dp(last)
+    own = weight_rows(ids, [inputs], [grad], groups, *regions[-1], block_rows, sub_count)
+    own = send_over_dp(own)
     groups = [[(j, None, j) for j in range(dp_count)]]
     arrays = [moved[j] for j in range(dp_count)]
-    first = weight_rows(ids, arrays, grads, groups, 0, first_half, block_rows, sub_count)
-    first = scatter_along_z(first, sub_count)
-    first = sum_of_halves(first, sub_count)
-    last = sum_of_halves(scatter_along_z(sum_of(last), sub_count, [first]), sub_count)
-    blocks = gather_parts(first, sub_count) + gather_parts(last, sub_count)
+    finals = []
+    for region in regions[:-1]:
+        part = weight_rows(ids, arrays, grads, groups, *region, block_rows, sub_count)
+        part = scatter_along_z(part, sub_count)
+        finals.append(sum_of_halves(part, sub_count))
+    part = scatter_along_z(sum_of(own), sub_count, finals[:TIED])
+    finals.append(sum_of_halves(part, sub_count))
+    blocks = [one for final in finals for one in gather_parts(final, sub_count)]
     key_rows, value_rows = assemble(ids, blocks, sub_count, regions)
     return query_grad[None], key_rows, value_rows
 

time: 171 us -> 166 us (0.971)
  waiting for transfers between devices: 102 us -> 90.6 us
  starting transfers between devices: 39.7 us -> 44.5 us
    ppermute x44 -> x50, waiting for transfers between devices: 102 us -> 90.6 us  [swap(): return lax.ppermute(array, axis, [(i, i ^ distance) for i in range(count)])]
    ppermute x44 -> x50, starting transfers between devices: 39.7 us -> 44.5 us  [swap(): return lax.ppermute(array, axis, [(i, i ^ distance) for i in range(count)])]
    pallas_call x7 -> x8, Pallas kernels: 11.2 us -> 11.9 us  [kernel_call(): pl.pallas_call(kernel, out_shape=outs, in_specs=[smem] * len(scalars) + [...]
  transfers between devices with their start and end apart: 44 -> 50, of which waited for: 28 -> 29; matrix products, arithmetic and copies ran while one was open for 3% -> 3% of each run, Pallas kernels for 9% -> 10%
where the time goes in v6:
time: 166 us
  waiting for transfers between devices  90.6 us (55%)
  starting transfers between devices  44.5 us (27%)
  Pallas kernels  21.5 us (13%)
  local copies, waits for them, and re-layouts  5.61 us (3%)
  other arithmetic  2.74 us (2%)
    ppermute x50, waiting for transfers between devices, swap(): return lax.ppermute(array, axis, [(i, i ^ distance) for i in range(count)])  90.6 us
    ppermute x50, starting transfers between devices, swap(): return lax.ppermute(array, axis, [(i, i ^ distance) for i in range(count)])  44.5 us
    pallas_call x8, Pallas kernels, kernel_call(): pl.pallas_call(kernel, out_shape=outs, in_specs=[smem] * len(scalars) + [...  11.9 us
    pallas_call x1, Pallas kernels, attention(): pl.pallas_call(functools.partial(attention_kernel, shape), out_shape=(jax...  9.6 us
  transfers between devices with their start and end apart: 50, of which 29 were waited for; matrix products, arithmetic and copies ran while one was open for 3% of the time, Pallas kernels for 10%

profile of v6, /device:TPU:0, one launch (start us, length us, event | category | flops | bytes accessed | tf_op | source)
XLA Modules:
  0.0 165.9 jit_solution(10527912378896526742)
XLA Ops:
  0.7 1.4 constant_dynamic-slice_fusion
  2.9 3.0 %collective-permute-start.4 = (bf16[1024,256]{1,0:T(8,128)(2,1)}, bf16[1024,256]{1,0:T(8,128)(2,1)S(1)}, u32[]{:S(2)}, u32[]{:S(2)}) collective-permute-start(bf16[1024,256]{1,0:T(8,128)(2,1)} %pad_maximum_fusion), channel_id=1, source_target_pairs={{0,16},{8,24},{16,0},{24,8},{1,17},{9,25},{17,1},{25,9},{2,18},{10... | collective-permute-start | bytes 1572872 | tf_op jit(solution)/shard_map/ppermute | solution.py:32
  5.9 1.5 collective-permute-start
  8.8 10.1 %collective-permute-done.4.refs_6_ = bf16[1024,256]{1,0:T(8,128)(2,1)S(1)} collective-permute-done((bf16[1024,256]{1,0:T(8,128)(2,1)}, bf16[1024,256]{1,0:T(8,128)(2,1)S(1)}, u32[]{:S(2)}, u32[]{:S(2)}) %collective-permute-start.4) | collective-permute-done | bytes 524320 | tf_op jit(solution)/shard_map/ppermute | solution.py:32
  18.9 2.1 %collective-permute-done.refs_2_ = bf16[1024,256]{1,0:T(8,128)(2,1)S(1)} collective-permute-done((bf16[1024,256]{1,0:T(8,128)(2,1)}, bf16[1024,256]{1,0:T(8,128)(2,1)S(1)}, u32[]{:S(2)}, u32[]{:S(2)}) %collective-permute-start) | collective-permute-done | bytes 524320 | tf_op jit(solution)/shard_map/ppermute | solution.py:32
  21.2 9.0 %collective-permute-done.5.refs_7_ = bf16[1024,256]{1,0:T(8,128)(2,1)} collective-permute-done((bf16[1024,256]{1,0:T(8,128)(2,1)}, bf16[1024,256]{1,0:T(8,128)(2,1)}, u32[]{:S(2)}, u32[]{:S(2)}) %collective-permute-start.5) | collective-permute-done | bytes 524320 | tf_op jit(solution)/shard_map/ppermute | solution.py:32
  30.2 2.0 %collective-permute-start.9 = (bf16[1024,256]{1,0:T(8,128)(2,1)}, bf16[1024,256]{1,0:T(8,128)(2,1)S(1)}, u32[]{:S(2)}, u32[]{:S(2)}) collective-permute-start(bf16[1024,256]{1,0:T(8,128)(2,1)} %collective-permute-done.5.refs_7_), channel_id=1, source_target_pairs={{0,8},{8,0},{16,24},{24,16},{1,9},{9,1},{17,25},{25,17},{2,10},{10... | collective-permute-start | bytes 1572872 | tf_op jit(solution)/shard_map/ppermute | solution.py:32
  32.8 2.6 %dynamic-slice_bitcast_fusion = (bf16[192,2816]{1,0:T(8,128)(2,1)S(1)}, bf16[192,2816]{1,0:T(8,128)(2,1)S(1)}, bf16[192,2816]{1,0:T(8,128)(2,1)S(1)}, bf16[192,2816]{1,0:T(8,128)(2,1)S(1)}) fusion(bf16[1,192,16384]{2,1,0:T(8,128)(2,1)} %param.7, s32[]{:T(128)S(6)} %select_n.42, s32[]{:T(128)S(6)} %select_n.40, s32[]{:T(128)S(6)} %select_n.39, s32[]{:T(128)S(6)} %select_n.41), kind=kLoop, calls=%fused_computation.1 | loop fusion | bytes 8650768 | tf_op jit(solution)/shard_map/dynamic_slice | solution.py:433
  36.9 3.2 %project.2.refs_0_ = f32[192,256]{1,0:T(8,128)S(1)} custom-call(s32[3]{0:T(128)S(1)} %pad_add_fusion.ids, bf16[192,16384]{1,0:T(8,128)(2,1)S(1)} %bitcast.19, bf16[4096,128]{1,0:T(8,128)(2,1)S(1)} %copy-done, bf16[4096,128]{1,0:T(8,128)(2,1)S(1)} %copy-done.1, bf16[1024,256]{1,0:T(8,128)(2,1)S(1)} %collective-permute-done.refs_2_, ...), custom_call_target="tpu_custom_call" | custom-call | bytes 16777216 | tf_op jit(solution)/shard_map/project/pallas_call | solution.py:48
  40.5 2.2 %collective-permute-done.9.refs_2_ = bf16[1024,256]{1,0:T(8,128)(2,1)S(1)} collective-permute-done((bf16[1024,256]{1,0:T(8,128)(2,1)}, bf16[1024,256]{1,0:T(8,128)(2,1)S(1)}, u32[]{:S(2)}, u32[]{:S(2)}) %collective-permute-start.9) | collective-permute-done | bytes 524320 | tf_op jit(solution)/shard_map/ppermute | solution.py:32
  43.3 1.4 collective-permute-done.10.refs_3_
  45.4 1.1 project.3.refs_0_
  46.6 3.6 %collective-permute-start.14 = (bf16[192,256]{1,0:T(8,128)(2,1)S(1)}, bf16[192,256]{1,0:T(8,128)(2,1)S(1)}, u32[]{:S(2)}, u32[]{:S(2)}) collective-permute-start(bf16[192,256]{1,0:T(8,128)(2,1)S(1)} %project.3.refs_0_), channel_id=1, source_target_pairs={{0,6},{1,7},{2,4},{3,5},{4,2},{5,3},{6,0},{7,1},{8,14},{9,15},{10,... | collective-permute-start | bytes 294920 | tf_op jit(solution)/shard_map/ppermute | solution.py:32
  51.0 1.4 collective-permute-start.26
  52.4 1.5 collective-permute-start.27
  54.2 4.5 %collective-permute-done.13.refs_4_ = bf16[192,256]{1,0:T(8,128)(2,1)S(1)} collective-permute-done((bf16[192,256]{1,0:T(8,128)(2,1)S(1)}, bf16[192,256]{1,0:T(8,128)(2,1)S(1)}, u32[]{:S(2)}, u32[]{:S(2)}) %collective-permute-start.13) | collective-permute-done | bytes 98336 | tf_op jit(solution)/shard_map/ppermute | solution.py:32
  58.7 2.4 %collective-permute-start.28 = (bf16[192,2816]{1,0:T(8,128)(2,1)S(1)}, bf16[192,2816]{1,0:T(8,128)(2,1)S(1)}, u32[]{:S(2)}, u32[]{:S(2)}) collective-permute-start(bf16[192,2816]{1,0:T(8,128)(2,1)S(1)} %get-tuple-element.54), channel_id=1, source_target_pairs={{0,24},{8,16},{16,8},{24,0},{1,25},{9,17},{17,9},{25,1},{2,26},{10... | collective-permute-start | bytes 3244040 | tf_op jit(solution)/shard_map/ppermute | solution.py:32
  63.9 9.6 %attention.1 = (bf16[192,1024]{1,0:T(8,128)(2,1)}, f32[768,256]{1,0:T(8,128)S(1)}, bf16[768,256]{1,0:T(8,128)(2,1)S(1)}) custom-call(s32[1]{0:T(128)} %bitcast.ids, s32[16]{0:T(128)S(1)} %copy-done.4, s32[8]{0:T(128)S(1)} %bitcast.24, bf16[192,1024]{1,0:T(8,128)(2,1)S(1)} %bitcast.22, bf16[192,1024]{1,0:T(8,128)(2,1)S(1)} %bitcast.23, ...), custom_call_target="tpu_custom_call" | custom-call | tf_op jit(solution)/shard_map/attention/pallas_call | solution.py:168
  73.9 1.4 collective-permute-done.19.came
  76.0 2.5 %collective-permute-start.21 = (bf16[192,256]{1,0:T(8,128)(2,1)S(1)}, bf16[192,256]{1,0:T(8,128)(2,1)S(1)}, u32[]{:S(2)}, u32[]{:S(2)}) collective-permute-start(bf16[192,256]{1,0:T(8,128)(2,1)S(1)} %get-tuple-element.50), channel_id=1, source_target_pairs={{0,4},{1,5},{2,6},{3,7},{4,0},{5,1},{6,2},{7,3},{8,12},{9,13},{10,... | collective-permute-start | bytes 294920 | tf_op jit(solution)/shard_map/ppermute | solution.py:32
  78.5 3.8 %collective-permute-done.20.refs_1_ = bf16[192,256]{1,0:T(8,128)(2,1)S(1)} collective-permute-done((bf16[192,256]{1,0:T(8,128)(2,1)S(1)}, bf16[192,256]{1,0:T(8,128)(2,1)S(1)}, u32[]{:S(2)}, u32[]{:S(2)}) %collective-permute-start.20) | collective-permute-done | bytes 98336 | tf_op jit(solution)/shard_map/ppermute | solution.py:32
  82.2 1.9 %collective-permute-start.22 = (bf16[192,256]{1,0:T(8,128)(2,1)S(1)}, bf16[192,256]{1,0:T(8,128)(2,1)S(1)}, u32[]{:S(2)}, u32[]{:S(2)}) collective-permute-start(bf16[192,256]{1,0:T(8,128)(2,1)S(1)} %get-tuple-element.51), channel_id=1, source_target_pairs={{0,6},{1,7},{2,4},{3,5},{4,2},{5,3},{6,0},{7,1},{8,14},{9,15},{10,... | collective-permute-start | bytes 294920 | tf_op jit(solution)/shard_map/ppermute | solution.py:32
  84.1 4.5 %collective-permute-done.22.refs_3_ = bf16[192,256]{1,0:T(8,128)(2,1)S(1)} collective-permute-done((bf16[192,256]{1,0:T(8,128)(2,1)S(1)}, bf16[192,256]{1,0:T(8,128)(2,1)S(1)}, u32[]{:S(2)}, u32[]{:S(2)}) %collective-permute-start.22) | collective-permute-done | bytes 98336 | tf_op jit(solution)/shard_map/ppermute | solution.py:32
  89.3 1.5 collective-permute-start.24
  90.8 1.5 collective-permute-start.23
  92.3 10.5 %collective-permute-done.27.refs_2_ = bf16[192,2816]{1,0:T(8,128)(2,1)S(1)} collective-permute-done((bf16[192,2816]{1,0:T(8,128)(2,1)S(1)}, bf16[192,2816]{1,0:T(8,128)(2,1)S(1)}, u32[]{:S(2)}, u32[]{:S(2)}) %collective-permute-start.27) | collective-permute-done | bytes 1081376 | tf_op jit(solution)/shard_map/ppermute | solution.py:32
  103.5 1.2 collective-permute-done.24.refs_6_
  104.7 1.5 weight_rows.5
  106.3 1.5 weight_rows.4
  108.3 1.6 weight_rows.3
  110.1 1.5 collective-permute-start.36
  111.9 1.4 collective-permute-start.30
  113.3 3.9 %collective-permute-done.36 = bf16[320,256]{1,0:T(8,128)(2,1)S(1)} collective-permute-done((bf16[320,256]{1,0:T(8,128)(2,1)S(1)}, bf16[320,256]{1,0:T(8,128)(2,1)S(1)}, u32[]{:S(2)}, u32[]{:S(2)}) %collective-permute-start.36) | collective-permute-done | bytes 163872 | tf_op jit(solution)/shard_map/ppermute | solution.py:32
  117.6 1.3 collective-permute-start.42
  118.9 1.8 %collective-permute-start.44 = (bf16[640,256]{1,0:T(8,128)(2,1)S(1)}, bf16[640,256]{1,0:T(8,128)(2,1)S(1)}, u32[]{:S(2)}, u32[]{:S(2)}) collective-permute-start(bf16[640,256]{1,0:T(8,128)(2,1)S(1)} %get-tuple-element.78), channel_id=1, source_target_pairs={{0,24},{8,16},{16,8},{24,0},{1,25},{9,17},{17,9},{25,1},{2,26},{10... | collective-permute-start | bytes 983048 | tf_op jit(solution)/shard_map/ppermute | solution.py:32
  121.2 2.4 %collective-permute-start.37 = (bf16[320,256]{1,0:T(8,128)(2,1)S(1)}, bf16[320,256]{1,0:T(8,128)(2,1)S(1)}, u32[]{:S(2)}, u32[]{:S(2)}) collective-permute-start(bf16[320,256]{1,0:T(8,128)(2,1)S(1)} %fusion.3), channel_id=1, source_target_pairs={{0,4},{1,5},{2,6},{3,7},{4,0},{5,1},{6,2},{7,3},{8,12},{9,13},{10,... | collective-permute-start | bytes 491528 | tf_op jit(solution)/shard_map/ppermute | solution.py:32
  124.4 4.0 %collective-permute-done.42 = bf16[640,256]{1,0:T(8,128)(2,1)S(1)} collective-permute-done((bf16[640,256]{1,0:T(8,128)(2,1)S(1)}, bf16[640,256]{1,0:T(8,128)(2,1)S(1)}, u32[]{:S(2)}, u32[]{:S(2)}) %collective-permute-start.42) | collective-permute-done | bytes 327712 | tf_op jit(solution)/shard_map/ppermute | solution.py:32
  128.4 6.4 %collective-permute-done.44 = bf16[640,256]{1,0:T(8,128)(2,1)S(1)} collective-permute-done((bf16[640,256]{1,0:T(8,128)(2,1)S(1)}, bf16[640,256]{1,0:T(8,128)(2,1)S(1)}, u32[]{:S(2)}, u32[]{:S(2)}) %collective-permute-start.44) | collective-permute-done | bytes 327712 | tf_op jit(solution)/shard_map/ppermute | solution.py:32
  134.7 1.4 collective-permute-done.43
  136.3 1.4 collective-permute-start.45
  138.9 3.3 %collective-permute-done.45 = bf16[320,256]{1,0:T(8,128)(2,1)S(1)} collective-permute-done((bf16[320,256]{1,0:T(8,128)(2,1)S(1)}, bf16[320,256]{1,0:T(8,128)(2,1)S(1)}, u32[]{:S(2)}, u32[]{:S(2)}) %collective-permute-start.45) | collective-permute-done | bytes 163872 | tf_op jit(solution)/shard_map/ppermute | solution.py:32
  142.3 1.8 %collective-permute-start.46 = (bf16[320,256]{1,0:T(8,128)(2,1)S(1)}, bf16[320,256]{1,0:T(8,128)(2,1)S(1)}, u32[]{:S(2)}, u32[]{:S(2)}) collective-permute-start(bf16[320,256]{1,0:T(8,128)(2,1)S(1)} %fusion.4), channel_id=1, source_target_pairs={{0,4},{1,5},{2,6},{3,7},{4,0},{5,1},{6,2},{7,3},{8,12},{9,13},{10,... | collective-permute-start | bytes 491528 | tf_op jit(solution)/shard_map/ppermute | solution.py:32
  144.2 2.1 %collective-permute-start.38 = (bf16[320,256]{1,0:T(8,128)(2,1)S(1)}, bf16[320,256]{1,0:T(8,128)(2,1)S(1)}, u32[]{:S(2)}, u32[]{:S(2)}) collective-permute-start(bf16[320,256]{1,0:T(8,128)(2,1)S(1)} %add_convert_fusion.2.refs_4_), channel_id=1, source_target_pairs={{0,2},{1,3},{2,0},{3,1},{4,6},{5,7},{6,4},{7,5},{8,10},{9,11},{10,... | collective-permute-start | bytes 491528 | tf_op jit(solution)/shard_map/ppermute | solution.py:32
  146.4 5.4 %collective-permute-done.46 = bf16[320,256]{1,0:T(8,128)(2,1)S(1)} collective-permute-done((bf16[320,256]{1,0:T(8,128)(2,1)S(1)}, bf16[320,256]{1,0:T(8,128)(2,1)S(1)}, u32[]{:S(2)}, u32[]{:S(2)}) %collective-permute-start.46) | collective-permute-done | bytes 163872 | tf_op jit(solution)/shard_map/ppermute | solution.py:32
  152.0 6.5 %collective-permute-done.32.refs_1_ = bf16[384,256]{1,0:T(8,128)(2,1)S(1)} collective-permute-done((bf16[384,256]{1,0:T(8,128)(2,1)S(1)}, bf16[384,256]{1,0:T(8,128)(2,1)S(1)}, u32[]{:S(2)}, u32[]{:S(2)}) %collective-permute-start.32) | collective-permute-done | bytes 196640 | tf_op jit(solution)/shard_map/ppermute | solution.py:32
  159.0 2.7 %collective-permute-done.47.refs_9_ = bf16[320,256]{1,0:T(8,128)(2,1)S(1)} collective-permute-done((bf16[320,256]{1,0:T(8,128)(2,1)S(1)}, bf16[320,256]{1,0:T(8,128)(2,1)S(1)}, u32[]{:S(2)}, u32[]{:S(2)}) %collective-permute-start.47) | collective-permute-done | bytes 163872 | tf_op jit(solution)/shard_map/ppermute | solution.py:32
  161.7 1.4 collective-permute-done.49.refs_11_
  163.1 2.8 %assemble.1 = (f32[4096,128]{1,0:T(8,128)}, f32[4096,128]{1,0:T(8,128)}) custom-call(s32[3]{0:T(128)S(1)} %pad_add_fusion.ids, bf16[384,256]{1,0:T(8,128)(2,1)S(1)} %add_convert_fusion.refs_0_, bf16[384,256]{1,0:T(8,128)(2,1)S(1)} %collective-permute-done.32.refs_1_, bf16[384,256]{1,0:T(8,128)(2,1)S(1)} %collective-permute-done.33.refs_2_, ...), custom_call_target="tpu_custom_call" | custom-call | tf_op jit(solution)/shard_map/assemble/pallas_call | solution.py:48
  (97 shorter events, 17.6 us)
Async XLA Ops:
  2.9 15.9 %collective-permute-start.4 = (bf16[1024,256]{1,0:T(8,128)(2,1)}, bf16[1024,256]{1,0:T(8,128)(2,1)S(1)}, u32[]{:S(2)}, u32[]{:S(2)}) collective-permute-start(bf16[1024,256]{1,0:T(8,128)(2,1)} %pad_maximum_fusion), channel_id=1, source_target_pairs={{0,16},{8,24},{16,0},{24,8},{1,17},{9,25},{17,1},{25,9},{2,18},{10... | collective-permute-start | bytes 1572872 | tf_op jit(solution)/shard_map/ppermute | solution.py:32
  5.9 15.1 %collective-permute-start = (bf16[1024,256]{1,0:T(8,128)(2,1)}, bf16[1024,256]{1,0:T(8,128)(2,1)S(1)}, u32[]{:S(2)}, u32[]{:S(2)}) collective-permute-start(bf16[1024,256]{1,0:T(8,128)(2,1)} %pad_maximum_fusion), channel_id=1, source_target_pairs={{0,8},{8,0},{16,24},{24,16},{1,9},{9,1},{17,25},{25,17},{2,10},{10... | collective-permute-start | bytes 1572872 | tf_op jit(solution)/shard_map/ppermute | solution.py:32
  8.2 22.0 %collective-permute-start.5 = (bf16[1024,256]{1,0:T(8,128)(2,1)}, bf16[1024,256]{1,0:T(8,128)(2,1)}, u32[]{:S(2)}, u32[]{:S(2)}) collective-permute-start(bf16[1024,256]{1,0:T(8,128)(2,1)} %pad_maximum_fusion.1), channel_id=1, source_target_pairs={{0,16},{8,24},{16,0},{24,8},{1,17},{9,25},{17,1},{25,9},{2,18},{10... | collective-permute-start | bytes 1572872 | tf_op jit(solution)/shard_map/ppermute | solution.py:32
  8.7 23.5 %collective-permute-start.1 = (bf16[1024,256]{1,0:T(8,128)(2,1)}, bf16[1024,256]{1,0:T(8,128)(2,1)}, u32[]{:S(2)}, u32[]{:S(2)}) collective-permute-start(bf16[1024,256]{1,0:T(8,128)(2,1)} %pad_maximum_fusion.1), channel_id=1, source_target_pairs={{0,8},{8,0},{16,24},{24,16},{1,9},{9,1},{17,25},{25,17},{2,10},{10... | collective-permute-start | bytes 1572872 | tf_op jit(solution)/shard_map/ppermute | solution.py:32
  18.9 13.4 %collective-permute-start.6 = (bf16[1024,256]{1,0:T(8,128)(2,1)S(1)}, bf16[1024,256]{1,0:T(8,128)(2,1)}, u32[]{:S(2)}, u32[]{:S(2)}) collective-permute-start(bf16[1024,256]{1,0:T(8,128)(2,1)S(1)} %collective-permute-done.4.refs_6_), channel_id=1, source_target_pairs={{0,1},{1,0},{2,3},{3,2},{4,5},{5,4},{6,7},{7,6},{8,9},{9,8},{10,11... | collective-permute-start | bytes 1572872 | tf_op jit(solution)/shard_map/ppermute | solution.py:32
  21.0 19.5 %collective-permute-start.8 = (bf16[1024,256]{1,0:T(8,128)(2,1)S(1)}, bf16[1024,256]{1,0:T(8,128)(2,1)S(1)}, u32[]{:S(2)}, u32[]{:S(2)}) collective-permute-start(bf16[1024,256]{1,0:T(8,128)(2,1)S(1)} %collective-permute-done.refs_2_), channel_id=1, source_target_pairs={{0,16},{8,24},{16,0},{24,8},{1,17},{9,25},{17,1},{25,9},{2,18},{10... | collective-permute-start | bytes 1572872 | tf_op jit(solution)/shard_map/ppermute | solution.py:32
  21.0 14.5 %collective-permute-start.2 = (bf16[1024,256]{1,0:T(8,128)(2,1)S(1)}, bf16[1024,256]{1,0:T(8,128)(2,1)S(1)}, u32[]{:S(2)}, u32[]{:S(2)}) collective-permute-start(bf16[1024,256]{1,0:T(8,128)(2,1)S(1)} %collective-permute-done.refs_2_), channel_id=1, source_target_pairs={{0,1},{1,0},{2,3},{3,2},{4,5},{5,4},{6,7},{7,6},{8,9},{9,8},{10,11... | collective-permute-start | bytes 1572872 | tf_op jit(solution)/shard_map/ppermute | solution.py:32
  30.2 12.5 %collective-permute-start.9 = (bf16[1024,256]{1,0:T(8,128)(2,1)}, bf16[1024,256]{1,0:T(8,128)(2,1)S(1)}, u32[]{:S(2)}, u32[]{:S(2)}) collective-permute-start(bf16[1024,256]{1,0:T(8,128)(2,1)} %collective-permute-done.5.refs_7_), channel_id=1, source_target_pairs={{0,8},{8,0},{16,24},{24,16},{1,9},{9,1},{17,25},{25,17},{2,10},{10... | collective-permute-start | bytes 1572872 | tf_op jit(solution)/shard_map/ppermute | solution.py:32
  32.2 3.3 %collective-permute-start.7 = (bf16[1024,256]{1,0:T(8,128)(2,1)}, bf16[1024,256]{1,0:T(8,128)(2,1)S(1)}, u32[]{:S(2)}, u32[]{:S(2)}) collective-permute-start(bf16[1024,256]{1,0:T(8,128)(2,1)} %collective-permute-done.5.refs_7_), channel_id=1, source_target_pairs={{0,1},{1,0},{2,3},{3,2},{4,5},{5,4},{6,7},{7,6},{8,9},{9,8},{10,11... | collective-permute-start | bytes 1572872 | tf_op jit(solution)/shard_map/ppermute | solution.py:32
  32.2 3.3 %collective-permute-start.3 = (bf16[1024,256]{1,0:T(8,128)(2,1)}, bf16[1024,256]{1,0:T(8,128)(2,1)S(1)}, u32[]{:S(2)}, u32[]{:S(2)}) collective-permute-start(bf16[1024,256]{1,0:T(8,128)(2,1)} %collective-permute-done.1.refs_3_), channel_id=1, source_target_pairs={{0,1},{1,0},{2,3},{3,2},{4,5},{5,4},{6,7},{7,6},{8,9},{9,8},{10,11... | collective-permute-start | bytes 1572872 | tf_op jit(solution)/shard_map/ppermute | solution.py:32
  42.7 2.0 %collective-permute-start.10 = (bf16[1024,256]{1,0:T(8,128)(2,1)S(1)}, bf16[1024,256]{1,0:T(8,128)(2,1)S(1)}, u32[]{:S(2)}, u32[]{:S(2)}) collective-permute-start(bf16[1024,256]{1,0:T(8,128)(2,1)S(1)} %collective-permute-done.8.refs_1_), channel_id=1, source_target_pairs={{0,1},{1,0},{2,3},{3,2},{4,5},{5,4},{6,7},{7,6},{8,9},{9,8},{10,11... | collective-permute-start | bytes 1572872 | tf_op jit(solution)/shard_map/ppermute | solution.py:32
  42.8 2.6 %collective-permute-start.11 = (bf16[1024,256]{1,0:T(8,128)(2,1)S(1)}, bf16[1024,256]{1,0:T(8,128)(2,1)S(1)}, u32[]{:S(2)}, u32[]{:S(2)}) collective-permute-start(bf16[1024,256]{1,0:T(8,128)(2,1)S(1)} %collective-permute-done.9.refs_2_), channel_id=1, source_target_pairs={{0,1},{1,0},{2,3},{3,2},{4,5},{5,4},{6,7},{7,6},{8,9},{9,8},{10,11... | collective-permute-start | bytes 1572872 | tf_op jit(solution)/shard_map/ppermute | solution.py:32
  46.6 7.6 %collective-permute-start.14 = (bf16[192,256]{1,0:T(8,128)(2,1)S(1)}, bf16[192,256]{1,0:T(8,128)(2,1)S(1)}, u32[]{:S(2)}, u32[]{:S(2)}) collective-permute-start(bf16[192,256]{1,0:T(8,128)(2,1)S(1)} %project.3.refs_0_), channel_id=1, source_target_pairs={{0,6},{1,7},{2,4},{3,5},{4,2},{5,3},{6,0},{7,1},{8,14},{9,15},{10,... | collective-permute-start | bytes 294920 | tf_op jit(solution)/shard_map/ppermute | solution.py:32
  50.2 8.6 %collective-permute-start.13 = (bf16[192,256]{1,0:T(8,128)(2,1)S(1)}, bf16[192,256]{1,0:T(8,128)(2,1)S(1)}, u32[]{:S(2)}, u32[]{:S(2)}) collective-permute-start(bf16[192,256]{1,0:T(8,128)(2,1)S(1)} %project.3.refs_0_), channel_id=1, source_target_pairs={{0,4},{1,5},{2,6},{3,7},{4,0},{5,1},{6,2},{7,3},{8,12},{9,13},{10,... | collective-permute-start | bytes 294920 | tf_op jit(solution)/shard_map/ppermute | solution.py:32
  50.2 8.6 %collective-permute-start.12 = (bf16[192,256]{1,0:T(8,128)(2,1)S(1)}, bf16[192,256]{1,0:T(8,128)(2,1)S(1)}, u32[]{:S(2)}, u32[]{:S(2)}) collective-permute-start(bf16[192,256]{1,0:T(8,128)(2,1)S(1)} %project.3.refs_0_), channel_id=1, source_target_pairs={{0,2},{1,3},{2,0},{3,1},{4,6},{5,7},{6,4},{7,5},{8,10},{9,11},{10,... | collective-permute-start | bytes 294920 | tf_op jit(solution)/shard_map/ppermute | solution.py:32
  51.0 39.8 %collective-permute-start.26 = (bf16[192,2816]{1,0:T(8,128)(2,1)S(1)}, bf16[192,2816]{1,0:T(8,128)(2,1)S(1)}, u32[]{:S(2)}, u32[]{:S(2)}) collective-permute-start(bf16[192,2816]{1,0:T(8,128)(2,1)S(1)} %get-tuple-element.52), channel_id=1, source_target_pairs={{0,8},{8,0},{16,24},{24,16},{1,9},{9,1},{17,25},{25,17},{2,10},{10... | collective-permute-start | bytes 3244040 | tf_op jit(solution)/shard_map/ppermute | solution.py:32
  52.4 50.3 %collective-permute-start.27 = (bf16[192,2816]{1,0:T(8,128)(2,1)S(1)}, bf16[192,2816]{1,0:T(8,128)(2,1)S(1)}, u32[]{:S(2)}, u32[]{:S(2)}) collective-permute-start(bf16[192,2816]{1,0:T(8,128)(2,1)S(1)} %get-tuple-element.53), channel_id=1, source_target_pairs={{0,16},{8,24},{16,0},{24,8},{1,17},{9,25},{17,1},{25,9},{2,18},{10... | collective-permute-start | bytes 3244040 | tf_op jit(solution)/shard_map/ppermute | solution.py:32
  58.7 46.0 %collective-permute-start.28 = (bf16[192,2816]{1,0:T(8,128)(2,1)S(1)}, bf16[192,2816]{1,0:T(8,128)(2,1)S(1)}, u32[]{:S(2)}, u32[]{:S(2)}) collective-permute-start(bf16[192,2816]{1,0:T(8,128)(2,1)S(1)} %get-tuple-element.54), channel_id=1, source_target_pairs={{0,24},{8,16},{16,8},{24,0},{1,25},{9,17},{17,9},{25,1},{2,26},{10... | collective-permute-start | bytes 3244040 | tf_op jit(solution)/shard_map/ppermute | solution.py:32
  61.2 1.5 collective-permute-start.16
  62.6 1.3 collective-permute-start.18
  73.5 1.7 %collective-permute-start.19 = (bf16[768,256]{1,0:T(8,128)(2,1)S(1)}, bf16[768,256]{1,0:T(8,128)(2,1)S(1)}, u32[]{:S(2)}, u32[]{:S(2)}) collective-permute-start(bf16[768,256]{1,0:T(8,128)(2,1)S(1)} %get-tuple-element.47), channel_id=1, source_target_pairs={{0,1},{1,0},{2,3},{3,2},{4,5},{5,4},{6,7},{7,6},{8,9},{9,8},{10,11... | collective-permute-start | bytes 1179656 | tf_op jit(solution)/shard_map/ppermute | solution.py:32
  75.4 6.9 %collective-permute-start.20 = (bf16[192,256]{1,0:T(8,128)(2,1)S(1)}, bf16[192,256]{1,0:T(8,128)(2,1)S(1)}, u32[]{:S(2)}, u32[]{:S(2)}) collective-permute-start(bf16[192,256]{1,0:T(8,128)(2,1)S(1)} %get-tuple-element.49), channel_id=1, source_target_pairs={{0,2},{1,3},{2,0},{3,1},{4,6},{5,7},{6,4},{7,5},{8,10},{9,11},{10,... | collective-permute-start | bytes 294920 | tf_op jit(solution)/shard_map/ppermute | solution.py:32
  76.0 8.2 %collective-permute-start.21 = (bf16[192,256]{1,0:T(8,128)(2,1)S(1)}, bf16[192,256]{1,0:T(8,128)(2,1)S(1)}, u32[]{:S(2)}, u32[]{:S(2)}) collective-permute-start(bf16[192,256]{1,0:T(8,128)(2,1)S(1)} %get-tuple-element.50), channel_id=1, source_target_pairs={{0,4},{1,5},{2,6},{3,7},{4,0},{5,1},{6,2},{7,3},{8,12},{9,13},{10,... | collective-permute-start | bytes 294920 | tf_op jit(solution)/shard_map/ppermute | solution.py:32
  82.2 6.4 %collective-permute-start.22 = (bf16[192,256]{1,0:T(8,128)(2,1)S(1)}, bf16[192,256]{1,0:T(8,128)(2,1)S(1)}, u32[]{:S(2)}, u32[]{:S(2)}) collective-permute-start(bf16[192,256]{1,0:T(8,128)(2,1)S(1)} %get-tuple-element.51), channel_id=1, source_target_pairs={{0,6},{1,7},{2,4},{3,5},{4,2},{5,3},{6,0},{7,1},{8,14},{9,15},{10,... | collective-permute-start | bytes 294920 | tf_op jit(solution)/shard_map/ppermute | solution.py:32
  88.7 14.8 %collective-permute-start.25 = (bf16[192,256]{1,0:T(8,128)(2,1)S(1)}, bf16[192,256]{1,0:T(8,128)(2,1)S(1)}, u32[]{:S(2)}, u32[]{:S(2)}) collective-permute-start(bf16[192,256]{1,0:T(8,128)(2,1)S(1)} %total.1.refs_4_.refs_1_), channel_id=1, source_target_pairs={{0,24},{8,16},{16,8},{24,0},{1,25},{9,17},{17,9},{25,1},{2,26},{10... | collective-permute-start | bytes 294920 | tf_op jit(solution)/shard_map/ppermute | solution.py:32
  89.3 15.5 %collective-permute-start.24 = (bf16[192,256]{1,0:T(8,128)(2,1)S(1)}, bf16[192,256]{1,0:T(8,128)(2,1)S(1)}, u32[]{:S(2)}, u32[]{:S(2)}) collective-permute-start(bf16[192,256]{1,0:T(8,128)(2,1)S(1)} %total.1.refs_4_.refs_1_), channel_id=1, source_target_pairs={{0,16},{8,24},{16,0},{24,8},{1,17},{9,25},{17,1},{25,9},{2,18},{10... | collective-permute-start | bytes 294920 | tf_op jit(solution)/shard_map/ppermute | solution.py:32
  90.8 14.0 %collective-permute-start.23 = (bf16[192,256]{1,0:T(8,128)(2,1)S(1)}, bf16[192,256]{1,0:T(8,128)(2,1)S(1)}, u32[]{:S(2)}, u32[]{:S(2)}) collective-permute-start(bf16[192,256]{1,0:T(8,128)(2,1)S(1)} %total.1.refs_4_.refs_1_), channel_id=1, source_target_pairs={{0,8},{8,0},{16,24},{24,16},{1,9},{9,1},{17,25},{25,17},{2,10},{10... | collective-permute-start | bytes 294920 | tf_op jit(solution)/shard_map/ppermute | solution.py:32
  106.2 11.0 %collective-permute-start.41 = (bf16[2560,256]{1,0:T(8,128)(2,1)S(1)}, bf16[2560,256]{1,0:T(8,128)(2,1)S(1)}, u32[]{:S(2)}, u32[]{:S(2)}) collective-permute-start(bf16[2560,256]{1,0:T(8,128)(2,1)S(1)} %get-tuple-element.67), channel_id=1, source_target_pairs={{0,1},{1,0},{2,3},{3,2},{4,5},{5,4},{6,7},{7,6},{8,9},{9,8},{10,11... | collective-permute-start | bytes 3932168 | tf_op jit(solution)/shard_map/ppermute | solution.py:32
  107.8 2.3 %collective-permute-start.35 = (bf16[640,256]{1,0:T(8,128)(2,1)S(1)}, bf16[640,256]{1,0:T(8,128)(2,1)S(1)}, u32[]{:S(2)}, u32[]{:S(2)}) collective-permute-start(bf16[640,256]{1,0:T(8,128)(2,1)S(1)} %get-tuple-element.64), channel_id=1, source_target_pairs={{0,1},{1,0},{2,3},{3,2},{4,5},{5,4},{6,7},{7,6},{8,9},{9,8},{10,11... | collective-permute-start | bytes 983048 | tf_op jit(solution)/shard_map/ppermute | solution.py:32
  110.0 1.8 %collective-permute-start.29 = (bf16[768,256]{1,0:T(8,128)(2,1)S(1)}, bf16[768,256]{1,0:T(8,128)(2,1)S(1)}, u32[]{:S(2)}, u32[]{:S(2)}) collective-permute-start(bf16[768,256]{1,0:T(8,128)(2,1)S(1)} %get-tuple-element.62), channel_id=1, source_target_pairs={{0,1},{1,0},{2,3},{3,2},{4,5},{5,4},{6,7},{7,6},{8,9},{9,8},{10,11... | collective-permute-start | bytes 1179656 | tf_op jit(solution)/shard_map/ppermute | solution.py:32
  110.1 7.1 %collective-permute-start.36 = (bf16[320,256]{1,0:T(8,128)(2,1)S(1)}, bf16[320,256]{1,0:T(8,128)(2,1)S(1)}, u32[]{:S(2)}, u32[]{:S(2)}) collective-permute-start(bf16[320,256]{1,0:T(8,128)(2,1)S(1)} %slice.81), channel_id=1, source_target_pairs={{0,2},{1,3},{2,0},{3,1},{4,6},{5,7},{6,4},{7,5},{8,10},{9,11},{10,... | collective-permute-start | bytes 491528 | tf_op jit(solution)/shard_map/ppermute | solution.py:32
  111.9 11.7 %collective-permute-start.30 = (bf16[384,256]{1,0:T(8,128)(2,1)S(1)}, bf16[384,256]{1,0:T(8,128)(2,1)S(1)}, u32[]{:S(2)}, u32[]{:S(2)}) collective-permute-start(bf16[384,256]{1,0:T(8,128)(2,1)S(1)} %slice.79), channel_id=1, source_target_pairs={{0,2},{1,3},{2,0},{3,1},{4,6},{5,7},{6,4},{7,5},{8,10},{9,11},{10,... | collective-permute-start | bytes 589832 | tf_op jit(solution)/shard_map/ppermute | solution.py:32
  117.6 10.7 %collective-permute-start.42 = (bf16[640,256]{1,0:T(8,128)(2,1)S(1)}, bf16[640,256]{1,0:T(8,128)(2,1)S(1)}, u32[]{:S(2)}, u32[]{:S(2)}) collective-permute-start(bf16[640,256]{1,0:T(8,128)(2,1)S(1)} %get-tuple-element.77), channel_id=1, source_target_pairs={{0,8},{8,0},{16,24},{24,16},{1,9},{9,1},{17,25},{25,17},{2,10},{10... | collective-permute-start | bytes 983048 | tf_op jit(solution)/shard_map/ppermute | solution.py:32
  118.9 15.8 %collective-permute-start.44 = (bf16[640,256]{1,0:T(8,128)(2,1)S(1)}, bf16[640,256]{1,0:T(8,128)(2,1)S(1)}, u32[]{:S(2)}, u32[]{:S(2)}) collective-permute-start(bf16[640,256]{1,0:T(8,128)(2,1)S(1)} %get-tuple-element.78), channel_id=1, source_target_pairs={{0,24},{8,16},{16,8},{24,0},{1,25},{9,17},{17,9},{25,1},{2,26},{10... | collective-permute-start | bytes 983048 | tf_op jit(solution)/shard_map/ppermute | solution.py:32
  120.7 15.4 %collective-permute-start.43 = (bf16[640,256]{1,0:T(8,128)(2,1)S(1)}, bf16[640,256]{1,0:T(8,128)(2,1)S(1)}, u32[]{:S(2)}, u32[]{:S(2)}) collective-permute-start(bf16[640,256]{1,0:T(8,128)(2,1)S(1)} %get-tuple-element.79), channel_id=1, source_target_pairs={{0,16},{8,24},{16,0},{24,8},{1,17},{9,25},{17,1},{25,9},{2,18},{10... | collective-permute-start | bytes 983048 | tf_op jit(solution)/shard_map/ppermute | solution.py:32
  121.2 22.8 %collective-permute-start.37 = (bf16[320,256]{1,0:T(8,128)(2,1)S(1)}, bf16[320,256]{1,0:T(8,128)(2,1)S(1)}, u32[]{:S(2)}, u32[]{:S(2)}) collective-permute-start(bf16[320,256]{1,0:T(8,128)(2,1)S(1)} %fusion.3), channel_id=1, source_target_pairs={{0,4},{1,5},{2,6},{3,7},{4,0},{5,1},{6,2},{7,3},{8,12},{9,13},{10,... | collective-permute-start | bytes 491528 | tf_op jit(solution)/shard_map/ppermute | solution.py:32
  123.7 15.2 %collective-permute-start.31 = (bf16[384,256]{1,0:T(8,128)(2,1)S(1)}, bf16[384,256]{1,0:T(8,128)(2,1)S(1)}, u32[]{:S(2)}, u32[]{:S(2)}) collective-permute-start(bf16[384,256]{1,0:T(8,128)(2,1)S(1)} %fusion.2), channel_id=1, source_target_pairs={{0,4},{1,5},{2,6},{3,7},{4,0},{5,1},{6,2},{7,3},{8,12},{9,13},{10,... | collective-permute-start | bytes 589832 | tf_op jit(solution)/shard_map/ppermute | solution.py:32
  136.3 6.0 %collective-permute-start.45 = (bf16[320,256]{1,0:T(8,128)(2,1)S(1)}, bf16[320,256]{1,0:T(8,128)(2,1)S(1)}, u32[]{:S(2)}, u32[]{:S(2)}) collective-permute-start(bf16[320,256]{1,0:T(8,128)(2,1)S(1)} %slice.80), channel_id=1, source_target_pairs={{0,2},{1,3},{2,0},{3,1},{4,6},{5,7},{6,4},{7,5},{8,10},{9,11},{10,... | collective-permute-start | bytes 491528 | tf_op jit(solution)/shard_map/ppermute | solution.py:32
  142.3 9.5 %collective-permute-start.46 = (bf16[320,256]{1,0:T(8,128)(2,1)S(1)}, bf16[320,256]{1,0:T(8,128)(2,1)S(1)}, u32[]{:S(2)}, u32[]{:S(2)}) collective-permute-start(bf16[320,256]{1,0:T(8,128)(2,1)S(1)} %fusion.4), channel_id=1, source_target_pairs={{0,4},{1,5},{2,6},{3,7},{4,0},{5,1},{6,2},{7,3},{8,12},{9,13},{10,... | collective-permute-start | bytes 491528 | tf_op jit(solution)/shard_map/ppermute | solution.py:32
  144.1 14.8 %collective-permute-start.39 = (bf16[320,256]{1,0:T(8,128)(2,1)S(1)}, bf16[320,256]{1,0:T(8,128)(2,1)S(1)}, u32[]{:S(2)}, u32[]{:S(2)}) collective-permute-start(bf16[320,256]{1,0:T(8,128)(2,1)S(1)} %add_convert_fusion.2.refs_4_), channel_id=1, source_target_pairs={{0,1},{1,0},{2,3},{3,2},{4,5},{5,4},{6,7},{7,6},{8,9},{9,8},{10,11... | collective-permute-start | bytes 491528 | tf_op jit(solution)/shard_map/ppermute | solution.py:32
  144.2 14.3 %collective-permute-start.38 = (bf16[320,256]{1,0:T(8,128)(2,1)S(1)}, bf16[320,256]{1,0:T(8,128)(2,1)S(1)}, u32[]{:S(2)}, u32[]{:S(2)}) collective-permute-start(bf16[320,256]{1,0:T(8,128)(2,1)S(1)} %add_convert_fusion.2.refs_4_), channel_id=1, source_target_pairs={{0,2},{1,3},{2,0},{3,1},{4,6},{5,7},{6,4},{7,5},{8,10},{9,11},{10,... | collective-permute-start | bytes 491528 | tf_op jit(solution)/shard_map/ppermute | solution.py:32
  146.3 12.1 %collective-permute-start.32 = (bf16[384,256]{1,0:T(8,128)(2,1)S(1)}, bf16[384,256]{1,0:T(8,128)(2,1)S(1)}, u32[]{:S(2)}, u32[]{:S(2)}) collective-permute-start(bf16[384,256]{1,0:T(8,128)(2,1)S(1)} %add_convert_fusion.refs_0_), channel_id=1, source_target_pairs={{0,2},{1,3},{2,0},{3,1},{4,6},{5,7},{6,4},{7,5},{8,10},{9,11},{10,... | collective-permute-start | bytes 589832 | tf_op jit(solution)/shard_map/ppermute | solution.py:32
  151.8 9.9 %collective-permute-start.47 = (bf16[320,256]{1,0:T(8,128)(2,1)S(1)}, bf16[320,256]{1,0:T(8,128)(2,1)S(1)}, u32[]{:S(2)}, u32[]{:S(2)}) collective-permute-start(bf16[320,256]{1,0:T(8,128)(2,1)S(1)} %add_convert_fusion.1.refs_8_), channel_id=1, source_target_pairs={{0,2},{1,3},{2,0},{3,1},{4,6},{5,7},{6,4},{7,5},{8,10},{9,11},{10,... | collective-permute-start | bytes 491528 | tf_op jit(solution)/shard_map/ppermute | solution.py:32
  151.9 9.8 %collective-permute-start.33 = (bf16[384,256]{1,0:T(8,128)(2,1)S(1)}, bf16[384,256]{1,0:T(8,128)(2,1)S(1)}, u32[]{:S(2)}, u32[]{:S(2)}) collective-permute-start(bf16[384,256]{1,0:T(8,128)(2,1)S(1)} %add_convert_fusion.refs_0_), channel_id=1, source_target_pairs={{0,1},{1,0},{2,3},{3,2},{4,5},{5,4},{6,7},{7,6},{8,9},{9,8},{10,11... | collective-permute-start | bytes 589832 | tf_op jit(solution)/shard_map/ppermute | solution.py:32
  158.4 3.3 %collective-permute-start.34 = (bf16[384,256]{1,0:T(8,128)(2,1)S(1)}, bf16[384,256]{1,0:T(8,128)(2,1)S(1)}, u32[]{:S(2)}, u32[]{:S(2)}) collective-permute-start(bf16[384,256]{1,0:T(8,128)(2,1)S(1)} %collective-permute-done.32.refs_1_), channel_id=1, source_target_pairs={{0,1},{1,0},{2,3},{3,2},{4,5},{5,4},{6,7},{7,6},{8,9},{9,8},{10,11... | collective-permute-start | bytes 589832 | tf_op jit(solution)/shard_map/ppermute | solution.py:32
  158.4 3.3 %collective-permute-start.40 = (bf16[320,256]{1,0:T(8,128)(2,1)S(1)}, bf16[320,256]{1,0:T(8,128)(2,1)S(1)}, u32[]{:S(2)}, u32[]{:S(2)}) collective-permute-start(bf16[320,256]{1,0:T(8,128)(2,1)S(1)} %collective-permute-done.38.refs_5_), channel_id=1, source_target_pairs={{0,1},{1,0},{2,3},{3,2},{4,5},{5,4},{6,7},{7,6},{8,9},{9,8},{10,11... | collective-permute-start | bytes 491528 | tf_op jit(solution)/shard_map/ppermute | solution.py:32
  159.0 2.8 %collective-permute-start.48 = (bf16[320,256]{1,0:T(8,128)(2,1)S(1)}, bf16[320,256]{1,0:T(8,128)(2,1)S(1)}, u32[]{:S(2)}, u32[]{:S(2)}) collective-permute-start(bf16[320,256]{1,0:T(8,128)(2,1)S(1)} %add_convert_fusion.1.refs_8_), channel_id=1, source_target_pairs={{0,1},{1,0},{2,3},{3,2},{4,5},{5,4},{6,7},{7,6},{8,9},{9,8},{10,11... | collective-permute-start | bytes 491528 | tf_op jit(solution)/shard_map/ppermute | solution.py:32
  161.7 1.4 collective-permute-start.49
  (10 other events, 133.8 us)

commit v7 on v6

--- a/solution.py
+++ b/solution.py
@@ -12,8 +12,8 @@
 NO_COST = pl.CostEstimate(flops=0, bytes_accessed=0, transcendentals=0)
 
 
-MOVED = (6, 5)
-TIED = 1
+MOVED = (4, 6)
+TIED = 2
 
 
 def region_sizes(block_rows):
@@ -297,18 +297,15 @@
         (out, out),
         (ids,),
         (*hidden, *grads),
-        cost=bytes_cost(1 << 23),
     )
     return ours.astype(jnp.float32) + swap(theirs, "ctx", 1).astype(jnp.float32)
 
 
-def send_over_dp(array):
+def parts_over_dp(array):
     count = lax.axis_size("dp")
     rows = array.shape[0] // count
-    leaving = [array[j * rows : (j + 1) * rows] for j in range(count)]
-    return leaving[:1] + [
-        swap(one.astype(jnp.bfloat16), "dp", j) for j, one in enumerate(leaving) if j
-    ]
+    parts = [array[j * rows : (j + 1) * rows] for j in range(count)]
+    return parts[:1] + [part.astype(jnp.bfloat16) for part in parts[1:]]
 
 
 def sum_of(arrays):
@@ -452,26 +449,33 @@
     moving.update(zip(far, tied))
     kv_blocks = both_cores(along)
 
+    kv_blocks, ended = after(kv_blocks, *[moved[j] for j in near])
+    moved.update(zip(near, ended))
+    tied, _ = after([moving[j] for j in far], *ended)
+    moved.update({j: swap(one, "dp", j) for j, one in zip(far, tied)})
     query_grad, keep, send = attention(
         me, stretch_order, doc_lengths[0], queries[0], grad_out[0], kv_blocks, head_dim
     )
-    moved.update({j: swap(moving[j], "dp", j) for j in far})
-
     own, *leaving = add_and_split(keep, swap(send, "ctx", 1), z_count)
     grad = add_all([own] + [swap(one, "ctx", 2 * m) for m, one in enumerate(leaving, 1)])
     grads = [grad] + [swap(grad, "dp", j) for j in range(1, dp_count)]
 
-    (grad,), ended = after([grad], *grads[1:], *[moved[j] for j in others])
+    (grad,), ended = after([grad], *grads[1:], *[moved[j] for j in far])
     grads[1:] = ended[: dp_count - 1]
-    moved.update(zip(others, ended[dp_count - 1 :]))
+    moved.update(zip(far, ended[dp_count - 1 :]))
     groups = [[(0, j, 0)] for j in range(dp_count)]
     own = weight_rows(ids, [inputs], [grad], groups, *regions[-1], block_rows, sub_count)
-    own = send_over_dp(own)
+    own = parts_over_dp(own)
     groups = [[(j, None, j) for j in range(dp_count)]]
     arrays = [moved[j] for j in range(dp_count)]
+    moved_parts = [
+        weight_rows(ids, arrays, grads, groups, *region, block_rows, sub_count)
+        for region in regions[:-1]
+    ]
+    moved_parts, own = after(moved_parts, *own)
+    own = [swap(one, "dp", j) if j else one for j, one in enumerate(own)]
     finals = []
-    for region in regions[:-1]:
-        part = weight_rows(ids, arrays, grads, groups, *region, block_rows, sub_count)
+    for part in moved_parts:
         part = scatter_along_z(part, sub_count)
         finals.append(sum_of_halves(part, sub_count))
     part = scatter_along_z(sum_of(own), sub_count, finals[:TIED])

time: 166 us -> 166 us (level)
  starting transfers between devices: 44.5 us -> 59.1 us
  waiting for transfers between devices: 90.6 us -> 76 us
    ppermute x50, starting transfers between devices: 44.5 us -> 59.1 us  [swap(): return lax.ppermute(array, axis, [(i, i ^ distance) for i in range(count)])]
    ppermute x50, waiting for transfers between devices: 90.6 us -> 76 us  [swap(): return lax.ppermute(array, axis, [(i, i ^ distance) for i in range(count)])]
  transfers between devices with their start and end apart: 50 -> 50, of which waited for: 29 -> 29; matrix products, arithmetic and copies ran while one was open for 3% -> 2% of each run, Pallas kernels for 10% -> 10%
where the time goes in v7:
time: 166 us
  waiting for transfers between devices  76 us (46%)
  starting transfers between devices  59.1 us (36%)
  Pallas kernels  21.5 us (13%)
  local copies, waits for them, and re-layouts  5.55 us (3%)
  other arithmetic  2.89 us (2%)
    ppermute x50, waiting for transfers between devices, swap(): return lax.ppermute(array, axis, [(i, i ^ distance) for i in range(count)])  76 us
    ppermute x50, starting transfers between devices, swap(): return lax.ppermute(array, axis, [(i, i ^ distance) for i in range(count)])  59.1 us
    pallas_call x8, Pallas kernels, kernel_call(): pl.pallas_call(kernel, out_shape=outs, in_specs=[smem] * len(scalars) + [...  11.9 us
    pallas_call x1, Pallas kernels, attention(): pl.pallas_call(functools.partial(attention_kernel, shape), out_shape=(jax...  9.6 us
  transfers between devices with their start and end apart: 50, of which 29 were waited for; matrix products, arithmetic and copies ran while one was open for 2% of the time, Pallas kernels for 10%

profile of v7, /device:TPU:0, one launch (start us, length us, event | category | flops | bytes accessed | tf_op | source)
XLA Modules:
  0.0 166.0 jit_solution(908918881234973603)
XLA Ops:
  0.7 1.4 constant_dynamic-slice_fusion
  2.9 3.0 %collective-permute-start.4 = (bf16[1024,256]{1,0:T(8,128)(2,1)}, bf16[1024,256]{1,0:T(8,128)(2,1)S(1)}, u32[]{:S(2)}, u32[]{:S(2)}) collective-permute-start(bf16[1024,256]{1,0:T(8,128)(2,1)} %pad_maximum_fusion), channel_id=1, source_target_pairs={{0,16},{8,24},{16,0},{24,8},{1,17},{9,25},{17,1},{25,9},{2,18},{10... | collective-permute-start | bytes 1572872 | tf_op jit(solution)/shard_map/ppermute | solution.py:32
  5.9 1.5 collective-permute-start
  8.8 10.1 %collective-permute-done.4.refs_6_ = bf16[1024,256]{1,0:T(8,128)(2,1)S(1)} collective-permute-done((bf16[1024,256]{1,0:T(8,128)(2,1)}, bf16[1024,256]{1,0:T(8,128)(2,1)S(1)}, u32[]{:S(2)}, u32[]{:S(2)}) %collective-permute-start.4) | collective-permute-done | bytes 524320 | tf_op jit(solution)/shard_map/ppermute | solution.py:32
  18.9 2.1 %collective-permute-done.refs_2_ = bf16[1024,256]{1,0:T(8,128)(2,1)S(1)} collective-permute-done((bf16[1024,256]{1,0:T(8,128)(2,1)}, bf16[1024,256]{1,0:T(8,128)(2,1)S(1)}, u32[]{:S(2)}, u32[]{:S(2)}) %collective-permute-start) | collective-permute-done | bytes 524320 | tf_op jit(solution)/shard_map/ppermute | solution.py:32
  21.2 9.0 %collective-permute-done.5.refs_7_ = bf16[1024,256]{1,0:T(8,128)(2,1)} collective-permute-done((bf16[1024,256]{1,0:T(8,128)(2,1)}, bf16[1024,256]{1,0:T(8,128)(2,1)}, u32[]{:S(2)}, u32[]{:S(2)}) %collective-permute-start.5) | collective-permute-done | bytes 524320 | tf_op jit(solution)/shard_map/ppermute | solution.py:32
  30.2 2.0 %collective-permute-start.9 = (bf16[1024,256]{1,0:T(8,128)(2,1)}, bf16[1024,256]{1,0:T(8,128)(2,1)S(1)}, u32[]{:S(2)}, u32[]{:S(2)}) collective-permute-start(bf16[1024,256]{1,0:T(8,128)(2,1)} %collective-permute-done.5.refs_7_), channel_id=1, source_target_pairs={{0,8},{8,0},{16,24},{24,16},{1,9},{9,1},{17,25},{25,17},{2,10},{10... | collective-permute-start | bytes 1572872 | tf_op jit(solution)/shard_map/ppermute | solution.py:32
  32.8 2.5 %dynamic-slice_bitcast_fusion = (bf16[192,2560]{1,0:T(8,128)(2,1)S(1)}, bf16[192,2560]{1,0:T(8,128)(2,1)S(1)}, bf16[192,2560]{1,0:T(8,128)(2,1)S(1)}, bf16[192,2560]{1,0:T(8,128)(2,1)S(1)}) fusion(bf16[1,192,16384]{2,1,0:T(8,128)(2,1)} %param.7, s32[]{:T(128)S(6)} %select_n.42, s32[]{:T(128)S(6)} %select_n.40, s32[]{:T(128)S(6)} %select_n.39, s32[]{:T(128)S(6)} %select_n.41), kind=kLoop, calls=%fused_computation.1 | loop fusion | bytes 7864336 | tf_op jit(solution)/shard_map/dynamic_slice | solution.py:430
  36.8 3.2 %project.2.refs_0_ = f32[192,256]{1,0:T(8,128)S(1)} custom-call(s32[3]{0:T(128)S(1)} %pad_add_fusion.ids, bf16[192,16384]{1,0:T(8,128)(2,1)S(1)} %bitcast.19, bf16[4096,128]{1,0:T(8,128)(2,1)S(1)} %copy-done, bf16[4096,128]{1,0:T(8,128)(2,1)S(1)} %copy-done.1, bf16[1024,256]{1,0:T(8,128)(2,1)S(1)} %collective-permute-done.refs_2_, ...), custom_call_target="tpu_custom_call" | custom-call | bytes 16777216 | tf_op jit(solution)/shard_map/project/pallas_call | solution.py:48
  40.5 2.2 %collective-permute-done.9.refs_2_ = bf16[1024,256]{1,0:T(8,128)(2,1)S(1)} collective-permute-done((bf16[1024,256]{1,0:T(8,128)(2,1)}, bf16[1024,256]{1,0:T(8,128)(2,1)S(1)}, u32[]{:S(2)}, u32[]{:S(2)}) %collective-permute-start.9) | collective-permute-done | bytes 524320 | tf_op jit(solution)/shard_map/ppermute | solution.py:32
  42.7 1.6 collective-permute-start.19
  44.3 1.5 collective-permute-start.20
  46.3 1.4 collective-permute-done.10.refs_3_
  48.5 1.1 project.3.refs_0_
  49.6 3.7 %collective-permute-start.14 = (bf16[192,256]{1,0:T(8,128)(2,1)S(1)}, bf16[192,256]{1,0:T(8,128)(2,1)S(1)}, u32[]{:S(2)}, u32[]{:S(2)}) collective-permute-start(bf16[192,256]{1,0:T(8,128)(2,1)S(1)} %project.3.refs_0_), channel_id=1, source_target_pairs={{0,6},{1,7},{2,4},{3,5},{4,2},{5,3},{6,0},{7,1},{8,14},{9,15},{10,... | collective-permute-start | bytes 294920 | tf_op jit(solution)/shard_map/ppermute | solution.py:32
  54.1 3.1 %collective-permute-done.14.refs_6_ = bf16[192,256]{1,0:T(8,128)(2,1)S(1)} collective-permute-done((bf16[192,256]{1,0:T(8,128)(2,1)S(1)}, bf16[192,256]{1,0:T(8,128)(2,1)S(1)}, u32[]{:S(2)}, u32[]{:S(2)}) %collective-permute-start.14) | collective-permute-done | bytes 98336 | tf_op jit(solution)/shard_map/ppermute | solution.py:32
  57.2 4.7 %collective-permute-done.13.refs_4_ = bf16[192,256]{1,0:T(8,128)(2,1)S(1)} collective-permute-done((bf16[192,256]{1,0:T(8,128)(2,1)S(1)}, bf16[192,256]{1,0:T(8,128)(2,1)S(1)}, u32[]{:S(2)}, u32[]{:S(2)}) %collective-permute-start.13) | collective-permute-done | bytes 98336 | tf_op jit(solution)/shard_map/ppermute | solution.py:32
  64.7 1.9 %collective-permute-start.28 = (bf16[192,2560]{1,0:T(8,128)(2,1)S(1)}, bf16[192,2560]{1,0:T(8,128)(2,1)S(1)}, u32[]{:S(2)}, u32[]{:S(2)}) collective-permute-start(bf16[192,2560]{1,0:T(8,128)(2,1)S(1)} %get-tuple-element.80), channel_id=1, source_target_pairs={{0,24},{8,16},{16,8},{24,0},{1,25},{9,17},{17,9},{25,1},{2,26},{10... | collective-permute-start | bytes 2949128 | tf_op jit(solution)/shard_map/ppermute | solution.py:32
  66.6 9.6 %attention.1 = (bf16[192,1024]{1,0:T(8,128)(2,1)}, f32[768,256]{1,0:T(8,128)S(1)}, bf16[768,256]{1,0:T(8,128)(2,1)S(1)}) custom-call(s32[1]{0:T(128)} %bitcast.ids, s32[16]{0:T(128)S(1)} %copy-done.4, s32[8]{0:T(128)S(1)} %bitcast.24, bf16[192,1024]{1,0:T(8,128)(2,1)S(1)} %bitcast.22, bf16[192,1024]{1,0:T(8,128)(2,1)S(1)} %bitcast.23, ...), custom_call_target="tpu_custom_call" | custom-call | tf_op jit(solution)/shard_map/attention/pallas_call | solution.py:168
  76.2 1.7 %collective-permute-done.21.came = bf16[768,256]{1,0:T(8,128)(2,1)S(1)} collective-permute-done((bf16[768,256]{1,0:T(8,128)(2,1)S(1)}, bf16[768,256]{1,0:T(8,128)(2,1)S(1)}, u32[]{:S(2)}, u32[]{:S(2)}) %collective-permute-start.21) | collective-permute-done | bytes 393248 | tf_op jit(solution)/shard_map/ppermute | solution.py:32
  78.0 1.6 collective-permute-start.22
  79.7 11.6 %collective-permute-start.23 = (bf16[192,256]{1,0:T(8,128)(2,1)S(1)}, bf16[192,256]{1,0:T(8,128)(2,1)S(1)}, u32[]{:S(2)}, u32[]{:S(2)}) collective-permute-start(bf16[192,256]{1,0:T(8,128)(2,1)S(1)} %get-tuple-element.77), channel_id=1, source_target_pairs={{0,4},{1,5},{2,6},{3,7},{4,0},{5,1},{6,2},{7,3},{8,12},{9,13},{10,... | collective-permute-start | bytes 294920 | tf_op jit(solution)/shard_map/ppermute | solution.py:32
  91.3 1.4 collective-permute-start.24
  92.7 1.8 %collective-permute-done.23.refs_2_ = bf16[192,256]{1,0:T(8,128)(2,1)S(1)} collective-permute-done((bf16[192,256]{1,0:T(8,128)(2,1)S(1)}, bf16[192,256]{1,0:T(8,128)(2,1)S(1)}, u32[]{:S(2)}, u32[]{:S(2)}) %collective-permute-start.23) | collective-permute-done | bytes 98336 | tf_op jit(solution)/shard_map/ppermute | solution.py:32
  94.5 5.3 %collective-permute-done.24.refs_3_ = bf16[192,256]{1,0:T(8,128)(2,1)S(1)} collective-permute-done((bf16[192,256]{1,0:T(8,128)(2,1)S(1)}, bf16[192,256]{1,0:T(8,128)(2,1)S(1)}, u32[]{:S(2)}, u32[]{:S(2)}) %collective-permute-start.24) | collective-permute-done | bytes 98336 | tf_op jit(solution)/shard_map/ppermute | solution.py:32
  100.0 3.4 %collective-permute-start.25 = (bf16[192,256]{1,0:T(8,128)(2,1)S(1)}, bf16[192,256]{1,0:T(8,128)(2,1)S(1)}, u32[]{:S(2)}, u32[]{:S(2)}) collective-permute-start(bf16[192,256]{1,0:T(8,128)(2,1)S(1)} %total.1.refs_4_.refs_1_), channel_id=1, source_target_pairs={{0,8},{8,0},{16,24},{24,16},{1,9},{9,1},{17,25},{25,17},{2,10},{10... | collective-permute-start | bytes 294920 | tf_op jit(solution)/shard_map/ppermute | solution.py:32
  103.4 2.6 %collective-permute-done.27.refs_7_ = bf16[192,256]{1,0:T(8,128)(2,1)S(1)} collective-permute-done((bf16[192,256]{1,0:T(8,128)(2,1)S(1)}, bf16[192,256]{1,0:T(8,128)(2,1)S(1)}, u32[]{:S(2)}, u32[]{:S(2)}) %collective-permute-start.27) | collective-permute-done | bytes 98336 | tf_op jit(solution)/shard_map/ppermute | solution.py:32
  106.1 1.7 weight_rows.5
  107.8 1.3 weight_rows.3
  109.7 1.6 weight_rows.4
  111.6 1.4 collective-permute-done.30
  113.9 2.5 %collective-permute-start.32 = (bf16[256,256]{1,0:T(8,128)(2,1)S(1)}, bf16[256,256]{1,0:T(8,128)(2,1)S(1)}, u32[]{:S(2)}, u32[]{:S(2)}) collective-permute-start(bf16[256,256]{1,0:T(8,128)(2,1)S(1)} %slice.74), channel_id=1, source_target_pairs={{0,2},{1,3},{2,0},{3,1},{4,6},{5,7},{6,4},{7,5},{8,10},{9,11},{10,... | collective-permute-start | bytes 393224 | tf_op jit(solution)/shard_map/ppermute | solution.py:32
  116.4 1.6 collective-permute-start.42
  118.2 1.8 %collective-permute-start.44 = (bf16[768,256]{1,0:T(8,128)(2,1)S(1)}, bf16[768,256]{1,0:T(8,128)(2,1)S(1)}, u32[]{:S(2)}, u32[]{:S(2)}) collective-permute-start(bf16[768,256]{1,0:T(8,128)(2,1)S(1)} %get-tuple-element.97), channel_id=1, source_target_pairs={{0,24},{8,16},{16,8},{24,0},{1,25},{9,17},{17,9},{25,1},{2,26},{10... | collective-permute-start | bytes 1179656 | tf_op jit(solution)/shard_map/ppermute | solution.py:32
  120.6 4.0 %collective-permute-start.33 = (bf16[256,256]{1,0:T(8,128)(2,1)S(1)}, bf16[256,256]{1,0:T(8,128)(2,1)S(1)}, u32[]{:S(2)}, u32[]{:S(2)}) collective-permute-start(bf16[256,256]{1,0:T(8,128)(2,1)S(1)} %fusion.2), channel_id=1, source_target_pairs={{0,4},{1,5},{2,6},{3,7},{4,0},{5,1},{6,2},{7,3},{8,12},{9,13},{10,... | collective-permute-start | bytes 393224 | tf_op jit(solution)/shard_map/ppermute | solution.py:32
  124.7 1.1 collective-permute-done.37
  125.8 3.1 %collective-permute-start.38 = (bf16[384,256]{1,0:T(8,128)(2,1)S(1)}, bf16[384,256]{1,0:T(8,128)(2,1)S(1)}, u32[]{:S(2)}, u32[]{:S(2)}) collective-permute-start(bf16[384,256]{1,0:T(8,128)(2,1)S(1)} %fusion), channel_id=1, source_target_pairs={{0,4},{1,5},{2,6},{3,7},{4,0},{5,1},{6,2},{7,3},{8,12},{9,13},{10,... | collective-permute-start | bytes 589832 | tf_op jit(solution)/shard_map/ppermute | solution.py:32
  128.9 5.8 %collective-permute-done.33 = bf16[256,256]{1,0:T(8,128)(2,1)S(1)} collective-permute-done((bf16[256,256]{1,0:T(8,128)(2,1)S(1)}, bf16[256,256]{1,0:T(8,128)(2,1)S(1)}, u32[]{:S(2)}, u32[]{:S(2)}) %collective-permute-start.33) | collective-permute-done | bytes 131104 | tf_op jit(solution)/shard_map/ppermute | solution.py:32
  134.8 2.1 %collective-permute-done.43 = bf16[768,256]{1,0:T(8,128)(2,1)S(1)} collective-permute-done((bf16[768,256]{1,0:T(8,128)(2,1)S(1)}, bf16[768,256]{1,0:T(8,128)(2,1)S(1)}, u32[]{:S(2)}, u32[]{:S(2)}) %collective-permute-start.43) | collective-permute-done | bytes 393248 | tf_op jit(solution)/shard_map/ppermute | solution.py:32
  137.1 1.7 %collective-permute-start.45 = (bf16[384,256]{1,0:T(8,128)(2,1)S(1)}, bf16[384,256]{1,0:T(8,128)(2,1)S(1)}, u32[]{:S(2)}, u32[]{:S(2)}) collective-permute-start(bf16[384,256]{1,0:T(8,128)(2,1)S(1)} %slice.72), channel_id=1, source_target_pairs={{0,2},{1,3},{2,0},{3,1},{4,6},{5,7},{6,4},{7,5},{8,10},{9,11},{10,... | collective-permute-start | bytes 589832 | tf_op jit(solution)/shard_map/ppermute | solution.py:32
  139.0 4.1 %collective-permute-done.45 = bf16[384,256]{1,0:T(8,128)(2,1)S(1)} collective-permute-done((bf16[384,256]{1,0:T(8,128)(2,1)S(1)}, bf16[384,256]{1,0:T(8,128)(2,1)S(1)}, u32[]{:S(2)}, u32[]{:S(2)}) %collective-permute-start.45) | collective-permute-done | bytes 196640 | tf_op jit(solution)/shard_map/ppermute | solution.py:32
  143.1 4.0 %collective-permute-start.46 = (bf16[384,256]{1,0:T(8,128)(2,1)S(1)}, bf16[384,256]{1,0:T(8,128)(2,1)S(1)}, u32[]{:S(2)}, u32[]{:S(2)}) collective-permute-start(bf16[384,256]{1,0:T(8,128)(2,1)S(1)} %fusion.1), channel_id=1, source_target_pairs={{0,4},{1,5},{2,6},{3,7},{4,0},{5,1},{6,2},{7,3},{8,12},{9,13},{10,... | collective-permute-start | bytes 589832 | tf_op jit(solution)/shard_map/ppermute | solution.py:32
  147.1 6.3 %collective-permute-done.46 = bf16[384,256]{1,0:T(8,128)(2,1)S(1)} collective-permute-done((bf16[384,256]{1,0:T(8,128)(2,1)S(1)}, bf16[384,256]{1,0:T(8,128)(2,1)S(1)}, u32[]{:S(2)}, u32[]{:S(2)}) %collective-permute-start.46) | collective-permute-done | bytes 196640 | tf_op jit(solution)/shard_map/ppermute | solution.py:32
  153.6 1.9 %collective-permute-start.34 = (bf16[256,256]{1,0:T(8,128)(2,1)S(1)}, bf16[256,256]{1,0:T(8,128)(2,1)S(1)}, u32[]{:S(2)}, u32[]{:S(2)}) collective-permute-start(bf16[256,256]{1,0:T(8,128)(2,1)S(1)} %add_convert_fusion.2.refs_0_), channel_id=1, source_target_pairs={{0,2},{1,3},{2,0},{3,1},{4,6},{5,7},{6,4},{7,5},{8,10},{9,11},{10,... | collective-permute-start | bytes 393224 | tf_op jit(solution)/shard_map/ppermute | solution.py:32
  156.3 4.1 %collective-permute-done.47.refs_9_ = bf16[384,256]{1,0:T(8,128)(2,1)S(1)} collective-permute-done((bf16[384,256]{1,0:T(8,128)(2,1)S(1)}, bf16[384,256]{1,0:T(8,128)(2,1)S(1)}, u32[]{:S(2)}, u32[]{:S(2)}) %collective-permute-start.47) | collective-permute-done | bytes 196640 | tf_op jit(solution)/shard_map/ppermute | solution.py:32
  160.4 1.4 collective-permute-done.34.refs_1_
  161.8 1.3 collective-permute-done.36.refs_3_
  163.2 2.8 %assemble.1 = (f32[4096,128]{1,0:T(8,128)}, f32[4096,128]{1,0:T(8,128)}) custom-call(s32[3]{0:T(128)S(1)} %pad_add_fusion.ids, bf16[256,256]{1,0:T(8,128)(2,1)S(1)} %add_convert_fusion.2.refs_0_, bf16[256,256]{1,0:T(8,128)(2,1)S(1)} %collective-permute-done.34.refs_1_, bf16[256,256]{1,0:T(8,128)(2,1)S(1)} %collective-permute-done.35.refs_2_, ...), custom_call_target="tpu_custom_call" | custom-call | tf_op jit(solution)/shard_map/assemble/pallas_call | solution.py:48
  (98 shorter events, 14.2 us)
Async XLA Ops:
  2.9 15.9 %collective-permute-start.4 = (bf16[1024,256]{1,0:T(8,128)(2,1)}, bf16[1024,256]{1,0:T(8,128)(2,1)S(1)}, u32[]{:S(2)}, u32[]{:S(2)}) collective-permute-start(bf16[1024,256]{1,0:T(8,128)(2,1)} %pad_maximum_fusion), channel_id=1, source_target_pairs={{0,16},{8,24},{16,0},{24,8},{1,17},{9,25},{17,1},{25,9},{2,18},{10... | collective-permute-start | bytes 1572872 | tf_op jit(solution)/shard_map/ppermute | solution.py:32
  5.9 15.1 %collective-permute-start = (bf16[1024,256]{1,0:T(8,128)(2,1)}, bf16[1024,256]{1,0:T(8,128)(2,1)S(1)}, u32[]{:S(2)}, u32[]{:S(2)}) collective-permute-start(bf16[1024,256]{1,0:T(8,128)(2,1)} %pad_maximum_fusion), channel_id=1, source_target_pairs={{0,8},{8,0},{16,24},{24,16},{1,9},{9,1},{17,25},{25,17},{2,10},{10... | collective-permute-start | bytes 1572872 | tf_op jit(solution)/shard_map/ppermute | solution.py:32
  8.2 22.0 %collective-permute-start.5 = (bf16[1024,256]{1,0:T(8,128)(2,1)}, bf16[1024,256]{1,0:T(8,128)(2,1)}, u32[]{:S(2)}, u32[]{:S(2)}) collective-permute-start(bf16[1024,256]{1,0:T(8,128)(2,1)} %pad_maximum_fusion.1), channel_id=1, source_target_pairs={{0,16},{8,24},{16,0},{24,8},{1,17},{9,25},{17,1},{25,9},{2,18},{10... | collective-permute-start | bytes 1572872 | tf_op jit(solution)/shard_map/ppermute | solution.py:32
  8.7 23.5 %collective-permute-start.1 = (bf16[1024,256]{1,0:T(8,128)(2,1)}, bf16[1024,256]{1,0:T(8,128)(2,1)}, u32[]{:S(2)}, u32[]{:S(2)}) collective-permute-start(bf16[1024,256]{1,0:T(8,128)(2,1)} %pad_maximum_fusion.1), channel_id=1, source_target_pairs={{0,8},{8,0},{16,24},{24,16},{1,9},{9,1},{17,25},{25,17},{2,10},{10... | collective-permute-start | bytes 1572872 | tf_op jit(solution)/shard_map/ppermute | solution.py:32
  18.9 13.4 %collective-permute-start.6 = (bf16[1024,256]{1,0:T(8,128)(2,1)S(1)}, bf16[1024,256]{1,0:T(8,128)(2,1)}, u32[]{:S(2)}, u32[]{:S(2)}) collective-permute-start(bf16[1024,256]{1,0:T(8,128)(2,1)S(1)} %collective-permute-done.4.refs_6_), channel_id=1, source_target_pairs={{0,1},{1,0},{2,3},{3,2},{4,5},{5,4},{6,7},{7,6},{8,9},{9,8},{10,11... | collective-permute-start | bytes 1572872 | tf_op jit(solution)/shard_map/ppermute | solution.py:32
  21.0 19.5 %collective-permute-start.8 = (bf16[1024,256]{1,0:T(8,128)(2,1)S(1)}, bf16[1024,256]{1,0:T(8,128)(2,1)S(1)}, u32[]{:S(2)}, u32[]{:S(2)}) collective-permute-start(bf16[1024,256]{1,0:T(8,128)(2,1)S(1)} %collective-permute-done.refs_2_), channel_id=1, source_target_pairs={{0,16},{8,24},{16,0},{24,8},{1,17},{9,25},{17,1},{25,9},{2,18},{10... | collective-permute-start | bytes 1572872 | tf_op jit(solution)/shard_map/ppermute | solution.py:32
  21.0 14.4 %collective-permute-start.2 = (bf16[1024,256]{1,0:T(8,128)(2,1)S(1)}, bf16[1024,256]{1,0:T(8,128)(2,1)S(1)}, u32[]{:S(2)}, u32[]{:S(2)}) collective-permute-start(bf16[1024,256]{1,0:T(8,128)(2,1)S(1)} %collective-permute-done.refs_2_), channel_id=1, source_target_pairs={{0,1},{1,0},{2,3},{3,2},{4,5},{5,4},{6,7},{7,6},{8,9},{9,8},{10,11... | collective-permute-start | bytes 1572872 | tf_op jit(solution)/shard_map/ppermute | solution.py:32
  30.2 12.5 %collective-permute-start.9 = (bf16[1024,256]{1,0:T(8,128)(2,1)}, bf16[1024,256]{1,0:T(8,128)(2,1)S(1)}, u32[]{:S(2)}, u32[]{:S(2)}) collective-permute-start(bf16[1024,256]{1,0:T(8,128)(2,1)} %collective-permute-done.5.refs_7_), channel_id=1, source_target_pairs={{0,8},{8,0},{16,24},{24,16},{1,9},{9,1},{17,25},{25,17},{2,10},{10... | collective-permute-start | bytes 1572872 | tf_op jit(solution)/shard_map/ppermute | solution.py:32
  32.2 3.1 %collective-permute-start.7 = (bf16[1024,256]{1,0:T(8,128)(2,1)}, bf16[1024,256]{1,0:T(8,128)(2,1)S(1)}, u32[]{:S(2)}, u32[]{:S(2)}) collective-permute-start(bf16[1024,256]{1,0:T(8,128)(2,1)} %collective-permute-done.5.refs_7_), channel_id=1, source_target_pairs={{0,1},{1,0},{2,3},{3,2},{4,5},{5,4},{6,7},{7,6},{8,9},{9,8},{10,11... | collective-permute-start | bytes 1572872 | tf_op jit(solution)/shard_map/ppermute | solution.py:32
  32.2 3.1 %collective-permute-start.3 = (bf16[1024,256]{1,0:T(8,128)(2,1)}, bf16[1024,256]{1,0:T(8,128)(2,1)S(1)}, u32[]{:S(2)}, u32[]{:S(2)}) collective-permute-start(bf16[1024,256]{1,0:T(8,128)(2,1)} %collective-permute-done.1.refs_3_), channel_id=1, source_target_pairs={{0,1},{1,0},{2,3},{3,2},{4,5},{5,4},{6,7},{7,6},{8,9},{9,8},{10,11... | collective-permute-start | bytes 1572872 | tf_op jit(solution)/shard_map/ppermute | solution.py:32
  42.7 21.8 %collective-permute-start.19 = (bf16[192,2560]{1,0:T(8,128)(2,1)S(1)}, bf16[192,2560]{1,0:T(8,128)(2,1)S(1)}, u32[]{:S(2)}, u32[]{:S(2)}) collective-permute-start(bf16[192,2560]{1,0:T(8,128)(2,1)S(1)} %get-tuple-element.60), channel_id=1, source_target_pairs={{0,8},{8,0},{16,24},{24,16},{1,9},{9,1},{17,25},{25,17},{2,10},{10... | collective-permute-start | bytes 2949128 | tf_op jit(solution)/shard_map/ppermute | solution.py:32
  44.3 20.3 %collective-permute-start.20 = (bf16[192,2560]{1,0:T(8,128)(2,1)S(1)}, bf16[192,2560]{1,0:T(8,128)(2,1)S(1)}, u32[]{:S(2)}, u32[]{:S(2)}) collective-permute-start(bf16[192,2560]{1,0:T(8,128)(2,1)S(1)} %get-tuple-element.61), channel_id=1, source_target_pairs={{0,16},{8,24},{16,0},{24,8},{1,17},{9,25},{17,1},{25,9},{2,18},{10... | collective-permute-start | bytes 2949128 | tf_op jit(solution)/shard_map/ppermute | solution.py:32
  45.8 1.9 %collective-permute-start.10 = (bf16[1024,256]{1,0:T(8,128)(2,1)S(1)}, bf16[1024,256]{1,0:T(8,128)(2,1)S(1)}, u32[]{:S(2)}, u32[]{:S(2)}) collective-permute-start(bf16[1024,256]{1,0:T(8,128)(2,1)S(1)} %collective-permute-done.8.refs_1_), channel_id=1, source_target_pairs={{0,1},{1,0},{2,3},{3,2},{4,5},{5,4},{6,7},{7,6},{8,9},{9,8},{10,11... | collective-permute-start | bytes 1572872 | tf_op jit(solution)/shard_map/ppermute | solution.py:32
  45.8 2.7 %collective-permute-start.11 = (bf16[1024,256]{1,0:T(8,128)(2,1)S(1)}, bf16[1024,256]{1,0:T(8,128)(2,1)S(1)}, u32[]{:S(2)}, u32[]{:S(2)}) collective-permute-start(bf16[1024,256]{1,0:T(8,128)(2,1)S(1)} %collective-permute-done.9.refs_2_), channel_id=1, source_target_pairs={{0,1},{1,0},{2,3},{3,2},{4,5},{5,4},{6,7},{7,6},{8,9},{9,8},{10,11... | collective-permute-start | bytes 1572872 | tf_op jit(solution)/shard_map/ppermute | solution.py:32
  49.6 7.6 %collective-permute-start.14 = (bf16[192,256]{1,0:T(8,128)(2,1)S(1)}, bf16[192,256]{1,0:T(8,128)(2,1)S(1)}, u32[]{:S(2)}, u32[]{:S(2)}) collective-permute-start(bf16[192,256]{1,0:T(8,128)(2,1)S(1)} %project.3.refs_0_), channel_id=1, source_target_pairs={{0,6},{1,7},{2,4},{3,5},{4,2},{5,3},{6,0},{7,1},{8,14},{9,15},{10,... | collective-permute-start | bytes 294920 | tf_op jit(solution)/shard_map/ppermute | solution.py:32
  53.3 8.6 %collective-permute-start.13 = (bf16[192,256]{1,0:T(8,128)(2,1)S(1)}, bf16[192,256]{1,0:T(8,128)(2,1)S(1)}, u32[]{:S(2)}, u32[]{:S(2)}) collective-permute-start(bf16[192,256]{1,0:T(8,128)(2,1)S(1)} %project.3.refs_0_), channel_id=1, source_target_pairs={{0,4},{1,5},{2,6},{3,7},{4,0},{5,1},{6,2},{7,3},{8,12},{9,13},{10,... | collective-permute-start | bytes 294920 | tf_op jit(solution)/shard_map/ppermute | solution.py:32
  53.3 8.6 %collective-permute-start.12 = (bf16[192,256]{1,0:T(8,128)(2,1)S(1)}, bf16[192,256]{1,0:T(8,128)(2,1)S(1)}, u32[]{:S(2)}, u32[]{:S(2)}) collective-permute-start(bf16[192,256]{1,0:T(8,128)(2,1)S(1)} %project.3.refs_0_), channel_id=1, source_target_pairs={{0,2},{1,3},{2,0},{3,1},{4,6},{5,7},{6,4},{7,5},{8,10},{9,11},{10,... | collective-permute-start | bytes 294920 | tf_op jit(solution)/shard_map/ppermute | solution.py:32
  61.9 1.3 collective-permute-start.15
  61.9 1.5 collective-permute-start.16
  64.7 41.4 %collective-permute-start.28 = (bf16[192,2560]{1,0:T(8,128)(2,1)S(1)}, bf16[192,2560]{1,0:T(8,128)(2,1)S(1)}, u32[]{:S(2)}, u32[]{:S(2)}) collective-permute-start(bf16[192,2560]{1,0:T(8,128)(2,1)S(1)} %get-tuple-element.80), channel_id=1, source_target_pairs={{0,24},{8,16},{16,8},{24,0},{1,25},{9,17},{17,9},{25,1},{2,26},{10... | collective-permute-start | bytes 2949128 | tf_op jit(solution)/shard_map/ppermute | solution.py:32
  76.2 1.7 %collective-permute-start.21 = (bf16[768,256]{1,0:T(8,128)(2,1)S(1)}, bf16[768,256]{1,0:T(8,128)(2,1)S(1)}, u32[]{:S(2)}, u32[]{:S(2)}) collective-permute-start(bf16[768,256]{1,0:T(8,128)(2,1)S(1)} %get-tuple-element.74), channel_id=1, source_target_pairs={{0,1},{1,0},{2,3},{3,2},{4,5},{5,4},{6,7},{7,6},{8,9},{9,8},{10,11... | collective-permute-start | bytes 1179656 | tf_op jit(solution)/shard_map/ppermute | solution.py:32
  78.0 14.7 %collective-permute-start.22 = (bf16[192,256]{1,0:T(8,128)(2,1)S(1)}, bf16[192,256]{1,0:T(8,128)(2,1)S(1)}, u32[]{:S(2)}, u32[]{:S(2)}) collective-permute-start(bf16[192,256]{1,0:T(8,128)(2,1)S(1)} %get-tuple-element.76), channel_id=1, source_target_pairs={{0,2},{1,3},{2,0},{3,1},{4,6},{5,7},{6,4},{7,5},{8,10},{9,11},{10,... | collective-permute-start | bytes 294920 | tf_op jit(solution)/shard_map/ppermute | solution.py:32
  79.7 14.8 %collective-permute-start.23 = (bf16[192,256]{1,0:T(8,128)(2,1)S(1)}, bf16[192,256]{1,0:T(8,128)(2,1)S(1)}, u32[]{:S(2)}, u32[]{:S(2)}) collective-permute-start(bf16[192,256]{1,0:T(8,128)(2,1)S(1)} %get-tuple-element.77), channel_id=1, source_target_pairs={{0,4},{1,5},{2,6},{3,7},{4,0},{5,1},{6,2},{7,3},{8,12},{9,13},{10,... | collective-permute-start | bytes 294920 | tf_op jit(solution)/shard_map/ppermute | solution.py:32
  91.3 8.5 %collective-permute-start.24 = (bf16[192,256]{1,0:T(8,128)(2,1)S(1)}, bf16[192,256]{1,0:T(8,128)(2,1)S(1)}, u32[]{:S(2)}, u32[]{:S(2)}) collective-permute-start(bf16[192,256]{1,0:T(8,128)(2,1)S(1)} %get-tuple-element.78), channel_id=1, source_target_pairs={{0,6},{1,7},{2,4},{3,5},{4,2},{5,3},{6,0},{7,1},{8,14},{9,15},{10,... | collective-permute-start | bytes 294920 | tf_op jit(solution)/shard_map/ppermute | solution.py:32
  99.8 6.1 %collective-permute-start.27 = (bf16[192,256]{1,0:T(8,128)(2,1)S(1)}, bf16[192,256]{1,0:T(8,128)(2,1)S(1)}, u32[]{:S(2)}, u32[]{:S(2)}) collective-permute-start(bf16[192,256]{1,0:T(8,128)(2,1)S(1)} %total.1.refs_4_.refs_1_), channel_id=1, source_target_pairs={{0,24},{8,16},{16,8},{24,0},{1,25},{9,17},{17,9},{25,1},{2,26},{10... | collective-permute-start | bytes 294920 | tf_op jit(solution)/shard_map/ppermute | solution.py:32
  99.9 6.1 %collective-permute-start.26 = (bf16[192,256]{1,0:T(8,128)(2,1)S(1)}, bf16[192,256]{1,0:T(8,128)(2,1)S(1)}, u32[]{:S(2)}, u32[]{:S(2)}) collective-permute-start(bf16[192,256]{1,0:T(8,128)(2,1)S(1)} %total.1.refs_4_.refs_1_), channel_id=1, source_target_pairs={{0,16},{8,24},{16,0},{24,8},{1,17},{9,25},{17,1},{25,9},{2,18},{10... | collective-permute-start | bytes 294920 | tf_op jit(solution)/shard_map/ppermute | solution.py:32
  100.0 6.0 %collective-permute-start.25 = (bf16[192,256]{1,0:T(8,128)(2,1)S(1)}, bf16[192,256]{1,0:T(8,128)(2,1)S(1)}, u32[]{:S(2)}, u32[]{:S(2)}) collective-permute-start(bf16[192,256]{1,0:T(8,128)(2,1)S(1)} %total.1.refs_4_.refs_1_), channel_id=1, source_target_pairs={{0,8},{8,0},{16,24},{24,16},{1,9},{9,1},{17,25},{25,17},{2,10},{10... | collective-permute-start | bytes 294920 | tf_op jit(solution)/shard_map/ppermute | solution.py:32
  107.7 5.4 %collective-permute-start.31 = (bf16[3072,256]{1,0:T(8,128)(2,1)S(1)}, bf16[3072,256]{1,0:T(8,128)(2,1)S(1)}, u32[]{:S(2)}, u32[]{:S(2)}) collective-permute-start(bf16[3072,256]{1,0:T(8,128)(2,1)S(1)} %get-tuple-element.91), channel_id=1, source_target_pairs={{0,1},{1,0},{2,3},{3,2},{4,5},{5,4},{6,7},{7,6},{8,9},{9,8},{10,11... | collective-permute-start | bytes 4718600 | tf_op jit(solution)/shard_map/ppermute | solution.py:32
  109.1 2.4 %collective-permute-start.29 = (bf16[512,256]{1,0:T(8,128)(2,1)S(1)}, bf16[512,256]{1,0:T(8,128)(2,1)S(1)}, u32[]{:S(2)}, u32[]{:S(2)}) collective-permute-start(bf16[512,256]{1,0:T(8,128)(2,1)S(1)} %get-tuple-element.86), channel_id=1, source_target_pairs={{0,1},{1,0},{2,3},{3,2},{4,5},{5,4},{6,7},{7,6},{8,9},{9,8},{10,11... | collective-permute-start | bytes 786440 | tf_op jit(solution)/shard_map/ppermute | solution.py:32
  111.3 1.8 %collective-permute-start.30 = (bf16[768,256]{1,0:T(8,128)(2,1)S(1)}, bf16[768,256]{1,0:T(8,128)(2,1)S(1)}, u32[]{:S(2)}, u32[]{:S(2)}) collective-permute-start(bf16[768,256]{1,0:T(8,128)(2,1)S(1)} %get-tuple-element.88), channel_id=1, source_target_pairs={{0,1},{1,0},{2,3},{3,2},{4,5},{5,4},{6,7},{7,6},{8,9},{9,8},{10,11... | collective-permute-start | bytes 1179656 | tf_op jit(solution)/shard_map/ppermute | solution.py:32
  113.9 6.7 %collective-permute-start.32 = (bf16[256,256]{1,0:T(8,128)(2,1)S(1)}, bf16[256,256]{1,0:T(8,128)(2,1)S(1)}, u32[]{:S(2)}, u32[]{:S(2)}) collective-permute-start(bf16[256,256]{1,0:T(8,128)(2,1)S(1)} %slice.74), channel_id=1, source_target_pairs={{0,2},{1,3},{2,0},{3,1},{4,6},{5,7},{6,4},{7,5},{8,10},{9,11},{10,... | collective-permute-start | bytes 393224 | tf_op jit(solution)/shard_map/ppermute | solution.py:32
  116.3 9.4 %collective-permute-start.37 = (bf16[384,256]{1,0:T(8,128)(2,1)S(1)}, bf16[384,256]{1,0:T(8,128)(2,1)S(1)}, u32[]{:S(2)}, u32[]{:S(2)}) collective-permute-start(bf16[384,256]{1,0:T(8,128)(2,1)S(1)} %slice.73), channel_id=1, source_target_pairs={{0,2},{1,3},{2,0},{3,1},{4,6},{5,7},{6,4},{7,5},{8,10},{9,11},{10,... | collective-permute-start | bytes 589832 | tf_op jit(solution)/shard_map/ppermute | solution.py:32
  116.4 18.4 %collective-permute-start.42 = (bf16[768,256]{1,0:T(8,128)(2,1)S(1)}, bf16[768,256]{1,0:T(8,128)(2,1)S(1)}, u32[]{:S(2)}, u32[]{:S(2)}) collective-permute-start(bf16[768,256]{1,0:T(8,128)(2,1)S(1)} %get-tuple-element.95), channel_id=1, source_target_pairs={{0,8},{8,0},{16,24},{24,16},{1,9},{9,1},{17,25},{25,17},{2,10},{10... | collective-permute-start | bytes 1179656 | tf_op jit(solution)/shard_map/ppermute | solution.py:32
  118.0 18.9 %collective-permute-start.43 = (bf16[768,256]{1,0:T(8,128)(2,1)S(1)}, bf16[768,256]{1,0:T(8,128)(2,1)S(1)}, u32[]{:S(2)}, u32[]{:S(2)}) collective-permute-start(bf16[768,256]{1,0:T(8,128)(2,1)S(1)} %get-tuple-element.96), channel_id=1, source_target_pairs={{0,16},{8,24},{16,0},{24,8},{1,17},{9,25},{17,1},{25,9},{2,18},{10... | collective-permute-start | bytes 1179656 | tf_op jit(solution)/shard_map/ppermute | solution.py:32
  118.2 18.8 %collective-permute-start.44 = (bf16[768,256]{1,0:T(8,128)(2,1)S(1)}, bf16[768,256]{1,0:T(8,128)(2,1)S(1)}, u32[]{:S(2)}, u32[]{:S(2)}) collective-permute-start(bf16[768,256]{1,0:T(8,128)(2,1)S(1)} %get-tuple-element.97), channel_id=1, source_target_pairs={{0,24},{8,16},{16,8},{24,0},{1,25},{9,17},{17,9},{25,1},{2,26},{10... | collective-permute-start | bytes 1179656 | tf_op jit(solution)/shard_map/ppermute | solution.py:32
  120.6 14.1 %collective-permute-start.33 = (bf16[256,256]{1,0:T(8,128)(2,1)S(1)}, bf16[256,256]{1,0:T(8,128)(2,1)S(1)}, u32[]{:S(2)}, u32[]{:S(2)}) collective-permute-start(bf16[256,256]{1,0:T(8,128)(2,1)S(1)} %fusion.2), channel_id=1, source_target_pairs={{0,4},{1,5},{2,6},{3,7},{4,0},{5,1},{6,2},{7,3},{8,12},{9,13},{10,... | collective-permute-start | bytes 393224 | tf_op jit(solution)/shard_map/ppermute | solution.py:32
  125.8 13.1 %collective-permute-start.38 = (bf16[384,256]{1,0:T(8,128)(2,1)S(1)}, bf16[384,256]{1,0:T(8,128)(2,1)S(1)}, u32[]{:S(2)}, u32[]{:S(2)}) collective-permute-start(bf16[384,256]{1,0:T(8,128)(2,1)S(1)} %fusion), channel_id=1, source_target_pairs={{0,4},{1,5},{2,6},{3,7},{4,0},{5,1},{6,2},{7,3},{8,12},{9,13},{10,... | collective-permute-start | bytes 589832 | tf_op jit(solution)/shard_map/ppermute | solution.py:32
  137.1 6.0 %collective-permute-start.45 = (bf16[384,256]{1,0:T(8,128)(2,1)S(1)}, bf16[384,256]{1,0:T(8,128)(2,1)S(1)}, u32[]{:S(2)}, u32[]{:S(2)}) collective-permute-start(bf16[384,256]{1,0:T(8,128)(2,1)S(1)} %slice.72), channel_id=1, source_target_pairs={{0,2},{1,3},{2,0},{3,1},{4,6},{5,7},{6,4},{7,5},{8,10},{9,11},{10,... | collective-permute-start | bytes 589832 | tf_op jit(solution)/shard_map/ppermute | solution.py:32
  143.1 10.2 %collective-permute-start.46 = (bf16[384,256]{1,0:T(8,128)(2,1)S(1)}, bf16[384,256]{1,0:T(8,128)(2,1)S(1)}, u32[]{:S(2)}, u32[]{:S(2)}) collective-permute-start(bf16[384,256]{1,0:T(8,128)(2,1)S(1)} %fusion.1), channel_id=1, source_target_pairs={{0,4},{1,5},{2,6},{3,7},{4,0},{5,1},{6,2},{7,3},{8,12},{9,13},{10,... | collective-permute-start | bytes 589832 | tf_op jit(solution)/shard_map/ppermute | solution.py:32
  147.1 8.7 %collective-permute-start.39 = (bf16[384,256]{1,0:T(8,128)(2,1)S(1)}, bf16[384,256]{1,0:T(8,128)(2,1)S(1)}, u32[]{:S(2)}, u32[]{:S(2)}) collective-permute-start(bf16[384,256]{1,0:T(8,128)(2,1)S(1)} %add_convert_fusion.1.refs_4_), channel_id=1, source_target_pairs={{0,2},{1,3},{2,0},{3,1},{4,6},{5,7},{6,4},{7,5},{8,10},{9,11},{10,... | collective-permute-start | bytes 589832 | tf_op jit(solution)/shard_map/ppermute | solution.py:32
  153.4 7.0 %collective-permute-start.47 = (bf16[384,256]{1,0:T(8,128)(2,1)S(1)}, bf16[384,256]{1,0:T(8,128)(2,1)S(1)}, u32[]{:S(2)}, u32[]{:S(2)}) collective-permute-start(bf16[384,256]{1,0:T(8,128)(2,1)S(1)} %add_convert_fusion.refs_8_), channel_id=1, source_target_pairs={{0,2},{1,3},{2,0},{3,1},{4,6},{5,7},{6,4},{7,5},{8,10},{9,11},{10,... | collective-permute-start | bytes 589832 | tf_op jit(solution)/shard_map/ppermute | solution.py:32
  153.5 2.5 %collective-permute-start.35 = (bf16[256,256]{1,0:T(8,128)(2,1)S(1)}, bf16[256,256]{1,0:T(8,128)(2,1)S(1)}, u32[]{:S(2)}, u32[]{:S(2)}) collective-permute-start(bf16[256,256]{1,0:T(8,128)(2,1)S(1)} %add_convert_fusion.2.refs_0_), channel_id=1, source_target_pairs={{0,1},{1,0},{2,3},{3,2},{4,5},{5,4},{6,7},{7,6},{8,9},{9,8},{10,11... | collective-permute-start | bytes 393224 | tf_op jit(solution)/shard_map/ppermute | solution.py:32
  153.6 8.2 %collective-permute-start.34 = (bf16[256,256]{1,0:T(8,128)(2,1)S(1)}, bf16[256,256]{1,0:T(8,128)(2,1)S(1)}, u32[]{:S(2)}, u32[]{:S(2)}) collective-permute-start(bf16[256,256]{1,0:T(8,128)(2,1)S(1)} %add_convert_fusion.2.refs_0_), channel_id=1, source_target_pairs={{0,2},{1,3},{2,0},{3,1},{4,6},{5,7},{6,4},{7,5},{8,10},{9,11},{10,... | collective-permute-start | bytes 393224 | tf_op jit(solution)/shard_map/ppermute | solution.py:32
  155.5 7.6 %collective-permute-start.40 = (bf16[384,256]{1,0:T(8,128)(2,1)S(1)}, bf16[384,256]{1,0:T(8,128)(2,1)S(1)}, u32[]{:S(2)}, u32[]{:S(2)}) collective-permute-start(bf16[384,256]{1,0:T(8,128)(2,1)S(1)} %add_convert_fusion.1.refs_4_), channel_id=1, source_target_pairs={{0,1},{1,0},{2,3},{3,2},{4,5},{5,4},{6,7},{7,6},{8,9},{9,8},{10,11... | collective-permute-start | bytes 589832 | tf_op jit(solution)/shard_map/ppermute | solution.py:32
  155.8 7.4 %collective-permute-start.41 = (bf16[384,256]{1,0:T(8,128)(2,1)S(1)}, bf16[384,256]{1,0:T(8,128)(2,1)S(1)}, u32[]{:S(2)}, u32[]{:S(2)}) collective-permute-start(bf16[384,256]{1,0:T(8,128)(2,1)S(1)} %collective-permute-done.39.refs_5_), channel_id=1, source_target_pairs={{0,1},{1,0},{2,3},{3,2},{4,5},{5,4},{6,7},{7,6},{8,9},{9,8},{10,11... | collective-permute-start | bytes 589832 | tf_op jit(solution)/shard_map/ppermute | solution.py:32
  156.0 7.1 %collective-permute-start.48 = (bf16[384,256]{1,0:T(8,128)(2,1)S(1)}, bf16[384,256]{1,0:T(8,128)(2,1)S(1)}, u32[]{:S(2)}, u32[]{:S(2)}) collective-permute-start(bf16[384,256]{1,0:T(8,128)(2,1)S(1)} %add_convert_fusion.refs_8_), channel_id=1, source_target_pairs={{0,1},{1,0},{2,3},{3,2},{4,5},{5,4},{6,7},{7,6},{8,9},{9,8},{10,11... | collective-permute-start | bytes 589832 | tf_op jit(solution)/shard_map/ppermute | solution.py:32
  160.4 2.8 %collective-permute-start.49 = (bf16[384,256]{1,0:T(8,128)(2,1)S(1)}, bf16[384,256]{1,0:T(8,128)(2,1)S(1)}, u32[]{:S(2)}, u32[]{:S(2)}) collective-permute-start(bf16[384,256]{1,0:T(8,128)(2,1)S(1)} %collective-permute-done.47.refs_9_), channel_id=1, source_target_pairs={{0,1},{1,0},{2,3},{3,2},{4,5},{5,4},{6,7},{7,6},{8,9},{9,8},{10,11... | collective-permute-start | bytes 589832 | tf_op jit(solution)/shard_map/ppermute | solution.py:32
  161.8 1.3 collective-permute-start.36
  (10 other events, 143.9 us)

commit v8 on v7

--- a/solution.py
+++ b/solution.py
@@ -117,9 +117,10 @@
         q = qs[part, :]
         g = gs[part, :]
         last = (((1,), (1,)), ((), ()))
-        scores = lax.dot_general(k, q, last, preferred_element_type=jnp.float32) * score_scale
+        scores = lax.dot_general(k, q, last, preferred_element_type=jnp.float32)
         masked = jnp.where(allowed, scores, -jnp.inf)
-        expsum = jnp.exp(masked - jnp.max(masked, axis=0, keepdims=True))
+        largest = jnp.max(masked, axis=0, keepdims=True)
+        expsum = jnp.exp2((masked - largest) * (score_scale * math.log2(math.e)))
         probs = expsum * (1.0 / jnp.sum(expsum, axis=0, keepdims=True))
         probs_low = probs.astype(jnp.bfloat16)
         dprob = lax.dot_general(v, g, last, preferred_element_type=jnp.float32)
@@ -135,7 +136,7 @@
         total[pl.ds(first, window), head_dim:] += dv
         return carry
 
-    lax.fori_loop(0, 2 * chunks_half, step, 0)
+    lax.fori_loop(0, 2 * chunks_half, step, 0, unroll=2)
     for half in range(2):
         for head in range(head_count):
             origin = slice((half * head_count + head) * stretch_rows, (half * head_count + head + 1) * stretch_rows)
@@ -445,24 +446,25 @@
     moved = {0: moving[0]}
     moved.update({j: swap(moving[j], "dp", j) for j in near})
     along = gather_along_z(own)
-    along, tied = after(along, *[moving[j] for j in far])
+    tied, _ = after([moving[j] for j in far], *along)
     moving.update(zip(far, tied))
+    along, _ = after(along)
     kv_blocks = both_cores(along)
 
-    kv_blocks, ended = after(kv_blocks, *[moved[j] for j in near])
-    moved.update(zip(near, ended))
-    tied, _ = after([moving[j] for j in far], *ended)
-    moved.update({j: swap(one, "dp", j) for j, one in zip(far, tied)})
+    moved.update({j: swap(moving[j], "dp", j) for j in far})
+
     query_grad, keep, send = attention(
         me, stretch_order, doc_lengths[0], queries[0], grad_out[0], kv_blocks, head_dim
     )
+    (send,), ended = after([send], moved[near[0]])
+    moved.update(zip(near, ended))
     own, *leaving = add_and_split(keep, swap(send, "ctx", 1), z_count)
     grad = add_all([own] + [swap(one, "ctx", 2 * m) for m, one in enumerate(leaving, 1)])
     grads = [grad] + [swap(grad, "dp", j) for j in range(1, dp_count)]
 
-    (grad,), ended = after([grad], *grads[1:], *[moved[j] for j in far])
+    (grad,), ended = after([grad], *grads[1:], *[moved[j] for j in others])
     grads[1:] = ended[: dp_count - 1]
-    moved.update(zip(far, ended[dp_count - 1 :]))
+    moved.update(zip(others, ended[dp_count - 1 :]))
     groups = [[(0, j, 0)] for j in range(dp_count)]
     own = weight_rows(ids, [inputs], [grad], groups, *regions[-1], block_rows, sub_count)
     own = parts_over_dp(own)

time: 166 us -> 158 us (0.952)
  starting transfers between devices: 59.1 us -> 46 us
  waiting for transfers between devices: 76 us -> 81.5 us
    ppermute x50, starting transfers between devices: 59.1 us -> 46 us  [swap(): return lax.ppermute(array, axis, [(i, i ^ distance) for i in range(count)])]
    ppermute x50, waiting for transfers between devices: 76 us -> 81.5 us  [swap(): return lax.ppermute(array, axis, [(i, i ^ distance) for i in range(count)])]
  transfers between devices with their start and end apart: 50 -> 50, of which waited for: 29 -> 27; matrix products, arithmetic and copies ran while one was open for 2% -> 3% of each run, Pallas kernels for 10% -> 10%
where the time goes in v8:
time: 158 us
  waiting for transfers between devices  81.5 us (52%)
  starting transfers between devices  46 us (29%)
  Pallas kernels  20.8 us (13%)
  local copies, waits for them, and re-layouts  5.55 us (4%)
  other arithmetic  2.89 us (2%)
    ppermute x50, waiting for transfers between devices, swap(): return lax.ppermute(array, axis, [(i, i ^ distance) for i in range(count)])  81.5 us
    ppermute x50, starting transfers between devices, swap(): return lax.ppermute(array, axis, [(i, i ^ distance) for i in range(count)])  46 us
    pallas_call x8, Pallas kernels, kernel_call(): pl.pallas_call(kernel, out_shape=outs, in_specs=[smem] * len(scalars) + [...  11.9 us
    pallas_call x1, Pallas kernels, attention(): pl.pallas_call(functools.partial(attention_kernel, shape), out_shape=(jax...  8.88 us
  transfers between devices with their start and end apart: 50, of which 27 were waited for; matrix products, arithmetic and copies ran while one was open for 3% of the time, Pallas kernels for 10%

profile of v8, /device:TPU:0, one launch (start us, length us, event | category | flops | bytes accessed | tf_op | source)
XLA Modules:
  0.0 157.7 jit_solution(16627963523318054397)
XLA Ops:
  0.7 1.4 constant_dynamic-slice_fusion
  2.9 3.0 %collective-permute-start.4 = (bf16[1024,256]{1,0:T(8,128)(2,1)}, bf16[1024,256]{1,0:T(8,128)(2,1)S(1)}, u32[]{:S(2)}, u32[]{:S(2)}) collective-permute-start(bf16[1024,256]{1,0:T(8,128)(2,1)} %pad_maximum_fusion), channel_id=1, source_target_pairs={{0,16},{8,24},{16,0},{24,8},{1,17},{9,25},{17,1},{25,9},{2,18},{10... | collective-permute-start | bytes 1572872 | tf_op jit(solution)/shard_map/ppermute | solution.py:32
  5.9 1.5 collective-permute-start
  8.8 10.1 %collective-permute-done.4.refs_6_ = bf16[1024,256]{1,0:T(8,128)(2,1)S(1)} collective-permute-done((bf16[1024,256]{1,0:T(8,128)(2,1)}, bf16[1024,256]{1,0:T(8,128)(2,1)S(1)}, u32[]{:S(2)}, u32[]{:S(2)}) %collective-permute-start.4) | collective-permute-done | bytes 524320 | tf_op jit(solution)/shard_map/ppermute | solution.py:32
  18.9 2.1 %collective-permute-done.refs_2_ = bf16[1024,256]{1,0:T(8,128)(2,1)S(1)} collective-permute-done((bf16[1024,256]{1,0:T(8,128)(2,1)}, bf16[1024,256]{1,0:T(8,128)(2,1)S(1)}, u32[]{:S(2)}, u32[]{:S(2)}) %collective-permute-start) | collective-permute-done | bytes 524320 | tf_op jit(solution)/shard_map/ppermute | solution.py:32
  21.2 9.0 %collective-permute-done.5.refs_7_ = bf16[1024,256]{1,0:T(8,128)(2,1)} collective-permute-done((bf16[1024,256]{1,0:T(8,128)(2,1)}, bf16[1024,256]{1,0:T(8,128)(2,1)}, u32[]{:S(2)}, u32[]{:S(2)}) %collective-permute-start.5) | collective-permute-done | bytes 524320 | tf_op jit(solution)/shard_map/ppermute | solution.py:32
  30.2 2.0 %collective-permute-start.9 = (bf16[1024,256]{1,0:T(8,128)(2,1)}, bf16[1024,256]{1,0:T(8,128)(2,1)S(1)}, u32[]{:S(2)}, u32[]{:S(2)}) collective-permute-start(bf16[1024,256]{1,0:T(8,128)(2,1)} %collective-permute-done.5.refs_7_), channel_id=1, source_target_pairs={{0,8},{8,0},{16,24},{24,16},{1,9},{9,1},{17,25},{25,17},{2,10},{10... | collective-permute-start | bytes 1572872 | tf_op jit(solution)/shard_map/ppermute | solution.py:32
  32.8 2.5 %dynamic-slice_bitcast_fusion = (bf16[192,2560]{1,0:T(8,128)(2,1)S(1)}, bf16[192,2560]{1,0:T(8,128)(2,1)S(1)}, bf16[192,2560]{1,0:T(8,128)(2,1)S(1)}, bf16[192,2560]{1,0:T(8,128)(2,1)S(1)}) fusion(bf16[1,192,16384]{2,1,0:T(8,128)(2,1)} %param.7, s32[]{:T(128)S(6)} %select_n.42, s32[]{:T(128)S(6)} %select_n.40, s32[]{:T(128)S(6)} %select_n.39, s32[]{:T(128)S(6)} %select_n.41), kind=kLoop, calls=%fused_computation.1 | loop fusion | bytes 7864336 | tf_op jit(solution)/shard_map/dynamic_slice | solution.py:431
  36.8 3.2 %project.2.refs_0_ = f32[192,256]{1,0:T(8,128)S(1)} custom-call(s32[3]{0:T(128)S(1)} %pad_add_fusion.ids, bf16[192,16384]{1,0:T(8,128)(2,1)S(1)} %bitcast.19, bf16[4096,128]{1,0:T(8,128)(2,1)S(1)} %copy-done, bf16[4096,128]{1,0:T(8,128)(2,1)S(1)} %copy-done.1, bf16[1024,256]{1,0:T(8,128)(2,1)S(1)} %collective-permute-done.refs_2_, ...), custom_call_target="tpu_custom_call" | custom-call | bytes 16777216 | tf_op jit(solution)/shard_map/project/pallas_call | solution.py:48
  40.5 2.2 %collective-permute-done.9.refs_2_ = bf16[1024,256]{1,0:T(8,128)(2,1)S(1)} collective-permute-done((bf16[1024,256]{1,0:T(8,128)(2,1)}, bf16[1024,256]{1,0:T(8,128)(2,1)S(1)}, u32[]{:S(2)}, u32[]{:S(2)}) %collective-permute-start.9) | collective-permute-done | bytes 524320 | tf_op jit(solution)/shard_map/ppermute | solution.py:32
  43.3 1.4 collective-permute-start.19
  45.4 1.1 project.3.refs_0_
  46.6 3.6 %collective-permute-start.14 = (bf16[192,256]{1,0:T(8,128)(2,1)S(1)}, bf16[192,256]{1,0:T(8,128)(2,1)S(1)}, u32[]{:S(2)}, u32[]{:S(2)}) collective-permute-start(bf16[192,256]{1,0:T(8,128)(2,1)S(1)} %project.3.refs_0_), channel_id=1, source_target_pairs={{0,6},{1,7},{2,4},{3,5},{4,2},{5,3},{6,0},{7,1},{8,14},{9,15},{10,... | collective-permute-start | bytes 294920 | tf_op jit(solution)/shard_map/ppermute | solution.py:32
  51.0 1.4 collective-permute-start.27
  52.5 1.7 %collective-permute-done.14.refs_6_ = bf16[192,256]{1,0:T(8,128)(2,1)S(1)} collective-permute-done((bf16[192,256]{1,0:T(8,128)(2,1)S(1)}, bf16[192,256]{1,0:T(8,128)(2,1)S(1)}, u32[]{:S(2)}, u32[]{:S(2)}) %collective-permute-start.14) | collective-permute-done | bytes 98336 | tf_op jit(solution)/shard_map/ppermute | solution.py:32
  54.2 4.5 %collective-permute-done.13.refs_4_ = bf16[192,256]{1,0:T(8,128)(2,1)S(1)} collective-permute-done((bf16[192,256]{1,0:T(8,128)(2,1)S(1)}, bf16[192,256]{1,0:T(8,128)(2,1)S(1)}, u32[]{:S(2)}, u32[]{:S(2)}) %collective-permute-start.13) | collective-permute-done | bytes 98336 | tf_op jit(solution)/shard_map/ppermute | solution.py:32
  58.7 2.4 %collective-permute-start.28 = (bf16[192,2560]{1,0:T(8,128)(2,1)S(1)}, bf16[192,2560]{1,0:T(8,128)(2,1)S(1)}, u32[]{:S(2)}, u32[]{:S(2)}) collective-permute-start(bf16[192,2560]{1,0:T(8,128)(2,1)S(1)} %get-tuple-element.64), channel_id=1, source_target_pairs={{0,24},{8,16},{16,8},{24,0},{1,25},{9,17},{17,9},{25,1},{2,26},{10... | collective-permute-start | bytes 2949128 | tf_op jit(solution)/shard_map/ppermute | solution.py:32
  63.9 8.9 %attention.1 = (bf16[192,1024]{1,0:T(8,128)(2,1)}, f32[768,256]{1,0:T(8,128)S(1)}, bf16[768,256]{1,0:T(8,128)(2,1)S(1)}) custom-call(s32[1]{0:T(128)} %bitcast.ids, s32[16]{0:T(128)S(1)} %copy-done.4, s32[8]{0:T(128)S(1)} %bitcast.24, bf16[192,1024]{1,0:T(8,128)(2,1)S(1)} %bitcast.22, bf16[192,1024]{1,0:T(8,128)(2,1)S(1)} %bitcast.23, ...), custom_call_target="tpu_custom_call" | custom-call | tf_op jit(solution)/shard_map/attention/pallas_call | solution.py:169
  73.2 1.4 collective-permute-done.20.came
  75.2 2.5 %collective-permute-start.22 = (bf16[192,256]{1,0:T(8,128)(2,1)S(1)}, bf16[192,256]{1,0:T(8,128)(2,1)S(1)}, u32[]{:S(2)}, u32[]{:S(2)}) collective-permute-start(bf16[192,256]{1,0:T(8,128)(2,1)S(1)} %get-tuple-element.59), channel_id=1, source_target_pairs={{0,4},{1,5},{2,6},{3,7},{4,0},{5,1},{6,2},{7,3},{8,12},{9,13},{10,... | collective-permute-start | bytes 294920 | tf_op jit(solution)/shard_map/ppermute | solution.py:32
  77.8 1.3 collective-permute-start.23
  79.1 2.2 %collective-permute-done.21.refs_1_ = bf16[192,256]{1,0:T(8,128)(2,1)S(1)} collective-permute-done((bf16[192,256]{1,0:T(8,128)(2,1)S(1)}, bf16[192,256]{1,0:T(8,128)(2,1)S(1)}, u32[]{:S(2)}, u32[]{:S(2)}) %collective-permute-start.21) | collective-permute-done | bytes 98336 | tf_op jit(solution)/shard_map/ppermute | solution.py:32
  81.3 4.8 %collective-permute-done.22.refs_2_ = bf16[192,256]{1,0:T(8,128)(2,1)S(1)} collective-permute-done((bf16[192,256]{1,0:T(8,128)(2,1)S(1)}, bf16[192,256]{1,0:T(8,128)(2,1)S(1)}, u32[]{:S(2)}, u32[]{:S(2)}) %collective-permute-start.22) | collective-permute-done | bytes 98336 | tf_op jit(solution)/shard_map/ppermute | solution.py:32
  86.7 1.5 collective-permute-start.25
  88.2 1.5 collective-permute-start.24
  89.7 8.6 %collective-permute-done.27.refs_2_ = bf16[192,2560]{1,0:T(8,128)(2,1)S(1)} collective-permute-done((bf16[192,2560]{1,0:T(8,128)(2,1)S(1)}, bf16[192,2560]{1,0:T(8,128)(2,1)S(1)}, u32[]{:S(2)}, u32[]{:S(2)}) %collective-permute-start.27) | collective-permute-done | bytes 983072 | tf_op jit(solution)/shard_map/ppermute | solution.py:32
  99.3 1.7 %weight_rows.5 = (bf16[3072,256]{1,0:T(8,128)(2,1)S(1)}, bf16[3072,256]{1,0:T(8,128)(2,1)S(1)}) custom-call(s32[3]{0:T(128)S(1)} %pad_add_fusion.ids, bf16[192,16384]{1,0:T(8,128)(2,1)S(1)} %bitcast.21, bf16[192,256]{1,0:T(8,128)(2,1)S(1)} %total.1.refs_4_.refs_1_), custom_call_target="tpu_custom_call" | custom-call | tf_op jit(solution)/shard_map/weight_rows/pallas_call | solution.py:48
  101.1 1.3 weight_rows.3
  102.9 1.6 %weight_rows.4 = (bf16[768,256]{1,0:T(8,128)(2,1)S(1)}, bf16[768,256]{1,0:T(8,128)(2,1)S(1)}) custom-call(s32[3]{0:T(128)S(1)} %pad_add_fusion.ids, bf16[192,2560]{1,0:T(8,128)(2,1)S(1)} %get-tuple-element.87.refs_0_, bf16[192,2560]{1,0:T(8,128)(2,1)S(1)} %collective-permute-done.19.refs_1_, bf16[192,2560]{1,0:T(8,128)(2,1)S(1)} %collective-permute-done.27.refs_2_, ...), custom_call_target="tpu_custom_call" | custom-call | tf_op jit(solution)/shard_map/weight_rows/pallas_call | solution.py:48
  104.9 1.4 collective-permute-done.30
  107.1 1.5 collective-permute-start.32
  109.3 1.5 collective-permute-start.42
  110.8 1.5 collective-permute-start.43
  113.6 2.4 %collective-permute-start.33 = (bf16[256,256]{1,0:T(8,128)(2,1)S(1)}, bf16[256,256]{1,0:T(8,128)(2,1)S(1)}, u32[]{:S(2)}, u32[]{:S(2)}) collective-permute-start(bf16[256,256]{1,0:T(8,128)(2,1)S(1)} %fusion.2), channel_id=1, source_target_pairs={{0,4},{1,5},{2,6},{3,7},{4,0},{5,1},{6,2},{7,3},{8,12},{9,13},{10,... | collective-permute-start | bytes 393224 | tf_op jit(solution)/shard_map/ppermute | solution.py:32
  115.9 2.7 %collective-permute-done.37 = bf16[384,256]{1,0:T(8,128)(2,1)S(1)} collective-permute-done((bf16[384,256]{1,0:T(8,128)(2,1)S(1)}, bf16[384,256]{1,0:T(8,128)(2,1)S(1)}, u32[]{:S(2)}, u32[]{:S(2)}) %collective-permute-start.37) | collective-permute-done | bytes 196640 | tf_op jit(solution)/shard_map/ppermute | solution.py:32
  118.6 1.5 collective-permute-start.38
  120.1 6.8 %collective-permute-done.33 = bf16[256,256]{1,0:T(8,128)(2,1)S(1)} collective-permute-done((bf16[256,256]{1,0:T(8,128)(2,1)S(1)}, bf16[256,256]{1,0:T(8,128)(2,1)S(1)}, u32[]{:S(2)}, u32[]{:S(2)}) %collective-permute-start.33) | collective-permute-done | bytes 131104 | tf_op jit(solution)/shard_map/ppermute | solution.py:32
  127.0 2.5 %collective-permute-done.43 = bf16[768,256]{1,0:T(8,128)(2,1)S(1)} collective-permute-done((bf16[768,256]{1,0:T(8,128)(2,1)S(1)}, bf16[768,256]{1,0:T(8,128)(2,1)S(1)}, u32[]{:S(2)}, u32[]{:S(2)}) %collective-permute-start.43) | collective-permute-done | bytes 393248 | tf_op jit(solution)/shard_map/ppermute | solution.py:32
  129.7 1.4 collective-permute-start.45
  131.3 4.2 %collective-permute-done.45 = bf16[384,256]{1,0:T(8,128)(2,1)S(1)} collective-permute-done((bf16[384,256]{1,0:T(8,128)(2,1)S(1)}, bf16[384,256]{1,0:T(8,128)(2,1)S(1)}, u32[]{:S(2)}, u32[]{:S(2)}) %collective-permute-start.45) | collective-permute-done | bytes 196640 | tf_op jit(solution)/shard_map/ppermute | solution.py:32
  135.5 2.4 %collective-permute-start.46 = (bf16[384,256]{1,0:T(8,128)(2,1)S(1)}, bf16[384,256]{1,0:T(8,128)(2,1)S(1)}, u32[]{:S(2)}, u32[]{:S(2)}) collective-permute-start(bf16[384,256]{1,0:T(8,128)(2,1)S(1)} %fusion.1), channel_id=1, source_target_pairs={{0,4},{1,5},{2,6},{3,7},{4,0},{5,1},{6,2},{7,3},{8,12},{9,13},{10,... | collective-permute-start | bytes 589832 | tf_op jit(solution)/shard_map/ppermute | solution.py:32
  137.9 1.7 %collective-permute-start.39 = (bf16[384,256]{1,0:T(8,128)(2,1)S(1)}, bf16[384,256]{1,0:T(8,128)(2,1)S(1)}, u32[]{:S(2)}, u32[]{:S(2)}) collective-permute-start(bf16[384,256]{1,0:T(8,128)(2,1)S(1)} %add_convert_fusion.1.refs_4_), channel_id=1, source_target_pairs={{0,2},{1,3},{2,0},{3,1},{4,6},{5,7},{6,4},{7,5},{8,10},{9,11},{10,... | collective-permute-start | bytes 589832 | tf_op jit(solution)/shard_map/ppermute | solution.py:32
  139.6 5.3 %collective-permute-done.46 = bf16[384,256]{1,0:T(8,128)(2,1)S(1)} collective-permute-done((bf16[384,256]{1,0:T(8,128)(2,1)S(1)}, bf16[384,256]{1,0:T(8,128)(2,1)S(1)}, u32[]{:S(2)}, u32[]{:S(2)}) %collective-permute-start.46) | collective-permute-done | bytes 196640 | tf_op jit(solution)/shard_map/ppermute | solution.py:32
  145.5 1.6 %collective-permute-start.34 = (bf16[256,256]{1,0:T(8,128)(2,1)S(1)}, bf16[256,256]{1,0:T(8,128)(2,1)S(1)}, u32[]{:S(2)}, u32[]{:S(2)}) collective-permute-start(bf16[256,256]{1,0:T(8,128)(2,1)S(1)} %add_convert_fusion.2.refs_0_), channel_id=1, source_target_pairs={{0,2},{1,3},{2,0},{3,1},{4,6},{5,7},{6,4},{7,5},{8,10},{9,11},{10,... | collective-permute-start | bytes 393224 | tf_op jit(solution)/shard_map/ppermute | solution.py:32
  147.9 4.2 %collective-permute-done.47.refs_9_ = bf16[384,256]{1,0:T(8,128)(2,1)S(1)} collective-permute-done((bf16[384,256]{1,0:T(8,128)(2,1)S(1)}, bf16[384,256]{1,0:T(8,128)(2,1)S(1)}, u32[]{:S(2)}, u32[]{:S(2)}) %collective-permute-start.47) | collective-permute-done | bytes 196640 | tf_op jit(solution)/shard_map/ppermute | solution.py:32
  152.1 1.4 collective-permute-done.34.refs_1_
  153.5 1.3 collective-permute-done.36.refs_3_
  154.9 2.8 %assemble.1 = (f32[4096,128]{1,0:T(8,128)}, f32[4096,128]{1,0:T(8,128)}) custom-call(s32[3]{0:T(128)S(1)} %pad_add_fusion.ids, bf16[256,256]{1,0:T(8,128)(2,1)S(1)} %add_convert_fusion.2.refs_0_, bf16[256,256]{1,0:T(8,128)(2,1)S(1)} %collective-permute-done.34.refs_1_, bf16[256,256]{1,0:T(8,128)(2,1)S(1)} %collective-permute-done.35.refs_2_, ...), custom_call_target="tpu_custom_call" | custom-call | tf_op jit(solution)/shard_map/assemble/pallas_call | solution.py:48
  (98 shorter events, 18.0 us)
Async XLA Ops:
  2.9 15.9 %collective-permute-start.4 = (bf16[1024,256]{1,0:T(8,128)(2,1)}, bf16[1024,256]{1,0:T(8,128)(2,1)S(1)}, u32[]{:S(2)}, u32[]{:S(2)}) collective-permute-start(bf16[1024,256]{1,0:T(8,128)(2,1)} %pad_maximum_fusion), channel_id=1, source_target_pairs={{0,16},{8,24},{16,0},{24,8},{1,17},{9,25},{17,1},{25,9},{2,18},{10... | collective-permute-start | bytes 1572872 | tf_op jit(solution)/shard_map/ppermute | solution.py:32
  5.9 15.1 %collective-permute-start = (bf16[1024,256]{1,0:T(8,128)(2,1)}, bf16[1024,256]{1,0:T(8,128)(2,1)S(1)}, u32[]{:S(2)}, u32[]{:S(2)}) collective-permute-start(bf16[1024,256]{1,0:T(8,128)(2,1)} %pad_maximum_fusion), channel_id=1, source_target_pairs={{0,8},{8,0},{16,24},{24,16},{1,9},{9,1},{17,25},{25,17},{2,10},{10... | collective-permute-start | bytes 1572872 | tf_op jit(solution)/shard_map/ppermute | solution.py:32
  8.2 22.0 %collective-permute-start.5 = (bf16[1024,256]{1,0:T(8,128)(2,1)}, bf16[1024,256]{1,0:T(8,128)(2,1)}, u32[]{:S(2)}, u32[]{:S(2)}) collective-permute-start(bf16[1024,256]{1,0:T(8,128)(2,1)} %pad_maximum_fusion.1), channel_id=1, source_target_pairs={{0,16},{8,24},{16,0},{24,8},{1,17},{9,25},{17,1},{25,9},{2,18},{10... | collective-permute-start | bytes 1572872 | tf_op jit(solution)/shard_map/ppermute | solution.py:32
  8.7 23.5 %collective-permute-start.1 = (bf16[1024,256]{1,0:T(8,128)(2,1)}, bf16[1024,256]{1,0:T(8,128)(2,1)}, u32[]{:S(2)}, u32[]{:S(2)}) collective-permute-start(bf16[1024,256]{1,0:T(8,128)(2,1)} %pad_maximum_fusion.1), channel_id=1, source_target_pairs={{0,8},{8,0},{16,24},{24,16},{1,9},{9,1},{17,25},{25,17},{2,10},{10... | collective-permute-start | bytes 1572872 | tf_op jit(solution)/shard_map/ppermute | solution.py:32
  18.9 13.4 %collective-permute-start.6 = (bf16[1024,256]{1,0:T(8,128)(2,1)S(1)}, bf16[1024,256]{1,0:T(8,128)(2,1)}, u32[]{:S(2)}, u32[]{:S(2)}) collective-permute-start(bf16[1024,256]{1,0:T(8,128)(2,1)S(1)} %collective-permute-done.4.refs_6_), channel_id=1, source_target_pairs={{0,1},{1,0},{2,3},{3,2},{4,5},{5,4},{6,7},{7,6},{8,9},{9,8},{10,11... | collective-permute-start | bytes 1572872 | tf_op jit(solution)/shard_map/ppermute | solution.py:32
  21.0 19.5 %collective-permute-start.8 = (bf16[1024,256]{1,0:T(8,128)(2,1)S(1)}, bf16[1024,256]{1,0:T(8,128)(2,1)S(1)}, u32[]{:S(2)}, u32[]{:S(2)}) collective-permute-start(bf16[1024,256]{1,0:T(8,128)(2,1)S(1)} %collective-permute-done.refs_2_), channel_id=1, source_target_pairs={{0,16},{8,24},{16,0},{24,8},{1,17},{9,25},{17,1},{25,9},{2,18},{10... | collective-permute-start | bytes 1572872 | tf_op jit(solution)/shard_map/ppermute | solution.py:32
  21.0 14.4 %collective-permute-start.2 = (bf16[1024,256]{1,0:T(8,128)(2,1)S(1)}, bf16[1024,256]{1,0:T(8,128)(2,1)S(1)}, u32[]{:S(2)}, u32[]{:S(2)}) collective-permute-start(bf16[1024,256]{1,0:T(8,128)(2,1)S(1)} %collective-permute-done.refs_2_), channel_id=1, source_target_pairs={{0,1},{1,0},{2,3},{3,2},{4,5},{5,4},{6,7},{7,6},{8,9},{9,8},{10,11... | collective-permute-start | bytes 1572872 | tf_op jit(solution)/shard_map/ppermute | solution.py:32
  30.2 12.5 %collective-permute-start.9 = (bf16[1024,256]{1,0:T(8,128)(2,1)}, bf16[1024,256]{1,0:T(8,128)(2,1)S(1)}, u32[]{:S(2)}, u32[]{:S(2)}) collective-permute-start(bf16[1024,256]{1,0:T(8,128)(2,1)} %collective-permute-done.5.refs_7_), channel_id=1, source_target_pairs={{0,8},{8,0},{16,24},{24,16},{1,9},{9,1},{17,25},{25,17},{2,10},{10... | collective-permute-start | bytes 1572872 | tf_op jit(solution)/shard_map/ppermute | solution.py:32
  32.2 3.1 %collective-permute-start.7 = (bf16[1024,256]{1,0:T(8,128)(2,1)}, bf16[1024,256]{1,0:T(8,128)(2,1)S(1)}, u32[]{:S(2)}, u32[]{:S(2)}) collective-permute-start(bf16[1024,256]{1,0:T(8,128)(2,1)} %collective-permute-done.5.refs_7_), channel_id=1, source_target_pairs={{0,1},{1,0},{2,3},{3,2},{4,5},{5,4},{6,7},{7,6},{8,9},{9,8},{10,11... | collective-permute-start | bytes 1572872 | tf_op jit(solution)/shard_map/ppermute | solution.py:32
  32.2 3.1 %collective-permute-start.3 = (bf16[1024,256]{1,0:T(8,128)(2,1)}, bf16[1024,256]{1,0:T(8,128)(2,1)S(1)}, u32[]{:S(2)}, u32[]{:S(2)}) collective-permute-start(bf16[1024,256]{1,0:T(8,128)(2,1)} %collective-permute-done.1.refs_3_), channel_id=1, source_target_pairs={{0,1},{1,0},{2,3},{3,2},{4,5},{5,4},{6,7},{7,6},{8,9},{9,8},{10,11... | collective-permute-start | bytes 1572872 | tf_op jit(solution)/shard_map/ppermute | solution.py:32
  42.7 2.0 %collective-permute-start.10 = (bf16[1024,256]{1,0:T(8,128)(2,1)S(1)}, bf16[1024,256]{1,0:T(8,128)(2,1)S(1)}, u32[]{:S(2)}, u32[]{:S(2)}) collective-permute-start(bf16[1024,256]{1,0:T(8,128)(2,1)S(1)} %collective-permute-done.8.refs_1_), channel_id=1, source_target_pairs={{0,1},{1,0},{2,3},{3,2},{4,5},{5,4},{6,7},{7,6},{8,9},{9,8},{10,11... | collective-permute-start | bytes 1572872 | tf_op jit(solution)/shard_map/ppermute | solution.py:32
  42.8 2.6 %collective-permute-start.11 = (bf16[1024,256]{1,0:T(8,128)(2,1)S(1)}, bf16[1024,256]{1,0:T(8,128)(2,1)S(1)}, u32[]{:S(2)}, u32[]{:S(2)}) collective-permute-start(bf16[1024,256]{1,0:T(8,128)(2,1)S(1)} %collective-permute-done.9.refs_2_), channel_id=1, source_target_pairs={{0,1},{1,0},{2,3},{3,2},{4,5},{5,4},{6,7},{7,6},{8,9},{9,8},{10,11... | collective-permute-start | bytes 1572872 | tf_op jit(solution)/shard_map/ppermute | solution.py:32
  43.3 29.6 %collective-permute-start.19 = (bf16[192,2560]{1,0:T(8,128)(2,1)S(1)}, bf16[192,2560]{1,0:T(8,128)(2,1)S(1)}, u32[]{:S(2)}, u32[]{:S(2)}) collective-permute-start(bf16[192,2560]{1,0:T(8,128)(2,1)S(1)} %get-tuple-element.55), channel_id=1, source_target_pairs={{0,8},{8,0},{16,24},{24,16},{1,9},{9,1},{17,25},{25,17},{2,10},{10... | collective-permute-start | bytes 2949128 | tf_op jit(solution)/shard_map/ppermute | solution.py:32
  46.6 7.6 %collective-permute-start.14 = (bf16[192,256]{1,0:T(8,128)(2,1)S(1)}, bf16[192,256]{1,0:T(8,128)(2,1)S(1)}, u32[]{:S(2)}, u32[]{:S(2)}) collective-permute-start(bf16[192,256]{1,0:T(8,128)(2,1)S(1)} %project.3.refs_0_), channel_id=1, source_target_pairs={{0,6},{1,7},{2,4},{3,5},{4,2},{5,3},{6,0},{7,1},{8,14},{9,15},{10,... | collective-permute-start | bytes 294920 | tf_op jit(solution)/shard_map/ppermute | solution.py:32
  50.2 8.6 %collective-permute-start.13 = (bf16[192,256]{1,0:T(8,128)(2,1)S(1)}, bf16[192,256]{1,0:T(8,128)(2,1)S(1)}, u32[]{:S(2)}, u32[]{:S(2)}) collective-permute-start(bf16[192,256]{1,0:T(8,128)(2,1)S(1)} %project.3.refs_0_), channel_id=1, source_target_pairs={{0,4},{1,5},{2,6},{3,7},{4,0},{5,1},{6,2},{7,3},{8,12},{9,13},{10,... | collective-permute-start | bytes 294920 | tf_op jit(solution)/shard_map/ppermute | solution.py:32
  50.2 8.6 %collective-permute-start.12 = (bf16[192,256]{1,0:T(8,128)(2,1)S(1)}, bf16[192,256]{1,0:T(8,128)(2,1)S(1)}, u32[]{:S(2)}, u32[]{:S(2)}) collective-permute-start(bf16[192,256]{1,0:T(8,128)(2,1)S(1)} %project.3.refs_0_), channel_id=1, source_target_pairs={{0,2},{1,3},{2,0},{3,1},{4,6},{5,7},{6,4},{7,5},{8,10},{9,11},{10,... | collective-permute-start | bytes 294920 | tf_op jit(solution)/shard_map/ppermute | solution.py:32
  51.0 47.2 %collective-permute-start.27 = (bf16[192,2560]{1,0:T(8,128)(2,1)S(1)}, bf16[192,2560]{1,0:T(8,128)(2,1)S(1)}, u32[]{:S(2)}, u32[]{:S(2)}) collective-permute-start(bf16[192,2560]{1,0:T(8,128)(2,1)S(1)} %get-tuple-element.62), channel_id=1, source_target_pairs={{0,16},{8,24},{16,0},{24,8},{1,17},{9,25},{17,1},{25,9},{2,18},{10... | collective-permute-start | bytes 2949128 | tf_op jit(solution)/shard_map/ppermute | solution.py:32
  58.7 40.6 %collective-permute-start.28 = (bf16[192,2560]{1,0:T(8,128)(2,1)S(1)}, bf16[192,2560]{1,0:T(8,128)(2,1)S(1)}, u32[]{:S(2)}, u32[]{:S(2)}) collective-permute-start(bf16[192,2560]{1,0:T(8,128)(2,1)S(1)} %get-tuple-element.64), channel_id=1, source_target_pairs={{0,24},{8,16},{16,8},{24,0},{1,25},{9,17},{17,9},{25,1},{2,26},{10... | collective-permute-start | bytes 2949128 | tf_op jit(solution)/shard_map/ppermute | solution.py:32
  61.2 1.5 collective-permute-start.16
  62.6 1.3 collective-permute-start.18
  72.8 1.7 %collective-permute-start.20 = (bf16[768,256]{1,0:T(8,128)(2,1)S(1)}, bf16[768,256]{1,0:T(8,128)(2,1)S(1)}, u32[]{:S(2)}, u32[]{:S(2)}) collective-permute-start(bf16[768,256]{1,0:T(8,128)(2,1)S(1)} %get-tuple-element.56), channel_id=1, source_target_pairs={{0,1},{1,0},{2,3},{3,2},{4,5},{5,4},{6,7},{7,6},{8,9},{9,8},{10,11... | collective-permute-start | bytes 1179656 | tf_op jit(solution)/shard_map/ppermute | solution.py:32
  74.7 6.6 %collective-permute-start.21 = (bf16[192,256]{1,0:T(8,128)(2,1)S(1)}, bf16[192,256]{1,0:T(8,128)(2,1)S(1)}, u32[]{:S(2)}, u32[]{:S(2)}) collective-permute-start(bf16[192,256]{1,0:T(8,128)(2,1)S(1)} %get-tuple-element.58), channel_id=1, source_target_pairs={{0,2},{1,3},{2,0},{3,1},{4,6},{5,7},{6,4},{7,5},{8,10},{9,11},{10,... | collective-permute-start | bytes 294920 | tf_op jit(solution)/shard_map/ppermute | solution.py:32
  75.2 10.8 %collective-permute-start.22 = (bf16[192,256]{1,0:T(8,128)(2,1)S(1)}, bf16[192,256]{1,0:T(8,128)(2,1)S(1)}, u32[]{:S(2)}, u32[]{:S(2)}) collective-permute-start(bf16[192,256]{1,0:T(8,128)(2,1)S(1)} %get-tuple-element.59), channel_id=1, source_target_pairs={{0,4},{1,5},{2,6},{3,7},{4,0},{5,1},{6,2},{7,3},{8,12},{9,13},{10,... | collective-permute-start | bytes 294920 | tf_op jit(solution)/shard_map/ppermute | solution.py:32
  77.8 8.3 %collective-permute-start.23 = (bf16[192,256]{1,0:T(8,128)(2,1)S(1)}, bf16[192,256]{1,0:T(8,128)(2,1)S(1)}, u32[]{:S(2)}, u32[]{:S(2)}) collective-permute-start(bf16[192,256]{1,0:T(8,128)(2,1)S(1)} %get-tuple-element.60), channel_id=1, source_target_pairs={{0,6},{1,7},{2,4},{3,5},{4,2},{5,3},{6,0},{7,1},{8,14},{9,15},{10,... | collective-permute-start | bytes 294920 | tf_op jit(solution)/shard_map/ppermute | solution.py:32
  86.1 12.2 %collective-permute-start.26 = (bf16[192,256]{1,0:T(8,128)(2,1)S(1)}, bf16[192,256]{1,0:T(8,128)(2,1)S(1)}, u32[]{:S(2)}, u32[]{:S(2)}) collective-permute-start(bf16[192,256]{1,0:T(8,128)(2,1)S(1)} %total.1.refs_4_.refs_1_), channel_id=1, source_target_pairs={{0,24},{8,16},{16,8},{24,0},{1,25},{9,17},{17,9},{25,1},{2,26},{10... | collective-permute-start | bytes 294920 | tf_op jit(solution)/shard_map/ppermute | solution.py:32
  86.7 12.7 %collective-permute-start.25 = (bf16[192,256]{1,0:T(8,128)(2,1)S(1)}, bf16[192,256]{1,0:T(8,128)(2,1)S(1)}, u32[]{:S(2)}, u32[]{:S(2)}) collective-permute-start(bf16[192,256]{1,0:T(8,128)(2,1)S(1)} %total.1.refs_4_.refs_1_), channel_id=1, source_target_pairs={{0,16},{8,24},{16,0},{24,8},{1,17},{9,25},{17,1},{25,9},{2,18},{10... | collective-permute-start | bytes 294920 | tf_op jit(solution)/shard_map/ppermute | solution.py:32
  88.2 11.1 %collective-permute-start.24 = (bf16[192,256]{1,0:T(8,128)(2,1)S(1)}, bf16[192,256]{1,0:T(8,128)(2,1)S(1)}, u32[]{:S(2)}, u32[]{:S(2)}) collective-permute-start(bf16[192,256]{1,0:T(8,128)(2,1)S(1)} %total.1.refs_4_.refs_1_), channel_id=1, source_target_pairs={{0,8},{8,0},{16,24},{24,16},{1,9},{9,1},{17,25},{25,17},{2,10},{10... | collective-permute-start | bytes 294920 | tf_op jit(solution)/shard_map/ppermute | solution.py:32
  101.0 5.4 %collective-permute-start.31 = (bf16[3072,256]{1,0:T(8,128)(2,1)S(1)}, bf16[3072,256]{1,0:T(8,128)(2,1)S(1)}, u32[]{:S(2)}, u32[]{:S(2)}) collective-permute-start(bf16[3072,256]{1,0:T(8,128)(2,1)S(1)} %get-tuple-element.77), channel_id=1, source_target_pairs={{0,1},{1,0},{2,3},{3,2},{4,5},{5,4},{6,7},{7,6},{8,9},{9,8},{10,11... | collective-permute-start | bytes 4718600 | tf_op jit(solution)/shard_map/ppermute | solution.py:32
  102.4 2.4 %collective-permute-start.29 = (bf16[512,256]{1,0:T(8,128)(2,1)S(1)}, bf16[512,256]{1,0:T(8,128)(2,1)S(1)}, u32[]{:S(2)}, u32[]{:S(2)}) collective-permute-start(bf16[512,256]{1,0:T(8,128)(2,1)S(1)} %get-tuple-element.72), channel_id=1, source_target_pairs={{0,1},{1,0},{2,3},{3,2},{4,5},{5,4},{6,7},{7,6},{8,9},{9,8},{10,11... | collective-permute-start | bytes 786440 | tf_op jit(solution)/shard_map/ppermute | solution.py:32
  104.5 1.8 %collective-permute-start.30 = (bf16[768,256]{1,0:T(8,128)(2,1)S(1)}, bf16[768,256]{1,0:T(8,128)(2,1)S(1)}, u32[]{:S(2)}, u32[]{:S(2)}) collective-permute-start(bf16[768,256]{1,0:T(8,128)(2,1)S(1)} %get-tuple-element.74), channel_id=1, source_target_pairs={{0,1},{1,0},{2,3},{3,2},{4,5},{5,4},{6,7},{7,6},{8,9},{9,8},{10,11... | collective-permute-start | bytes 1179656 | tf_op jit(solution)/shard_map/ppermute | solution.py:32
  107.1 6.4 %collective-permute-start.32 = (bf16[256,256]{1,0:T(8,128)(2,1)S(1)}, bf16[256,256]{1,0:T(8,128)(2,1)S(1)}, u32[]{:S(2)}, u32[]{:S(2)}) collective-permute-start(bf16[256,256]{1,0:T(8,128)(2,1)S(1)} %slice.74), channel_id=1, source_target_pairs={{0,2},{1,3},{2,0},{3,1},{4,6},{5,7},{6,4},{7,5},{8,10},{9,11},{10,... | collective-permute-start | bytes 393224 | tf_op jit(solution)/shard_map/ppermute | solution.py:32
  108.6 10.0 %collective-permute-start.37 = (bf16[384,256]{1,0:T(8,128)(2,1)S(1)}, bf16[384,256]{1,0:T(8,128)(2,1)S(1)}, u32[]{:S(2)}, u32[]{:S(2)}) collective-permute-start(bf16[384,256]{1,0:T(8,128)(2,1)S(1)} %slice.73), channel_id=1, source_target_pairs={{0,2},{1,3},{2,0},{3,1},{4,6},{5,7},{6,4},{7,5},{8,10},{9,11},{10,... | collective-permute-start | bytes 589832 | tf_op jit(solution)/shard_map/ppermute | solution.py:32
  109.3 17.7 %collective-permute-start.42 = (bf16[768,256]{1,0:T(8,128)(2,1)S(1)}, bf16[768,256]{1,0:T(8,128)(2,1)S(1)}, u32[]{:S(2)}, u32[]{:S(2)}) collective-permute-start(bf16[768,256]{1,0:T(8,128)(2,1)S(1)} %get-tuple-element.81), channel_id=1, source_target_pairs={{0,8},{8,0},{16,24},{24,16},{1,9},{9,1},{17,25},{25,17},{2,10},{10... | collective-permute-start | bytes 1179656 | tf_op jit(solution)/shard_map/ppermute | solution.py:32
  110.8 18.7 %collective-permute-start.43 = (bf16[768,256]{1,0:T(8,128)(2,1)S(1)}, bf16[768,256]{1,0:T(8,128)(2,1)S(1)}, u32[]{:S(2)}, u32[]{:S(2)}) collective-permute-start(bf16[768,256]{1,0:T(8,128)(2,1)S(1)} %get-tuple-element.82), channel_id=1, source_target_pairs={{0,16},{8,24},{16,0},{24,8},{1,17},{9,25},{17,1},{25,9},{2,18},{10... | collective-permute-start | bytes 1179656 | tf_op jit(solution)/shard_map/ppermute | solution.py:32
  112.3 17.2 %collective-permute-start.44 = (bf16[768,256]{1,0:T(8,128)(2,1)S(1)}, bf16[768,256]{1,0:T(8,128)(2,1)S(1)}, u32[]{:S(2)}, u32[]{:S(2)}) collective-permute-start(bf16[768,256]{1,0:T(8,128)(2,1)S(1)} %get-tuple-element.83), channel_id=1, source_target_pairs={{0,24},{8,16},{16,8},{24,0},{1,25},{9,17},{17,9},{25,1},{2,26},{10... | collective-permute-start | bytes 1179656 | tf_op jit(solution)/shard_map/ppermute | solution.py:32
  113.6 13.4 %collective-permute-start.33 = (bf16[256,256]{1,0:T(8,128)(2,1)S(1)}, bf16[256,256]{1,0:T(8,128)(2,1)S(1)}, u32[]{:S(2)}, u32[]{:S(2)}) collective-permute-start(bf16[256,256]{1,0:T(8,128)(2,1)S(1)} %fusion.2), channel_id=1, source_target_pairs={{0,4},{1,5},{2,6},{3,7},{4,0},{5,1},{6,2},{7,3},{8,12},{9,13},{10,... | collective-permute-start | bytes 393224 | tf_op jit(solution)/shard_map/ppermute | solution.py:32
  118.6 12.5 %collective-permute-start.38 = (bf16[384,256]{1,0:T(8,128)(2,1)S(1)}, bf16[384,256]{1,0:T(8,128)(2,1)S(1)}, u32[]{:S(2)}, u32[]{:S(2)}) collective-permute-start(bf16[384,256]{1,0:T(8,128)(2,1)S(1)} %fusion), channel_id=1, source_target_pairs={{0,4},{1,5},{2,6},{3,7},{4,0},{5,1},{6,2},{7,3},{8,12},{9,13},{10,... | collective-permute-start | bytes 589832 | tf_op jit(solution)/shard_map/ppermute | solution.py:32
  129.7 5.7 %collective-permute-start.45 = (bf16[384,256]{1,0:T(8,128)(2,1)S(1)}, bf16[384,256]{1,0:T(8,128)(2,1)S(1)}, u32[]{:S(2)}, u32[]{:S(2)}) collective-permute-start(bf16[384,256]{1,0:T(8,128)(2,1)S(1)} %slice.72), channel_id=1, source_target_pairs={{0,2},{1,3},{2,0},{3,1},{4,6},{5,7},{6,4},{7,5},{8,10},{9,11},{10,... | collective-permute-start | bytes 589832 | tf_op jit(solution)/shard_map/ppermute | solution.py:32
  135.5 9.4 %collective-permute-start.46 = (bf16[384,256]{1,0:T(8,128)(2,1)S(1)}, bf16[384,256]{1,0:T(8,128)(2,1)S(1)}, u32[]{:S(2)}, u32[]{:S(2)}) collective-permute-start(bf16[384,256]{1,0:T(8,128)(2,1)S(1)} %fusion.1), channel_id=1, source_target_pairs={{0,4},{1,5},{2,6},{3,7},{4,0},{5,1},{6,2},{7,3},{8,12},{9,13},{10,... | collective-permute-start | bytes 589832 | tf_op jit(solution)/shard_map/ppermute | solution.py:32
  137.9 9.4 %collective-permute-start.39 = (bf16[384,256]{1,0:T(8,128)(2,1)S(1)}, bf16[384,256]{1,0:T(8,128)(2,1)S(1)}, u32[]{:S(2)}, u32[]{:S(2)}) collective-permute-start(bf16[384,256]{1,0:T(8,128)(2,1)S(1)} %add_convert_fusion.1.refs_4_), channel_id=1, source_target_pairs={{0,2},{1,3},{2,0},{3,1},{4,6},{5,7},{6,4},{7,5},{8,10},{9,11},{10,... | collective-permute-start | bytes 589832 | tf_op jit(solution)/shard_map/ppermute | solution.py:32
  145.0 7.1 %collective-permute-start.47 = (bf16[384,256]{1,0:T(8,128)(2,1)S(1)}, bf16[384,256]{1,0:T(8,128)(2,1)S(1)}, u32[]{:S(2)}, u32[]{:S(2)}) collective-permute-start(bf16[384,256]{1,0:T(8,128)(2,1)S(1)} %add_convert_fusion.refs_8_), channel_id=1, source_target_pairs={{0,2},{1,3},{2,0},{3,1},{4,6},{5,7},{6,4},{7,5},{8,10},{9,11},{10,... | collective-permute-start | bytes 589832 | tf_op jit(solution)/shard_map/ppermute | solution.py:32
  145.5 2.2 %collective-permute-start.35 = (bf16[256,256]{1,0:T(8,128)(2,1)S(1)}, bf16[256,256]{1,0:T(8,128)(2,1)S(1)}, u32[]{:S(2)}, u32[]{:S(2)}) collective-permute-start(bf16[256,256]{1,0:T(8,128)(2,1)S(1)} %add_convert_fusion.2.refs_0_), channel_id=1, source_target_pairs={{0,1},{1,0},{2,3},{3,2},{4,5},{5,4},{6,7},{7,6},{8,9},{9,8},{10,11... | collective-permute-start | bytes 393224 | tf_op jit(solution)/shard_map/ppermute | solution.py:32
  145.5 8.0 %collective-permute-start.34 = (bf16[256,256]{1,0:T(8,128)(2,1)S(1)}, bf16[256,256]{1,0:T(8,128)(2,1)S(1)}, u32[]{:S(2)}, u32[]{:S(2)}) collective-permute-start(bf16[256,256]{1,0:T(8,128)(2,1)S(1)} %add_convert_fusion.2.refs_0_), channel_id=1, source_target_pairs={{0,2},{1,3},{2,0},{3,1},{4,6},{5,7},{6,4},{7,5},{8,10},{9,11},{10,... | collective-permute-start | bytes 393224 | tf_op jit(solution)/shard_map/ppermute | solution.py:32
  147.1 7.7 %collective-permute-start.40 = (bf16[384,256]{1,0:T(8,128)(2,1)S(1)}, bf16[384,256]{1,0:T(8,128)(2,1)S(1)}, u32[]{:S(2)}, u32[]{:S(2)}) collective-permute-start(bf16[384,256]{1,0:T(8,128)(2,1)S(1)} %add_convert_fusion.1.refs_4_), channel_id=1, source_target_pairs={{0,1},{1,0},{2,3},{3,2},{4,5},{5,4},{6,7},{7,6},{8,9},{9,8},{10,11... | collective-permute-start | bytes 589832 | tf_op jit(solution)/shard_map/ppermute | solution.py:32
  147.3 7.5 %collective-permute-start.41 = (bf16[384,256]{1,0:T(8,128)(2,1)S(1)}, bf16[384,256]{1,0:T(8,128)(2,1)S(1)}, u32[]{:S(2)}, u32[]{:S(2)}) collective-permute-start(bf16[384,256]{1,0:T(8,128)(2,1)S(1)} %collective-permute-done.39.refs_5_), channel_id=1, source_target_pairs={{0,1},{1,0},{2,3},{3,2},{4,5},{5,4},{6,7},{7,6},{8,9},{9,8},{10,11... | collective-permute-start | bytes 589832 | tf_op jit(solution)/shard_map/ppermute | solution.py:32
  147.6 7.2 %collective-permute-start.48 = (bf16[384,256]{1,0:T(8,128)(2,1)S(1)}, bf16[384,256]{1,0:T(8,128)(2,1)S(1)}, u32[]{:S(2)}, u32[]{:S(2)}) collective-permute-start(bf16[384,256]{1,0:T(8,128)(2,1)S(1)} %add_convert_fusion.refs_8_), channel_id=1, source_target_pairs={{0,1},{1,0},{2,3},{3,2},{4,5},{5,4},{6,7},{7,6},{8,9},{9,8},{10,11... | collective-permute-start | bytes 589832 | tf_op jit(solution)/shard_map/ppermute | solution.py:32
  152.1 2.8 %collective-permute-start.49 = (bf16[384,256]{1,0:T(8,128)(2,1)S(1)}, bf16[384,256]{1,0:T(8,128)(2,1)S(1)}, u32[]{:S(2)}, u32[]{:S(2)}) collective-permute-start(bf16[384,256]{1,0:T(8,128)(2,1)S(1)} %collective-permute-done.47.refs_9_), channel_id=1, source_target_pairs={{0,1},{1,0},{2,3},{3,2},{4,5},{5,4},{6,7},{7,6},{8,9},{9,8},{10,11... | collective-permute-start | bytes 589832 | tf_op jit(solution)/shard_map/ppermute | solution.py:32
  153.5 1.3 collective-permute-start.36
  (10 other events, 133.3 us)

commit v9 on v8

--- a/solution.py
+++ b/solution.py
@@ -263,8 +263,8 @@
         for at, group in enumerate(plan.groups):
             for start in range(0, rows, tile):
                 product = None
-                for array, block, grad in group:
-                    origin = plan.origin + (core ^ side) * rows + start
+                for array, block, grad, shift in group:
+                    origin = plan.origin - shift + (core ^ side) * rows + start
                     if block is not None:
                         origin = origin + (dp ^ block) * plan.block_rows
                     columns = pl.ds(pl.multiple_of(origin, 128), tile)
@@ -299,7 +299,11 @@
         (ids,),
         (*hidden, *grads),
     )
-    return ours.astype(jnp.float32) + swap(theirs, "ctx", 1).astype(jnp.float32)
+    return ours, swap(theirs, "ctx", 1)
+
+
+def add_cores(ours, came):
+    return ours.astype(jnp.float32) + came.astype(jnp.float32)
 
 
 def parts_over_dp(array):
@@ -427,10 +431,12 @@
     sizes = region_sizes(block_rows)
     regions = [(sum(sizes[:at]), size // 2) for at, size in enumerate(sizes)]
     first_rows = sum(sizes[:-1])
-    moving = {
-        j: lax.dynamic_slice_in_dim(inputs, (dp ^ j) * block_rows, first_rows, 1)
-        for j in range(dp_count)
-    }
+    def columns(j, start, count):
+        return lax.dynamic_slice_in_dim(inputs, (dp ^ j) * block_rows + start, count, 1)
+
+    moving = {j: columns(j, 0, first_rows) for j in range(dp_count) if j != near[-1]}
+    cuts = {"early": (near[-1], sizes[0], sizes[1]), "late": (near[-1], 0, sizes[0])}
+    moving.update({name: columns(*cut) for name, cut in cuts.items()})
 
     near_pieces = gather_near(w_key, w_value)
     far_pieces = gather_far(near_pieces)
@@ -438,42 +444,49 @@
     early = project(
         ids, (w_key, w_value), inputs, block_rows, near_pieces, jnp.float32, bytes_cost(1 << 24)
     )
-    others = near + far
+    others = [j for j in near if j in moving] + far + list(cuts)
     early, *tied = hold([early] + [moving[j] for j in others], far_pieces)
     moving.update(zip(others, tied))
     far_pieces.update(from_other_core(far_pieces))
     own = project(ids, (early,), inputs, block_rows, far_pieces, jnp.bfloat16)
     moved = {0: moving[0]}
-    moved.update({j: swap(moving[j], "dp", j) for j in near})
+    moved.update({j: swap(moving[j], "dp", j) for j in near if j in moving})
+    moved["early"] = swap(moving["early"], "dp", near[-1])
     along = gather_along_z(own)
-    tied, _ = after([moving[j] for j in far], *along)
-    moving.update(zip(far, tied))
+    rest = ["late"] + far
+    tied, _ = after([moving[j] for j in rest], *along)
+    moving.update(zip(rest, tied))
     along, _ = after(along)
     kv_blocks = both_cores(along)
 
+    moved["late"] = swap(moving["late"], "dp", near[-1])
     moved.update({j: swap(moving[j], "dp", j) for j in far})
 
     query_grad, keep, send = attention(
         me, stretch_order, doc_lengths[0], queries[0], grad_out[0], kv_blocks, head_dim
     )
-    (send,), ended = after([send], moved[near[0]])
-    moved.update(zip(near, ended))
+    soon = [j for j in moved if j and j not in rest]
+    (send,), ended = after([send], *[moved[j] for j in soon])
+    moved.update(zip(soon, ended))
     own, *leaving = add_and_split(keep, swap(send, "ctx", 1), z_count)
     grad = add_all([own] + [swap(one, "ctx", 2 * m) for m, one in enumerate(leaving, 1)])
     grads = [grad] + [swap(grad, "dp", j) for j in range(1, dp_count)]
 
-    (grad,), ended = after([grad], *grads[1:], *[moved[j] for j in others])
+    (grad,), ended = after([grad], *grads[1:], *[moved[j] for j in rest])
     grads[1:] = ended[: dp_count - 1]
-    moved.update(zip(others, ended[dp_count - 1 :]))
-    groups = [[(0, j, 0)] for j in range(dp_count)]
-    own = weight_rows(ids, [inputs], [grad], groups, *regions[-1], block_rows, sub_count)
-    own = parts_over_dp(own)
-    groups = [[(j, None, j) for j in range(dp_count)]]
-    arrays = [moved[j] for j in range(dp_count)]
-    moved_parts = [
-        weight_rows(ids, arrays, grads, groups, *region, block_rows, sub_count)
-        for region in regions[:-1]
-    ]
+    moved.update(zip(rest, ended[dp_count - 1 :]))
+    groups = [[(0, j, 0, 0)] for j in range(dp_count)]
+    ours, came = weight_rows(
+        ids, [inputs], [grad], groups, *regions[-1], block_rows, sub_count
+    )
+    own = parts_over_dp(add_cores(ours, came))
+    moved_parts = []
+    for region, name in zip(regions[:-1], ("late", "early")):
+        arrays = [moved[name if j == near[-1] else j] for j in range(dp_count)]
+        shifts = [cuts[name][1] if j == near[-1] else 0 for j in range(dp_count)]
+        groups = [[(j, None, j, shifts[j]) for j in range(dp_count)]]
+        pair = weight_rows(ids, arrays, grads, groups, *region, block_rows, sub_count)
+        moved_parts.append(add_cores(*pair))
     moved_parts, own = after(moved_parts, *own)
     own = [swap(one, "dp", j) if j else one for j, one in enumerate(own)]
     finals = []

time: 158 us -> 160 us (1.013)
  starting transfers between devices: 46 us -> 50.4 us
  waiting for transfers between devices: 81.5 us -> 79.3 us
    ppermute x50 -> x51, starting transfers between devices: 46 us -> 50.4 us  [swap(): return lax.ppermute(array, axis, [(i, i ^ distance) for i in range(count)])]
    ppermute x50 -> x51, waiting for transfers between devices: 81.5 us -> 79.3 us  [swap(): return lax.ppermute(array, axis, [(i, i ^ distance) for i in range(count)])]
    dynamic_slice x1 -> x3, local copies, waits for them, and re-layouts: 2.49 us -> 4.36 us  [columns(): lax.dynamic_slice_in_dim(inputs, (dp ^ j) * block_rows + start, count, 1)]
  transfers between devices with their start and end apart: 50 -> 51, of which waited for: 27 -> 27; matrix products, arithmetic and copies ran while one was open for 3% -> 4% of each run, Pallas kernels for 10% -> 10%
where the time goes in v9:
time: 160 us
  waiting for transfers between devices  79.3 us (50%)
  starting transfers between devices  50.4 us (32%)
  Pallas kernels  20.4 us (13%)
  local copies, waits for them, and re-layouts  5.84 us (4%)
  other arithmetic  2.81 us (2%)
    ppermute x51, waiting for transfers between devices, swap(): return lax.ppermute(array, axis, [(i, i ^ distance) for i in range(count)])  79.3 us
    ppermute x51, starting transfers between devices, swap(): return lax.ppermute(array, axis, [(i, i ^ distance) for i in range(count)])  50.4 us
    pallas_call x8, Pallas kernels, kernel_call(): pl.pallas_call(kernel, out_shape=outs, in_specs=[smem] * len(scalars) + [...  11.5 us
    pallas_call x1, Pallas kernels, attention(): pl.pallas_call(functools.partial(attention_kernel, shape), out_shape=(jax...  8.87 us
    dynamic_slice x3, local copies, waits for them, and re-layouts, columns(): lax.dynamic_slice_in_dim(inputs, (dp ^ j) * block_rows + start, count, 1)  4.36 us
  transfers between devices with their start and end apart: 51, of which 27 were waited for; matrix products, arithmetic and copies ran while one was open for 4% of the time, Pallas kernels for 10%

profile of v9, /device:TPU:0, one launch (start us, length us, event | category | flops | bytes accessed | tf_op | source)
XLA Modules:
  0.0 159.7 jit_solution(15626589850528200732)
XLA Ops:
  0.7 1.3 constant_dynamic-slice_fusion
  2.8 3.0 %collective-permute-start.4 = (bf16[1024,256]{1,0:T(8,128)(2,1)}, bf16[1024,256]{1,0:T(8,128)(2,1)S(1)}, u32[]{:S(2)}, u32[]{:S(2)}) collective-permute-start(bf16[1024,256]{1,0:T(8,128)(2,1)} %pad_maximum_fusion), channel_id=1, source_target_pairs={{0,16},{8,24},{16,0},{24,8},{1,17},{9,25},{17,1},{25,9},{2,18},{10... | collective-permute-start | bytes 1572872 | tf_op jit(solution)/shard_map/ppermute | solution.py:32
  5.7 1.5 collective-permute-start
  8.6 10.1 %collective-permute-done.4.refs_6_ = bf16[1024,256]{1,0:T(8,128)(2,1)S(1)} collective-permute-done((bf16[1024,256]{1,0:T(8,128)(2,1)}, bf16[1024,256]{1,0:T(8,128)(2,1)S(1)}, u32[]{:S(2)}, u32[]{:S(2)}) %collective-permute-start.4) | collective-permute-done | bytes 524320 | tf_op jit(solution)/shard_map/ppermute | solution.py:32
  19.8 1.3 dynamic-slice_bitcast_fusion.3
  21.1 2.1 %collective-permute-start.8 = (bf16[1024,256]{1,0:T(8,128)(2,1)S(1)}, bf16[1024,256]{1,0:T(8,128)(2,1)S(1)}, u32[]{:S(2)}, u32[]{:S(2)}) collective-permute-start(bf16[1024,256]{1,0:T(8,128)(2,1)S(1)} %collective-permute-done.refs_2_), channel_id=1, source_target_pairs={{0,16},{8,24},{16,0},{24,8},{1,17},{9,25},{17,1},{25,9},{2,18},{10... | collective-permute-start | bytes 1572872 | tf_op jit(solution)/shard_map/ppermute | solution.py:32
  23.5 6.5 %collective-permute-done.5.refs_7_ = bf16[1024,256]{1,0:T(8,128)(2,1)S(1)} collective-permute-done((bf16[1024,256]{1,0:T(8,128)(2,1)}, bf16[1024,256]{1,0:T(8,128)(2,1)S(1)}, u32[]{:S(2)}, u32[]{:S(2)}) %collective-permute-start.5) | collective-permute-done | bytes 524320 | tf_op jit(solution)/shard_map/ppermute | solution.py:32
  29.9 2.0 %collective-permute-start.9 = (bf16[1024,256]{1,0:T(8,128)(2,1)S(1)}, bf16[1024,256]{1,0:T(8,128)(2,1)S(1)}, u32[]{:S(2)}, u32[]{:S(2)}) collective-permute-start(bf16[1024,256]{1,0:T(8,128)(2,1)S(1)} %collective-permute-done.5.refs_7_), channel_id=1, source_target_pairs={{0,8},{8,0},{16,24},{24,16},{1,9},{9,1},{17,25},{25,17},{2,10},{10... | collective-permute-start | bytes 1572872 | tf_op jit(solution)/shard_map/ppermute | solution.py:32
  32.6 2.0 %dynamic-slice_bitcast_fusion = (bf16[192,2560]{1,0:T(8,128)(2,1)S(1)}, bf16[192,2560]{1,0:T(8,128)(2,1)S(1)}, bf16[192,2560]{1,0:T(8,128)(2,1)S(1)}) fusion(bf16[1,192,16384]{2,1,0:T(8,128)(2,1)} %param.7, s32[]{:T(128)S(6)} %select_n.46, s32[]{:T(128)S(6)} %select_n.43, s32[]{:T(128)S(6)} %select_n.42), kind=kLoop, calls=%fused_computation.1 | loop fusion | bytes 5898252 | tf_op jit(solution)/shard_map/dynamic_slice | solution.py:435
  34.6 2.9 %project.2.refs_0_ = f32[192,256]{1,0:T(8,128)S(1)} custom-call(s32[3]{0:T(128)S(1)} %pad_add_fusion.ids, bf16[192,16384]{1,0:T(8,128)(2,1)S(1)} %bitcast.19, bf16[4096,128]{1,0:T(8,128)(2,1)S(1)} %copy-done.1, bf16[4096,128]{1,0:T(8,128)(2,1)S(1)} %copy-done.2, bf16[1024,256]{1,0:T(8,128)(2,1)S(1)} %collective-permute-done.refs_2_, ...), custom_call_target="tpu_custom_call" | custom-call | bytes 16777216 | tf_op jit(solution)/shard_map/project/pallas_call | solution.py:48
  37.6 2.8 %collective-permute-done.8.refs_1_ = bf16[1024,256]{1,0:T(8,128)(2,1)S(1)} collective-permute-done((bf16[1024,256]{1,0:T(8,128)(2,1)S(1)}, bf16[1024,256]{1,0:T(8,128)(2,1)S(1)}, u32[]{:S(2)}, u32[]{:S(2)}) %collective-permute-start.8) | collective-permute-done | bytes 524320 | tf_op jit(solution)/shard_map/ppermute | solution.py:32
  40.3 1.9 %collective-permute-done.9.refs_2_ = bf16[1024,256]{1,0:T(8,128)(2,1)S(1)} collective-permute-done((bf16[1024,256]{1,0:T(8,128)(2,1)S(1)}, bf16[1024,256]{1,0:T(8,128)(2,1)S(1)}, u32[]{:S(2)}, u32[]{:S(2)}) %collective-permute-start.9) | collective-permute-done | bytes 524320 | tf_op jit(solution)/shard_map/ppermute | solution.py:32
  42.8 1.4 collective-permute-start.19
  44.2 1.5 collective-permute-start.20
  46.9 3.7 %collective-permute-start.14 = (bf16[192,256]{1,0:T(8,128)(2,1)S(1)}, bf16[192,256]{1,0:T(8,128)(2,1)S(1)}, u32[]{:S(2)}, u32[]{:S(2)}) collective-permute-start(bf16[192,256]{1,0:T(8,128)(2,1)S(1)} %project.3.refs_0_), channel_id=1, source_target_pairs={{0,6},{1,7},{2,4},{3,5},{4,2},{5,3},{6,0},{7,1},{8,14},{9,15},{10,... | collective-permute-start | bytes 294920 | tf_op jit(solution)/shard_map/ppermute | solution.py:32
  51.3 3.2 %collective-permute-done.14.refs_6_ = bf16[192,256]{1,0:T(8,128)(2,1)S(1)} collective-permute-done((bf16[192,256]{1,0:T(8,128)(2,1)S(1)}, bf16[192,256]{1,0:T(8,128)(2,1)S(1)}, u32[]{:S(2)}, u32[]{:S(2)}) %collective-permute-start.14) | collective-permute-done | bytes 98336 | tf_op jit(solution)/shard_map/ppermute | solution.py:32
  54.5 4.0 %collective-permute-done.13.refs_4_ = bf16[192,256]{1,0:T(8,128)(2,1)S(1)} collective-permute-done((bf16[192,256]{1,0:T(8,128)(2,1)S(1)}, bf16[192,256]{1,0:T(8,128)(2,1)S(1)}, u32[]{:S(2)}, u32[]{:S(2)}) %collective-permute-start.13) | collective-permute-done | bytes 98336 | tf_op jit(solution)/shard_map/ppermute | solution.py:32
  58.5 2.2 %collective-permute-start.29 = (bf16[192,2560]{1,0:T(8,128)(2,1)S(1)}, bf16[192,2560]{1,0:T(8,128)(2,1)S(1)}, u32[]{:S(2)}, u32[]{:S(2)}) collective-permute-start(bf16[192,2560]{1,0:T(8,128)(2,1)S(1)} %get-tuple-element.68), channel_id=1, source_target_pairs={{0,24},{8,16},{16,8},{24,0},{1,25},{9,17},{17,9},{25,1},{2,26},{10... | collective-permute-start | bytes 2949128 | tf_op jit(solution)/shard_map/ppermute | solution.py:32
  63.5 8.9 %attention.1 = (bf16[192,1024]{1,0:T(8,128)(2,1)}, f32[768,256]{1,0:T(8,128)S(1)}, bf16[768,256]{1,0:T(8,128)(2,1)S(1)}) custom-call(s32[1]{0:T(128)} %bitcast.ids, s32[16]{0:T(128)S(1)} %copy-done.5, s32[8]{0:T(128)S(1)} %bitcast.24, bf16[192,1024]{1,0:T(8,128)(2,1)S(1)} %bitcast.22, bf16[192,1024]{1,0:T(8,128)(2,1)S(1)} %bitcast.23, ...), custom_call_target="tpu_custom_call" | custom-call | tf_op jit(solution)/shard_map/attention/pallas_call | solution.py:169
  74.8 2.5 %collective-permute-start.23 = (bf16[192,256]{1,0:T(8,128)(2,1)S(1)}, bf16[192,256]{1,0:T(8,128)(2,1)S(1)}, u32[]{:S(2)}, u32[]{:S(2)}) collective-permute-start(bf16[192,256]{1,0:T(8,128)(2,1)S(1)} %get-tuple-element.63), channel_id=1, source_target_pairs={{0,4},{1,5},{2,6},{3,7},{4,0},{5,1},{6,2},{7,3},{8,12},{9,13},{10,... | collective-permute-start | bytes 294920 | tf_op jit(solution)/shard_map/ppermute | solution.py:32
  77.3 1.4 collective-permute-start.24
  78.6 2.1 %collective-permute-done.22.refs_1_ = bf16[192,256]{1,0:T(8,128)(2,1)S(1)} collective-permute-done((bf16[192,256]{1,0:T(8,128)(2,1)S(1)}, bf16[192,256]{1,0:T(8,128)(2,1)S(1)}, u32[]{:S(2)}, u32[]{:S(2)}) %collective-permute-start.22) | collective-permute-done | bytes 98336 | tf_op jit(solution)/shard_map/ppermute | solution.py:32
  80.7 4.8 %collective-permute-done.23.refs_2_ = bf16[192,256]{1,0:T(8,128)(2,1)S(1)} collective-permute-done((bf16[192,256]{1,0:T(8,128)(2,1)S(1)}, bf16[192,256]{1,0:T(8,128)(2,1)S(1)}, u32[]{:S(2)}, u32[]{:S(2)}) %collective-permute-start.23) | collective-permute-done | bytes 98336 | tf_op jit(solution)/shard_map/ppermute | solution.py:32
  86.4 1.3 collective-permute-start.26
  87.7 1.5 collective-permute-start.25
  89.2 9.9 %collective-permute-done.28.refs_2_ = bf16[192,1024]{1,0:T(8,128)(2,1)S(1)} collective-permute-done((bf16[192,1024]{1,0:T(8,128)(2,1)S(1)}, bf16[192,1024]{1,0:T(8,128)(2,1)S(1)}, u32[]{:S(2)}, u32[]{:S(2)}) %collective-permute-start.28) | collective-permute-done | bytes 393248 | tf_op jit(solution)/shard_map/ppermute | solution.py:32
  99.1 2.0 %collective-permute-done.26.refs_6_ = bf16[192,256]{1,0:T(8,128)(2,1)S(1)} collective-permute-done((bf16[192,256]{1,0:T(8,128)(2,1)S(1)}, bf16[192,256]{1,0:T(8,128)(2,1)S(1)}, u32[]{:S(2)}, u32[]{:S(2)}) %collective-permute-start.26) | collective-permute-done | bytes 98336 | tf_op jit(solution)/shard_map/ppermute | solution.py:32
  101.1 1.7 %weight_rows.5 = (bf16[3072,256]{1,0:T(8,128)(2,1)S(1)}, bf16[3072,256]{1,0:T(8,128)(2,1)S(1)}) custom-call(s32[3]{0:T(128)S(1)} %pad_add_fusion.ids, bf16[192,16384]{1,0:T(8,128)(2,1)S(1)} %bitcast.21, bf16[192,256]{1,0:T(8,128)(2,1)S(1)} %total.1.refs_4_.refs_1_), custom_call_target="tpu_custom_call" | custom-call | tf_op jit(solution)/shard_map/weight_rows/pallas_call | solution.py:48
  102.9 1.3 weight_rows.3
  104.7 1.6 weight_rows.4
  106.7 1.4 collective-permute-done.31
  108.8 1.6 %collective-permute-start.33 = (bf16[256,256]{1,0:T(8,128)(2,1)S(1)}, bf16[256,256]{1,0:T(8,128)(2,1)S(1)}, u32[]{:S(2)}, u32[]{:S(2)}) collective-permute-start(bf16[256,256]{1,0:T(8,128)(2,1)S(1)} %slice.74), channel_id=1, source_target_pairs={{0,2},{1,3},{2,0},{3,1},{4,6},{5,7},{6,4},{7,5},{8,10},{9,11},{10,... | collective-permute-start | bytes 393224 | tf_op jit(solution)/shard_map/ppermute | solution.py:32
  111.0 1.5 collective-permute-start.43
  113.0 1.5 collective-permute-start.45
  115.2 2.7 %collective-permute-start.34 = (bf16[256,256]{1,0:T(8,128)(2,1)S(1)}, bf16[256,256]{1,0:T(8,128)(2,1)S(1)}, u32[]{:S(2)}, u32[]{:S(2)}) collective-permute-start(bf16[256,256]{1,0:T(8,128)(2,1)S(1)} %fusion.2), channel_id=1, source_target_pairs={{0,4},{1,5},{2,6},{3,7},{4,0},{5,1},{6,2},{7,3},{8,12},{9,13},{10,... | collective-permute-start | bytes 393224 | tf_op jit(solution)/shard_map/ppermute | solution.py:32
  117.9 2.5 %collective-permute-done.38 = bf16[384,256]{1,0:T(8,128)(2,1)S(1)} collective-permute-done((bf16[384,256]{1,0:T(8,128)(2,1)S(1)}, bf16[384,256]{1,0:T(8,128)(2,1)S(1)}, u32[]{:S(2)}, u32[]{:S(2)}) %collective-permute-start.38) | collective-permute-done | bytes 196640 | tf_op jit(solution)/shard_map/ppermute | solution.py:32
  120.4 1.7 %collective-permute-start.39 = (bf16[384,256]{1,0:T(8,128)(2,1)S(1)}, bf16[384,256]{1,0:T(8,128)(2,1)S(1)}, u32[]{:S(2)}, u32[]{:S(2)}) collective-permute-start(bf16[384,256]{1,0:T(8,128)(2,1)S(1)} %fusion), channel_id=1, source_target_pairs={{0,4},{1,5},{2,6},{3,7},{4,0},{5,1},{6,2},{7,3},{8,12},{9,13},{10,... | collective-permute-start | bytes 589832 | tf_op jit(solution)/shard_map/ppermute | solution.py:32
  122.1 6.4 %collective-permute-done.34 = bf16[256,256]{1,0:T(8,128)(2,1)S(1)} collective-permute-done((bf16[256,256]{1,0:T(8,128)(2,1)S(1)}, bf16[256,256]{1,0:T(8,128)(2,1)S(1)}, u32[]{:S(2)}, u32[]{:S(2)}) %collective-permute-start.34) | collective-permute-done | bytes 131104 | tf_op jit(solution)/shard_map/ppermute | solution.py:32
  128.6 2.6 %collective-permute-done.44 = bf16[768,256]{1,0:T(8,128)(2,1)S(1)} collective-permute-done((bf16[768,256]{1,0:T(8,128)(2,1)S(1)}, bf16[768,256]{1,0:T(8,128)(2,1)S(1)}, u32[]{:S(2)}, u32[]{:S(2)}) %collective-permute-start.44) | collective-permute-done | bytes 393248 | tf_op jit(solution)/shard_map/ppermute | solution.py:32
  131.4 1.6 %collective-permute-start.46 = (bf16[384,256]{1,0:T(8,128)(2,1)S(1)}, bf16[384,256]{1,0:T(8,128)(2,1)S(1)}, u32[]{:S(2)}, u32[]{:S(2)}) collective-permute-start(bf16[384,256]{1,0:T(8,128)(2,1)S(1)} %slice.72), channel_id=1, source_target_pairs={{0,2},{1,3},{2,0},{3,1},{4,6},{5,7},{6,4},{7,5},{8,10},{9,11},{10,... | collective-permute-start | bytes 589832 | tf_op jit(solution)/shard_map/ppermute | solution.py:32
  133.2 4.0 %collective-permute-done.46 = bf16[384,256]{1,0:T(8,128)(2,1)S(1)} collective-permute-done((bf16[384,256]{1,0:T(8,128)(2,1)S(1)}, bf16[384,256]{1,0:T(8,128)(2,1)S(1)}, u32[]{:S(2)}, u32[]{:S(2)}) %collective-permute-start.46) | collective-permute-done | bytes 196640 | tf_op jit(solution)/shard_map/ppermute | solution.py:32
  137.2 3.8 %collective-permute-start.47 = (bf16[384,256]{1,0:T(8,128)(2,1)S(1)}, bf16[384,256]{1,0:T(8,128)(2,1)S(1)}, u32[]{:S(2)}, u32[]{:S(2)}) collective-permute-start(bf16[384,256]{1,0:T(8,128)(2,1)S(1)} %fusion.1), channel_id=1, source_target_pairs={{0,4},{1,5},{2,6},{3,7},{4,0},{5,1},{6,2},{7,3},{8,12},{9,13},{10,... | collective-permute-start | bytes 589832 | tf_op jit(solution)/shard_map/ppermute | solution.py:32
  141.1 1.4 collective-permute-start.40
  142.5 4.5 %collective-permute-done.47 = bf16[384,256]{1,0:T(8,128)(2,1)S(1)} collective-permute-done((bf16[384,256]{1,0:T(8,128)(2,1)S(1)}, bf16[384,256]{1,0:T(8,128)(2,1)S(1)}, u32[]{:S(2)}, u32[]{:S(2)}) %collective-permute-start.47) | collective-permute-done | bytes 196640 | tf_op jit(solution)/shard_map/ppermute | solution.py:32
  150.3 3.8 %collective-permute-done.48.refs_9_ = bf16[384,256]{1,0:T(8,128)(2,1)S(1)} collective-permute-done((bf16[384,256]{1,0:T(8,128)(2,1)S(1)}, bf16[384,256]{1,0:T(8,128)(2,1)S(1)}, u32[]{:S(2)}, u32[]{:S(2)}) %collective-permute-start.48) | collective-permute-done | bytes 196640 | tf_op jit(solution)/shard_map/ppermute | solution.py:32
  154.2 1.4 collective-permute-done.35.refs_1_
  155.6 1.3 collective-permute-done.37.refs_3_
  156.9 2.8 %assemble.1 = (f32[4096,128]{1,0:T(8,128)}, f32[4096,128]{1,0:T(8,128)}) custom-call(s32[3]{0:T(128)S(1)} %pad_add_fusion.ids, bf16[256,256]{1,0:T(8,128)(2,1)S(1)} %add_convert_fusion.2.refs_0_, bf16[256,256]{1,0:T(8,128)(2,1)S(1)} %collective-permute-done.35.refs_1_, bf16[256,256]{1,0:T(8,128)(2,1)S(1)} %collective-permute-done.36.refs_2_, ...), custom_call_target="tpu_custom_call" | custom-call | tf_op jit(solution)/shard_map/assemble/pallas_call | solution.py:48
  (99 shorter events, 20.0 us)
Async XLA Ops:
  2.8 15.9 %collective-permute-start.4 = (bf16[1024,256]{1,0:T(8,128)(2,1)}, bf16[1024,256]{1,0:T(8,128)(2,1)S(1)}, u32[]{:S(2)}, u32[]{:S(2)}) collective-permute-start(bf16[1024,256]{1,0:T(8,128)(2,1)} %pad_maximum_fusion), channel_id=1, source_target_pairs={{0,16},{8,24},{16,0},{24,8},{1,17},{9,25},{17,1},{25,9},{2,18},{10... | collective-permute-start | bytes 1572872 | tf_op jit(solution)/shard_map/ppermute | solution.py:32
  5.7 15.4 %collective-permute-start = (bf16[1024,256]{1,0:T(8,128)(2,1)}, bf16[1024,256]{1,0:T(8,128)(2,1)S(1)}, u32[]{:S(2)}, u32[]{:S(2)}) collective-permute-start(bf16[1024,256]{1,0:T(8,128)(2,1)} %pad_maximum_fusion), channel_id=1, source_target_pairs={{0,8},{8,0},{16,24},{24,16},{1,9},{9,1},{17,25},{25,17},{2,10},{10... | collective-permute-start | bytes 1572872 | tf_op jit(solution)/shard_map/ppermute | solution.py:32
  8.1 21.9 %collective-permute-start.5 = (bf16[1024,256]{1,0:T(8,128)(2,1)}, bf16[1024,256]{1,0:T(8,128)(2,1)S(1)}, u32[]{:S(2)}, u32[]{:S(2)}) collective-permute-start(bf16[1024,256]{1,0:T(8,128)(2,1)} %pad_maximum_fusion.1), channel_id=1, source_target_pairs={{0,16},{8,24},{16,0},{24,8},{1,17},{9,25},{17,1},{25,9},{2,18},{10... | collective-permute-start | bytes 1572872 | tf_op jit(solution)/shard_map/ppermute | solution.py:32
  8.6 23.4 %collective-permute-start.1 = (bf16[1024,256]{1,0:T(8,128)(2,1)}, bf16[1024,256]{1,0:T(8,128)(2,1)S(1)}, u32[]{:S(2)}, u32[]{:S(2)}) collective-permute-start(bf16[1024,256]{1,0:T(8,128)(2,1)} %pad_maximum_fusion.1), channel_id=1, source_target_pairs={{0,8},{8,0},{16,24},{24,16},{1,9},{9,1},{17,25},{25,17},{2,10},{10... | collective-permute-start | bytes 1572872 | tf_op jit(solution)/shard_map/ppermute | solution.py:32
  18.7 13.3 %collective-permute-start.6 = (bf16[1024,256]{1,0:T(8,128)(2,1)S(1)}, bf16[1024,256]{1,0:T(8,128)(2,1)}, u32[]{:S(2)}, u32[]{:S(2)}) collective-permute-start(bf16[1024,256]{1,0:T(8,128)(2,1)S(1)} %collective-permute-done.4.refs_6_), channel_id=1, source_target_pairs={{0,1},{1,0},{2,3},{3,2},{4,5},{5,4},{6,7},{7,6},{8,9},{9,8},{10,11... | collective-permute-start | bytes 1572872 | tf_op jit(solution)/shard_map/ppermute | solution.py:32
  21.1 19.2 %collective-permute-start.8 = (bf16[1024,256]{1,0:T(8,128)(2,1)S(1)}, bf16[1024,256]{1,0:T(8,128)(2,1)S(1)}, u32[]{:S(2)}, u32[]{:S(2)}) collective-permute-start(bf16[1024,256]{1,0:T(8,128)(2,1)S(1)} %collective-permute-done.refs_2_), channel_id=1, source_target_pairs={{0,16},{8,24},{16,0},{24,8},{1,17},{9,25},{17,1},{25,9},{2,18},{10... | collective-permute-start | bytes 1572872 | tf_op jit(solution)/shard_map/ppermute | solution.py:32
  23.2 11.3 %collective-permute-start.2 = (bf16[1024,256]{1,0:T(8,128)(2,1)S(1)}, bf16[1024,256]{1,0:T(8,128)(2,1)S(1)}, u32[]{:S(2)}, u32[]{:S(2)}) collective-permute-start(bf16[1024,256]{1,0:T(8,128)(2,1)S(1)} %collective-permute-done.refs_2_), channel_id=1, source_target_pairs={{0,1},{1,0},{2,3},{3,2},{4,5},{5,4},{6,7},{7,6},{8,9},{9,8},{10,11... | collective-permute-start | bytes 1572872 | tf_op jit(solution)/shard_map/ppermute | solution.py:32
  29.9 12.3 %collective-permute-start.9 = (bf16[1024,256]{1,0:T(8,128)(2,1)S(1)}, bf16[1024,256]{1,0:T(8,128)(2,1)S(1)}, u32[]{:S(2)}, u32[]{:S(2)}) collective-permute-start(bf16[1024,256]{1,0:T(8,128)(2,1)S(1)} %collective-permute-done.5.refs_7_), channel_id=1, source_target_pairs={{0,8},{8,0},{16,24},{24,16},{1,9},{9,1},{17,25},{25,17},{2,10},{10... | collective-permute-start | bytes 1572872 | tf_op jit(solution)/shard_map/ppermute | solution.py:32
  32.0 2.6 %collective-permute-start.7 = (bf16[1024,256]{1,0:T(8,128)(2,1)S(1)}, bf16[1024,256]{1,0:T(8,128)(2,1)S(1)}, u32[]{:S(2)}, u32[]{:S(2)}) collective-permute-start(bf16[1024,256]{1,0:T(8,128)(2,1)S(1)} %collective-permute-done.5.refs_7_), channel_id=1, source_target_pairs={{0,1},{1,0},{2,3},{3,2},{4,5},{5,4},{6,7},{7,6},{8,9},{9,8},{10,11... | collective-permute-start | bytes 1572872 | tf_op jit(solution)/shard_map/ppermute | solution.py:32
  32.0 2.7 %collective-permute-start.3 = (bf16[1024,256]{1,0:T(8,128)(2,1)S(1)}, bf16[1024,256]{1,0:T(8,128)(2,1)S(1)}, u32[]{:S(2)}, u32[]{:S(2)}) collective-permute-start(bf16[1024,256]{1,0:T(8,128)(2,1)S(1)} %collective-permute-done.1.refs_3_), channel_id=1, source_target_pairs={{0,1},{1,0},{2,3},{3,2},{4,5},{5,4},{6,7},{7,6},{8,9},{9,8},{10,11... | collective-permute-start | bytes 1572872 | tf_op jit(solution)/shard_map/ppermute | solution.py:32
  42.2 3.5 %collective-permute-start.10 = (bf16[1024,256]{1,0:T(8,128)(2,1)S(1)}, bf16[1024,256]{1,0:T(8,128)(2,1)S(1)}, u32[]{:S(2)}, u32[]{:S(2)}) collective-permute-start(bf16[1024,256]{1,0:T(8,128)(2,1)S(1)} %collective-permute-done.8.refs_1_), channel_id=1, source_target_pairs={{0,1},{1,0},{2,3},{3,2},{4,5},{5,4},{6,7},{7,6},{8,9},{9,8},{10,11... | collective-permute-start | bytes 1572872 | tf_op jit(solution)/shard_map/ppermute | solution.py:32
  42.3 3.4 %collective-permute-start.11 = (bf16[1024,256]{1,0:T(8,128)(2,1)S(1)}, bf16[1024,256]{1,0:T(8,128)(2,1)S(1)}, u32[]{:S(2)}, u32[]{:S(2)}) collective-permute-start(bf16[1024,256]{1,0:T(8,128)(2,1)S(1)} %collective-permute-done.9.refs_2_), channel_id=1, source_target_pairs={{0,1},{1,0},{2,3},{3,2},{4,5},{5,4},{6,7},{7,6},{8,9},{9,8},{10,11... | collective-permute-start | bytes 1572872 | tf_op jit(solution)/shard_map/ppermute | solution.py:32
  42.8 29.5 %collective-permute-start.19 = (bf16[192,2560]{1,0:T(8,128)(2,1)S(1)}, bf16[192,2560]{1,0:T(8,128)(2,1)S(1)}, u32[]{:S(2)}, u32[]{:S(2)}) collective-permute-start(bf16[192,2560]{1,0:T(8,128)(2,1)S(1)} %get-tuple-element.56), channel_id=1, source_target_pairs={{0,8},{8,0},{16,24},{24,16},{1,9},{9,1},{17,25},{25,17},{2,10},{10... | collective-permute-start | bytes 2949128 | tf_op jit(solution)/shard_map/ppermute | solution.py:32
  44.2 28.1 %collective-permute-start.20 = (bf16[192,1536]{1,0:T(8,128)(2,1)S(1)}, bf16[192,1536]{1,0:T(8,128)(2,1)S(1)}, u32[]{:S(2)}, u32[]{:S(2)}) collective-permute-start(bf16[192,1536]{1,0:T(8,128)(2,1)S(1)} %dynamic-slice_bitcast_fusion.3), channel_id=1, source_target_pairs={{0,16},{8,24},{16,0},{24,8},{1,17},{9,25},{17,1},{25,9},{2,18},{10... | collective-permute-start | bytes 1769480 | tf_op jit(solution)/shard_map/ppermute | solution.py:32
  46.9 7.6 %collective-permute-start.14 = (bf16[192,256]{1,0:T(8,128)(2,1)S(1)}, bf16[192,256]{1,0:T(8,128)(2,1)S(1)}, u32[]{:S(2)}, u32[]{:S(2)}) collective-permute-start(bf16[192,256]{1,0:T(8,128)(2,1)S(1)} %project.3.refs_0_), channel_id=1, source_target_pairs={{0,6},{1,7},{2,4},{3,5},{4,2},{5,3},{6,0},{7,1},{8,14},{9,15},{10,... | collective-permute-start | bytes 294920 | tf_op jit(solution)/shard_map/ppermute | solution.py:32
  50.5 7.9 %collective-permute-start.13 = (bf16[192,256]{1,0:T(8,128)(2,1)S(1)}, bf16[192,256]{1,0:T(8,128)(2,1)S(1)}, u32[]{:S(2)}, u32[]{:S(2)}) collective-permute-start(bf16[192,256]{1,0:T(8,128)(2,1)S(1)} %project.3.refs_0_), channel_id=1, source_target_pairs={{0,4},{1,5},{2,6},{3,7},{4,0},{5,1},{6,2},{7,3},{8,12},{9,13},{10,... | collective-permute-start | bytes 294920 | tf_op jit(solution)/shard_map/ppermute | solution.py:32
  50.5 7.9 %collective-permute-start.12 = (bf16[192,256]{1,0:T(8,128)(2,1)S(1)}, bf16[192,256]{1,0:T(8,128)(2,1)S(1)}, u32[]{:S(2)}, u32[]{:S(2)}) collective-permute-start(bf16[192,256]{1,0:T(8,128)(2,1)S(1)} %project.3.refs_0_), channel_id=1, source_target_pairs={{0,2},{1,3},{2,0},{3,1},{4,6},{5,7},{6,4},{7,5},{8,10},{9,11},{10,... | collective-permute-start | bytes 294920 | tf_op jit(solution)/shard_map/ppermute | solution.py:32
  58.5 42.6 %collective-permute-start.29 = (bf16[192,2560]{1,0:T(8,128)(2,1)S(1)}, bf16[192,2560]{1,0:T(8,128)(2,1)S(1)}, u32[]{:S(2)}, u32[]{:S(2)}) collective-permute-start(bf16[192,2560]{1,0:T(8,128)(2,1)S(1)} %get-tuple-element.68), channel_id=1, source_target_pairs={{0,24},{8,16},{16,8},{24,0},{1,25},{9,17},{17,9},{25,1},{2,26},{10... | collective-permute-start | bytes 2949128 | tf_op jit(solution)/shard_map/ppermute | solution.py:32
  60.7 1.5 collective-permute-start.16
  72.3 1.7 %collective-permute-start.21 = (bf16[768,256]{1,0:T(8,128)(2,1)S(1)}, bf16[768,256]{1,0:T(8,128)(2,1)S(1)}, u32[]{:S(2)}, u32[]{:S(2)}) collective-permute-start(bf16[768,256]{1,0:T(8,128)(2,1)S(1)} %get-tuple-element.60), channel_id=1, source_target_pairs={{0,1},{1,0},{2,3},{3,2},{4,5},{5,4},{6,7},{7,6},{8,9},{9,8},{10,11... | collective-permute-start | bytes 1179656 | tf_op jit(solution)/shard_map/ppermute | solution.py:32
  72.7 26.4 %collective-permute-start.28 = (bf16[192,1024]{1,0:T(8,128)(2,1)S(1)}, bf16[192,1024]{1,0:T(8,128)(2,1)S(1)}, u32[]{:S(2)}, u32[]{:S(2)}) collective-permute-start(bf16[192,1024]{1,0:T(8,128)(2,1)S(1)} %dynamic-slice_bitcast_fusion.4), channel_id=1, source_target_pairs={{0,16},{8,24},{16,0},{24,8},{1,17},{9,25},{17,1},{25,9},{2,18},{10... | collective-permute-start | bytes 1179656 | tf_op jit(solution)/shard_map/ppermute | solution.py:32
  74.2 6.6 %collective-permute-start.22 = (bf16[192,256]{1,0:T(8,128)(2,1)S(1)}, bf16[192,256]{1,0:T(8,128)(2,1)S(1)}, u32[]{:S(2)}, u32[]{:S(2)}) collective-permute-start(bf16[192,256]{1,0:T(8,128)(2,1)S(1)} %get-tuple-element.62), channel_id=1, source_target_pairs={{0,2},{1,3},{2,0},{3,1},{4,6},{5,7},{6,4},{7,5},{8,10},{9,11},{10,... | collective-permute-start | bytes 294920 | tf_op jit(solution)/shard_map/ppermute | solution.py:32
  74.8 10.8 %collective-permute-start.23 = (bf16[192,256]{1,0:T(8,128)(2,1)S(1)}, bf16[192,256]{1,0:T(8,128)(2,1)S(1)}, u32[]{:S(2)}, u32[]{:S(2)}) collective-permute-start(bf16[192,256]{1,0:T(8,128)(2,1)S(1)} %get-tuple-element.63), channel_id=1, source_target_pairs={{0,4},{1,5},{2,6},{3,7},{4,0},{5,1},{6,2},{7,3},{8,12},{9,13},{10,... | collective-permute-start | bytes 294920 | tf_op jit(solution)/shard_map/ppermute | solution.py:32
  77.3 8.3 %collective-permute-start.24 = (bf16[192,256]{1,0:T(8,128)(2,1)S(1)}, bf16[192,256]{1,0:T(8,128)(2,1)S(1)}, u32[]{:S(2)}, u32[]{:S(2)}) collective-permute-start(bf16[192,256]{1,0:T(8,128)(2,1)S(1)} %get-tuple-element.64), channel_id=1, source_target_pairs={{0,6},{1,7},{2,4},{3,5},{4,2},{5,3},{6,0},{7,1},{8,14},{9,15},{10,... | collective-permute-start | bytes 294920 | tf_op jit(solution)/shard_map/ppermute | solution.py:32
  85.6 13.4 %collective-permute-start.27 = (bf16[192,256]{1,0:T(8,128)(2,1)S(1)}, bf16[192,256]{1,0:T(8,128)(2,1)S(1)}, u32[]{:S(2)}, u32[]{:S(2)}) collective-permute-start(bf16[192,256]{1,0:T(8,128)(2,1)S(1)} %total.1.refs_4_.refs_1_), channel_id=1, source_target_pairs={{0,24},{8,16},{16,8},{24,0},{1,25},{9,17},{17,9},{25,1},{2,26},{10... | collective-permute-start | bytes 294920 | tf_op jit(solution)/shard_map/ppermute | solution.py:32
  86.4 14.7 %collective-permute-start.26 = (bf16[192,256]{1,0:T(8,128)(2,1)S(1)}, bf16[192,256]{1,0:T(8,128)(2,1)S(1)}, u32[]{:S(2)}, u32[]{:S(2)}) collective-permute-start(bf16[192,256]{1,0:T(8,128)(2,1)S(1)} %total.1.refs_4_.refs_1_), channel_id=1, source_target_pairs={{0,16},{8,24},{16,0},{24,8},{1,17},{9,25},{17,1},{25,9},{2,18},{10... | collective-permute-start | bytes 294920 | tf_op jit(solution)/shard_map/ppermute | solution.py:32
  87.7 13.4 %collective-permute-start.25 = (bf16[192,256]{1,0:T(8,128)(2,1)S(1)}, bf16[192,256]{1,0:T(8,128)(2,1)S(1)}, u32[]{:S(2)}, u32[]{:S(2)}) collective-permute-start(bf16[192,256]{1,0:T(8,128)(2,1)S(1)} %total.1.refs_4_.refs_1_), channel_id=1, source_target_pairs={{0,8},{8,0},{16,24},{24,16},{1,9},{9,1},{17,25},{25,17},{2,10},{10... | collective-permute-start | bytes 294920 | tf_op jit(solution)/shard_map/ppermute | solution.py:32
  102.8 5.4 %collective-permute-start.32 = (bf16[3072,256]{1,0:T(8,128)(2,1)S(1)}, bf16[3072,256]{1,0:T(8,128)(2,1)S(1)}, u32[]{:S(2)}, u32[]{:S(2)}) collective-permute-start(bf16[3072,256]{1,0:T(8,128)(2,1)S(1)} %get-tuple-element.81), channel_id=1, source_target_pairs={{0,1},{1,0},{2,3},{3,2},{4,5},{5,4},{6,7},{7,6},{8,9},{9,8},{10,11... | collective-permute-start | bytes 4718600 | tf_op jit(solution)/shard_map/ppermute | solution.py:32
  104.2 2.4 %collective-permute-start.30 = (bf16[512,256]{1,0:T(8,128)(2,1)S(1)}, bf16[512,256]{1,0:T(8,128)(2,1)S(1)}, u32[]{:S(2)}, u32[]{:S(2)}) collective-permute-start(bf16[512,256]{1,0:T(8,128)(2,1)S(1)} %get-tuple-element.75), channel_id=1, source_target_pairs={{0,1},{1,0},{2,3},{3,2},{4,5},{5,4},{6,7},{7,6},{8,9},{9,8},{10,11... | collective-permute-start | bytes 786440 | tf_op jit(solution)/shard_map/ppermute | solution.py:32
  106.3 1.8 %collective-permute-start.31 = (bf16[768,256]{1,0:T(8,128)(2,1)S(1)}, bf16[768,256]{1,0:T(8,128)(2,1)S(1)}, u32[]{:S(2)}, u32[]{:S(2)}) collective-permute-start(bf16[768,256]{1,0:T(8,128)(2,1)S(1)} %get-tuple-element.78), channel_id=1, source_target_pairs={{0,1},{1,0},{2,3},{3,2},{4,5},{5,4},{6,7},{7,6},{8,9},{9,8},{10,11... | collective-permute-start | bytes 1179656 | tf_op jit(solution)/shard_map/ppermute | solution.py:32
  108.8 6.4 %collective-permute-start.33 = (bf16[256,256]{1,0:T(8,128)(2,1)S(1)}, bf16[256,256]{1,0:T(8,128)(2,1)S(1)}, u32[]{:S(2)}, u32[]{:S(2)}) collective-permute-start(bf16[256,256]{1,0:T(8,128)(2,1)S(1)} %slice.74), channel_id=1, source_target_pairs={{0,2},{1,3},{2,0},{3,1},{4,6},{5,7},{6,4},{7,5},{8,10},{9,11},{10,... | collective-permute-start | bytes 393224 | tf_op jit(solution)/shard_map/ppermute | solution.py:32
  110.5 9.9 %collective-permute-start.38 = (bf16[384,256]{1,0:T(8,128)(2,1)S(1)}, bf16[384,256]{1,0:T(8,128)(2,1)S(1)}, u32[]{:S(2)}, u32[]{:S(2)}) collective-permute-start(bf16[384,256]{1,0:T(8,128)(2,1)S(1)} %slice.73), channel_id=1, source_target_pairs={{0,2},{1,3},{2,0},{3,1},{4,6},{5,7},{6,4},{7,5},{8,10},{9,11},{10,... | collective-permute-start | bytes 589832 | tf_op jit(solution)/shard_map/ppermute | solution.py:32
  111.0 17.6 %collective-permute-start.43 = (bf16[768,256]{1,0:T(8,128)(2,1)S(1)}, bf16[768,256]{1,0:T(8,128)(2,1)S(1)}, u32[]{:S(2)}, u32[]{:S(2)}) collective-permute-start(bf16[768,256]{1,0:T(8,128)(2,1)S(1)} %get-tuple-element.85), channel_id=1, source_target_pairs={{0,8},{8,0},{16,24},{24,16},{1,9},{9,1},{17,25},{25,17},{2,10},{10... | collective-permute-start | bytes 1179656 | tf_op jit(solution)/shard_map/ppermute | solution.py:32
  112.5 18.7 %collective-permute-start.44 = (bf16[768,256]{1,0:T(8,128)(2,1)S(1)}, bf16[768,256]{1,0:T(8,128)(2,1)S(1)}, u32[]{:S(2)}, u32[]{:S(2)}) collective-permute-start(bf16[768,256]{1,0:T(8,128)(2,1)S(1)} %get-tuple-element.86), channel_id=1, source_target_pairs={{0,16},{8,24},{16,0},{24,8},{1,17},{9,25},{17,1},{25,9},{2,18},{10... | collective-permute-start | bytes 1179656 | tf_op jit(solution)/shard_map/ppermute | solution.py:32
  113.0 18.2 %collective-permute-start.45 = (bf16[768,256]{1,0:T(8,128)(2,1)S(1)}, bf16[768,256]{1,0:T(8,128)(2,1)S(1)}, u32[]{:S(2)}, u32[]{:S(2)}) collective-permute-start(bf16[768,256]{1,0:T(8,128)(2,1)S(1)} %get-tuple-element.87), channel_id=1, source_target_pairs={{0,24},{8,16},{16,8},{24,0},{1,25},{9,17},{17,9},{25,1},{2,26},{10... | collective-permute-start | bytes 1179656 | tf_op jit(solution)/shard_map/ppermute | solution.py:32
  115.2 13.3 %collective-permute-start.34 = (bf16[256,256]{1,0:T(8,128)(2,1)S(1)}, bf16[256,256]{1,0:T(8,128)(2,1)S(1)}, u32[]{:S(2)}, u32[]{:S(2)}) collective-permute-start(bf16[256,256]{1,0:T(8,128)(2,1)S(1)} %fusion.2), channel_id=1, source_target_pairs={{0,4},{1,5},{2,6},{3,7},{4,0},{5,1},{6,2},{7,3},{8,12},{9,13},{10,... | collective-permute-start | bytes 393224 | tf_op jit(solution)/shard_map/ppermute | solution.py:32
  120.4 12.7 %collective-permute-start.39 = (bf16[384,256]{1,0:T(8,128)(2,1)S(1)}, bf16[384,256]{1,0:T(8,128)(2,1)S(1)}, u32[]{:S(2)}, u32[]{:S(2)}) collective-permute-start(bf16[384,256]{1,0:T(8,128)(2,1)S(1)} %fusion), channel_id=1, source_target_pairs={{0,4},{1,5},{2,6},{3,7},{4,0},{5,1},{6,2},{7,3},{8,12},{9,13},{10,... | collective-permute-start | bytes 589832 | tf_op jit(solution)/shard_map/ppermute | solution.py:32
  131.4 5.7 %collective-permute-start.46 = (bf16[384,256]{1,0:T(8,128)(2,1)S(1)}, bf16[384,256]{1,0:T(8,128)(2,1)S(1)}, u32[]{:S(2)}, u32[]{:S(2)}) collective-permute-start(bf16[384,256]{1,0:T(8,128)(2,1)S(1)} %slice.72), channel_id=1, source_target_pairs={{0,2},{1,3},{2,0},{3,1},{4,6},{5,7},{6,4},{7,5},{8,10},{9,11},{10,... | collective-permute-start | bytes 589832 | tf_op jit(solution)/shard_map/ppermute | solution.py:32
  137.2 9.7 %collective-permute-start.47 = (bf16[384,256]{1,0:T(8,128)(2,1)S(1)}, bf16[384,256]{1,0:T(8,128)(2,1)S(1)}, u32[]{:S(2)}, u32[]{:S(2)}) collective-permute-start(bf16[384,256]{1,0:T(8,128)(2,1)S(1)} %fusion.1), channel_id=1, source_target_pairs={{0,4},{1,5},{2,6},{3,7},{4,0},{5,1},{6,2},{7,3},{8,12},{9,13},{10,... | collective-permute-start | bytes 589832 | tf_op jit(solution)/shard_map/ppermute | solution.py:32
  141.1 8.7 %collective-permute-start.40 = (bf16[384,256]{1,0:T(8,128)(2,1)S(1)}, bf16[384,256]{1,0:T(8,128)(2,1)S(1)}, u32[]{:S(2)}, u32[]{:S(2)}) collective-permute-start(bf16[384,256]{1,0:T(8,128)(2,1)S(1)} %add_convert_fusion.1.refs_4_), channel_id=1, source_target_pairs={{0,2},{1,3},{2,0},{3,1},{4,6},{5,7},{6,4},{7,5},{8,10},{9,11},{10,... | collective-permute-start | bytes 589832 | tf_op jit(solution)/shard_map/ppermute | solution.py:32
  147.0 7.1 %collective-permute-start.48 = (bf16[384,256]{1,0:T(8,128)(2,1)S(1)}, bf16[384,256]{1,0:T(8,128)(2,1)S(1)}, u32[]{:S(2)}, u32[]{:S(2)}) collective-permute-start(bf16[384,256]{1,0:T(8,128)(2,1)S(1)} %add_convert_fusion.refs_8_), channel_id=1, source_target_pairs={{0,2},{1,3},{2,0},{3,1},{4,6},{5,7},{6,4},{7,5},{8,10},{9,11},{10,... | collective-permute-start | bytes 589832 | tf_op jit(solution)/shard_map/ppermute | solution.py:32
  148.0 1.9 %collective-permute-start.36 = (bf16[256,256]{1,0:T(8,128)(2,1)S(1)}, bf16[256,256]{1,0:T(8,128)(2,1)S(1)}, u32[]{:S(2)}, u32[]{:S(2)}) collective-permute-start(bf16[256,256]{1,0:T(8,128)(2,1)S(1)} %add_convert_fusion.2.refs_0_), channel_id=1, source_target_pairs={{0,1},{1,0},{2,3},{3,2},{4,5},{5,4},{6,7},{7,6},{8,9},{9,8},{10,11... | collective-permute-start | bytes 393224 | tf_op jit(solution)/shard_map/ppermute | solution.py:32
  148.0 7.6 %collective-permute-start.35 = (bf16[256,256]{1,0:T(8,128)(2,1)S(1)}, bf16[256,256]{1,0:T(8,128)(2,1)S(1)}, u32[]{:S(2)}, u32[]{:S(2)}) collective-permute-start(bf16[256,256]{1,0:T(8,128)(2,1)S(1)} %add_convert_fusion.2.refs_0_), channel_id=1, source_target_pairs={{0,2},{1,3},{2,0},{3,1},{4,6},{5,7},{6,4},{7,5},{8,10},{9,11},{10,... | collective-permute-start | bytes 393224 | tf_op jit(solution)/shard_map/ppermute | solution.py:32
  149.1 7.8 %collective-permute-start.41 = (bf16[384,256]{1,0:T(8,128)(2,1)S(1)}, bf16[384,256]{1,0:T(8,128)(2,1)S(1)}, u32[]{:S(2)}, u32[]{:S(2)}) collective-permute-start(bf16[384,256]{1,0:T(8,128)(2,1)S(1)} %add_convert_fusion.1.refs_4_), channel_id=1, source_target_pairs={{0,1},{1,0},{2,3},{3,2},{4,5},{5,4},{6,7},{7,6},{8,9},{9,8},{10,11... | collective-permute-start | bytes 589832 | tf_op jit(solution)/shard_map/ppermute | solution.py:32
  149.8 7.1 %collective-permute-start.42 = (bf16[384,256]{1,0:T(8,128)(2,1)S(1)}, bf16[384,256]{1,0:T(8,128)(2,1)S(1)}, u32[]{:S(2)}, u32[]{:S(2)}) collective-permute-start(bf16[384,256]{1,0:T(8,128)(2,1)S(1)} %collective-permute-done.40.refs_5_), channel_id=1, source_target_pairs={{0,1},{1,0},{2,3},{3,2},{4,5},{5,4},{6,7},{7,6},{8,9},{9,8},{10,11... | collective-permute-start | bytes 589832 | tf_op jit(solution)/shard_map/ppermute | solution.py:32
  149.8 7.1 %collective-permute-start.49 = (bf16[384,256]{1,0:T(8,128)(2,1)S(1)}, bf16[384,256]{1,0:T(8,128)(2,1)S(1)}, u32[]{:S(2)}, u32[]{:S(2)}) collective-permute-start(bf16[384,256]{1,0:T(8,128)(2,1)S(1)} %add_convert_fusion.refs_8_), channel_id=1, source_target_pairs={{0,1},{1,0},{2,3},{3,2},{4,5},{5,4},{6,7},{7,6},{8,9},{9,8},{10,11... | collective-permute-start | bytes 589832 | tf_op jit(solution)/shard_map/ppermute | solution.py:32
  154.2 2.8 %collective-permute-start.50 = (bf16[384,256]{1,0:T(8,128)(2,1)S(1)}, bf16[384,256]{1,0:T(8,128)(2,1)S(1)}, u32[]{:S(2)}, u32[]{:S(2)}) collective-permute-start(bf16[384,256]{1,0:T(8,128)(2,1)S(1)} %collective-permute-done.48.refs_9_), channel_id=1, source_target_pairs={{0,1},{1,0},{2,3},{3,2},{4,5},{5,4},{6,7},{7,6},{8,9},{9,8},{10,11... | collective-permute-start | bytes 589832 | tf_op jit(solution)/shard_map/ppermute | solution.py:32
  155.6 1.3 collective-permute-start.37
  (10 other events, 146.9 us)

commit v10 on v8

--- a/solution.py
+++ b/solution.py
@@ -263,8 +263,8 @@
         for at, group in enumerate(plan.groups):
             for start in range(0, rows, tile):
                 product = None
-                for array, block, grad in group:
-                    origin = plan.origin + (core ^ side) * rows + start
+                for array, block, grad, shift in group:
+                    origin = plan.origin - shift + (core ^ side) * rows + start
                     if block is not None:
                         origin = origin + (dp ^ block) * plan.block_rows
                     columns = pl.ds(pl.multiple_of(origin, 128), tile)
@@ -299,7 +299,11 @@
         (ids,),
         (*hidden, *grads),
     )
-    return ours.astype(jnp.float32) + swap(theirs, "ctx", 1).astype(jnp.float32)
+    return ours, swap(theirs, "ctx", 1)
+
+
+def add_cores(ours, came):
+    return ours.astype(jnp.float32) + came.astype(jnp.float32)
 
 
 def parts_over_dp(array):
@@ -332,8 +336,9 @@
     return parts[0]
 
 
-def sum_of_halves(part, sub_count):
+def sum_of_halves(part, sub_count, earlier=()):
     low = swap(part.astype(jnp.bfloat16), "ctx", 2 * sub_count)
+    (low,), _ = after([low], *earlier)
     return (part + low.astype(jnp.float32)).astype(jnp.bfloat16)
 
 
@@ -442,9 +447,12 @@
     early, *tied = hold([early] + [moving[j] for j in others], far_pieces)
     moving.update(zip(others, tied))
     far_pieces.update(from_other_core(far_pieces))
+    tied = hold([moving[j] for j in near[:-1]], far_pieces)
+    moving.update(zip(near[:-1], tied))
     own = project(ids, (early,), inputs, block_rows, far_pieces, jnp.bfloat16)
     moved = {0: moving[0]}
-    moved.update({j: swap(moving[j], "dp", j) for j in near})
+    moved[near[-1]] = swap(moving[near[-1]], "dp", near[-1])
+    moved.update({j: swap(moving[j], "dp", j) for j in near[:-1]})
     along = gather_along_z(own)
     tied, _ = after([moving[j] for j in far], *along)
     moving.update(zip(far, tied))
@@ -456,22 +464,24 @@
     query_grad, keep, send = attention(
         me, stretch_order, doc_lengths[0], queries[0], grad_out[0], kv_blocks, head_dim
     )
-    (send,), ended = after([send], moved[near[0]])
+    (send,), ended = after([send], *[moved[j] for j in near])
     moved.update(zip(near, ended))
     own, *leaving = add_and_split(keep, swap(send, "ctx", 1), z_count)
     grad = add_all([own] + [swap(one, "ctx", 2 * m) for m, one in enumerate(leaving, 1)])
     grads = [grad] + [swap(grad, "dp", j) for j in range(1, dp_count)]
 
-    (grad,), ended = after([grad], *grads[1:], *[moved[j] for j in others])
+    (grad,), ended = after([grad], *grads[1:], *[moved[j] for j in far])
     grads[1:] = ended[: dp_count - 1]
-    moved.update(zip(others, ended[dp_count - 1 :]))
-    groups = [[(0, j, 0)] for j in range(dp_count)]
-    own = weight_rows(ids, [inputs], [grad], groups, *regions[-1], block_rows, sub_count)
-    own = parts_over_dp(own)
-    groups = [[(j, None, j) for j in range(dp_count)]]
+    moved.update(zip(far, ended[dp_count - 1 :]))
+    groups = [[(0, j, 0, 0)] for j in range(dp_count)]
+    ours, came = weight_rows(
+        ids, [inputs], [grad], groups, *regions[-1], block_rows, sub_count
+    )
+    own = parts_over_dp(add_cores(ours, came))
+    groups = [[(j, None, j, 0) for j in range(dp_count)]]
     arrays = [moved[j] for j in range(dp_count)]
     moved_parts = [
-        weight_rows(ids, arrays, grads, groups, *region, block_rows, sub_count)
+        add_cores(*weight_rows(ids, arrays, grads, groups, *region, block_rows, sub_count))
         for region in regions[:-1]
     ]
     moved_parts, own = after(moved_parts, *own)
@@ -481,8 +491,9 @@
         part = scatter_along_z(part, sub_count)
         finals.append(sum_of_halves(part, sub_count))
     part = scatter_along_z(sum_of(own), sub_count, finals[:TIED])
-    finals.append(sum_of_halves(part, sub_count))
-    blocks = [one for final in finals for one in gather_parts(final, sub_count)]
+    blocks = gather_parts(finals[0], sub_count)
+    finals.append(sum_of_halves(part, sub_count, blocks))
+    blocks += [one for final in finals[1:] for one in gather_parts(final, sub_count)]
     key_rows, value_rows = assemble(ids, blocks, sub_count, regions)
     return query_grad[None], key_rows, value_rows
 

time: 158 us -> 154 us (0.975)
  waiting for transfers between devices: 81.5 us -> 79.2 us
    ppermute x50, waiting for transfers between devices: 81.5 us -> 79.2 us  [swap(): return lax.ppermute(array, axis, [(i, i ^ distance) for i in range(count)])]
  transfers between devices with their start and end apart: 50 -> 50, of which waited for: 27 -> 28; matrix products, arithmetic and copies ran while one was open for 3% -> 3% of each run, Pallas kernels for 10% -> 11%
where the time goes in v10:
time: 154 us
  waiting for transfers between devices  79.2 us (51%)
  starting transfers between devices  44.7 us (29%)
  Pallas kernels  20.7 us (13%)
  local copies, waits for them, and re-layouts  5.55 us (4%)
  other arithmetic  2.93 us (2%)
    ppermute x50, waiting for transfers between devices, swap(): return lax.ppermute(array, axis, [(i, i ^ distance) for i in range(count)])  79.2 us
    ppermute x50, starting transfers between devices, swap(): return lax.ppermute(array, axis, [(i, i ^ distance) for i in range(count)])  44.7 us
    pallas_call x8, Pallas kernels, kernel_call(): pl.pallas_call(kernel, out_shape=outs, in_specs=[smem] * len(scalars) + [...  11.9 us
    pallas_call x1, Pallas kernels, attention(): pl.pallas_call(functools.partial(attention_kernel, shape), out_shape=(jax...  8.87 us
  transfers between devices with their start and end apart: 50, of which 28 were waited for; matrix products, arithmetic and copies ran while one was open for 3% of the time, Pallas kernels for 11%

profile of v10, /device:TPU:0, one launch (start us, length us, event | category | flops | bytes accessed | tf_op | source)
XLA Modules:
  0.0 154.0 jit_solution(8854878125105209690)
XLA Ops:
  0.7 1.4 constant_dynamic-slice_fusion
  2.9 3.0 %collective-permute-start.4 = (bf16[1024,256]{1,0:T(8,128)(2,1)}, bf16[1024,256]{1,0:T(8,128)(2,1)S(1)}, u32[]{:S(2)}, u32[]{:S(2)}) collective-permute-start(bf16[1024,256]{1,0:T(8,128)(2,1)} %pad_maximum_fusion), channel_id=1, source_target_pairs={{0,16},{8,24},{16,0},{24,8},{1,17},{9,25},{17,1},{25,9},{2,18},{10... | collective-permute-start | bytes 1572872 | tf_op jit(solution)/shard_map/ppermute | solution.py:32
  5.9 1.5 collective-permute-start
  8.8 10.1 %collective-permute-done.4.refs_6_ = bf16[1024,256]{1,0:T(8,128)(2,1)S(1)} collective-permute-done((bf16[1024,256]{1,0:T(8,128)(2,1)}, bf16[1024,256]{1,0:T(8,128)(2,1)S(1)}, u32[]{:S(2)}, u32[]{:S(2)}) %collective-permute-start.4) | collective-permute-done | bytes 524320 | tf_op jit(solution)/shard_map/ppermute | solution.py:32
  18.9 2.1 %collective-permute-done.refs_2_ = bf16[1024,256]{1,0:T(8,128)(2,1)S(1)} collective-permute-done((bf16[1024,256]{1,0:T(8,128)(2,1)}, bf16[1024,256]{1,0:T(8,128)(2,1)S(1)}, u32[]{:S(2)}, u32[]{:S(2)}) %collective-permute-start) | collective-permute-done | bytes 524320 | tf_op jit(solution)/shard_map/ppermute | solution.py:32
  21.2 9.0 %collective-permute-done.5.refs_7_ = bf16[1024,256]{1,0:T(8,128)(2,1)} collective-permute-done((bf16[1024,256]{1,0:T(8,128)(2,1)}, bf16[1024,256]{1,0:T(8,128)(2,1)}, u32[]{:S(2)}, u32[]{:S(2)}) %collective-permute-start.5) | collective-permute-done | bytes 524320 | tf_op jit(solution)/shard_map/ppermute | solution.py:32
  30.2 2.0 %collective-permute-start.9 = (bf16[1024,256]{1,0:T(8,128)(2,1)}, bf16[1024,256]{1,0:T(8,128)(2,1)S(1)}, u32[]{:S(2)}, u32[]{:S(2)}) collective-permute-start(bf16[1024,256]{1,0:T(8,128)(2,1)} %collective-permute-done.5.refs_7_), channel_id=1, source_target_pairs={{0,8},{8,0},{16,24},{24,16},{1,9},{9,1},{17,25},{25,17},{2,10},{10... | collective-permute-start | bytes 1572872 | tf_op jit(solution)/shard_map/ppermute | solution.py:32
  32.8 2.5 %dynamic-slice_bitcast_fusion = (bf16[192,2560]{1,0:T(8,128)(2,1)S(1)}, bf16[192,2560]{1,0:T(8,128)(2,1)S(1)}, bf16[192,2560]{1,0:T(8,128)(2,1)S(1)}, bf16[192,2560]{1,0:T(8,128)(2,1)S(1)}) fusion(bf16[1,192,16384]{2,1,0:T(8,128)(2,1)} %param.7, s32[]{:T(128)S(6)} %select_n.42, s32[]{:T(128)S(6)} %select_n.40, s32[]{:T(128)S(6)} %select_n.39, s32[]{:T(128)S(6)} %select_n.41), kind=kLoop, calls=%fused_computation.1 | loop fusion | bytes 7864336 | tf_op jit(solution)/shard_map/dynamic_slice | solution.py:436
  36.8 3.2 %project.2.refs_0_ = f32[192,256]{1,0:T(8,128)S(1)} custom-call(s32[3]{0:T(128)S(1)} %pad_add_fusion.ids, bf16[192,16384]{1,0:T(8,128)(2,1)S(1)} %bitcast.19, bf16[4096,128]{1,0:T(8,128)(2,1)S(1)} %copy-done, bf16[4096,128]{1,0:T(8,128)(2,1)S(1)} %copy-done.1, bf16[1024,256]{1,0:T(8,128)(2,1)S(1)} %collective-permute-done.refs_2_, ...), custom_call_target="tpu_custom_call" | custom-call | bytes 16777216 | tf_op jit(solution)/shard_map/project/pallas_call | solution.py:48
  40.5 2.2 %collective-permute-done.9.refs_2_ = bf16[1024,256]{1,0:T(8,128)(2,1)S(1)} collective-permute-done((bf16[1024,256]{1,0:T(8,128)(2,1)}, bf16[1024,256]{1,0:T(8,128)(2,1)S(1)}, u32[]{:S(2)}, u32[]{:S(2)}) %collective-permute-start.9) | collective-permute-done | bytes 524320 | tf_op jit(solution)/shard_map/ppermute | solution.py:32
  43.3 1.4 collective-permute-start.20
  45.4 1.4 collective-permute-start.19
  48.0 3.7 %collective-permute-start.14 = (bf16[192,256]{1,0:T(8,128)(2,1)S(1)}, bf16[192,256]{1,0:T(8,128)(2,1)S(1)}, u32[]{:S(2)}, u32[]{:S(2)}) collective-permute-start(bf16[192,256]{1,0:T(8,128)(2,1)S(1)} %project.3.refs_0_), channel_id=1, source_target_pairs={{0,6},{1,7},{2,4},{3,5},{4,2},{5,3},{6,0},{7,1},{8,14},{9,15},{10,... | collective-permute-start | bytes 294920 | tf_op jit(solution)/shard_map/ppermute | solution.py:32
  52.4 2.9 %collective-permute-done.14.refs_6_ = bf16[192,256]{1,0:T(8,128)(2,1)S(1)} collective-permute-done((bf16[192,256]{1,0:T(8,128)(2,1)S(1)}, bf16[192,256]{1,0:T(8,128)(2,1)S(1)}, u32[]{:S(2)}, u32[]{:S(2)}) %collective-permute-start.14) | collective-permute-done | bytes 98336 | tf_op jit(solution)/shard_map/ppermute | solution.py:32
  55.4 4.6 %collective-permute-done.13.refs_4_ = bf16[192,256]{1,0:T(8,128)(2,1)S(1)} collective-permute-done((bf16[192,256]{1,0:T(8,128)(2,1)S(1)}, bf16[192,256]{1,0:T(8,128)(2,1)S(1)}, u32[]{:S(2)}, u32[]{:S(2)}) %collective-permute-start.13) | collective-permute-done | bytes 98336 | tf_op jit(solution)/shard_map/ppermute | solution.py:32
  59.9 1.5 collective-permute-start.28
  64.2 8.9 %attention.1 = (bf16[192,1024]{1,0:T(8,128)(2,1)}, f32[768,256]{1,0:T(8,128)S(1)}, bf16[768,256]{1,0:T(8,128)(2,1)S(1)}) custom-call(s32[1]{0:T(128)} %bitcast.ids, s32[16]{0:T(128)S(1)} %copy-done.4, s32[8]{0:T(128)S(1)} %bitcast.24, bf16[192,1024]{1,0:T(8,128)(2,1)S(1)} %bitcast.22, bf16[192,1024]{1,0:T(8,128)(2,1)S(1)} %bitcast.23, ...), custom_call_target="tpu_custom_call" | custom-call | tf_op jit(solution)/shard_map/attention/pallas_call | solution.py:169
  73.5 1.4 collective-permute-done.21.came
  75.5 2.6 %collective-permute-start.23 = (bf16[192,256]{1,0:T(8,128)(2,1)S(1)}, bf16[192,256]{1,0:T(8,128)(2,1)S(1)}, u32[]{:S(2)}, u32[]{:S(2)}) collective-permute-start(bf16[192,256]{1,0:T(8,128)(2,1)S(1)} %get-tuple-element.72), channel_id=1, source_target_pairs={{0,4},{1,5},{2,6},{3,7},{4,0},{5,1},{6,2},{7,3},{8,12},{9,13},{10,... | collective-permute-start | bytes 294920 | tf_op jit(solution)/shard_map/ppermute | solution.py:32
  78.1 1.3 collective-permute-start.24
  79.4 2.2 %collective-permute-done.22.refs_1_ = bf16[192,256]{1,0:T(8,128)(2,1)S(1)} collective-permute-done((bf16[192,256]{1,0:T(8,128)(2,1)S(1)}, bf16[192,256]{1,0:T(8,128)(2,1)S(1)}, u32[]{:S(2)}, u32[]{:S(2)}) %collective-permute-start.22) | collective-permute-done | bytes 98336 | tf_op jit(solution)/shard_map/ppermute | solution.py:32
  81.5 4.8 %collective-permute-done.23.refs_2_ = bf16[192,256]{1,0:T(8,128)(2,1)S(1)} collective-permute-done((bf16[192,256]{1,0:T(8,128)(2,1)S(1)}, bf16[192,256]{1,0:T(8,128)(2,1)S(1)}, u32[]{:S(2)}, u32[]{:S(2)}) %collective-permute-start.23) | collective-permute-done | bytes 98336 | tf_op jit(solution)/shard_map/ppermute | solution.py:32
  86.4 1.5 collective-permute-start.27
  87.9 1.5 collective-permute-start.26
  89.9 2.1 %collective-permute-done.28.refs_3_ = bf16[192,2560]{1,0:T(8,128)(2,1)S(1)} collective-permute-done((bf16[192,2560]{1,0:T(8,128)(2,1)S(1)}, bf16[192,2560]{1,0:T(8,128)(2,1)S(1)}, u32[]{:S(2)}, u32[]{:S(2)}) %collective-permute-start.28) | collective-permute-done | bytes 983072 | tf_op jit(solution)/shard_map/ppermute | solution.py:32
  92.1 2.1 %collective-permute-done.27.refs_7_ = bf16[192,256]{1,0:T(8,128)(2,1)S(1)} collective-permute-done((bf16[192,256]{1,0:T(8,128)(2,1)S(1)}, bf16[192,256]{1,0:T(8,128)(2,1)S(1)}, u32[]{:S(2)}, u32[]{:S(2)}) %collective-permute-start.27) | collective-permute-done | bytes 98336 | tf_op jit(solution)/shard_map/ppermute | solution.py:32
  94.1 1.3 collective-permute-done.26.refs_6_
  95.4 1.7 %weight_rows.5 = (bf16[3072,256]{1,0:T(8,128)(2,1)S(1)}, bf16[3072,256]{1,0:T(8,128)(2,1)S(1)}) custom-call(s32[3]{0:T(128)S(1)} %pad_add_fusion.ids, bf16[192,16384]{1,0:T(8,128)(2,1)S(1)} %bitcast.21, bf16[192,256]{1,0:T(8,128)(2,1)S(1)} %total.1.refs_4_.refs_1_), custom_call_target="tpu_custom_call" | custom-call | tf_op jit(solution)/shard_map/weight_rows/pallas_call | solution.py:48
  97.1 1.3 weight_rows.3
  99.0 1.6 %weight_rows.4 = (bf16[768,256]{1,0:T(8,128)(2,1)S(1)}, bf16[768,256]{1,0:T(8,128)(2,1)S(1)}) custom-call(s32[3]{0:T(128)S(1)} %pad_add_fusion.ids, bf16[192,2560]{1,0:T(8,128)(2,1)S(1)} %get-tuple-element.97.refs_0_, bf16[192,2560]{1,0:T(8,128)(2,1)S(1)} %collective-permute-done.19.refs_1_, bf16[192,2560]{1,0:T(8,128)(2,1)S(1)} %collective-permute-done.20.refs_2_, ...), custom_call_target="tpu_custom_call" | custom-call | tf_op jit(solution)/shard_map/weight_rows/pallas_call | solution.py:48
  101.0 1.4 collective-permute-done.30
  103.2 1.6 %collective-permute-start.32 = (bf16[256,256]{1,0:T(8,128)(2,1)S(1)}, bf16[256,256]{1,0:T(8,128)(2,1)S(1)}, u32[]{:S(2)}, u32[]{:S(2)}) collective-permute-start(bf16[256,256]{1,0:T(8,128)(2,1)S(1)} %slice.74), channel_id=1, source_target_pairs={{0,2},{1,3},{2,0},{3,1},{4,6},{5,7},{6,4},{7,5},{8,10},{9,11},{10,... | collective-permute-start | bytes 393224 | tf_op jit(solution)/shard_map/ppermute | solution.py:32
  105.4 1.5 collective-permute-start.42
  107.4 1.4 collective-permute-start.44
  109.6 2.7 %collective-permute-start.33 = (bf16[256,256]{1,0:T(8,128)(2,1)S(1)}, bf16[256,256]{1,0:T(8,128)(2,1)S(1)}, u32[]{:S(2)}, u32[]{:S(2)}) collective-permute-start(bf16[256,256]{1,0:T(8,128)(2,1)S(1)} %fusion.2), channel_id=1, source_target_pairs={{0,4},{1,5},{2,6},{3,7},{4,0},{5,1},{6,2},{7,3},{8,12},{9,13},{10,... | collective-permute-start | bytes 393224 | tf_op jit(solution)/shard_map/ppermute | solution.py:32
  112.3 2.5 %collective-permute-done.37 = bf16[384,256]{1,0:T(8,128)(2,1)S(1)} collective-permute-done((bf16[384,256]{1,0:T(8,128)(2,1)S(1)}, bf16[384,256]{1,0:T(8,128)(2,1)S(1)}, u32[]{:S(2)}, u32[]{:S(2)}) %collective-permute-start.37) | collective-permute-done | bytes 196640 | tf_op jit(solution)/shard_map/ppermute | solution.py:32
  114.8 1.7 %collective-permute-start.38 = (bf16[384,256]{1,0:T(8,128)(2,1)S(1)}, bf16[384,256]{1,0:T(8,128)(2,1)S(1)}, u32[]{:S(2)}, u32[]{:S(2)}) collective-permute-start(bf16[384,256]{1,0:T(8,128)(2,1)S(1)} %fusion), channel_id=1, source_target_pairs={{0,4},{1,5},{2,6},{3,7},{4,0},{5,1},{6,2},{7,3},{8,12},{9,13},{10,... | collective-permute-start | bytes 589832 | tf_op jit(solution)/shard_map/ppermute | solution.py:32
  116.5 6.4 %collective-permute-done.33 = bf16[256,256]{1,0:T(8,128)(2,1)S(1)} collective-permute-done((bf16[256,256]{1,0:T(8,128)(2,1)S(1)}, bf16[256,256]{1,0:T(8,128)(2,1)S(1)}, u32[]{:S(2)}, u32[]{:S(2)}) %collective-permute-start.33) | collective-permute-done | bytes 131104 | tf_op jit(solution)/shard_map/ppermute | solution.py:32
  123.7 2.0 %collective-permute-done.43 = bf16[768,256]{1,0:T(8,128)(2,1)S(1)} collective-permute-done((bf16[768,256]{1,0:T(8,128)(2,1)S(1)}, bf16[768,256]{1,0:T(8,128)(2,1)S(1)}, u32[]{:S(2)}, u32[]{:S(2)}) %collective-permute-start.43) | collective-permute-done | bytes 393248 | tf_op jit(solution)/shard_map/ppermute | solution.py:32
  125.8 1.6 %collective-permute-start.45 = (bf16[384,256]{1,0:T(8,128)(2,1)S(1)}, bf16[384,256]{1,0:T(8,128)(2,1)S(1)}, u32[]{:S(2)}, u32[]{:S(2)}) collective-permute-start(bf16[384,256]{1,0:T(8,128)(2,1)S(1)} %slice.72), channel_id=1, source_target_pairs={{0,2},{1,3},{2,0},{3,1},{4,6},{5,7},{6,4},{7,5},{8,10},{9,11},{10,... | collective-permute-start | bytes 589832 | tf_op jit(solution)/shard_map/ppermute | solution.py:32
  127.5 4.9 %collective-permute-done.45 = bf16[384,256]{1,0:T(8,128)(2,1)S(1)} collective-permute-done((bf16[384,256]{1,0:T(8,128)(2,1)S(1)}, bf16[384,256]{1,0:T(8,128)(2,1)S(1)}, u32[]{:S(2)}, u32[]{:S(2)}) %collective-permute-start.45) | collective-permute-done | bytes 196640 | tf_op jit(solution)/shard_map/ppermute | solution.py:32
  132.4 1.9 %collective-permute-start.46 = (bf16[384,256]{1,0:T(8,128)(2,1)S(1)}, bf16[384,256]{1,0:T(8,128)(2,1)S(1)}, u32[]{:S(2)}, u32[]{:S(2)}) collective-permute-start(bf16[384,256]{1,0:T(8,128)(2,1)S(1)} %fusion.1), channel_id=1, source_target_pairs={{0,4},{1,5},{2,6},{3,7},{4,0},{5,1},{6,2},{7,3},{8,12},{9,13},{10,... | collective-permute-start | bytes 589832 | tf_op jit(solution)/shard_map/ppermute | solution.py:32
  134.9 2.0 %collective-permute-start.39 = (bf16[384,256]{1,0:T(8,128)(2,1)S(1)}, bf16[384,256]{1,0:T(8,128)(2,1)S(1)}, u32[]{:S(2)}, u32[]{:S(2)}) collective-permute-start(bf16[384,256]{1,0:T(8,128)(2,1)S(1)} %add_convert_fusion.1.refs_4_), channel_id=1, source_target_pairs={{0,2},{1,3},{2,0},{3,1},{4,6},{5,7},{6,4},{7,5},{8,10},{9,11},{10,... | collective-permute-start | bytes 589832 | tf_op jit(solution)/shard_map/ppermute | solution.py:32
  137.0 6.2 %collective-permute-done.46 = bf16[384,256]{1,0:T(8,128)(2,1)S(1)} collective-permute-done((bf16[384,256]{1,0:T(8,128)(2,1)S(1)}, bf16[384,256]{1,0:T(8,128)(2,1)S(1)}, u32[]{:S(2)}, u32[]{:S(2)}) %collective-permute-start.46) | collective-permute-done | bytes 196640 | tf_op jit(solution)/shard_map/ppermute | solution.py:32
  143.4 2.4 %collective-permute-done.39.refs_5_ = bf16[384,256]{1,0:T(8,128)(2,1)S(1)} collective-permute-done((bf16[384,256]{1,0:T(8,128)(2,1)S(1)}, bf16[384,256]{1,0:T(8,128)(2,1)S(1)}, u32[]{:S(2)}, u32[]{:S(2)}) %collective-permute-start.39) | collective-permute-done | bytes 196640 | tf_op jit(solution)/shard_map/ppermute | solution.py:32
  146.3 3.4 %collective-permute-done.47.refs_9_ = bf16[384,256]{1,0:T(8,128)(2,1)S(1)} collective-permute-done((bf16[384,256]{1,0:T(8,128)(2,1)S(1)}, bf16[384,256]{1,0:T(8,128)(2,1)S(1)}, u32[]{:S(2)}, u32[]{:S(2)}) %collective-permute-start.47) | collective-permute-done | bytes 196640 | tf_op jit(solution)/shard_map/ppermute | solution.py:32
  149.8 1.4 collective-permute-done.49.refs_11_
  151.2 2.8 %assemble.1 = (f32[4096,128]{1,0:T(8,128)}, f32[4096,128]{1,0:T(8,128)}) custom-call(s32[3]{0:T(128)S(1)} %pad_add_fusion.ids, bf16[256,256]{1,0:T(8,128)(2,1)S(1)} %add_convert_fusion.2.refs_0_, bf16[256,256]{1,0:T(8,128)(2,1)S(1)} %collective-permute-done.34.refs_1_, bf16[256,256]{1,0:T(8,128)(2,1)S(1)} %collective-permute-done.35.refs_2_, ...), custom_call_target="tpu_custom_call" | custom-call | tf_op jit(solution)/shard_map/assemble/pallas_call | solution.py:48
  (98 shorter events, 18.6 us)
Async XLA Ops:
  2.9 15.9 %collective-permute-start.4 = (bf16[1024,256]{1,0:T(8,128)(2,1)}, bf16[1024,256]{1,0:T(8,128)(2,1)S(1)}, u32[]{:S(2)}, u32[]{:S(2)}) collective-permute-start(bf16[1024,256]{1,0:T(8,128)(2,1)} %pad_maximum_fusion), channel_id=1, source_target_pairs={{0,16},{8,24},{16,0},{24,8},{1,17},{9,25},{17,1},{25,9},{2,18},{10... | collective-permute-start | bytes 1572872 | tf_op jit(solution)/shard_map/ppermute | solution.py:32
  5.9 15.1 %collective-permute-start = (bf16[1024,256]{1,0:T(8,128)(2,1)}, bf16[1024,256]{1,0:T(8,128)(2,1)S(1)}, u32[]{:S(2)}, u32[]{:S(2)}) collective-permute-start(bf16[1024,256]{1,0:T(8,128)(2,1)} %pad_maximum_fusion), channel_id=1, source_target_pairs={{0,8},{8,0},{16,24},{24,16},{1,9},{9,1},{17,25},{25,17},{2,10},{10... | collective-permute-start | bytes 1572872 | tf_op jit(solution)/shard_map/ppermute | solution.py:32
  8.2 22.0 %collective-permute-start.5 = (bf16[1024,256]{1,0:T(8,128)(2,1)}, bf16[1024,256]{1,0:T(8,128)(2,1)}, u32[]{:S(2)}, u32[]{:S(2)}) collective-permute-start(bf16[1024,256]{1,0:T(8,128)(2,1)} %pad_maximum_fusion.1), channel_id=1, source_target_pairs={{0,16},{8,24},{16,0},{24,8},{1,17},{9,25},{17,1},{25,9},{2,18},{10... | collective-permute-start | bytes 1572872 | tf_op jit(solution)/shard_map/ppermute | solution.py:32
  8.7 23.5 %collective-permute-start.1 = (bf16[1024,256]{1,0:T(8,128)(2,1)}, bf16[1024,256]{1,0:T(8,128)(2,1)}, u32[]{:S(2)}, u32[]{:S(2)}) collective-permute-start(bf16[1024,256]{1,0:T(8,128)(2,1)} %pad_maximum_fusion.1), channel_id=1, source_target_pairs={{0,8},{8,0},{16,24},{24,16},{1,9},{9,1},{17,25},{25,17},{2,10},{10... | collective-permute-start | bytes 1572872 | tf_op jit(solution)/shard_map/ppermute | solution.py:32
  18.9 13.4 %collective-permute-start.6 = (bf16[1024,256]{1,0:T(8,128)(2,1)S(1)}, bf16[1024,256]{1,0:T(8,128)(2,1)}, u32[]{:S(2)}, u32[]{:S(2)}) collective-permute-start(bf16[1024,256]{1,0:T(8,128)(2,1)S(1)} %collective-permute-done.4.refs_6_), channel_id=1, source_target_pairs={{0,1},{1,0},{2,3},{3,2},{4,5},{5,4},{6,7},{7,6},{8,9},{9,8},{10,11... | collective-permute-start | bytes 1572872 | tf_op jit(solution)/shard_map/ppermute | solution.py:32
  21.0 19.5 %collective-permute-start.8 = (bf16[1024,256]{1,0:T(8,128)(2,1)S(1)}, bf16[1024,256]{1,0:T(8,128)(2,1)S(1)}, u32[]{:S(2)}, u32[]{:S(2)}) collective-permute-start(bf16[1024,256]{1,0:T(8,128)(2,1)S(1)} %collective-permute-done.refs_2_), channel_id=1, source_target_pairs={{0,16},{8,24},{16,0},{24,8},{1,17},{9,25},{17,1},{25,9},{2,18},{10... | collective-permute-start | bytes 1572872 | tf_op jit(solution)/shard_map/ppermute | solution.py:32
  21.0 14.4 %collective-permute-start.2 = (bf16[1024,256]{1,0:T(8,128)(2,1)S(1)}, bf16[1024,256]{1,0:T(8,128)(2,1)S(1)}, u32[]{:S(2)}, u32[]{:S(2)}) collective-permute-start(bf16[1024,256]{1,0:T(8,128)(2,1)S(1)} %collective-permute-done.refs_2_), channel_id=1, source_target_pairs={{0,1},{1,0},{2,3},{3,2},{4,5},{5,4},{6,7},{7,6},{8,9},{9,8},{10,11... | collective-permute-start | bytes 1572872 | tf_op jit(solution)/shard_map/ppermute | solution.py:32
  30.2 12.5 %collective-permute-start.9 = (bf16[1024,256]{1,0:T(8,128)(2,1)}, bf16[1024,256]{1,0:T(8,128)(2,1)S(1)}, u32[]{:S(2)}, u32[]{:S(2)}) collective-permute-start(bf16[1024,256]{1,0:T(8,128)(2,1)} %collective-permute-done.5.refs_7_), channel_id=1, source_target_pairs={{0,8},{8,0},{16,24},{24,16},{1,9},{9,1},{17,25},{25,17},{2,10},{10... | collective-permute-start | bytes 1572872 | tf_op jit(solution)/shard_map/ppermute | solution.py:32
  32.2 3.1 %collective-permute-start.7 = (bf16[1024,256]{1,0:T(8,128)(2,1)}, bf16[1024,256]{1,0:T(8,128)(2,1)S(1)}, u32[]{:S(2)}, u32[]{:S(2)}) collective-permute-start(bf16[1024,256]{1,0:T(8,128)(2,1)} %collective-permute-done.5.refs_7_), channel_id=1, source_target_pairs={{0,1},{1,0},{2,3},{3,2},{4,5},{5,4},{6,7},{7,6},{8,9},{9,8},{10,11... | collective-permute-start | bytes 1572872 | tf_op jit(solution)/shard_map/ppermute | solution.py:32
  32.2 3.1 %collective-permute-start.3 = (bf16[1024,256]{1,0:T(8,128)(2,1)}, bf16[1024,256]{1,0:T(8,128)(2,1)S(1)}, u32[]{:S(2)}, u32[]{:S(2)}) collective-permute-start(bf16[1024,256]{1,0:T(8,128)(2,1)} %collective-permute-done.1.refs_3_), channel_id=1, source_target_pairs={{0,1},{1,0},{2,3},{3,2},{4,5},{5,4},{6,7},{7,6},{8,9},{9,8},{10,11... | collective-permute-start | bytes 1572872 | tf_op jit(solution)/shard_map/ppermute | solution.py:32
  42.7 2.0 %collective-permute-start.10 = (bf16[1024,256]{1,0:T(8,128)(2,1)S(1)}, bf16[1024,256]{1,0:T(8,128)(2,1)S(1)}, u32[]{:S(2)}, u32[]{:S(2)}) collective-permute-start(bf16[1024,256]{1,0:T(8,128)(2,1)S(1)} %collective-permute-done.8.refs_1_), channel_id=1, source_target_pairs={{0,1},{1,0},{2,3},{3,2},{4,5},{5,4},{6,7},{7,6},{8,9},{9,8},{10,11... | collective-permute-start | bytes 1572872 | tf_op jit(solution)/shard_map/ppermute | solution.py:32
  42.8 2.6 %collective-permute-start.11 = (bf16[1024,256]{1,0:T(8,128)(2,1)S(1)}, bf16[1024,256]{1,0:T(8,128)(2,1)S(1)}, u32[]{:S(2)}, u32[]{:S(2)}) collective-permute-start(bf16[1024,256]{1,0:T(8,128)(2,1)S(1)} %collective-permute-done.9.refs_2_), channel_id=1, source_target_pairs={{0,1},{1,0},{2,3},{3,2},{4,5},{5,4},{6,7},{7,6},{8,9},{9,8},{10,11... | collective-permute-start | bytes 1572872 | tf_op jit(solution)/shard_map/ppermute | solution.py:32
  43.3 29.8 %collective-permute-start.20 = (bf16[192,2560]{1,0:T(8,128)(2,1)S(1)}, bf16[192,2560]{1,0:T(8,128)(2,1)S(1)}, u32[]{:S(2)}, u32[]{:S(2)}) collective-permute-start(bf16[192,2560]{1,0:T(8,128)(2,1)S(1)} %get-tuple-element.65), channel_id=1, source_target_pairs={{0,16},{8,24},{16,0},{24,8},{1,17},{9,25},{17,1},{25,9},{2,18},{10... | collective-permute-start | bytes 2949128 | tf_op jit(solution)/shard_map/ppermute | solution.py:32
  45.4 27.7 %collective-permute-start.19 = (bf16[192,2560]{1,0:T(8,128)(2,1)S(1)}, bf16[192,2560]{1,0:T(8,128)(2,1)S(1)}, u32[]{:S(2)}, u32[]{:S(2)}) collective-permute-start(bf16[192,2560]{1,0:T(8,128)(2,1)S(1)} %get-tuple-element.64), channel_id=1, source_target_pairs={{0,8},{8,0},{16,24},{24,16},{1,9},{9,1},{17,25},{25,17},{2,10},{10... | collective-permute-start | bytes 2949128 | tf_op jit(solution)/shard_map/ppermute | solution.py:32
  48.0 7.4 %collective-permute-start.14 = (bf16[192,256]{1,0:T(8,128)(2,1)S(1)}, bf16[192,256]{1,0:T(8,128)(2,1)S(1)}, u32[]{:S(2)}, u32[]{:S(2)}) collective-permute-start(bf16[192,256]{1,0:T(8,128)(2,1)S(1)} %project.3.refs_0_), channel_id=1, source_target_pairs={{0,6},{1,7},{2,4},{3,5},{4,2},{5,3},{6,0},{7,1},{8,14},{9,15},{10,... | collective-permute-start | bytes 294920 | tf_op jit(solution)/shard_map/ppermute | solution.py:32
  51.6 8.3 %collective-permute-start.13 = (bf16[192,256]{1,0:T(8,128)(2,1)S(1)}, bf16[192,256]{1,0:T(8,128)(2,1)S(1)}, u32[]{:S(2)}, u32[]{:S(2)}) collective-permute-start(bf16[192,256]{1,0:T(8,128)(2,1)S(1)} %project.3.refs_0_), channel_id=1, source_target_pairs={{0,4},{1,5},{2,6},{3,7},{4,0},{5,1},{6,2},{7,3},{8,12},{9,13},{10,... | collective-permute-start | bytes 294920 | tf_op jit(solution)/shard_map/ppermute | solution.py:32
  51.6 8.3 %collective-permute-start.12 = (bf16[192,256]{1,0:T(8,128)(2,1)S(1)}, bf16[192,256]{1,0:T(8,128)(2,1)S(1)}, u32[]{:S(2)}, u32[]{:S(2)}) collective-permute-start(bf16[192,256]{1,0:T(8,128)(2,1)S(1)} %project.3.refs_0_), channel_id=1, source_target_pairs={{0,2},{1,3},{2,0},{3,1},{4,6},{5,7},{6,4},{7,5},{8,10},{9,11},{10,... | collective-permute-start | bytes 294920 | tf_op jit(solution)/shard_map/ppermute | solution.py:32
  59.9 32.1 %collective-permute-start.28 = (bf16[192,2560]{1,0:T(8,128)(2,1)S(1)}, bf16[192,2560]{1,0:T(8,128)(2,1)S(1)}, u32[]{:S(2)}, u32[]{:S(2)}) collective-permute-start(bf16[192,2560]{1,0:T(8,128)(2,1)S(1)} %get-tuple-element.75), channel_id=1, source_target_pairs={{0,24},{8,16},{16,8},{24,0},{1,25},{9,17},{17,9},{25,1},{2,26},{10... | collective-permute-start | bytes 2949128 | tf_op jit(solution)/shard_map/ppermute | solution.py:32
  61.4 1.5 collective-permute-start.16
  62.9 1.3 collective-permute-start.18
  73.1 1.7 %collective-permute-start.21 = (bf16[768,256]{1,0:T(8,128)(2,1)S(1)}, bf16[768,256]{1,0:T(8,128)(2,1)S(1)}, u32[]{:S(2)}, u32[]{:S(2)}) collective-permute-start(bf16[768,256]{1,0:T(8,128)(2,1)S(1)} %get-tuple-element.69), channel_id=1, source_target_pairs={{0,1},{1,0},{2,3},{3,2},{4,5},{5,4},{6,7},{7,6},{8,9},{9,8},{10,11... | collective-permute-start | bytes 1179656 | tf_op jit(solution)/shard_map/ppermute | solution.py:32
  74.9 6.6 %collective-permute-start.22 = (bf16[192,256]{1,0:T(8,128)(2,1)S(1)}, bf16[192,256]{1,0:T(8,128)(2,1)S(1)}, u32[]{:S(2)}, u32[]{:S(2)}) collective-permute-start(bf16[192,256]{1,0:T(8,128)(2,1)S(1)} %get-tuple-element.71), channel_id=1, source_target_pairs={{0,2},{1,3},{2,0},{3,1},{4,6},{5,7},{6,4},{7,5},{8,10},{9,11},{10,... | collective-permute-start | bytes 294920 | tf_op jit(solution)/shard_map/ppermute | solution.py:32
  75.5 10.8 %collective-permute-start.23 = (bf16[192,256]{1,0:T(8,128)(2,1)S(1)}, bf16[192,256]{1,0:T(8,128)(2,1)S(1)}, u32[]{:S(2)}, u32[]{:S(2)}) collective-permute-start(bf16[192,256]{1,0:T(8,128)(2,1)S(1)} %get-tuple-element.72), channel_id=1, source_target_pairs={{0,4},{1,5},{2,6},{3,7},{4,0},{5,1},{6,2},{7,3},{8,12},{9,13},{10,... | collective-permute-start | bytes 294920 | tf_op jit(solution)/shard_map/ppermute | solution.py:32
  78.1 8.2 %collective-permute-start.24 = (bf16[192,256]{1,0:T(8,128)(2,1)S(1)}, bf16[192,256]{1,0:T(8,128)(2,1)S(1)}, u32[]{:S(2)}, u32[]{:S(2)}) collective-permute-start(bf16[192,256]{1,0:T(8,128)(2,1)S(1)} %get-tuple-element.73), channel_id=1, source_target_pairs={{0,6},{1,7},{2,4},{3,5},{4,2},{5,3},{6,0},{7,1},{8,14},{9,15},{10,... | collective-permute-start | bytes 294920 | tf_op jit(solution)/shard_map/ppermute | solution.py:32
  86.4 7.7 %collective-permute-start.27 = (bf16[192,256]{1,0:T(8,128)(2,1)S(1)}, bf16[192,256]{1,0:T(8,128)(2,1)S(1)}, u32[]{:S(2)}, u32[]{:S(2)}) collective-permute-start(bf16[192,256]{1,0:T(8,128)(2,1)S(1)} %total.1.refs_4_.refs_1_), channel_id=1, source_target_pairs={{0,24},{8,16},{16,8},{24,0},{1,25},{9,17},{17,9},{25,1},{2,26},{10... | collective-permute-start | bytes 294920 | tf_op jit(solution)/shard_map/ppermute | solution.py:32
  87.9 7.5 %collective-permute-start.26 = (bf16[192,256]{1,0:T(8,128)(2,1)S(1)}, bf16[192,256]{1,0:T(8,128)(2,1)S(1)}, u32[]{:S(2)}, u32[]{:S(2)}) collective-permute-start(bf16[192,256]{1,0:T(8,128)(2,1)S(1)} %total.1.refs_4_.refs_1_), channel_id=1, source_target_pairs={{0,16},{8,24},{16,0},{24,8},{1,17},{9,25},{17,1},{25,9},{2,18},{10... | collective-permute-start | bytes 294920 | tf_op jit(solution)/shard_map/ppermute | solution.py:32
  89.4 6.0 %collective-permute-start.25 = (bf16[192,256]{1,0:T(8,128)(2,1)S(1)}, bf16[192,256]{1,0:T(8,128)(2,1)S(1)}, u32[]{:S(2)}, u32[]{:S(2)}) collective-permute-start(bf16[192,256]{1,0:T(8,128)(2,1)S(1)} %total.1.refs_4_.refs_1_), channel_id=1, source_target_pairs={{0,8},{8,0},{16,24},{24,16},{1,9},{9,1},{17,25},{25,17},{2,10},{10... | collective-permute-start | bytes 294920 | tf_op jit(solution)/shard_map/ppermute | solution.py:32
  97.0 5.4 %collective-permute-start.31 = (bf16[3072,256]{1,0:T(8,128)(2,1)S(1)}, bf16[3072,256]{1,0:T(8,128)(2,1)S(1)}, u32[]{:S(2)}, u32[]{:S(2)}) collective-permute-start(bf16[3072,256]{1,0:T(8,128)(2,1)S(1)} %get-tuple-element.86), channel_id=1, source_target_pairs={{0,1},{1,0},{2,3},{3,2},{4,5},{5,4},{6,7},{7,6},{8,9},{9,8},{10,11... | collective-permute-start | bytes 4718600 | tf_op jit(solution)/shard_map/ppermute | solution.py:32
  98.4 2.4 %collective-permute-start.29 = (bf16[512,256]{1,0:T(8,128)(2,1)S(1)}, bf16[512,256]{1,0:T(8,128)(2,1)S(1)}, u32[]{:S(2)}, u32[]{:S(2)}) collective-permute-start(bf16[512,256]{1,0:T(8,128)(2,1)S(1)} %get-tuple-element.81), channel_id=1, source_target_pairs={{0,1},{1,0},{2,3},{3,2},{4,5},{5,4},{6,7},{7,6},{8,9},{9,8},{10,11... | collective-permute-start | bytes 786440 | tf_op jit(solution)/shard_map/ppermute | solution.py:32
  100.6 1.8 %collective-permute-start.30 = (bf16[768,256]{1,0:T(8,128)(2,1)S(1)}, bf16[768,256]{1,0:T(8,128)(2,1)S(1)}, u32[]{:S(2)}, u32[]{:S(2)}) collective-permute-start(bf16[768,256]{1,0:T(8,128)(2,1)S(1)} %get-tuple-element.83), channel_id=1, source_target_pairs={{0,1},{1,0},{2,3},{3,2},{4,5},{5,4},{6,7},{7,6},{8,9},{9,8},{10,11... | collective-permute-start | bytes 1179656 | tf_op jit(solution)/shard_map/ppermute | solution.py:32
  103.2 6.4 %collective-permute-start.32 = (bf16[256,256]{1,0:T(8,128)(2,1)S(1)}, bf16[256,256]{1,0:T(8,128)(2,1)S(1)}, u32[]{:S(2)}, u32[]{:S(2)}) collective-permute-start(bf16[256,256]{1,0:T(8,128)(2,1)S(1)} %slice.74), channel_id=1, source_target_pairs={{0,2},{1,3},{2,0},{3,1},{4,6},{5,7},{6,4},{7,5},{8,10},{9,11},{10,... | collective-permute-start | bytes 393224 | tf_op jit(solution)/shard_map/ppermute | solution.py:32
  104.8 9.9 %collective-permute-start.37 = (bf16[384,256]{1,0:T(8,128)(2,1)S(1)}, bf16[384,256]{1,0:T(8,128)(2,1)S(1)}, u32[]{:S(2)}, u32[]{:S(2)}) collective-permute-start(bf16[384,256]{1,0:T(8,128)(2,1)S(1)} %slice.73), channel_id=1, source_target_pairs={{0,2},{1,3},{2,0},{3,1},{4,6},{5,7},{6,4},{7,5},{8,10},{9,11},{10,... | collective-permute-start | bytes 589832 | tf_op jit(solution)/shard_map/ppermute | solution.py:32
  105.4 18.3 %collective-permute-start.42 = (bf16[768,256]{1,0:T(8,128)(2,1)S(1)}, bf16[768,256]{1,0:T(8,128)(2,1)S(1)}, u32[]{:S(2)}, u32[]{:S(2)}) collective-permute-start(bf16[768,256]{1,0:T(8,128)(2,1)S(1)} %get-tuple-element.90), channel_id=1, source_target_pairs={{0,8},{8,0},{16,24},{24,16},{1,9},{9,1},{17,25},{25,17},{2,10},{10... | collective-permute-start | bytes 1179656 | tf_op jit(solution)/shard_map/ppermute | solution.py:32
  106.8 18.8 %collective-permute-start.43 = (bf16[768,256]{1,0:T(8,128)(2,1)S(1)}, bf16[768,256]{1,0:T(8,128)(2,1)S(1)}, u32[]{:S(2)}, u32[]{:S(2)}) collective-permute-start(bf16[768,256]{1,0:T(8,128)(2,1)S(1)} %get-tuple-element.91), channel_id=1, source_target_pairs={{0,16},{8,24},{16,0},{24,8},{1,17},{9,25},{17,1},{25,9},{2,18},{10... | collective-permute-start | bytes 1179656 | tf_op jit(solution)/shard_map/ppermute | solution.py:32
  107.4 18.2 %collective-permute-start.44 = (bf16[768,256]{1,0:T(8,128)(2,1)S(1)}, bf16[768,256]{1,0:T(8,128)(2,1)S(1)}, u32[]{:S(2)}, u32[]{:S(2)}) collective-permute-start(bf16[768,256]{1,0:T(8,128)(2,1)S(1)} %get-tuple-element.92), channel_id=1, source_target_pairs={{0,24},{8,16},{16,8},{24,0},{1,25},{9,17},{17,9},{25,1},{2,26},{10... | collective-permute-start | bytes 1179656 | tf_op jit(solution)/shard_map/ppermute | solution.py:32
  109.6 13.3 %collective-permute-start.33 = (bf16[256,256]{1,0:T(8,128)(2,1)S(1)}, bf16[256,256]{1,0:T(8,128)(2,1)S(1)}, u32[]{:S(2)}, u32[]{:S(2)}) collective-permute-start(bf16[256,256]{1,0:T(8,128)(2,1)S(1)} %fusion.2), channel_id=1, source_target_pairs={{0,4},{1,5},{2,6},{3,7},{4,0},{5,1},{6,2},{7,3},{8,12},{9,13},{10,... | collective-permute-start | bytes 393224 | tf_op jit(solution)/shard_map/ppermute | solution.py:32
  114.8 12.7 %collective-permute-start.38 = (bf16[384,256]{1,0:T(8,128)(2,1)S(1)}, bf16[384,256]{1,0:T(8,128)(2,1)S(1)}, u32[]{:S(2)}, u32[]{:S(2)}) collective-permute-start(bf16[384,256]{1,0:T(8,128)(2,1)S(1)} %fusion), channel_id=1, source_target_pairs={{0,4},{1,5},{2,6},{3,7},{4,0},{5,1},{6,2},{7,3},{8,12},{9,13},{10,... | collective-permute-start | bytes 589832 | tf_op jit(solution)/shard_map/ppermute | solution.py:32
  123.0 11.4 %collective-permute-start.34 = (bf16[256,256]{1,0:T(8,128)(2,1)S(1)}, bf16[256,256]{1,0:T(8,128)(2,1)S(1)}, u32[]{:S(2)}, u32[]{:S(2)}) collective-permute-start(bf16[256,256]{1,0:T(8,128)(2,1)S(1)} %add_convert_fusion.2.refs_0_), channel_id=1, source_target_pairs={{0,2},{1,3},{2,0},{3,1},{4,6},{5,7},{6,4},{7,5},{8,10},{9,11},{10,... | collective-permute-start | bytes 393224 | tf_op jit(solution)/shard_map/ppermute | solution.py:32
  125.8 6.6 %collective-permute-start.45 = (bf16[384,256]{1,0:T(8,128)(2,1)S(1)}, bf16[384,256]{1,0:T(8,128)(2,1)S(1)}, u32[]{:S(2)}, u32[]{:S(2)}) collective-permute-start(bf16[384,256]{1,0:T(8,128)(2,1)S(1)} %slice.72), channel_id=1, source_target_pairs={{0,2},{1,3},{2,0},{3,1},{4,6},{5,7},{6,4},{7,5},{8,10},{9,11},{10,... | collective-permute-start | bytes 589832 | tf_op jit(solution)/shard_map/ppermute | solution.py:32
  132.4 10.7 %collective-permute-start.46 = (bf16[384,256]{1,0:T(8,128)(2,1)S(1)}, bf16[384,256]{1,0:T(8,128)(2,1)S(1)}, u32[]{:S(2)}, u32[]{:S(2)}) collective-permute-start(bf16[384,256]{1,0:T(8,128)(2,1)S(1)} %fusion.1), channel_id=1, source_target_pairs={{0,4},{1,5},{2,6},{3,7},{4,0},{5,1},{6,2},{7,3},{8,12},{9,13},{10,... | collective-permute-start | bytes 589832 | tf_op jit(solution)/shard_map/ppermute | solution.py:32
  134.4 2.6 %collective-permute-start.35 = (bf16[256,256]{1,0:T(8,128)(2,1)S(1)}, bf16[256,256]{1,0:T(8,128)(2,1)S(1)}, u32[]{:S(2)}, u32[]{:S(2)}) collective-permute-start(bf16[256,256]{1,0:T(8,128)(2,1)S(1)} %add_convert_fusion.2.refs_0_), channel_id=1, source_target_pairs={{0,1},{1,0},{2,3},{3,2},{4,5},{5,4},{6,7},{7,6},{8,9},{9,8},{10,11... | collective-permute-start | bytes 393224 | tf_op jit(solution)/shard_map/ppermute | solution.py:32
  134.4 2.6 %collective-permute-start.36 = (bf16[256,256]{1,0:T(8,128)(2,1)S(1)}, bf16[256,256]{1,0:T(8,128)(2,1)S(1)}, u32[]{:S(2)}, u32[]{:S(2)}) collective-permute-start(bf16[256,256]{1,0:T(8,128)(2,1)S(1)} %collective-permute-done.34.refs_1_), channel_id=1, source_target_pairs={{0,1},{1,0},{2,3},{3,2},{4,5},{5,4},{6,7},{7,6},{8,9},{9,8},{10,11... | collective-permute-start | bytes 393224 | tf_op jit(solution)/shard_map/ppermute | solution.py:32
  134.9 10.9 %collective-permute-start.39 = (bf16[384,256]{1,0:T(8,128)(2,1)S(1)}, bf16[384,256]{1,0:T(8,128)(2,1)S(1)}, u32[]{:S(2)}, u32[]{:S(2)}) collective-permute-start(bf16[384,256]{1,0:T(8,128)(2,1)S(1)} %add_convert_fusion.1.refs_4_), channel_id=1, source_target_pairs={{0,2},{1,3},{2,0},{3,1},{4,6},{5,7},{6,4},{7,5},{8,10},{9,11},{10,... | collective-permute-start | bytes 589832 | tf_op jit(solution)/shard_map/ppermute | solution.py:32
  143.2 6.5 %collective-permute-start.47 = (bf16[384,256]{1,0:T(8,128)(2,1)S(1)}, bf16[384,256]{1,0:T(8,128)(2,1)S(1)}, u32[]{:S(2)}, u32[]{:S(2)}) collective-permute-start(bf16[384,256]{1,0:T(8,128)(2,1)S(1)} %add_convert_fusion.refs_8_), channel_id=1, source_target_pairs={{0,2},{1,3},{2,0},{3,1},{4,6},{5,7},{6,4},{7,5},{8,10},{9,11},{10,... | collective-permute-start | bytes 589832 | tf_op jit(solution)/shard_map/ppermute | solution.py:32
  143.3 6.4 %collective-permute-start.40 = (bf16[384,256]{1,0:T(8,128)(2,1)S(1)}, bf16[384,256]{1,0:T(8,128)(2,1)S(1)}, u32[]{:S(2)}, u32[]{:S(2)}) collective-permute-start(bf16[384,256]{1,0:T(8,128)(2,1)S(1)} %add_convert_fusion.1.refs_4_), channel_id=1, source_target_pairs={{0,1},{1,0},{2,3},{3,2},{4,5},{5,4},{6,7},{7,6},{8,9},{9,8},{10,11... | collective-permute-start | bytes 589832 | tf_op jit(solution)/shard_map/ppermute | solution.py:32
  145.8 3.9 %collective-permute-start.41 = (bf16[384,256]{1,0:T(8,128)(2,1)S(1)}, bf16[384,256]{1,0:T(8,128)(2,1)S(1)}, u32[]{:S(2)}, u32[]{:S(2)}) collective-permute-start(bf16[384,256]{1,0:T(8,128)(2,1)S(1)} %collective-permute-done.39.refs_5_), channel_id=1, source_target_pairs={{0,1},{1,0},{2,3},{3,2},{4,5},{5,4},{6,7},{7,6},{8,9},{9,8},{10,11... | collective-permute-start | bytes 589832 | tf_op jit(solution)/shard_map/ppermute | solution.py:32
  145.8 3.9 %collective-permute-start.48 = (bf16[384,256]{1,0:T(8,128)(2,1)S(1)}, bf16[384,256]{1,0:T(8,128)(2,1)S(1)}, u32[]{:S(2)}, u32[]{:S(2)}) collective-permute-start(bf16[384,256]{1,0:T(8,128)(2,1)S(1)} %add_convert_fusion.refs_8_), channel_id=1, source_target_pairs={{0,1},{1,0},{2,3},{3,2},{4,5},{5,4},{6,7},{7,6},{8,9},{9,8},{10,11... | collective-permute-start | bytes 589832 | tf_op jit(solution)/shard_map/ppermute | solution.py:32
  149.7 1.4 collective-permute-start.49
  (10 other events, 134.3 us)

commit v11 on v10

--- a/solution.py
+++ b/solution.py
@@ -342,18 +342,22 @@
     return (part + low.astype(jnp.float32)).astype(jnp.bfloat16)
 
 
-def gather_parts(part, sub_count):
+def gather_parts(part, sub_count, earlier=()):
     rows = {0: part}
     for bit in z_bits(sub_count)[::-1]:
-        rows.update({m | bit: swap(one, "ctx", 2 * bit) for m, one in list(rows.items())})
+        for m, one in list(rows.items()):
+            (rows[m | bit],), _ = after([swap(one, "ctx", 2 * bit)], *earlier)
     own = [rows[m] for m in range(sub_count)]
     return own + [swap(one, "ctx", 1) for one in own]
 
 
-def assemble_kernel(sub_count, regions, ids, *refs):
-    key_ref, value_ref = refs[-2:]
-    blocks = iter(refs[:-2])
+def assemble_kernel(sub_count, regions, first, ids, *refs):
+    count = 2 * sub_count * len(regions)
+    blocks = iter(refs[2 * (not first) :][:count])
+    *outs, buffer, sems = refs[2 * (not first) + count :]
     z, core = ids[0] % sub_count, ids[1]
+    copies = []
+    filled = 0
     for origin, rows in regions:
         share = rows // sub_count
         for side in range(2):
@@ -362,20 +366,42 @@
                 to = pl.multiple_of(to, share)
                 block_ref = next(blocks)
                 width = block_ref.shape[1] // 2
-                key_ref[pl.ds(to, share), :] = block_ref[:, :width].astype(jnp.float32)
-                value_ref[pl.ds(to, share), :] = block_ref[:, width:].astype(jnp.float32)
-
-
-def assemble(ids, blocks, sub_count, regions):
+                for which, out_ref in enumerate(outs):
+                    piece = buffer.at[which, pl.ds(filled, share), :]
+                    piece[...] = block_ref[:, which * width : (which + 1) * width].astype(
+                        jnp.float32
+                    )
+                    copy = pltpu.make_async_copy(
+                        piece, out_ref.at[pl.ds(to, share), :], sems.at[len(copies)]
+                    )
+                    copy.start()
+                    copies.append(copy)
+                filled += share
+    for copy in copies:
+        copy.wait()
+
+
+def assemble(ids, before, blocks, sub_count, regions, block_rows):
     rows = sum(block.shape[0] for block in blocks)
-    out = shape_of(rows, blocks[0].shape[1] // 2, jnp.float32)
-    return kernel_call(
-        functools.partial(assemble_kernel, sub_count, regions),
-        "assemble",
-        (out, out),
-        (ids,),
-        blocks,
-    )
+    width = blocks[0].shape[1] // 2
+    out = shape_of(block_rows, width, jnp.float32)
+    smem = pl.BlockSpec(memory_space=pltpu.SMEM)
+    vmem = pl.BlockSpec(memory_space=pltpu.VMEM)
+    anywhere = pl.BlockSpec(memory_space=pl.ANY)
+    return pl.pallas_call(
+        functools.partial(assemble_kernel, sub_count, regions, not before),
+        out_shape=(out, out),
+        in_specs=[smem] + [anywhere] * len(before) + [vmem] * len(blocks),
+        out_specs=(anywhere, anywhere),
+        scratch_shapes=[
+            pltpu.VMEM((2, rows, width), jnp.float32),
+            pltpu.SemaphoreType.DMA((2 * len(blocks),)),
+        ],
+        input_output_aliases={1: 0, 2: 1} if before else {},
+        compiler_params=pltpu.CompilerParams(vmem_limit_bytes=VMEM_LIMIT),
+        cost_estimate=NO_COST,
+        name="assemble",
+    )(ids, *before, *blocks)
 
 
 def on_device(hidden_in, queries, grad_out, w_key, w_value, stretch_order, doc_lengths):
@@ -439,7 +465,14 @@
 
     near_pieces = gather_near(w_key, w_value)
     far_pieces = gather_far(near_pieces)
-    near_pieces.update(from_other_core(near_pieces))
+    names = list(near_pieces)
+    waiting, _ = after([near_pieces[name] for name in names[: len(near)]])
+    others = {}
+    for name, one in zip(names, waiting):
+        (one,), _ = after([one], *others.values())
+        others.update(from_other_core({name: one}))
+    others.update(from_other_core({name: near_pieces[name] for name in names[len(near) :]}))
+    near_pieces.update(others)
     early = project(
         ids, (w_key, w_value), inputs, block_rows, near_pieces, jnp.float32, bytes_cost(1 << 24)
     )
@@ -492,9 +525,11 @@
         finals.append(sum_of_halves(part, sub_count))
     part = scatter_along_z(sum_of(own), sub_count, finals[:TIED])
     blocks = gather_parts(finals[0], sub_count)
-    finals.append(sum_of_halves(part, sub_count, blocks))
+    last = sum_of_halves(part, sub_count, blocks)
     blocks += [one for final in finals[1:] for one in gather_parts(final, sub_count)]
-    key_rows, value_rows = assemble(ids, blocks, sub_count, regions)
+    outs = assemble(ids, (), blocks, sub_count, regions[:-1], block_rows)
+    last = gather_parts(last, sub_count, outs)
+    key_rows, value_rows = assemble(ids, outs, last, sub_count, regions[-1:], block_rows)
     return query_grad[None], key_rows, value_rows
 
 

time: 154 us -> 153 us (level)
  starting transfers between devices: 44.7 us -> 42.3 us
    pallas_call x0 -> x2, Pallas kernels: none -> 3.92 us  [assemble(): pl.pallas_call(functools.partial(assemble_kernel, sub_count, regions, not...]
    pallas_call x8 -> x7, Pallas kernels: 11.9 us -> 9.06 us  [kernel_call(): pl.pallas_call(kernel, out_shape=outs, in_specs=[smem] * len(scalars) + [...]
    ppermute x50, starting transfers between devices: 44.7 us -> 42.3 us  [swap(): return lax.ppermute(array, axis, [(i, i ^ distance) for i in range(count)])]
  transfers between devices with their start and end apart: 50 -> 50, of which waited for: 28 -> 29; matrix products, arithmetic and copies ran while one was open for 3% -> 3% of each run, Pallas kernels for 11% -> 12%
where the time goes in v11:
time: 153 us
  waiting for transfers between devices  79.9 us (52%)
  starting transfers between devices  42.3 us (28%)
  Pallas kernels  21.9 us (14%)
  local copies, waits for them, and re-layouts  5.14 us (3%)
  other arithmetic  2.92 us (2%)
    ppermute x50, waiting for transfers between devices, swap(): return lax.ppermute(array, axis, [(i, i ^ distance) for i in range(count)])  79.9 us
    ppermute x50, starting transfers between devices, swap(): return lax.ppermute(array, axis, [(i, i ^ distance) for i in range(count)])  42.3 us
    pallas_call x7, Pallas kernels, kernel_call(): pl.pallas_call(kernel, out_shape=outs, in_specs=[smem] * len(scalars) + [...  9.06 us
    pallas_call x1, Pallas kernels, attention(): pl.pallas_call(functools.partial(attention_kernel, shape), out_shape=(jax...  8.88 us
    pallas_call x2, Pallas kernels, assemble(): pl.pallas_call(functools.partial(assemble_kernel, sub_count, regions, not...  3.92 us
  transfers between devices with their start and end apart: 50, of which 29 were waited for; matrix products, arithmetic and copies ran while one was open for 3% of the time, Pallas kernels for 12%

profile of v11, /device:TPU:0, one launch (start us, length us, event | category | flops | bytes accessed | tf_op | source)
XLA Modules:
  0.0 153.2 jit_solution(14934094122295338759)
XLA Ops:
  0.7 1.4 constant_dynamic-slice_fusion
  2.1 0.9 pad_maximum_fusion
  2.9 2.9 %collective-permute-start = (bf16[1024,256]{1,0:T(8,128)(2,1)}, bf16[1024,256]{1,0:T(8,128)(2,1)S(1)}, u32[]{:S(2)}, u32[]{:S(2)}) collective-permute-start(bf16[1024,256]{1,0:T(8,128)(2,1)} %pad_maximum_fusion), channel_id=1, source_target_pairs={{0,8},{8,0},{16,24},{24,16},{1,9},{9,1},{17,25},{25,17},{2,10},{10... | collective-permute-start | bytes 1572872 | tf_op jit(solution)/shard_map/ppermute | solution.py:32
  6.7 1.5 collective-permute-start.2
  8.8 10.0 %collective-permute-done.refs_2_ = bf16[1024,256]{1,0:T(8,128)(2,1)S(1)} collective-permute-done((bf16[1024,256]{1,0:T(8,128)(2,1)}, bf16[1024,256]{1,0:T(8,128)(2,1)S(1)}, u32[]{:S(2)}, u32[]{:S(2)}) %collective-permute-start) | collective-permute-done | bytes 524320 | tf_op jit(solution)/shard_map/ppermute | solution.py:32
  18.8 3.0 %collective-permute-done.2.refs_7_ = bf16[1024,256]{1,0:T(8,128)(2,1)S(1)} collective-permute-done((bf16[1024,256]{1,0:T(8,128)(2,1)}, bf16[1024,256]{1,0:T(8,128)(2,1)S(1)}, u32[]{:S(2)}, u32[]{:S(2)}) %collective-permute-start.2) | collective-permute-done | bytes 524320 | tf_op jit(solution)/shard_map/ppermute | solution.py:32
  21.8 1.5 collective-permute-start.8
  23.8 9.3 %collective-permute-done.5.refs_6_ = bf16[1024,256]{1,0:T(8,128)(2,1)} collective-permute-done((bf16[1024,256]{1,0:T(8,128)(2,1)}, bf16[1024,256]{1,0:T(8,128)(2,1)}, u32[]{:S(2)}, u32[]{:S(2)}) %collective-permute-start.5) | collective-permute-done | bytes 524320 | tf_op jit(solution)/shard_map/ppermute | solution.py:32
  33.8 2.5 %dynamic-slice_bitcast_fusion = (bf16[192,2560]{1,0:T(8,128)(2,1)S(1)}, bf16[192,2560]{1,0:T(8,128)(2,1)S(1)}, bf16[192,2560]{1,0:T(8,128)(2,1)S(1)}, bf16[192,2560]{1,0:T(8,128)(2,1)S(1)}) fusion(bf16[1,192,16384]{2,1,0:T(8,128)(2,1)} %param.7, s32[]{:T(128)S(6)} %select_n.42, s32[]{:T(128)S(6)} %select_n.40, s32[]{:T(128)S(6)} %select_n.39, s32[]{:T(128)S(6)} %select_n.41), kind=kLoop, calls=%fused_computation.1 | loop fusion | bytes 7864336 | tf_op jit(solution)/shard_map/dynamic_slice | solution.py:462
  37.8 3.2 %project.2.refs_0_ = f32[192,256]{1,0:T(8,128)S(1)} custom-call(s32[3]{0:T(128)S(1)} %pad_add_fusion.ids, bf16[192,16384]{1,0:T(8,128)(2,1)S(1)} %bitcast.19, bf16[4096,128]{1,0:T(8,128)(2,1)S(1)} %copy-done, bf16[4096,128]{1,0:T(8,128)(2,1)S(1)} %copy-done.1, bf16[1024,256]{1,0:T(8,128)(2,1)S(1)} %collective-permute-done.refs_2_, ...), custom_call_target="tpu_custom_call" | custom-call | bytes 16777216 | tf_op jit(solution)/shard_map/project/pallas_call | solution.py:48
  41.0 1.8 %collective-permute-done.8.refs_1_ = bf16[1024,256]{1,0:T(8,128)(2,1)S(1)} collective-permute-done((bf16[1024,256]{1,0:T(8,128)(2,1)S(1)}, bf16[1024,256]{1,0:T(8,128)(2,1)S(1)}, u32[]{:S(2)}, u32[]{:S(2)}) %collective-permute-start.8) | collective-permute-done | bytes 524320 | tf_op jit(solution)/shard_map/ppermute | solution.py:32
  43.4 1.5 collective-permute-start.20
  45.9 1.1 project.3.refs_0_
  47.0 3.9 %collective-permute-start.14 = (bf16[192,256]{1,0:T(8,128)(2,1)S(1)}, bf16[192,256]{1,0:T(8,128)(2,1)S(1)}, u32[]{:S(2)}, u32[]{:S(2)}) collective-permute-start(bf16[192,256]{1,0:T(8,128)(2,1)S(1)} %project.3.refs_0_), channel_id=1, source_target_pairs={{0,6},{1,7},{2,4},{3,5},{4,2},{5,3},{6,0},{7,1},{8,14},{9,15},{10,... | collective-permute-start | bytes 294920 | tf_op jit(solution)/shard_map/ppermute | solution.py:32
  51.5 3.1 %collective-permute-done.14.refs_6_ = bf16[192,256]{1,0:T(8,128)(2,1)S(1)} collective-permute-done((bf16[192,256]{1,0:T(8,128)(2,1)S(1)}, bf16[192,256]{1,0:T(8,128)(2,1)S(1)}, u32[]{:S(2)}, u32[]{:S(2)}) %collective-permute-start.14) | collective-permute-done | bytes 98336 | tf_op jit(solution)/shard_map/ppermute | solution.py:32
  54.6 4.6 %collective-permute-done.13.refs_4_ = bf16[192,256]{1,0:T(8,128)(2,1)S(1)} collective-permute-done((bf16[192,256]{1,0:T(8,128)(2,1)S(1)}, bf16[192,256]{1,0:T(8,128)(2,1)S(1)}, u32[]{:S(2)}, u32[]{:S(2)}) %collective-permute-start.13) | collective-permute-done | bytes 98336 | tf_op jit(solution)/shard_map/ppermute | solution.py:32
  59.2 2.5 %collective-permute-start.28 = (bf16[192,2560]{1,0:T(8,128)(2,1)S(1)}, bf16[192,2560]{1,0:T(8,128)(2,1)S(1)}, u32[]{:S(2)}, u32[]{:S(2)}) collective-permute-start(bf16[192,2560]{1,0:T(8,128)(2,1)S(1)} %get-tuple-element.84), channel_id=1, source_target_pairs={{0,24},{8,16},{16,8},{24,0},{1,25},{9,17},{17,9},{25,1},{2,26},{10... | collective-permute-start | bytes 2949128 | tf_op jit(solution)/shard_map/ppermute | solution.py:32
  64.4 8.9 %attention.1 = (bf16[192,1024]{1,0:T(8,128)(2,1)}, f32[768,256]{1,0:T(8,128)S(1)}, bf16[768,256]{1,0:T(8,128)(2,1)S(1)}) custom-call(s32[1]{0:T(128)} %bitcast.ids, s32[16]{0:T(128)S(1)} %copy-done.4, s32[8]{0:T(128)S(1)} %bitcast.24, bf16[192,1024]{1,0:T(8,128)(2,1)S(1)} %bitcast.22, bf16[192,1024]{1,0:T(8,128)(2,1)S(1)} %bitcast.23, ...), custom_call_target="tpu_custom_call" | custom-call | tf_op jit(solution)/shard_map/attention/pallas_call | solution.py:169
  73.7 1.4 collective-permute-done.21.came
  75.7 2.6 %collective-permute-start.23 = (bf16[192,256]{1,0:T(8,128)(2,1)S(1)}, bf16[192,256]{1,0:T(8,128)(2,1)S(1)}, u32[]{:S(2)}, u32[]{:S(2)}) collective-permute-start(bf16[192,256]{1,0:T(8,128)(2,1)S(1)} %get-tuple-element.81), channel_id=1, source_target_pairs={{0,4},{1,5},{2,6},{3,7},{4,0},{5,1},{6,2},{7,3},{8,12},{9,13},{10,... | collective-permute-start | bytes 294920 | tf_op jit(solution)/shard_map/ppermute | solution.py:32
  78.3 1.3 collective-permute-start.24
  79.6 2.2 %collective-permute-done.22.refs_1_ = bf16[192,256]{1,0:T(8,128)(2,1)S(1)} collective-permute-done((bf16[192,256]{1,0:T(8,128)(2,1)S(1)}, bf16[192,256]{1,0:T(8,128)(2,1)S(1)}, u32[]{:S(2)}, u32[]{:S(2)}) %collective-permute-start.22) | collective-permute-done | bytes 98336 | tf_op jit(solution)/shard_map/ppermute | solution.py:32
  81.8 4.8 %collective-permute-done.23.refs_2_ = bf16[192,256]{1,0:T(8,128)(2,1)S(1)} collective-permute-done((bf16[192,256]{1,0:T(8,128)(2,1)S(1)}, bf16[192,256]{1,0:T(8,128)(2,1)S(1)}, u32[]{:S(2)}, u32[]{:S(2)}) %collective-permute-start.23) | collective-permute-done | bytes 98336 | tf_op jit(solution)/shard_map/ppermute | solution.py:32
  87.1 1.5 collective-permute-start.26
  88.6 1.5 collective-permute-start.25
  90.1 2.1 %collective-permute-done.28.refs_3_ = bf16[192,2560]{1,0:T(8,128)(2,1)S(1)} collective-permute-done((bf16[192,2560]{1,0:T(8,128)(2,1)S(1)}, bf16[192,2560]{1,0:T(8,128)(2,1)S(1)}, u32[]{:S(2)}, u32[]{:S(2)}) %collective-permute-start.28) | collective-permute-done | bytes 983072 | tf_op jit(solution)/shard_map/ppermute | solution.py:32
  92.3 2.1 %collective-permute-done.27.refs_7_ = bf16[192,256]{1,0:T(8,128)(2,1)S(1)} collective-permute-done((bf16[192,256]{1,0:T(8,128)(2,1)S(1)}, bf16[192,256]{1,0:T(8,128)(2,1)S(1)}, u32[]{:S(2)}, u32[]{:S(2)}) %collective-permute-start.27) | collective-permute-done | bytes 98336 | tf_op jit(solution)/shard_map/ppermute | solution.py:32
  94.3 1.3 collective-permute-done.26.refs_6_
  95.6 1.7 %weight_rows.5 = (bf16[3072,256]{1,0:T(8,128)(2,1)S(1)}, bf16[3072,256]{1,0:T(8,128)(2,1)S(1)}) custom-call(s32[3]{0:T(128)S(1)} %pad_add_fusion.ids, bf16[192,16384]{1,0:T(8,128)(2,1)S(1)} %bitcast.21, bf16[192,256]{1,0:T(8,128)(2,1)S(1)} %total.1.refs_4_.refs_1_), custom_call_target="tpu_custom_call" | custom-call | tf_op jit(solution)/shard_map/weight_rows/pallas_call | solution.py:48
  97.3 1.3 weight_rows.3
  99.2 1.6 %weight_rows.4 = (bf16[768,256]{1,0:T(8,128)(2,1)S(1)}, bf16[768,256]{1,0:T(8,128)(2,1)S(1)}) custom-call(s32[3]{0:T(128)S(1)} %pad_add_fusion.ids, bf16[192,2560]{1,0:T(8,128)(2,1)S(1)} %get-tuple-element.109.refs_0_, bf16[192,2560]{1,0:T(8,128)(2,1)S(1)} %collective-permute-done.19.refs_1_, bf16[192,2560]{1,0:T(8,128)(2,1)S(1)} %collective-permute-done.20.refs_2_, ...), custom_call_target="tpu_custom_call" | custom-call | tf_op jit(solution)/shard_map/weight_rows/pallas_call | solution.py:48
  101.2 1.4 collective-permute-done.30
  103.4 1.6 %collective-permute-start.32 = (bf16[256,256]{1,0:T(8,128)(2,1)S(1)}, bf16[256,256]{1,0:T(8,128)(2,1)S(1)}, u32[]{:S(2)}, u32[]{:S(2)}) collective-permute-start(bf16[256,256]{1,0:T(8,128)(2,1)S(1)} %slice.74), channel_id=1, source_target_pairs={{0,2},{1,3},{2,0},{3,1},{4,6},{5,7},{6,4},{7,5},{8,10},{9,11},{10,... | collective-permute-start | bytes 393224 | tf_op jit(solution)/shard_map/ppermute | solution.py:32
  106.7 2.4 %collective-permute-start.44 = (bf16[768,256]{1,0:T(8,128)(2,1)S(1)}, bf16[768,256]{1,0:T(8,128)(2,1)S(1)}, u32[]{:S(2)}, u32[]{:S(2)}) collective-permute-start(bf16[768,256]{1,0:T(8,128)(2,1)S(1)} %get-tuple-element.103), channel_id=1, source_target_pairs={{0,24},{8,16},{16,8},{24,0},{1,25},{9,17},{17,9},{25,1},{2,26},{10... | collective-permute-start | bytes 1179656 | tf_op jit(solution)/shard_map/ppermute | solution.py:32
  109.8 2.7 %collective-permute-start.33 = (bf16[256,256]{1,0:T(8,128)(2,1)S(1)}, bf16[256,256]{1,0:T(8,128)(2,1)S(1)}, u32[]{:S(2)}, u32[]{:S(2)}) collective-permute-start(bf16[256,256]{1,0:T(8,128)(2,1)S(1)} %fusion.2), channel_id=1, source_target_pairs={{0,4},{1,5},{2,6},{3,7},{4,0},{5,1},{6,2},{7,3},{8,12},{9,13},{10,... | collective-permute-start | bytes 393224 | tf_op jit(solution)/shard_map/ppermute | solution.py:32
  112.5 2.5 %collective-permute-done.37 = bf16[384,256]{1,0:T(8,128)(2,1)S(1)} collective-permute-done((bf16[384,256]{1,0:T(8,128)(2,1)S(1)}, bf16[384,256]{1,0:T(8,128)(2,1)S(1)}, u32[]{:S(2)}, u32[]{:S(2)}) %collective-permute-start.37) | collective-permute-done | bytes 196640 | tf_op jit(solution)/shard_map/ppermute | solution.py:32
  115.0 1.7 %collective-permute-start.38 = (bf16[384,256]{1,0:T(8,128)(2,1)S(1)}, bf16[384,256]{1,0:T(8,128)(2,1)S(1)}, u32[]{:S(2)}, u32[]{:S(2)}) collective-permute-start(bf16[384,256]{1,0:T(8,128)(2,1)S(1)} %fusion), channel_id=1, source_target_pairs={{0,4},{1,5},{2,6},{3,7},{4,0},{5,1},{6,2},{7,3},{8,12},{9,13},{10,... | collective-permute-start | bytes 589832 | tf_op jit(solution)/shard_map/ppermute | solution.py:32
  116.7 6.4 %collective-permute-done.33 = bf16[256,256]{1,0:T(8,128)(2,1)S(1)} collective-permute-done((bf16[256,256]{1,0:T(8,128)(2,1)S(1)}, bf16[256,256]{1,0:T(8,128)(2,1)S(1)}, u32[]{:S(2)}, u32[]{:S(2)}) %collective-permute-start.33) | collective-permute-done | bytes 131104 | tf_op jit(solution)/shard_map/ppermute | solution.py:32
  123.9 1.0 collective-permute-done.43
  125.1 1.6 %collective-permute-start.45 = (bf16[384,256]{1,0:T(8,128)(2,1)S(1)}, bf16[384,256]{1,0:T(8,128)(2,1)S(1)}, u32[]{:S(2)}, u32[]{:S(2)}) collective-permute-start(bf16[384,256]{1,0:T(8,128)(2,1)S(1)} %slice.72), channel_id=1, source_target_pairs={{0,2},{1,3},{2,0},{3,1},{4,6},{5,7},{6,4},{7,5},{8,10},{9,11},{10,... | collective-permute-start | bytes 589832 | tf_op jit(solution)/shard_map/ppermute | solution.py:32
  127.3 6.7 %collective-permute-done.45 = bf16[384,256]{1,0:T(8,128)(2,1)S(1)} collective-permute-done((bf16[384,256]{1,0:T(8,128)(2,1)S(1)}, bf16[384,256]{1,0:T(8,128)(2,1)S(1)}, u32[]{:S(2)}, u32[]{:S(2)}) %collective-permute-start.45) | collective-permute-done | bytes 196640 | tf_op jit(solution)/shard_map/ppermute | solution.py:32
  134.1 1.9 %collective-permute-start.46 = (bf16[384,256]{1,0:T(8,128)(2,1)S(1)}, bf16[384,256]{1,0:T(8,128)(2,1)S(1)}, u32[]{:S(2)}, u32[]{:S(2)}) collective-permute-start(bf16[384,256]{1,0:T(8,128)(2,1)S(1)} %fusion.1), channel_id=1, source_target_pairs={{0,4},{1,5},{2,6},{3,7},{4,0},{5,1},{6,2},{7,3},{8,12},{9,13},{10,... | collective-permute-start | bytes 589832 | tf_op jit(solution)/shard_map/ppermute | solution.py:32
  136.5 2.7 %collective-permute-done.39.refs_5_ = bf16[384,256]{1,0:T(8,128)(2,1)S(1)} collective-permute-done((bf16[384,256]{1,0:T(8,128)(2,1)S(1)}, bf16[384,256]{1,0:T(8,128)(2,1)S(1)}, u32[]{:S(2)}, u32[]{:S(2)}) %collective-permute-start.39) | collective-permute-done | bytes 196640 | tf_op jit(solution)/shard_map/ppermute | solution.py:32
  139.2 4.8 %collective-permute-done.46 = bf16[384,256]{1,0:T(8,128)(2,1)S(1)} collective-permute-done((bf16[384,256]{1,0:T(8,128)(2,1)S(1)}, bf16[384,256]{1,0:T(8,128)(2,1)S(1)}, u32[]{:S(2)}, u32[]{:S(2)}) %collective-permute-start.46) | collective-permute-done | bytes 196640 | tf_op jit(solution)/shard_map/ppermute | solution.py:32
  144.3 2.2 %assemble.2 = (f32[4096,128]{1,0:T(8,128)}, f32[4096,128]{1,0:T(8,128)}) custom-call(s32[3]{0:T(128)S(1)} %pad_add_fusion.ids, bf16[256,256]{1,0:T(8,128)(2,1)S(1)} %add_convert_fusion.2.refs_0_, bf16[256,256]{1,0:T(8,128)(2,1)S(1)} %collective-permute-done.34.refs_1_, bf16[256,256]{1,0:T(8,128)(2,1)S(1)} %collective-permute-done.35.refs_2_, ...), custom_call_target="tpu_custom_call" | custom-call | tf_op jit(solution)/shard_map/assemble/pallas_call | solution.py:391
  146.5 3.4 %collective-permute-done.47.refs_3_ = bf16[384,256]{1,0:T(8,128)(2,1)S(1)} collective-permute-done((bf16[384,256]{1,0:T(8,128)(2,1)S(1)}, bf16[384,256]{1,0:T(8,128)(2,1)S(1)}, u32[]{:S(2)}, u32[]{:S(2)}) %collective-permute-start.47) | collective-permute-done | bytes 196640 | tf_op jit(solution)/shard_map/ppermute | solution.py:32
  149.9 1.4 collective-permute-done.49.refs_5_
  151.3 1.8 %assemble.3 = (f32[4096,128]{1,0:T(8,128)}, f32[4096,128]{1,0:T(8,128)}) custom-call(s32[3]{0:T(128)S(1)} %pad_add_fusion.ids, f32[4096,128]{1,0:T(8,128)} %get-tuple-element.98.refs_0_, f32[4096,128]{1,0:T(8,128)} %get-tuple-element.99.refs_1_, bf16[384,256]{1,0:T(8,128)(2,1)S(1)} %add_convert_fusion.refs_2_, ...), custom_call_target="tpu_custom_call", output_to_operand_aliasing={{0}: (1, {}), {1}: (2, {})} | custom-call | tf_op jit(solution)/shard_map/assemble/pallas_call | solution.py:391
  (99 shorter events, 17.2 us)
Async XLA Ops:
  2.9 15.9 %collective-permute-start = (bf16[1024,256]{1,0:T(8,128)(2,1)}, bf16[1024,256]{1,0:T(8,128)(2,1)S(1)}, u32[]{:S(2)}, u32[]{:S(2)}) collective-permute-start(bf16[1024,256]{1,0:T(8,128)(2,1)} %pad_maximum_fusion), channel_id=1, source_target_pairs={{0,8},{8,0},{16,24},{24,16},{1,9},{9,1},{17,25},{25,17},{2,10},{10... | collective-permute-start | bytes 1572872 | tf_op jit(solution)/shard_map/ppermute | solution.py:32
  6.7 15.1 %collective-permute-start.2 = (bf16[1024,256]{1,0:T(8,128)(2,1)}, bf16[1024,256]{1,0:T(8,128)(2,1)S(1)}, u32[]{:S(2)}, u32[]{:S(2)}) collective-permute-start(bf16[1024,256]{1,0:T(8,128)(2,1)} %pad_maximum_fusion.1), channel_id=1, source_target_pairs={{0,16},{8,24},{16,0},{24,8},{1,17},{9,25},{17,1},{25,9},{2,18},{10... | collective-permute-start | bytes 1572872 | tf_op jit(solution)/shard_map/ppermute | solution.py:32
  8.2 24.9 %collective-permute-start.5 = (bf16[1024,256]{1,0:T(8,128)(2,1)}, bf16[1024,256]{1,0:T(8,128)(2,1)}, u32[]{:S(2)}, u32[]{:S(2)}) collective-permute-start(bf16[1024,256]{1,0:T(8,128)(2,1)} %pad_maximum_fusion), channel_id=1, source_target_pairs={{0,16},{8,24},{16,0},{24,8},{1,17},{9,25},{17,1},{25,9},{2,18},{10... | collective-permute-start | bytes 1572872 | tf_op jit(solution)/shard_map/ppermute | solution.py:32
  8.7 24.4 %collective-permute-start.1 = (bf16[1024,256]{1,0:T(8,128)(2,1)}, bf16[1024,256]{1,0:T(8,128)(2,1)}, u32[]{:S(2)}, u32[]{:S(2)}) collective-permute-start(bf16[1024,256]{1,0:T(8,128)(2,1)} %pad_maximum_fusion.1), channel_id=1, source_target_pairs={{0,8},{8,0},{16,24},{24,16},{1,9},{9,1},{17,25},{25,17},{2,10},{10... | collective-permute-start | bytes 1572872 | tf_op jit(solution)/shard_map/ppermute | solution.py:32
  21.8 11.9 %collective-permute-start.3 = (bf16[1024,256]{1,0:T(8,128)(2,1)S(1)}, bf16[1024,256]{1,0:T(8,128)(2,1)}, u32[]{:S(2)}, u32[]{:S(2)}) collective-permute-start(bf16[1024,256]{1,0:T(8,128)(2,1)S(1)} %collective-permute-done.refs_2_), channel_id=1, source_target_pairs={{0,1},{1,0},{2,3},{3,2},{4,5},{5,4},{6,7},{7,6},{8,9},{9,8},{10,11... | collective-permute-start | bytes 1572872 | tf_op jit(solution)/shard_map/ppermute | solution.py:32
  21.8 21.0 %collective-permute-start.8 = (bf16[1024,256]{1,0:T(8,128)(2,1)S(1)}, bf16[1024,256]{1,0:T(8,128)(2,1)S(1)}, u32[]{:S(2)}, u32[]{:S(2)}) collective-permute-start(bf16[1024,256]{1,0:T(8,128)(2,1)S(1)} %collective-permute-done.refs_2_), channel_id=1, source_target_pairs={{0,16},{8,24},{16,0},{24,8},{1,17},{9,25},{17,1},{25,9},{2,18},{10... | collective-permute-start | bytes 1572872 | tf_op jit(solution)/shard_map/ppermute | solution.py:32
  23.3 19.5 %collective-permute-start.9 = (bf16[1024,256]{1,0:T(8,128)(2,1)S(1)}, bf16[1024,256]{1,0:T(8,128)(2,1)S(1)}, u32[]{:S(2)}, u32[]{:S(2)}) collective-permute-start(bf16[1024,256]{1,0:T(8,128)(2,1)S(1)} %collective-permute-done.2.refs_7_), channel_id=1, source_target_pairs={{0,8},{8,0},{16,24},{24,16},{1,9},{9,1},{17,25},{25,17},{2,10},{10... | collective-permute-start | bytes 1572872 | tf_op jit(solution)/shard_map/ppermute | solution.py:32
  33.1 3.2 %collective-permute-start.6 = (bf16[1024,256]{1,0:T(8,128)(2,1)}, bf16[1024,256]{1,0:T(8,128)(2,1)S(1)}, u32[]{:S(2)}, u32[]{:S(2)}) collective-permute-start(bf16[1024,256]{1,0:T(8,128)(2,1)} %collective-permute-done.5.refs_6_), channel_id=1, source_target_pairs={{0,1},{1,0},{2,3},{3,2},{4,5},{5,4},{6,7},{7,6},{8,9},{9,8},{10,11... | collective-permute-start | bytes 1572872 | tf_op jit(solution)/shard_map/ppermute | solution.py:32
  33.1 3.6 %collective-permute-start.4 = (bf16[1024,256]{1,0:T(8,128)(2,1)}, bf16[1024,256]{1,0:T(8,128)(2,1)S(1)}, u32[]{:S(2)}, u32[]{:S(2)}) collective-permute-start(bf16[1024,256]{1,0:T(8,128)(2,1)} %collective-permute-done.1.refs_3_), channel_id=1, source_target_pairs={{0,1},{1,0},{2,3},{3,2},{4,5},{5,4},{6,7},{7,6},{8,9},{9,8},{10,11... | collective-permute-start | bytes 1572872 | tf_op jit(solution)/shard_map/ppermute | solution.py:32
  33.6 3.1 %collective-permute-start.7 = (bf16[1024,256]{1,0:T(8,128)(2,1)S(1)}, bf16[1024,256]{1,0:T(8,128)(2,1)S(1)}, u32[]{:S(2)}, u32[]{:S(2)}) collective-permute-start(bf16[1024,256]{1,0:T(8,128)(2,1)S(1)} %collective-permute-done.2.refs_7_), channel_id=1, source_target_pairs={{0,1},{1,0},{2,3},{3,2},{4,5},{5,4},{6,7},{7,6},{8,9},{9,8},{10,11... | collective-permute-start | bytes 1572872 | tf_op jit(solution)/shard_map/ppermute | solution.py:32
  42.8 2.1 %collective-permute-start.10 = (bf16[1024,256]{1,0:T(8,128)(2,1)S(1)}, bf16[1024,256]{1,0:T(8,128)(2,1)S(1)}, u32[]{:S(2)}, u32[]{:S(2)}) collective-permute-start(bf16[1024,256]{1,0:T(8,128)(2,1)S(1)} %collective-permute-done.8.refs_1_), channel_id=1, source_target_pairs={{0,1},{1,0},{2,3},{3,2},{4,5},{5,4},{6,7},{7,6},{8,9},{9,8},{10,11... | collective-permute-start | bytes 1572872 | tf_op jit(solution)/shard_map/ppermute | solution.py:32
  42.9 2.6 %collective-permute-start.11 = (bf16[1024,256]{1,0:T(8,128)(2,1)S(1)}, bf16[1024,256]{1,0:T(8,128)(2,1)S(1)}, u32[]{:S(2)}, u32[]{:S(2)}) collective-permute-start(bf16[1024,256]{1,0:T(8,128)(2,1)S(1)} %collective-permute-done.9.refs_2_), channel_id=1, source_target_pairs={{0,1},{1,0},{2,3},{3,2},{4,5},{5,4},{6,7},{7,6},{8,9},{9,8},{10,11... | collective-permute-start | bytes 1572872 | tf_op jit(solution)/shard_map/ppermute | solution.py:32
  43.4 29.9 %collective-permute-start.20 = (bf16[192,2560]{1,0:T(8,128)(2,1)S(1)}, bf16[192,2560]{1,0:T(8,128)(2,1)S(1)}, u32[]{:S(2)}, u32[]{:S(2)}) collective-permute-start(bf16[192,2560]{1,0:T(8,128)(2,1)S(1)} %get-tuple-element.74), channel_id=1, source_target_pairs={{0,16},{8,24},{16,0},{24,8},{1,17},{9,25},{17,1},{25,9},{2,18},{10... | collective-permute-start | bytes 2949128 | tf_op jit(solution)/shard_map/ppermute | solution.py:32
  45.5 27.8 %collective-permute-start.19 = (bf16[192,2560]{1,0:T(8,128)(2,1)S(1)}, bf16[192,2560]{1,0:T(8,128)(2,1)S(1)}, u32[]{:S(2)}, u32[]{:S(2)}) collective-permute-start(bf16[192,2560]{1,0:T(8,128)(2,1)S(1)} %get-tuple-element.73), channel_id=1, source_target_pairs={{0,8},{8,0},{16,24},{24,16},{1,9},{9,1},{17,25},{25,17},{2,10},{10... | collective-permute-start | bytes 2949128 | tf_op jit(solution)/shard_map/ppermute | solution.py:32
  47.0 7.6 %collective-permute-start.14 = (bf16[192,256]{1,0:T(8,128)(2,1)S(1)}, bf16[192,256]{1,0:T(8,128)(2,1)S(1)}, u32[]{:S(2)}, u32[]{:S(2)}) collective-permute-start(bf16[192,256]{1,0:T(8,128)(2,1)S(1)} %project.3.refs_0_), channel_id=1, source_target_pairs={{0,6},{1,7},{2,4},{3,5},{4,2},{5,3},{6,0},{7,1},{8,14},{9,15},{10,... | collective-permute-start | bytes 294920 | tf_op jit(solution)/shard_map/ppermute | solution.py:32
  50.9 8.3 %collective-permute-start.13 = (bf16[192,256]{1,0:T(8,128)(2,1)S(1)}, bf16[192,256]{1,0:T(8,128)(2,1)S(1)}, u32[]{:S(2)}, u32[]{:S(2)}) collective-permute-start(bf16[192,256]{1,0:T(8,128)(2,1)S(1)} %project.3.refs_0_), channel_id=1, source_target_pairs={{0,4},{1,5},{2,6},{3,7},{4,0},{5,1},{6,2},{7,3},{8,12},{9,13},{10,... | collective-permute-start | bytes 294920 | tf_op jit(solution)/shard_map/ppermute | solution.py:32
  50.9 8.3 %collective-permute-start.12 = (bf16[192,256]{1,0:T(8,128)(2,1)S(1)}, bf16[192,256]{1,0:T(8,128)(2,1)S(1)}, u32[]{:S(2)}, u32[]{:S(2)}) collective-permute-start(bf16[192,256]{1,0:T(8,128)(2,1)S(1)} %project.3.refs_0_), channel_id=1, source_target_pairs={{0,2},{1,3},{2,0},{3,1},{4,6},{5,7},{6,4},{7,5},{8,10},{9,11},{10,... | collective-permute-start | bytes 294920 | tf_op jit(solution)/shard_map/ppermute | solution.py:32
  59.2 33.1 %collective-permute-start.28 = (bf16[192,2560]{1,0:T(8,128)(2,1)S(1)}, bf16[192,2560]{1,0:T(8,128)(2,1)S(1)}, u32[]{:S(2)}, u32[]{:S(2)}) collective-permute-start(bf16[192,2560]{1,0:T(8,128)(2,1)S(1)} %get-tuple-element.84), channel_id=1, source_target_pairs={{0,24},{8,16},{16,8},{24,0},{1,25},{9,17},{17,9},{25,1},{2,26},{10... | collective-permute-start | bytes 2949128 | tf_op jit(solution)/shard_map/ppermute | solution.py:32
  61.6 1.5 collective-permute-start.16
  63.1 1.3 collective-permute-start.18
  73.3 1.7 %collective-permute-start.21 = (bf16[768,256]{1,0:T(8,128)(2,1)S(1)}, bf16[768,256]{1,0:T(8,128)(2,1)S(1)}, u32[]{:S(2)}, u32[]{:S(2)}) collective-permute-start(bf16[768,256]{1,0:T(8,128)(2,1)S(1)} %get-tuple-element.78), channel_id=1, source_target_pairs={{0,1},{1,0},{2,3},{3,2},{4,5},{5,4},{6,7},{7,6},{8,9},{9,8},{10,11... | collective-permute-start | bytes 1179656 | tf_op jit(solution)/shard_map/ppermute | solution.py:32
  75.1 6.6 %collective-permute-start.22 = (bf16[192,256]{1,0:T(8,128)(2,1)S(1)}, bf16[192,256]{1,0:T(8,128)(2,1)S(1)}, u32[]{:S(2)}, u32[]{:S(2)}) collective-permute-start(bf16[192,256]{1,0:T(8,128)(2,1)S(1)} %get-tuple-element.80), channel_id=1, source_target_pairs={{0,2},{1,3},{2,0},{3,1},{4,6},{5,7},{6,4},{7,5},{8,10},{9,11},{10,... | collective-permute-start | bytes 294920 | tf_op jit(solution)/shard_map/ppermute | solution.py:32
  75.7 10.8 %collective-permute-start.23 = (bf16[192,256]{1,0:T(8,128)(2,1)S(1)}, bf16[192,256]{1,0:T(8,128)(2,1)S(1)}, u32[]{:S(2)}, u32[]{:S(2)}) collective-permute-start(bf16[192,256]{1,0:T(8,128)(2,1)S(1)} %get-tuple-element.81), channel_id=1, source_target_pairs={{0,4},{1,5},{2,6},{3,7},{4,0},{5,1},{6,2},{7,3},{8,12},{9,13},{10,... | collective-permute-start | bytes 294920 | tf_op jit(solution)/shard_map/ppermute | solution.py:32
  78.3 8.3 %collective-permute-start.24 = (bf16[192,256]{1,0:T(8,128)(2,1)S(1)}, bf16[192,256]{1,0:T(8,128)(2,1)S(1)}, u32[]{:S(2)}, u32[]{:S(2)}) collective-permute-start(bf16[192,256]{1,0:T(8,128)(2,1)S(1)} %get-tuple-element.82), channel_id=1, source_target_pairs={{0,6},{1,7},{2,4},{3,5},{4,2},{5,3},{6,0},{7,1},{8,14},{9,15},{10,... | collective-permute-start | bytes 294920 | tf_op jit(solution)/shard_map/ppermute | solution.py:32
  86.6 7.7 %collective-permute-start.27 = (bf16[192,256]{1,0:T(8,128)(2,1)S(1)}, bf16[192,256]{1,0:T(8,128)(2,1)S(1)}, u32[]{:S(2)}, u32[]{:S(2)}) collective-permute-start(bf16[192,256]{1,0:T(8,128)(2,1)S(1)} %total.1.refs_4_.refs_1_), channel_id=1, source_target_pairs={{0,24},{8,16},{16,8},{24,0},{1,25},{9,17},{17,9},{25,1},{2,26},{10... | collective-permute-start | bytes 294920 | tf_op jit(solution)/shard_map/ppermute | solution.py:32
  87.1 8.5 %collective-permute-start.26 = (bf16[192,256]{1,0:T(8,128)(2,1)S(1)}, bf16[192,256]{1,0:T(8,128)(2,1)S(1)}, u32[]{:S(2)}, u32[]{:S(2)}) collective-permute-start(bf16[192,256]{1,0:T(8,128)(2,1)S(1)} %total.1.refs_4_.refs_1_), channel_id=1, source_target_pairs={{0,16},{8,24},{16,0},{24,8},{1,17},{9,25},{17,1},{25,9},{2,18},{10... | collective-permute-start | bytes 294920 | tf_op jit(solution)/shard_map/ppermute | solution.py:32
  88.6 6.9 %collective-permute-start.25 = (bf16[192,256]{1,0:T(8,128)(2,1)S(1)}, bf16[192,256]{1,0:T(8,128)(2,1)S(1)}, u32[]{:S(2)}, u32[]{:S(2)}) collective-permute-start(bf16[192,256]{1,0:T(8,128)(2,1)S(1)} %total.1.refs_4_.refs_1_), channel_id=1, source_target_pairs={{0,8},{8,0},{16,24},{24,16},{1,9},{9,1},{17,25},{25,17},{2,10},{10... | collective-permute-start | bytes 294920 | tf_op jit(solution)/shard_map/ppermute | solution.py:32
  97.2 5.5 %collective-permute-start.31 = (bf16[3072,256]{1,0:T(8,128)(2,1)S(1)}, bf16[3072,256]{1,0:T(8,128)(2,1)S(1)}, u32[]{:S(2)}, u32[]{:S(2)}) collective-permute-start(bf16[3072,256]{1,0:T(8,128)(2,1)S(1)} %get-tuple-element.95), channel_id=1, source_target_pairs={{0,1},{1,0},{2,3},{3,2},{4,5},{5,4},{6,7},{7,6},{8,9},{9,8},{10,11... | collective-permute-start | bytes 4718600 | tf_op jit(solution)/shard_map/ppermute | solution.py:32
  98.6 2.4 %collective-permute-start.29 = (bf16[512,256]{1,0:T(8,128)(2,1)S(1)}, bf16[512,256]{1,0:T(8,128)(2,1)S(1)}, u32[]{:S(2)}, u32[]{:S(2)}) collective-permute-start(bf16[512,256]{1,0:T(8,128)(2,1)S(1)} %get-tuple-element.90), channel_id=1, source_target_pairs={{0,1},{1,0},{2,3},{3,2},{4,5},{5,4},{6,7},{7,6},{8,9},{9,8},{10,11... | collective-permute-start | bytes 786440 | tf_op jit(solution)/shard_map/ppermute | solution.py:32
  100.8 1.8 %collective-permute-start.30 = (bf16[768,256]{1,0:T(8,128)(2,1)S(1)}, bf16[768,256]{1,0:T(8,128)(2,1)S(1)}, u32[]{:S(2)}, u32[]{:S(2)}) collective-permute-start(bf16[768,256]{1,0:T(8,128)(2,1)S(1)} %get-tuple-element.92), channel_id=1, source_target_pairs={{0,1},{1,0},{2,3},{3,2},{4,5},{5,4},{6,7},{7,6},{8,9},{9,8},{10,11... | collective-permute-start | bytes 1179656 | tf_op jit(solution)/shard_map/ppermute | solution.py:32
  103.4 6.4 %collective-permute-start.32 = (bf16[256,256]{1,0:T(8,128)(2,1)S(1)}, bf16[256,256]{1,0:T(8,128)(2,1)S(1)}, u32[]{:S(2)}, u32[]{:S(2)}) collective-permute-start(bf16[256,256]{1,0:T(8,128)(2,1)S(1)} %slice.74), channel_id=1, source_target_pairs={{0,2},{1,3},{2,0},{3,1},{4,6},{5,7},{6,4},{7,5},{8,10},{9,11},{10,... | collective-permute-start | bytes 393224 | tf_op jit(solution)/shard_map/ppermute | solution.py:32
  105.1 9.9 %collective-permute-start.37 = (bf16[384,256]{1,0:T(8,128)(2,1)S(1)}, bf16[384,256]{1,0:T(8,128)(2,1)S(1)}, u32[]{:S(2)}, u32[]{:S(2)}) collective-permute-start(bf16[384,256]{1,0:T(8,128)(2,1)S(1)} %slice.73), channel_id=1, source_target_pairs={{0,2},{1,3},{2,0},{3,1},{4,6},{5,7},{6,4},{7,5},{8,10},{9,11},{10,... | collective-permute-start | bytes 589832 | tf_op jit(solution)/shard_map/ppermute | solution.py:32
  105.6 18.3 %collective-permute-start.42 = (bf16[768,256]{1,0:T(8,128)(2,1)S(1)}, bf16[768,256]{1,0:T(8,128)(2,1)S(1)}, u32[]{:S(2)}, u32[]{:S(2)}) collective-permute-start(bf16[768,256]{1,0:T(8,128)(2,1)S(1)} %get-tuple-element.101), channel_id=1, source_target_pairs={{0,8},{8,0},{16,24},{24,16},{1,9},{9,1},{17,25},{25,17},{2,10},{10... | collective-permute-start | bytes 1179656 | tf_op jit(solution)/shard_map/ppermute | solution.py:32
  106.1 18.8 %collective-permute-start.43 = (bf16[768,256]{1,0:T(8,128)(2,1)S(1)}, bf16[768,256]{1,0:T(8,128)(2,1)S(1)}, u32[]{:S(2)}, u32[]{:S(2)}) collective-permute-start(bf16[768,256]{1,0:T(8,128)(2,1)S(1)} %get-tuple-element.102), channel_id=1, source_target_pairs={{0,16},{8,24},{16,0},{24,8},{1,17},{9,25},{17,1},{25,9},{2,18},{10... | collective-permute-start | bytes 1179656 | tf_op jit(solution)/shard_map/ppermute | solution.py:32
  106.7 18.2 %collective-permute-start.44 = (bf16[768,256]{1,0:T(8,128)(2,1)S(1)}, bf16[768,256]{1,0:T(8,128)(2,1)S(1)}, u32[]{:S(2)}, u32[]{:S(2)}) collective-permute-start(bf16[768,256]{1,0:T(8,128)(2,1)S(1)} %get-tuple-element.103), channel_id=1, source_target_pairs={{0,24},{8,16},{16,8},{24,0},{1,25},{9,17},{17,9},{25,1},{2,26},{10... | collective-permute-start | bytes 1179656 | tf_op jit(solution)/shard_map/ppermute | solution.py:32
  109.8 13.3 %collective-permute-start.33 = (bf16[256,256]{1,0:T(8,128)(2,1)S(1)}, bf16[256,256]{1,0:T(8,128)(2,1)S(1)}, u32[]{:S(2)}, u32[]{:S(2)}) collective-permute-start(bf16[256,256]{1,0:T(8,128)(2,1)S(1)} %fusion.2), channel_id=1, source_target_pairs={{0,4},{1,5},{2,6},{3,7},{4,0},{5,1},{6,2},{7,3},{8,12},{9,13},{10,... | collective-permute-start | bytes 393224 | tf_op jit(solution)/shard_map/ppermute | solution.py:32
  115.0 12.1 %collective-permute-start.38 = (bf16[384,256]{1,0:T(8,128)(2,1)S(1)}, bf16[384,256]{1,0:T(8,128)(2,1)S(1)}, u32[]{:S(2)}, u32[]{:S(2)}) collective-permute-start(bf16[384,256]{1,0:T(8,128)(2,1)S(1)} %fusion), channel_id=1, source_target_pairs={{0,4},{1,5},{2,6},{3,7},{4,0},{5,1},{6,2},{7,3},{8,12},{9,13},{10,... | collective-permute-start | bytes 589832 | tf_op jit(solution)/shard_map/ppermute | solution.py:32
  123.2 12.9 %collective-permute-start.34 = (bf16[256,256]{1,0:T(8,128)(2,1)S(1)}, bf16[256,256]{1,0:T(8,128)(2,1)S(1)}, u32[]{:S(2)}, u32[]{:S(2)}) collective-permute-start(bf16[256,256]{1,0:T(8,128)(2,1)S(1)} %add_convert_fusion.2.refs_0_), channel_id=1, source_target_pairs={{0,2},{1,3},{2,0},{3,1},{4,6},{5,7},{6,4},{7,5},{8,10},{9,11},{10,... | collective-permute-start | bytes 393224 | tf_op jit(solution)/shard_map/ppermute | solution.py:32
  125.1 8.9 %collective-permute-start.45 = (bf16[384,256]{1,0:T(8,128)(2,1)S(1)}, bf16[384,256]{1,0:T(8,128)(2,1)S(1)}, u32[]{:S(2)}, u32[]{:S(2)}) collective-permute-start(bf16[384,256]{1,0:T(8,128)(2,1)S(1)} %slice.72), channel_id=1, source_target_pairs={{0,2},{1,3},{2,0},{3,1},{4,6},{5,7},{6,4},{7,5},{8,10},{9,11},{10,... | collective-permute-start | bytes 589832 | tf_op jit(solution)/shard_map/ppermute | solution.py:32
  127.1 12.1 %collective-permute-start.39 = (bf16[384,256]{1,0:T(8,128)(2,1)S(1)}, bf16[384,256]{1,0:T(8,128)(2,1)S(1)}, u32[]{:S(2)}, u32[]{:S(2)}) collective-permute-start(bf16[384,256]{1,0:T(8,128)(2,1)S(1)} %add_convert_fusion.1.refs_4_), channel_id=1, source_target_pairs={{0,2},{1,3},{2,0},{3,1},{4,6},{5,7},{6,4},{7,5},{8,10},{9,11},{10,... | collective-permute-start | bytes 589832 | tf_op jit(solution)/shard_map/ppermute | solution.py:32
  134.1 10.0 %collective-permute-start.46 = (bf16[384,256]{1,0:T(8,128)(2,1)S(1)}, bf16[384,256]{1,0:T(8,128)(2,1)S(1)}, u32[]{:S(2)}, u32[]{:S(2)}) collective-permute-start(bf16[384,256]{1,0:T(8,128)(2,1)S(1)} %fusion.1), channel_id=1, source_target_pairs={{0,4},{1,5},{2,6},{3,7},{4,0},{5,1},{6,2},{7,3},{8,12},{9,13},{10,... | collective-permute-start | bytes 589832 | tf_op jit(solution)/shard_map/ppermute | solution.py:32
  136.0 3.2 %collective-permute-start.35 = (bf16[256,256]{1,0:T(8,128)(2,1)S(1)}, bf16[256,256]{1,0:T(8,128)(2,1)S(1)}, u32[]{:S(2)}, u32[]{:S(2)}) collective-permute-start(bf16[256,256]{1,0:T(8,128)(2,1)S(1)} %add_convert_fusion.2.refs_0_), channel_id=1, source_target_pairs={{0,1},{1,0},{2,3},{3,2},{4,5},{5,4},{6,7},{7,6},{8,9},{9,8},{10,11... | collective-permute-start | bytes 393224 | tf_op jit(solution)/shard_map/ppermute | solution.py:32
  136.0 3.2 %collective-permute-start.36 = (bf16[256,256]{1,0:T(8,128)(2,1)S(1)}, bf16[256,256]{1,0:T(8,128)(2,1)S(1)}, u32[]{:S(2)}, u32[]{:S(2)}) collective-permute-start(bf16[256,256]{1,0:T(8,128)(2,1)S(1)} %collective-permute-done.34.refs_1_), channel_id=1, source_target_pairs={{0,1},{1,0},{2,3},{3,2},{4,5},{5,4},{6,7},{7,6},{8,9},{9,8},{10,11... | collective-permute-start | bytes 393224 | tf_op jit(solution)/shard_map/ppermute | solution.py:32
  136.5 7.8 %collective-permute-start.40 = (bf16[384,256]{1,0:T(8,128)(2,1)S(1)}, bf16[384,256]{1,0:T(8,128)(2,1)S(1)}, u32[]{:S(2)}, u32[]{:S(2)}) collective-permute-start(bf16[384,256]{1,0:T(8,128)(2,1)S(1)} %add_convert_fusion.1.refs_4_), channel_id=1, source_target_pairs={{0,1},{1,0},{2,3},{3,2},{4,5},{5,4},{6,7},{7,6},{8,9},{9,8},{10,11... | collective-permute-start | bytes 589832 | tf_op jit(solution)/shard_map/ppermute | solution.py:32
  139.2 5.1 %collective-permute-start.41 = (bf16[384,256]{1,0:T(8,128)(2,1)S(1)}, bf16[384,256]{1,0:T(8,128)(2,1)S(1)}, u32[]{:S(2)}, u32[]{:S(2)}) collective-permute-start(bf16[384,256]{1,0:T(8,128)(2,1)S(1)} %collective-permute-done.39.refs_5_), channel_id=1, source_target_pairs={{0,1},{1,0},{2,3},{3,2},{4,5},{5,4},{6,7},{7,6},{8,9},{9,8},{10,11... | collective-permute-start | bytes 589832 | tf_op jit(solution)/shard_map/ppermute | solution.py:32
  144.1 5.7 %collective-permute-start.47 = (bf16[384,256]{1,0:T(8,128)(2,1)S(1)}, bf16[384,256]{1,0:T(8,128)(2,1)S(1)}, u32[]{:S(2)}, u32[]{:S(2)}) collective-permute-start(bf16[384,256]{1,0:T(8,128)(2,1)S(1)} %add_convert_fusion.refs_2_), channel_id=1, source_target_pairs={{0,2},{1,3},{2,0},{3,1},{4,6},{5,7},{6,4},{7,5},{8,10},{9,11},{10,... | collective-permute-start | bytes 589832 | tf_op jit(solution)/shard_map/ppermute | solution.py:32
  144.2 5.7 %collective-permute-start.48 = (bf16[384,256]{1,0:T(8,128)(2,1)S(1)}, bf16[384,256]{1,0:T(8,128)(2,1)S(1)}, u32[]{:S(2)}, u32[]{:S(2)}) collective-permute-start(bf16[384,256]{1,0:T(8,128)(2,1)S(1)} %add_convert_fusion.refs_2_), channel_id=1, source_target_pairs={{0,1},{1,0},{2,3},{3,2},{4,5},{5,4},{6,7},{7,6},{8,9},{9,8},{10,11... | collective-permute-start | bytes 589832 | tf_op jit(solution)/shard_map/ppermute | solution.py:32
  149.9 1.4 collective-permute-start.49
  (10 other events, 136.2 us)

commit v12 on v11

--- a/solution.py
+++ b/solution.py
@@ -12,13 +12,12 @@
 NO_COST = pl.CostEstimate(flops=0, bytes_accessed=0, transcendentals=0)
 
 
-MOVED = (4, 6)
-TIED = 2
+MOVED = (2, 8)
 
 
 def region_sizes(block_rows):
     units = block_rows // 256
-    sizes = [256 * (units * share // 16) for share in MOVED]
+    sizes = [256 * max(1, units * share // 16) for share in MOVED]
     return sizes + [block_rows - sum(sizes)]
 
 
@@ -492,7 +491,7 @@
     along, _ = after(along)
     kv_blocks = both_cores(along)
 
-    moved.update({j: swap(moving[j], "dp", j) for j in far})
+    far_second = [swap(moving[j][:, sizes[0] :], "dp", j) for j in far]
 
     query_grad, keep, send = attention(
         me, stretch_order, doc_lengths[0], queries[0], grad_out[0], kv_blocks, head_dim
@@ -501,29 +500,31 @@
     moved.update(zip(near, ended))
     own, *leaving = add_and_split(keep, swap(send, "ctx", 1), z_count)
     grad = add_all([own] + [swap(one, "ctx", 2 * m) for m, one in enumerate(leaving, 1)])
+    (grad,), far_second = after([grad], *far_second)
     grads = [grad] + [swap(grad, "dp", j) for j in range(1, dp_count)]
 
-    (grad,), ended = after([grad], *grads[1:], *[moved[j] for j in far])
-    grads[1:] = ended[: dp_count - 1]
-    moved.update(zip(far, ended[dp_count - 1 :]))
     groups = [[(0, j, 0, 0)] for j in range(dp_count)]
     ours, came = weight_rows(
         ids, [inputs], [grad], groups, *regions[-1], block_rows, sub_count
     )
     own = parts_over_dp(add_cores(ours, came))
-    groups = [[(j, None, j, 0) for j in range(dp_count)]]
-    arrays = [moved[j] for j in range(dp_count)]
-    moved_parts = [
-        add_cores(*weight_rows(ids, arrays, grads, groups, *region, block_rows, sub_count))
-        for region in regions[:-1]
-    ]
-    moved_parts, own = after(moved_parts, *own)
+    tied, _ = after([moving[j][:, : sizes[0]] for j in far], grad)
+    far_first = [swap(one, "dp", j) for one, j in zip(tied, far)]
+    grads, ended = after(grads, *own, *far_first)
+    own, far_first = ended[: len(own)], ended[len(own) :]
+    moved_parts = []
+    for region, pieces, shift in zip(regions, (far_first, far_second), (0, sizes[0])):
+        groups = [[(j, None, j, shift if j in far else 0) for j in range(dp_count)]]
+        arrays = [pieces[far.index(j)] if j in far else moved[j] for j in range(dp_count)]
+        pair = weight_rows(ids, arrays, grads, groups, *region, block_rows, sub_count)
+        moved_parts.append(add_cores(*pair))
     own = [swap(one, "dp", j) if j else one for j, one in enumerate(own)]
-    finals = []
-    for part in moved_parts:
-        part = scatter_along_z(part, sub_count)
-        finals.append(sum_of_halves(part, sub_count))
-    part = scatter_along_z(sum_of(own), sub_count, finals[:TIED])
+    second = scatter_along_z(moved_parts[1], sub_count)
+    (first,), _ = after(moved_parts[:1], second)
+    first = scatter_along_z(first, sub_count)
+    finals = [sum_of_halves(first, sub_count), sum_of_halves(second, sub_count)]
+    part = scatter_along_z(sum_of(own), sub_count, finals[1:])
+    finals, _ = after(finals, part)
     blocks = gather_parts(finals[0], sub_count)
     last = sum_of_halves(part, sub_count, blocks)
     blocks += [one for final in finals[1:] for one in gather_parts(final, sub_count)]

time: 153 us -> 163 us (1.065)
  waiting for transfers between devices: 79.9 us -> 87.1 us
  starting transfers between devices: 42.3 us -> 44.6 us
    ppermute x50 -> x51, waiting for transfers between devices: 79.9 us -> 87.1 us  [swap(): return lax.ppermute(array, axis, [(i, i ^ distance) for i in range(count)])]
    ppermute x50 -> x51, starting transfers between devices: 42.3 us -> 44.6 us  [swap(): return lax.ppermute(array, axis, [(i, i ^ distance) for i in range(count)])]
  transfers between devices with their start and end apart: 50 -> 51, of which waited for: 29 -> 29; matrix products, arithmetic and copies ran while one was open for 3% -> 3% of each run, Pallas kernels for 12% -> 10%
where the time goes in v12:
time: 163 us
  waiting for transfers between devices  87.1 us (53%)
  starting transfers between devices  44.6 us (27%)
  Pallas kernels  21.9 us (13%)
  local copies, waits for them, and re-layouts  5.23 us (3%)
  other arithmetic  2.81 us (2%)
    ppermute x51, waiting for transfers between devices, swap(): return lax.ppermute(array, axis, [(i, i ^ distance) for i in range(count)])  87.1 us
    ppermute x51, starting transfers between devices, swap(): return lax.ppermute(array, axis, [(i, i ^ distance) for i in range(count)])  44.6 us
    pallas_call x7, Pallas kernels, kernel_call(): pl.pallas_call(kernel, out_shape=outs, in_specs=[smem] * len(scalars) + [...  9.12 us
    pallas_call x1, Pallas kernels, attention(): pl.pallas_call(functools.partial(attention_kernel, shape), out_shape=(jax...  8.87 us
    pallas_call x2, Pallas kernels, assemble(): pl.pallas_call(functools.partial(assemble_kernel, sub_count, regions, not...  3.92 us
  transfers between devices with their start and end apart: 51, of which 29 were waited for; matrix products, arithmetic and copies ran while one was open for 3% of the time, Pallas kernels for 10%

profile of v12, /device:TPU:0, one launch (start us, length us, event | category | flops | bytes accessed | tf_op | source)
XLA Modules:
  0.0 162.7 jit_solution(8967493948229296829)
XLA Ops:
  0.7 1.4 constant_dynamic-slice_fusion
  2.9 3.0 %collective-permute-start.2 = (bf16[1024,256]{1,0:T(8,128)(2,1)}, bf16[1024,256]{1,0:T(8,128)(2,1)S(1)}, u32[]{:S(2)}, u32[]{:S(2)}) collective-permute-start(bf16[1024,256]{1,0:T(8,128)(2,1)} %pad_maximum_fusion.1), channel_id=1, source_target_pairs={{0,16},{8,24},{16,0},{24,8},{1,17},{9,25},{17,1},{25,9},{2,18},{10... | collective-permute-start | bytes 1572872 | tf_op jit(solution)/shard_map/ppermute | solution.py:31
  6.7 1.5 collective-permute-start
  8.8 10.1 %collective-permute-done.2.refs_7_ = bf16[1024,256]{1,0:T(8,128)(2,1)S(1)} collective-permute-done((bf16[1024,256]{1,0:T(8,128)(2,1)}, bf16[1024,256]{1,0:T(8,128)(2,1)S(1)}, u32[]{:S(2)}, u32[]{:S(2)}) %collective-permute-start.2) | collective-permute-done | bytes 524320 | tf_op jit(solution)/shard_map/ppermute | solution.py:31
  18.9 3.0 %collective-permute-done.refs_2_ = bf16[1024,256]{1,0:T(8,128)(2,1)S(1)} collective-permute-done((bf16[1024,256]{1,0:T(8,128)(2,1)}, bf16[1024,256]{1,0:T(8,128)(2,1)S(1)}, u32[]{:S(2)}, u32[]{:S(2)}) %collective-permute-start) | collective-permute-done | bytes 524320 | tf_op jit(solution)/shard_map/ppermute | solution.py:31
  21.8 1.5 collective-permute-start.9
  23.8 9.3 %collective-permute-done.1.refs_3_ = bf16[1024,256]{1,0:T(8,128)(2,1)} collective-permute-done((bf16[1024,256]{1,0:T(8,128)(2,1)}, bf16[1024,256]{1,0:T(8,128)(2,1)}, u32[]{:S(2)}, u32[]{:S(2)}) %collective-permute-start.1) | collective-permute-done | bytes 524320 | tf_op jit(solution)/shard_map/ppermute | solution.py:31
  33.8 2.5 %dynamic-slice_bitcast_fusion = (bf16[192,2560]{1,0:T(8,128)(2,1)S(1)}, bf16[192,2560]{1,0:T(8,128)(2,1)S(1)}, bf16[192,2560]{1,0:T(8,128)(2,1)S(1)}, bf16[192,2560]{1,0:T(8,128)(2,1)S(1)}) fusion(bf16[1,192,16384]{2,1,0:T(8,128)(2,1)} %param.7, s32[]{:T(128)S(6)} %select_n.42, s32[]{:T(128)S(6)} %select_n.40, s32[]{:T(128)S(6)} %select_n.39, s32[]{:T(128)S(6)} %select_n.41), kind=kLoop, calls=%fused_computation.2 | loop fusion | bytes 7864336 | tf_op jit(solution)/shard_map/dynamic_slice | solution.py:461
  37.8 3.2 %project.2.refs_0_ = f32[192,256]{1,0:T(8,128)S(1)} custom-call(s32[3]{0:T(128)S(1)} %pad_add_fusion.ids, bf16[192,16384]{1,0:T(8,128)(2,1)S(1)} %bitcast.19, bf16[4096,128]{1,0:T(8,128)(2,1)S(1)} %copy-done, bf16[4096,128]{1,0:T(8,128)(2,1)S(1)} %copy-done.1, bf16[1024,256]{1,0:T(8,128)(2,1)S(1)} %collective-permute-done.refs_2_, ...), custom_call_target="tpu_custom_call" | custom-call | bytes 16777216 | tf_op jit(solution)/shard_map/project/pallas_call | solution.py:47
  41.0 1.8 %collective-permute-done.9.refs_2_ = bf16[1024,256]{1,0:T(8,128)(2,1)S(1)} collective-permute-done((bf16[1024,256]{1,0:T(8,128)(2,1)S(1)}, bf16[1024,256]{1,0:T(8,128)(2,1)S(1)}, u32[]{:S(2)}, u32[]{:S(2)}) %collective-permute-start.9) | collective-permute-done | bytes 524320 | tf_op jit(solution)/shard_map/ppermute | solution.py:31
  43.7 1.1 collective-permute-done.10.refs_3_
  45.6 1.5 collective-permute-start.19
  47.1 1.1 project.3.refs_0_
  48.2 1.6 %collective-permute-start.12 = (bf16[192,256]{1,0:T(8,128)(2,1)S(1)}, bf16[192,256]{1,0:T(8,128)(2,1)S(1)}, u32[]{:S(2)}, u32[]{:S(2)}) collective-permute-start(bf16[192,256]{1,0:T(8,128)(2,1)S(1)} %project.3.refs_0_), channel_id=1, source_target_pairs={{0,2},{1,3},{2,0},{3,1},{4,6},{5,7},{6,4},{7,5},{8,10},{9,11},{10,... | collective-permute-start | bytes 294920 | tf_op jit(solution)/shard_map/ppermute | solution.py:31
  49.9 2.6 %collective-permute-start.13 = (bf16[192,256]{1,0:T(8,128)(2,1)S(1)}, bf16[192,256]{1,0:T(8,128)(2,1)S(1)}, u32[]{:S(2)}, u32[]{:S(2)}) collective-permute-start(bf16[192,256]{1,0:T(8,128)(2,1)S(1)} %project.3.refs_0_), channel_id=1, source_target_pairs={{0,4},{1,5},{2,6},{3,7},{4,0},{5,1},{6,2},{7,3},{8,12},{9,13},{10,... | collective-permute-start | bytes 294920 | tf_op jit(solution)/shard_map/ppermute | solution.py:31
  52.9 7.4 %collective-permute-done.13.refs_4_ = bf16[192,256]{1,0:T(8,128)(2,1)S(1)} collective-permute-done((bf16[192,256]{1,0:T(8,128)(2,1)S(1)}, bf16[192,256]{1,0:T(8,128)(2,1)S(1)}, u32[]{:S(2)}, u32[]{:S(2)}) %collective-permute-start.13) | collective-permute-done | bytes 98336 | tf_op jit(solution)/shard_map/ppermute | solution.py:31
  63.7 8.9 %attention.1 = (bf16[192,1024]{1,0:T(8,128)(2,1)}, f32[768,256]{1,0:T(8,128)S(1)}, bf16[768,256]{1,0:T(8,128)(2,1)S(1)}) custom-call(s32[1]{0:T(128)} %bitcast.ids, s32[16]{0:T(128)S(1)} %copy-done.4, s32[8]{0:T(128)S(1)} %bitcast.24, bf16[192,1024]{1,0:T(8,128)(2,1)S(1)} %bitcast.22, bf16[192,1024]{1,0:T(8,128)(2,1)S(1)} %bitcast.23, ...), custom_call_target="tpu_custom_call" | custom-call | tf_op jit(solution)/shard_map/attention/pallas_call | solution.py:168
  73.0 1.4 collective-permute-done.21.came
  74.4 1.7 %collective-permute-start.22 = (bf16[192,256]{1,0:T(8,128)(2,1)S(1)}, bf16[192,256]{1,0:T(8,128)(2,1)S(1)}, u32[]{:S(2)}, u32[]{:S(2)}) collective-permute-start(bf16[192,256]{1,0:T(8,128)(2,1)S(1)} %get-tuple-element.84), channel_id=1, source_target_pairs={{0,2},{1,3},{2,0},{3,1},{4,6},{5,7},{6,4},{7,5},{8,10},{9,11},{10,... | collective-permute-start | bytes 294920 | tf_op jit(solution)/shard_map/ppermute | solution.py:31
  76.1 1.4 collective-permute-start.23
  77.5 1.4 collective-permute-start.24
  79.5 7.3 %collective-permute-done.23.refs_2_ = bf16[192,256]{1,0:T(8,128)(2,1)S(1)} collective-permute-done((bf16[192,256]{1,0:T(8,128)(2,1)S(1)}, bf16[192,256]{1,0:T(8,128)(2,1)S(1)}, u32[]{:S(2)}, u32[]{:S(2)}) %collective-permute-start.23) | collective-permute-done | bytes 98336 | tf_op jit(solution)/shard_map/ppermute | solution.py:31
  86.9 1.7 %weight_rows.3 = (bf16[3072,256]{1,0:T(8,128)(2,1)S(1)}, bf16[3072,256]{1,0:T(8,128)(2,1)S(1)}) custom-call(s32[3]{0:T(128)S(1)} %pad_add_fusion.ids, bf16[192,16384]{1,0:T(8,128)(2,1)S(1)} %bitcast.21, bf16[192,256]{1,0:T(8,128)(2,1)S(1)} %total.1.refs_1_.refs_4_), custom_call_target="tpu_custom_call" | custom-call | tf_op jit(solution)/shard_map/weight_rows/pallas_call | solution.py:47
  88.7 1.5 collective-permute-start.26
  90.2 1.5 collective-permute-start.27
  92.2 2.4 %collective-permute-start.30 = (bf16[192,512]{1,0:T(8,128)(2,1)S(1)}, bf16[192,512]{1,0:T(8,128)(2,1)S(1)}, u32[]{:S(2)}, u32[]{:S(2)}) collective-permute-start(bf16[192,512]{1,0:T(8,128)(2,1)S(1)} %slice.47), channel_id=1, source_target_pairs={{0,24},{8,16},{16,8},{24,0},{1,25},{9,17},{17,9},{25,1},{2,26},{10... | collective-permute-start | bytes 589832 | tf_op jit(solution)/shard_map/ppermute | solution.py:31
  95.3 5.2 %collective-permute-done.27.refs_6_ = bf16[192,256]{1,0:T(8,128)(2,1)S(1)} collective-permute-done((bf16[192,256]{1,0:T(8,128)(2,1)S(1)}, bf16[192,256]{1,0:T(8,128)(2,1)S(1)}, u32[]{:S(2)}, u32[]{:S(2)}) %collective-permute-start.27) | collective-permute-done | bytes 98336 | tf_op jit(solution)/shard_map/ppermute | solution.py:31
  100.5 1.0 collective-permute-done.30.refs_3_
  101.5 1.9 %weight_rows.5 = (bf16[1024,256]{1,0:T(8,128)(2,1)S(1)}, bf16[1024,256]{1,0:T(8,128)(2,1)S(1)}) custom-call(s32[3]{0:T(128)S(1)} %pad_add_fusion.ids, bf16[192,2560]{1,0:T(8,128)(2,1)S(1)} %get-tuple-element.121.refs_0_, bf16[192,2560]{1,0:T(8,128)(2,1)S(1)} %collective-permute-done.19.refs_1_, bf16[192,2560]{1,0:T(8,128)(2,1)S(1)} %collective-permute-done.20.refs_2_, ...), custom_call_target="tpu_custom_call" | custom-call | tf_op jit(solution)/shard_map/weight_rows/pallas_call | solution.py:47
  103.5 1.0 weight_rows.4
  105.5 1.9 %collective-permute-start.33 = (bf16[512,256]{1,0:T(8,128)(2,1)S(1)}, bf16[512,256]{1,0:T(8,128)(2,1)S(1)}, u32[]{:S(2)}, u32[]{:S(2)}) collective-permute-start(bf16[512,256]{1,0:T(8,128)(2,1)S(1)} %slice.73), channel_id=1, source_target_pairs={{0,2},{1,3},{2,0},{3,1},{4,6},{5,7},{6,4},{7,5},{8,10},{9,11},{10,... | collective-permute-start | bytes 786440 | tf_op jit(solution)/shard_map/ppermute | solution.py:31
  107.4 1.2 collective-permute-start.37
  109.5 1.4 collective-permute-start.39
  111.0 3.1 %collective-permute-done.33 = bf16[512,256]{1,0:T(8,128)(2,1)S(1)} collective-permute-done((bf16[512,256]{1,0:T(8,128)(2,1)S(1)}, bf16[512,256]{1,0:T(8,128)(2,1)S(1)}, u32[]{:S(2)}, u32[]{:S(2)}) %collective-permute-start.33) | collective-permute-done | bytes 262176 | tf_op jit(solution)/shard_map/ppermute | solution.py:31
  114.1 1.8 %collective-permute-start.34 = (bf16[128,256]{1,0:T(8,128)(2,1)S(1)}, bf16[128,256]{1,0:T(8,128)(2,1)S(1)}, u32[]{:S(2)}, u32[]{:S(2)}) collective-permute-start(bf16[128,256]{1,0:T(8,128)(2,1)S(1)} %slice.75), channel_id=1, source_target_pairs={{0,2},{1,3},{2,0},{3,1},{4,6},{5,7},{6,4},{7,5},{8,10},{9,11},{10,... | collective-permute-start | bytes 196616 | tf_op jit(solution)/shard_map/ppermute | solution.py:31
  116.0 1.6 collective-permute-start.36
  117.5 0.9 collective-permute-done.34
  118.5 3.6 %collective-permute-start.35 = (bf16[128,256]{1,0:T(8,128)(2,1)S(1)}, bf16[128,256]{1,0:T(8,128)(2,1)S(1)}, u32[]{:S(2)}, u32[]{:S(2)}) collective-permute-start(bf16[128,256]{1,0:T(8,128)(2,1)S(1)} %fusion), channel_id=1, source_target_pairs={{0,4},{1,5},{2,6},{3,7},{4,0},{5,1},{6,2},{7,3},{8,12},{9,13},{10,... | collective-permute-start | bytes 196616 | tf_op jit(solution)/shard_map/ppermute | solution.py:31
  122.1 4.0 %collective-permute-done.38 = bf16[768,256]{1,0:T(8,128)(2,1)S(1)} collective-permute-done((bf16[768,256]{1,0:T(8,128)(2,1)S(1)}, bf16[768,256]{1,0:T(8,128)(2,1)S(1)}, u32[]{:S(2)}, u32[]{:S(2)}) %collective-permute-start.38) | collective-permute-done | bytes 393248 | tf_op jit(solution)/shard_map/ppermute | solution.py:31
  126.1 1.6 collective-permute-done.39
  128.3 4.3 %collective-permute-done.35 = bf16[128,256]{1,0:T(8,128)(2,1)S(1)} collective-permute-done((bf16[128,256]{1,0:T(8,128)(2,1)S(1)}, bf16[128,256]{1,0:T(8,128)(2,1)S(1)}, u32[]{:S(2)}, u32[]{:S(2)}) %collective-permute-start.35) | collective-permute-done | bytes 65568 | tf_op jit(solution)/shard_map/ppermute | solution.py:31
  132.7 4.0 %collective-permute-done.40 = bf16[384,256]{1,0:T(8,128)(2,1)S(1)} collective-permute-done((bf16[384,256]{1,0:T(8,128)(2,1)S(1)}, bf16[384,256]{1,0:T(8,128)(2,1)S(1)}, u32[]{:S(2)}, u32[]{:S(2)}) %collective-permute-start.40) | collective-permute-done | bytes 196640 | tf_op jit(solution)/shard_map/ppermute | solution.py:31
  136.9 3.0 %collective-permute-start.47 = (bf16[384,256]{1,0:T(8,128)(2,1)S(1)}, bf16[384,256]{1,0:T(8,128)(2,1)S(1)}, u32[]{:S(2)}, u32[]{:S(2)}) collective-permute-start(bf16[384,256]{1,0:T(8,128)(2,1)S(1)} %get-tuple-element.117), channel_id=1, source_target_pairs={{0,4},{1,5},{2,6},{3,7},{4,0},{5,1},{6,2},{7,3},{8,12},{9,13},{10,... | collective-permute-start | bytes 589832 | tf_op jit(solution)/shard_map/ppermute | solution.py:31
  139.9 10.7 %collective-permute-done.41.refs_1_ = bf16[128,256]{1,0:T(8,128)(2,1)S(1)} collective-permute-done((bf16[128,256]{1,0:T(8,128)(2,1)S(1)}, bf16[128,256]{1,0:T(8,128)(2,1)S(1)}, u32[]{:S(2)}, u32[]{:S(2)}) %collective-permute-start.41) | collective-permute-done | bytes 65568 | tf_op jit(solution)/shard_map/ppermute | solution.py:31
  153.5 2.2 %assemble.2 = (f32[4096,128]{1,0:T(8,128)}, f32[4096,128]{1,0:T(8,128)}) custom-call(s32[3]{0:T(128)S(1)} %pad_add_fusion.ids, bf16[128,256]{1,0:T(8,128)(2,1)S(1)} %add_convert_fusion.2.refs_0_, bf16[128,256]{1,0:T(8,128)(2,1)S(1)} %collective-permute-done.41.refs_1_, bf16[128,256]{1,0:T(8,128)(2,1)S(1)} %collective-permute-done.42.refs_2_, ...), custom_call_target="tpu_custom_call" | custom-call | tf_op jit(solution)/shard_map/assemble/pallas_call | solution.py:390
  155.7 3.7 %collective-permute-done.48.refs_3_ = bf16[384,256]{1,0:T(8,128)(2,1)S(1)} collective-permute-done((bf16[384,256]{1,0:T(8,128)(2,1)S(1)}, bf16[384,256]{1,0:T(8,128)(2,1)S(1)}, u32[]{:S(2)}, u32[]{:S(2)}) %collective-permute-start.48) | collective-permute-done | bytes 196640 | tf_op jit(solution)/shard_map/ppermute | solution.py:31
  159.4 1.4 collective-permute-done.50.refs_5_
  160.8 1.8 %assemble.3 = (f32[4096,128]{1,0:T(8,128)}, f32[4096,128]{1,0:T(8,128)}) custom-call(s32[3]{0:T(128)S(1)} %pad_add_fusion.ids, f32[4096,128]{1,0:T(8,128)} %get-tuple-element.111.refs_0_, f32[4096,128]{1,0:T(8,128)} %get-tuple-element.112.refs_1_, bf16[384,256]{1,0:T(8,128)(2,1)S(1)} %add_convert_fusion.1.refs_2_, ...), custom_call_target="tpu_custom_call", output_to_operand_aliasing={{0}: (1, {}), {1}: (2, {})} | custom-call | tf_op jit(solution)/shard_map/assemble/pallas_call | solution.py:390
  (103 shorter events, 18.4 us)
Async XLA Ops:
  2.9 15.9 %collective-permute-start.2 = (bf16[1024,256]{1,0:T(8,128)(2,1)}, bf16[1024,256]{1,0:T(8,128)(2,1)S(1)}, u32[]{:S(2)}, u32[]{:S(2)}) collective-permute-start(bf16[1024,256]{1,0:T(8,128)(2,1)} %pad_maximum_fusion.1), channel_id=1, source_target_pairs={{0,16},{8,24},{16,0},{24,8},{1,17},{9,25},{17,1},{25,9},{2,18},{10... | collective-permute-start | bytes 1572872 | tf_op jit(solution)/shard_map/ppermute | solution.py:31
  6.7 15.1 %collective-permute-start = (bf16[1024,256]{1,0:T(8,128)(2,1)}, bf16[1024,256]{1,0:T(8,128)(2,1)S(1)}, u32[]{:S(2)}, u32[]{:S(2)}) collective-permute-start(bf16[1024,256]{1,0:T(8,128)(2,1)} %pad_maximum_fusion), channel_id=1, source_target_pairs={{0,8},{8,0},{16,24},{24,16},{1,9},{9,1},{17,25},{25,17},{2,10},{10... | collective-permute-start | bytes 1572872 | tf_op jit(solution)/shard_map/ppermute | solution.py:31
  8.2 24.9 %collective-permute-start.1 = (bf16[1024,256]{1,0:T(8,128)(2,1)}, bf16[1024,256]{1,0:T(8,128)(2,1)}, u32[]{:S(2)}, u32[]{:S(2)}) collective-permute-start(bf16[1024,256]{1,0:T(8,128)(2,1)} %pad_maximum_fusion.1), channel_id=1, source_target_pairs={{0,8},{8,0},{16,24},{24,16},{1,9},{9,1},{17,25},{25,17},{2,10},{10... | collective-permute-start | bytes 1572872 | tf_op jit(solution)/shard_map/ppermute | solution.py:31
  8.8 24.4 %collective-permute-start.5 = (bf16[1024,256]{1,0:T(8,128)(2,1)}, bf16[1024,256]{1,0:T(8,128)(2,1)}, u32[]{:S(2)}, u32[]{:S(2)}) collective-permute-start(bf16[1024,256]{1,0:T(8,128)(2,1)} %pad_maximum_fusion), channel_id=1, source_target_pairs={{0,16},{8,24},{16,0},{24,8},{1,17},{9,25},{17,1},{25,9},{2,18},{10... | collective-permute-start | bytes 1572872 | tf_op jit(solution)/shard_map/ppermute | solution.py:31
  21.8 11.9 %collective-permute-start.3 = (bf16[1024,256]{1,0:T(8,128)(2,1)S(1)}, bf16[1024,256]{1,0:T(8,128)(2,1)}, u32[]{:S(2)}, u32[]{:S(2)}) collective-permute-start(bf16[1024,256]{1,0:T(8,128)(2,1)S(1)} %collective-permute-done.refs_2_), channel_id=1, source_target_pairs={{0,1},{1,0},{2,3},{3,2},{4,5},{5,4},{6,7},{7,6},{8,9},{9,8},{10,11... | collective-permute-start | bytes 1572872 | tf_op jit(solution)/shard_map/ppermute | solution.py:31
  21.8 21.0 %collective-permute-start.9 = (bf16[1024,256]{1,0:T(8,128)(2,1)S(1)}, bf16[1024,256]{1,0:T(8,128)(2,1)S(1)}, u32[]{:S(2)}, u32[]{:S(2)}) collective-permute-start(bf16[1024,256]{1,0:T(8,128)(2,1)S(1)} %collective-permute-done.2.refs_7_), channel_id=1, source_target_pairs={{0,8},{8,0},{16,24},{24,16},{1,9},{9,1},{17,25},{25,17},{2,10},{10... | collective-permute-start | bytes 1572872 | tf_op jit(solution)/shard_map/ppermute | solution.py:31
  23.3 19.5 %collective-permute-start.8 = (bf16[1024,256]{1,0:T(8,128)(2,1)S(1)}, bf16[1024,256]{1,0:T(8,128)(2,1)S(1)}, u32[]{:S(2)}, u32[]{:S(2)}) collective-permute-start(bf16[1024,256]{1,0:T(8,128)(2,1)S(1)} %collective-permute-done.refs_2_), channel_id=1, source_target_pairs={{0,16},{8,24},{16,0},{24,8},{1,17},{9,25},{17,1},{25,9},{2,18},{10... | collective-permute-start | bytes 1572872 | tf_op jit(solution)/shard_map/ppermute | solution.py:31
  33.1 3.2 %collective-permute-start.4 = (bf16[1024,256]{1,0:T(8,128)(2,1)}, bf16[1024,256]{1,0:T(8,128)(2,1)S(1)}, u32[]{:S(2)}, u32[]{:S(2)}) collective-permute-start(bf16[1024,256]{1,0:T(8,128)(2,1)} %collective-permute-done.1.refs_3_), channel_id=1, source_target_pairs={{0,1},{1,0},{2,3},{3,2},{4,5},{5,4},{6,7},{7,6},{8,9},{9,8},{10,11... | collective-permute-start | bytes 1572872 | tf_op jit(solution)/shard_map/ppermute | solution.py:31
  33.2 3.6 %collective-permute-start.6 = (bf16[1024,256]{1,0:T(8,128)(2,1)}, bf16[1024,256]{1,0:T(8,128)(2,1)S(1)}, u32[]{:S(2)}, u32[]{:S(2)}) collective-permute-start(bf16[1024,256]{1,0:T(8,128)(2,1)} %collective-permute-done.5.refs_6_), channel_id=1, source_target_pairs={{0,1},{1,0},{2,3},{3,2},{4,5},{5,4},{6,7},{7,6},{8,9},{9,8},{10,11... | collective-permute-start | bytes 1572872 | tf_op jit(solution)/shard_map/ppermute | solution.py:31
  33.7 3.1 %collective-permute-start.7 = (bf16[1024,256]{1,0:T(8,128)(2,1)S(1)}, bf16[1024,256]{1,0:T(8,128)(2,1)S(1)}, u32[]{:S(2)}, u32[]{:S(2)}) collective-permute-start(bf16[1024,256]{1,0:T(8,128)(2,1)S(1)} %collective-permute-done.2.refs_7_), channel_id=1, source_target_pairs={{0,1},{1,0},{2,3},{3,2},{4,5},{5,4},{6,7},{7,6},{8,9},{9,8},{10,11... | collective-permute-start | bytes 1572872 | tf_op jit(solution)/shard_map/ppermute | solution.py:31
  42.8 2.0 %collective-permute-start.10 = (bf16[1024,256]{1,0:T(8,128)(2,1)S(1)}, bf16[1024,256]{1,0:T(8,128)(2,1)S(1)}, u32[]{:S(2)}, u32[]{:S(2)}) collective-permute-start(bf16[1024,256]{1,0:T(8,128)(2,1)S(1)} %collective-permute-done.8.refs_1_), channel_id=1, source_target_pairs={{0,1},{1,0},{2,3},{3,2},{4,5},{5,4},{6,7},{7,6},{8,9},{9,8},{10,11... | collective-permute-start | bytes 1572872 | tf_op jit(solution)/shard_map/ppermute | solution.py:31
  42.9 2.6 %collective-permute-start.11 = (bf16[1024,256]{1,0:T(8,128)(2,1)S(1)}, bf16[1024,256]{1,0:T(8,128)(2,1)S(1)}, u32[]{:S(2)}, u32[]{:S(2)}) collective-permute-start(bf16[1024,256]{1,0:T(8,128)(2,1)S(1)} %collective-permute-done.9.refs_2_), channel_id=1, source_target_pairs={{0,1},{1,0},{2,3},{3,2},{4,5},{5,4},{6,7},{7,6},{8,9},{9,8},{10,11... | collective-permute-start | bytes 1572872 | tf_op jit(solution)/shard_map/ppermute | solution.py:31
  43.4 29.2 %collective-permute-start.20 = (bf16[192,2560]{1,0:T(8,128)(2,1)S(1)}, bf16[192,2560]{1,0:T(8,128)(2,1)S(1)}, u32[]{:S(2)}, u32[]{:S(2)}) collective-permute-start(bf16[192,2560]{1,0:T(8,128)(2,1)S(1)} %get-tuple-element.78), channel_id=1, source_target_pairs={{0,16},{8,24},{16,0},{24,8},{1,17},{9,25},{17,1},{25,9},{2,18},{10... | collective-permute-start | bytes 2949128 | tf_op jit(solution)/shard_map/ppermute | solution.py:31
  45.6 27.0 %collective-permute-start.19 = (bf16[192,2560]{1,0:T(8,128)(2,1)S(1)}, bf16[192,2560]{1,0:T(8,128)(2,1)S(1)}, u32[]{:S(2)}, u32[]{:S(2)}) collective-permute-start(bf16[192,2560]{1,0:T(8,128)(2,1)S(1)} %get-tuple-element.77), channel_id=1, source_target_pairs={{0,8},{8,0},{16,24},{24,16},{1,9},{9,1},{17,25},{25,17},{2,10},{10... | collective-permute-start | bytes 2949128 | tf_op jit(solution)/shard_map/ppermute | solution.py:31
  48.2 4.7 %collective-permute-start.12 = (bf16[192,256]{1,0:T(8,128)(2,1)S(1)}, bf16[192,256]{1,0:T(8,128)(2,1)S(1)}, u32[]{:S(2)}, u32[]{:S(2)}) collective-permute-start(bf16[192,256]{1,0:T(8,128)(2,1)S(1)} %project.3.refs_0_), channel_id=1, source_target_pairs={{0,2},{1,3},{2,0},{3,1},{4,6},{5,7},{6,4},{7,5},{8,10},{9,11},{10,... | collective-permute-start | bytes 294920 | tf_op jit(solution)/shard_map/ppermute | solution.py:31
  49.9 10.4 %collective-permute-start.13 = (bf16[192,256]{1,0:T(8,128)(2,1)S(1)}, bf16[192,256]{1,0:T(8,128)(2,1)S(1)}, u32[]{:S(2)}, u32[]{:S(2)}) collective-permute-start(bf16[192,256]{1,0:T(8,128)(2,1)S(1)} %project.3.refs_0_), channel_id=1, source_target_pairs={{0,4},{1,5},{2,6},{3,7},{4,0},{5,1},{6,2},{7,3},{8,12},{9,13},{10,... | collective-permute-start | bytes 294920 | tf_op jit(solution)/shard_map/ppermute | solution.py:31
  52.4 7.8 %collective-permute-start.14 = (bf16[192,256]{1,0:T(8,128)(2,1)S(1)}, bf16[192,256]{1,0:T(8,128)(2,1)S(1)}, u32[]{:S(2)}, u32[]{:S(2)}) collective-permute-start(bf16[192,256]{1,0:T(8,128)(2,1)S(1)} %project.3.refs_0_), channel_id=1, source_target_pairs={{0,6},{1,7},{2,4},{3,5},{4,2},{5,3},{6,0},{7,1},{8,14},{9,15},{10,... | collective-permute-start | bytes 294920 | tf_op jit(solution)/shard_map/ppermute | solution.py:31
  60.4 26.5 %collective-permute-start.25 = (bf16[192,2048]{1,0:T(8,128)(2,1)S(1)}, bf16[192,2048]{1,0:T(8,128)(2,1)S(1)}, u32[]{:S(2)}, u32[]{:S(2)}) collective-permute-start(bf16[192,2048]{1,0:T(8,128)(2,1)S(1)} %slice.42), channel_id=1, source_target_pairs={{0,24},{8,16},{16,8},{24,0},{1,25},{9,17},{17,9},{25,1},{2,26},{10... | collective-permute-start | bytes 2359304 | tf_op jit(solution)/shard_map/ppermute | solution.py:31
  60.9 1.5 collective-permute-start.16
  62.4 1.3 collective-permute-start.18
  72.6 1.7 %collective-permute-start.21 = (bf16[768,256]{1,0:T(8,128)(2,1)S(1)}, bf16[768,256]{1,0:T(8,128)(2,1)S(1)}, u32[]{:S(2)}, u32[]{:S(2)}) collective-permute-start(bf16[768,256]{1,0:T(8,128)(2,1)S(1)} %get-tuple-element.82), channel_id=1, source_target_pairs={{0,1},{1,0},{2,3},{3,2},{4,5},{5,4},{6,7},{7,6},{8,9},{9,8},{10,11... | collective-permute-start | bytes 1179656 | tf_op jit(solution)/shard_map/ppermute | solution.py:31
  74.4 5.1 %collective-permute-start.22 = (bf16[192,256]{1,0:T(8,128)(2,1)S(1)}, bf16[192,256]{1,0:T(8,128)(2,1)S(1)}, u32[]{:S(2)}, u32[]{:S(2)}) collective-permute-start(bf16[192,256]{1,0:T(8,128)(2,1)S(1)} %get-tuple-element.84), channel_id=1, source_target_pairs={{0,2},{1,3},{2,0},{3,1},{4,6},{5,7},{6,4},{7,5},{8,10},{9,11},{10,... | collective-permute-start | bytes 294920 | tf_op jit(solution)/shard_map/ppermute | solution.py:31
  76.1 10.7 %collective-permute-start.23 = (bf16[192,256]{1,0:T(8,128)(2,1)S(1)}, bf16[192,256]{1,0:T(8,128)(2,1)S(1)}, u32[]{:S(2)}, u32[]{:S(2)}) collective-permute-start(bf16[192,256]{1,0:T(8,128)(2,1)S(1)} %get-tuple-element.85), channel_id=1, source_target_pairs={{0,4},{1,5},{2,6},{3,7},{4,0},{5,1},{6,2},{7,3},{8,12},{9,13},{10,... | collective-permute-start | bytes 294920 | tf_op jit(solution)/shard_map/ppermute | solution.py:31
  77.5 9.3 %collective-permute-start.24 = (bf16[192,256]{1,0:T(8,128)(2,1)S(1)}, bf16[192,256]{1,0:T(8,128)(2,1)S(1)}, u32[]{:S(2)}, u32[]{:S(2)}) collective-permute-start(bf16[192,256]{1,0:T(8,128)(2,1)S(1)} %get-tuple-element.86), channel_id=1, source_target_pairs={{0,6},{1,7},{2,4},{3,5},{4,2},{5,3},{6,0},{7,1},{8,14},{9,15},{10,... | collective-permute-start | bytes 294920 | tf_op jit(solution)/shard_map/ppermute | solution.py:31
  88.6 6.1 %collective-permute-start.29 = (bf16[3072,256]{1,0:T(8,128)(2,1)S(1)}, bf16[3072,256]{1,0:T(8,128)(2,1)S(1)}, u32[]{:S(2)}, u32[]{:S(2)}) collective-permute-start(bf16[3072,256]{1,0:T(8,128)(2,1)S(1)} %get-tuple-element.91), channel_id=1, source_target_pairs={{0,1},{1,0},{2,3},{3,2},{4,5},{5,4},{6,7},{7,6},{8,9},{9,8},{10,11... | collective-permute-start | bytes 4718600 | tf_op jit(solution)/shard_map/ppermute | solution.py:31
  88.7 6.6 %collective-permute-start.26 = (bf16[192,256]{1,0:T(8,128)(2,1)S(1)}, bf16[192,256]{1,0:T(8,128)(2,1)S(1)}, u32[]{:S(2)}, u32[]{:S(2)}) collective-permute-start(bf16[192,256]{1,0:T(8,128)(2,1)S(1)} %total.1.refs_1_.refs_4_), channel_id=1, source_target_pairs={{0,8},{8,0},{16,24},{24,16},{1,9},{9,1},{17,25},{25,17},{2,10},{10... | collective-permute-start | bytes 294920 | tf_op jit(solution)/shard_map/ppermute | solution.py:31
  90.2 10.3 %collective-permute-start.27 = (bf16[192,256]{1,0:T(8,128)(2,1)S(1)}, bf16[192,256]{1,0:T(8,128)(2,1)S(1)}, u32[]{:S(2)}, u32[]{:S(2)}) collective-permute-start(bf16[192,256]{1,0:T(8,128)(2,1)S(1)} %total.1.refs_1_.refs_4_), channel_id=1, source_target_pairs={{0,16},{8,24},{16,0},{24,8},{1,17},{9,25},{17,1},{25,9},{2,18},{10... | collective-permute-start | bytes 294920 | tf_op jit(solution)/shard_map/ppermute | solution.py:31
  91.7 8.8 %collective-permute-start.28 = (bf16[192,256]{1,0:T(8,128)(2,1)S(1)}, bf16[192,256]{1,0:T(8,128)(2,1)S(1)}, u32[]{:S(2)}, u32[]{:S(2)}) collective-permute-start(bf16[192,256]{1,0:T(8,128)(2,1)S(1)} %total.1.refs_1_.refs_4_), channel_id=1, source_target_pairs={{0,24},{8,16},{16,8},{24,0},{1,25},{9,17},{17,9},{25,1},{2,26},{10... | collective-permute-start | bytes 294920 | tf_op jit(solution)/shard_map/ppermute | solution.py:31
  92.2 9.2 %collective-permute-start.30 = (bf16[192,512]{1,0:T(8,128)(2,1)S(1)}, bf16[192,512]{1,0:T(8,128)(2,1)S(1)}, u32[]{:S(2)}, u32[]{:S(2)}) collective-permute-start(bf16[192,512]{1,0:T(8,128)(2,1)S(1)} %slice.47), channel_id=1, source_target_pairs={{0,24},{8,16},{16,8},{24,0},{1,25},{9,17},{17,9},{25,1},{2,26},{10... | collective-permute-start | bytes 589832 | tf_op jit(solution)/shard_map/ppermute | solution.py:31
  103.4 2.0 %collective-permute-start.32 = (bf16[1024,256]{1,0:T(8,128)(2,1)S(1)}, bf16[1024,256]{1,0:T(8,128)(2,1)S(1)}, u32[]{:S(2)}, u32[]{:S(2)}) collective-permute-start(bf16[1024,256]{1,0:T(8,128)(2,1)S(1)} %get-tuple-element.102), channel_id=1, source_target_pairs={{0,1},{1,0},{2,3},{3,2},{4,5},{5,4},{6,7},{7,6},{8,9},{9,8},{10,11... | collective-permute-start | bytes 1572872 | tf_op jit(solution)/shard_map/ppermute | solution.py:31
  104.5 6.4 %collective-permute-start.31 = (bf16[256,256]{1,0:T(8,128)(2,1)S(1)}, bf16[256,256]{1,0:T(8,128)(2,1)S(1)}, u32[]{:S(2)}, u32[]{:S(2)}) collective-permute-start(bf16[256,256]{1,0:T(8,128)(2,1)S(1)} %get-tuple-element.99), channel_id=1, source_target_pairs={{0,1},{1,0},{2,3},{3,2},{4,5},{5,4},{6,7},{7,6},{8,9},{9,8},{10,11... | collective-permute-start | bytes 393224 | tf_op jit(solution)/shard_map/ppermute | solution.py:31
  105.5 8.5 %collective-permute-start.33 = (bf16[512,256]{1,0:T(8,128)(2,1)S(1)}, bf16[512,256]{1,0:T(8,128)(2,1)S(1)}, u32[]{:S(2)}, u32[]{:S(2)}) collective-permute-start(bf16[512,256]{1,0:T(8,128)(2,1)S(1)} %slice.73), channel_id=1, source_target_pairs={{0,2},{1,3},{2,0},{3,1},{4,6},{5,7},{6,4},{7,5},{8,10},{9,11},{10,... | collective-permute-start | bytes 786440 | tf_op jit(solution)/shard_map/ppermute | solution.py:31
  107.4 14.7 %collective-permute-start.37 = (bf16[768,256]{1,0:T(8,128)(2,1)S(1)}, bf16[768,256]{1,0:T(8,128)(2,1)S(1)}, u32[]{:S(2)}, u32[]{:S(2)}) collective-permute-start(bf16[768,256]{1,0:T(8,128)(2,1)S(1)} %get-tuple-element.105), channel_id=1, source_target_pairs={{0,8},{8,0},{16,24},{24,16},{1,9},{9,1},{17,25},{25,17},{2,10},{10... | collective-permute-start | bytes 1179656 | tf_op jit(solution)/shard_map/ppermute | solution.py:31
  108.6 17.4 %collective-permute-start.38 = (bf16[768,256]{1,0:T(8,128)(2,1)S(1)}, bf16[768,256]{1,0:T(8,128)(2,1)S(1)}, u32[]{:S(2)}, u32[]{:S(2)}) collective-permute-start(bf16[768,256]{1,0:T(8,128)(2,1)S(1)} %get-tuple-element.106), channel_id=1, source_target_pairs={{0,16},{8,24},{16,0},{24,8},{1,17},{9,25},{17,1},{25,9},{2,18},{10... | collective-permute-start | bytes 1179656 | tf_op jit(solution)/shard_map/ppermute | solution.py:31
  109.5 18.2 %collective-permute-start.39 = (bf16[768,256]{1,0:T(8,128)(2,1)S(1)}, bf16[768,256]{1,0:T(8,128)(2,1)S(1)}, u32[]{:S(2)}, u32[]{:S(2)}) collective-permute-start(bf16[768,256]{1,0:T(8,128)(2,1)S(1)} %get-tuple-element.107), channel_id=1, source_target_pairs={{0,24},{8,16},{16,8},{24,0},{1,25},{9,17},{17,9},{25,1},{2,26},{10... | collective-permute-start | bytes 1179656 | tf_op jit(solution)/shard_map/ppermute | solution.py:31
  114.1 4.3 %collective-permute-start.34 = (bf16[128,256]{1,0:T(8,128)(2,1)S(1)}, bf16[128,256]{1,0:T(8,128)(2,1)S(1)}, u32[]{:S(2)}, u32[]{:S(2)}) collective-permute-start(bf16[128,256]{1,0:T(8,128)(2,1)S(1)} %slice.75), channel_id=1, source_target_pairs={{0,2},{1,3},{2,0},{3,1},{4,6},{5,7},{6,4},{7,5},{8,10},{9,11},{10,... | collective-permute-start | bytes 196616 | tf_op jit(solution)/shard_map/ppermute | solution.py:31
  116.0 16.7 %collective-permute-start.36 = (bf16[512,256]{1,0:T(8,128)(2,1)S(1)}, bf16[512,256]{1,0:T(8,128)(2,1)S(1)}, u32[]{:S(2)}, u32[]{:S(2)}) collective-permute-start(bf16[512,256]{1,0:T(8,128)(2,1)S(1)} %get-tuple-element.119), channel_id=1, source_target_pairs={{0,4},{1,5},{2,6},{3,7},{4,0},{5,1},{6,2},{7,3},{8,12},{9,13},{10,... | collective-permute-start | bytes 786440 | tf_op jit(solution)/shard_map/ppermute | solution.py:31
  118.5 14.1 %collective-permute-start.35 = (bf16[128,256]{1,0:T(8,128)(2,1)S(1)}, bf16[128,256]{1,0:T(8,128)(2,1)S(1)}, u32[]{:S(2)}, u32[]{:S(2)}) collective-permute-start(bf16[128,256]{1,0:T(8,128)(2,1)S(1)} %fusion), channel_id=1, source_target_pairs={{0,4},{1,5},{2,6},{3,7},{4,0},{5,1},{6,2},{7,3},{8,12},{9,13},{10,... | collective-permute-start | bytes 196616 | tf_op jit(solution)/shard_map/ppermute | solution.py:31
  127.9 8.8 %collective-permute-start.40 = (bf16[384,256]{1,0:T(8,128)(2,1)S(1)}, bf16[384,256]{1,0:T(8,128)(2,1)S(1)}, u32[]{:S(2)}, u32[]{:S(2)}) collective-permute-start(bf16[384,256]{1,0:T(8,128)(2,1)S(1)} %slice.74), channel_id=1, source_target_pairs={{0,2},{1,3},{2,0},{3,1},{4,6},{5,7},{6,4},{7,5},{8,10},{9,11},{10,... | collective-permute-start | bytes 589832 | tf_op jit(solution)/shard_map/ppermute | solution.py:31
  136.8 15.2 %collective-permute-start.44 = (bf16[512,256]{1,0:T(8,128)(2,1)S(1)}, bf16[512,256]{1,0:T(8,128)(2,1)S(1)}, u32[]{:S(2)}, u32[]{:S(2)}) collective-permute-start(bf16[512,256]{1,0:T(8,128)(2,1)S(1)} %add_convert_fusion.refs_4_), channel_id=1, source_target_pairs={{0,2},{1,3},{2,0},{3,1},{4,6},{5,7},{6,4},{7,5},{8,10},{9,11},{10,... | collective-permute-start | bytes 786440 | tf_op jit(solution)/shard_map/ppermute | solution.py:31
  136.9 15.1 %collective-permute-start.47 = (bf16[384,256]{1,0:T(8,128)(2,1)S(1)}, bf16[384,256]{1,0:T(8,128)(2,1)S(1)}, u32[]{:S(2)}, u32[]{:S(2)}) collective-permute-start(bf16[384,256]{1,0:T(8,128)(2,1)S(1)} %get-tuple-element.117), channel_id=1, source_target_pairs={{0,4},{1,5},{2,6},{3,7},{4,0},{5,1},{6,2},{7,3},{8,12},{9,13},{10,... | collective-permute-start | bytes 589832 | tf_op jit(solution)/shard_map/ppermute | solution.py:31
  139.9 10.8 %collective-permute-start.41 = (bf16[128,256]{1,0:T(8,128)(2,1)S(1)}, bf16[128,256]{1,0:T(8,128)(2,1)S(1)}, u32[]{:S(2)}, u32[]{:S(2)}) collective-permute-start(bf16[128,256]{1,0:T(8,128)(2,1)S(1)} %add_convert_fusion.2.refs_0_), channel_id=1, source_target_pairs={{0,2},{1,3},{2,0},{3,1},{4,6},{5,7},{6,4},{7,5},{8,10},{9,11},{10,... | collective-permute-start | bytes 196616 | tf_op jit(solution)/shard_map/ppermute | solution.py:31
  139.9 11.3 %collective-permute-start.42 = (bf16[128,256]{1,0:T(8,128)(2,1)S(1)}, bf16[128,256]{1,0:T(8,128)(2,1)S(1)}, u32[]{:S(2)}, u32[]{:S(2)}) collective-permute-start(bf16[128,256]{1,0:T(8,128)(2,1)S(1)} %add_convert_fusion.2.refs_0_), channel_id=1, source_target_pairs={{0,1},{1,0},{2,3},{3,2},{4,5},{5,4},{6,7},{7,6},{8,9},{9,8},{10,11... | collective-permute-start | bytes 196616 | tf_op jit(solution)/shard_map/ppermute | solution.py:31
  150.7 2.0 %collective-permute-start.45 = (bf16[512,256]{1,0:T(8,128)(2,1)S(1)}, bf16[512,256]{1,0:T(8,128)(2,1)S(1)}, u32[]{:S(2)}, u32[]{:S(2)}) collective-permute-start(bf16[512,256]{1,0:T(8,128)(2,1)S(1)} %add_convert_fusion.refs_4_), channel_id=1, source_target_pairs={{0,1},{1,0},{2,3},{3,2},{4,5},{5,4},{6,7},{7,6},{8,9},{9,8},{10,11... | collective-permute-start | bytes 786440 | tf_op jit(solution)/shard_map/ppermute | solution.py:31
  152.0 1.5 collective-permute-start.46
  152.2 7.2 %collective-permute-start.48 = (bf16[384,256]{1,0:T(8,128)(2,1)S(1)}, bf16[384,256]{1,0:T(8,128)(2,1)S(1)}, u32[]{:S(2)}, u32[]{:S(2)}) collective-permute-start(bf16[384,256]{1,0:T(8,128)(2,1)S(1)} %add_convert_fusion.1.refs_2_), channel_id=1, source_target_pairs={{0,2},{1,3},{2,0},{3,1},{4,6},{5,7},{6,4},{7,5},{8,10},{9,11},{10,... | collective-permute-start | bytes 589832 | tf_op jit(solution)/shard_map/ppermute | solution.py:31
  152.5 6.9 %collective-permute-start.49 = (bf16[384,256]{1,0:T(8,128)(2,1)S(1)}, bf16[384,256]{1,0:T(8,128)(2,1)S(1)}, u32[]{:S(2)}, u32[]{:S(2)}) collective-permute-start(bf16[384,256]{1,0:T(8,128)(2,1)S(1)} %add_convert_fusion.1.refs_2_), channel_id=1, source_target_pairs={{0,1},{1,0},{2,3},{3,2},{4,5},{5,4},{6,7},{7,6},{8,9},{9,8},{10,11... | collective-permute-start | bytes 589832 | tf_op jit(solution)/shard_map/ppermute | solution.py:31
  159.4 1.4 collective-permute-start.50
  (11 other events, 134.5 us)

commit v13 on v11

--- a/solution.py
+++ b/solution.py
@@ -12,7 +12,7 @@
 NO_COST = pl.CostEstimate(flops=0, bytes_accessed=0, transcendentals=0)
 
 
-MOVED = (4, 6)
+MOVED = (5, 6)
 TIED = 2
 
 
@@ -257,7 +257,7 @@
     z, core, dp = ids[0] % plan.sub_count, ids[1], ids[2]
     rows = plan.rows
     share = rows // plan.sub_count
-    tile = next(size for size in (512, 256, 128) if rows % size == 0)
+    tile = next(size for size in (768, 640, 512, 384, 256, 128) if rows % size == 0)
     step = math.gcd(share, tile)
     for side, out_ref in ((1, refs[-2]), (0, refs[-1])):
         for at, group in enumerate(plan.groups):
@@ -528,7 +528,7 @@
     last = sum_of_halves(part, sub_count, blocks)
     blocks += [one for final in finals[1:] for one in gather_parts(final, sub_count)]
     outs = assemble(ids, (), blocks, sub_count, regions[:-1], block_rows)
-    last = gather_parts(last, sub_count, outs)
+    last = gather_parts(last, sub_count)
     key_rows, value_rows = assemble(ids, outs, last, sub_count, regions[-1:], block_rows)
     return query_grad[None], key_rows, value_rows
 

time: 153 us -> 161 us (1.052)
  waiting for transfers between devices: 79.9 us -> 86.1 us
    ppermute x50, waiting for transfers between devices: 79.9 us -> 86.1 us  [swap(): return lax.ppermute(array, axis, [(i, i ^ distance) for i in range(count)])]
  transfers between devices with their start and end apart: 50 -> 50, of which waited for: 29 -> 27; matrix products, arithmetic and copies ran while one was open for 3% -> 3% of each run, Pallas kernels for 12% -> 12%
where the time goes in v13:
time: 161 us; the launch traced here: 160 us
  waiting for transfers between devices  86.1 us (53%)
  starting transfers between devices  43.1 us (27%)
  Pallas kernels  22 us (14%)
  local copies, waits for them, and re-layouts  5.38 us (3%)
  other arithmetic  2.67 us (2%)
    ppermute x50, waiting for transfers between devices, swap(): return lax.ppermute(array, axis, [(i, i ^ distance) for i in range(count)])  86.1 us
    ppermute x50, starting transfers between devices, swap(): return lax.ppermute(array, axis, [(i, i ^ distance) for i in range(count)])  43.1 us
    pallas_call x7, Pallas kernels, kernel_call(): pl.pallas_call(kernel, out_shape=outs, in_specs=[smem] * len(scalars) + [...  9.23 us
    pallas_call x1, Pallas kernels, attention(): pl.pallas_call(functools.partial(attention_kernel, shape), out_shape=(jax...  8.88 us
    pallas_call x2, Pallas kernels, assemble(): pl.pallas_call(functools.partial(assemble_kernel, sub_count, regions, not...  3.93 us
  transfers between devices with their start and end apart: 50, of which 27 were waited for; matrix products, arithmetic and copies ran while one was open for 3% of the time, Pallas kernels for 12%

profile of v13, /device:TPU:0, one launch (start us, length us, event | category | flops | bytes accessed | tf_op | source)
XLA Modules:
  0.0 160.4 jit_solution(14542379870217349604)
XLA Ops:
  0.7 1.4 constant_dynamic-slice_fusion
  2.9 2.9 %collective-permute-start = (bf16[1024,256]{1,0:T(8,128)(2,1)}, bf16[1024,256]{1,0:T(8,128)(2,1)S(1)}, u32[]{:S(2)}, u32[]{:S(2)}) collective-permute-start(bf16[1024,256]{1,0:T(8,128)(2,1)} %pad_maximum_fusion), channel_id=1, source_target_pairs={{0,8},{8,0},{16,24},{24,16},{1,9},{9,1},{17,25},{25,17},{2,10},{10... | collective-permute-start | bytes 1572872 | tf_op jit(solution)/shard_map/ppermute | solution.py:32
  6.7 1.5 collective-permute-start.2
  8.8 10.0 %collective-permute-done.refs_2_ = bf16[1024,256]{1,0:T(8,128)(2,1)S(1)} collective-permute-done((bf16[1024,256]{1,0:T(8,128)(2,1)}, bf16[1024,256]{1,0:T(8,128)(2,1)S(1)}, u32[]{:S(2)}, u32[]{:S(2)}) %collective-permute-start) | collective-permute-done | bytes 524320 | tf_op jit(solution)/shard_map/ppermute | solution.py:32
  18.8 3.0 %collective-permute-done.2.refs_7_ = bf16[1024,256]{1,0:T(8,128)(2,1)S(1)} collective-permute-done((bf16[1024,256]{1,0:T(8,128)(2,1)}, bf16[1024,256]{1,0:T(8,128)(2,1)S(1)}, u32[]{:S(2)}, u32[]{:S(2)}) %collective-permute-start.2) | collective-permute-done | bytes 524320 | tf_op jit(solution)/shard_map/ppermute | solution.py:32
  21.8 1.5 collective-permute-start.8
  23.8 9.3 %collective-permute-done.5.refs_6_ = bf16[1024,256]{1,0:T(8,128)(2,1)} collective-permute-done((bf16[1024,256]{1,0:T(8,128)(2,1)}, bf16[1024,256]{1,0:T(8,128)(2,1)}, u32[]{:S(2)}, u32[]{:S(2)}) %collective-permute-start.5) | collective-permute-done | bytes 524320 | tf_op jit(solution)/shard_map/ppermute | solution.py:32
  33.8 2.6 %dynamic-slice_bitcast_fusion = (bf16[192,2816]{1,0:T(8,128)(2,1)S(1)}, bf16[192,2816]{1,0:T(8,128)(2,1)S(1)}, bf16[192,2816]{1,0:T(8,128)(2,1)S(1)}, bf16[192,2816]{1,0:T(8,128)(2,1)S(1)}) fusion(bf16[1,192,16384]{2,1,0:T(8,128)(2,1)} %param.7, s32[]{:T(128)S(6)} %select_n.42, s32[]{:T(128)S(6)} %select_n.40, s32[]{:T(128)S(6)} %select_n.39, s32[]{:T(128)S(6)} %select_n.41), kind=kLoop, calls=%fused_computation.1 | loop fusion | bytes 8650768 | tf_op jit(solution)/shard_map/dynamic_slice | solution.py:462
  37.9 3.2 %project.2.refs_0_ = f32[192,256]{1,0:T(8,128)S(1)} custom-call(s32[3]{0:T(128)S(1)} %pad_add_fusion.ids, bf16[192,16384]{1,0:T(8,128)(2,1)S(1)} %bitcast.19, bf16[4096,128]{1,0:T(8,128)(2,1)S(1)} %copy-done, bf16[4096,128]{1,0:T(8,128)(2,1)S(1)} %copy-done.1, bf16[1024,256]{1,0:T(8,128)(2,1)S(1)} %collective-permute-done.refs_2_, ...), custom_call_target="tpu_custom_call" | custom-call | bytes 16777216 | tf_op jit(solution)/shard_map/project/pallas_call | solution.py:48
  41.1 1.7 %collective-permute-done.8.refs_1_ = bf16[1024,256]{1,0:T(8,128)(2,1)S(1)} collective-permute-done((bf16[1024,256]{1,0:T(8,128)(2,1)S(1)}, bf16[1024,256]{1,0:T(8,128)(2,1)S(1)}, u32[]{:S(2)}, u32[]{:S(2)}) %collective-permute-start.8) | collective-permute-done | bytes 524320 | tf_op jit(solution)/shard_map/ppermute | solution.py:32
  43.4 1.5 collective-permute-start.20
  45.9 1.2 project.3.refs_0_
  47.0 3.9 %collective-permute-start.14 = (bf16[192,256]{1,0:T(8,128)(2,1)S(1)}, bf16[192,256]{1,0:T(8,128)(2,1)S(1)}, u32[]{:S(2)}, u32[]{:S(2)}) collective-permute-start(bf16[192,256]{1,0:T(8,128)(2,1)S(1)} %project.3.refs_0_), channel_id=1, source_target_pairs={{0,6},{1,7},{2,4},{3,5},{4,2},{5,3},{6,0},{7,1},{8,14},{9,15},{10,... | collective-permute-start | bytes 294920 | tf_op jit(solution)/shard_map/ppermute | solution.py:32
  51.5 3.1 %collective-permute-done.14.refs_6_ = bf16[192,256]{1,0:T(8,128)(2,1)S(1)} collective-permute-done((bf16[192,256]{1,0:T(8,128)(2,1)S(1)}, bf16[192,256]{1,0:T(8,128)(2,1)S(1)}, u32[]{:S(2)}, u32[]{:S(2)}) %collective-permute-start.14) | collective-permute-done | bytes 98336 | tf_op jit(solution)/shard_map/ppermute | solution.py:32
  54.6 4.6 %collective-permute-done.13.refs_4_ = bf16[192,256]{1,0:T(8,128)(2,1)S(1)} collective-permute-done((bf16[192,256]{1,0:T(8,128)(2,1)S(1)}, bf16[192,256]{1,0:T(8,128)(2,1)S(1)}, u32[]{:S(2)}, u32[]{:S(2)}) %collective-permute-start.13) | collective-permute-done | bytes 98336 | tf_op jit(solution)/shard_map/ppermute | solution.py:32
  59.2 2.4 %collective-permute-start.28 = (bf16[192,2816]{1,0:T(8,128)(2,1)S(1)}, bf16[192,2816]{1,0:T(8,128)(2,1)S(1)}, u32[]{:S(2)}, u32[]{:S(2)}) collective-permute-start(bf16[192,2816]{1,0:T(8,128)(2,1)S(1)} %get-tuple-element.83), channel_id=1, source_target_pairs={{0,24},{8,16},{16,8},{24,0},{1,25},{9,17},{17,9},{25,1},{2,26},{10... | collective-permute-start | bytes 3244040 | tf_op jit(solution)/shard_map/ppermute | solution.py:32
  64.4 8.9 %attention.1 = (bf16[192,1024]{1,0:T(8,128)(2,1)}, f32[768,256]{1,0:T(8,128)S(1)}, bf16[768,256]{1,0:T(8,128)(2,1)S(1)}) custom-call(s32[1]{0:T(128)} %bitcast.ids, s32[16]{0:T(128)S(1)} %copy-done.4, s32[8]{0:T(128)S(1)} %bitcast.24, bf16[192,1024]{1,0:T(8,128)(2,1)S(1)} %bitcast.22, bf16[192,1024]{1,0:T(8,128)(2,1)S(1)} %bitcast.23, ...), custom_call_target="tpu_custom_call" | custom-call | tf_op jit(solution)/shard_map/attention/pallas_call | solution.py:169
  73.7 1.4 collective-permute-done.21.came
  75.7 2.6 %collective-permute-start.23 = (bf16[192,256]{1,0:T(8,128)(2,1)S(1)}, bf16[192,256]{1,0:T(8,128)(2,1)S(1)}, u32[]{:S(2)}, u32[]{:S(2)}) collective-permute-start(bf16[192,256]{1,0:T(8,128)(2,1)S(1)} %get-tuple-element.80), channel_id=1, source_target_pairs={{0,4},{1,5},{2,6},{3,7},{4,0},{5,1},{6,2},{7,3},{8,12},{9,13},{10,... | collective-permute-start | bytes 294920 | tf_op jit(solution)/shard_map/ppermute | solution.py:32
  78.3 1.3 collective-permute-start.24
  79.6 2.1 %collective-permute-done.22.refs_1_ = bf16[192,256]{1,0:T(8,128)(2,1)S(1)} collective-permute-done((bf16[192,256]{1,0:T(8,128)(2,1)S(1)}, bf16[192,256]{1,0:T(8,128)(2,1)S(1)}, u32[]{:S(2)}, u32[]{:S(2)}) %collective-permute-start.22) | collective-permute-done | bytes 98336 | tf_op jit(solution)/shard_map/ppermute | solution.py:32
  81.7 4.8 %collective-permute-done.23.refs_2_ = bf16[192,256]{1,0:T(8,128)(2,1)S(1)} collective-permute-done((bf16[192,256]{1,0:T(8,128)(2,1)S(1)}, bf16[192,256]{1,0:T(8,128)(2,1)S(1)}, u32[]{:S(2)}, u32[]{:S(2)}) %collective-permute-start.23) | collective-permute-done | bytes 98336 | tf_op jit(solution)/shard_map/ppermute | solution.py:32
  86.6 1.4 collective-permute-start.27
  88.6 1.5 collective-permute-start.25
  90.1 6.3 %collective-permute-done.28.refs_3_ = bf16[192,2816]{1,0:T(8,128)(2,1)S(1)} collective-permute-done((bf16[192,2816]{1,0:T(8,128)(2,1)S(1)}, bf16[192,2816]{1,0:T(8,128)(2,1)S(1)}, u32[]{:S(2)}, u32[]{:S(2)}) %collective-permute-start.28) | collective-permute-done | bytes 1081376 | tf_op jit(solution)/shard_map/ppermute | solution.py:32
  96.5 2.1 %collective-permute-done.27.refs_7_ = bf16[192,256]{1,0:T(8,128)(2,1)S(1)} collective-permute-done((bf16[192,256]{1,0:T(8,128)(2,1)S(1)}, bf16[192,256]{1,0:T(8,128)(2,1)S(1)}, u32[]{:S(2)}, u32[]{:S(2)}) %collective-permute-start.27) | collective-permute-done | bytes 98336 | tf_op jit(solution)/shard_map/ppermute | solution.py:32
  98.5 1.3 collective-permute-done.26.refs_6_
  99.8 1.6 %weight_rows.5 = (bf16[2560,256]{1,0:T(8,128)(2,1)S(1)}, bf16[2560,256]{1,0:T(8,128)(2,1)S(1)}) custom-call(s32[3]{0:T(128)S(1)} %pad_add_fusion.ids, bf16[192,16384]{1,0:T(8,128)(2,1)S(1)} %bitcast.21, bf16[192,256]{1,0:T(8,128)(2,1)S(1)} %total.1.refs_4_.refs_1_), custom_call_target="tpu_custom_call" | custom-call | tf_op jit(solution)/shard_map/weight_rows/pallas_call | solution.py:48
  101.5 1.5 weight_rows.3
  103.5 1.6 %weight_rows.4 = (bf16[768,256]{1,0:T(8,128)(2,1)S(1)}, bf16[768,256]{1,0:T(8,128)(2,1)S(1)}) custom-call(s32[3]{0:T(128)S(1)} %pad_add_fusion.ids, bf16[192,2816]{1,0:T(8,128)(2,1)S(1)} %get-tuple-element.107.refs_0_, bf16[192,2816]{1,0:T(8,128)(2,1)S(1)} %collective-permute-done.19.refs_1_, bf16[192,2816]{1,0:T(8,128)(2,1)S(1)} %collective-permute-done.20.refs_2_, ...), custom_call_target="tpu_custom_call" | custom-call | tf_op jit(solution)/shard_map/weight_rows/pallas_call | solution.py:48
  105.3 1.6 %collective-permute-done.30 = bf16[768,256]{1,0:T(8,128)(2,1)S(1)} collective-permute-done((bf16[768,256]{1,0:T(8,128)(2,1)S(1)}, bf16[768,256]{1,0:T(8,128)(2,1)S(1)}, u32[]{:S(2)}, u32[]{:S(2)}) %collective-permute-start.30) | collective-permute-done | bytes 393248 | tf_op jit(solution)/shard_map/ppermute | solution.py:32
  107.5 1.6 %collective-permute-start.32 = (bf16[320,256]{1,0:T(8,128)(2,1)S(1)}, bf16[320,256]{1,0:T(8,128)(2,1)S(1)}, u32[]{:S(2)}, u32[]{:S(2)}) collective-permute-start(bf16[320,256]{1,0:T(8,128)(2,1)S(1)} %slice.74), channel_id=1, source_target_pairs={{0,2},{1,3},{2,0},{3,1},{4,6},{5,7},{6,4},{7,5},{8,10},{9,11},{10,... | collective-permute-start | bytes 491528 | tf_op jit(solution)/shard_map/ppermute | solution.py:32
  110.8 2.3 %collective-permute-start.44 = (bf16[640,256]{1,0:T(8,128)(2,1)S(1)}, bf16[640,256]{1,0:T(8,128)(2,1)S(1)}, u32[]{:S(2)}, u32[]{:S(2)}) collective-permute-start(bf16[640,256]{1,0:T(8,128)(2,1)S(1)} %get-tuple-element.102), channel_id=1, source_target_pairs={{0,24},{8,16},{16,8},{24,0},{1,25},{9,17},{17,9},{25,1},{2,26},{10... | collective-permute-start | bytes 983048 | tf_op jit(solution)/shard_map/ppermute | solution.py:32
  113.2 1.4 collective-permute-done.32
  114.7 2.7 %collective-permute-start.33 = (bf16[320,256]{1,0:T(8,128)(2,1)S(1)}, bf16[320,256]{1,0:T(8,128)(2,1)S(1)}, u32[]{:S(2)}, u32[]{:S(2)}) collective-permute-start(bf16[320,256]{1,0:T(8,128)(2,1)S(1)} %fusion.1), channel_id=1, source_target_pairs={{0,4},{1,5},{2,6},{3,7},{4,0},{5,1},{6,2},{7,3},{8,12},{9,13},{10,... | collective-permute-start | bytes 491528 | tf_op jit(solution)/shard_map/ppermute | solution.py:32
  117.3 3.1 %collective-permute-done.37 = bf16[384,256]{1,0:T(8,128)(2,1)S(1)} collective-permute-done((bf16[384,256]{1,0:T(8,128)(2,1)S(1)}, bf16[384,256]{1,0:T(8,128)(2,1)S(1)}, u32[]{:S(2)}, u32[]{:S(2)}) %collective-permute-start.37) | collective-permute-done | bytes 196640 | tf_op jit(solution)/shard_map/ppermute | solution.py:32
  120.5 1.0 collective-permute-start.38
  121.5 7.9 %collective-permute-done.33 = bf16[320,256]{1,0:T(8,128)(2,1)S(1)} collective-permute-done((bf16[320,256]{1,0:T(8,128)(2,1)S(1)}, bf16[320,256]{1,0:T(8,128)(2,1)S(1)}, u32[]{:S(2)}, u32[]{:S(2)}) %collective-permute-start.33) | collective-permute-done | bytes 163872 | tf_op jit(solution)/shard_map/ppermute | solution.py:32
  130.4 1.5 collective-permute-start.45
  131.9 1.0 collective-permute-done.38
  133.0 3.7 %collective-permute-done.34.refs_1_ = bf16[320,256]{1,0:T(8,128)(2,1)S(1)} collective-permute-done((bf16[320,256]{1,0:T(8,128)(2,1)S(1)}, bf16[320,256]{1,0:T(8,128)(2,1)S(1)}, u32[]{:S(2)}, u32[]{:S(2)}) %collective-permute-start.34) | collective-permute-done | bytes 163872 | tf_op jit(solution)/shard_map/ppermute | solution.py:32
  136.7 3.2 %collective-permute-done.45 = bf16[320,256]{1,0:T(8,128)(2,1)S(1)} collective-permute-done((bf16[320,256]{1,0:T(8,128)(2,1)S(1)}, bf16[320,256]{1,0:T(8,128)(2,1)S(1)}, u32[]{:S(2)}, u32[]{:S(2)}) %collective-permute-start.45) | collective-permute-done | bytes 163872 | tf_op jit(solution)/shard_map/ppermute | solution.py:32
  139.9 2.0 %collective-permute-start.46 = (bf16[320,256]{1,0:T(8,128)(2,1)S(1)}, bf16[320,256]{1,0:T(8,128)(2,1)S(1)}, u32[]{:S(2)}, u32[]{:S(2)}) collective-permute-start(bf16[320,256]{1,0:T(8,128)(2,1)S(1)} %fusion.2), channel_id=1, source_target_pairs={{0,4},{1,5},{2,6},{3,7},{4,0},{5,1},{6,2},{7,3},{8,12},{9,13},{10,... | collective-permute-start | bytes 491528 | tf_op jit(solution)/shard_map/ppermute | solution.py:32
  142.0 1.8 %collective-permute-start.39 = (bf16[384,256]{1,0:T(8,128)(2,1)S(1)}, bf16[384,256]{1,0:T(8,128)(2,1)S(1)}, u32[]{:S(2)}, u32[]{:S(2)}) collective-permute-start(bf16[384,256]{1,0:T(8,128)(2,1)S(1)} %add_convert_fusion.refs_4_), channel_id=1, source_target_pairs={{0,2},{1,3},{2,0},{3,1},{4,6},{5,7},{6,4},{7,5},{8,10},{9,11},{10,... | collective-permute-start | bytes 589832 | tf_op jit(solution)/shard_map/ppermute | solution.py:32
  143.7 6.7 %collective-permute-done.46 = bf16[320,256]{1,0:T(8,128)(2,1)S(1)} collective-permute-done((bf16[320,256]{1,0:T(8,128)(2,1)S(1)}, bf16[320,256]{1,0:T(8,128)(2,1)S(1)}, u32[]{:S(2)}, u32[]{:S(2)}) %collective-permute-start.46) | collective-permute-done | bytes 163872 | tf_op jit(solution)/shard_map/ppermute | solution.py:32
  151.9 4.3 %collective-permute-done.47.refs_3_ = bf16[320,256]{1,0:T(8,128)(2,1)S(1)} collective-permute-done((bf16[320,256]{1,0:T(8,128)(2,1)S(1)}, bf16[320,256]{1,0:T(8,128)(2,1)S(1)}, u32[]{:S(2)}, u32[]{:S(2)}) %collective-permute-start.47) | collective-permute-done | bytes 163872 | tf_op jit(solution)/shard_map/ppermute | solution.py:32
  156.3 2.3 %assemble.2 = (f32[4096,128]{1,0:T(8,128)}, f32[4096,128]{1,0:T(8,128)}) custom-call(s32[3]{0:T(128)S(1)} %pad_add_fusion.ids, bf16[320,256]{1,0:T(8,128)(2,1)S(1)} %add_convert_fusion.2.refs_0_, bf16[320,256]{1,0:T(8,128)(2,1)S(1)} %collective-permute-done.34.refs_1_, bf16[320,256]{1,0:T(8,128)(2,1)S(1)} %collective-permute-done.35.refs_2_, ...), custom_call_target="tpu_custom_call" | custom-call | tf_op jit(solution)/shard_map/assemble/pallas_call | solution.py:391
  158.6 1.7 %assemble.3 = (f32[4096,128]{1,0:T(8,128)}, f32[4096,128]{1,0:T(8,128)}) custom-call(s32[3]{0:T(128)S(1)} %pad_add_fusion.ids, f32[4096,128]{1,0:T(8,128)} %get-tuple-element.97.refs_0_, f32[4096,128]{1,0:T(8,128)} %get-tuple-element.98.refs_1_, bf16[320,256]{1,0:T(8,128)(2,1)S(1)} %add_convert_fusion.1.refs_2_, ...), custom_call_target="tpu_custom_call", output_to_operand_aliasing={{0}: (1, {}), {1}: (2, {})} | custom-call | tf_op jit(solution)/shard_map/assemble/pallas_call | solution.py:391
  (99 shorter events, 17.2 us)
Async XLA Ops:
  2.9 15.9 %collective-permute-start = (bf16[1024,256]{1,0:T(8,128)(2,1)}, bf16[1024,256]{1,0:T(8,128)(2,1)S(1)}, u32[]{:S(2)}, u32[]{:S(2)}) collective-permute-start(bf16[1024,256]{1,0:T(8,128)(2,1)} %pad_maximum_fusion), channel_id=1, source_target_pairs={{0,8},{8,0},{16,24},{24,16},{1,9},{9,1},{17,25},{25,17},{2,10},{10... | collective-permute-start | bytes 1572872 | tf_op jit(solution)/shard_map/ppermute | solution.py:32
  6.7 15.1 %collective-permute-start.2 = (bf16[1024,256]{1,0:T(8,128)(2,1)}, bf16[1024,256]{1,0:T(8,128)(2,1)S(1)}, u32[]{:S(2)}, u32[]{:S(2)}) collective-permute-start(bf16[1024,256]{1,0:T(8,128)(2,1)} %pad_maximum_fusion.1), channel_id=1, source_target_pairs={{0,16},{8,24},{16,0},{24,8},{1,17},{9,25},{17,1},{25,9},{2,18},{10... | collective-permute-start | bytes 1572872 | tf_op jit(solution)/shard_map/ppermute | solution.py:32
  8.2 24.9 %collective-permute-start.5 = (bf16[1024,256]{1,0:T(8,128)(2,1)}, bf16[1024,256]{1,0:T(8,128)(2,1)}, u32[]{:S(2)}, u32[]{:S(2)}) collective-permute-start(bf16[1024,256]{1,0:T(8,128)(2,1)} %pad_maximum_fusion), channel_id=1, source_target_pairs={{0,16},{8,24},{16,0},{24,8},{1,17},{9,25},{17,1},{25,9},{2,18},{10... | collective-permute-start | bytes 1572872 | tf_op jit(solution)/shard_map/ppermute | solution.py:32
  8.7 24.4 %collective-permute-start.1 = (bf16[1024,256]{1,0:T(8,128)(2,1)}, bf16[1024,256]{1,0:T(8,128)(2,1)}, u32[]{:S(2)}, u32[]{:S(2)}) collective-permute-start(bf16[1024,256]{1,0:T(8,128)(2,1)} %pad_maximum_fusion.1), channel_id=1, source_target_pairs={{0,8},{8,0},{16,24},{24,16},{1,9},{9,1},{17,25},{25,17},{2,10},{10... | collective-permute-start | bytes 1572872 | tf_op jit(solution)/shard_map/ppermute | solution.py:32
  21.8 11.9 %collective-permute-start.3 = (bf16[1024,256]{1,0:T(8,128)(2,1)S(1)}, bf16[1024,256]{1,0:T(8,128)(2,1)}, u32[]{:S(2)}, u32[]{:S(2)}) collective-permute-start(bf16[1024,256]{1,0:T(8,128)(2,1)S(1)} %collective-permute-done.refs_2_), channel_id=1, source_target_pairs={{0,1},{1,0},{2,3},{3,2},{4,5},{5,4},{6,7},{7,6},{8,9},{9,8},{10,11... | collective-permute-start | bytes 1572872 | tf_op jit(solution)/shard_map/ppermute | solution.py:32
  21.8 21.0 %collective-permute-start.8 = (bf16[1024,256]{1,0:T(8,128)(2,1)S(1)}, bf16[1024,256]{1,0:T(8,128)(2,1)S(1)}, u32[]{:S(2)}, u32[]{:S(2)}) collective-permute-start(bf16[1024,256]{1,0:T(8,128)(2,1)S(1)} %collective-permute-done.refs_2_), channel_id=1, source_target_pairs={{0,16},{8,24},{16,0},{24,8},{1,17},{9,25},{17,1},{25,9},{2,18},{10... | collective-permute-start | bytes 1572872 | tf_op jit(solution)/shard_map/ppermute | solution.py:32
  23.3 19.5 %collective-permute-start.9 = (bf16[1024,256]{1,0:T(8,128)(2,1)S(1)}, bf16[1024,256]{1,0:T(8,128)(2,1)S(1)}, u32[]{:S(2)}, u32[]{:S(2)}) collective-permute-start(bf16[1024,256]{1,0:T(8,128)(2,1)S(1)} %collective-permute-done.2.refs_7_), channel_id=1, source_target_pairs={{0,8},{8,0},{16,24},{24,16},{1,9},{9,1},{17,25},{25,17},{2,10},{10... | collective-permute-start | bytes 1572872 | tf_op jit(solution)/shard_map/ppermute | solution.py:32
  33.1 3.3 %collective-permute-start.6 = (bf16[1024,256]{1,0:T(8,128)(2,1)}, bf16[1024,256]{1,0:T(8,128)(2,1)S(1)}, u32[]{:S(2)}, u32[]{:S(2)}) collective-permute-start(bf16[1024,256]{1,0:T(8,128)(2,1)} %collective-permute-done.5.refs_6_), channel_id=1, source_target_pairs={{0,1},{1,0},{2,3},{3,2},{4,5},{5,4},{6,7},{7,6},{8,9},{9,8},{10,11... | collective-permute-start | bytes 1572872 | tf_op jit(solution)/shard_map/ppermute | solution.py:32
  33.1 3.6 %collective-permute-start.4 = (bf16[1024,256]{1,0:T(8,128)(2,1)}, bf16[1024,256]{1,0:T(8,128)(2,1)S(1)}, u32[]{:S(2)}, u32[]{:S(2)}) collective-permute-start(bf16[1024,256]{1,0:T(8,128)(2,1)} %collective-permute-done.1.refs_3_), channel_id=1, source_target_pairs={{0,1},{1,0},{2,3},{3,2},{4,5},{5,4},{6,7},{7,6},{8,9},{9,8},{10,11... | collective-permute-start | bytes 1572872 | tf_op jit(solution)/shard_map/ppermute | solution.py:32
  33.6 3.1 %collective-permute-start.7 = (bf16[1024,256]{1,0:T(8,128)(2,1)S(1)}, bf16[1024,256]{1,0:T(8,128)(2,1)S(1)}, u32[]{:S(2)}, u32[]{:S(2)}) collective-permute-start(bf16[1024,256]{1,0:T(8,128)(2,1)S(1)} %collective-permute-done.2.refs_7_), channel_id=1, source_target_pairs={{0,1},{1,0},{2,3},{3,2},{4,5},{5,4},{6,7},{7,6},{8,9},{9,8},{10,11... | collective-permute-start | bytes 1572872 | tf_op jit(solution)/shard_map/ppermute | solution.py:32
  42.8 2.1 %collective-permute-start.10 = (bf16[1024,256]{1,0:T(8,128)(2,1)S(1)}, bf16[1024,256]{1,0:T(8,128)(2,1)S(1)}, u32[]{:S(2)}, u32[]{:S(2)}) collective-permute-start(bf16[1024,256]{1,0:T(8,128)(2,1)S(1)} %collective-permute-done.8.refs_1_), channel_id=1, source_target_pairs={{0,1},{1,0},{2,3},{3,2},{4,5},{5,4},{6,7},{7,6},{8,9},{9,8},{10,11... | collective-permute-start | bytes 1572872 | tf_op jit(solution)/shard_map/ppermute | solution.py:32
  42.9 2.6 %collective-permute-start.11 = (bf16[1024,256]{1,0:T(8,128)(2,1)S(1)}, bf16[1024,256]{1,0:T(8,128)(2,1)S(1)}, u32[]{:S(2)}, u32[]{:S(2)}) collective-permute-start(bf16[1024,256]{1,0:T(8,128)(2,1)S(1)} %collective-permute-done.9.refs_2_), channel_id=1, source_target_pairs={{0,1},{1,0},{2,3},{3,2},{4,5},{5,4},{6,7},{7,6},{8,9},{9,8},{10,11... | collective-permute-start | bytes 1572872 | tf_op jit(solution)/shard_map/ppermute | solution.py:32
  43.4 29.9 %collective-permute-start.20 = (bf16[192,2816]{1,0:T(8,128)(2,1)S(1)}, bf16[192,2816]{1,0:T(8,128)(2,1)S(1)}, u32[]{:S(2)}, u32[]{:S(2)}) collective-permute-start(bf16[192,2816]{1,0:T(8,128)(2,1)S(1)} %get-tuple-element.73), channel_id=1, source_target_pairs={{0,16},{8,24},{16,0},{24,8},{1,17},{9,25},{17,1},{25,9},{2,18},{10... | collective-permute-start | bytes 3244040 | tf_op jit(solution)/shard_map/ppermute | solution.py:32
  45.5 27.8 %collective-permute-start.19 = (bf16[192,2816]{1,0:T(8,128)(2,1)S(1)}, bf16[192,2816]{1,0:T(8,128)(2,1)S(1)}, u32[]{:S(2)}, u32[]{:S(2)}) collective-permute-start(bf16[192,2816]{1,0:T(8,128)(2,1)S(1)} %get-tuple-element.72), channel_id=1, source_target_pairs={{0,8},{8,0},{16,24},{24,16},{1,9},{9,1},{17,25},{25,17},{2,10},{10... | collective-permute-start | bytes 3244040 | tf_op jit(solution)/shard_map/ppermute | solution.py:32
  47.0 7.6 %collective-permute-start.14 = (bf16[192,256]{1,0:T(8,128)(2,1)S(1)}, bf16[192,256]{1,0:T(8,128)(2,1)S(1)}, u32[]{:S(2)}, u32[]{:S(2)}) collective-permute-start(bf16[192,256]{1,0:T(8,128)(2,1)S(1)} %project.3.refs_0_), channel_id=1, source_target_pairs={{0,6},{1,7},{2,4},{3,5},{4,2},{5,3},{6,0},{7,1},{8,14},{9,15},{10,... | collective-permute-start | bytes 294920 | tf_op jit(solution)/shard_map/ppermute | solution.py:32
  50.9 8.3 %collective-permute-start.13 = (bf16[192,256]{1,0:T(8,128)(2,1)S(1)}, bf16[192,256]{1,0:T(8,128)(2,1)S(1)}, u32[]{:S(2)}, u32[]{:S(2)}) collective-permute-start(bf16[192,256]{1,0:T(8,128)(2,1)S(1)} %project.3.refs_0_), channel_id=1, source_target_pairs={{0,4},{1,5},{2,6},{3,7},{4,0},{5,1},{6,2},{7,3},{8,12},{9,13},{10,... | collective-permute-start | bytes 294920 | tf_op jit(solution)/shard_map/ppermute | solution.py:32
  50.9 8.3 %collective-permute-start.12 = (bf16[192,256]{1,0:T(8,128)(2,1)S(1)}, bf16[192,256]{1,0:T(8,128)(2,1)S(1)}, u32[]{:S(2)}, u32[]{:S(2)}) collective-permute-start(bf16[192,256]{1,0:T(8,128)(2,1)S(1)} %project.3.refs_0_), channel_id=1, source_target_pairs={{0,2},{1,3},{2,0},{3,1},{4,6},{5,7},{6,4},{7,5},{8,10},{9,11},{10,... | collective-permute-start | bytes 294920 | tf_op jit(solution)/shard_map/ppermute | solution.py:32
  59.2 37.3 %collective-permute-start.28 = (bf16[192,2816]{1,0:T(8,128)(2,1)S(1)}, bf16[192,2816]{1,0:T(8,128)(2,1)S(1)}, u32[]{:S(2)}, u32[]{:S(2)}) collective-permute-start(bf16[192,2816]{1,0:T(8,128)(2,1)S(1)} %get-tuple-element.83), channel_id=1, source_target_pairs={{0,24},{8,16},{16,8},{24,0},{1,25},{9,17},{17,9},{25,1},{2,26},{10... | collective-permute-start | bytes 3244040 | tf_op jit(solution)/shard_map/ppermute | solution.py:32
  61.6 1.5 collective-permute-start.16
  63.1 1.3 collective-permute-start.18
  73.3 1.7 %collective-permute-start.21 = (bf16[768,256]{1,0:T(8,128)(2,1)S(1)}, bf16[768,256]{1,0:T(8,128)(2,1)S(1)}, u32[]{:S(2)}, u32[]{:S(2)}) collective-permute-start(bf16[768,256]{1,0:T(8,128)(2,1)S(1)} %get-tuple-element.77), channel_id=1, source_target_pairs={{0,1},{1,0},{2,3},{3,2},{4,5},{5,4},{6,7},{7,6},{8,9},{9,8},{10,11... | collective-permute-start | bytes 1179656 | tf_op jit(solution)/shard_map/ppermute | solution.py:32
  75.1 6.5 %collective-permute-start.22 = (bf16[192,256]{1,0:T(8,128)(2,1)S(1)}, bf16[192,256]{1,0:T(8,128)(2,1)S(1)}, u32[]{:S(2)}, u32[]{:S(2)}) collective-permute-start(bf16[192,256]{1,0:T(8,128)(2,1)S(1)} %get-tuple-element.79), channel_id=1, source_target_pairs={{0,2},{1,3},{2,0},{3,1},{4,6},{5,7},{6,4},{7,5},{8,10},{9,11},{10,... | collective-permute-start | bytes 294920 | tf_op jit(solution)/shard_map/ppermute | solution.py:32
  75.7 10.8 %collective-permute-start.23 = (bf16[192,256]{1,0:T(8,128)(2,1)S(1)}, bf16[192,256]{1,0:T(8,128)(2,1)S(1)}, u32[]{:S(2)}, u32[]{:S(2)}) collective-permute-start(bf16[192,256]{1,0:T(8,128)(2,1)S(1)} %get-tuple-element.80), channel_id=1, source_target_pairs={{0,4},{1,5},{2,6},{3,7},{4,0},{5,1},{6,2},{7,3},{8,12},{9,13},{10,... | collective-permute-start | bytes 294920 | tf_op jit(solution)/shard_map/ppermute | solution.py:32
  78.3 8.2 %collective-permute-start.24 = (bf16[192,256]{1,0:T(8,128)(2,1)S(1)}, bf16[192,256]{1,0:T(8,128)(2,1)S(1)}, u32[]{:S(2)}, u32[]{:S(2)}) collective-permute-start(bf16[192,256]{1,0:T(8,128)(2,1)S(1)} %get-tuple-element.81), channel_id=1, source_target_pairs={{0,6},{1,7},{2,4},{3,5},{4,2},{5,3},{6,0},{7,1},{8,14},{9,15},{10,... | collective-permute-start | bytes 294920 | tf_op jit(solution)/shard_map/ppermute | solution.py:32
  86.6 11.9 %collective-permute-start.27 = (bf16[192,256]{1,0:T(8,128)(2,1)S(1)}, bf16[192,256]{1,0:T(8,128)(2,1)S(1)}, u32[]{:S(2)}, u32[]{:S(2)}) collective-permute-start(bf16[192,256]{1,0:T(8,128)(2,1)S(1)} %total.1.refs_4_.refs_1_), channel_id=1, source_target_pairs={{0,24},{8,16},{16,8},{24,0},{1,25},{9,17},{17,9},{25,1},{2,26},{10... | collective-permute-start | bytes 294920 | tf_op jit(solution)/shard_map/ppermute | solution.py:32
  88.0 11.8 %collective-permute-start.26 = (bf16[192,256]{1,0:T(8,128)(2,1)S(1)}, bf16[192,256]{1,0:T(8,128)(2,1)S(1)}, u32[]{:S(2)}, u32[]{:S(2)}) collective-permute-start(bf16[192,256]{1,0:T(8,128)(2,1)S(1)} %total.1.refs_4_.refs_1_), channel_id=1, source_target_pairs={{0,16},{8,24},{16,0},{24,8},{1,17},{9,25},{17,1},{25,9},{2,18},{10... | collective-permute-start | bytes 294920 | tf_op jit(solution)/shard_map/ppermute | solution.py:32
  88.6 11.2 %collective-permute-start.25 = (bf16[192,256]{1,0:T(8,128)(2,1)S(1)}, bf16[192,256]{1,0:T(8,128)(2,1)S(1)}, u32[]{:S(2)}, u32[]{:S(2)}) collective-permute-start(bf16[192,256]{1,0:T(8,128)(2,1)S(1)} %total.1.refs_4_.refs_1_), channel_id=1, source_target_pairs={{0,8},{8,0},{16,24},{24,16},{1,9},{9,1},{17,25},{25,17},{2,10},{10... | collective-permute-start | bytes 294920 | tf_op jit(solution)/shard_map/ppermute | solution.py:32
  101.4 5.6 %collective-permute-start.31 = (bf16[2560,256]{1,0:T(8,128)(2,1)S(1)}, bf16[2560,256]{1,0:T(8,128)(2,1)S(1)}, u32[]{:S(2)}, u32[]{:S(2)}) collective-permute-start(bf16[2560,256]{1,0:T(8,128)(2,1)S(1)} %get-tuple-element.94), channel_id=1, source_target_pairs={{0,1},{1,0},{2,3},{3,2},{4,5},{5,4},{6,7},{7,6},{8,9},{9,8},{10,11... | collective-permute-start | bytes 3932168 | tf_op jit(solution)/shard_map/ppermute | solution.py:32
  103.0 2.3 %collective-permute-start.29 = (bf16[640,256]{1,0:T(8,128)(2,1)S(1)}, bf16[640,256]{1,0:T(8,128)(2,1)S(1)}, u32[]{:S(2)}, u32[]{:S(2)}) collective-permute-start(bf16[640,256]{1,0:T(8,128)(2,1)S(1)} %get-tuple-element.89), channel_id=1, source_target_pairs={{0,1},{1,0},{2,3},{3,2},{4,5},{5,4},{6,7},{7,6},{8,9},{9,8},{10,11... | collective-permute-start | bytes 983048 | tf_op jit(solution)/shard_map/ppermute | solution.py:32
  105.1 1.8 %collective-permute-start.30 = (bf16[768,256]{1,0:T(8,128)(2,1)S(1)}, bf16[768,256]{1,0:T(8,128)(2,1)S(1)}, u32[]{:S(2)}, u32[]{:S(2)}) collective-permute-start(bf16[768,256]{1,0:T(8,128)(2,1)S(1)} %get-tuple-element.91), channel_id=1, source_target_pairs={{0,1},{1,0},{2,3},{3,2},{4,5},{5,4},{6,7},{7,6},{8,9},{9,8},{10,11... | collective-permute-start | bytes 1179656 | tf_op jit(solution)/shard_map/ppermute | solution.py:32
  107.5 7.1 %collective-permute-start.32 = (bf16[320,256]{1,0:T(8,128)(2,1)S(1)}, bf16[320,256]{1,0:T(8,128)(2,1)S(1)}, u32[]{:S(2)}, u32[]{:S(2)}) collective-permute-start(bf16[320,256]{1,0:T(8,128)(2,1)S(1)} %slice.74), channel_id=1, source_target_pairs={{0,2},{1,3},{2,0},{3,1},{4,6},{5,7},{6,4},{7,5},{8,10},{9,11},{10,... | collective-permute-start | bytes 491528 | tf_op jit(solution)/shard_map/ppermute | solution.py:32
  109.2 11.3 %collective-permute-start.37 = (bf16[384,256]{1,0:T(8,128)(2,1)S(1)}, bf16[384,256]{1,0:T(8,128)(2,1)S(1)}, u32[]{:S(2)}, u32[]{:S(2)}) collective-permute-start(bf16[384,256]{1,0:T(8,128)(2,1)S(1)} %slice.72), channel_id=1, source_target_pairs={{0,2},{1,3},{2,0},{3,1},{4,6},{5,7},{6,4},{7,5},{8,10},{9,11},{10,... | collective-permute-start | bytes 589832 | tf_op jit(solution)/shard_map/ppermute | solution.py:32
  109.7 19.8 %collective-permute-start.42 = (bf16[640,256]{1,0:T(8,128)(2,1)S(1)}, bf16[640,256]{1,0:T(8,128)(2,1)S(1)}, u32[]{:S(2)}, u32[]{:S(2)}) collective-permute-start(bf16[640,256]{1,0:T(8,128)(2,1)S(1)} %get-tuple-element.100), channel_id=1, source_target_pairs={{0,8},{8,0},{16,24},{24,16},{1,9},{9,1},{17,25},{25,17},{2,10},{10... | collective-permute-start | bytes 983048 | tf_op jit(solution)/shard_map/ppermute | solution.py:32
  110.2 20.0 %collective-permute-start.43 = (bf16[640,256]{1,0:T(8,128)(2,1)S(1)}, bf16[640,256]{1,0:T(8,128)(2,1)S(1)}, u32[]{:S(2)}, u32[]{:S(2)}) collective-permute-start(bf16[640,256]{1,0:T(8,128)(2,1)S(1)} %get-tuple-element.101), channel_id=1, source_target_pairs={{0,16},{8,24},{16,0},{24,8},{1,17},{9,25},{17,1},{25,9},{2,18},{10... | collective-permute-start | bytes 983048 | tf_op jit(solution)/shard_map/ppermute | solution.py:32
  110.8 19.4 %collective-permute-start.44 = (bf16[640,256]{1,0:T(8,128)(2,1)S(1)}, bf16[640,256]{1,0:T(8,128)(2,1)S(1)}, u32[]{:S(2)}, u32[]{:S(2)}) collective-permute-start(bf16[640,256]{1,0:T(8,128)(2,1)S(1)} %get-tuple-element.102), channel_id=1, source_target_pairs={{0,24},{8,16},{16,8},{24,0},{1,25},{9,17},{17,9},{25,1},{2,26},{10... | collective-permute-start | bytes 983048 | tf_op jit(solution)/shard_map/ppermute | solution.py:32
  114.7 14.7 %collective-permute-start.33 = (bf16[320,256]{1,0:T(8,128)(2,1)S(1)}, bf16[320,256]{1,0:T(8,128)(2,1)S(1)}, u32[]{:S(2)}, u32[]{:S(2)}) collective-permute-start(bf16[320,256]{1,0:T(8,128)(2,1)S(1)} %fusion.1), channel_id=1, source_target_pairs={{0,4},{1,5},{2,6},{3,7},{4,0},{5,1},{6,2},{7,3},{8,12},{9,13},{10,... | collective-permute-start | bytes 491528 | tf_op jit(solution)/shard_map/ppermute | solution.py:32
  120.5 12.4 %collective-permute-start.38 = (bf16[384,256]{1,0:T(8,128)(2,1)S(1)}, bf16[384,256]{1,0:T(8,128)(2,1)S(1)}, u32[]{:S(2)}, u32[]{:S(2)}) collective-permute-start(bf16[384,256]{1,0:T(8,128)(2,1)S(1)} %fusion), channel_id=1, source_target_pairs={{0,4},{1,5},{2,6},{3,7},{4,0},{5,1},{6,2},{7,3},{8,12},{9,13},{10,... | collective-permute-start | bytes 589832 | tf_op jit(solution)/shard_map/ppermute | solution.py:32
  129.4 14.3 %collective-permute-start.35 = (bf16[320,256]{1,0:T(8,128)(2,1)S(1)}, bf16[320,256]{1,0:T(8,128)(2,1)S(1)}, u32[]{:S(2)}, u32[]{:S(2)}) collective-permute-start(bf16[320,256]{1,0:T(8,128)(2,1)S(1)} %add_convert_fusion.2.refs_0_), channel_id=1, source_target_pairs={{0,1},{1,0},{2,3},{3,2},{4,5},{5,4},{6,7},{7,6},{8,9},{9,8},{10,11... | collective-permute-start | bytes 491528 | tf_op jit(solution)/shard_map/ppermute | solution.py:32
  129.5 7.1 %collective-permute-start.34 = (bf16[320,256]{1,0:T(8,128)(2,1)S(1)}, bf16[320,256]{1,0:T(8,128)(2,1)S(1)}, u32[]{:S(2)}, u32[]{:S(2)}) collective-permute-start(bf16[320,256]{1,0:T(8,128)(2,1)S(1)} %add_convert_fusion.2.refs_0_), channel_id=1, source_target_pairs={{0,2},{1,3},{2,0},{3,1},{4,6},{5,7},{6,4},{7,5},{8,10},{9,11},{10,... | collective-permute-start | bytes 491528 | tf_op jit(solution)/shard_map/ppermute | solution.py:32
  130.4 9.5 %collective-permute-start.45 = (bf16[320,256]{1,0:T(8,128)(2,1)S(1)}, bf16[320,256]{1,0:T(8,128)(2,1)S(1)}, u32[]{:S(2)}, u32[]{:S(2)}) collective-permute-start(bf16[320,256]{1,0:T(8,128)(2,1)S(1)} %slice.73), channel_id=1, source_target_pairs={{0,2},{1,3},{2,0},{3,1},{4,6},{5,7},{6,4},{7,5},{8,10},{9,11},{10,... | collective-permute-start | bytes 491528 | tf_op jit(solution)/shard_map/ppermute | solution.py:32
  136.7 7.1 %collective-permute-start.36 = (bf16[320,256]{1,0:T(8,128)(2,1)S(1)}, bf16[320,256]{1,0:T(8,128)(2,1)S(1)}, u32[]{:S(2)}, u32[]{:S(2)}) collective-permute-start(bf16[320,256]{1,0:T(8,128)(2,1)S(1)} %collective-permute-done.34.refs_1_), channel_id=1, source_target_pairs={{0,1},{1,0},{2,3},{3,2},{4,5},{5,4},{6,7},{7,6},{8,9},{9,8},{10,11... | collective-permute-start | bytes 491528 | tf_op jit(solution)/shard_map/ppermute | solution.py:32
  139.9 10.5 %collective-permute-start.46 = (bf16[320,256]{1,0:T(8,128)(2,1)S(1)}, bf16[320,256]{1,0:T(8,128)(2,1)S(1)}, u32[]{:S(2)}, u32[]{:S(2)}) collective-permute-start(bf16[320,256]{1,0:T(8,128)(2,1)S(1)} %fusion.2), channel_id=1, source_target_pairs={{0,4},{1,5},{2,6},{3,7},{4,0},{5,1},{6,2},{7,3},{8,12},{9,13},{10,... | collective-permute-start | bytes 491528 | tf_op jit(solution)/shard_map/ppermute | solution.py:32
  142.0 9.4 %collective-permute-start.39 = (bf16[384,256]{1,0:T(8,128)(2,1)S(1)}, bf16[384,256]{1,0:T(8,128)(2,1)S(1)}, u32[]{:S(2)}, u32[]{:S(2)}) collective-permute-start(bf16[384,256]{1,0:T(8,128)(2,1)S(1)} %add_convert_fusion.refs_4_), channel_id=1, source_target_pairs={{0,2},{1,3},{2,0},{3,1},{4,6},{5,7},{6,4},{7,5},{8,10},{9,11},{10,... | collective-permute-start | bytes 589832 | tf_op jit(solution)/shard_map/ppermute | solution.py:32
  150.5 5.8 %collective-permute-start.47 = (bf16[320,256]{1,0:T(8,128)(2,1)S(1)}, bf16[320,256]{1,0:T(8,128)(2,1)S(1)}, u32[]{:S(2)}, u32[]{:S(2)}) collective-permute-start(bf16[320,256]{1,0:T(8,128)(2,1)S(1)} %add_convert_fusion.1.refs_2_), channel_id=1, source_target_pairs={{0,2},{1,3},{2,0},{3,1},{4,6},{5,7},{6,4},{7,5},{8,10},{9,11},{10,... | collective-permute-start | bytes 491528 | tf_op jit(solution)/shard_map/ppermute | solution.py:32
  150.6 5.7 %collective-permute-start.40 = (bf16[384,256]{1,0:T(8,128)(2,1)S(1)}, bf16[384,256]{1,0:T(8,128)(2,1)S(1)}, u32[]{:S(2)}, u32[]{:S(2)}) collective-permute-start(bf16[384,256]{1,0:T(8,128)(2,1)S(1)} %add_convert_fusion.refs_4_), channel_id=1, source_target_pairs={{0,1},{1,0},{2,3},{3,2},{4,5},{5,4},{6,7},{7,6},{8,9},{9,8},{10,11... | collective-permute-start | bytes 589832 | tf_op jit(solution)/shard_map/ppermute | solution.py:32
  151.4 4.9 %collective-permute-start.41 = (bf16[384,256]{1,0:T(8,128)(2,1)S(1)}, bf16[384,256]{1,0:T(8,128)(2,1)S(1)}, u32[]{:S(2)}, u32[]{:S(2)}) collective-permute-start(bf16[384,256]{1,0:T(8,128)(2,1)S(1)} %collective-permute-done.39.refs_5_), channel_id=1, source_target_pairs={{0,1},{1,0},{2,3},{3,2},{4,5},{5,4},{6,7},{7,6},{8,9},{9,8},{10,11... | collective-permute-start | bytes 589832 | tf_op jit(solution)/shard_map/ppermute | solution.py:32
  151.4 7.1 %collective-permute-start.48 = (bf16[320,256]{1,0:T(8,128)(2,1)S(1)}, bf16[320,256]{1,0:T(8,128)(2,1)S(1)}, u32[]{:S(2)}, u32[]{:S(2)}) collective-permute-start(bf16[320,256]{1,0:T(8,128)(2,1)S(1)} %add_convert_fusion.1.refs_2_), channel_id=1, source_target_pairs={{0,1},{1,0},{2,3},{3,2},{4,5},{5,4},{6,7},{7,6},{8,9},{9,8},{10,11... | collective-permute-start | bytes 491528 | tf_op jit(solution)/shard_map/ppermute | solution.py:32
  156.3 2.3 %collective-permute-start.49 = (bf16[320,256]{1,0:T(8,128)(2,1)S(1)}, bf16[320,256]{1,0:T(8,128)(2,1)S(1)}, u32[]{:S(2)}, u32[]{:S(2)}) collective-permute-start(bf16[320,256]{1,0:T(8,128)(2,1)S(1)} %collective-permute-done.47.refs_3_), channel_id=1, source_target_pairs={{0,1},{1,0},{2,3},{3,2},{4,5},{5,4},{6,7},{7,6},{8,9},{9,8},{10,11... | collective-permute-start | bytes 491528 | tf_op jit(solution)/shard_map/ppermute | solution.py:32
  (10 other events, 136.5 us)

commit v14 on v11

--- a/solution.py
+++ b/solution.py
@@ -110,8 +110,10 @@
         begin = jnp.zeros_like(at_query)
         for end in ends:
             begin = jnp.where(at_query >= end, end, begin)
-        at_key = first + lax.broadcasted_iota(jnp.int32, (window, chunk), 0)
-        allowed = (at_key >= begin) & (at_key <= at_query)
+        at_key = lax.broadcasted_iota(jnp.int32, (window, chunk), 0)
+        allowed = (at_key + (first - begin)).astype(jnp.uint32) <= (at_query - begin).astype(
+            jnp.uint32
+        )
         k = keys[pl.ds(first, window), :]
         v = values[pl.ds(first, window), :]
         q = qs[part, :]
@@ -136,7 +138,7 @@
         total[pl.ds(first, window), head_dim:] += dv
         return carry
 
-    lax.fori_loop(0, 2 * chunks_half, step, 0, unroll=2)
+    lax.fori_loop(0, 2 * chunks_half, step, 0, unroll=3)
     for half in range(2):
         for head in range(head_count):
             origin = slice((half * head_count + head) * stretch_rows, (half * head_count + head + 1) * stretch_rows)
@@ -524,11 +526,13 @@
         part = scatter_along_z(part, sub_count)
         finals.append(sum_of_halves(part, sub_count))
     part = scatter_along_z(sum_of(own), sub_count, finals[:TIED])
+    finals, _ = after(finals, part)
     blocks = gather_parts(finals[0], sub_count)
-    last = sum_of_halves(part, sub_count, blocks)
+    last = sum_of_halves(part, sub_count)
+    (last,), _ = after([last], *blocks)
     blocks += [one for final in finals[1:] for one in gather_parts(final, sub_count)]
     outs = assemble(ids, (), blocks, sub_count, regions[:-1], block_rows)
-    last = gather_parts(last, sub_count, outs)
+    last = gather_parts(last, sub_count)
     key_rows, value_rows = assemble(ids, outs, last, sub_count, regions[-1:], block_rows)
     return query_grad[None], key_rows, value_rows
 

time: 153 us -> 154 us (level)
  starting transfers between devices: 42.3 us -> 44.7 us
    ppermute x50, starting transfers between devices: 42.3 us -> 44.7 us  [swap(): return lax.ppermute(array, axis, [(i, i ^ distance) for i in range(count)])]
where the time goes in v14:
time: 154 us
  waiting for transfers between devices  78.8 us (51%)
  starting transfers between devices  44.7 us (29%)
  Pallas kernels  21.4 us (14%)
  local copies, waits for them, and re-layouts  5.14 us (3%)
  other arithmetic  2.89 us (2%)
    ppermute x50, waiting for transfers between devices, swap(): return lax.ppermute(array, axis, [(i, i ^ distance) for i in range(count)])  78.8 us
    ppermute x50, starting transfers between devices, swap(): return lax.ppermute(array, axis, [(i, i ^ distance) for i in range(count)])  44.7 us
    pallas_call x7, Pallas kernels, kernel_call(): pl.pallas_call(kernel, out_shape=outs, in_specs=[smem] * len(scalars) + [...  9.06 us
    pallas_call x1, Pallas kernels, attention(): pl.pallas_call(functools.partial(attention_kernel, shape), out_shape=(jax...  8.45 us
    pallas_call x2, Pallas kernels, assemble(): pl.pallas_call(functools.partial(assemble_kernel, sub_count, regions, not...  3.92 us
  transfers between devices with their start and end apart: 50, of which 29 were waited for; matrix products, arithmetic and copies ran while one was open for 3% of the time, Pallas kernels for 12%

profile of v14, /device:TPU:0, one launch (start us, length us, event | category | flops | bytes accessed | tf_op | source)
XLA Modules:
  0.0 154.0 jit_solution(13733034002401266254)
XLA Ops:
  0.7 1.4 constant_dynamic-slice_fusion
  2.9 2.9 %collective-permute-start = (bf16[1024,256]{1,0:T(8,128)(2,1)}, bf16[1024,256]{1,0:T(8,128)(2,1)S(1)}, u32[]{:S(2)}, u32[]{:S(2)}) collective-permute-start(bf16[1024,256]{1,0:T(8,128)(2,1)} %pad_maximum_fusion), channel_id=1, source_target_pairs={{0,8},{8,0},{16,24},{24,16},{1,9},{9,1},{17,25},{25,17},{2,10},{10... | collective-permute-start | bytes 1572872 | tf_op jit(solution)/shard_map/ppermute | solution.py:32
  6.7 1.5 collective-permute-start.2
  8.8 10.0 %collective-permute-done.refs_2_ = bf16[1024,256]{1,0:T(8,128)(2,1)S(1)} collective-permute-done((bf16[1024,256]{1,0:T(8,128)(2,1)}, bf16[1024,256]{1,0:T(8,128)(2,1)S(1)}, u32[]{:S(2)}, u32[]{:S(2)}) %collective-permute-start) | collective-permute-done | bytes 524320 | tf_op jit(solution)/shard_map/ppermute | solution.py:32
  18.8 3.0 %collective-permute-done.2.refs_7_ = bf16[1024,256]{1,0:T(8,128)(2,1)S(1)} collective-permute-done((bf16[1024,256]{1,0:T(8,128)(2,1)}, bf16[1024,256]{1,0:T(8,128)(2,1)S(1)}, u32[]{:S(2)}, u32[]{:S(2)}) %collective-permute-start.2) | collective-permute-done | bytes 524320 | tf_op jit(solution)/shard_map/ppermute | solution.py:32
  21.8 1.5 collective-permute-start.8
  23.8 9.3 %collective-permute-done.5.refs_6_ = bf16[1024,256]{1,0:T(8,128)(2,1)} collective-permute-done((bf16[1024,256]{1,0:T(8,128)(2,1)}, bf16[1024,256]{1,0:T(8,128)(2,1)}, u32[]{:S(2)}, u32[]{:S(2)}) %collective-permute-start.5) | collective-permute-done | bytes 524320 | tf_op jit(solution)/shard_map/ppermute | solution.py:32
  33.8 2.5 %dynamic-slice_bitcast_fusion = (bf16[192,2560]{1,0:T(8,128)(2,1)S(1)}, bf16[192,2560]{1,0:T(8,128)(2,1)S(1)}, bf16[192,2560]{1,0:T(8,128)(2,1)S(1)}, bf16[192,2560]{1,0:T(8,128)(2,1)S(1)}) fusion(bf16[1,192,16384]{2,1,0:T(8,128)(2,1)} %param.7, s32[]{:T(128)S(6)} %select_n.42, s32[]{:T(128)S(6)} %select_n.40, s32[]{:T(128)S(6)} %select_n.39, s32[]{:T(128)S(6)} %select_n.41), kind=kLoop, calls=%fused_computation.1 | loop fusion | bytes 7864336 | tf_op jit(solution)/shard_map/dynamic_slice | solution.py:464
  37.8 3.2 %project.2.refs_0_ = f32[192,256]{1,0:T(8,128)S(1)} custom-call(s32[3]{0:T(128)S(1)} %pad_add_fusion.ids, bf16[192,16384]{1,0:T(8,128)(2,1)S(1)} %bitcast.19, bf16[4096,128]{1,0:T(8,128)(2,1)S(1)} %copy-done, bf16[4096,128]{1,0:T(8,128)(2,1)S(1)} %copy-done.1, bf16[1024,256]{1,0:T(8,128)(2,1)S(1)} %collective-permute-done.refs_2_, ...), custom_call_target="tpu_custom_call" | custom-call | bytes 16777216 | tf_op jit(solution)/shard_map/project/pallas_call | solution.py:48
  41.0 1.8 %collective-permute-done.8.refs_1_ = bf16[1024,256]{1,0:T(8,128)(2,1)S(1)} collective-permute-done((bf16[1024,256]{1,0:T(8,128)(2,1)S(1)}, bf16[1024,256]{1,0:T(8,128)(2,1)S(1)}, u32[]{:S(2)}, u32[]{:S(2)}) %collective-permute-start.8) | collective-permute-done | bytes 524320 | tf_op jit(solution)/shard_map/ppermute | solution.py:32
  43.4 1.5 collective-permute-start.20
  45.9 1.1 project.3.refs_0_
  47.0 3.9 %collective-permute-start.14 = (bf16[192,256]{1,0:T(8,128)(2,1)S(1)}, bf16[192,256]{1,0:T(8,128)(2,1)S(1)}, u32[]{:S(2)}, u32[]{:S(2)}) collective-permute-start(bf16[192,256]{1,0:T(8,128)(2,1)S(1)} %project.3.refs_0_), channel_id=1, source_target_pairs={{0,6},{1,7},{2,4},{3,5},{4,2},{5,3},{6,0},{7,1},{8,14},{9,15},{10,... | collective-permute-start | bytes 294920 | tf_op jit(solution)/shard_map/ppermute | solution.py:32
  51.5 3.1 %collective-permute-done.14.refs_6_ = bf16[192,256]{1,0:T(8,128)(2,1)S(1)} collective-permute-done((bf16[192,256]{1,0:T(8,128)(2,1)S(1)}, bf16[192,256]{1,0:T(8,128)(2,1)S(1)}, u32[]{:S(2)}, u32[]{:S(2)}) %collective-permute-start.14) | collective-permute-done | bytes 98336 | tf_op jit(solution)/shard_map/ppermute | solution.py:32
  54.6 4.6 %collective-permute-done.13.refs_4_ = bf16[192,256]{1,0:T(8,128)(2,1)S(1)} collective-permute-done((bf16[192,256]{1,0:T(8,128)(2,1)S(1)}, bf16[192,256]{1,0:T(8,128)(2,1)S(1)}, u32[]{:S(2)}, u32[]{:S(2)}) %collective-permute-start.13) | collective-permute-done | bytes 98336 | tf_op jit(solution)/shard_map/ppermute | solution.py:32
  59.2 2.5 %collective-permute-start.28 = (bf16[192,2560]{1,0:T(8,128)(2,1)S(1)}, bf16[192,2560]{1,0:T(8,128)(2,1)S(1)}, u32[]{:S(2)}, u32[]{:S(2)}) collective-permute-start(bf16[192,2560]{1,0:T(8,128)(2,1)S(1)} %get-tuple-element.85), channel_id=1, source_target_pairs={{0,24},{8,16},{16,8},{24,0},{1,25},{9,17},{17,9},{25,1},{2,26},{10... | collective-permute-start | bytes 2949128 | tf_op jit(solution)/shard_map/ppermute | solution.py:32
  64.4 8.5 %attention.1 = (bf16[192,1024]{1,0:T(8,128)(2,1)}, f32[768,256]{1,0:T(8,128)S(1)}, bf16[768,256]{1,0:T(8,128)(2,1)S(1)}) custom-call(s32[1]{0:T(128)} %bitcast.ids, s32[16]{0:T(128)S(1)} %copy-done.4, s32[8]{0:T(128)S(1)} %bitcast.24, bf16[192,1024]{1,0:T(8,128)(2,1)S(1)} %bitcast.22, bf16[192,1024]{1,0:T(8,128)(2,1)S(1)} %bitcast.23, ...), custom_call_target="tpu_custom_call" | custom-call | tf_op jit(solution)/shard_map/attention/pallas_call | solution.py:171
  73.2 1.4 collective-permute-done.21.came
  75.3 2.6 %collective-permute-start.23 = (bf16[192,256]{1,0:T(8,128)(2,1)S(1)}, bf16[192,256]{1,0:T(8,128)(2,1)S(1)}, u32[]{:S(2)}, u32[]{:S(2)}) collective-permute-start(bf16[192,256]{1,0:T(8,128)(2,1)S(1)} %get-tuple-element.82), channel_id=1, source_target_pairs={{0,4},{1,5},{2,6},{3,7},{4,0},{5,1},{6,2},{7,3},{8,12},{9,13},{10,... | collective-permute-start | bytes 294920 | tf_op jit(solution)/shard_map/ppermute | solution.py:32
  77.8 1.3 collective-permute-start.24
  79.2 2.2 %collective-permute-done.22.refs_1_ = bf16[192,256]{1,0:T(8,128)(2,1)S(1)} collective-permute-done((bf16[192,256]{1,0:T(8,128)(2,1)S(1)}, bf16[192,256]{1,0:T(8,128)(2,1)S(1)}, u32[]{:S(2)}, u32[]{:S(2)}) %collective-permute-start.22) | collective-permute-done | bytes 98336 | tf_op jit(solution)/shard_map/ppermute | solution.py:32
  81.3 4.8 %collective-permute-done.23.refs_2_ = bf16[192,256]{1,0:T(8,128)(2,1)S(1)} collective-permute-done((bf16[192,256]{1,0:T(8,128)(2,1)S(1)}, bf16[192,256]{1,0:T(8,128)(2,1)S(1)}, u32[]{:S(2)}, u32[]{:S(2)}) %collective-permute-start.23) | collective-permute-done | bytes 98336 | tf_op jit(solution)/shard_map/ppermute | solution.py:32
  86.7 1.5 collective-permute-start.26
  88.2 1.5 collective-permute-start.25
  89.7 2.5 %collective-permute-done.28.refs_3_ = bf16[192,2560]{1,0:T(8,128)(2,1)S(1)} collective-permute-done((bf16[192,2560]{1,0:T(8,128)(2,1)S(1)}, bf16[192,2560]{1,0:T(8,128)(2,1)S(1)}, u32[]{:S(2)}, u32[]{:S(2)}) %collective-permute-start.28) | collective-permute-done | bytes 983072 | tf_op jit(solution)/shard_map/ppermute | solution.py:32
  92.3 2.1 %collective-permute-done.27.refs_7_ = bf16[192,256]{1,0:T(8,128)(2,1)S(1)} collective-permute-done((bf16[192,256]{1,0:T(8,128)(2,1)S(1)}, bf16[192,256]{1,0:T(8,128)(2,1)S(1)}, u32[]{:S(2)}, u32[]{:S(2)}) %collective-permute-start.27) | collective-permute-done | bytes 98336 | tf_op jit(solution)/shard_map/ppermute | solution.py:32
  94.3 1.3 collective-permute-done.26.refs_6_
  95.6 1.7 %weight_rows.5 = (bf16[3072,256]{1,0:T(8,128)(2,1)S(1)}, bf16[3072,256]{1,0:T(8,128)(2,1)S(1)}) custom-call(s32[3]{0:T(128)S(1)} %pad_add_fusion.ids, bf16[192,16384]{1,0:T(8,128)(2,1)S(1)} %bitcast.21, bf16[192,256]{1,0:T(8,128)(2,1)S(1)} %total.1.refs_4_.refs_1_), custom_call_target="tpu_custom_call" | custom-call | tf_op jit(solution)/shard_map/weight_rows/pallas_call | solution.py:48
  97.3 1.3 weight_rows.3
  99.2 1.6 %weight_rows.4 = (bf16[768,256]{1,0:T(8,128)(2,1)S(1)}, bf16[768,256]{1,0:T(8,128)(2,1)S(1)}) custom-call(s32[3]{0:T(128)S(1)} %pad_add_fusion.ids, bf16[192,2560]{1,0:T(8,128)(2,1)S(1)} %get-tuple-element.113.refs_0_, bf16[192,2560]{1,0:T(8,128)(2,1)S(1)} %collective-permute-done.19.refs_1_, bf16[192,2560]{1,0:T(8,128)(2,1)S(1)} %collective-permute-done.20.refs_2_, ...), custom_call_target="tpu_custom_call" | custom-call | tf_op jit(solution)/shard_map/weight_rows/pallas_call | solution.py:48
  101.2 1.4 collective-permute-done.30
  103.4 1.6 %collective-permute-start.32 = (bf16[256,256]{1,0:T(8,128)(2,1)S(1)}, bf16[256,256]{1,0:T(8,128)(2,1)S(1)}, u32[]{:S(2)}, u32[]{:S(2)}) collective-permute-start(bf16[256,256]{1,0:T(8,128)(2,1)S(1)} %slice.70), channel_id=1, source_target_pairs={{0,2},{1,3},{2,0},{3,1},{4,6},{5,7},{6,4},{7,5},{8,10},{9,11},{10,... | collective-permute-start | bytes 393224 | tf_op jit(solution)/shard_map/ppermute | solution.py:32
  106.7 2.4 %collective-permute-start.38 = (bf16[768,256]{1,0:T(8,128)(2,1)S(1)}, bf16[768,256]{1,0:T(8,128)(2,1)S(1)}, u32[]{:S(2)}, u32[]{:S(2)}) collective-permute-start(bf16[768,256]{1,0:T(8,128)(2,1)S(1)} %get-tuple-element.102), channel_id=1, source_target_pairs={{0,24},{8,16},{16,8},{24,0},{1,25},{9,17},{17,9},{25,1},{2,26},{10... | collective-permute-start | bytes 1179656 | tf_op jit(solution)/shard_map/ppermute | solution.py:32
  109.8 2.7 %collective-permute-start.33 = (bf16[256,256]{1,0:T(8,128)(2,1)S(1)}, bf16[256,256]{1,0:T(8,128)(2,1)S(1)}, u32[]{:S(2)}, u32[]{:S(2)}) collective-permute-start(bf16[256,256]{1,0:T(8,128)(2,1)S(1)} %fusion.1), channel_id=1, source_target_pairs={{0,4},{1,5},{2,6},{3,7},{4,0},{5,1},{6,2},{7,3},{8,12},{9,13},{10,... | collective-permute-start | bytes 393224 | tf_op jit(solution)/shard_map/ppermute | solution.py:32
  112.5 2.5 %collective-permute-done.34 = bf16[384,256]{1,0:T(8,128)(2,1)S(1)} collective-permute-done((bf16[384,256]{1,0:T(8,128)(2,1)S(1)}, bf16[384,256]{1,0:T(8,128)(2,1)S(1)}, u32[]{:S(2)}, u32[]{:S(2)}) %collective-permute-start.34) | collective-permute-done | bytes 196640 | tf_op jit(solution)/shard_map/ppermute | solution.py:32
  115.0 1.7 %collective-permute-start.35 = (bf16[384,256]{1,0:T(8,128)(2,1)S(1)}, bf16[384,256]{1,0:T(8,128)(2,1)S(1)}, u32[]{:S(2)}, u32[]{:S(2)}) collective-permute-start(bf16[384,256]{1,0:T(8,128)(2,1)S(1)} %fusion), channel_id=1, source_target_pairs={{0,4},{1,5},{2,6},{3,7},{4,0},{5,1},{6,2},{7,3},{8,12},{9,13},{10,... | collective-permute-start | bytes 589832 | tf_op jit(solution)/shard_map/ppermute | solution.py:32
  116.7 6.4 %collective-permute-done.33 = bf16[256,256]{1,0:T(8,128)(2,1)S(1)} collective-permute-done((bf16[256,256]{1,0:T(8,128)(2,1)S(1)}, bf16[256,256]{1,0:T(8,128)(2,1)S(1)}, u32[]{:S(2)}, u32[]{:S(2)}) %collective-permute-start.33) | collective-permute-done | bytes 131104 | tf_op jit(solution)/shard_map/ppermute | solution.py:32
  123.2 1.7 %collective-permute-done.37 = bf16[768,256]{1,0:T(8,128)(2,1)S(1)} collective-permute-done((bf16[768,256]{1,0:T(8,128)(2,1)S(1)}, bf16[768,256]{1,0:T(8,128)(2,1)S(1)}, u32[]{:S(2)}, u32[]{:S(2)}) %collective-permute-start.37) | collective-permute-done | bytes 393248 | tf_op jit(solution)/shard_map/ppermute | solution.py:32
  125.1 1.6 %collective-permute-start.39 = (bf16[384,256]{1,0:T(8,128)(2,1)S(1)}, bf16[384,256]{1,0:T(8,128)(2,1)S(1)}, u32[]{:S(2)}, u32[]{:S(2)}) collective-permute-start(bf16[384,256]{1,0:T(8,128)(2,1)S(1)} %slice.68), channel_id=1, source_target_pairs={{0,2},{1,3},{2,0},{3,1},{4,6},{5,7},{6,4},{7,5},{8,10},{9,11},{10,... | collective-permute-start | bytes 589832 | tf_op jit(solution)/shard_map/ppermute | solution.py:32
  127.1 4.1 %collective-permute-done.39 = bf16[384,256]{1,0:T(8,128)(2,1)S(1)} collective-permute-done((bf16[384,256]{1,0:T(8,128)(2,1)S(1)}, bf16[384,256]{1,0:T(8,128)(2,1)S(1)}, u32[]{:S(2)}, u32[]{:S(2)}) %collective-permute-start.39) | collective-permute-done | bytes 196640 | tf_op jit(solution)/shard_map/ppermute | solution.py:32
  131.3 2.3 %collective-permute-start.46 = (bf16[384,256]{1,0:T(8,128)(2,1)S(1)}, bf16[384,256]{1,0:T(8,128)(2,1)S(1)}, u32[]{:S(2)}, u32[]{:S(2)}) collective-permute-start(bf16[384,256]{1,0:T(8,128)(2,1)S(1)} %get-tuple-element.111), channel_id=1, source_target_pairs={{0,4},{1,5},{2,6},{3,7},{4,0},{5,1},{6,2},{7,3},{8,12},{9,13},{10,... | collective-permute-start | bytes 589832 | tf_op jit(solution)/shard_map/ppermute | solution.py:32
  133.5 1.5 collective-permute-start.40
  135.6 6.0 %collective-permute-done.40.refs_1_ = bf16[256,256]{1,0:T(8,128)(2,1)S(1)} collective-permute-done((bf16[256,256]{1,0:T(8,128)(2,1)S(1)}, bf16[256,256]{1,0:T(8,128)(2,1)S(1)}, u32[]{:S(2)}, u32[]{:S(2)}) %collective-permute-start.40) | collective-permute-done | bytes 131104 | tf_op jit(solution)/shard_map/ppermute | solution.py:32
  141.6 1.3 collective-permute-done.42.refs_3_
  143.9 1.5 collective-permute-done.43.refs_5_
  145.9 3.9 %collective-permute-done.47.refs_3_ = bf16[384,256]{1,0:T(8,128)(2,1)S(1)} collective-permute-done((bf16[384,256]{1,0:T(8,128)(2,1)S(1)}, bf16[384,256]{1,0:T(8,128)(2,1)S(1)}, u32[]{:S(2)}, u32[]{:S(2)}) %collective-permute-start.47) | collective-permute-done | bytes 196640 | tf_op jit(solution)/shard_map/ppermute | solution.py:32
  149.9 2.2 %assemble.2 = (f32[4096,128]{1,0:T(8,128)}, f32[4096,128]{1,0:T(8,128)}) custom-call(s32[3]{0:T(128)S(1)} %pad_add_fusion.ids, bf16[256,256]{1,0:T(8,128)(2,1)S(1)} %add_convert_fusion.2.refs_0_, bf16[256,256]{1,0:T(8,128)(2,1)S(1)} %collective-permute-done.40.refs_1_, bf16[256,256]{1,0:T(8,128)(2,1)S(1)} %collective-permute-done.41.refs_2_, ...), custom_call_target="tpu_custom_call" | custom-call | tf_op jit(solution)/shard_map/assemble/pallas_call | solution.py:393
  152.1 1.8 %assemble.3 = (f32[4096,128]{1,0:T(8,128)}, f32[4096,128]{1,0:T(8,128)}) custom-call(s32[3]{0:T(128)S(1)} %pad_add_fusion.ids, f32[4096,128]{1,0:T(8,128)} %get-tuple-element.106.refs_0_, f32[4096,128]{1,0:T(8,128)} %get-tuple-element.107.refs_1_, bf16[384,256]{1,0:T(8,128)(2,1)S(1)} %add_convert_fusion.refs_2_, ...), custom_call_target="tpu_custom_call", output_to_operand_aliasing={{0}: (1, {}), {1}: (2, {})} | custom-call | tf_op jit(solution)/shard_map/assemble/pallas_call | solution.py:393
  (99 shorter events, 18.6 us)
Async XLA Ops:
  2.9 15.9 %collective-permute-start = (bf16[1024,256]{1,0:T(8,128)(2,1)}, bf16[1024,256]{1,0:T(8,128)(2,1)S(1)}, u32[]{:S(2)}, u32[]{:S(2)}) collective-permute-start(bf16[1024,256]{1,0:T(8,128)(2,1)} %pad_maximum_fusion), channel_id=1, source_target_pairs={{0,8},{8,0},{16,24},{24,16},{1,9},{9,1},{17,25},{25,17},{2,10},{10... | collective-permute-start | bytes 1572872 | tf_op jit(solution)/shard_map/ppermute | solution.py:32
  6.7 15.1 %collective-permute-start.2 = (bf16[1024,256]{1,0:T(8,128)(2,1)}, bf16[1024,256]{1,0:T(8,128)(2,1)S(1)}, u32[]{:S(2)}, u32[]{:S(2)}) collective-permute-start(bf16[1024,256]{1,0:T(8,128)(2,1)} %pad_maximum_fusion.1), channel_id=1, source_target_pairs={{0,16},{8,24},{16,0},{24,8},{1,17},{9,25},{17,1},{25,9},{2,18},{10... | collective-permute-start | bytes 1572872 | tf_op jit(solution)/shard_map/ppermute | solution.py:32
  8.2 24.9 %collective-permute-start.5 = (bf16[1024,256]{1,0:T(8,128)(2,1)}, bf16[1024,256]{1,0:T(8,128)(2,1)}, u32[]{:S(2)}, u32[]{:S(2)}) collective-permute-start(bf16[1024,256]{1,0:T(8,128)(2,1)} %pad_maximum_fusion), channel_id=1, source_target_pairs={{0,16},{8,24},{16,0},{24,8},{1,17},{9,25},{17,1},{25,9},{2,18},{10... | collective-permute-start | bytes 1572872 | tf_op jit(solution)/shard_map/ppermute | solution.py:32
  8.7 24.4 %collective-permute-start.1 = (bf16[1024,256]{1,0:T(8,128)(2,1)}, bf16[1024,256]{1,0:T(8,128)(2,1)}, u32[]{:S(2)}, u32[]{:S(2)}) collective-permute-start(bf16[1024,256]{1,0:T(8,128)(2,1)} %pad_maximum_fusion.1), channel_id=1, source_target_pairs={{0,8},{8,0},{16,24},{24,16},{1,9},{9,1},{17,25},{25,17},{2,10},{10... | collective-permute-start | bytes 1572872 | tf_op jit(solution)/shard_map/ppermute | solution.py:32
  21.8 11.9 %collective-permute-start.3 = (bf16[1024,256]{1,0:T(8,128)(2,1)S(1)}, bf16[1024,256]{1,0:T(8,128)(2,1)}, u32[]{:S(2)}, u32[]{:S(2)}) collective-permute-start(bf16[1024,256]{1,0:T(8,128)(2,1)S(1)} %collective-permute-done.refs_2_), channel_id=1, source_target_pairs={{0,1},{1,0},{2,3},{3,2},{4,5},{5,4},{6,7},{7,6},{8,9},{9,8},{10,11... | collective-permute-start | bytes 1572872 | tf_op jit(solution)/shard_map/ppermute | solution.py:32
  21.8 21.0 %collective-permute-start.8 = (bf16[1024,256]{1,0:T(8,128)(2,1)S(1)}, bf16[1024,256]{1,0:T(8,128)(2,1)S(1)}, u32[]{:S(2)}, u32[]{:S(2)}) collective-permute-start(bf16[1024,256]{1,0:T(8,128)(2,1)S(1)} %collective-permute-done.refs_2_), channel_id=1, source_target_pairs={{0,16},{8,24},{16,0},{24,8},{1,17},{9,25},{17,1},{25,9},{2,18},{10... | collective-permute-start | bytes 1572872 | tf_op jit(solution)/shard_map/ppermute | solution.py:32
  23.3 19.5 %collective-permute-start.9 = (bf16[1024,256]{1,0:T(8,128)(2,1)S(1)}, bf16[1024,256]{1,0:T(8,128)(2,1)S(1)}, u32[]{:S(2)}, u32[]{:S(2)}) collective-permute-start(bf16[1024,256]{1,0:T(8,128)(2,1)S(1)} %collective-permute-done.2.refs_7_), channel_id=1, source_target_pairs={{0,8},{8,0},{16,24},{24,16},{1,9},{9,1},{17,25},{25,17},{2,10},{10... | collective-permute-start | bytes 1572872 | tf_op jit(solution)/shard_map/ppermute | solution.py:32
  33.1 3.2 %collective-permute-start.6 = (bf16[1024,256]{1,0:T(8,128)(2,1)}, bf16[1024,256]{1,0:T(8,128)(2,1)S(1)}, u32[]{:S(2)}, u32[]{:S(2)}) collective-permute-start(bf16[1024,256]{1,0:T(8,128)(2,1)} %collective-permute-done.5.refs_6_), channel_id=1, source_target_pairs={{0,1},{1,0},{2,3},{3,2},{4,5},{5,4},{6,7},{7,6},{8,9},{9,8},{10,11... | collective-permute-start | bytes 1572872 | tf_op jit(solution)/shard_map/ppermute | solution.py:32
  33.1 3.6 %collective-permute-start.4 = (bf16[1024,256]{1,0:T(8,128)(2,1)}, bf16[1024,256]{1,0:T(8,128)(2,1)S(1)}, u32[]{:S(2)}, u32[]{:S(2)}) collective-permute-start(bf16[1024,256]{1,0:T(8,128)(2,1)} %collective-permute-done.1.refs_3_), channel_id=1, source_target_pairs={{0,1},{1,0},{2,3},{3,2},{4,5},{5,4},{6,7},{7,6},{8,9},{9,8},{10,11... | collective-permute-start | bytes 1572872 | tf_op jit(solution)/shard_map/ppermute | solution.py:32
  33.6 3.1 %collective-permute-start.7 = (bf16[1024,256]{1,0:T(8,128)(2,1)S(1)}, bf16[1024,256]{1,0:T(8,128)(2,1)S(1)}, u32[]{:S(2)}, u32[]{:S(2)}) collective-permute-start(bf16[1024,256]{1,0:T(8,128)(2,1)S(1)} %collective-permute-done.2.refs_7_), channel_id=1, source_target_pairs={{0,1},{1,0},{2,3},{3,2},{4,5},{5,4},{6,7},{7,6},{8,9},{9,8},{10,11... | collective-permute-start | bytes 1572872 | tf_op jit(solution)/shard_map/ppermute | solution.py:32
  42.8 2.1 %collective-permute-start.10 = (bf16[1024,256]{1,0:T(8,128)(2,1)S(1)}, bf16[1024,256]{1,0:T(8,128)(2,1)S(1)}, u32[]{:S(2)}, u32[]{:S(2)}) collective-permute-start(bf16[1024,256]{1,0:T(8,128)(2,1)S(1)} %collective-permute-done.8.refs_1_), channel_id=1, source_target_pairs={{0,1},{1,0},{2,3},{3,2},{4,5},{5,4},{6,7},{7,6},{8,9},{9,8},{10,11... | collective-permute-start | bytes 1572872 | tf_op jit(solution)/shard_map/ppermute | solution.py:32
  42.9 2.6 %collective-permute-start.11 = (bf16[1024,256]{1,0:T(8,128)(2,1)S(1)}, bf16[1024,256]{1,0:T(8,128)(2,1)S(1)}, u32[]{:S(2)}, u32[]{:S(2)}) collective-permute-start(bf16[1024,256]{1,0:T(8,128)(2,1)S(1)} %collective-permute-done.9.refs_2_), channel_id=1, source_target_pairs={{0,1},{1,0},{2,3},{3,2},{4,5},{5,4},{6,7},{7,6},{8,9},{9,8},{10,11... | collective-permute-start | bytes 1572872 | tf_op jit(solution)/shard_map/ppermute | solution.py:32
  43.4 29.5 %collective-permute-start.20 = (bf16[192,2560]{1,0:T(8,128)(2,1)S(1)}, bf16[192,2560]{1,0:T(8,128)(2,1)S(1)}, u32[]{:S(2)}, u32[]{:S(2)}) collective-permute-start(bf16[192,2560]{1,0:T(8,128)(2,1)S(1)} %get-tuple-element.75), channel_id=1, source_target_pairs={{0,16},{8,24},{16,0},{24,8},{1,17},{9,25},{17,1},{25,9},{2,18},{10... | collective-permute-start | bytes 2949128 | tf_op jit(solution)/shard_map/ppermute | solution.py:32
  45.5 27.3 %collective-permute-start.19 = (bf16[192,2560]{1,0:T(8,128)(2,1)S(1)}, bf16[192,2560]{1,0:T(8,128)(2,1)S(1)}, u32[]{:S(2)}, u32[]{:S(2)}) collective-permute-start(bf16[192,2560]{1,0:T(8,128)(2,1)S(1)} %get-tuple-element.74), channel_id=1, source_target_pairs={{0,8},{8,0},{16,24},{24,16},{1,9},{9,1},{17,25},{25,17},{2,10},{10... | collective-permute-start | bytes 2949128 | tf_op jit(solution)/shard_map/ppermute | solution.py:32
  47.0 7.6 %collective-permute-start.14 = (bf16[192,256]{1,0:T(8,128)(2,1)S(1)}, bf16[192,256]{1,0:T(8,128)(2,1)S(1)}, u32[]{:S(2)}, u32[]{:S(2)}) collective-permute-start(bf16[192,256]{1,0:T(8,128)(2,1)S(1)} %project.3.refs_0_), channel_id=1, source_target_pairs={{0,6},{1,7},{2,4},{3,5},{4,2},{5,3},{6,0},{7,1},{8,14},{9,15},{10,... | collective-permute-start | bytes 294920 | tf_op jit(solution)/shard_map/ppermute | solution.py:32
  50.9 8.3 %collective-permute-start.13 = (bf16[192,256]{1,0:T(8,128)(2,1)S(1)}, bf16[192,256]{1,0:T(8,128)(2,1)S(1)}, u32[]{:S(2)}, u32[]{:S(2)}) collective-permute-start(bf16[192,256]{1,0:T(8,128)(2,1)S(1)} %project.3.refs_0_), channel_id=1, source_target_pairs={{0,4},{1,5},{2,6},{3,7},{4,0},{5,1},{6,2},{7,3},{8,12},{9,13},{10,... | collective-permute-start | bytes 294920 | tf_op jit(solution)/shard_map/ppermute | solution.py:32
  50.9 8.3 %collective-permute-start.12 = (bf16[192,256]{1,0:T(8,128)(2,1)S(1)}, bf16[192,256]{1,0:T(8,128)(2,1)S(1)}, u32[]{:S(2)}, u32[]{:S(2)}) collective-permute-start(bf16[192,256]{1,0:T(8,128)(2,1)S(1)} %project.3.refs_0_), channel_id=1, source_target_pairs={{0,2},{1,3},{2,0},{3,1},{4,6},{5,7},{6,4},{7,5},{8,10},{9,11},{10,... | collective-permute-start | bytes 294920 | tf_op jit(solution)/shard_map/ppermute | solution.py:32
  59.2 33.1 %collective-permute-start.28 = (bf16[192,2560]{1,0:T(8,128)(2,1)S(1)}, bf16[192,2560]{1,0:T(8,128)(2,1)S(1)}, u32[]{:S(2)}, u32[]{:S(2)}) collective-permute-start(bf16[192,2560]{1,0:T(8,128)(2,1)S(1)} %get-tuple-element.85), channel_id=1, source_target_pairs={{0,24},{8,16},{16,8},{24,0},{1,25},{9,17},{17,9},{25,1},{2,26},{10... | collective-permute-start | bytes 2949128 | tf_op jit(solution)/shard_map/ppermute | solution.py:32
  61.6 1.5 collective-permute-start.16
  63.1 1.3 collective-permute-start.18
  72.9 1.7 %collective-permute-start.21 = (bf16[768,256]{1,0:T(8,128)(2,1)S(1)}, bf16[768,256]{1,0:T(8,128)(2,1)S(1)}, u32[]{:S(2)}, u32[]{:S(2)}) collective-permute-start(bf16[768,256]{1,0:T(8,128)(2,1)S(1)} %get-tuple-element.79), channel_id=1, source_target_pairs={{0,1},{1,0},{2,3},{3,2},{4,5},{5,4},{6,7},{7,6},{8,9},{9,8},{10,11... | collective-permute-start | bytes 1179656 | tf_op jit(solution)/shard_map/ppermute | solution.py:32
  74.7 6.6 %collective-permute-start.22 = (bf16[192,256]{1,0:T(8,128)(2,1)S(1)}, bf16[192,256]{1,0:T(8,128)(2,1)S(1)}, u32[]{:S(2)}, u32[]{:S(2)}) collective-permute-start(bf16[192,256]{1,0:T(8,128)(2,1)S(1)} %get-tuple-element.81), channel_id=1, source_target_pairs={{0,2},{1,3},{2,0},{3,1},{4,6},{5,7},{6,4},{7,5},{8,10},{9,11},{10,... | collective-permute-start | bytes 294920 | tf_op jit(solution)/shard_map/ppermute | solution.py:32
  75.3 10.8 %collective-permute-start.23 = (bf16[192,256]{1,0:T(8,128)(2,1)S(1)}, bf16[192,256]{1,0:T(8,128)(2,1)S(1)}, u32[]{:S(2)}, u32[]{:S(2)}) collective-permute-start(bf16[192,256]{1,0:T(8,128)(2,1)S(1)} %get-tuple-element.82), channel_id=1, source_target_pairs={{0,4},{1,5},{2,6},{3,7},{4,0},{5,1},{6,2},{7,3},{8,12},{9,13},{10,... | collective-permute-start | bytes 294920 | tf_op jit(solution)/shard_map/ppermute | solution.py:32
  77.8 8.3 %collective-permute-start.24 = (bf16[192,256]{1,0:T(8,128)(2,1)S(1)}, bf16[192,256]{1,0:T(8,128)(2,1)S(1)}, u32[]{:S(2)}, u32[]{:S(2)}) collective-permute-start(bf16[192,256]{1,0:T(8,128)(2,1)S(1)} %get-tuple-element.83), channel_id=1, source_target_pairs={{0,6},{1,7},{2,4},{3,5},{4,2},{5,3},{6,0},{7,1},{8,14},{9,15},{10,... | collective-permute-start | bytes 294920 | tf_op jit(solution)/shard_map/ppermute | solution.py:32
  86.2 8.2 %collective-permute-start.27 = (bf16[192,256]{1,0:T(8,128)(2,1)S(1)}, bf16[192,256]{1,0:T(8,128)(2,1)S(1)}, u32[]{:S(2)}, u32[]{:S(2)}) collective-permute-start(bf16[192,256]{1,0:T(8,128)(2,1)S(1)} %total.1.refs_4_.refs_1_), channel_id=1, source_target_pairs={{0,24},{8,16},{16,8},{24,0},{1,25},{9,17},{17,9},{25,1},{2,26},{10... | collective-permute-start | bytes 294920 | tf_op jit(solution)/shard_map/ppermute | solution.py:32
  86.7 8.9 %collective-permute-start.26 = (bf16[192,256]{1,0:T(8,128)(2,1)S(1)}, bf16[192,256]{1,0:T(8,128)(2,1)S(1)}, u32[]{:S(2)}, u32[]{:S(2)}) collective-permute-start(bf16[192,256]{1,0:T(8,128)(2,1)S(1)} %total.1.refs_4_.refs_1_), channel_id=1, source_target_pairs={{0,16},{8,24},{16,0},{24,8},{1,17},{9,25},{17,1},{25,9},{2,18},{10... | collective-permute-start | bytes 294920 | tf_op jit(solution)/shard_map/ppermute | solution.py:32
  88.2 7.4 %collective-permute-start.25 = (bf16[192,256]{1,0:T(8,128)(2,1)S(1)}, bf16[192,256]{1,0:T(8,128)(2,1)S(1)}, u32[]{:S(2)}, u32[]{:S(2)}) collective-permute-start(bf16[192,256]{1,0:T(8,128)(2,1)S(1)} %total.1.refs_4_.refs_1_), channel_id=1, source_target_pairs={{0,8},{8,0},{16,24},{24,16},{1,9},{9,1},{17,25},{25,17},{2,10},{10... | collective-permute-start | bytes 294920 | tf_op jit(solution)/shard_map/ppermute | solution.py:32
  97.2 5.5 %collective-permute-start.31 = (bf16[3072,256]{1,0:T(8,128)(2,1)S(1)}, bf16[3072,256]{1,0:T(8,128)(2,1)S(1)}, u32[]{:S(2)}, u32[]{:S(2)}) collective-permute-start(bf16[3072,256]{1,0:T(8,128)(2,1)S(1)} %get-tuple-element.96), channel_id=1, source_target_pairs={{0,1},{1,0},{2,3},{3,2},{4,5},{5,4},{6,7},{7,6},{8,9},{9,8},{10,11... | collective-permute-start | bytes 4718600 | tf_op jit(solution)/shard_map/ppermute | solution.py:32
  98.6 2.4 %collective-permute-start.29 = (bf16[512,256]{1,0:T(8,128)(2,1)S(1)}, bf16[512,256]{1,0:T(8,128)(2,1)S(1)}, u32[]{:S(2)}, u32[]{:S(2)}) collective-permute-start(bf16[512,256]{1,0:T(8,128)(2,1)S(1)} %get-tuple-element.91), channel_id=1, source_target_pairs={{0,1},{1,0},{2,3},{3,2},{4,5},{5,4},{6,7},{7,6},{8,9},{9,8},{10,11... | collective-permute-start | bytes 786440 | tf_op jit(solution)/shard_map/ppermute | solution.py:32
  100.8 1.8 %collective-permute-start.30 = (bf16[768,256]{1,0:T(8,128)(2,1)S(1)}, bf16[768,256]{1,0:T(8,128)(2,1)S(1)}, u32[]{:S(2)}, u32[]{:S(2)}) collective-permute-start(bf16[768,256]{1,0:T(8,128)(2,1)S(1)} %get-tuple-element.93), channel_id=1, source_target_pairs={{0,1},{1,0},{2,3},{3,2},{4,5},{5,4},{6,7},{7,6},{8,9},{9,8},{10,11... | collective-permute-start | bytes 1179656 | tf_op jit(solution)/shard_map/ppermute | solution.py:32
  103.4 6.4 %collective-permute-start.32 = (bf16[256,256]{1,0:T(8,128)(2,1)S(1)}, bf16[256,256]{1,0:T(8,128)(2,1)S(1)}, u32[]{:S(2)}, u32[]{:S(2)}) collective-permute-start(bf16[256,256]{1,0:T(8,128)(2,1)S(1)} %slice.70), channel_id=1, source_target_pairs={{0,2},{1,3},{2,0},{3,1},{4,6},{5,7},{6,4},{7,5},{8,10},{9,11},{10,... | collective-permute-start | bytes 393224 | tf_op jit(solution)/shard_map/ppermute | solution.py:32
  105.1 9.9 %collective-permute-start.34 = (bf16[384,256]{1,0:T(8,128)(2,1)S(1)}, bf16[384,256]{1,0:T(8,128)(2,1)S(1)}, u32[]{:S(2)}, u32[]{:S(2)}) collective-permute-start(bf16[384,256]{1,0:T(8,128)(2,1)S(1)} %slice.69), channel_id=1, source_target_pairs={{0,2},{1,3},{2,0},{3,1},{4,6},{5,7},{6,4},{7,5},{8,10},{9,11},{10,... | collective-permute-start | bytes 589832 | tf_op jit(solution)/shard_map/ppermute | solution.py:32
  105.6 17.6 %collective-permute-start.36 = (bf16[768,256]{1,0:T(8,128)(2,1)S(1)}, bf16[768,256]{1,0:T(8,128)(2,1)S(1)}, u32[]{:S(2)}, u32[]{:S(2)}) collective-permute-start(bf16[768,256]{1,0:T(8,128)(2,1)S(1)} %get-tuple-element.100), channel_id=1, source_target_pairs={{0,8},{8,0},{16,24},{24,16},{1,9},{9,1},{17,25},{25,17},{2,10},{10... | collective-permute-start | bytes 1179656 | tf_op jit(solution)/shard_map/ppermute | solution.py:32
  106.1 18.8 %collective-permute-start.37 = (bf16[768,256]{1,0:T(8,128)(2,1)S(1)}, bf16[768,256]{1,0:T(8,128)(2,1)S(1)}, u32[]{:S(2)}, u32[]{:S(2)}) collective-permute-start(bf16[768,256]{1,0:T(8,128)(2,1)S(1)} %get-tuple-element.101), channel_id=1, source_target_pairs={{0,16},{8,24},{16,0},{24,8},{1,17},{9,25},{17,1},{25,9},{2,18},{10... | collective-permute-start | bytes 1179656 | tf_op jit(solution)/shard_map/ppermute | solution.py:32
  106.7 18.2 %collective-permute-start.38 = (bf16[768,256]{1,0:T(8,128)(2,1)S(1)}, bf16[768,256]{1,0:T(8,128)(2,1)S(1)}, u32[]{:S(2)}, u32[]{:S(2)}) collective-permute-start(bf16[768,256]{1,0:T(8,128)(2,1)S(1)} %get-tuple-element.102), channel_id=1, source_target_pairs={{0,24},{8,16},{16,8},{24,0},{1,25},{9,17},{17,9},{25,1},{2,26},{10... | collective-permute-start | bytes 1179656 | tf_op jit(solution)/shard_map/ppermute | solution.py:32
  109.8 13.3 %collective-permute-start.33 = (bf16[256,256]{1,0:T(8,128)(2,1)S(1)}, bf16[256,256]{1,0:T(8,128)(2,1)S(1)}, u32[]{:S(2)}, u32[]{:S(2)}) collective-permute-start(bf16[256,256]{1,0:T(8,128)(2,1)S(1)} %fusion.1), channel_id=1, source_target_pairs={{0,4},{1,5},{2,6},{3,7},{4,0},{5,1},{6,2},{7,3},{8,12},{9,13},{10,... | collective-permute-start | bytes 393224 | tf_op jit(solution)/shard_map/ppermute | solution.py:32
  115.0 12.1 %collective-permute-start.35 = (bf16[384,256]{1,0:T(8,128)(2,1)S(1)}, bf16[384,256]{1,0:T(8,128)(2,1)S(1)}, u32[]{:S(2)}, u32[]{:S(2)}) collective-permute-start(bf16[384,256]{1,0:T(8,128)(2,1)S(1)} %fusion), channel_id=1, source_target_pairs={{0,4},{1,5},{2,6},{3,7},{4,0},{5,1},{6,2},{7,3},{8,12},{9,13},{10,... | collective-permute-start | bytes 589832 | tf_op jit(solution)/shard_map/ppermute | solution.py:32
  125.1 6.1 %collective-permute-start.39 = (bf16[384,256]{1,0:T(8,128)(2,1)S(1)}, bf16[384,256]{1,0:T(8,128)(2,1)S(1)}, u32[]{:S(2)}, u32[]{:S(2)}) collective-permute-start(bf16[384,256]{1,0:T(8,128)(2,1)S(1)} %slice.68), channel_id=1, source_target_pairs={{0,2},{1,3},{2,0},{3,1},{4,6},{5,7},{6,4},{7,5},{8,10},{9,11},{10,... | collective-permute-start | bytes 589832 | tf_op jit(solution)/shard_map/ppermute | solution.py:32
  131.3 10.3 %collective-permute-start.46 = (bf16[384,256]{1,0:T(8,128)(2,1)S(1)}, bf16[384,256]{1,0:T(8,128)(2,1)S(1)}, u32[]{:S(2)}, u32[]{:S(2)}) collective-permute-start(bf16[384,256]{1,0:T(8,128)(2,1)S(1)} %get-tuple-element.111), channel_id=1, source_target_pairs={{0,4},{1,5},{2,6},{3,7},{4,0},{5,1},{6,2},{7,3},{8,12},{9,13},{10,... | collective-permute-start | bytes 589832 | tf_op jit(solution)/shard_map/ppermute | solution.py:32
  133.5 8.0 %collective-permute-start.40 = (bf16[256,256]{1,0:T(8,128)(2,1)S(1)}, bf16[256,256]{1,0:T(8,128)(2,1)S(1)}, u32[]{:S(2)}, u32[]{:S(2)}) collective-permute-start(bf16[256,256]{1,0:T(8,128)(2,1)S(1)} %add_convert_fusion.2.refs_0_), channel_id=1, source_target_pairs={{0,2},{1,3},{2,0},{3,1},{4,6},{5,7},{6,4},{7,5},{8,10},{9,11},{10,... | collective-permute-start | bytes 393224 | tf_op jit(solution)/shard_map/ppermute | solution.py:32
  135.1 6.5 %collective-permute-start.41 = (bf16[256,256]{1,0:T(8,128)(2,1)S(1)}, bf16[256,256]{1,0:T(8,128)(2,1)S(1)}, u32[]{:S(2)}, u32[]{:S(2)}) collective-permute-start(bf16[256,256]{1,0:T(8,128)(2,1)S(1)} %add_convert_fusion.2.refs_0_), channel_id=1, source_target_pairs={{0,1},{1,0},{2,3},{3,2},{4,5},{5,4},{6,7},{7,6},{8,9},{9,8},{10,11... | collective-permute-start | bytes 393224 | tf_op jit(solution)/shard_map/ppermute | solution.py:32
  135.1 10.3 %collective-permute-start.43 = (bf16[384,256]{1,0:T(8,128)(2,1)S(1)}, bf16[384,256]{1,0:T(8,128)(2,1)S(1)}, u32[]{:S(2)}, u32[]{:S(2)}) collective-permute-start(bf16[384,256]{1,0:T(8,128)(2,1)S(1)} %add_convert_fusion.1.refs_4_), channel_id=1, source_target_pairs={{0,2},{1,3},{2,0},{3,1},{4,6},{5,7},{6,4},{7,5},{8,10},{9,11},{10,... | collective-permute-start | bytes 589832 | tf_op jit(solution)/shard_map/ppermute | solution.py:32
  141.5 1.3 collective-permute-start.42
  142.9 7.0 %collective-permute-start.47 = (bf16[384,256]{1,0:T(8,128)(2,1)S(1)}, bf16[384,256]{1,0:T(8,128)(2,1)S(1)}, u32[]{:S(2)}, u32[]{:S(2)}) collective-permute-start(bf16[384,256]{1,0:T(8,128)(2,1)S(1)} %add_convert_fusion.refs_2_), channel_id=1, source_target_pairs={{0,2},{1,3},{2,0},{3,1},{4,6},{5,7},{6,4},{7,5},{8,10},{9,11},{10,... | collective-permute-start | bytes 589832 | tf_op jit(solution)/shard_map/ppermute | solution.py:32
  143.9 5.9 %collective-permute-start.44 = (bf16[384,256]{1,0:T(8,128)(2,1)S(1)}, bf16[384,256]{1,0:T(8,128)(2,1)S(1)}, u32[]{:S(2)}, u32[]{:S(2)}) collective-permute-start(bf16[384,256]{1,0:T(8,128)(2,1)S(1)} %add_convert_fusion.1.refs_4_), channel_id=1, source_target_pairs={{0,1},{1,0},{2,3},{3,2},{4,5},{5,4},{6,7},{7,6},{8,9},{9,8},{10,11... | collective-permute-start | bytes 589832 | tf_op jit(solution)/shard_map/ppermute | solution.py:32
  145.4 4.5 %collective-permute-start.45 = (bf16[384,256]{1,0:T(8,128)(2,1)S(1)}, bf16[384,256]{1,0:T(8,128)(2,1)S(1)}, u32[]{:S(2)}, u32[]{:S(2)}) collective-permute-start(bf16[384,256]{1,0:T(8,128)(2,1)S(1)} %collective-permute-done.43.refs_5_), channel_id=1, source_target_pairs={{0,1},{1,0},{2,3},{3,2},{4,5},{5,4},{6,7},{7,6},{8,9},{9,8},{10,11... | collective-permute-start | bytes 589832 | tf_op jit(solution)/shard_map/ppermute | solution.py:32
  145.4 6.6 %collective-permute-start.48 = (bf16[384,256]{1,0:T(8,128)(2,1)S(1)}, bf16[384,256]{1,0:T(8,128)(2,1)S(1)}, u32[]{:S(2)}, u32[]{:S(2)}) collective-permute-start(bf16[384,256]{1,0:T(8,128)(2,1)S(1)} %add_convert_fusion.refs_2_), channel_id=1, source_target_pairs={{0,1},{1,0},{2,3},{3,2},{4,5},{5,4},{6,7},{7,6},{8,9},{9,8},{10,11... | collective-permute-start | bytes 589832 | tf_op jit(solution)/shard_map/ppermute | solution.py:32
  149.9 2.2 %collective-permute-start.49 = (bf16[384,256]{1,0:T(8,128)(2,1)S(1)}, bf16[384,256]{1,0:T(8,128)(2,1)S(1)}, u32[]{:S(2)}, u32[]{:S(2)}) collective-permute-start(bf16[384,256]{1,0:T(8,128)(2,1)S(1)} %collective-permute-done.47.refs_3_), channel_id=1, source_target_pairs={{0,1},{1,0},{2,3},{3,2},{4,5},{5,4},{6,7},{7,6},{8,9},{9,8},{10,11... | collective-permute-start | bytes 589832 | tf_op jit(solution)/shard_map/ppermute | solution.py:32
  (10 other events, 136.2 us)

commit v15 on v14

--- a/solution.py
+++ b/solution.py
@@ -525,9 +525,9 @@
     for part in moved_parts:
         part = scatter_along_z(part, sub_count)
         finals.append(sum_of_halves(part, sub_count))
-    part = scatter_along_z(sum_of(own), sub_count, finals[:TIED])
-    finals, _ = after(finals, part)
     blocks = gather_parts(finals[0], sub_count)
+    part = scatter_along_z(sum_of(own), sub_count, finals + blocks[:sub_count])
+    finals[1:], _ = after(finals[1:], part)
     last = sum_of_halves(part, sub_count)
     (last,), _ = after([last], *blocks)
     blocks += [one for final in finals[1:] for one in gather_parts(final, sub_count)]

time: 154 us -> 154 us (level)
  transfers between devices with their start and end apart: 50 -> 50, of which waited for: 29 -> 28; matrix products, arithmetic and copies ran while one was open for 3% -> 3% of each run, Pallas kernels for 12% -> 12%
where the time goes in v15:
time: 154 us
  waiting for transfers between devices  78.8 us (51%)
  starting transfers between devices  44.6 us (29%)
  Pallas kernels  21.4 us (14%)
  local copies, waits for them, and re-layouts  5.14 us (3%)
  other arithmetic  2.93 us (2%)
    ppermute x50, waiting for transfers between devices, swap(): return lax.ppermute(array, axis, [(i, i ^ distance) for i in range(count)])  78.8 us
    ppermute x50, starting transfers between devices, swap(): return lax.ppermute(array, axis, [(i, i ^ distance) for i in range(count)])  44.6 us
    pallas_call x7, Pallas kernels, kernel_call(): pl.pallas_call(kernel, out_shape=outs, in_specs=[smem] * len(scalars) + [...  9.06 us
    pallas_call x1, Pallas kernels, attention(): pl.pallas_call(functools.partial(attention_kernel, shape), out_shape=(jax...  8.45 us
    pallas_call x2, Pallas kernels, assemble(): pl.pallas_call(functools.partial(assemble_kernel, sub_count, regions, not...  3.92 us
  transfers between devices with their start and end apart: 50, of which 28 were waited for; matrix products, arithmetic and copies ran while one was open for 3% of the time, Pallas kernels for 12%

profile of v15, /device:TPU:0, one launch (start us, length us, event | category | flops | bytes accessed | tf_op | source)
XLA Modules:
  0.0 154.0 jit_solution(11522054194167189119)
XLA Ops:
  0.7 1.4 constant_dynamic-slice_fusion
  2.9 2.9 %collective-permute-start = (bf16[1024,256]{1,0:T(8,128)(2,1)}, bf16[1024,256]{1,0:T(8,128)(2,1)S(1)}, u32[]{:S(2)}, u32[]{:S(2)}) collective-permute-start(bf16[1024,256]{1,0:T(8,128)(2,1)} %pad_maximum_fusion), channel_id=1, source_target_pairs={{0,8},{8,0},{16,24},{24,16},{1,9},{9,1},{17,25},{25,17},{2,10},{10... | collective-permute-start | bytes 1572872 | tf_op jit(solution)/shard_map/ppermute | solution.py:32
  6.7 1.5 collective-permute-start.2
  8.8 10.0 %collective-permute-done.refs_2_ = bf16[1024,256]{1,0:T(8,128)(2,1)S(1)} collective-permute-done((bf16[1024,256]{1,0:T(8,128)(2,1)}, bf16[1024,256]{1,0:T(8,128)(2,1)S(1)}, u32[]{:S(2)}, u32[]{:S(2)}) %collective-permute-start) | collective-permute-done | bytes 524320 | tf_op jit(solution)/shard_map/ppermute | solution.py:32
  18.8 3.0 %collective-permute-done.2.refs_7_ = bf16[1024,256]{1,0:T(8,128)(2,1)S(1)} collective-permute-done((bf16[1024,256]{1,0:T(8,128)(2,1)}, bf16[1024,256]{1,0:T(8,128)(2,1)S(1)}, u32[]{:S(2)}, u32[]{:S(2)}) %collective-permute-start.2) | collective-permute-done | bytes 524320 | tf_op jit(solution)/shard_map/ppermute | solution.py:32
  21.8 1.5 collective-permute-start.8
  23.8 9.3 %collective-permute-done.5.refs_6_ = bf16[1024,256]{1,0:T(8,128)(2,1)} collective-permute-done((bf16[1024,256]{1,0:T(8,128)(2,1)}, bf16[1024,256]{1,0:T(8,128)(2,1)}, u32[]{:S(2)}, u32[]{:S(2)}) %collective-permute-start.5) | collective-permute-done | bytes 524320 | tf_op jit(solution)/shard_map/ppermute | solution.py:32
  33.8 2.5 %dynamic-slice_bitcast_fusion = (bf16[192,2560]{1,0:T(8,128)(2,1)S(1)}, bf16[192,2560]{1,0:T(8,128)(2,1)S(1)}, bf16[192,2560]{1,0:T(8,128)(2,1)S(1)}, bf16[192,2560]{1,0:T(8,128)(2,1)S(1)}) fusion(bf16[1,192,16384]{2,1,0:T(8,128)(2,1)} %param.7, s32[]{:T(128)S(6)} %select_n.42, s32[]{:T(128)S(6)} %select_n.40, s32[]{:T(128)S(6)} %select_n.39, s32[]{:T(128)S(6)} %select_n.41), kind=kLoop, calls=%fused_computation.1 | loop fusion | bytes 7864336 | tf_op jit(solution)/shard_map/dynamic_slice | solution.py:464
  37.8 3.2 %project.2.refs_0_ = f32[192,256]{1,0:T(8,128)S(1)} custom-call(s32[3]{0:T(128)S(1)} %pad_add_fusion.ids, bf16[192,16384]{1,0:T(8,128)(2,1)S(1)} %bitcast.19, bf16[4096,128]{1,0:T(8,128)(2,1)S(1)} %copy-done, bf16[4096,128]{1,0:T(8,128)(2,1)S(1)} %copy-done.1, bf16[1024,256]{1,0:T(8,128)(2,1)S(1)} %collective-permute-done.refs_2_, ...), custom_call_target="tpu_custom_call" | custom-call | bytes 16777216 | tf_op jit(solution)/shard_map/project/pallas_call | solution.py:48
  41.0 1.8 %collective-permute-done.8.refs_1_ = bf16[1024,256]{1,0:T(8,128)(2,1)S(1)} collective-permute-done((bf16[1024,256]{1,0:T(8,128)(2,1)S(1)}, bf16[1024,256]{1,0:T(8,128)(2,1)S(1)}, u32[]{:S(2)}, u32[]{:S(2)}) %collective-permute-start.8) | collective-permute-done | bytes 524320 | tf_op jit(solution)/shard_map/ppermute | solution.py:32
  43.4 1.5 collective-permute-start.20
  45.9 1.1 project.3.refs_0_
  47.0 3.9 %collective-permute-start.14 = (bf16[192,256]{1,0:T(8,128)(2,1)S(1)}, bf16[192,256]{1,0:T(8,128)(2,1)S(1)}, u32[]{:S(2)}, u32[]{:S(2)}) collective-permute-start(bf16[192,256]{1,0:T(8,128)(2,1)S(1)} %project.3.refs_0_), channel_id=1, source_target_pairs={{0,6},{1,7},{2,4},{3,5},{4,2},{5,3},{6,0},{7,1},{8,14},{9,15},{10,... | collective-permute-start | bytes 294920 | tf_op jit(solution)/shard_map/ppermute | solution.py:32
  51.5 3.1 %collective-permute-done.14.refs_6_ = bf16[192,256]{1,0:T(8,128)(2,1)S(1)} collective-permute-done((bf16[192,256]{1,0:T(8,128)(2,1)S(1)}, bf16[192,256]{1,0:T(8,128)(2,1)S(1)}, u32[]{:S(2)}, u32[]{:S(2)}) %collective-permute-start.14) | collective-permute-done | bytes 98336 | tf_op jit(solution)/shard_map/ppermute | solution.py:32
  54.6 4.6 %collective-permute-done.13.refs_4_ = bf16[192,256]{1,0:T(8,128)(2,1)S(1)} collective-permute-done((bf16[192,256]{1,0:T(8,128)(2,1)S(1)}, bf16[192,256]{1,0:T(8,128)(2,1)S(1)}, u32[]{:S(2)}, u32[]{:S(2)}) %collective-permute-start.13) | collective-permute-done | bytes 98336 | tf_op jit(solution)/shard_map/ppermute | solution.py:32
  59.2 2.5 %collective-permute-start.28 = (bf16[192,2560]{1,0:T(8,128)(2,1)S(1)}, bf16[192,2560]{1,0:T(8,128)(2,1)S(1)}, u32[]{:S(2)}, u32[]{:S(2)}) collective-permute-start(bf16[192,2560]{1,0:T(8,128)(2,1)S(1)} %get-tuple-element.84), channel_id=1, source_target_pairs={{0,24},{8,16},{16,8},{24,0},{1,25},{9,17},{17,9},{25,1},{2,26},{10... | collective-permute-start | bytes 2949128 | tf_op jit(solution)/shard_map/ppermute | solution.py:32
  64.4 8.4 %attention.1 = (bf16[192,1024]{1,0:T(8,128)(2,1)}, f32[768,256]{1,0:T(8,128)S(1)}, bf16[768,256]{1,0:T(8,128)(2,1)S(1)}) custom-call(s32[1]{0:T(128)} %bitcast.ids, s32[16]{0:T(128)S(1)} %copy-done.4, s32[8]{0:T(128)S(1)} %bitcast.24, bf16[192,1024]{1,0:T(8,128)(2,1)S(1)} %bitcast.22, bf16[192,1024]{1,0:T(8,128)(2,1)S(1)} %bitcast.23, ...), custom_call_target="tpu_custom_call" | custom-call | tf_op jit(solution)/shard_map/attention/pallas_call | solution.py:171
  73.2 1.4 collective-permute-done.21.came
  75.3 2.6 %collective-permute-start.23 = (bf16[192,256]{1,0:T(8,128)(2,1)S(1)}, bf16[192,256]{1,0:T(8,128)(2,1)S(1)}, u32[]{:S(2)}, u32[]{:S(2)}) collective-permute-start(bf16[192,256]{1,0:T(8,128)(2,1)S(1)} %get-tuple-element.81), channel_id=1, source_target_pairs={{0,4},{1,5},{2,6},{3,7},{4,0},{5,1},{6,2},{7,3},{8,12},{9,13},{10,... | collective-permute-start | bytes 294920 | tf_op jit(solution)/shard_map/ppermute | solution.py:32
  77.9 1.3 collective-permute-start.24
  79.2 2.2 %collective-permute-done.22.refs_1_ = bf16[192,256]{1,0:T(8,128)(2,1)S(1)} collective-permute-done((bf16[192,256]{1,0:T(8,128)(2,1)S(1)}, bf16[192,256]{1,0:T(8,128)(2,1)S(1)}, u32[]{:S(2)}, u32[]{:S(2)}) %collective-permute-start.22) | collective-permute-done | bytes 98336 | tf_op jit(solution)/shard_map/ppermute | solution.py:32
  81.3 4.8 %collective-permute-done.23.refs_2_ = bf16[192,256]{1,0:T(8,128)(2,1)S(1)} collective-permute-done((bf16[192,256]{1,0:T(8,128)(2,1)S(1)}, bf16[192,256]{1,0:T(8,128)(2,1)S(1)}, u32[]{:S(2)}, u32[]{:S(2)}) %collective-permute-start.23) | collective-permute-done | bytes 98336 | tf_op jit(solution)/shard_map/ppermute | solution.py:32
  86.7 1.5 collective-permute-start.26
  88.2 1.5 collective-permute-start.25
  89.7 2.6 %collective-permute-done.28.refs_3_ = bf16[192,2560]{1,0:T(8,128)(2,1)S(1)} collective-permute-done((bf16[192,2560]{1,0:T(8,128)(2,1)S(1)}, bf16[192,2560]{1,0:T(8,128)(2,1)S(1)}, u32[]{:S(2)}, u32[]{:S(2)}) %collective-permute-start.28) | collective-permute-done | bytes 983072 | tf_op jit(solution)/shard_map/ppermute | solution.py:32
  92.3 2.1 %collective-permute-done.27.refs_7_ = bf16[192,256]{1,0:T(8,128)(2,1)S(1)} collective-permute-done((bf16[192,256]{1,0:T(8,128)(2,1)S(1)}, bf16[192,256]{1,0:T(8,128)(2,1)S(1)}, u32[]{:S(2)}, u32[]{:S(2)}) %collective-permute-start.27) | collective-permute-done | bytes 98336 | tf_op jit(solution)/shard_map/ppermute | solution.py:32
  94.3 1.3 collective-permute-done.26.refs_6_
  95.6 1.7 %weight_rows.5 = (bf16[3072,256]{1,0:T(8,128)(2,1)S(1)}, bf16[3072,256]{1,0:T(8,128)(2,1)S(1)}) custom-call(s32[3]{0:T(128)S(1)} %pad_add_fusion.ids, bf16[192,16384]{1,0:T(8,128)(2,1)S(1)} %bitcast.21, bf16[192,256]{1,0:T(8,128)(2,1)S(1)} %total.1.refs_4_.refs_1_), custom_call_target="tpu_custom_call" | custom-call | tf_op jit(solution)/shard_map/weight_rows/pallas_call | solution.py:48
  97.3 1.3 weight_rows.3
  99.2 1.6 %weight_rows.4 = (bf16[768,256]{1,0:T(8,128)(2,1)S(1)}, bf16[768,256]{1,0:T(8,128)(2,1)S(1)}) custom-call(s32[3]{0:T(128)S(1)} %pad_add_fusion.ids, bf16[192,2560]{1,0:T(8,128)(2,1)S(1)} %get-tuple-element.111.refs_0_, bf16[192,2560]{1,0:T(8,128)(2,1)S(1)} %collective-permute-done.19.refs_1_, bf16[192,2560]{1,0:T(8,128)(2,1)S(1)} %collective-permute-done.20.refs_2_, ...), custom_call_target="tpu_custom_call" | custom-call | tf_op jit(solution)/shard_map/weight_rows/pallas_call | solution.py:48
  101.2 1.4 collective-permute-done.30
  103.4 1.6 %collective-permute-start.32 = (bf16[256,256]{1,0:T(8,128)(2,1)S(1)}, bf16[256,256]{1,0:T(8,128)(2,1)S(1)}, u32[]{:S(2)}, u32[]{:S(2)}) collective-permute-start(bf16[256,256]{1,0:T(8,128)(2,1)S(1)} %slice.70), channel_id=1, source_target_pairs={{0,2},{1,3},{2,0},{3,1},{4,6},{5,7},{6,4},{7,5},{8,10},{9,11},{10,... | collective-permute-start | bytes 393224 | tf_op jit(solution)/shard_map/ppermute | solution.py:32
  106.7 2.4 %collective-permute-start.41 = (bf16[768,256]{1,0:T(8,128)(2,1)S(1)}, bf16[768,256]{1,0:T(8,128)(2,1)S(1)}, u32[]{:S(2)}, u32[]{:S(2)}) collective-permute-start(bf16[768,256]{1,0:T(8,128)(2,1)S(1)} %get-tuple-element.101), channel_id=1, source_target_pairs={{0,24},{8,16},{16,8},{24,0},{1,25},{9,17},{17,9},{25,1},{2,26},{10... | collective-permute-start | bytes 1179656 | tf_op jit(solution)/shard_map/ppermute | solution.py:32
  109.8 2.7 %collective-permute-start.33 = (bf16[256,256]{1,0:T(8,128)(2,1)S(1)}, bf16[256,256]{1,0:T(8,128)(2,1)S(1)}, u32[]{:S(2)}, u32[]{:S(2)}) collective-permute-start(bf16[256,256]{1,0:T(8,128)(2,1)S(1)} %fusion.1), channel_id=1, source_target_pairs={{0,4},{1,5},{2,6},{3,7},{4,0},{5,1},{6,2},{7,3},{8,12},{9,13},{10,... | collective-permute-start | bytes 393224 | tf_op jit(solution)/shard_map/ppermute | solution.py:32
  112.5 2.4 %collective-permute-done.37 = bf16[384,256]{1,0:T(8,128)(2,1)S(1)} collective-permute-done((bf16[384,256]{1,0:T(8,128)(2,1)S(1)}, bf16[384,256]{1,0:T(8,128)(2,1)S(1)}, u32[]{:S(2)}, u32[]{:S(2)}) %collective-permute-start.37) | collective-permute-done | bytes 196640 | tf_op jit(solution)/shard_map/ppermute | solution.py:32
  115.0 1.7 %collective-permute-start.38 = (bf16[384,256]{1,0:T(8,128)(2,1)S(1)}, bf16[384,256]{1,0:T(8,128)(2,1)S(1)}, u32[]{:S(2)}, u32[]{:S(2)}) collective-permute-start(bf16[384,256]{1,0:T(8,128)(2,1)S(1)} %fusion), channel_id=1, source_target_pairs={{0,4},{1,5},{2,6},{3,7},{4,0},{5,1},{6,2},{7,3},{8,12},{9,13},{10,... | collective-permute-start | bytes 589832 | tf_op jit(solution)/shard_map/ppermute | solution.py:32
  116.7 6.4 %collective-permute-done.33 = bf16[256,256]{1,0:T(8,128)(2,1)S(1)} collective-permute-done((bf16[256,256]{1,0:T(8,128)(2,1)S(1)}, bf16[256,256]{1,0:T(8,128)(2,1)S(1)}, u32[]{:S(2)}, u32[]{:S(2)}) %collective-permute-start.33) | collective-permute-done | bytes 131104 | tf_op jit(solution)/shard_map/ppermute | solution.py:32
  123.9 1.0 collective-permute-done.40
  125.1 1.6 %collective-permute-start.42 = (bf16[384,256]{1,0:T(8,128)(2,1)S(1)}, bf16[384,256]{1,0:T(8,128)(2,1)S(1)}, u32[]{:S(2)}, u32[]{:S(2)}) collective-permute-start(bf16[384,256]{1,0:T(8,128)(2,1)S(1)} %slice.68), channel_id=1, source_target_pairs={{0,2},{1,3},{2,0},{3,1},{4,6},{5,7},{6,4},{7,5},{8,10},{9,11},{10,... | collective-permute-start | bytes 589832 | tf_op jit(solution)/shard_map/ppermute | solution.py:32
  126.7 3.1 %collective-permute-done.34.refs_1_ = bf16[256,256]{1,0:T(8,128)(2,1)S(1)} collective-permute-done((bf16[256,256]{1,0:T(8,128)(2,1)S(1)}, bf16[256,256]{1,0:T(8,128)(2,1)S(1)}, u32[]{:S(2)}, u32[]{:S(2)}) %collective-permute-start.34) | collective-permute-done | bytes 131104 | tf_op jit(solution)/shard_map/ppermute | solution.py:32
  129.9 2.7 %collective-permute-done.42 = bf16[384,256]{1,0:T(8,128)(2,1)S(1)} collective-permute-done((bf16[384,256]{1,0:T(8,128)(2,1)S(1)}, bf16[384,256]{1,0:T(8,128)(2,1)S(1)}, u32[]{:S(2)}, u32[]{:S(2)}) %collective-permute-start.42) | collective-permute-done | bytes 196640 | tf_op jit(solution)/shard_map/ppermute | solution.py:32
  132.7 1.9 %collective-permute-start.46 = (bf16[384,256]{1,0:T(8,128)(2,1)S(1)}, bf16[384,256]{1,0:T(8,128)(2,1)S(1)}, u32[]{:S(2)}, u32[]{:S(2)}) collective-permute-start(bf16[384,256]{1,0:T(8,128)(2,1)S(1)} %get-tuple-element.109), channel_id=1, source_target_pairs={{0,4},{1,5},{2,6},{3,7},{4,0},{5,1},{6,2},{7,3},{8,12},{9,13},{10,... | collective-permute-start | bytes 589832 | tf_op jit(solution)/shard_map/ppermute | solution.py:32
  135.1 2.0 %collective-permute-start.43 = (bf16[384,256]{1,0:T(8,128)(2,1)S(1)}, bf16[384,256]{1,0:T(8,128)(2,1)S(1)}, u32[]{:S(2)}, u32[]{:S(2)}) collective-permute-start(bf16[384,256]{1,0:T(8,128)(2,1)S(1)} %add_convert_fusion.1.refs_4_), channel_id=1, source_target_pairs={{0,2},{1,3},{2,0},{3,1},{4,6},{5,7},{6,4},{7,5},{8,10},{9,11},{10,... | collective-permute-start | bytes 589832 | tf_op jit(solution)/shard_map/ppermute | solution.py:32
  137.2 6.2 %collective-permute-done.46 = bf16[384,256]{1,0:T(8,128)(2,1)S(1)} collective-permute-done((bf16[384,256]{1,0:T(8,128)(2,1)S(1)}, bf16[384,256]{1,0:T(8,128)(2,1)S(1)}, u32[]{:S(2)}, u32[]{:S(2)}) %collective-permute-start.46) | collective-permute-done | bytes 196640 | tf_op jit(solution)/shard_map/ppermute | solution.py:32
  144.1 1.8 %collective-permute-done.43.refs_5_ = bf16[384,256]{1,0:T(8,128)(2,1)S(1)} collective-permute-done((bf16[384,256]{1,0:T(8,128)(2,1)S(1)}, bf16[384,256]{1,0:T(8,128)(2,1)S(1)}, u32[]{:S(2)}, u32[]{:S(2)}) %collective-permute-start.43) | collective-permute-done | bytes 196640 | tf_op jit(solution)/shard_map/ppermute | solution.py:32
  145.9 3.9 %collective-permute-done.47.refs_3_ = bf16[384,256]{1,0:T(8,128)(2,1)S(1)} collective-permute-done((bf16[384,256]{1,0:T(8,128)(2,1)S(1)}, bf16[384,256]{1,0:T(8,128)(2,1)S(1)}, u32[]{:S(2)}, u32[]{:S(2)}) %collective-permute-start.47) | collective-permute-done | bytes 196640 | tf_op jit(solution)/shard_map/ppermute | solution.py:32
  149.9 2.2 %assemble.2 = (f32[4096,128]{1,0:T(8,128)}, f32[4096,128]{1,0:T(8,128)}) custom-call(s32[3]{0:T(128)S(1)} %pad_add_fusion.ids, bf16[256,256]{1,0:T(8,128)(2,1)S(1)} %add_convert_fusion.2.refs_0_, bf16[256,256]{1,0:T(8,128)(2,1)S(1)} %collective-permute-done.34.refs_1_, bf16[256,256]{1,0:T(8,128)(2,1)S(1)} %collective-permute-done.35.refs_2_, ...), custom_call_target="tpu_custom_call" | custom-call | tf_op jit(solution)/shard_map/assemble/pallas_call | solution.py:393
  152.1 1.8 %assemble.3 = (f32[4096,128]{1,0:T(8,128)}, f32[4096,128]{1,0:T(8,128)}) custom-call(s32[3]{0:T(128)S(1)} %pad_add_fusion.ids, f32[4096,128]{1,0:T(8,128)} %get-tuple-element.104.refs_0_, f32[4096,128]{1,0:T(8,128)} %get-tuple-element.105.refs_1_, bf16[384,256]{1,0:T(8,128)(2,1)S(1)} %add_convert_fusion.refs_2_, ...), custom_call_target="tpu_custom_call", output_to_operand_aliasing={{0}: (1, {}), {1}: (2, {})} | custom-call | tf_op jit(solution)/shard_map/assemble/pallas_call | solution.py:393
  (99 shorter events, 18.0 us)
Async XLA Ops:
  2.9 15.9 %collective-permute-start = (bf16[1024,256]{1,0:T(8,128)(2,1)}, bf16[1024,256]{1,0:T(8,128)(2,1)S(1)}, u32[]{:S(2)}, u32[]{:S(2)}) collective-permute-start(bf16[1024,256]{1,0:T(8,128)(2,1)} %pad_maximum_fusion), channel_id=1, source_target_pairs={{0,8},{8,0},{16,24},{24,16},{1,9},{9,1},{17,25},{25,17},{2,10},{10... | collective-permute-start | bytes 1572872 | tf_op jit(solution)/shard_map/ppermute | solution.py:32
  6.7 15.1 %collective-permute-start.2 = (bf16[1024,256]{1,0:T(8,128)(2,1)}, bf16[1024,256]{1,0:T(8,128)(2,1)S(1)}, u32[]{:S(2)}, u32[]{:S(2)}) collective-permute-start(bf16[1024,256]{1,0:T(8,128)(2,1)} %pad_maximum_fusion.1), channel_id=1, source_target_pairs={{0,16},{8,24},{16,0},{24,8},{1,17},{9,25},{17,1},{25,9},{2,18},{10... | collective-permute-start | bytes 1572872 | tf_op jit(solution)/shard_map/ppermute | solution.py:32
  8.2 24.9 %collective-permute-start.5 = (bf16[1024,256]{1,0:T(8,128)(2,1)}, bf16[1024,256]{1,0:T(8,128)(2,1)}, u32[]{:S(2)}, u32[]{:S(2)}) collective-permute-start(bf16[1024,256]{1,0:T(8,128)(2,1)} %pad_maximum_fusion), channel_id=1, source_target_pairs={{0,16},{8,24},{16,0},{24,8},{1,17},{9,25},{17,1},{25,9},{2,18},{10... | collective-permute-start | bytes 1572872 | tf_op jit(solution)/shard_map/ppermute | solution.py:32
  8.7 24.4 %collective-permute-start.1 = (bf16[1024,256]{1,0:T(8,128)(2,1)}, bf16[1024,256]{1,0:T(8,128)(2,1)}, u32[]{:S(2)}, u32[]{:S(2)}) collective-permute-start(bf16[1024,256]{1,0:T(8,128)(2,1)} %pad_maximum_fusion.1), channel_id=1, source_target_pairs={{0,8},{8,0},{16,24},{24,16},{1,9},{9,1},{17,25},{25,17},{2,10},{10... | collective-permute-start | bytes 1572872 | tf_op jit(solution)/shard_map/ppermute | solution.py:32
  21.8 11.9 %collective-permute-start.3 = (bf16[1024,256]{1,0:T(8,128)(2,1)S(1)}, bf16[1024,256]{1,0:T(8,128)(2,1)}, u32[]{:S(2)}, u32[]{:S(2)}) collective-permute-start(bf16[1024,256]{1,0:T(8,128)(2,1)S(1)} %collective-permute-done.refs_2_), channel_id=1, source_target_pairs={{0,1},{1,0},{2,3},{3,2},{4,5},{5,4},{6,7},{7,6},{8,9},{9,8},{10,11... | collective-permute-start | bytes 1572872 | tf_op jit(solution)/shard_map/ppermute | solution.py:32
  21.8 21.0 %collective-permute-start.8 = (bf16[1024,256]{1,0:T(8,128)(2,1)S(1)}, bf16[1024,256]{1,0:T(8,128)(2,1)S(1)}, u32[]{:S(2)}, u32[]{:S(2)}) collective-permute-start(bf16[1024,256]{1,0:T(8,128)(2,1)S(1)} %collective-permute-done.refs_2_), channel_id=1, source_target_pairs={{0,16},{8,24},{16,0},{24,8},{1,17},{9,25},{17,1},{25,9},{2,18},{10... | collective-permute-start | bytes 1572872 | tf_op jit(solution)/shard_map/ppermute | solution.py:32
  23.3 19.5 %collective-permute-start.9 = (bf16[1024,256]{1,0:T(8,128)(2,1)S(1)}, bf16[1024,256]{1,0:T(8,128)(2,1)S(1)}, u32[]{:S(2)}, u32[]{:S(2)}) collective-permute-start(bf16[1024,256]{1,0:T(8,128)(2,1)S(1)} %collective-permute-done.2.refs_7_), channel_id=1, source_target_pairs={{0,8},{8,0},{16,24},{24,16},{1,9},{9,1},{17,25},{25,17},{2,10},{10... | collective-permute-start | bytes 1572872 | tf_op jit(solution)/shard_map/ppermute | solution.py:32
  33.1 3.2 %collective-permute-start.6 = (bf16[1024,256]{1,0:T(8,128)(2,1)}, bf16[1024,256]{1,0:T(8,128)(2,1)S(1)}, u32[]{:S(2)}, u32[]{:S(2)}) collective-permute-start(bf16[1024,256]{1,0:T(8,128)(2,1)} %collective-permute-done.5.refs_6_), channel_id=1, source_target_pairs={{0,1},{1,0},{2,3},{3,2},{4,5},{5,4},{6,7},{7,6},{8,9},{9,8},{10,11... | collective-permute-start | bytes 1572872 | tf_op jit(solution)/shard_map/ppermute | solution.py:32
  33.1 3.6 %collective-permute-start.4 = (bf16[1024,256]{1,0:T(8,128)(2,1)}, bf16[1024,256]{1,0:T(8,128)(2,1)S(1)}, u32[]{:S(2)}, u32[]{:S(2)}) collective-permute-start(bf16[1024,256]{1,0:T(8,128)(2,1)} %collective-permute-done.1.refs_3_), channel_id=1, source_target_pairs={{0,1},{1,0},{2,3},{3,2},{4,5},{5,4},{6,7},{7,6},{8,9},{9,8},{10,11... | collective-permute-start | bytes 1572872 | tf_op jit(solution)/shard_map/ppermute | solution.py:32
  33.6 3.1 %collective-permute-start.7 = (bf16[1024,256]{1,0:T(8,128)(2,1)S(1)}, bf16[1024,256]{1,0:T(8,128)(2,1)S(1)}, u32[]{:S(2)}, u32[]{:S(2)}) collective-permute-start(bf16[1024,256]{1,0:T(8,128)(2,1)S(1)} %collective-permute-done.2.refs_7_), channel_id=1, source_target_pairs={{0,1},{1,0},{2,3},{3,2},{4,5},{5,4},{6,7},{7,6},{8,9},{9,8},{10,11... | collective-permute-start | bytes 1572872 | tf_op jit(solution)/shard_map/ppermute | solution.py:32
  42.8 2.1 %collective-permute-start.10 = (bf16[1024,256]{1,0:T(8,128)(2,1)S(1)}, bf16[1024,256]{1,0:T(8,128)(2,1)S(1)}, u32[]{:S(2)}, u32[]{:S(2)}) collective-permute-start(bf16[1024,256]{1,0:T(8,128)(2,1)S(1)} %collective-permute-done.8.refs_1_), channel_id=1, source_target_pairs={{0,1},{1,0},{2,3},{3,2},{4,5},{5,4},{6,7},{7,6},{8,9},{9,8},{10,11... | collective-permute-start | bytes 1572872 | tf_op jit(solution)/shard_map/ppermute | solution.py:32
  42.9 2.6 %collective-permute-start.11 = (bf16[1024,256]{1,0:T(8,128)(2,1)S(1)}, bf16[1024,256]{1,0:T(8,128)(2,1)S(1)}, u32[]{:S(2)}, u32[]{:S(2)}) collective-permute-start(bf16[1024,256]{1,0:T(8,128)(2,1)S(1)} %collective-permute-done.9.refs_2_), channel_id=1, source_target_pairs={{0,1},{1,0},{2,3},{3,2},{4,5},{5,4},{6,7},{7,6},{8,9},{9,8},{10,11... | collective-permute-start | bytes 1572872 | tf_op jit(solution)/shard_map/ppermute | solution.py:32
  43.4 29.5 %collective-permute-start.20 = (bf16[192,2560]{1,0:T(8,128)(2,1)S(1)}, bf16[192,2560]{1,0:T(8,128)(2,1)S(1)}, u32[]{:S(2)}, u32[]{:S(2)}) collective-permute-start(bf16[192,2560]{1,0:T(8,128)(2,1)S(1)} %get-tuple-element.74), channel_id=1, source_target_pairs={{0,16},{8,24},{16,0},{24,8},{1,17},{9,25},{17,1},{25,9},{2,18},{10... | collective-permute-start | bytes 2949128 | tf_op jit(solution)/shard_map/ppermute | solution.py:32
  45.5 27.3 %collective-permute-start.19 = (bf16[192,2560]{1,0:T(8,128)(2,1)S(1)}, bf16[192,2560]{1,0:T(8,128)(2,1)S(1)}, u32[]{:S(2)}, u32[]{:S(2)}) collective-permute-start(bf16[192,2560]{1,0:T(8,128)(2,1)S(1)} %get-tuple-element.73), channel_id=1, source_target_pairs={{0,8},{8,0},{16,24},{24,16},{1,9},{9,1},{17,25},{25,17},{2,10},{10... | collective-permute-start | bytes 2949128 | tf_op jit(solution)/shard_map/ppermute | solution.py:32
  47.0 7.6 %collective-permute-start.14 = (bf16[192,256]{1,0:T(8,128)(2,1)S(1)}, bf16[192,256]{1,0:T(8,128)(2,1)S(1)}, u32[]{:S(2)}, u32[]{:S(2)}) collective-permute-start(bf16[192,256]{1,0:T(8,128)(2,1)S(1)} %project.3.refs_0_), channel_id=1, source_target_pairs={{0,6},{1,7},{2,4},{3,5},{4,2},{5,3},{6,0},{7,1},{8,14},{9,15},{10,... | collective-permute-start | bytes 294920 | tf_op jit(solution)/shard_map/ppermute | solution.py:32
  50.9 8.3 %collective-permute-start.13 = (bf16[192,256]{1,0:T(8,128)(2,1)S(1)}, bf16[192,256]{1,0:T(8,128)(2,1)S(1)}, u32[]{:S(2)}, u32[]{:S(2)}) collective-permute-start(bf16[192,256]{1,0:T(8,128)(2,1)S(1)} %project.3.refs_0_), channel_id=1, source_target_pairs={{0,4},{1,5},{2,6},{3,7},{4,0},{5,1},{6,2},{7,3},{8,12},{9,13},{10,... | collective-permute-start | bytes 294920 | tf_op jit(solution)/shard_map/ppermute | solution.py:32
  50.9 8.3 %collective-permute-start.12 = (bf16[192,256]{1,0:T(8,128)(2,1)S(1)}, bf16[192,256]{1,0:T(8,128)(2,1)S(1)}, u32[]{:S(2)}, u32[]{:S(2)}) collective-permute-start(bf16[192,256]{1,0:T(8,128)(2,1)S(1)} %project.3.refs_0_), channel_id=1, source_target_pairs={{0,2},{1,3},{2,0},{3,1},{4,6},{5,7},{6,4},{7,5},{8,10},{9,11},{10,... | collective-permute-start | bytes 294920 | tf_op jit(solution)/shard_map/ppermute | solution.py:32
  59.2 33.1 %collective-permute-start.28 = (bf16[192,2560]{1,0:T(8,128)(2,1)S(1)}, bf16[192,2560]{1,0:T(8,128)(2,1)S(1)}, u32[]{:S(2)}, u32[]{:S(2)}) collective-permute-start(bf16[192,2560]{1,0:T(8,128)(2,1)S(1)} %get-tuple-element.84), channel_id=1, source_target_pairs={{0,24},{8,16},{16,8},{24,0},{1,25},{9,17},{17,9},{25,1},{2,26},{10... | collective-permute-start | bytes 2949128 | tf_op jit(solution)/shard_map/ppermute | solution.py:32
  61.6 1.5 collective-permute-start.16
  63.1 1.3 collective-permute-start.18
  72.9 1.7 %collective-permute-start.21 = (bf16[768,256]{1,0:T(8,128)(2,1)S(1)}, bf16[768,256]{1,0:T(8,128)(2,1)S(1)}, u32[]{:S(2)}, u32[]{:S(2)}) collective-permute-start(bf16[768,256]{1,0:T(8,128)(2,1)S(1)} %get-tuple-element.78), channel_id=1, source_target_pairs={{0,1},{1,0},{2,3},{3,2},{4,5},{5,4},{6,7},{7,6},{8,9},{9,8},{10,11... | collective-permute-start | bytes 1179656 | tf_op jit(solution)/shard_map/ppermute | solution.py:32
  74.7 6.6 %collective-permute-start.22 = (bf16[192,256]{1,0:T(8,128)(2,1)S(1)}, bf16[192,256]{1,0:T(8,128)(2,1)S(1)}, u32[]{:S(2)}, u32[]{:S(2)}) collective-permute-start(bf16[192,256]{1,0:T(8,128)(2,1)S(1)} %get-tuple-element.80), channel_id=1, source_target_pairs={{0,2},{1,3},{2,0},{3,1},{4,6},{5,7},{6,4},{7,5},{8,10},{9,11},{10,... | collective-permute-start | bytes 294920 | tf_op jit(solution)/shard_map/ppermute | solution.py:32
  75.3 10.8 %collective-permute-start.23 = (bf16[192,256]{1,0:T(8,128)(2,1)S(1)}, bf16[192,256]{1,0:T(8,128)(2,1)S(1)}, u32[]{:S(2)}, u32[]{:S(2)}) collective-permute-start(bf16[192,256]{1,0:T(8,128)(2,1)S(1)} %get-tuple-element.81), channel_id=1, source_target_pairs={{0,4},{1,5},{2,6},{3,7},{4,0},{5,1},{6,2},{7,3},{8,12},{9,13},{10,... | collective-permute-start | bytes 294920 | tf_op jit(solution)/shard_map/ppermute | solution.py:32
  77.9 8.2 %collective-permute-start.24 = (bf16[192,256]{1,0:T(8,128)(2,1)S(1)}, bf16[192,256]{1,0:T(8,128)(2,1)S(1)}, u32[]{:S(2)}, u32[]{:S(2)}) collective-permute-start(bf16[192,256]{1,0:T(8,128)(2,1)S(1)} %get-tuple-element.82), channel_id=1, source_target_pairs={{0,6},{1,7},{2,4},{3,5},{4,2},{5,3},{6,0},{7,1},{8,14},{9,15},{10,... | collective-permute-start | bytes 294920 | tf_op jit(solution)/shard_map/ppermute | solution.py:32
  86.2 8.2 %collective-permute-start.27 = (bf16[192,256]{1,0:T(8,128)(2,1)S(1)}, bf16[192,256]{1,0:T(8,128)(2,1)S(1)}, u32[]{:S(2)}, u32[]{:S(2)}) collective-permute-start(bf16[192,256]{1,0:T(8,128)(2,1)S(1)} %total.1.refs_4_.refs_1_), channel_id=1, source_target_pairs={{0,24},{8,16},{16,8},{24,0},{1,25},{9,17},{17,9},{25,1},{2,26},{10... | collective-permute-start | bytes 294920 | tf_op jit(solution)/shard_map/ppermute | solution.py:32
  86.7 8.9 %collective-permute-start.26 = (bf16[192,256]{1,0:T(8,128)(2,1)S(1)}, bf16[192,256]{1,0:T(8,128)(2,1)S(1)}, u32[]{:S(2)}, u32[]{:S(2)}) collective-permute-start(bf16[192,256]{1,0:T(8,128)(2,1)S(1)} %total.1.refs_4_.refs_1_), channel_id=1, source_target_pairs={{0,16},{8,24},{16,0},{24,8},{1,17},{9,25},{17,1},{25,9},{2,18},{10... | collective-permute-start | bytes 294920 | tf_op jit(solution)/shard_map/ppermute | solution.py:32
  88.2 7.4 %collective-permute-start.25 = (bf16[192,256]{1,0:T(8,128)(2,1)S(1)}, bf16[192,256]{1,0:T(8,128)(2,1)S(1)}, u32[]{:S(2)}, u32[]{:S(2)}) collective-permute-start(bf16[192,256]{1,0:T(8,128)(2,1)S(1)} %total.1.refs_4_.refs_1_), channel_id=1, source_target_pairs={{0,8},{8,0},{16,24},{24,16},{1,9},{9,1},{17,25},{25,17},{2,10},{10... | collective-permute-start | bytes 294920 | tf_op jit(solution)/shard_map/ppermute | solution.py:32
  97.2 5.5 %collective-permute-start.31 = (bf16[3072,256]{1,0:T(8,128)(2,1)S(1)}, bf16[3072,256]{1,0:T(8,128)(2,1)S(1)}, u32[]{:S(2)}, u32[]{:S(2)}) collective-permute-start(bf16[3072,256]{1,0:T(8,128)(2,1)S(1)} %get-tuple-element.95), channel_id=1, source_target_pairs={{0,1},{1,0},{2,3},{3,2},{4,5},{5,4},{6,7},{7,6},{8,9},{9,8},{10,11... | collective-permute-start | bytes 4718600 | tf_op jit(solution)/shard_map/ppermute | solution.py:32
  98.6 2.4 %collective-permute-start.29 = (bf16[512,256]{1,0:T(8,128)(2,1)S(1)}, bf16[512,256]{1,0:T(8,128)(2,1)S(1)}, u32[]{:S(2)}, u32[]{:S(2)}) collective-permute-start(bf16[512,256]{1,0:T(8,128)(2,1)S(1)} %get-tuple-element.90), channel_id=1, source_target_pairs={{0,1},{1,0},{2,3},{3,2},{4,5},{5,4},{6,7},{7,6},{8,9},{9,8},{10,11... | collective-permute-start | bytes 786440 | tf_op jit(solution)/shard_map/ppermute | solution.py:32
  100.8 1.8 %collective-permute-start.30 = (bf16[768,256]{1,0:T(8,128)(2,1)S(1)}, bf16[768,256]{1,0:T(8,128)(2,1)S(1)}, u32[]{:S(2)}, u32[]{:S(2)}) collective-permute-start(bf16[768,256]{1,0:T(8,128)(2,1)S(1)} %get-tuple-element.92), channel_id=1, source_target_pairs={{0,1},{1,0},{2,3},{3,2},{4,5},{5,4},{6,7},{7,6},{8,9},{9,8},{10,11... | collective-permute-start | bytes 1179656 | tf_op jit(solution)/shard_map/ppermute | solution.py:32
  103.4 6.4 %collective-permute-start.32 = (bf16[256,256]{1,0:T(8,128)(2,1)S(1)}, bf16[256,256]{1,0:T(8,128)(2,1)S(1)}, u32[]{:S(2)}, u32[]{:S(2)}) collective-permute-start(bf16[256,256]{1,0:T(8,128)(2,1)S(1)} %slice.70), channel_id=1, source_target_pairs={{0,2},{1,3},{2,0},{3,1},{4,6},{5,7},{6,4},{7,5},{8,10},{9,11},{10,... | collective-permute-start | bytes 393224 | tf_op jit(solution)/shard_map/ppermute | solution.py:32
  105.1 9.9 %collective-permute-start.37 = (bf16[384,256]{1,0:T(8,128)(2,1)S(1)}, bf16[384,256]{1,0:T(8,128)(2,1)S(1)}, u32[]{:S(2)}, u32[]{:S(2)}) collective-permute-start(bf16[384,256]{1,0:T(8,128)(2,1)S(1)} %slice.69), channel_id=1, source_target_pairs={{0,2},{1,3},{2,0},{3,1},{4,6},{5,7},{6,4},{7,5},{8,10},{9,11},{10,... | collective-permute-start | bytes 589832 | tf_op jit(solution)/shard_map/ppermute | solution.py:32
  105.6 18.3 %collective-permute-start.39 = (bf16[768,256]{1,0:T(8,128)(2,1)S(1)}, bf16[768,256]{1,0:T(8,128)(2,1)S(1)}, u32[]{:S(2)}, u32[]{:S(2)}) collective-permute-start(bf16[768,256]{1,0:T(8,128)(2,1)S(1)} %get-tuple-element.99), channel_id=1, source_target_pairs={{0,8},{8,0},{16,24},{24,16},{1,9},{9,1},{17,25},{25,17},{2,10},{10... | collective-permute-start | bytes 1179656 | tf_op jit(solution)/shard_map/ppermute | solution.py:32
  106.1 18.8 %collective-permute-start.40 = (bf16[768,256]{1,0:T(8,128)(2,1)S(1)}, bf16[768,256]{1,0:T(8,128)(2,1)S(1)}, u32[]{:S(2)}, u32[]{:S(2)}) collective-permute-start(bf16[768,256]{1,0:T(8,128)(2,1)S(1)} %get-tuple-element.100), channel_id=1, source_target_pairs={{0,16},{8,24},{16,0},{24,8},{1,17},{9,25},{17,1},{25,9},{2,18},{10... | collective-permute-start | bytes 1179656 | tf_op jit(solution)/shard_map/ppermute | solution.py:32
  106.7 18.2 %collective-permute-start.41 = (bf16[768,256]{1,0:T(8,128)(2,1)S(1)}, bf16[768,256]{1,0:T(8,128)(2,1)S(1)}, u32[]{:S(2)}, u32[]{:S(2)}) collective-permute-start(bf16[768,256]{1,0:T(8,128)(2,1)S(1)} %get-tuple-element.101), channel_id=1, source_target_pairs={{0,24},{8,16},{16,8},{24,0},{1,25},{9,17},{17,9},{25,1},{2,26},{10... | collective-permute-start | bytes 1179656 | tf_op jit(solution)/shard_map/ppermute | solution.py:32
  109.8 13.3 %collective-permute-start.33 = (bf16[256,256]{1,0:T(8,128)(2,1)S(1)}, bf16[256,256]{1,0:T(8,128)(2,1)S(1)}, u32[]{:S(2)}, u32[]{:S(2)}) collective-permute-start(bf16[256,256]{1,0:T(8,128)(2,1)S(1)} %fusion.1), channel_id=1, source_target_pairs={{0,4},{1,5},{2,6},{3,7},{4,0},{5,1},{6,2},{7,3},{8,12},{9,13},{10,... | collective-permute-start | bytes 393224 | tf_op jit(solution)/shard_map/ppermute | solution.py:32
  115.0 14.9 %collective-permute-start.38 = (bf16[384,256]{1,0:T(8,128)(2,1)S(1)}, bf16[384,256]{1,0:T(8,128)(2,1)S(1)}, u32[]{:S(2)}, u32[]{:S(2)}) collective-permute-start(bf16[384,256]{1,0:T(8,128)(2,1)S(1)} %fusion), channel_id=1, source_target_pairs={{0,4},{1,5},{2,6},{3,7},{4,0},{5,1},{6,2},{7,3},{8,12},{9,13},{10,... | collective-permute-start | bytes 589832 | tf_op jit(solution)/shard_map/ppermute | solution.py:32
  123.2 6.6 %collective-permute-start.34 = (bf16[256,256]{1,0:T(8,128)(2,1)S(1)}, bf16[256,256]{1,0:T(8,128)(2,1)S(1)}, u32[]{:S(2)}, u32[]{:S(2)}) collective-permute-start(bf16[256,256]{1,0:T(8,128)(2,1)S(1)} %add_convert_fusion.2.refs_0_), channel_id=1, source_target_pairs={{0,2},{1,3},{2,0},{3,1},{4,6},{5,7},{6,4},{7,5},{8,10},{9,11},{10,... | collective-permute-start | bytes 393224 | tf_op jit(solution)/shard_map/ppermute | solution.py:32
  125.1 7.5 %collective-permute-start.42 = (bf16[384,256]{1,0:T(8,128)(2,1)S(1)}, bf16[384,256]{1,0:T(8,128)(2,1)S(1)}, u32[]{:S(2)}, u32[]{:S(2)}) collective-permute-start(bf16[384,256]{1,0:T(8,128)(2,1)S(1)} %slice.68), channel_id=1, source_target_pairs={{0,2},{1,3},{2,0},{3,1},{4,6},{5,7},{6,4},{7,5},{8,10},{9,11},{10,... | collective-permute-start | bytes 589832 | tf_op jit(solution)/shard_map/ppermute | solution.py:32
  132.7 10.7 %collective-permute-start.46 = (bf16[384,256]{1,0:T(8,128)(2,1)S(1)}, bf16[384,256]{1,0:T(8,128)(2,1)S(1)}, u32[]{:S(2)}, u32[]{:S(2)}) collective-permute-start(bf16[384,256]{1,0:T(8,128)(2,1)S(1)} %get-tuple-element.109), channel_id=1, source_target_pairs={{0,4},{1,5},{2,6},{3,7},{4,0},{5,1},{6,2},{7,3},{8,12},{9,13},{10,... | collective-permute-start | bytes 589832 | tf_op jit(solution)/shard_map/ppermute | solution.py:32
  134.6 8.8 %collective-permute-start.35 = (bf16[256,256]{1,0:T(8,128)(2,1)S(1)}, bf16[256,256]{1,0:T(8,128)(2,1)S(1)}, u32[]{:S(2)}, u32[]{:S(2)}) collective-permute-start(bf16[256,256]{1,0:T(8,128)(2,1)S(1)} %add_convert_fusion.2.refs_0_), channel_id=1, source_target_pairs={{0,1},{1,0},{2,3},{3,2},{4,5},{5,4},{6,7},{7,6},{8,9},{9,8},{10,11... | collective-permute-start | bytes 393224 | tf_op jit(solution)/shard_map/ppermute | solution.py:32
  134.6 8.8 %collective-permute-start.36 = (bf16[256,256]{1,0:T(8,128)(2,1)S(1)}, bf16[256,256]{1,0:T(8,128)(2,1)S(1)}, u32[]{:S(2)}, u32[]{:S(2)}) collective-permute-start(bf16[256,256]{1,0:T(8,128)(2,1)S(1)} %collective-permute-done.34.refs_1_), channel_id=1, source_target_pairs={{0,1},{1,0},{2,3},{3,2},{4,5},{5,4},{6,7},{7,6},{8,9},{9,8},{10,11... | collective-permute-start | bytes 393224 | tf_op jit(solution)/shard_map/ppermute | solution.py:32
  135.1 10.8 %collective-permute-start.43 = (bf16[384,256]{1,0:T(8,128)(2,1)S(1)}, bf16[384,256]{1,0:T(8,128)(2,1)S(1)}, u32[]{:S(2)}, u32[]{:S(2)}) collective-permute-start(bf16[384,256]{1,0:T(8,128)(2,1)S(1)} %add_convert_fusion.1.refs_4_), channel_id=1, source_target_pairs={{0,2},{1,3},{2,0},{3,1},{4,6},{5,7},{6,4},{7,5},{8,10},{9,11},{10,... | collective-permute-start | bytes 589832 | tf_op jit(solution)/shard_map/ppermute | solution.py:32
  143.4 6.4 %collective-permute-start.47 = (bf16[384,256]{1,0:T(8,128)(2,1)S(1)}, bf16[384,256]{1,0:T(8,128)(2,1)S(1)}, u32[]{:S(2)}, u32[]{:S(2)}) collective-permute-start(bf16[384,256]{1,0:T(8,128)(2,1)S(1)} %add_convert_fusion.refs_2_), channel_id=1, source_target_pairs={{0,2},{1,3},{2,0},{3,1},{4,6},{5,7},{6,4},{7,5},{8,10},{9,11},{10,... | collective-permute-start | bytes 589832 | tf_op jit(solution)/shard_map/ppermute | solution.py:32
  143.5 6.4 %collective-permute-start.44 = (bf16[384,256]{1,0:T(8,128)(2,1)S(1)}, bf16[384,256]{1,0:T(8,128)(2,1)S(1)}, u32[]{:S(2)}, u32[]{:S(2)}) collective-permute-start(bf16[384,256]{1,0:T(8,128)(2,1)S(1)} %add_convert_fusion.1.refs_4_), channel_id=1, source_target_pairs={{0,1},{1,0},{2,3},{3,2},{4,5},{5,4},{6,7},{7,6},{8,9},{9,8},{10,11... | collective-permute-start | bytes 589832 | tf_op jit(solution)/shard_map/ppermute | solution.py:32
  143.6 8.5 %collective-permute-start.48 = (bf16[384,256]{1,0:T(8,128)(2,1)S(1)}, bf16[384,256]{1,0:T(8,128)(2,1)S(1)}, u32[]{:S(2)}, u32[]{:S(2)}) collective-permute-start(bf16[384,256]{1,0:T(8,128)(2,1)S(1)} %add_convert_fusion.refs_2_), channel_id=1, source_target_pairs={{0,1},{1,0},{2,3},{3,2},{4,5},{5,4},{6,7},{7,6},{8,9},{9,8},{10,11... | collective-permute-start | bytes 589832 | tf_op jit(solution)/shard_map/ppermute | solution.py:32
  145.9 3.9 %collective-permute-start.45 = (bf16[384,256]{1,0:T(8,128)(2,1)S(1)}, bf16[384,256]{1,0:T(8,128)(2,1)S(1)}, u32[]{:S(2)}, u32[]{:S(2)}) collective-permute-start(bf16[384,256]{1,0:T(8,128)(2,1)S(1)} %collective-permute-done.43.refs_5_), channel_id=1, source_target_pairs={{0,1},{1,0},{2,3},{3,2},{4,5},{5,4},{6,7},{7,6},{8,9},{9,8},{10,11... | collective-permute-start | bytes 589832 | tf_op jit(solution)/shard_map/ppermute | solution.py:32
  149.9 2.2 %collective-permute-start.49 = (bf16[384,256]{1,0:T(8,128)(2,1)S(1)}, bf16[384,256]{1,0:T(8,128)(2,1)S(1)}, u32[]{:S(2)}, u32[]{:S(2)}) collective-permute-start(bf16[384,256]{1,0:T(8,128)(2,1)S(1)} %collective-permute-done.47.refs_3_), channel_id=1, source_target_pairs={{0,1},{1,0},{2,3},{3,2},{4,5},{5,4},{6,7},{7,6},{8,9},{9,8},{10,11... | collective-permute-start | bytes 589832 | tf_op jit(solution)/shard_map/ppermute | solution.py:32
  (10 other events, 136.2 us)

commit v16 on v14

--- a/solution.py
+++ b/solution.py
@@ -365,7 +365,7 @@
         for side in range(2):
             for m in range(sub_count):
                 to = origin + (core ^ side) * rows + (z ^ m) * share
-                to = pl.multiple_of(to, share)
+                to = pl.multiple_of(to, math.gcd(origin, share))
                 block_ref = next(blocks)
                 width = block_ref.shape[1] // 2
                 for which, out_ref in enumerate(outs):
@@ -482,7 +482,8 @@
     early, *tied = hold([early] + [moving[j] for j in others], far_pieces)
     moving.update(zip(others, tied))
     far_pieces.update(from_other_core(far_pieces))
-    tied = hold([moving[j] for j in near[:-1]], far_pieces)
+    soonest = list(far_pieces)[len(far_pieces) // 2]
+    tied, (far_pieces[soonest],) = after([moving[j] for j in near[:-1]], far_pieces[soonest])
     moving.update(zip(near[:-1], tied))
     own = project(ids, (early,), inputs, block_rows, far_pieces, jnp.bfloat16)
     moved = {0: moving[0]}
@@ -526,13 +527,11 @@
         part = scatter_along_z(part, sub_count)
         finals.append(sum_of_halves(part, sub_count))
     part = scatter_along_z(sum_of(own), sub_count, finals[:TIED])
-    finals, _ = after(finals, part)
     blocks = gather_parts(finals[0], sub_count)
-    last = sum_of_halves(part, sub_count)
-    (last,), _ = after([last], *blocks)
+    last = sum_of_halves(part, sub_count, blocks)
     blocks += [one for final in finals[1:] for one in gather_parts(final, sub_count)]
     outs = assemble(ids, (), blocks, sub_count, regions[:-1], block_rows)
-    last = gather_parts(last, sub_count)
+    last = gather_parts(last, sub_count, outs)
     key_rows, value_rows = assemble(ids, outs, last, sub_count, regions[-1:], block_rows)
     return query_grad[None], key_rows, value_rows
 

time: 154 us -> 153 us (level)
  starting transfers between devices: 44.7 us -> 41.9 us
    ppermute x50, starting transfers between devices: 44.7 us -> 41.9 us  [swap(): return lax.ppermute(array, axis, [(i, i ^ distance) for i in range(count)])]
where the time goes in v16:
time: 153 us; the launch traced here: 152 us
  waiting for transfers between devices  80 us (52%)
  starting transfers between devices  41.9 us (27%)
  Pallas kernels  21.4 us (14%)
  local copies, waits for them, and re-layouts  5.14 us (3%)
  other arithmetic  2.92 us (2%)
    ppermute x50, waiting for transfers between devices, swap(): return lax.ppermute(array, axis, [(i, i ^ distance) for i in range(count)])  80 us
    ppermute x50, starting transfers between devices, swap(): return lax.ppermute(array, axis, [(i, i ^ distance) for i in range(count)])  41.9 us
    pallas_call x7, Pallas kernels, kernel_call(): pl.pallas_call(kernel, out_shape=outs, in_specs=[smem] * len(scalars) + [...  9.06 us
    pallas_call x1, Pallas kernels, attention(): pl.pallas_call(functools.partial(attention_kernel, shape), out_shape=(jax...  8.47 us
    pallas_call x2, Pallas kernels, assemble(): pl.pallas_call(functools.partial(assemble_kernel, sub_count, regions, not...  3.92 us
  transfers between devices with their start and end apart: 50, of which 29 were waited for; matrix products, arithmetic and copies ran while one was open for 3% of the time, Pallas kernels for 12%

profile of v16, /device:TPU:0, one launch (start us, length us, event | category | flops | bytes accessed | tf_op | source)
XLA Modules:
  0.0 152.5 jit_solution(16990864534754826126)
XLA Ops:
  0.7 1.4 constant_dynamic-slice_fusion
  2.9 2.9 %collective-permute-start = (bf16[1024,256]{1,0:T(8,128)(2,1)}, bf16[1024,256]{1,0:T(8,128)(2,1)S(1)}, u32[]{:S(2)}, u32[]{:S(2)}) collective-permute-start(bf16[1024,256]{1,0:T(8,128)(2,1)} %pad_maximum_fusion), channel_id=1, source_target_pairs={{0,8},{8,0},{16,24},{24,16},{1,9},{9,1},{17,25},{25,17},{2,10},{10... | collective-permute-start | bytes 1572872 | tf_op jit(solution)/shard_map/ppermute | solution.py:32
  6.7 1.5 collective-permute-start.2
  8.8 10.0 %collective-permute-done.refs_2_ = bf16[1024,256]{1,0:T(8,128)(2,1)S(1)} collective-permute-done((bf16[1024,256]{1,0:T(8,128)(2,1)}, bf16[1024,256]{1,0:T(8,128)(2,1)S(1)}, u32[]{:S(2)}, u32[]{:S(2)}) %collective-permute-start) | collective-permute-done | bytes 524320 | tf_op jit(solution)/shard_map/ppermute | solution.py:32
  18.8 3.0 %collective-permute-done.2.refs_7_ = bf16[1024,256]{1,0:T(8,128)(2,1)S(1)} collective-permute-done((bf16[1024,256]{1,0:T(8,128)(2,1)}, bf16[1024,256]{1,0:T(8,128)(2,1)S(1)}, u32[]{:S(2)}, u32[]{:S(2)}) %collective-permute-start.2) | collective-permute-done | bytes 524320 | tf_op jit(solution)/shard_map/ppermute | solution.py:32
  21.8 1.5 collective-permute-start.8
  23.8 9.3 %collective-permute-done.5.refs_6_ = bf16[1024,256]{1,0:T(8,128)(2,1)} collective-permute-done((bf16[1024,256]{1,0:T(8,128)(2,1)}, bf16[1024,256]{1,0:T(8,128)(2,1)}, u32[]{:S(2)}, u32[]{:S(2)}) %collective-permute-start.5) | collective-permute-done | bytes 524320 | tf_op jit(solution)/shard_map/ppermute | solution.py:32
  33.8 2.5 %dynamic-slice_bitcast_fusion = (bf16[192,2560]{1,0:T(8,128)(2,1)S(1)}, bf16[192,2560]{1,0:T(8,128)(2,1)S(1)}, bf16[192,2560]{1,0:T(8,128)(2,1)S(1)}, bf16[192,2560]{1,0:T(8,128)(2,1)S(1)}) fusion(bf16[1,192,16384]{2,1,0:T(8,128)(2,1)} %param.7, s32[]{:T(128)S(6)} %select_n.42, s32[]{:T(128)S(6)} %select_n.40, s32[]{:T(128)S(6)} %select_n.39, s32[]{:T(128)S(6)} %select_n.41), kind=kLoop, calls=%fused_computation.1 | loop fusion | bytes 7864336 | tf_op jit(solution)/shard_map/dynamic_slice | solution.py:464
  37.8 3.2 %project.2.refs_0_ = f32[192,256]{1,0:T(8,128)S(1)} custom-call(s32[3]{0:T(128)S(1)} %pad_add_fusion.ids, bf16[192,16384]{1,0:T(8,128)(2,1)S(1)} %bitcast.19, bf16[4096,128]{1,0:T(8,128)(2,1)S(1)} %copy-done, bf16[4096,128]{1,0:T(8,128)(2,1)S(1)} %copy-done.1, bf16[1024,256]{1,0:T(8,128)(2,1)S(1)} %collective-permute-done.refs_2_, ...), custom_call_target="tpu_custom_call" | custom-call | bytes 16777216 | tf_op jit(solution)/shard_map/project/pallas_call | solution.py:48
  41.0 1.8 %collective-permute-done.8.refs_1_ = bf16[1024,256]{1,0:T(8,128)(2,1)S(1)} collective-permute-done((bf16[1024,256]{1,0:T(8,128)(2,1)S(1)}, bf16[1024,256]{1,0:T(8,128)(2,1)S(1)}, u32[]{:S(2)}, u32[]{:S(2)}) %collective-permute-start.8) | collective-permute-done | bytes 524320 | tf_op jit(solution)/shard_map/ppermute | solution.py:32
  43.4 1.5 collective-permute-start.20
  45.5 1.1 project.3.refs_0_
  46.7 3.7 %collective-permute-start.14 = (bf16[192,256]{1,0:T(8,128)(2,1)S(1)}, bf16[192,256]{1,0:T(8,128)(2,1)S(1)}, u32[]{:S(2)}, u32[]{:S(2)}) collective-permute-start(bf16[192,256]{1,0:T(8,128)(2,1)S(1)} %project.3.refs_0_), channel_id=1, source_target_pairs={{0,6},{1,7},{2,4},{3,5},{4,2},{5,3},{6,0},{7,1},{8,14},{9,15},{10,... | collective-permute-start | bytes 294920 | tf_op jit(solution)/shard_map/ppermute | solution.py:32
  51.1 3.1 %collective-permute-done.14.refs_6_ = bf16[192,256]{1,0:T(8,128)(2,1)S(1)} collective-permute-done((bf16[192,256]{1,0:T(8,128)(2,1)S(1)}, bf16[192,256]{1,0:T(8,128)(2,1)S(1)}, u32[]{:S(2)}, u32[]{:S(2)}) %collective-permute-start.14) | collective-permute-done | bytes 98336 | tf_op jit(solution)/shard_map/ppermute | solution.py:32
  54.3 4.6 %collective-permute-done.13.refs_4_ = bf16[192,256]{1,0:T(8,128)(2,1)S(1)} collective-permute-done((bf16[192,256]{1,0:T(8,128)(2,1)S(1)}, bf16[192,256]{1,0:T(8,128)(2,1)S(1)}, u32[]{:S(2)}, u32[]{:S(2)}) %collective-permute-start.13) | collective-permute-done | bytes 98336 | tf_op jit(solution)/shard_map/ppermute | solution.py:32
  58.9 2.0 %collective-permute-start.28 = (bf16[192,2560]{1,0:T(8,128)(2,1)S(1)}, bf16[192,2560]{1,0:T(8,128)(2,1)S(1)}, u32[]{:S(2)}, u32[]{:S(2)}) collective-permute-start(bf16[192,2560]{1,0:T(8,128)(2,1)S(1)} %get-tuple-element.78), channel_id=1, source_target_pairs={{0,24},{8,16},{16,8},{24,0},{1,25},{9,17},{17,9},{25,1},{2,26},{10... | collective-permute-start | bytes 2949128 | tf_op jit(solution)/shard_map/ppermute | solution.py:32
  63.7 8.5 %attention.1 = (bf16[192,1024]{1,0:T(8,128)(2,1)}, f32[768,256]{1,0:T(8,128)S(1)}, bf16[768,256]{1,0:T(8,128)(2,1)S(1)}) custom-call(s32[1]{0:T(128)} %bitcast.ids, s32[16]{0:T(128)S(1)} %copy-done.4, s32[8]{0:T(128)S(1)} %bitcast.24, bf16[192,1024]{1,0:T(8,128)(2,1)S(1)} %bitcast.22, bf16[192,1024]{1,0:T(8,128)(2,1)S(1)} %bitcast.23, ...), custom_call_target="tpu_custom_call" | custom-call | tf_op jit(solution)/shard_map/attention/pallas_call | solution.py:171
  72.5 1.4 collective-permute-done.21.came
  74.5 2.5 %collective-permute-start.23 = (bf16[192,256]{1,0:T(8,128)(2,1)S(1)}, bf16[192,256]{1,0:T(8,128)(2,1)S(1)}, u32[]{:S(2)}, u32[]{:S(2)}) collective-permute-start(bf16[192,256]{1,0:T(8,128)(2,1)S(1)} %get-tuple-element.75), channel_id=1, source_target_pairs={{0,4},{1,5},{2,6},{3,7},{4,0},{5,1},{6,2},{7,3},{8,12},{9,13},{10,... | collective-permute-start | bytes 294920 | tf_op jit(solution)/shard_map/ppermute | solution.py:32
  77.1 1.3 collective-permute-start.24
  78.4 2.2 %collective-permute-done.22.refs_1_ = bf16[192,256]{1,0:T(8,128)(2,1)S(1)} collective-permute-done((bf16[192,256]{1,0:T(8,128)(2,1)S(1)}, bf16[192,256]{1,0:T(8,128)(2,1)S(1)}, u32[]{:S(2)}, u32[]{:S(2)}) %collective-permute-start.22) | collective-permute-done | bytes 98336 | tf_op jit(solution)/shard_map/ppermute | solution.py:32
  80.6 4.8 %collective-permute-done.23.refs_2_ = bf16[192,256]{1,0:T(8,128)(2,1)S(1)} collective-permute-done((bf16[192,256]{1,0:T(8,128)(2,1)S(1)}, bf16[192,256]{1,0:T(8,128)(2,1)S(1)}, u32[]{:S(2)}, u32[]{:S(2)}) %collective-permute-start.23) | collective-permute-done | bytes 98336 | tf_op jit(solution)/shard_map/ppermute | solution.py:32
  85.4 1.0 collective-permute-start.27
  86.5 1.5 collective-permute-start.26
  88.0 1.0 collective-permute-start.25
  89.0 2.5 %collective-permute-done.28.refs_3_ = bf16[192,2560]{1,0:T(8,128)(2,1)S(1)} collective-permute-done((bf16[192,2560]{1,0:T(8,128)(2,1)S(1)}, bf16[192,2560]{1,0:T(8,128)(2,1)S(1)}, u32[]{:S(2)}, u32[]{:S(2)}) %collective-permute-start.28) | collective-permute-done | bytes 983072 | tf_op jit(solution)/shard_map/ppermute | solution.py:32
  91.5 2.1 %collective-permute-done.27.refs_7_ = bf16[192,256]{1,0:T(8,128)(2,1)S(1)} collective-permute-done((bf16[192,256]{1,0:T(8,128)(2,1)S(1)}, bf16[192,256]{1,0:T(8,128)(2,1)S(1)}, u32[]{:S(2)}, u32[]{:S(2)}) %collective-permute-start.27) | collective-permute-done | bytes 98336 | tf_op jit(solution)/shard_map/ppermute | solution.py:32
  93.6 1.3 collective-permute-done.26.refs_6_
  94.8 1.7 %weight_rows.5 = (bf16[3072,256]{1,0:T(8,128)(2,1)S(1)}, bf16[3072,256]{1,0:T(8,128)(2,1)S(1)}) custom-call(s32[3]{0:T(128)S(1)} %pad_add_fusion.ids, bf16[192,16384]{1,0:T(8,128)(2,1)S(1)} %bitcast.21, bf16[192,256]{1,0:T(8,128)(2,1)S(1)} %total.1.refs_4_.refs_1_), custom_call_target="tpu_custom_call" | custom-call | tf_op jit(solution)/shard_map/weight_rows/pallas_call | solution.py:48
  96.6 1.3 weight_rows.3
  98.5 1.6 %weight_rows.4 = (bf16[768,256]{1,0:T(8,128)(2,1)S(1)}, bf16[768,256]{1,0:T(8,128)(2,1)S(1)}) custom-call(s32[3]{0:T(128)S(1)} %pad_add_fusion.ids, bf16[192,2560]{1,0:T(8,128)(2,1)S(1)} %get-tuple-element.103.refs_0_, bf16[192,2560]{1,0:T(8,128)(2,1)S(1)} %collective-permute-done.19.refs_1_, bf16[192,2560]{1,0:T(8,128)(2,1)S(1)} %collective-permute-done.20.refs_2_, ...), custom_call_target="tpu_custom_call" | custom-call | tf_op jit(solution)/shard_map/weight_rows/pallas_call | solution.py:48
  100.4 1.4 collective-permute-done.30
  102.6 1.6 %collective-permute-start.32 = (bf16[256,256]{1,0:T(8,128)(2,1)S(1)}, bf16[256,256]{1,0:T(8,128)(2,1)S(1)}, u32[]{:S(2)}, u32[]{:S(2)}) collective-permute-start(bf16[256,256]{1,0:T(8,128)(2,1)S(1)} %slice.74), channel_id=1, source_target_pairs={{0,2},{1,3},{2,0},{3,1},{4,6},{5,7},{6,4},{7,5},{8,10},{9,11},{10,... | collective-permute-start | bytes 393224 | tf_op jit(solution)/shard_map/ppermute | solution.py:32
  106.0 2.4 %collective-permute-start.44 = (bf16[768,256]{1,0:T(8,128)(2,1)S(1)}, bf16[768,256]{1,0:T(8,128)(2,1)S(1)}, u32[]{:S(2)}, u32[]{:S(2)}) collective-permute-start(bf16[768,256]{1,0:T(8,128)(2,1)S(1)} %get-tuple-element.97), channel_id=1, source_target_pairs={{0,24},{8,16},{16,8},{24,0},{1,25},{9,17},{17,9},{25,1},{2,26},{10... | collective-permute-start | bytes 1179656 | tf_op jit(solution)/shard_map/ppermute | solution.py:32
  109.1 2.7 %collective-permute-start.33 = (bf16[256,256]{1,0:T(8,128)(2,1)S(1)}, bf16[256,256]{1,0:T(8,128)(2,1)S(1)}, u32[]{:S(2)}, u32[]{:S(2)}) collective-permute-start(bf16[256,256]{1,0:T(8,128)(2,1)S(1)} %fusion.2), channel_id=1, source_target_pairs={{0,4},{1,5},{2,6},{3,7},{4,0},{5,1},{6,2},{7,3},{8,12},{9,13},{10,... | collective-permute-start | bytes 393224 | tf_op jit(solution)/shard_map/ppermute | solution.py:32
  111.7 2.5 %collective-permute-done.37 = bf16[384,256]{1,0:T(8,128)(2,1)S(1)} collective-permute-done((bf16[384,256]{1,0:T(8,128)(2,1)S(1)}, bf16[384,256]{1,0:T(8,128)(2,1)S(1)}, u32[]{:S(2)}, u32[]{:S(2)}) %collective-permute-start.37) | collective-permute-done | bytes 196640 | tf_op jit(solution)/shard_map/ppermute | solution.py:32
  114.2 1.7 %collective-permute-start.38 = (bf16[384,256]{1,0:T(8,128)(2,1)S(1)}, bf16[384,256]{1,0:T(8,128)(2,1)S(1)}, u32[]{:S(2)}, u32[]{:S(2)}) collective-permute-start(bf16[384,256]{1,0:T(8,128)(2,1)S(1)} %fusion), channel_id=1, source_target_pairs={{0,4},{1,5},{2,6},{3,7},{4,0},{5,1},{6,2},{7,3},{8,12},{9,13},{10,... | collective-permute-start | bytes 589832 | tf_op jit(solution)/shard_map/ppermute | solution.py:32
  116.0 6.4 %collective-permute-done.33 = bf16[256,256]{1,0:T(8,128)(2,1)S(1)} collective-permute-done((bf16[256,256]{1,0:T(8,128)(2,1)S(1)}, bf16[256,256]{1,0:T(8,128)(2,1)S(1)}, u32[]{:S(2)}, u32[]{:S(2)}) %collective-permute-start.33) | collective-permute-done | bytes 131104 | tf_op jit(solution)/shard_map/ppermute | solution.py:32
  123.1 1.0 collective-permute-done.43
  124.4 1.6 %collective-permute-start.45 = (bf16[384,256]{1,0:T(8,128)(2,1)S(1)}, bf16[384,256]{1,0:T(8,128)(2,1)S(1)}, u32[]{:S(2)}, u32[]{:S(2)}) collective-permute-start(bf16[384,256]{1,0:T(8,128)(2,1)S(1)} %slice.72), channel_id=1, source_target_pairs={{0,2},{1,3},{2,0},{3,1},{4,6},{5,7},{6,4},{7,5},{8,10},{9,11},{10,... | collective-permute-start | bytes 589832 | tf_op jit(solution)/shard_map/ppermute | solution.py:32
  126.6 6.7 %collective-permute-done.45 = bf16[384,256]{1,0:T(8,128)(2,1)S(1)} collective-permute-done((bf16[384,256]{1,0:T(8,128)(2,1)S(1)}, bf16[384,256]{1,0:T(8,128)(2,1)S(1)}, u32[]{:S(2)}, u32[]{:S(2)}) %collective-permute-start.45) | collective-permute-done | bytes 196640 | tf_op jit(solution)/shard_map/ppermute | solution.py:32
  133.4 1.9 %collective-permute-start.46 = (bf16[384,256]{1,0:T(8,128)(2,1)S(1)}, bf16[384,256]{1,0:T(8,128)(2,1)S(1)}, u32[]{:S(2)}, u32[]{:S(2)}) collective-permute-start(bf16[384,256]{1,0:T(8,128)(2,1)S(1)} %fusion.1), channel_id=1, source_target_pairs={{0,4},{1,5},{2,6},{3,7},{4,0},{5,1},{6,2},{7,3},{8,12},{9,13},{10,... | collective-permute-start | bytes 589832 | tf_op jit(solution)/shard_map/ppermute | solution.py:32
  135.8 2.7 %collective-permute-done.39.refs_5_ = bf16[384,256]{1,0:T(8,128)(2,1)S(1)} collective-permute-done((bf16[384,256]{1,0:T(8,128)(2,1)S(1)}, bf16[384,256]{1,0:T(8,128)(2,1)S(1)}, u32[]{:S(2)}, u32[]{:S(2)}) %collective-permute-start.39) | collective-permute-done | bytes 196640 | tf_op jit(solution)/shard_map/ppermute | solution.py:32
  138.5 4.8 %collective-permute-done.46 = bf16[384,256]{1,0:T(8,128)(2,1)S(1)} collective-permute-done((bf16[384,256]{1,0:T(8,128)(2,1)S(1)}, bf16[384,256]{1,0:T(8,128)(2,1)S(1)}, u32[]{:S(2)}, u32[]{:S(2)}) %collective-permute-start.46) | collective-permute-done | bytes 196640 | tf_op jit(solution)/shard_map/ppermute | solution.py:32
  143.6 2.2 %assemble.2 = (f32[4096,128]{1,0:T(8,128)}, f32[4096,128]{1,0:T(8,128)}) custom-call(s32[3]{0:T(128)S(1)} %pad_add_fusion.ids, bf16[256,256]{1,0:T(8,128)(2,1)S(1)} %add_convert_fusion.2.refs_0_, bf16[256,256]{1,0:T(8,128)(2,1)S(1)} %collective-permute-done.34.refs_1_, bf16[256,256]{1,0:T(8,128)(2,1)S(1)} %collective-permute-done.35.refs_2_, ...), custom_call_target="tpu_custom_call" | custom-call | tf_op jit(solution)/shard_map/assemble/pallas_call | solution.py:393
  145.7 3.4 %collective-permute-done.47.refs_3_ = bf16[384,256]{1,0:T(8,128)(2,1)S(1)} collective-permute-done((bf16[384,256]{1,0:T(8,128)(2,1)S(1)}, bf16[384,256]{1,0:T(8,128)(2,1)S(1)}, u32[]{:S(2)}, u32[]{:S(2)}) %collective-permute-start.47) | collective-permute-done | bytes 196640 | tf_op jit(solution)/shard_map/ppermute | solution.py:32
  149.1 1.4 collective-permute-done.49.refs_5_
  150.6 1.8 %assemble.3 = (f32[4096,128]{1,0:T(8,128)}, f32[4096,128]{1,0:T(8,128)}) custom-call(s32[3]{0:T(128)S(1)} %pad_add_fusion.ids, f32[4096,128]{1,0:T(8,128)} %get-tuple-element.92.refs_0_, f32[4096,128]{1,0:T(8,128)} %get-tuple-element.93.refs_1_, bf16[384,256]{1,0:T(8,128)(2,1)S(1)} %add_convert_fusion.refs_2_, ...), custom_call_target="tpu_custom_call", output_to_operand_aliasing={{0}: (1, {}), {1}: (2, {})} | custom-call | tf_op jit(solution)/shard_map/assemble/pallas_call | solution.py:393
  (99 shorter events, 17.4 us)
Async XLA Ops:
  2.9 15.9 %collective-permute-start = (bf16[1024,256]{1,0:T(8,128)(2,1)}, bf16[1024,256]{1,0:T(8,128)(2,1)S(1)}, u32[]{:S(2)}, u32[]{:S(2)}) collective-permute-start(bf16[1024,256]{1,0:T(8,128)(2,1)} %pad_maximum_fusion), channel_id=1, source_target_pairs={{0,8},{8,0},{16,24},{24,16},{1,9},{9,1},{17,25},{25,17},{2,10},{10... | collective-permute-start | bytes 1572872 | tf_op jit(solution)/shard_map/ppermute | solution.py:32
  6.7 15.1 %collective-permute-start.2 = (bf16[1024,256]{1,0:T(8,128)(2,1)}, bf16[1024,256]{1,0:T(8,128)(2,1)S(1)}, u32[]{:S(2)}, u32[]{:S(2)}) collective-permute-start(bf16[1024,256]{1,0:T(8,128)(2,1)} %pad_maximum_fusion.1), channel_id=1, source_target_pairs={{0,16},{8,24},{16,0},{24,8},{1,17},{9,25},{17,1},{25,9},{2,18},{10... | collective-permute-start | bytes 1572872 | tf_op jit(solution)/shard_map/ppermute | solution.py:32
  8.2 24.9 %collective-permute-start.5 = (bf16[1024,256]{1,0:T(8,128)(2,1)}, bf16[1024,256]{1,0:T(8,128)(2,1)}, u32[]{:S(2)}, u32[]{:S(2)}) collective-permute-start(bf16[1024,256]{1,0:T(8,128)(2,1)} %pad_maximum_fusion), channel_id=1, source_target_pairs={{0,16},{8,24},{16,0},{24,8},{1,17},{9,25},{17,1},{25,9},{2,18},{10... | collective-permute-start | bytes 1572872 | tf_op jit(solution)/shard_map/ppermute | solution.py:32
  8.7 24.4 %collective-permute-start.1 = (bf16[1024,256]{1,0:T(8,128)(2,1)}, bf16[1024,256]{1,0:T(8,128)(2,1)}, u32[]{:S(2)}, u32[]{:S(2)}) collective-permute-start(bf16[1024,256]{1,0:T(8,128)(2,1)} %pad_maximum_fusion.1), channel_id=1, source_target_pairs={{0,8},{8,0},{16,24},{24,16},{1,9},{9,1},{17,25},{25,17},{2,10},{10... | collective-permute-start | bytes 1572872 | tf_op jit(solution)/shard_map/ppermute | solution.py:32
  21.8 11.9 %collective-permute-start.3 = (bf16[1024,256]{1,0:T(8,128)(2,1)S(1)}, bf16[1024,256]{1,0:T(8,128)(2,1)}, u32[]{:S(2)}, u32[]{:S(2)}) collective-permute-start(bf16[1024,256]{1,0:T(8,128)(2,1)S(1)} %collective-permute-done.refs_2_), channel_id=1, source_target_pairs={{0,1},{1,0},{2,3},{3,2},{4,5},{5,4},{6,7},{7,6},{8,9},{9,8},{10,11... | collective-permute-start | bytes 1572872 | tf_op jit(solution)/shard_map/ppermute | solution.py:32
  21.8 21.0 %collective-permute-start.8 = (bf16[1024,256]{1,0:T(8,128)(2,1)S(1)}, bf16[1024,256]{1,0:T(8,128)(2,1)S(1)}, u32[]{:S(2)}, u32[]{:S(2)}) collective-permute-start(bf16[1024,256]{1,0:T(8,128)(2,1)S(1)} %collective-permute-done.refs_2_), channel_id=1, source_target_pairs={{0,16},{8,24},{16,0},{24,8},{1,17},{9,25},{17,1},{25,9},{2,18},{10... | collective-permute-start | bytes 1572872 | tf_op jit(solution)/shard_map/ppermute | solution.py:32
  23.3 19.5 %collective-permute-start.9 = (bf16[1024,256]{1,0:T(8,128)(2,1)S(1)}, bf16[1024,256]{1,0:T(8,128)(2,1)S(1)}, u32[]{:S(2)}, u32[]{:S(2)}) collective-permute-start(bf16[1024,256]{1,0:T(8,128)(2,1)S(1)} %collective-permute-done.2.refs_7_), channel_id=1, source_target_pairs={{0,8},{8,0},{16,24},{24,16},{1,9},{9,1},{17,25},{25,17},{2,10},{10... | collective-permute-start | bytes 1572872 | tf_op jit(solution)/shard_map/ppermute | solution.py:32
  33.1 3.2 %collective-permute-start.6 = (bf16[1024,256]{1,0:T(8,128)(2,1)}, bf16[1024,256]{1,0:T(8,128)(2,1)S(1)}, u32[]{:S(2)}, u32[]{:S(2)}) collective-permute-start(bf16[1024,256]{1,0:T(8,128)(2,1)} %collective-permute-done.5.refs_6_), channel_id=1, source_target_pairs={{0,1},{1,0},{2,3},{3,2},{4,5},{5,4},{6,7},{7,6},{8,9},{9,8},{10,11... | collective-permute-start | bytes 1572872 | tf_op jit(solution)/shard_map/ppermute | solution.py:32
  33.1 3.6 %collective-permute-start.4 = (bf16[1024,256]{1,0:T(8,128)(2,1)}, bf16[1024,256]{1,0:T(8,128)(2,1)S(1)}, u32[]{:S(2)}, u32[]{:S(2)}) collective-permute-start(bf16[1024,256]{1,0:T(8,128)(2,1)} %collective-permute-done.1.refs_3_), channel_id=1, source_target_pairs={{0,1},{1,0},{2,3},{3,2},{4,5},{5,4},{6,7},{7,6},{8,9},{9,8},{10,11... | collective-permute-start | bytes 1572872 | tf_op jit(solution)/shard_map/ppermute | solution.py:32
  33.6 3.1 %collective-permute-start.7 = (bf16[1024,256]{1,0:T(8,128)(2,1)S(1)}, bf16[1024,256]{1,0:T(8,128)(2,1)S(1)}, u32[]{:S(2)}, u32[]{:S(2)}) collective-permute-start(bf16[1024,256]{1,0:T(8,128)(2,1)S(1)} %collective-permute-done.2.refs_7_), channel_id=1, source_target_pairs={{0,1},{1,0},{2,3},{3,2},{4,5},{5,4},{6,7},{7,6},{8,9},{9,8},{10,11... | collective-permute-start | bytes 1572872 | tf_op jit(solution)/shard_map/ppermute | solution.py:32
  42.8 2.1 %collective-permute-start.10 = (bf16[1024,256]{1,0:T(8,128)(2,1)S(1)}, bf16[1024,256]{1,0:T(8,128)(2,1)S(1)}, u32[]{:S(2)}, u32[]{:S(2)}) collective-permute-start(bf16[1024,256]{1,0:T(8,128)(2,1)S(1)} %collective-permute-done.8.refs_1_), channel_id=1, source_target_pairs={{0,1},{1,0},{2,3},{3,2},{4,5},{5,4},{6,7},{7,6},{8,9},{9,8},{10,11... | collective-permute-start | bytes 1572872 | tf_op jit(solution)/shard_map/ppermute | solution.py:32
  42.9 2.6 %collective-permute-start.11 = (bf16[1024,256]{1,0:T(8,128)(2,1)S(1)}, bf16[1024,256]{1,0:T(8,128)(2,1)S(1)}, u32[]{:S(2)}, u32[]{:S(2)}) collective-permute-start(bf16[1024,256]{1,0:T(8,128)(2,1)S(1)} %collective-permute-done.9.refs_2_), channel_id=1, source_target_pairs={{0,1},{1,0},{2,3},{3,2},{4,5},{5,4},{6,7},{7,6},{8,9},{9,8},{10,11... | collective-permute-start | bytes 1572872 | tf_op jit(solution)/shard_map/ppermute | solution.py:32
  43.4 28.7 %collective-permute-start.20 = (bf16[192,2560]{1,0:T(8,128)(2,1)S(1)}, bf16[192,2560]{1,0:T(8,128)(2,1)S(1)}, u32[]{:S(2)}, u32[]{:S(2)}) collective-permute-start(bf16[192,2560]{1,0:T(8,128)(2,1)S(1)} %get-tuple-element.68), channel_id=1, source_target_pairs={{0,16},{8,24},{16,0},{24,8},{1,17},{9,25},{17,1},{25,9},{2,18},{10... | collective-permute-start | bytes 2949128 | tf_op jit(solution)/shard_map/ppermute | solution.py:32
  44.9 27.2 %collective-permute-start.19 = (bf16[192,2560]{1,0:T(8,128)(2,1)S(1)}, bf16[192,2560]{1,0:T(8,128)(2,1)S(1)}, u32[]{:S(2)}, u32[]{:S(2)}) collective-permute-start(bf16[192,2560]{1,0:T(8,128)(2,1)S(1)} %get-tuple-element.67), channel_id=1, source_target_pairs={{0,8},{8,0},{16,24},{24,16},{1,9},{9,1},{17,25},{25,17},{2,10},{10... | collective-permute-start | bytes 2949128 | tf_op jit(solution)/shard_map/ppermute | solution.py:32
  46.7 7.6 %collective-permute-start.14 = (bf16[192,256]{1,0:T(8,128)(2,1)S(1)}, bf16[192,256]{1,0:T(8,128)(2,1)S(1)}, u32[]{:S(2)}, u32[]{:S(2)}) collective-permute-start(bf16[192,256]{1,0:T(8,128)(2,1)S(1)} %project.3.refs_0_), channel_id=1, source_target_pairs={{0,6},{1,7},{2,4},{3,5},{4,2},{5,3},{6,0},{7,1},{8,14},{9,15},{10,... | collective-permute-start | bytes 294920 | tf_op jit(solution)/shard_map/ppermute | solution.py:32
  50.3 8.6 %collective-permute-start.13 = (bf16[192,256]{1,0:T(8,128)(2,1)S(1)}, bf16[192,256]{1,0:T(8,128)(2,1)S(1)}, u32[]{:S(2)}, u32[]{:S(2)}) collective-permute-start(bf16[192,256]{1,0:T(8,128)(2,1)S(1)} %project.3.refs_0_), channel_id=1, source_target_pairs={{0,4},{1,5},{2,6},{3,7},{4,0},{5,1},{6,2},{7,3},{8,12},{9,13},{10,... | collective-permute-start | bytes 294920 | tf_op jit(solution)/shard_map/ppermute | solution.py:32
  50.4 8.6 %collective-permute-start.12 = (bf16[192,256]{1,0:T(8,128)(2,1)S(1)}, bf16[192,256]{1,0:T(8,128)(2,1)S(1)}, u32[]{:S(2)}, u32[]{:S(2)}) collective-permute-start(bf16[192,256]{1,0:T(8,128)(2,1)S(1)} %project.3.refs_0_), channel_id=1, source_target_pairs={{0,2},{1,3},{2,0},{3,1},{4,6},{5,7},{6,4},{7,5},{8,10},{9,11},{10,... | collective-permute-start | bytes 294920 | tf_op jit(solution)/shard_map/ppermute | solution.py:32
  58.9 32.6 %collective-permute-start.28 = (bf16[192,2560]{1,0:T(8,128)(2,1)S(1)}, bf16[192,2560]{1,0:T(8,128)(2,1)S(1)}, u32[]{:S(2)}, u32[]{:S(2)}) collective-permute-start(bf16[192,2560]{1,0:T(8,128)(2,1)S(1)} %get-tuple-element.78), channel_id=1, source_target_pairs={{0,24},{8,16},{16,8},{24,0},{1,25},{9,17},{17,9},{25,1},{2,26},{10... | collective-permute-start | bytes 2949128 | tf_op jit(solution)/shard_map/ppermute | solution.py:32
  60.9 1.5 collective-permute-start.16
  62.3 1.3 collective-permute-start.18
  72.1 1.7 %collective-permute-start.21 = (bf16[768,256]{1,0:T(8,128)(2,1)S(1)}, bf16[768,256]{1,0:T(8,128)(2,1)S(1)}, u32[]{:S(2)}, u32[]{:S(2)}) collective-permute-start(bf16[768,256]{1,0:T(8,128)(2,1)S(1)} %get-tuple-element.72), channel_id=1, source_target_pairs={{0,1},{1,0},{2,3},{3,2},{4,5},{5,4},{6,7},{7,6},{8,9},{9,8},{10,11... | collective-permute-start | bytes 1179656 | tf_op jit(solution)/shard_map/ppermute | solution.py:32
  74.0 6.6 %collective-permute-start.22 = (bf16[192,256]{1,0:T(8,128)(2,1)S(1)}, bf16[192,256]{1,0:T(8,128)(2,1)S(1)}, u32[]{:S(2)}, u32[]{:S(2)}) collective-permute-start(bf16[192,256]{1,0:T(8,128)(2,1)S(1)} %get-tuple-element.74), channel_id=1, source_target_pairs={{0,2},{1,3},{2,0},{3,1},{4,6},{5,7},{6,4},{7,5},{8,10},{9,11},{10,... | collective-permute-start | bytes 294920 | tf_op jit(solution)/shard_map/ppermute | solution.py:32
  74.5 10.8 %collective-permute-start.23 = (bf16[192,256]{1,0:T(8,128)(2,1)S(1)}, bf16[192,256]{1,0:T(8,128)(2,1)S(1)}, u32[]{:S(2)}, u32[]{:S(2)}) collective-permute-start(bf16[192,256]{1,0:T(8,128)(2,1)S(1)} %get-tuple-element.75), channel_id=1, source_target_pairs={{0,4},{1,5},{2,6},{3,7},{4,0},{5,1},{6,2},{7,3},{8,12},{9,13},{10,... | collective-permute-start | bytes 294920 | tf_op jit(solution)/shard_map/ppermute | solution.py:32
  77.1 8.3 %collective-permute-start.24 = (bf16[192,256]{1,0:T(8,128)(2,1)S(1)}, bf16[192,256]{1,0:T(8,128)(2,1)S(1)}, u32[]{:S(2)}, u32[]{:S(2)}) collective-permute-start(bf16[192,256]{1,0:T(8,128)(2,1)S(1)} %get-tuple-element.76), channel_id=1, source_target_pairs={{0,6},{1,7},{2,4},{3,5},{4,2},{5,3},{6,0},{7,1},{8,14},{9,15},{10,... | collective-permute-start | bytes 294920 | tf_op jit(solution)/shard_map/ppermute | solution.py:32
  85.4 8.1 %collective-permute-start.27 = (bf16[192,256]{1,0:T(8,128)(2,1)S(1)}, bf16[192,256]{1,0:T(8,128)(2,1)S(1)}, u32[]{:S(2)}, u32[]{:S(2)}) collective-permute-start(bf16[192,256]{1,0:T(8,128)(2,1)S(1)} %total.1.refs_4_.refs_1_), channel_id=1, source_target_pairs={{0,24},{8,16},{16,8},{24,0},{1,25},{9,17},{17,9},{25,1},{2,26},{10... | collective-permute-start | bytes 294920 | tf_op jit(solution)/shard_map/ppermute | solution.py:32
  86.5 8.4 %collective-permute-start.26 = (bf16[192,256]{1,0:T(8,128)(2,1)S(1)}, bf16[192,256]{1,0:T(8,128)(2,1)S(1)}, u32[]{:S(2)}, u32[]{:S(2)}) collective-permute-start(bf16[192,256]{1,0:T(8,128)(2,1)S(1)} %total.1.refs_4_.refs_1_), channel_id=1, source_target_pairs={{0,16},{8,24},{16,0},{24,8},{1,17},{9,25},{17,1},{25,9},{2,18},{10... | collective-permute-start | bytes 294920 | tf_op jit(solution)/shard_map/ppermute | solution.py:32
  88.0 6.9 %collective-permute-start.25 = (bf16[192,256]{1,0:T(8,128)(2,1)S(1)}, bf16[192,256]{1,0:T(8,128)(2,1)S(1)}, u32[]{:S(2)}, u32[]{:S(2)}) collective-permute-start(bf16[192,256]{1,0:T(8,128)(2,1)S(1)} %total.1.refs_4_.refs_1_), channel_id=1, source_target_pairs={{0,8},{8,0},{16,24},{24,16},{1,9},{9,1},{17,25},{25,17},{2,10},{10... | collective-permute-start | bytes 294920 | tf_op jit(solution)/shard_map/ppermute | solution.py:32
  96.5 5.5 %collective-permute-start.31 = (bf16[3072,256]{1,0:T(8,128)(2,1)S(1)}, bf16[3072,256]{1,0:T(8,128)(2,1)S(1)}, u32[]{:S(2)}, u32[]{:S(2)}) collective-permute-start(bf16[3072,256]{1,0:T(8,128)(2,1)S(1)} %get-tuple-element.89), channel_id=1, source_target_pairs={{0,1},{1,0},{2,3},{3,2},{4,5},{5,4},{6,7},{7,6},{8,9},{9,8},{10,11... | collective-permute-start | bytes 4718600 | tf_op jit(solution)/shard_map/ppermute | solution.py:32
  97.9 2.4 %collective-permute-start.29 = (bf16[512,256]{1,0:T(8,128)(2,1)S(1)}, bf16[512,256]{1,0:T(8,128)(2,1)S(1)}, u32[]{:S(2)}, u32[]{:S(2)}) collective-permute-start(bf16[512,256]{1,0:T(8,128)(2,1)S(1)} %get-tuple-element.84), channel_id=1, source_target_pairs={{0,1},{1,0},{2,3},{3,2},{4,5},{5,4},{6,7},{7,6},{8,9},{9,8},{10,11... | collective-permute-start | bytes 786440 | tf_op jit(solution)/shard_map/ppermute | solution.py:32
  100.1 1.8 %collective-permute-start.30 = (bf16[768,256]{1,0:T(8,128)(2,1)S(1)}, bf16[768,256]{1,0:T(8,128)(2,1)S(1)}, u32[]{:S(2)}, u32[]{:S(2)}) collective-permute-start(bf16[768,256]{1,0:T(8,128)(2,1)S(1)} %get-tuple-element.86), channel_id=1, source_target_pairs={{0,1},{1,0},{2,3},{3,2},{4,5},{5,4},{6,7},{7,6},{8,9},{9,8},{10,11... | collective-permute-start | bytes 1179656 | tf_op jit(solution)/shard_map/ppermute | solution.py:32
  102.6 6.4 %collective-permute-start.32 = (bf16[256,256]{1,0:T(8,128)(2,1)S(1)}, bf16[256,256]{1,0:T(8,128)(2,1)S(1)}, u32[]{:S(2)}, u32[]{:S(2)}) collective-permute-start(bf16[256,256]{1,0:T(8,128)(2,1)S(1)} %slice.74), channel_id=1, source_target_pairs={{0,2},{1,3},{2,0},{3,1},{4,6},{5,7},{6,4},{7,5},{8,10},{9,11},{10,... | collective-permute-start | bytes 393224 | tf_op jit(solution)/shard_map/ppermute | solution.py:32
  104.3 9.9 %collective-permute-start.37 = (bf16[384,256]{1,0:T(8,128)(2,1)S(1)}, bf16[384,256]{1,0:T(8,128)(2,1)S(1)}, u32[]{:S(2)}, u32[]{:S(2)}) collective-permute-start(bf16[384,256]{1,0:T(8,128)(2,1)S(1)} %slice.73), channel_id=1, source_target_pairs={{0,2},{1,3},{2,0},{3,1},{4,6},{5,7},{6,4},{7,5},{8,10},{9,11},{10,... | collective-permute-start | bytes 589832 | tf_op jit(solution)/shard_map/ppermute | solution.py:32
  104.8 18.3 %collective-permute-start.42 = (bf16[768,256]{1,0:T(8,128)(2,1)S(1)}, bf16[768,256]{1,0:T(8,128)(2,1)S(1)}, u32[]{:S(2)}, u32[]{:S(2)}) collective-permute-start(bf16[768,256]{1,0:T(8,128)(2,1)S(1)} %get-tuple-element.95), channel_id=1, source_target_pairs={{0,8},{8,0},{16,24},{24,16},{1,9},{9,1},{17,25},{25,17},{2,10},{10... | collective-permute-start | bytes 1179656 | tf_op jit(solution)/shard_map/ppermute | solution.py:32
  105.4 18.8 %collective-permute-start.43 = (bf16[768,256]{1,0:T(8,128)(2,1)S(1)}, bf16[768,256]{1,0:T(8,128)(2,1)S(1)}, u32[]{:S(2)}, u32[]{:S(2)}) collective-permute-start(bf16[768,256]{1,0:T(8,128)(2,1)S(1)} %get-tuple-element.96), channel_id=1, source_target_pairs={{0,16},{8,24},{16,0},{24,8},{1,17},{9,25},{17,1},{25,9},{2,18},{10... | collective-permute-start | bytes 1179656 | tf_op jit(solution)/shard_map/ppermute | solution.py:32
  106.0 18.2 %collective-permute-start.44 = (bf16[768,256]{1,0:T(8,128)(2,1)S(1)}, bf16[768,256]{1,0:T(8,128)(2,1)S(1)}, u32[]{:S(2)}, u32[]{:S(2)}) collective-permute-start(bf16[768,256]{1,0:T(8,128)(2,1)S(1)} %get-tuple-element.97), channel_id=1, source_target_pairs={{0,24},{8,16},{16,8},{24,0},{1,25},{9,17},{17,9},{25,1},{2,26},{10... | collective-permute-start | bytes 1179656 | tf_op jit(solution)/shard_map/ppermute | solution.py:32
  109.1 13.3 %collective-permute-start.33 = (bf16[256,256]{1,0:T(8,128)(2,1)S(1)}, bf16[256,256]{1,0:T(8,128)(2,1)S(1)}, u32[]{:S(2)}, u32[]{:S(2)}) collective-permute-start(bf16[256,256]{1,0:T(8,128)(2,1)S(1)} %fusion.2), channel_id=1, source_target_pairs={{0,4},{1,5},{2,6},{3,7},{4,0},{5,1},{6,2},{7,3},{8,12},{9,13},{10,... | collective-permute-start | bytes 393224 | tf_op jit(solution)/shard_map/ppermute | solution.py:32
  114.2 12.1 %collective-permute-start.38 = (bf16[384,256]{1,0:T(8,128)(2,1)S(1)}, bf16[384,256]{1,0:T(8,128)(2,1)S(1)}, u32[]{:S(2)}, u32[]{:S(2)}) collective-permute-start(bf16[384,256]{1,0:T(8,128)(2,1)S(1)} %fusion), channel_id=1, source_target_pairs={{0,4},{1,5},{2,6},{3,7},{4,0},{5,1},{6,2},{7,3},{8,12},{9,13},{10,... | collective-permute-start | bytes 589832 | tf_op jit(solution)/shard_map/ppermute | solution.py:32
  122.4 12.9 %collective-permute-start.34 = (bf16[256,256]{1,0:T(8,128)(2,1)S(1)}, bf16[256,256]{1,0:T(8,128)(2,1)S(1)}, u32[]{:S(2)}, u32[]{:S(2)}) collective-permute-start(bf16[256,256]{1,0:T(8,128)(2,1)S(1)} %add_convert_fusion.2.refs_0_), channel_id=1, source_target_pairs={{0,2},{1,3},{2,0},{3,1},{4,6},{5,7},{6,4},{7,5},{8,10},{9,11},{10,... | collective-permute-start | bytes 393224 | tf_op jit(solution)/shard_map/ppermute | solution.py:32
  124.4 9.0 %collective-permute-start.45 = (bf16[384,256]{1,0:T(8,128)(2,1)S(1)}, bf16[384,256]{1,0:T(8,128)(2,1)S(1)}, u32[]{:S(2)}, u32[]{:S(2)}) collective-permute-start(bf16[384,256]{1,0:T(8,128)(2,1)S(1)} %slice.72), channel_id=1, source_target_pairs={{0,2},{1,3},{2,0},{3,1},{4,6},{5,7},{6,4},{7,5},{8,10},{9,11},{10,... | collective-permute-start | bytes 589832 | tf_op jit(solution)/shard_map/ppermute | solution.py:32
  126.4 12.1 %collective-permute-start.39 = (bf16[384,256]{1,0:T(8,128)(2,1)S(1)}, bf16[384,256]{1,0:T(8,128)(2,1)S(1)}, u32[]{:S(2)}, u32[]{:S(2)}) collective-permute-start(bf16[384,256]{1,0:T(8,128)(2,1)S(1)} %add_convert_fusion.1.refs_4_), channel_id=1, source_target_pairs={{0,2},{1,3},{2,0},{3,1},{4,6},{5,7},{6,4},{7,5},{8,10},{9,11},{10,... | collective-permute-start | bytes 589832 | tf_op jit(solution)/shard_map/ppermute | solution.py:32
  133.4 10.0 %collective-permute-start.46 = (bf16[384,256]{1,0:T(8,128)(2,1)S(1)}, bf16[384,256]{1,0:T(8,128)(2,1)S(1)}, u32[]{:S(2)}, u32[]{:S(2)}) collective-permute-start(bf16[384,256]{1,0:T(8,128)(2,1)S(1)} %fusion.1), channel_id=1, source_target_pairs={{0,4},{1,5},{2,6},{3,7},{4,0},{5,1},{6,2},{7,3},{8,12},{9,13},{10,... | collective-permute-start | bytes 589832 | tf_op jit(solution)/shard_map/ppermute | solution.py:32
  135.3 3.2 %collective-permute-start.35 = (bf16[256,256]{1,0:T(8,128)(2,1)S(1)}, bf16[256,256]{1,0:T(8,128)(2,1)S(1)}, u32[]{:S(2)}, u32[]{:S(2)}) collective-permute-start(bf16[256,256]{1,0:T(8,128)(2,1)S(1)} %add_convert_fusion.2.refs_0_), channel_id=1, source_target_pairs={{0,1},{1,0},{2,3},{3,2},{4,5},{5,4},{6,7},{7,6},{8,9},{9,8},{10,11... | collective-permute-start | bytes 393224 | tf_op jit(solution)/shard_map/ppermute | solution.py:32
  135.3 3.2 %collective-permute-start.36 = (bf16[256,256]{1,0:T(8,128)(2,1)S(1)}, bf16[256,256]{1,0:T(8,128)(2,1)S(1)}, u32[]{:S(2)}, u32[]{:S(2)}) collective-permute-start(bf16[256,256]{1,0:T(8,128)(2,1)S(1)} %collective-permute-done.34.refs_1_), channel_id=1, source_target_pairs={{0,1},{1,0},{2,3},{3,2},{4,5},{5,4},{6,7},{7,6},{8,9},{9,8},{10,11... | collective-permute-start | bytes 393224 | tf_op jit(solution)/shard_map/ppermute | solution.py:32
  135.8 7.8 %collective-permute-start.40 = (bf16[384,256]{1,0:T(8,128)(2,1)S(1)}, bf16[384,256]{1,0:T(8,128)(2,1)S(1)}, u32[]{:S(2)}, u32[]{:S(2)}) collective-permute-start(bf16[384,256]{1,0:T(8,128)(2,1)S(1)} %add_convert_fusion.1.refs_4_), channel_id=1, source_target_pairs={{0,1},{1,0},{2,3},{3,2},{4,5},{5,4},{6,7},{7,6},{8,9},{9,8},{10,11... | collective-permute-start | bytes 589832 | tf_op jit(solution)/shard_map/ppermute | solution.py:32
  138.5 5.1 %collective-permute-start.41 = (bf16[384,256]{1,0:T(8,128)(2,1)S(1)}, bf16[384,256]{1,0:T(8,128)(2,1)S(1)}, u32[]{:S(2)}, u32[]{:S(2)}) collective-permute-start(bf16[384,256]{1,0:T(8,128)(2,1)S(1)} %collective-permute-done.39.refs_5_), channel_id=1, source_target_pairs={{0,1},{1,0},{2,3},{3,2},{4,5},{5,4},{6,7},{7,6},{8,9},{9,8},{10,11... | collective-permute-start | bytes 589832 | tf_op jit(solution)/shard_map/ppermute | solution.py:32
  143.4 5.7 %collective-permute-start.47 = (bf16[384,256]{1,0:T(8,128)(2,1)S(1)}, bf16[384,256]{1,0:T(8,128)(2,1)S(1)}, u32[]{:S(2)}, u32[]{:S(2)}) collective-permute-start(bf16[384,256]{1,0:T(8,128)(2,1)S(1)} %add_convert_fusion.refs_2_), channel_id=1, source_target_pairs={{0,2},{1,3},{2,0},{3,1},{4,6},{5,7},{6,4},{7,5},{8,10},{9,11},{10,... | collective-permute-start | bytes 589832 | tf_op jit(solution)/shard_map/ppermute | solution.py:32
  143.5 5.7 %collective-permute-start.48 = (bf16[384,256]{1,0:T(8,128)(2,1)S(1)}, bf16[384,256]{1,0:T(8,128)(2,1)S(1)}, u32[]{:S(2)}, u32[]{:S(2)}) collective-permute-start(bf16[384,256]{1,0:T(8,128)(2,1)S(1)} %add_convert_fusion.refs_2_), channel_id=1, source_target_pairs={{0,1},{1,0},{2,3},{3,2},{4,5},{5,4},{6,7},{7,6},{8,9},{9,8},{10,11... | collective-permute-start | bytes 589832 | tf_op jit(solution)/shard_map/ppermute | solution.py:32
  149.1 1.4 collective-permute-start.49
  (10 other events, 133.1 us)

commit v17 on v16

--- a/solution.py
+++ b/solution.py
@@ -284,7 +284,7 @@
                     out_ref[pl.ds(to, step), :] = piece.astype(out_ref.dtype)
 
 
-def weight_rows(ids, hidden, grads, groups, origin, rows, block_rows, sub_count):
+def weight_rows(ids, hidden, grads, groups, origin, rows, block_rows, sub_count, earlier=()):
     plan = Plan(
         hidden=len(hidden),
         groups=groups,
@@ -301,6 +301,7 @@
         (ids,),
         (*hidden, *grads),
     )
+    (theirs,), _ = after([theirs], *earlier)
     return ours, swap(theirs, "ctx", 1)
 
 
@@ -506,12 +507,12 @@
     grad = add_all([own] + [swap(one, "ctx", 2 * m) for m, one in enumerate(leaving, 1)])
     grads = [grad] + [swap(grad, "dp", j) for j in range(1, dp_count)]
 
-    (grad,), ended = after([grad], *grads[1:], *[moved[j] for j in far])
-    grads[1:] = ended[: dp_count - 1]
-    moved.update(zip(far, ended[dp_count - 1 :]))
+    (grad,), ended = after([grad], grads[near[0]], *[moved[j] for j in far])
+    grads[near[0]] = ended[0]
+    moved.update(zip(far, ended[1:]))
     groups = [[(0, j, 0, 0)] for j in range(dp_count)]
     ours, came = weight_rows(
-        ids, [inputs], [grad], groups, *regions[-1], block_rows, sub_count
+        ids, [inputs], [grad], groups, *regions[-1], block_rows, sub_count, grads[1:]
     )
     own = parts_over_dp(add_cores(ours, came))
     groups = [[(j, None, j, 0) for j in range(dp_count)]]

time: 153 us -> 151 us (0.987)
  transfers between devices with their start and end apart: 50 -> 50, of which waited for: 29 -> 29; matrix products, arithmetic and copies ran while one was open for 3% -> 3% of each run, Pallas kernels for 12% -> 13%
where the time goes in v17:
time: 151 us
  waiting for transfers between devices  78.6 us (52%)
  starting transfers between devices  41.7 us (28%)
  Pallas kernels  21.4 us (14%)
  local copies, waits for them, and re-layouts  5.14 us (3%)
  other arithmetic  2.92 us (2%)
    ppermute x50, waiting for transfers between devices, swap(): return lax.ppermute(array, axis, [(i, i ^ distance) for i in range(count)])  78.6 us
    ppermute x50, starting transfers between devices, swap(): return lax.ppermute(array, axis, [(i, i ^ distance) for i in range(count)])  41.7 us
    pallas_call x7, Pallas kernels, kernel_call(): pl.pallas_call(kernel, out_shape=outs, in_specs=[smem] * len(scalars) + [...  9.06 us
    pallas_call x1, Pallas kernels, attention(): pl.pallas_call(functools.partial(attention_kernel, shape), out_shape=(jax...  8.46 us
    pallas_call x2, Pallas kernels, assemble(): pl.pallas_call(functools.partial(assemble_kernel, sub_count, regions, not...  3.92 us
  transfers between devices with their start and end apart: 50, of which 29 were waited for; matrix products, arithmetic and copies ran while one was open for 3% of the time, Pallas kernels for 13%

profile of v17, /device:TPU:0, one launch (start us, length us, event | category | flops | bytes accessed | tf_op | source)
XLA Modules:
  0.0 150.8 jit_solution(4482806344823600269)
XLA Ops:
  0.7 1.4 constant_dynamic-slice_fusion
  2.9 2.9 %collective-permute-start = (bf16[1024,256]{1,0:T(8,128)(2,1)}, bf16[1024,256]{1,0:T(8,128)(2,1)S(1)}, u32[]{:S(2)}, u32[]{:S(2)}) collective-permute-start(bf16[1024,256]{1,0:T(8,128)(2,1)} %pad_maximum_fusion), channel_id=1, source_target_pairs={{0,8},{8,0},{16,24},{24,16},{1,9},{9,1},{17,25},{25,17},{2,10},{10... | collective-permute-start | bytes 1572872 | tf_op jit(solution)/shard_map/ppermute | solution.py:32
  6.7 1.5 %collective-permute-start.2 = (bf16[1024,256]{1,0:T(8,128)(2,1)}, bf16[1024,256]{1,0:T(8,128)(2,1)S(1)}, u32[]{:S(2)}, u32[]{:S(2)}) collective-permute-start(bf16[1024,256]{1,0:T(8,128)(2,1)} %pad_maximum_fusion.1), channel_id=1, source_target_pairs={{0,16},{8,24},{16,0},{24,8},{1,17},{9,25},{17,1},{25,9},{2,18},{10... | collective-permute-start | bytes 1572872 | tf_op jit(solution)/shard_map/ppermute | solution.py:32
  8.8 10.0 %collective-permute-done.refs_2_ = bf16[1024,256]{1,0:T(8,128)(2,1)S(1)} collective-permute-done((bf16[1024,256]{1,0:T(8,128)(2,1)}, bf16[1024,256]{1,0:T(8,128)(2,1)S(1)}, u32[]{:S(2)}, u32[]{:S(2)}) %collective-permute-start) | collective-permute-done | bytes 524320 | tf_op jit(solution)/shard_map/ppermute | solution.py:32
  18.8 3.0 %collective-permute-done.2.refs_7_ = bf16[1024,256]{1,0:T(8,128)(2,1)S(1)} collective-permute-done((bf16[1024,256]{1,0:T(8,128)(2,1)}, bf16[1024,256]{1,0:T(8,128)(2,1)S(1)}, u32[]{:S(2)}, u32[]{:S(2)}) %collective-permute-start.2) | collective-permute-done | bytes 524320 | tf_op jit(solution)/shard_map/ppermute | solution.py:32
  21.8 1.5 %collective-permute-start.8 = (bf16[1024,256]{1,0:T(8,128)(2,1)S(1)}, bf16[1024,256]{1,0:T(8,128)(2,1)S(1)}, u32[]{:S(2)}, u32[]{:S(2)}) collective-permute-start(bf16[1024,256]{1,0:T(8,128)(2,1)S(1)} %collective-permute-done.refs_2_), channel_id=1, source_target_pairs={{0,16},{8,24},{16,0},{24,8},{1,17},{9,25},{17,1},{25,9},{2,18},{10... | collective-permute-start | bytes 1572872 | tf_op jit(solution)/shard_map/ppermute | solution.py:32
  23.8 9.3 %collective-permute-done.5.refs_6_ = bf16[1024,256]{1,0:T(8,128)(2,1)} collective-permute-done((bf16[1024,256]{1,0:T(8,128)(2,1)}, bf16[1024,256]{1,0:T(8,128)(2,1)}, u32[]{:S(2)}, u32[]{:S(2)}) %collective-permute-start.5) | collective-permute-done | bytes 524320 | tf_op jit(solution)/shard_map/ppermute | solution.py:32
  33.8 2.5 %dynamic-slice_bitcast_fusion = (bf16[192,2560]{1,0:T(8,128)(2,1)S(1)}, bf16[192,2560]{1,0:T(8,128)(2,1)S(1)}, bf16[192,2560]{1,0:T(8,128)(2,1)S(1)}, bf16[192,2560]{1,0:T(8,128)(2,1)S(1)}) fusion(bf16[1,192,16384]{2,1,0:T(8,128)(2,1)} %param.7, s32[]{:T(128)S(6)} %select_n.42, s32[]{:T(128)S(6)} %select_n.40, s32[]{:T(128)S(6)} %select_n.39, s32[]{:T(128)S(6)} %select_n.41), kind=kLoop, calls=%fused_computation.1 | loop fusion | bytes 7864336 | tf_op jit(solution)/shard_map/dynamic_slice | solution.py:465
  37.8 3.2 %project.2.refs_0_ = f32[192,256]{1,0:T(8,128)S(1)} custom-call(s32[3]{0:T(128)S(1)} %pad_add_fusion.ids, bf16[192,16384]{1,0:T(8,128)(2,1)S(1)} %bitcast.19, bf16[4096,128]{1,0:T(8,128)(2,1)S(1)} %copy-done, bf16[4096,128]{1,0:T(8,128)(2,1)S(1)} %copy-done.1, bf16[1024,256]{1,0:T(8,128)(2,1)S(1)} %collective-permute-done.refs_2_, ...), custom_call_target="tpu_custom_call" | custom-call | bytes 16777216 | tf_op jit(solution)/shard_map/project/pallas_call | solution.py:48
  41.0 1.8 %collective-permute-done.8.refs_1_ = bf16[1024,256]{1,0:T(8,128)(2,1)S(1)} collective-permute-done((bf16[1024,256]{1,0:T(8,128)(2,1)S(1)}, bf16[1024,256]{1,0:T(8,128)(2,1)S(1)}, u32[]{:S(2)}, u32[]{:S(2)}) %collective-permute-start.8) | collective-permute-done | bytes 524320 | tf_op jit(solution)/shard_map/ppermute | solution.py:32
  43.4 1.5 %collective-permute-start.20 = (bf16[192,2560]{1,0:T(8,128)(2,1)S(1)}, bf16[192,2560]{1,0:T(8,128)(2,1)S(1)}, u32[]{:S(2)}, u32[]{:S(2)}) collective-permute-start(bf16[192,2560]{1,0:T(8,128)(2,1)S(1)} %get-tuple-element.67), channel_id=1, source_target_pairs={{0,16},{8,24},{16,0},{24,8},{1,17},{9,25},{17,1},{25,9},{2,18},{10... | collective-permute-start | bytes 2949128 | tf_op jit(solution)/shard_map/ppermute | solution.py:32
  45.5 1.1 project.3.refs_0_
  46.7 3.7 %collective-permute-start.14 = (bf16[192,256]{1,0:T(8,128)(2,1)S(1)}, bf16[192,256]{1,0:T(8,128)(2,1)S(1)}, u32[]{:S(2)}, u32[]{:S(2)}) collective-permute-start(bf16[192,256]{1,0:T(8,128)(2,1)S(1)} %project.3.refs_0_), channel_id=1, source_target_pairs={{0,6},{1,7},{2,4},{3,5},{4,2},{5,3},{6,0},{7,1},{8,14},{9,15},{10,... | collective-permute-start | bytes 294920 | tf_op jit(solution)/shard_map/ppermute | solution.py:32
  51.1 3.1 %collective-permute-done.14.refs_6_ = bf16[192,256]{1,0:T(8,128)(2,1)S(1)} collective-permute-done((bf16[192,256]{1,0:T(8,128)(2,1)S(1)}, bf16[192,256]{1,0:T(8,128)(2,1)S(1)}, u32[]{:S(2)}, u32[]{:S(2)}) %collective-permute-start.14) | collective-permute-done | bytes 98336 | tf_op jit(solution)/shard_map/ppermute | solution.py:32
  54.3 4.6 %collective-permute-done.13.refs_4_ = bf16[192,256]{1,0:T(8,128)(2,1)S(1)} collective-permute-done((bf16[192,256]{1,0:T(8,128)(2,1)S(1)}, bf16[192,256]{1,0:T(8,128)(2,1)S(1)}, u32[]{:S(2)}, u32[]{:S(2)}) %collective-permute-start.13) | collective-permute-done | bytes 98336 | tf_op jit(solution)/shard_map/ppermute | solution.py:32
  58.9 2.0 %collective-permute-start.26 = (bf16[192,2560]{1,0:T(8,128)(2,1)S(1)}, bf16[192,2560]{1,0:T(8,128)(2,1)S(1)}, u32[]{:S(2)}, u32[]{:S(2)}) collective-permute-start(bf16[192,2560]{1,0:T(8,128)(2,1)S(1)} %get-tuple-element.77), channel_id=1, source_target_pairs={{0,24},{8,16},{16,8},{24,0},{1,25},{9,17},{17,9},{25,1},{2,26},{10... | collective-permute-start | bytes 2949128 | tf_op jit(solution)/shard_map/ppermute | solution.py:32
  63.7 8.5 %attention.1 = (bf16[192,1024]{1,0:T(8,128)(2,1)}, f32[768,256]{1,0:T(8,128)S(1)}, bf16[768,256]{1,0:T(8,128)(2,1)S(1)}) custom-call(s32[1]{0:T(128)} %bitcast.ids, s32[16]{0:T(128)S(1)} %copy-done.4, s32[8]{0:T(128)S(1)} %bitcast.24, bf16[192,1024]{1,0:T(8,128)(2,1)S(1)} %bitcast.22, bf16[192,1024]{1,0:T(8,128)(2,1)S(1)} %bitcast.23, ...), custom_call_target="tpu_custom_call" | custom-call | tf_op jit(solution)/shard_map/attention/pallas_call | solution.py:171
  72.5 1.4 collective-permute-done.21.came
  74.5 2.6 %collective-permute-start.23 = (bf16[192,256]{1,0:T(8,128)(2,1)S(1)}, bf16[192,256]{1,0:T(8,128)(2,1)S(1)}, u32[]{:S(2)}, u32[]{:S(2)}) collective-permute-start(bf16[192,256]{1,0:T(8,128)(2,1)S(1)} %get-tuple-element.74), channel_id=1, source_target_pairs={{0,4},{1,5},{2,6},{3,7},{4,0},{5,1},{6,2},{7,3},{8,12},{9,13},{10,... | collective-permute-start | bytes 294920 | tf_op jit(solution)/shard_map/ppermute | solution.py:32
  77.1 1.3 collective-permute-start.24
  78.4 2.2 %collective-permute-done.22.refs_1_ = bf16[192,256]{1,0:T(8,128)(2,1)S(1)} collective-permute-done((bf16[192,256]{1,0:T(8,128)(2,1)S(1)}, bf16[192,256]{1,0:T(8,128)(2,1)S(1)}, u32[]{:S(2)}, u32[]{:S(2)}) %collective-permute-start.22) | collective-permute-done | bytes 98336 | tf_op jit(solution)/shard_map/ppermute | solution.py:32
  80.6 4.8 %collective-permute-done.23.refs_2_ = bf16[192,256]{1,0:T(8,128)(2,1)S(1)} collective-permute-done((bf16[192,256]{1,0:T(8,128)(2,1)S(1)}, bf16[192,256]{1,0:T(8,128)(2,1)S(1)}, u32[]{:S(2)}, u32[]{:S(2)}) %collective-permute-start.23) | collective-permute-done | bytes 98336 | tf_op jit(solution)/shard_map/ppermute | solution.py:32
  85.4 1.1 collective-permute-start.25
  86.5 0.9 collective-permute-start.28
  87.4 1.5 %collective-permute-start.27 = (bf16[192,256]{1,0:T(8,128)(2,1)S(1)}, bf16[192,256]{1,0:T(8,128)(2,1)S(1)}, u32[]{:S(2)}, u32[]{:S(2)}) collective-permute-start(bf16[192,256]{1,0:T(8,128)(2,1)S(1)} %total.1.refs_4_.refs_1_), channel_id=1, source_target_pairs={{0,16},{8,24},{16,0},{24,8},{1,17},{9,25},{17,1},{25,9},{2,18},{10... | collective-permute-start | bytes 294920 | tf_op jit(solution)/shard_map/ppermute | solution.py:32
  89.0 2.5 %collective-permute-done.26.refs_3_ = bf16[192,2560]{1,0:T(8,128)(2,1)S(1)} collective-permute-done((bf16[192,2560]{1,0:T(8,128)(2,1)S(1)}, bf16[192,2560]{1,0:T(8,128)(2,1)S(1)}, u32[]{:S(2)}, u32[]{:S(2)}) %collective-permute-start.26) | collective-permute-done | bytes 983072 | tf_op jit(solution)/shard_map/ppermute | solution.py:32
  91.5 1.2 collective-permute-done.25.refs_5_
  92.7 1.7 %weight_rows.5 = (bf16[3072,256]{1,0:T(8,128)(2,1)S(1)}, bf16[3072,256]{1,0:T(8,128)(2,1)S(1)}) custom-call(s32[3]{0:T(128)S(1)} %pad_add_fusion.ids, bf16[192,16384]{1,0:T(8,128)(2,1)S(1)} %bitcast.21, bf16[192,256]{1,0:T(8,128)(2,1)S(1)} %total.1.refs_4_.refs_1_), custom_call_target="tpu_custom_call" | custom-call | tf_op jit(solution)/shard_map/weight_rows/pallas_call | solution.py:48
  94.9 1.3 weight_rows.3
  96.8 1.6 %weight_rows.4 = (bf16[768,256]{1,0:T(8,128)(2,1)S(1)}, bf16[768,256]{1,0:T(8,128)(2,1)S(1)}) custom-call(s32[3]{0:T(128)S(1)} %pad_add_fusion.ids, bf16[192,2560]{1,0:T(8,128)(2,1)S(1)} %get-tuple-element.101.refs_0_, bf16[192,2560]{1,0:T(8,128)(2,1)S(1)} %collective-permute-done.19.refs_1_, bf16[192,2560]{1,0:T(8,128)(2,1)S(1)} %collective-permute-done.20.refs_2_, ...), custom_call_target="tpu_custom_call" | custom-call | tf_op jit(solution)/shard_map/weight_rows/pallas_call | solution.py:48
  98.7 1.4 collective-permute-done.30
  101.0 1.6 %collective-permute-start.32 = (bf16[256,256]{1,0:T(8,128)(2,1)S(1)}, bf16[256,256]{1,0:T(8,128)(2,1)S(1)}, u32[]{:S(2)}, u32[]{:S(2)}) collective-permute-start(bf16[256,256]{1,0:T(8,128)(2,1)S(1)} %slice.74), channel_id=1, source_target_pairs={{0,2},{1,3},{2,0},{3,1},{4,6},{5,7},{6,4},{7,5},{8,10},{9,11},{10,... | collective-permute-start | bytes 393224 | tf_op jit(solution)/shard_map/ppermute | solution.py:32
  103.6 1.0 collective-permute-start.43
  104.6 2.0 %collective-permute-start.44 = (bf16[768,256]{1,0:T(8,128)(2,1)S(1)}, bf16[768,256]{1,0:T(8,128)(2,1)S(1)}, u32[]{:S(2)}, u32[]{:S(2)}) collective-permute-start(bf16[768,256]{1,0:T(8,128)(2,1)S(1)} %get-tuple-element.95), channel_id=1, source_target_pairs={{0,24},{8,16},{16,8},{24,0},{1,25},{9,17},{17,9},{25,1},{2,26},{10... | collective-permute-start | bytes 1179656 | tf_op jit(solution)/shard_map/ppermute | solution.py:32
  107.4 2.6 %collective-permute-start.33 = (bf16[256,256]{1,0:T(8,128)(2,1)S(1)}, bf16[256,256]{1,0:T(8,128)(2,1)S(1)}, u32[]{:S(2)}, u32[]{:S(2)}) collective-permute-start(bf16[256,256]{1,0:T(8,128)(2,1)S(1)} %fusion.2), channel_id=1, source_target_pairs={{0,4},{1,5},{2,6},{3,7},{4,0},{5,1},{6,2},{7,3},{8,12},{9,13},{10,... | collective-permute-start | bytes 393224 | tf_op jit(solution)/shard_map/ppermute | solution.py:32
  110.0 2.5 %collective-permute-done.37 = bf16[384,256]{1,0:T(8,128)(2,1)S(1)} collective-permute-done((bf16[384,256]{1,0:T(8,128)(2,1)S(1)}, bf16[384,256]{1,0:T(8,128)(2,1)S(1)}, u32[]{:S(2)}, u32[]{:S(2)}) %collective-permute-start.37) | collective-permute-done | bytes 196640 | tf_op jit(solution)/shard_map/ppermute | solution.py:32
  112.5 1.7 %collective-permute-start.38 = (bf16[384,256]{1,0:T(8,128)(2,1)S(1)}, bf16[384,256]{1,0:T(8,128)(2,1)S(1)}, u32[]{:S(2)}, u32[]{:S(2)}) collective-permute-start(bf16[384,256]{1,0:T(8,128)(2,1)S(1)} %fusion), channel_id=1, source_target_pairs={{0,4},{1,5},{2,6},{3,7},{4,0},{5,1},{6,2},{7,3},{8,12},{9,13},{10,... | collective-permute-start | bytes 589832 | tf_op jit(solution)/shard_map/ppermute | solution.py:32
  114.2 6.5 %collective-permute-done.33 = bf16[256,256]{1,0:T(8,128)(2,1)S(1)} collective-permute-done((bf16[256,256]{1,0:T(8,128)(2,1)S(1)}, bf16[256,256]{1,0:T(8,128)(2,1)S(1)}, u32[]{:S(2)}, u32[]{:S(2)}) %collective-permute-start.33) | collective-permute-done | bytes 131104 | tf_op jit(solution)/shard_map/ppermute | solution.py:32
  121.4 1.2 collective-permute-done.44
  122.8 1.6 %collective-permute-start.45 = (bf16[384,256]{1,0:T(8,128)(2,1)S(1)}, bf16[384,256]{1,0:T(8,128)(2,1)S(1)}, u32[]{:S(2)}, u32[]{:S(2)}) collective-permute-start(bf16[384,256]{1,0:T(8,128)(2,1)S(1)} %slice.72), channel_id=1, source_target_pairs={{0,2},{1,3},{2,0},{3,1},{4,6},{5,7},{6,4},{7,5},{8,10},{9,11},{10,... | collective-permute-start | bytes 589832 | tf_op jit(solution)/shard_map/ppermute | solution.py:32
  125.0 6.6 %collective-permute-done.45 = bf16[384,256]{1,0:T(8,128)(2,1)S(1)} collective-permute-done((bf16[384,256]{1,0:T(8,128)(2,1)S(1)}, bf16[384,256]{1,0:T(8,128)(2,1)S(1)}, u32[]{:S(2)}, u32[]{:S(2)}) %collective-permute-start.45) | collective-permute-done | bytes 196640 | tf_op jit(solution)/shard_map/ppermute | solution.py:32
  131.6 1.7 %collective-permute-start.46 = (bf16[384,256]{1,0:T(8,128)(2,1)S(1)}, bf16[384,256]{1,0:T(8,128)(2,1)S(1)}, u32[]{:S(2)}, u32[]{:S(2)}) collective-permute-start(bf16[384,256]{1,0:T(8,128)(2,1)S(1)} %fusion.1), channel_id=1, source_target_pairs={{0,4},{1,5},{2,6},{3,7},{4,0},{5,1},{6,2},{7,3},{8,12},{9,13},{10,... | collective-permute-start | bytes 589832 | tf_op jit(solution)/shard_map/ppermute | solution.py:32
  133.9 2.9 %collective-permute-done.39.refs_5_ = bf16[384,256]{1,0:T(8,128)(2,1)S(1)} collective-permute-done((bf16[384,256]{1,0:T(8,128)(2,1)S(1)}, bf16[384,256]{1,0:T(8,128)(2,1)S(1)}, u32[]{:S(2)}, u32[]{:S(2)}) %collective-permute-start.39) | collective-permute-done | bytes 196640 | tf_op jit(solution)/shard_map/ppermute | solution.py:32
  136.8 4.8 %collective-permute-done.46 = bf16[384,256]{1,0:T(8,128)(2,1)S(1)} collective-permute-done((bf16[384,256]{1,0:T(8,128)(2,1)S(1)}, bf16[384,256]{1,0:T(8,128)(2,1)S(1)}, u32[]{:S(2)}, u32[]{:S(2)}) %collective-permute-start.46) | collective-permute-done | bytes 196640 | tf_op jit(solution)/shard_map/ppermute | solution.py:32
  141.9 2.2 %assemble.2 = (f32[4096,128]{1,0:T(8,128)}, f32[4096,128]{1,0:T(8,128)}) custom-call(s32[3]{0:T(128)S(1)} %pad_add_fusion.ids, bf16[256,256]{1,0:T(8,128)(2,1)S(1)} %add_convert_fusion.2.refs_0_, bf16[256,256]{1,0:T(8,128)(2,1)S(1)} %collective-permute-done.34.refs_1_, bf16[256,256]{1,0:T(8,128)(2,1)S(1)} %collective-permute-done.35.refs_2_, ...), custom_call_target="tpu_custom_call" | custom-call | tf_op jit(solution)/shard_map/assemble/pallas_call | solution.py:394
  144.1 3.4 %collective-permute-done.47.refs_3_ = bf16[384,256]{1,0:T(8,128)(2,1)S(1)} collective-permute-done((bf16[384,256]{1,0:T(8,128)(2,1)S(1)}, bf16[384,256]{1,0:T(8,128)(2,1)S(1)}, u32[]{:S(2)}, u32[]{:S(2)}) %collective-permute-start.47) | collective-permute-done | bytes 196640 | tf_op jit(solution)/shard_map/ppermute | solution.py:32
  147.5 1.4 collective-permute-done.49.refs_5_
  148.9 1.8 %assemble.3 = (f32[4096,128]{1,0:T(8,128)}, f32[4096,128]{1,0:T(8,128)}) custom-call(s32[3]{0:T(128)S(1)} %pad_add_fusion.ids, f32[4096,128]{1,0:T(8,128)} %get-tuple-element.90.refs_0_, f32[4096,128]{1,0:T(8,128)} %get-tuple-element.91.refs_1_, bf16[384,256]{1,0:T(8,128)(2,1)S(1)} %add_convert_fusion.refs_2_, ...), custom_call_target="tpu_custom_call", output_to_operand_aliasing={{0}: (1, {}), {1}: (2, {})} | custom-call | tf_op jit(solution)/shard_map/assemble/pallas_call | solution.py:394
  (99 shorter events, 17.1 us)
Async XLA Ops:
  2.9 15.9 %collective-permute-start = (bf16[1024,256]{1,0:T(8,128)(2,1)}, bf16[1024,256]{1,0:T(8,128)(2,1)S(1)}, u32[]{:S(2)}, u32[]{:S(2)}) collective-permute-start(bf16[1024,256]{1,0:T(8,128)(2,1)} %pad_maximum_fusion), channel_id=1, source_target_pairs={{0,8},{8,0},{16,24},{24,16},{1,9},{9,1},{17,25},{25,17},{2,10},{10... | collective-permute-start | bytes 1572872 | tf_op jit(solution)/shard_map/ppermute | solution.py:32
  6.7 15.1 %collective-permute-start.2 = (bf16[1024,256]{1,0:T(8,128)(2,1)}, bf16[1024,256]{1,0:T(8,128)(2,1)S(1)}, u32[]{:S(2)}, u32[]{:S(2)}) collective-permute-start(bf16[1024,256]{1,0:T(8,128)(2,1)} %pad_maximum_fusion.1), channel_id=1, source_target_pairs={{0,16},{8,24},{16,0},{24,8},{1,17},{9,25},{17,1},{25,9},{2,18},{10... | collective-permute-start | bytes 1572872 | tf_op jit(solution)/shard_map/ppermute | solution.py:32
  8.2 24.9 %collective-permute-start.5 = (bf16[1024,256]{1,0:T(8,128)(2,1)}, bf16[1024,256]{1,0:T(8,128)(2,1)}, u32[]{:S(2)}, u32[]{:S(2)}) collective-permute-start(bf16[1024,256]{1,0:T(8,128)(2,1)} %pad_maximum_fusion), channel_id=1, source_target_pairs={{0,16},{8,24},{16,0},{24,8},{1,17},{9,25},{17,1},{25,9},{2,18},{10... | collective-permute-start | bytes 1572872 | tf_op jit(solution)/shard_map/ppermute | solution.py:32
  8.7 24.4 %collective-permute-start.1 = (bf16[1024,256]{1,0:T(8,128)(2,1)}, bf16[1024,256]{1,0:T(8,128)(2,1)}, u32[]{:S(2)}, u32[]{:S(2)}) collective-permute-start(bf16[1024,256]{1,0:T(8,128)(2,1)} %pad_maximum_fusion.1), channel_id=1, source_target_pairs={{0,8},{8,0},{16,24},{24,16},{1,9},{9,1},{17,25},{25,17},{2,10},{10... | collective-permute-start | bytes 1572872 | tf_op jit(solution)/shard_map/ppermute | solution.py:32
  21.8 11.9 %collective-permute-start.3 = (bf16[1024,256]{1,0:T(8,128)(2,1)S(1)}, bf16[1024,256]{1,0:T(8,128)(2,1)}, u32[]{:S(2)}, u32[]{:S(2)}) collective-permute-start(bf16[1024,256]{1,0:T(8,128)(2,1)S(1)} %collective-permute-done.refs_2_), channel_id=1, source_target_pairs={{0,1},{1,0},{2,3},{3,2},{4,5},{5,4},{6,7},{7,6},{8,9},{9,8},{10,11... | collective-permute-start | bytes 1572872 | tf_op jit(solution)/shard_map/ppermute | solution.py:32
  21.8 21.0 %collective-permute-start.8 = (bf16[1024,256]{1,0:T(8,128)(2,1)S(1)}, bf16[1024,256]{1,0:T(8,128)(2,1)S(1)}, u32[]{:S(2)}, u32[]{:S(2)}) collective-permute-start(bf16[1024,256]{1,0:T(8,128)(2,1)S(1)} %collective-permute-done.refs_2_), channel_id=1, source_target_pairs={{0,16},{8,24},{16,0},{24,8},{1,17},{9,25},{17,1},{25,9},{2,18},{10... | collective-permute-start | bytes 1572872 | tf_op jit(solution)/shard_map/ppermute | solution.py:32
  23.3 19.5 %collective-permute-start.9 = (bf16[1024,256]{1,0:T(8,128)(2,1)S(1)}, bf16[1024,256]{1,0:T(8,128)(2,1)S(1)}, u32[]{:S(2)}, u32[]{:S(2)}) collective-permute-start(bf16[1024,256]{1,0:T(8,128)(2,1)S(1)} %collective-permute-done.2.refs_7_), channel_id=1, source_target_pairs={{0,8},{8,0},{16,24},{24,16},{1,9},{9,1},{17,25},{25,17},{2,10},{10... | collective-permute-start | bytes 1572872 | tf_op jit(solution)/shard_map/ppermute | solution.py:32
  33.1 3.2 %collective-permute-start.6 = (bf16[1024,256]{1,0:T(8,128)(2,1)}, bf16[1024,256]{1,0:T(8,128)(2,1)S(1)}, u32[]{:S(2)}, u32[]{:S(2)}) collective-permute-start(bf16[1024,256]{1,0:T(8,128)(2,1)} %collective-permute-done.5.refs_6_), channel_id=1, source_target_pairs={{0,1},{1,0},{2,3},{3,2},{4,5},{5,4},{6,7},{7,6},{8,9},{9,8},{10,11... | collective-permute-start | bytes 1572872 | tf_op jit(solution)/shard_map/ppermute | solution.py:32
  33.1 3.6 %collective-permute-start.4 = (bf16[1024,256]{1,0:T(8,128)(2,1)}, bf16[1024,256]{1,0:T(8,128)(2,1)S(1)}, u32[]{:S(2)}, u32[]{:S(2)}) collective-permute-start(bf16[1024,256]{1,0:T(8,128)(2,1)} %collective-permute-done.1.refs_3_), channel_id=1, source_target_pairs={{0,1},{1,0},{2,3},{3,2},{4,5},{5,4},{6,7},{7,6},{8,9},{9,8},{10,11... | collective-permute-start | bytes 1572872 | tf_op jit(solution)/shard_map/ppermute | solution.py:32
  33.6 3.1 %collective-permute-start.7 = (bf16[1024,256]{1,0:T(8,128)(2,1)S(1)}, bf16[1024,256]{1,0:T(8,128)(2,1)S(1)}, u32[]{:S(2)}, u32[]{:S(2)}) collective-permute-start(bf16[1024,256]{1,0:T(8,128)(2,1)S(1)} %collective-permute-done.2.refs_7_), channel_id=1, source_target_pairs={{0,1},{1,0},{2,3},{3,2},{4,5},{5,4},{6,7},{7,6},{8,9},{9,8},{10,11... | collective-permute-start | bytes 1572872 | tf_op jit(solution)/shard_map/ppermute | solution.py:32
  42.8 2.1 %collective-permute-start.10 = (bf16[1024,256]{1,0:T(8,128)(2,1)S(1)}, bf16[1024,256]{1,0:T(8,128)(2,1)S(1)}, u32[]{:S(2)}, u32[]{:S(2)}) collective-permute-start(bf16[1024,256]{1,0:T(8,128)(2,1)S(1)} %collective-permute-done.8.refs_1_), channel_id=1, source_target_pairs={{0,1},{1,0},{2,3},{3,2},{4,5},{5,4},{6,7},{7,6},{8,9},{9,8},{10,11... | collective-permute-start | bytes 1572872 | tf_op jit(solution)/shard_map/ppermute | solution.py:32
  42.9 2.6 %collective-permute-start.11 = (bf16[1024,256]{1,0:T(8,128)(2,1)S(1)}, bf16[1024,256]{1,0:T(8,128)(2,1)S(1)}, u32[]{:S(2)}, u32[]{:S(2)}) collective-permute-start(bf16[1024,256]{1,0:T(8,128)(2,1)S(1)} %collective-permute-done.9.refs_2_), channel_id=1, source_target_pairs={{0,1},{1,0},{2,3},{3,2},{4,5},{5,4},{6,7},{7,6},{8,9},{9,8},{10,11... | collective-permute-start | bytes 1572872 | tf_op jit(solution)/shard_map/ppermute | solution.py:32
  43.4 28.7 %collective-permute-start.20 = (bf16[192,2560]{1,0:T(8,128)(2,1)S(1)}, bf16[192,2560]{1,0:T(8,128)(2,1)S(1)}, u32[]{:S(2)}, u32[]{:S(2)}) collective-permute-start(bf16[192,2560]{1,0:T(8,128)(2,1)S(1)} %get-tuple-element.67), channel_id=1, source_target_pairs={{0,16},{8,24},{16,0},{24,8},{1,17},{9,25},{17,1},{25,9},{2,18},{10... | collective-permute-start | bytes 2949128 | tf_op jit(solution)/shard_map/ppermute | solution.py:32
  44.9 27.2 %collective-permute-start.19 = (bf16[192,2560]{1,0:T(8,128)(2,1)S(1)}, bf16[192,2560]{1,0:T(8,128)(2,1)S(1)}, u32[]{:S(2)}, u32[]{:S(2)}) collective-permute-start(bf16[192,2560]{1,0:T(8,128)(2,1)S(1)} %get-tuple-element.66), channel_id=1, source_target_pairs={{0,8},{8,0},{16,24},{24,16},{1,9},{9,1},{17,25},{25,17},{2,10},{10... | collective-permute-start | bytes 2949128 | tf_op jit(solution)/shard_map/ppermute | solution.py:32
  46.7 7.6 %collective-permute-start.14 = (bf16[192,256]{1,0:T(8,128)(2,1)S(1)}, bf16[192,256]{1,0:T(8,128)(2,1)S(1)}, u32[]{:S(2)}, u32[]{:S(2)}) collective-permute-start(bf16[192,256]{1,0:T(8,128)(2,1)S(1)} %project.3.refs_0_), channel_id=1, source_target_pairs={{0,6},{1,7},{2,4},{3,5},{4,2},{5,3},{6,0},{7,1},{8,14},{9,15},{10,... | collective-permute-start | bytes 294920 | tf_op jit(solution)/shard_map/ppermute | solution.py:32
  50.3 8.6 %collective-permute-start.13 = (bf16[192,256]{1,0:T(8,128)(2,1)S(1)}, bf16[192,256]{1,0:T(8,128)(2,1)S(1)}, u32[]{:S(2)}, u32[]{:S(2)}) collective-permute-start(bf16[192,256]{1,0:T(8,128)(2,1)S(1)} %project.3.refs_0_), channel_id=1, source_target_pairs={{0,4},{1,5},{2,6},{3,7},{4,0},{5,1},{6,2},{7,3},{8,12},{9,13},{10,... | collective-permute-start | bytes 294920 | tf_op jit(solution)/shard_map/ppermute | solution.py:32
  50.4 8.6 %collective-permute-start.12 = (bf16[192,256]{1,0:T(8,128)(2,1)S(1)}, bf16[192,256]{1,0:T(8,128)(2,1)S(1)}, u32[]{:S(2)}, u32[]{:S(2)}) collective-permute-start(bf16[192,256]{1,0:T(8,128)(2,1)S(1)} %project.3.refs_0_), channel_id=1, source_target_pairs={{0,2},{1,3},{2,0},{3,1},{4,6},{5,7},{6,4},{7,5},{8,10},{9,11},{10,... | collective-permute-start | bytes 294920 | tf_op jit(solution)/shard_map/ppermute | solution.py:32
  58.9 32.5 %collective-permute-start.26 = (bf16[192,2560]{1,0:T(8,128)(2,1)S(1)}, bf16[192,2560]{1,0:T(8,128)(2,1)S(1)}, u32[]{:S(2)}, u32[]{:S(2)}) collective-permute-start(bf16[192,2560]{1,0:T(8,128)(2,1)S(1)} %get-tuple-element.77), channel_id=1, source_target_pairs={{0,24},{8,16},{16,8},{24,0},{1,25},{9,17},{17,9},{25,1},{2,26},{10... | collective-permute-start | bytes 2949128 | tf_op jit(solution)/shard_map/ppermute | solution.py:32
  60.9 1.5 collective-permute-start.16
  62.3 1.3 collective-permute-start.18
  72.1 1.7 %collective-permute-start.21 = (bf16[768,256]{1,0:T(8,128)(2,1)S(1)}, bf16[768,256]{1,0:T(8,128)(2,1)S(1)}, u32[]{:S(2)}, u32[]{:S(2)}) collective-permute-start(bf16[768,256]{1,0:T(8,128)(2,1)S(1)} %get-tuple-element.71), channel_id=1, source_target_pairs={{0,1},{1,0},{2,3},{3,2},{4,5},{5,4},{6,7},{7,6},{8,9},{9,8},{10,11... | collective-permute-start | bytes 1179656 | tf_op jit(solution)/shard_map/ppermute | solution.py:32
  73.9 6.6 %collective-permute-start.22 = (bf16[192,256]{1,0:T(8,128)(2,1)S(1)}, bf16[192,256]{1,0:T(8,128)(2,1)S(1)}, u32[]{:S(2)}, u32[]{:S(2)}) collective-permute-start(bf16[192,256]{1,0:T(8,128)(2,1)S(1)} %get-tuple-element.73), channel_id=1, source_target_pairs={{0,2},{1,3},{2,0},{3,1},{4,6},{5,7},{6,4},{7,5},{8,10},{9,11},{10,... | collective-permute-start | bytes 294920 | tf_op jit(solution)/shard_map/ppermute | solution.py:32
  74.5 10.8 %collective-permute-start.23 = (bf16[192,256]{1,0:T(8,128)(2,1)S(1)}, bf16[192,256]{1,0:T(8,128)(2,1)S(1)}, u32[]{:S(2)}, u32[]{:S(2)}) collective-permute-start(bf16[192,256]{1,0:T(8,128)(2,1)S(1)} %get-tuple-element.74), channel_id=1, source_target_pairs={{0,4},{1,5},{2,6},{3,7},{4,0},{5,1},{6,2},{7,3},{8,12},{9,13},{10,... | collective-permute-start | bytes 294920 | tf_op jit(solution)/shard_map/ppermute | solution.py:32
  77.1 8.3 %collective-permute-start.24 = (bf16[192,256]{1,0:T(8,128)(2,1)S(1)}, bf16[192,256]{1,0:T(8,128)(2,1)S(1)}, u32[]{:S(2)}, u32[]{:S(2)}) collective-permute-start(bf16[192,256]{1,0:T(8,128)(2,1)S(1)} %get-tuple-element.75), channel_id=1, source_target_pairs={{0,6},{1,7},{2,4},{3,5},{4,2},{5,3},{6,0},{7,1},{8,14},{9,15},{10,... | collective-permute-start | bytes 294920 | tf_op jit(solution)/shard_map/ppermute | solution.py:32
  85.4 7.3 %collective-permute-start.25 = (bf16[192,256]{1,0:T(8,128)(2,1)S(1)}, bf16[192,256]{1,0:T(8,128)(2,1)S(1)}, u32[]{:S(2)}, u32[]{:S(2)}) collective-permute-start(bf16[192,256]{1,0:T(8,128)(2,1)S(1)} %total.1.refs_4_.refs_1_), channel_id=1, source_target_pairs={{0,8},{8,0},{16,24},{24,16},{1,9},{9,1},{17,25},{25,17},{2,10},{10... | collective-permute-start | bytes 294920 | tf_op jit(solution)/shard_map/ppermute | solution.py:32
  86.5 8.4 %collective-permute-start.28 = (bf16[192,256]{1,0:T(8,128)(2,1)S(1)}, bf16[192,256]{1,0:T(8,128)(2,1)S(1)}, u32[]{:S(2)}, u32[]{:S(2)}) collective-permute-start(bf16[192,256]{1,0:T(8,128)(2,1)S(1)} %total.1.refs_4_.refs_1_), channel_id=1, source_target_pairs={{0,24},{8,16},{16,8},{24,0},{1,25},{9,17},{17,9},{25,1},{2,26},{10... | collective-permute-start | bytes 294920 | tf_op jit(solution)/shard_map/ppermute | solution.py:32
  87.4 7.4 %collective-permute-start.27 = (bf16[192,256]{1,0:T(8,128)(2,1)S(1)}, bf16[192,256]{1,0:T(8,128)(2,1)S(1)}, u32[]{:S(2)}, u32[]{:S(2)}) collective-permute-start(bf16[192,256]{1,0:T(8,128)(2,1)S(1)} %total.1.refs_4_.refs_1_), channel_id=1, source_target_pairs={{0,16},{8,24},{16,0},{24,8},{1,17},{9,25},{17,1},{25,9},{2,18},{10... | collective-permute-start | bytes 294920 | tf_op jit(solution)/shard_map/ppermute | solution.py:32
  94.9 5.4 %collective-permute-start.31 = (bf16[3072,256]{1,0:T(8,128)(2,1)S(1)}, bf16[3072,256]{1,0:T(8,128)(2,1)S(1)}, u32[]{:S(2)}, u32[]{:S(2)}) collective-permute-start(bf16[3072,256]{1,0:T(8,128)(2,1)S(1)} %get-tuple-element.87), channel_id=1, source_target_pairs={{0,1},{1,0},{2,3},{3,2},{4,5},{5,4},{6,7},{7,6},{8,9},{9,8},{10,11... | collective-permute-start | bytes 4718600 | tf_op jit(solution)/shard_map/ppermute | solution.py:32
  96.2 2.5 %collective-permute-start.29 = (bf16[512,256]{1,0:T(8,128)(2,1)S(1)}, bf16[512,256]{1,0:T(8,128)(2,1)S(1)}, u32[]{:S(2)}, u32[]{:S(2)}) collective-permute-start(bf16[512,256]{1,0:T(8,128)(2,1)S(1)} %get-tuple-element.81), channel_id=1, source_target_pairs={{0,1},{1,0},{2,3},{3,2},{4,5},{5,4},{6,7},{7,6},{8,9},{9,8},{10,11... | collective-permute-start | bytes 786440 | tf_op jit(solution)/shard_map/ppermute | solution.py:32
  98.4 1.8 %collective-permute-start.30 = (bf16[768,256]{1,0:T(8,128)(2,1)S(1)}, bf16[768,256]{1,0:T(8,128)(2,1)S(1)}, u32[]{:S(2)}, u32[]{:S(2)}) collective-permute-start(bf16[768,256]{1,0:T(8,128)(2,1)S(1)} %get-tuple-element.83), channel_id=1, source_target_pairs={{0,1},{1,0},{2,3},{3,2},{4,5},{5,4},{6,7},{7,6},{8,9},{9,8},{10,11... | collective-permute-start | bytes 1179656 | tf_op jit(solution)/shard_map/ppermute | solution.py:32
  101.0 6.4 %collective-permute-start.32 = (bf16[256,256]{1,0:T(8,128)(2,1)S(1)}, bf16[256,256]{1,0:T(8,128)(2,1)S(1)}, u32[]{:S(2)}, u32[]{:S(2)}) collective-permute-start(bf16[256,256]{1,0:T(8,128)(2,1)S(1)} %slice.74), channel_id=1, source_target_pairs={{0,2},{1,3},{2,0},{3,1},{4,6},{5,7},{6,4},{7,5},{8,10},{9,11},{10,... | collective-permute-start | bytes 393224 | tf_op jit(solution)/shard_map/ppermute | solution.py:32
  102.6 9.9 %collective-permute-start.37 = (bf16[384,256]{1,0:T(8,128)(2,1)S(1)}, bf16[384,256]{1,0:T(8,128)(2,1)S(1)}, u32[]{:S(2)}, u32[]{:S(2)}) collective-permute-start(bf16[384,256]{1,0:T(8,128)(2,1)S(1)} %slice.73), channel_id=1, source_target_pairs={{0,2},{1,3},{2,0},{3,1},{4,6},{5,7},{6,4},{7,5},{8,10},{9,11},{10,... | collective-permute-start | bytes 589832 | tf_op jit(solution)/shard_map/ppermute | solution.py:32
  103.1 18.3 %collective-permute-start.42 = (bf16[768,256]{1,0:T(8,128)(2,1)S(1)}, bf16[768,256]{1,0:T(8,128)(2,1)S(1)}, u32[]{:S(2)}, u32[]{:S(2)}) collective-permute-start(bf16[768,256]{1,0:T(8,128)(2,1)S(1)} %get-tuple-element.93), channel_id=1, source_target_pairs={{0,8},{8,0},{16,24},{24,16},{1,9},{9,1},{17,25},{25,17},{2,10},{10... | collective-permute-start | bytes 1179656 | tf_op jit(solution)/shard_map/ppermute | solution.py:32
  103.6 17.8 %collective-permute-start.43 = (bf16[768,256]{1,0:T(8,128)(2,1)S(1)}, bf16[768,256]{1,0:T(8,128)(2,1)S(1)}, u32[]{:S(2)}, u32[]{:S(2)}) collective-permute-start(bf16[768,256]{1,0:T(8,128)(2,1)S(1)} %get-tuple-element.94), channel_id=1, source_target_pairs={{0,16},{8,24},{16,0},{24,8},{1,17},{9,25},{17,1},{25,9},{2,18},{10... | collective-permute-start | bytes 1179656 | tf_op jit(solution)/shard_map/ppermute | solution.py:32
  104.6 18.0 %collective-permute-start.44 = (bf16[768,256]{1,0:T(8,128)(2,1)S(1)}, bf16[768,256]{1,0:T(8,128)(2,1)S(1)}, u32[]{:S(2)}, u32[]{:S(2)}) collective-permute-start(bf16[768,256]{1,0:T(8,128)(2,1)S(1)} %get-tuple-element.95), channel_id=1, source_target_pairs={{0,24},{8,16},{16,8},{24,0},{1,25},{9,17},{17,9},{25,1},{2,26},{10... | collective-permute-start | bytes 1179656 | tf_op jit(solution)/shard_map/ppermute | solution.py:32
  107.4 13.4 %collective-permute-start.33 = (bf16[256,256]{1,0:T(8,128)(2,1)S(1)}, bf16[256,256]{1,0:T(8,128)(2,1)S(1)}, u32[]{:S(2)}, u32[]{:S(2)}) collective-permute-start(bf16[256,256]{1,0:T(8,128)(2,1)S(1)} %fusion.2), channel_id=1, source_target_pairs={{0,4},{1,5},{2,6},{3,7},{4,0},{5,1},{6,2},{7,3},{8,12},{9,13},{10,... | collective-permute-start | bytes 393224 | tf_op jit(solution)/shard_map/ppermute | solution.py:32
  112.5 12.1 %collective-permute-start.38 = (bf16[384,256]{1,0:T(8,128)(2,1)S(1)}, bf16[384,256]{1,0:T(8,128)(2,1)S(1)}, u32[]{:S(2)}, u32[]{:S(2)}) collective-permute-start(bf16[384,256]{1,0:T(8,128)(2,1)S(1)} %fusion), channel_id=1, source_target_pairs={{0,4},{1,5},{2,6},{3,7},{4,0},{5,1},{6,2},{7,3},{8,12},{9,13},{10,... | collective-permute-start | bytes 589832 | tf_op jit(solution)/shard_map/ppermute | solution.py:32
  120.8 12.6 %collective-permute-start.34 = (bf16[256,256]{1,0:T(8,128)(2,1)S(1)}, bf16[256,256]{1,0:T(8,128)(2,1)S(1)}, u32[]{:S(2)}, u32[]{:S(2)}) collective-permute-start(bf16[256,256]{1,0:T(8,128)(2,1)S(1)} %add_convert_fusion.2.refs_0_), channel_id=1, source_target_pairs={{0,2},{1,3},{2,0},{3,1},{4,6},{5,7},{6,4},{7,5},{8,10},{9,11},{10,... | collective-permute-start | bytes 393224 | tf_op jit(solution)/shard_map/ppermute | solution.py:32
  122.8 8.8 %collective-permute-start.45 = (bf16[384,256]{1,0:T(8,128)(2,1)S(1)}, bf16[384,256]{1,0:T(8,128)(2,1)S(1)}, u32[]{:S(2)}, u32[]{:S(2)}) collective-permute-start(bf16[384,256]{1,0:T(8,128)(2,1)S(1)} %slice.72), channel_id=1, source_target_pairs={{0,2},{1,3},{2,0},{3,1},{4,6},{5,7},{6,4},{7,5},{8,10},{9,11},{10,... | collective-permute-start | bytes 589832 | tf_op jit(solution)/shard_map/ppermute | solution.py:32
  124.7 12.1 %collective-permute-start.39 = (bf16[384,256]{1,0:T(8,128)(2,1)S(1)}, bf16[384,256]{1,0:T(8,128)(2,1)S(1)}, u32[]{:S(2)}, u32[]{:S(2)}) collective-permute-start(bf16[384,256]{1,0:T(8,128)(2,1)S(1)} %add_convert_fusion.1.refs_4_), channel_id=1, source_target_pairs={{0,2},{1,3},{2,0},{3,1},{4,6},{5,7},{6,4},{7,5},{8,10},{9,11},{10,... | collective-permute-start | bytes 589832 | tf_op jit(solution)/shard_map/ppermute | solution.py:32
  131.6 10.0 %collective-permute-start.46 = (bf16[384,256]{1,0:T(8,128)(2,1)S(1)}, bf16[384,256]{1,0:T(8,128)(2,1)S(1)}, u32[]{:S(2)}, u32[]{:S(2)}) collective-permute-start(bf16[384,256]{1,0:T(8,128)(2,1)S(1)} %fusion.1), channel_id=1, source_target_pairs={{0,4},{1,5},{2,6},{3,7},{4,0},{5,1},{6,2},{7,3},{8,12},{9,13},{10,... | collective-permute-start | bytes 589832 | tf_op jit(solution)/shard_map/ppermute | solution.py:32
  133.4 3.4 %collective-permute-start.35 = (bf16[256,256]{1,0:T(8,128)(2,1)S(1)}, bf16[256,256]{1,0:T(8,128)(2,1)S(1)}, u32[]{:S(2)}, u32[]{:S(2)}) collective-permute-start(bf16[256,256]{1,0:T(8,128)(2,1)S(1)} %add_convert_fusion.2.refs_0_), channel_id=1, source_target_pairs={{0,1},{1,0},{2,3},{3,2},{4,5},{5,4},{6,7},{7,6},{8,9},{9,8},{10,11... | collective-permute-start | bytes 393224 | tf_op jit(solution)/shard_map/ppermute | solution.py:32
  133.4 3.4 %collective-permute-start.36 = (bf16[256,256]{1,0:T(8,128)(2,1)S(1)}, bf16[256,256]{1,0:T(8,128)(2,1)S(1)}, u32[]{:S(2)}, u32[]{:S(2)}) collective-permute-start(bf16[256,256]{1,0:T(8,128)(2,1)S(1)} %collective-permute-done.34.refs_1_), channel_id=1, source_target_pairs={{0,1},{1,0},{2,3},{3,2},{4,5},{5,4},{6,7},{7,6},{8,9},{9,8},{10,11... | collective-permute-start | bytes 393224 | tf_op jit(solution)/shard_map/ppermute | solution.py:32
  133.9 8.0 %collective-permute-start.40 = (bf16[384,256]{1,0:T(8,128)(2,1)S(1)}, bf16[384,256]{1,0:T(8,128)(2,1)S(1)}, u32[]{:S(2)}, u32[]{:S(2)}) collective-permute-start(bf16[384,256]{1,0:T(8,128)(2,1)S(1)} %add_convert_fusion.1.refs_4_), channel_id=1, source_target_pairs={{0,1},{1,0},{2,3},{3,2},{4,5},{5,4},{6,7},{7,6},{8,9},{9,8},{10,11... | collective-permute-start | bytes 589832 | tf_op jit(solution)/shard_map/ppermute | solution.py:32
  136.8 5.1 %collective-permute-start.41 = (bf16[384,256]{1,0:T(8,128)(2,1)S(1)}, bf16[384,256]{1,0:T(8,128)(2,1)S(1)}, u32[]{:S(2)}, u32[]{:S(2)}) collective-permute-start(bf16[384,256]{1,0:T(8,128)(2,1)S(1)} %collective-permute-done.39.refs_5_), channel_id=1, source_target_pairs={{0,1},{1,0},{2,3},{3,2},{4,5},{5,4},{6,7},{7,6},{8,9},{9,8},{10,11... | collective-permute-start | bytes 589832 | tf_op jit(solution)/shard_map/ppermute | solution.py:32
  141.7 5.7 %collective-permute-start.47 = (bf16[384,256]{1,0:T(8,128)(2,1)S(1)}, bf16[384,256]{1,0:T(8,128)(2,1)S(1)}, u32[]{:S(2)}, u32[]{:S(2)}) collective-permute-start(bf16[384,256]{1,0:T(8,128)(2,1)S(1)} %add_convert_fusion.refs_2_), channel_id=1, source_target_pairs={{0,2},{1,3},{2,0},{3,1},{4,6},{5,7},{6,4},{7,5},{8,10},{9,11},{10,... | collective-permute-start | bytes 589832 | tf_op jit(solution)/shard_map/ppermute | solution.py:32
  141.8 5.7 %collective-permute-start.48 = (bf16[384,256]{1,0:T(8,128)(2,1)S(1)}, bf16[384,256]{1,0:T(8,128)(2,1)S(1)}, u32[]{:S(2)}, u32[]{:S(2)}) collective-permute-start(bf16[384,256]{1,0:T(8,128)(2,1)S(1)} %add_convert_fusion.refs_2_), channel_id=1, source_target_pairs={{0,1},{1,0},{2,3},{3,2},{4,5},{5,4},{6,7},{7,6},{8,9},{9,8},{10,11... | collective-permute-start | bytes 589832 | tf_op jit(solution)/shard_map/ppermute | solution.py:32
  147.5 1.4 collective-permute-start.49
  (10 other events, 133.1 us)

commit v18 on v17

--- a/solution.py
+++ b/solution.py
@@ -507,12 +507,9 @@
     grad = add_all([own] + [swap(one, "ctx", 2 * m) for m, one in enumerate(leaving, 1)])
     grads = [grad] + [swap(grad, "dp", j) for j in range(1, dp_count)]
 
-    (grad,), ended = after([grad], grads[near[0]], *[moved[j] for j in far])
-    grads[near[0]] = ended[0]
-    moved.update(zip(far, ended[1:]))
     groups = [[(0, j, 0, 0)] for j in range(dp_count)]
     ours, came = weight_rows(
-        ids, [inputs], [grad], groups, *regions[-1], block_rows, sub_count, grads[1:]
+        ids, [inputs], [grad], groups, *regions[-1], block_rows, sub_count, [*grads[1:], *[moved[j] for j in far]]
     )
     own = parts_over_dp(add_cores(ours, came))
     groups = [[(j, None, j, 0) for j in range(dp_count)]]

time: 151 us -> 151 us (level)
  no operation moved by 1% of the time
where the time goes in v18:
time: 151 us
  waiting for transfers between devices  78.4 us (52%)
  starting transfers between devices  41.8 us (28%)
  Pallas kernels  21.4 us (14%)
  local copies, waits for them, and re-layouts  5.14 us (3%)
  other arithmetic  2.92 us (2%)
    ppermute x50, waiting for transfers between devices, swap(): return lax.ppermute(array, axis, [(i, i ^ distance) for i in range(count)])  78.4 us
    ppermute x50, starting transfers between devices, swap(): return lax.ppermute(array, axis, [(i, i ^ distance) for i in range(count)])  41.8 us
    pallas_call x7, Pallas kernels, kernel_call(): pl.pallas_call(kernel, out_shape=outs, in_specs=[smem] * len(scalars) + [...  9.06 us
    pallas_call x1, Pallas kernels, attention(): pl.pallas_call(functools.partial(attention_kernel, shape), out_shape=(jax...  8.45 us
    pallas_call x2, Pallas kernels, assemble(): pl.pallas_call(functools.partial(assemble_kernel, sub_count, regions, not...  3.92 us
  transfers between devices with their start and end apart: 50, of which 29 were waited for; matrix products, arithmetic and copies ran while one was open for 3% of the time, Pallas kernels for 13%

profile of v18, /device:TPU:0, one launch (start us, length us, event | category | flops | bytes accessed | tf_op | source)
XLA Modules:
  0.0 150.8 jit_solution(13016612089792654992)
XLA Ops:
  0.7 1.4 constant_dynamic-slice_fusion
  2.9 2.9 %collective-permute-start = (bf16[1024,256]{1,0:T(8,128)(2,1)}, bf16[1024,256]{1,0:T(8,128)(2,1)S(1)}, u32[]{:S(2)}, u32[]{:S(2)}) collective-permute-start(bf16[1024,256]{1,0:T(8,128)(2,1)} %pad_maximum_fusion), channel_id=1, source_target_pairs={{0,8},{8,0},{16,24},{24,16},{1,9},{9,1},{17,25},{25,17},{2,10},{10... | collective-permute-start | bytes 1572872 | tf_op jit(solution)/shard_map/ppermute | solution.py:32
  6.7 1.5 %collective-permute-start.2 = (bf16[1024,256]{1,0:T(8,128)(2,1)}, bf16[1024,256]{1,0:T(8,128)(2,1)S(1)}, u32[]{:S(2)}, u32[]{:S(2)}) collective-permute-start(bf16[1024,256]{1,0:T(8,128)(2,1)} %pad_maximum_fusion.1), channel_id=1, source_target_pairs={{0,16},{8,24},{16,0},{24,8},{1,17},{9,25},{17,1},{25,9},{2,18},{10... | collective-permute-start | bytes 1572872 | tf_op jit(solution)/shard_map/ppermute | solution.py:32
  8.8 10.0 %collective-permute-done.refs_2_ = bf16[1024,256]{1,0:T(8,128)(2,1)S(1)} collective-permute-done((bf16[1024,256]{1,0:T(8,128)(2,1)}, bf16[1024,256]{1,0:T(8,128)(2,1)S(1)}, u32[]{:S(2)}, u32[]{:S(2)}) %collective-permute-start) | collective-permute-done | bytes 524320 | tf_op jit(solution)/shard_map/ppermute | solution.py:32
  18.8 3.0 %collective-permute-done.2.refs_7_ = bf16[1024,256]{1,0:T(8,128)(2,1)S(1)} collective-permute-done((bf16[1024,256]{1,0:T(8,128)(2,1)}, bf16[1024,256]{1,0:T(8,128)(2,1)S(1)}, u32[]{:S(2)}, u32[]{:S(2)}) %collective-permute-start.2) | collective-permute-done | bytes 524320 | tf_op jit(solution)/shard_map/ppermute | solution.py:32
  21.8 1.5 %collective-permute-start.8 = (bf16[1024,256]{1,0:T(8,128)(2,1)S(1)}, bf16[1024,256]{1,0:T(8,128)(2,1)S(1)}, u32[]{:S(2)}, u32[]{:S(2)}) collective-permute-start(bf16[1024,256]{1,0:T(8,128)(2,1)S(1)} %collective-permute-done.refs_2_), channel_id=1, source_target_pairs={{0,16},{8,24},{16,0},{24,8},{1,17},{9,25},{17,1},{25,9},{2,18},{10... | collective-permute-start | bytes 1572872 | tf_op jit(solution)/shard_map/ppermute | solution.py:32
  23.8 9.3 %collective-permute-done.5.refs_6_ = bf16[1024,256]{1,0:T(8,128)(2,1)} collective-permute-done((bf16[1024,256]{1,0:T(8,128)(2,1)}, bf16[1024,256]{1,0:T(8,128)(2,1)}, u32[]{:S(2)}, u32[]{:S(2)}) %collective-permute-start.5) | collective-permute-done | bytes 524320 | tf_op jit(solution)/shard_map/ppermute | solution.py:32
  33.8 2.5 %dynamic-slice_bitcast_fusion = (bf16[192,2560]{1,0:T(8,128)(2,1)S(1)}, bf16[192,2560]{1,0:T(8,128)(2,1)S(1)}, bf16[192,2560]{1,0:T(8,128)(2,1)S(1)}, bf16[192,2560]{1,0:T(8,128)(2,1)S(1)}) fusion(bf16[1,192,16384]{2,1,0:T(8,128)(2,1)} %param.7, s32[]{:T(128)S(6)} %select_n.42, s32[]{:T(128)S(6)} %select_n.40, s32[]{:T(128)S(6)} %select_n.39, s32[]{:T(128)S(6)} %select_n.41), kind=kLoop, calls=%fused_computation.1 | loop fusion | bytes 7864336 | tf_op jit(solution)/shard_map/dynamic_slice | solution.py:465
  37.8 3.2 %project.2.refs_0_ = f32[192,256]{1,0:T(8,128)S(1)} custom-call(s32[3]{0:T(128)S(1)} %pad_add_fusion.ids, bf16[192,16384]{1,0:T(8,128)(2,1)S(1)} %bitcast.19, bf16[4096,128]{1,0:T(8,128)(2,1)S(1)} %copy-done, bf16[4096,128]{1,0:T(8,128)(2,1)S(1)} %copy-done.1, bf16[1024,256]{1,0:T(8,128)(2,1)S(1)} %collective-permute-done.refs_2_, ...), custom_call_target="tpu_custom_call" | custom-call | bytes 16777216 | tf_op jit(solution)/shard_map/project/pallas_call | solution.py:48
  41.0 1.8 %collective-permute-done.8.refs_1_ = bf16[1024,256]{1,0:T(8,128)(2,1)S(1)} collective-permute-done((bf16[1024,256]{1,0:T(8,128)(2,1)S(1)}, bf16[1024,256]{1,0:T(8,128)(2,1)S(1)}, u32[]{:S(2)}, u32[]{:S(2)}) %collective-permute-start.8) | collective-permute-done | bytes 524320 | tf_op jit(solution)/shard_map/ppermute | solution.py:32
  43.4 1.5 %collective-permute-start.20 = (bf16[192,2560]{1,0:T(8,128)(2,1)S(1)}, bf16[192,2560]{1,0:T(8,128)(2,1)S(1)}, u32[]{:S(2)}, u32[]{:S(2)}) collective-permute-start(bf16[192,2560]{1,0:T(8,128)(2,1)S(1)} %get-tuple-element.64), channel_id=1, source_target_pairs={{0,16},{8,24},{16,0},{24,8},{1,17},{9,25},{17,1},{25,9},{2,18},{10... | collective-permute-start | bytes 2949128 | tf_op jit(solution)/shard_map/ppermute | solution.py:32
  45.5 1.1 project.3.refs_0_
  46.7 3.7 %collective-permute-start.14 = (bf16[192,256]{1,0:T(8,128)(2,1)S(1)}, bf16[192,256]{1,0:T(8,128)(2,1)S(1)}, u32[]{:S(2)}, u32[]{:S(2)}) collective-permute-start(bf16[192,256]{1,0:T(8,128)(2,1)S(1)} %project.3.refs_0_), channel_id=1, source_target_pairs={{0,6},{1,7},{2,4},{3,5},{4,2},{5,3},{6,0},{7,1},{8,14},{9,15},{10,... | collective-permute-start | bytes 294920 | tf_op jit(solution)/shard_map/ppermute | solution.py:32
  51.1 3.1 %collective-permute-done.14.refs_6_ = bf16[192,256]{1,0:T(8,128)(2,1)S(1)} collective-permute-done((bf16[192,256]{1,0:T(8,128)(2,1)S(1)}, bf16[192,256]{1,0:T(8,128)(2,1)S(1)}, u32[]{:S(2)}, u32[]{:S(2)}) %collective-permute-start.14) | collective-permute-done | bytes 98336 | tf_op jit(solution)/shard_map/ppermute | solution.py:32
  54.3 4.6 %collective-permute-done.13.refs_4_ = bf16[192,256]{1,0:T(8,128)(2,1)S(1)} collective-permute-done((bf16[192,256]{1,0:T(8,128)(2,1)S(1)}, bf16[192,256]{1,0:T(8,128)(2,1)S(1)}, u32[]{:S(2)}, u32[]{:S(2)}) %collective-permute-start.13) | collective-permute-done | bytes 98336 | tf_op jit(solution)/shard_map/ppermute | solution.py:32
  58.9 2.0 %collective-permute-start.21 = (bf16[192,2560]{1,0:T(8,128)(2,1)S(1)}, bf16[192,2560]{1,0:T(8,128)(2,1)S(1)}, u32[]{:S(2)}, u32[]{:S(2)}) collective-permute-start(bf16[192,2560]{1,0:T(8,128)(2,1)S(1)} %get-tuple-element.68), channel_id=1, source_target_pairs={{0,24},{8,16},{16,8},{24,0},{1,25},{9,17},{17,9},{25,1},{2,26},{10... | collective-permute-start | bytes 2949128 | tf_op jit(solution)/shard_map/ppermute | solution.py:32
  63.7 8.4 %attention.1 = (bf16[192,1024]{1,0:T(8,128)(2,1)}, f32[768,256]{1,0:T(8,128)S(1)}, bf16[768,256]{1,0:T(8,128)(2,1)S(1)}) custom-call(s32[1]{0:T(128)} %bitcast.ids, s32[16]{0:T(128)S(1)} %copy-done.4, s32[8]{0:T(128)S(1)} %bitcast.24, bf16[192,1024]{1,0:T(8,128)(2,1)S(1)} %bitcast.22, bf16[192,1024]{1,0:T(8,128)(2,1)S(1)} %bitcast.23, ...), custom_call_target="tpu_custom_call" | custom-call | tf_op jit(solution)/shard_map/attention/pallas_call | solution.py:171
  72.5 1.4 collective-permute-done.22.came
  74.5 2.6 %collective-permute-start.24 = (bf16[192,256]{1,0:T(8,128)(2,1)S(1)}, bf16[192,256]{1,0:T(8,128)(2,1)S(1)}, u32[]{:S(2)}, u32[]{:S(2)}) collective-permute-start(bf16[192,256]{1,0:T(8,128)(2,1)S(1)} %get-tuple-element.73), channel_id=1, source_target_pairs={{0,4},{1,5},{2,6},{3,7},{4,0},{5,1},{6,2},{7,3},{8,12},{9,13},{10,... | collective-permute-start | bytes 294920 | tf_op jit(solution)/shard_map/ppermute | solution.py:32
  77.1 1.3 collective-permute-start.25
  78.4 2.2 %collective-permute-done.23.refs_1_ = bf16[192,256]{1,0:T(8,128)(2,1)S(1)} collective-permute-done((bf16[192,256]{1,0:T(8,128)(2,1)S(1)}, bf16[192,256]{1,0:T(8,128)(2,1)S(1)}, u32[]{:S(2)}, u32[]{:S(2)}) %collective-permute-start.23) | collective-permute-done | bytes 98336 | tf_op jit(solution)/shard_map/ppermute | solution.py:32
  80.6 4.8 %collective-permute-done.24.refs_2_ = bf16[192,256]{1,0:T(8,128)(2,1)S(1)} collective-permute-done((bf16[192,256]{1,0:T(8,128)(2,1)S(1)}, bf16[192,256]{1,0:T(8,128)(2,1)S(1)}, u32[]{:S(2)}, u32[]{:S(2)}) %collective-permute-start.24) | collective-permute-done | bytes 98336 | tf_op jit(solution)/shard_map/ppermute | solution.py:32
  85.4 1.0 collective-permute-start.28
  86.4 1.5 %collective-permute-start.27 = (bf16[192,256]{1,0:T(8,128)(2,1)S(1)}, bf16[192,256]{1,0:T(8,128)(2,1)S(1)}, u32[]{:S(2)}, u32[]{:S(2)}) collective-permute-start(bf16[192,256]{1,0:T(8,128)(2,1)S(1)} %total.1.refs_4_.refs_1_), channel_id=1, source_target_pairs={{0,16},{8,24},{16,0},{24,8},{1,17},{9,25},{17,1},{25,9},{2,18},{10... | collective-permute-start | bytes 294920 | tf_op jit(solution)/shard_map/ppermute | solution.py:32
  88.0 1.0 collective-permute-start.26
  89.0 1.7 %weight_rows.5 = (bf16[3072,256]{1,0:T(8,128)(2,1)S(1)}, bf16[3072,256]{1,0:T(8,128)(2,1)S(1)}) custom-call(s32[3]{0:T(128)S(1)} %pad_add_fusion.ids, bf16[192,16384]{1,0:T(8,128)(2,1)S(1)} %bitcast.21, bf16[192,256]{1,0:T(8,128)(2,1)S(1)} %total.1.refs_4_.refs_1_), custom_call_target="tpu_custom_call" | custom-call | tf_op jit(solution)/shard_map/weight_rows/pallas_call | solution.py:48
  90.6 0.9 collective-permute-done.21.refs_3_
  91.5 2.1 %collective-permute-done.28.refs_7_ = bf16[192,256]{1,0:T(8,128)(2,1)S(1)} collective-permute-done((bf16[192,256]{1,0:T(8,128)(2,1)S(1)}, bf16[192,256]{1,0:T(8,128)(2,1)S(1)}, u32[]{:S(2)}, u32[]{:S(2)}) %collective-permute-start.28) | collective-permute-done | bytes 98336 | tf_op jit(solution)/shard_map/ppermute | solution.py:32
  93.6 1.3 collective-permute-done.27.refs_6_
  94.8 1.3 weight_rows.3
  96.7 1.6 %weight_rows.4 = (bf16[768,256]{1,0:T(8,128)(2,1)S(1)}, bf16[768,256]{1,0:T(8,128)(2,1)S(1)}) custom-call(s32[3]{0:T(128)S(1)} %pad_add_fusion.ids, bf16[192,2560]{1,0:T(8,128)(2,1)S(1)} %get-tuple-element.95.refs_0_, bf16[192,2560]{1,0:T(8,128)(2,1)S(1)} %collective-permute-done.19.refs_1_, bf16[192,2560]{1,0:T(8,128)(2,1)S(1)} %collective-permute-done.20.refs_2_, ...), custom_call_target="tpu_custom_call" | custom-call | tf_op jit(solution)/shard_map/weight_rows/pallas_call | solution.py:48
  98.7 1.4 collective-permute-done.30
  100.9 1.6 %collective-permute-start.32 = (bf16[256,256]{1,0:T(8,128)(2,1)S(1)}, bf16[256,256]{1,0:T(8,128)(2,1)S(1)}, u32[]{:S(2)}, u32[]{:S(2)}) collective-permute-start(bf16[256,256]{1,0:T(8,128)(2,1)S(1)} %slice.74), channel_id=1, source_target_pairs={{0,2},{1,3},{2,0},{3,1},{4,6},{5,7},{6,4},{7,5},{8,10},{9,11},{10,... | collective-permute-start | bytes 393224 | tf_op jit(solution)/shard_map/ppermute | solution.py:32
  104.2 2.4 %collective-permute-start.44 = (bf16[768,256]{1,0:T(8,128)(2,1)S(1)}, bf16[768,256]{1,0:T(8,128)(2,1)S(1)}, u32[]{:S(2)}, u32[]{:S(2)}) collective-permute-start(bf16[768,256]{1,0:T(8,128)(2,1)S(1)} %get-tuple-element.89), channel_id=1, source_target_pairs={{0,24},{8,16},{16,8},{24,0},{1,25},{9,17},{17,9},{25,1},{2,26},{10... | collective-permute-start | bytes 1179656 | tf_op jit(solution)/shard_map/ppermute | solution.py:32
  107.3 2.7 %collective-permute-start.33 = (bf16[256,256]{1,0:T(8,128)(2,1)S(1)}, bf16[256,256]{1,0:T(8,128)(2,1)S(1)}, u32[]{:S(2)}, u32[]{:S(2)}) collective-permute-start(bf16[256,256]{1,0:T(8,128)(2,1)S(1)} %fusion.2), channel_id=1, source_target_pairs={{0,4},{1,5},{2,6},{3,7},{4,0},{5,1},{6,2},{7,3},{8,12},{9,13},{10,... | collective-permute-start | bytes 393224 | tf_op jit(solution)/shard_map/ppermute | solution.py:32
  110.0 2.5 %collective-permute-done.37 = bf16[384,256]{1,0:T(8,128)(2,1)S(1)} collective-permute-done((bf16[384,256]{1,0:T(8,128)(2,1)S(1)}, bf16[384,256]{1,0:T(8,128)(2,1)S(1)}, u32[]{:S(2)}, u32[]{:S(2)}) %collective-permute-start.37) | collective-permute-done | bytes 196640 | tf_op jit(solution)/shard_map/ppermute | solution.py:32
  112.5 1.7 %collective-permute-start.38 = (bf16[384,256]{1,0:T(8,128)(2,1)S(1)}, bf16[384,256]{1,0:T(8,128)(2,1)S(1)}, u32[]{:S(2)}, u32[]{:S(2)}) collective-permute-start(bf16[384,256]{1,0:T(8,128)(2,1)S(1)} %fusion), channel_id=1, source_target_pairs={{0,4},{1,5},{2,6},{3,7},{4,0},{5,1},{6,2},{7,3},{8,12},{9,13},{10,... | collective-permute-start | bytes 589832 | tf_op jit(solution)/shard_map/ppermute | solution.py:32
  114.2 6.4 %collective-permute-done.33 = bf16[256,256]{1,0:T(8,128)(2,1)S(1)} collective-permute-done((bf16[256,256]{1,0:T(8,128)(2,1)S(1)}, bf16[256,256]{1,0:T(8,128)(2,1)S(1)}, u32[]{:S(2)}, u32[]{:S(2)}) %collective-permute-start.33) | collective-permute-done | bytes 131104 | tf_op jit(solution)/shard_map/ppermute | solution.py:32
  121.4 1.0 collective-permute-done.43
  122.6 1.6 %collective-permute-start.45 = (bf16[384,256]{1,0:T(8,128)(2,1)S(1)}, bf16[384,256]{1,0:T(8,128)(2,1)S(1)}, u32[]{:S(2)}, u32[]{:S(2)}) collective-permute-start(bf16[384,256]{1,0:T(8,128)(2,1)S(1)} %slice.72), channel_id=1, source_target_pairs={{0,2},{1,3},{2,0},{3,1},{4,6},{5,7},{6,4},{7,5},{8,10},{9,11},{10,... | collective-permute-start | bytes 589832 | tf_op jit(solution)/shard_map/ppermute | solution.py:32
  124.9 6.7 %collective-permute-done.45 = bf16[384,256]{1,0:T(8,128)(2,1)S(1)} collective-permute-done((bf16[384,256]{1,0:T(8,128)(2,1)S(1)}, bf16[384,256]{1,0:T(8,128)(2,1)S(1)}, u32[]{:S(2)}, u32[]{:S(2)}) %collective-permute-start.45) | collective-permute-done | bytes 196640 | tf_op jit(solution)/shard_map/ppermute | solution.py:32
  131.6 1.9 %collective-permute-start.46 = (bf16[384,256]{1,0:T(8,128)(2,1)S(1)}, bf16[384,256]{1,0:T(8,128)(2,1)S(1)}, u32[]{:S(2)}, u32[]{:S(2)}) collective-permute-start(bf16[384,256]{1,0:T(8,128)(2,1)S(1)} %fusion.1), channel_id=1, source_target_pairs={{0,4},{1,5},{2,6},{3,7},{4,0},{5,1},{6,2},{7,3},{8,12},{9,13},{10,... | collective-permute-start | bytes 589832 | tf_op jit(solution)/shard_map/ppermute | solution.py:32
  134.1 2.7 %collective-permute-done.39.refs_5_ = bf16[384,256]{1,0:T(8,128)(2,1)S(1)} collective-permute-done((bf16[384,256]{1,0:T(8,128)(2,1)S(1)}, bf16[384,256]{1,0:T(8,128)(2,1)S(1)}, u32[]{:S(2)}, u32[]{:S(2)}) %collective-permute-start.39) | collective-permute-done | bytes 196640 | tf_op jit(solution)/shard_map/ppermute | solution.py:32
  136.8 4.8 %collective-permute-done.46 = bf16[384,256]{1,0:T(8,128)(2,1)S(1)} collective-permute-done((bf16[384,256]{1,0:T(8,128)(2,1)S(1)}, bf16[384,256]{1,0:T(8,128)(2,1)S(1)}, u32[]{:S(2)}, u32[]{:S(2)}) %collective-permute-start.46) | collective-permute-done | bytes 196640 | tf_op jit(solution)/shard_map/ppermute | solution.py:32
  141.8 2.2 %assemble.2 = (f32[4096,128]{1,0:T(8,128)}, f32[4096,128]{1,0:T(8,128)}) custom-call(s32[3]{0:T(128)S(1)} %pad_add_fusion.ids, bf16[256,256]{1,0:T(8,128)(2,1)S(1)} %add_convert_fusion.2.refs_0_, bf16[256,256]{1,0:T(8,128)(2,1)S(1)} %collective-permute-done.34.refs_1_, bf16[256,256]{1,0:T(8,128)(2,1)S(1)} %collective-permute-done.35.refs_2_, ...), custom_call_target="tpu_custom_call" | custom-call | tf_op jit(solution)/shard_map/assemble/pallas_call | solution.py:394
  144.0 3.4 %collective-permute-done.47.refs_3_ = bf16[384,256]{1,0:T(8,128)(2,1)S(1)} collective-permute-done((bf16[384,256]{1,0:T(8,128)(2,1)S(1)}, bf16[384,256]{1,0:T(8,128)(2,1)S(1)}, u32[]{:S(2)}, u32[]{:S(2)}) %collective-permute-start.47) | collective-permute-done | bytes 196640 | tf_op jit(solution)/shard_map/ppermute | solution.py:32
  147.4 1.4 collective-permute-done.49.refs_5_
  148.8 1.8 %assemble.3 = (f32[4096,128]{1,0:T(8,128)}, f32[4096,128]{1,0:T(8,128)}) custom-call(s32[3]{0:T(128)S(1)} %pad_add_fusion.ids, f32[4096,128]{1,0:T(8,128)} %get-tuple-element.84.refs_0_, f32[4096,128]{1,0:T(8,128)} %get-tuple-element.85.refs_1_, bf16[384,256]{1,0:T(8,128)(2,1)S(1)} %add_convert_fusion.refs_2_, ...), custom_call_target="tpu_custom_call", output_to_operand_aliasing={{0}: (1, {}), {1}: (2, {})} | custom-call | tf_op jit(solution)/shard_map/assemble/pallas_call | solution.py:394
  (99 shorter events, 17.3 us)
Async XLA Ops:
  2.9 15.9 %collective-permute-start = (bf16[1024,256]{1,0:T(8,128)(2,1)}, bf16[1024,256]{1,0:T(8,128)(2,1)S(1)}, u32[]{:S(2)}, u32[]{:S(2)}) collective-permute-start(bf16[1024,256]{1,0:T(8,128)(2,1)} %pad_maximum_fusion), channel_id=1, source_target_pairs={{0,8},{8,0},{16,24},{24,16},{1,9},{9,1},{17,25},{25,17},{2,10},{10... | collective-permute-start | bytes 1572872 | tf_op jit(solution)/shard_map/ppermute | solution.py:32
  6.7 15.1 %collective-permute-start.2 = (bf16[1024,256]{1,0:T(8,128)(2,1)}, bf16[1024,256]{1,0:T(8,128)(2,1)S(1)}, u32[]{:S(2)}, u32[]{:S(2)}) collective-permute-start(bf16[1024,256]{1,0:T(8,128)(2,1)} %pad_maximum_fusion.1), channel_id=1, source_target_pairs={{0,16},{8,24},{16,0},{24,8},{1,17},{9,25},{17,1},{25,9},{2,18},{10... | collective-permute-start | bytes 1572872 | tf_op jit(solution)/shard_map/ppermute | solution.py:32
  8.2 24.9 %collective-permute-start.5 = (bf16[1024,256]{1,0:T(8,128)(2,1)}, bf16[1024,256]{1,0:T(8,128)(2,1)}, u32[]{:S(2)}, u32[]{:S(2)}) collective-permute-start(bf16[1024,256]{1,0:T(8,128)(2,1)} %pad_maximum_fusion), channel_id=1, source_target_pairs={{0,16},{8,24},{16,0},{24,8},{1,17},{9,25},{17,1},{25,9},{2,18},{10... | collective-permute-start | bytes 1572872 | tf_op jit(solution)/shard_map/ppermute | solution.py:32
  8.7 24.4 %collective-permute-start.1 = (bf16[1024,256]{1,0:T(8,128)(2,1)}, bf16[1024,256]{1,0:T(8,128)(2,1)}, u32[]{:S(2)}, u32[]{:S(2)}) collective-permute-start(bf16[1024,256]{1,0:T(8,128)(2,1)} %pad_maximum_fusion.1), channel_id=1, source_target_pairs={{0,8},{8,0},{16,24},{24,16},{1,9},{9,1},{17,25},{25,17},{2,10},{10... | collective-permute-start | bytes 1572872 | tf_op jit(solution)/shard_map/ppermute | solution.py:32
  21.8 11.9 %collective-permute-start.3 = (bf16[1024,256]{1,0:T(8,128)(2,1)S(1)}, bf16[1024,256]{1,0:T(8,128)(2,1)}, u32[]{:S(2)}, u32[]{:S(2)}) collective-permute-start(bf16[1024,256]{1,0:T(8,128)(2,1)S(1)} %collective-permute-done.refs_2_), channel_id=1, source_target_pairs={{0,1},{1,0},{2,3},{3,2},{4,5},{5,4},{6,7},{7,6},{8,9},{9,8},{10,11... | collective-permute-start | bytes 1572872 | tf_op jit(solution)/shard_map/ppermute | solution.py:32
  21.8 21.0 %collective-permute-start.8 = (bf16[1024,256]{1,0:T(8,128)(2,1)S(1)}, bf16[1024,256]{1,0:T(8,128)(2,1)S(1)}, u32[]{:S(2)}, u32[]{:S(2)}) collective-permute-start(bf16[1024,256]{1,0:T(8,128)(2,1)S(1)} %collective-permute-done.refs_2_), channel_id=1, source_target_pairs={{0,16},{8,24},{16,0},{24,8},{1,17},{9,25},{17,1},{25,9},{2,18},{10... | collective-permute-start | bytes 1572872 | tf_op jit(solution)/shard_map/ppermute | solution.py:32
  23.3 19.5 %collective-permute-start.9 = (bf16[1024,256]{1,0:T(8,128)(2,1)S(1)}, bf16[1024,256]{1,0:T(8,128)(2,1)S(1)}, u32[]{:S(2)}, u32[]{:S(2)}) collective-permute-start(bf16[1024,256]{1,0:T(8,128)(2,1)S(1)} %collective-permute-done.2.refs_7_), channel_id=1, source_target_pairs={{0,8},{8,0},{16,24},{24,16},{1,9},{9,1},{17,25},{25,17},{2,10},{10... | collective-permute-start | bytes 1572872 | tf_op jit(solution)/shard_map/ppermute | solution.py:32
  33.1 3.2 %collective-permute-start.6 = (bf16[1024,256]{1,0:T(8,128)(2,1)}, bf16[1024,256]{1,0:T(8,128)(2,1)S(1)}, u32[]{:S(2)}, u32[]{:S(2)}) collective-permute-start(bf16[1024,256]{1,0:T(8,128)(2,1)} %collective-permute-done.5.refs_6_), channel_id=1, source_target_pairs={{0,1},{1,0},{2,3},{3,2},{4,5},{5,4},{6,7},{7,6},{8,9},{9,8},{10,11... | collective-permute-start | bytes 1572872 | tf_op jit(solution)/shard_map/ppermute | solution.py:32
  33.1 3.6 %collective-permute-start.4 = (bf16[1024,256]{1,0:T(8,128)(2,1)}, bf16[1024,256]{1,0:T(8,128)(2,1)S(1)}, u32[]{:S(2)}, u32[]{:S(2)}) collective-permute-start(bf16[1024,256]{1,0:T(8,128)(2,1)} %collective-permute-done.1.refs_3_), channel_id=1, source_target_pairs={{0,1},{1,0},{2,3},{3,2},{4,5},{5,4},{6,7},{7,6},{8,9},{9,8},{10,11... | collective-permute-start | bytes 1572872 | tf_op jit(solution)/shard_map/ppermute | solution.py:32
  33.6 3.1 %collective-permute-start.7 = (bf16[1024,256]{1,0:T(8,128)(2,1)S(1)}, bf16[1024,256]{1,0:T(8,128)(2,1)S(1)}, u32[]{:S(2)}, u32[]{:S(2)}) collective-permute-start(bf16[1024,256]{1,0:T(8,128)(2,1)S(1)} %collective-permute-done.2.refs_7_), channel_id=1, source_target_pairs={{0,1},{1,0},{2,3},{3,2},{4,5},{5,4},{6,7},{7,6},{8,9},{9,8},{10,11... | collective-permute-start | bytes 1572872 | tf_op jit(solution)/shard_map/ppermute | solution.py:32
  42.8 2.1 %collective-permute-start.10 = (bf16[1024,256]{1,0:T(8,128)(2,1)S(1)}, bf16[1024,256]{1,0:T(8,128)(2,1)S(1)}, u32[]{:S(2)}, u32[]{:S(2)}) collective-permute-start(bf16[1024,256]{1,0:T(8,128)(2,1)S(1)} %collective-permute-done.8.refs_1_), channel_id=1, source_target_pairs={{0,1},{1,0},{2,3},{3,2},{4,5},{5,4},{6,7},{7,6},{8,9},{9,8},{10,11... | collective-permute-start | bytes 1572872 | tf_op jit(solution)/shard_map/ppermute | solution.py:32
  42.9 2.6 %collective-permute-start.11 = (bf16[1024,256]{1,0:T(8,128)(2,1)S(1)}, bf16[1024,256]{1,0:T(8,128)(2,1)S(1)}, u32[]{:S(2)}, u32[]{:S(2)}) collective-permute-start(bf16[1024,256]{1,0:T(8,128)(2,1)S(1)} %collective-permute-done.9.refs_2_), channel_id=1, source_target_pairs={{0,1},{1,0},{2,3},{3,2},{4,5},{5,4},{6,7},{7,6},{8,9},{9,8},{10,11... | collective-permute-start | bytes 1572872 | tf_op jit(solution)/shard_map/ppermute | solution.py:32
  43.4 28.7 %collective-permute-start.20 = (bf16[192,2560]{1,0:T(8,128)(2,1)S(1)}, bf16[192,2560]{1,0:T(8,128)(2,1)S(1)}, u32[]{:S(2)}, u32[]{:S(2)}) collective-permute-start(bf16[192,2560]{1,0:T(8,128)(2,1)S(1)} %get-tuple-element.64), channel_id=1, source_target_pairs={{0,16},{8,24},{16,0},{24,8},{1,17},{9,25},{17,1},{25,9},{2,18},{10... | collective-permute-start | bytes 2949128 | tf_op jit(solution)/shard_map/ppermute | solution.py:32
  44.9 27.2 %collective-permute-start.19 = (bf16[192,2560]{1,0:T(8,128)(2,1)S(1)}, bf16[192,2560]{1,0:T(8,128)(2,1)S(1)}, u32[]{:S(2)}, u32[]{:S(2)}) collective-permute-start(bf16[192,2560]{1,0:T(8,128)(2,1)S(1)} %get-tuple-element.63), channel_id=1, source_target_pairs={{0,8},{8,0},{16,24},{24,16},{1,9},{9,1},{17,25},{25,17},{2,10},{10... | collective-permute-start | bytes 2949128 | tf_op jit(solution)/shard_map/ppermute | solution.py:32
  46.7 7.6 %collective-permute-start.14 = (bf16[192,256]{1,0:T(8,128)(2,1)S(1)}, bf16[192,256]{1,0:T(8,128)(2,1)S(1)}, u32[]{:S(2)}, u32[]{:S(2)}) collective-permute-start(bf16[192,256]{1,0:T(8,128)(2,1)S(1)} %project.3.refs_0_), channel_id=1, source_target_pairs={{0,6},{1,7},{2,4},{3,5},{4,2},{5,3},{6,0},{7,1},{8,14},{9,15},{10,... | collective-permute-start | bytes 294920 | tf_op jit(solution)/shard_map/ppermute | solution.py:32
  50.3 8.6 %collective-permute-start.13 = (bf16[192,256]{1,0:T(8,128)(2,1)S(1)}, bf16[192,256]{1,0:T(8,128)(2,1)S(1)}, u32[]{:S(2)}, u32[]{:S(2)}) collective-permute-start(bf16[192,256]{1,0:T(8,128)(2,1)S(1)} %project.3.refs_0_), channel_id=1, source_target_pairs={{0,4},{1,5},{2,6},{3,7},{4,0},{5,1},{6,2},{7,3},{8,12},{9,13},{10,... | collective-permute-start | bytes 294920 | tf_op jit(solution)/shard_map/ppermute | solution.py:32
  50.4 8.6 %collective-permute-start.12 = (bf16[192,256]{1,0:T(8,128)(2,1)S(1)}, bf16[192,256]{1,0:T(8,128)(2,1)S(1)}, u32[]{:S(2)}, u32[]{:S(2)}) collective-permute-start(bf16[192,256]{1,0:T(8,128)(2,1)S(1)} %project.3.refs_0_), channel_id=1, source_target_pairs={{0,2},{1,3},{2,0},{3,1},{4,6},{5,7},{6,4},{7,5},{8,10},{9,11},{10,... | collective-permute-start | bytes 294920 | tf_op jit(solution)/shard_map/ppermute | solution.py:32
  58.9 32.6 %collective-permute-start.21 = (bf16[192,2560]{1,0:T(8,128)(2,1)S(1)}, bf16[192,2560]{1,0:T(8,128)(2,1)S(1)}, u32[]{:S(2)}, u32[]{:S(2)}) collective-permute-start(bf16[192,2560]{1,0:T(8,128)(2,1)S(1)} %get-tuple-element.68), channel_id=1, source_target_pairs={{0,24},{8,16},{16,8},{24,0},{1,25},{9,17},{17,9},{25,1},{2,26},{10... | collective-permute-start | bytes 2949128 | tf_op jit(solution)/shard_map/ppermute | solution.py:32
  60.9 1.5 collective-permute-start.16
  62.3 1.3 collective-permute-start.18
  72.1 1.7 %collective-permute-start.22 = (bf16[768,256]{1,0:T(8,128)(2,1)S(1)}, bf16[768,256]{1,0:T(8,128)(2,1)S(1)}, u32[]{:S(2)}, u32[]{:S(2)}) collective-permute-start(bf16[768,256]{1,0:T(8,128)(2,1)S(1)} %get-tuple-element.70), channel_id=1, source_target_pairs={{0,1},{1,0},{2,3},{3,2},{4,5},{5,4},{6,7},{7,6},{8,9},{9,8},{10,11... | collective-permute-start | bytes 1179656 | tf_op jit(solution)/shard_map/ppermute | solution.py:32
  73.9 6.6 %collective-permute-start.23 = (bf16[192,256]{1,0:T(8,128)(2,1)S(1)}, bf16[192,256]{1,0:T(8,128)(2,1)S(1)}, u32[]{:S(2)}, u32[]{:S(2)}) collective-permute-start(bf16[192,256]{1,0:T(8,128)(2,1)S(1)} %get-tuple-element.72), channel_id=1, source_target_pairs={{0,2},{1,3},{2,0},{3,1},{4,6},{5,7},{6,4},{7,5},{8,10},{9,11},{10,... | collective-permute-start | bytes 294920 | tf_op jit(solution)/shard_map/ppermute | solution.py:32
  74.5 10.8 %collective-permute-start.24 = (bf16[192,256]{1,0:T(8,128)(2,1)S(1)}, bf16[192,256]{1,0:T(8,128)(2,1)S(1)}, u32[]{:S(2)}, u32[]{:S(2)}) collective-permute-start(bf16[192,256]{1,0:T(8,128)(2,1)S(1)} %get-tuple-element.73), channel_id=1, source_target_pairs={{0,4},{1,5},{2,6},{3,7},{4,0},{5,1},{6,2},{7,3},{8,12},{9,13},{10,... | collective-permute-start | bytes 294920 | tf_op jit(solution)/shard_map/ppermute | solution.py:32
  77.1 8.3 %collective-permute-start.25 = (bf16[192,256]{1,0:T(8,128)(2,1)S(1)}, bf16[192,256]{1,0:T(8,128)(2,1)S(1)}, u32[]{:S(2)}, u32[]{:S(2)}) collective-permute-start(bf16[192,256]{1,0:T(8,128)(2,1)S(1)} %get-tuple-element.74), channel_id=1, source_target_pairs={{0,6},{1,7},{2,4},{3,5},{4,2},{5,3},{6,0},{7,1},{8,14},{9,15},{10,... | collective-permute-start | bytes 294920 | tf_op jit(solution)/shard_map/ppermute | solution.py:32
  85.4 8.1 %collective-permute-start.28 = (bf16[192,256]{1,0:T(8,128)(2,1)S(1)}, bf16[192,256]{1,0:T(8,128)(2,1)S(1)}, u32[]{:S(2)}, u32[]{:S(2)}) collective-permute-start(bf16[192,256]{1,0:T(8,128)(2,1)S(1)} %total.1.refs_4_.refs_1_), channel_id=1, source_target_pairs={{0,24},{8,16},{16,8},{24,0},{1,25},{9,17},{17,9},{25,1},{2,26},{10... | collective-permute-start | bytes 294920 | tf_op jit(solution)/shard_map/ppermute | solution.py:32
  86.4 8.4 %collective-permute-start.27 = (bf16[192,256]{1,0:T(8,128)(2,1)S(1)}, bf16[192,256]{1,0:T(8,128)(2,1)S(1)}, u32[]{:S(2)}, u32[]{:S(2)}) collective-permute-start(bf16[192,256]{1,0:T(8,128)(2,1)S(1)} %total.1.refs_4_.refs_1_), channel_id=1, source_target_pairs={{0,16},{8,24},{16,0},{24,8},{1,17},{9,25},{17,1},{25,9},{2,18},{10... | collective-permute-start | bytes 294920 | tf_op jit(solution)/shard_map/ppermute | solution.py:32
  88.0 6.9 %collective-permute-start.26 = (bf16[192,256]{1,0:T(8,128)(2,1)S(1)}, bf16[192,256]{1,0:T(8,128)(2,1)S(1)}, u32[]{:S(2)}, u32[]{:S(2)}) collective-permute-start(bf16[192,256]{1,0:T(8,128)(2,1)S(1)} %total.1.refs_4_.refs_1_), channel_id=1, source_target_pairs={{0,8},{8,0},{16,24},{24,16},{1,9},{9,1},{17,25},{25,17},{2,10},{10... | collective-permute-start | bytes 294920 | tf_op jit(solution)/shard_map/ppermute | solution.py:32
  94.8 5.4 %collective-permute-start.31 = (bf16[3072,256]{1,0:T(8,128)(2,1)S(1)}, bf16[3072,256]{1,0:T(8,128)(2,1)S(1)}, u32[]{:S(2)}, u32[]{:S(2)}) collective-permute-start(bf16[3072,256]{1,0:T(8,128)(2,1)S(1)} %get-tuple-element.81), channel_id=1, source_target_pairs={{0,1},{1,0},{2,3},{3,2},{4,5},{5,4},{6,7},{7,6},{8,9},{9,8},{10,11... | collective-permute-start | bytes 4718600 | tf_op jit(solution)/shard_map/ppermute | solution.py:32
  96.2 2.4 %collective-permute-start.29 = (bf16[512,256]{1,0:T(8,128)(2,1)S(1)}, bf16[512,256]{1,0:T(8,128)(2,1)S(1)}, u32[]{:S(2)}, u32[]{:S(2)}) collective-permute-start(bf16[512,256]{1,0:T(8,128)(2,1)S(1)} %get-tuple-element.76), channel_id=1, source_target_pairs={{0,1},{1,0},{2,3},{3,2},{4,5},{5,4},{6,7},{7,6},{8,9},{9,8},{10,11... | collective-permute-start | bytes 786440 | tf_op jit(solution)/shard_map/ppermute | solution.py:32
  98.3 1.8 %collective-permute-start.30 = (bf16[768,256]{1,0:T(8,128)(2,1)S(1)}, bf16[768,256]{1,0:T(8,128)(2,1)S(1)}, u32[]{:S(2)}, u32[]{:S(2)}) collective-permute-start(bf16[768,256]{1,0:T(8,128)(2,1)S(1)} %get-tuple-element.78), channel_id=1, source_target_pairs={{0,1},{1,0},{2,3},{3,2},{4,5},{5,4},{6,7},{7,6},{8,9},{9,8},{10,11... | collective-permute-start | bytes 1179656 | tf_op jit(solution)/shard_map/ppermute | solution.py:32
  100.9 6.4 %collective-permute-start.32 = (bf16[256,256]{1,0:T(8,128)(2,1)S(1)}, bf16[256,256]{1,0:T(8,128)(2,1)S(1)}, u32[]{:S(2)}, u32[]{:S(2)}) collective-permute-start(bf16[256,256]{1,0:T(8,128)(2,1)S(1)} %slice.74), channel_id=1, source_target_pairs={{0,2},{1,3},{2,0},{3,1},{4,6},{5,7},{6,4},{7,5},{8,10},{9,11},{10,... | collective-permute-start | bytes 393224 | tf_op jit(solution)/shard_map/ppermute | solution.py:32
  102.6 9.9 %collective-permute-start.37 = (bf16[384,256]{1,0:T(8,128)(2,1)S(1)}, bf16[384,256]{1,0:T(8,128)(2,1)S(1)}, u32[]{:S(2)}, u32[]{:S(2)}) collective-permute-start(bf16[384,256]{1,0:T(8,128)(2,1)S(1)} %slice.73), channel_id=1, source_target_pairs={{0,2},{1,3},{2,0},{3,1},{4,6},{5,7},{6,4},{7,5},{8,10},{9,11},{10,... | collective-permute-start | bytes 589832 | tf_op jit(solution)/shard_map/ppermute | solution.py:32
  103.1 18.3 %collective-permute-start.42 = (bf16[768,256]{1,0:T(8,128)(2,1)S(1)}, bf16[768,256]{1,0:T(8,128)(2,1)S(1)}, u32[]{:S(2)}, u32[]{:S(2)}) collective-permute-start(bf16[768,256]{1,0:T(8,128)(2,1)S(1)} %get-tuple-element.87), channel_id=1, source_target_pairs={{0,8},{8,0},{16,24},{24,16},{1,9},{9,1},{17,25},{25,17},{2,10},{10... | collective-permute-start | bytes 1179656 | tf_op jit(solution)/shard_map/ppermute | solution.py:32
  103.6 18.8 %collective-permute-start.43 = (bf16[768,256]{1,0:T(8,128)(2,1)S(1)}, bf16[768,256]{1,0:T(8,128)(2,1)S(1)}, u32[]{:S(2)}, u32[]{:S(2)}) collective-permute-start(bf16[768,256]{1,0:T(8,128)(2,1)S(1)} %get-tuple-element.88), channel_id=1, source_target_pairs={{0,16},{8,24},{16,0},{24,8},{1,17},{9,25},{17,1},{25,9},{2,18},{10... | collective-permute-start | bytes 1179656 | tf_op jit(solution)/shard_map/ppermute | solution.py:32
  104.2 18.2 %collective-permute-start.44 = (bf16[768,256]{1,0:T(8,128)(2,1)S(1)}, bf16[768,256]{1,0:T(8,128)(2,1)S(1)}, u32[]{:S(2)}, u32[]{:S(2)}) collective-permute-start(bf16[768,256]{1,0:T(8,128)(2,1)S(1)} %get-tuple-element.89), channel_id=1, source_target_pairs={{0,24},{8,16},{16,8},{24,0},{1,25},{9,17},{17,9},{25,1},{2,26},{10... | collective-permute-start | bytes 1179656 | tf_op jit(solution)/shard_map/ppermute | solution.py:32
  107.3 13.3 %collective-permute-start.33 = (bf16[256,256]{1,0:T(8,128)(2,1)S(1)}, bf16[256,256]{1,0:T(8,128)(2,1)S(1)}, u32[]{:S(2)}, u32[]{:S(2)}) collective-permute-start(bf16[256,256]{1,0:T(8,128)(2,1)S(1)} %fusion.2), channel_id=1, source_target_pairs={{0,4},{1,5},{2,6},{3,7},{4,0},{5,1},{6,2},{7,3},{8,12},{9,13},{10,... | collective-permute-start | bytes 393224 | tf_op jit(solution)/shard_map/ppermute | solution.py:32
  112.5 12.1 %collective-permute-start.38 = (bf16[384,256]{1,0:T(8,128)(2,1)S(1)}, bf16[384,256]{1,0:T(8,128)(2,1)S(1)}, u32[]{:S(2)}, u32[]{:S(2)}) collective-permute-start(bf16[384,256]{1,0:T(8,128)(2,1)S(1)} %fusion), channel_id=1, source_target_pairs={{0,4},{1,5},{2,6},{3,7},{4,0},{5,1},{6,2},{7,3},{8,12},{9,13},{10,... | collective-permute-start | bytes 589832 | tf_op jit(solution)/shard_map/ppermute | solution.py:32
  120.7 12.8 %collective-permute-start.34 = (bf16[256,256]{1,0:T(8,128)(2,1)S(1)}, bf16[256,256]{1,0:T(8,128)(2,1)S(1)}, u32[]{:S(2)}, u32[]{:S(2)}) collective-permute-start(bf16[256,256]{1,0:T(8,128)(2,1)S(1)} %add_convert_fusion.2.refs_0_), channel_id=1, source_target_pairs={{0,2},{1,3},{2,0},{3,1},{4,6},{5,7},{6,4},{7,5},{8,10},{9,11},{10,... | collective-permute-start | bytes 393224 | tf_op jit(solution)/shard_map/ppermute | solution.py:32
  122.6 9.0 %collective-permute-start.45 = (bf16[384,256]{1,0:T(8,128)(2,1)S(1)}, bf16[384,256]{1,0:T(8,128)(2,1)S(1)}, u32[]{:S(2)}, u32[]{:S(2)}) collective-permute-start(bf16[384,256]{1,0:T(8,128)(2,1)S(1)} %slice.72), channel_id=1, source_target_pairs={{0,2},{1,3},{2,0},{3,1},{4,6},{5,7},{6,4},{7,5},{8,10},{9,11},{10,... | collective-permute-start | bytes 589832 | tf_op jit(solution)/shard_map/ppermute | solution.py:32
  124.7 12.1 %collective-permute-start.39 = (bf16[384,256]{1,0:T(8,128)(2,1)S(1)}, bf16[384,256]{1,0:T(8,128)(2,1)S(1)}, u32[]{:S(2)}, u32[]{:S(2)}) collective-permute-start(bf16[384,256]{1,0:T(8,128)(2,1)S(1)} %add_convert_fusion.1.refs_4_), channel_id=1, source_target_pairs={{0,2},{1,3},{2,0},{3,1},{4,6},{5,7},{6,4},{7,5},{8,10},{9,11},{10,... | collective-permute-start | bytes 589832 | tf_op jit(solution)/shard_map/ppermute | solution.py:32
  131.6 10.0 %collective-permute-start.46 = (bf16[384,256]{1,0:T(8,128)(2,1)S(1)}, bf16[384,256]{1,0:T(8,128)(2,1)S(1)}, u32[]{:S(2)}, u32[]{:S(2)}) collective-permute-start(bf16[384,256]{1,0:T(8,128)(2,1)S(1)} %fusion.1), channel_id=1, source_target_pairs={{0,4},{1,5},{2,6},{3,7},{4,0},{5,1},{6,2},{7,3},{8,12},{9,13},{10,... | collective-permute-start | bytes 589832 | tf_op jit(solution)/shard_map/ppermute | solution.py:32
  133.5 3.2 %collective-permute-start.35 = (bf16[256,256]{1,0:T(8,128)(2,1)S(1)}, bf16[256,256]{1,0:T(8,128)(2,1)S(1)}, u32[]{:S(2)}, u32[]{:S(2)}) collective-permute-start(bf16[256,256]{1,0:T(8,128)(2,1)S(1)} %add_convert_fusion.2.refs_0_), channel_id=1, source_target_pairs={{0,1},{1,0},{2,3},{3,2},{4,5},{5,4},{6,7},{7,6},{8,9},{9,8},{10,11... | collective-permute-start | bytes 393224 | tf_op jit(solution)/shard_map/ppermute | solution.py:32
  133.6 3.2 %collective-permute-start.36 = (bf16[256,256]{1,0:T(8,128)(2,1)S(1)}, bf16[256,256]{1,0:T(8,128)(2,1)S(1)}, u32[]{:S(2)}, u32[]{:S(2)}) collective-permute-start(bf16[256,256]{1,0:T(8,128)(2,1)S(1)} %collective-permute-done.34.refs_1_), channel_id=1, source_target_pairs={{0,1},{1,0},{2,3},{3,2},{4,5},{5,4},{6,7},{7,6},{8,9},{9,8},{10,11... | collective-permute-start | bytes 393224 | tf_op jit(solution)/shard_map/ppermute | solution.py:32
  134.1 7.8 %collective-permute-start.40 = (bf16[384,256]{1,0:T(8,128)(2,1)S(1)}, bf16[384,256]{1,0:T(8,128)(2,1)S(1)}, u32[]{:S(2)}, u32[]{:S(2)}) collective-permute-start(bf16[384,256]{1,0:T(8,128)(2,1)S(1)} %add_convert_fusion.1.refs_4_), channel_id=1, source_target_pairs={{0,1},{1,0},{2,3},{3,2},{4,5},{5,4},{6,7},{7,6},{8,9},{9,8},{10,11... | collective-permute-start | bytes 589832 | tf_op jit(solution)/shard_map/ppermute | solution.py:32
  136.7 5.1 %collective-permute-start.41 = (bf16[384,256]{1,0:T(8,128)(2,1)S(1)}, bf16[384,256]{1,0:T(8,128)(2,1)S(1)}, u32[]{:S(2)}, u32[]{:S(2)}) collective-permute-start(bf16[384,256]{1,0:T(8,128)(2,1)S(1)} %collective-permute-done.39.refs_5_), channel_id=1, source_target_pairs={{0,1},{1,0},{2,3},{3,2},{4,5},{5,4},{6,7},{7,6},{8,9},{9,8},{10,11... | collective-permute-start | bytes 589832 | tf_op jit(solution)/shard_map/ppermute | solution.py:32
  141.7 5.7 %collective-permute-start.47 = (bf16[384,256]{1,0:T(8,128)(2,1)S(1)}, bf16[384,256]{1,0:T(8,128)(2,1)S(1)}, u32[]{:S(2)}, u32[]{:S(2)}) collective-permute-start(bf16[384,256]{1,0:T(8,128)(2,1)S(1)} %add_convert_fusion.refs_2_), channel_id=1, source_target_pairs={{0,2},{1,3},{2,0},{3,1},{4,6},{5,7},{6,4},{7,5},{8,10},{9,11},{10,... | collective-permute-start | bytes 589832 | tf_op jit(solution)/shard_map/ppermute | solution.py:32
  141.7 5.7 %collective-permute-start.48 = (bf16[384,256]{1,0:T(8,128)(2,1)S(1)}, bf16[384,256]{1,0:T(8,128)(2,1)S(1)}, u32[]{:S(2)}, u32[]{:S(2)}) collective-permute-start(bf16[384,256]{1,0:T(8,128)(2,1)S(1)} %add_convert_fusion.refs_2_), channel_id=1, source_target_pairs={{0,1},{1,0},{2,3},{3,2},{4,5},{5,4},{6,7},{7,6},{8,9},{9,8},{10,11... | collective-permute-start | bytes 589832 | tf_op jit(solution)/shard_map/ppermute | solution.py:32
  147.4 1.4 collective-permute-start.49
  (10 other events, 133.1 us)

commit v19 on v17

--- a/solution.py
+++ b/solution.py
@@ -521,11 +521,12 @@
         add_cores(*weight_rows(ids, arrays, grads, groups, *region, block_rows, sub_count))
         for region in regions[:-1]
     ]
-    moved_parts, own = after(moved_parts, *own)
+    moved_parts[1:], own = after(moved_parts[1:], *own)
+    ready = [own, ()]
     own = [swap(one, "dp", j) if j else one for j, one in enumerate(own)]
     finals = []
-    for part in moved_parts:
-        part = scatter_along_z(part, sub_count)
+    for part, earlier in zip(moved_parts, ready):
+        part = scatter_along_z(part, sub_count, earlier)
         finals.append(sum_of_halves(part, sub_count))
     part = scatter_along_z(sum_of(own), sub_count, finals[:TIED])
     blocks = gather_parts(finals[0], sub_count)

time: 151 us -> 153 us (1.013)
  waiting for transfers between devices: 78.6 us -> 82.2 us
  starting transfers between devices: 41.7 us -> 39.6 us
    ppermute x50, waiting for transfers between devices: 78.6 us -> 82.2 us  [swap(): return lax.ppermute(array, axis, [(i, i ^ distance) for i in range(count)])]
    ppermute x50, starting transfers between devices: 41.7 us -> 39.6 us  [swap(): return lax.ppermute(array, axis, [(i, i ^ distance) for i in range(count)])]
  transfers between devices with their start and end apart: 50 -> 50, of which waited for: 29 -> 30; matrix products, arithmetic and copies ran while one was open for 3% -> 3% of each run, Pallas kernels for 13% -> 13%
where the time goes in v19:
time: 153 us; the launch traced here: 152 us
  waiting for transfers between devices  82.2 us (54%)
  starting transfers between devices  39.6 us (26%)
  Pallas kernels  21.4 us (14%)
  local copies, waits for them, and re-layouts  5.14 us (3%)
  other arithmetic  2.92 us (2%)
    ppermute x50, waiting for transfers between devices, swap(): return lax.ppermute(array, axis, [(i, i ^ distance) for i in range(count)])  82.2 us
    ppermute x50, starting transfers between devices, swap(): return lax.ppermute(array, axis, [(i, i ^ distance) for i in range(count)])  39.6 us
    pallas_call x7, Pallas kernels, kernel_call(): pl.pallas_call(kernel, out_shape=outs, in_specs=[smem] * len(scalars) + [...  9.06 us
    pallas_call x1, Pallas kernels, attention(): pl.pallas_call(functools.partial(attention_kernel, shape), out_shape=(jax...  8.45 us
    pallas_call x2, Pallas kernels, assemble(): pl.pallas_call(functools.partial(assemble_kernel, sub_count, regions, not...  3.92 us
  transfers between devices with their start and end apart: 50, of which 30 were waited for; matrix products, arithmetic and copies ran while one was open for 3% of the time, Pallas kernels for 13%

profile of v19, /device:TPU:0, one launch (start us, length us, event | category | flops | bytes accessed | tf_op | source)
XLA Modules:
  0.0 152.4 jit_solution(14170593080448986558)
XLA Ops:
  0.7 1.4 constant_dynamic-slice_fusion
  2.1 0.9 pad_maximum_fusion
  2.9 2.9 %collective-permute-start = (bf16[1024,256]{1,0:T(8,128)(2,1)}, bf16[1024,256]{1,0:T(8,128)(2,1)S(1)}, u32[]{:S(2)}, u32[]{:S(2)}) collective-permute-start(bf16[1024,256]{1,0:T(8,128)(2,1)} %pad_maximum_fusion), channel_id=1, source_target_pairs={{0,8},{8,0},{16,24},{24,16},{1,9},{9,1},{17,25},{25,17},{2,10},{10... | collective-permute-start | bytes 1572872 | tf_op jit(solution)/shard_map/ppermute | solution.py:32
  6.7 1.5 collective-permute-start.2
  8.8 10.0 %collective-permute-done.refs_2_ = bf16[1024,256]{1,0:T(8,128)(2,1)S(1)} collective-permute-done((bf16[1024,256]{1,0:T(8,128)(2,1)}, bf16[1024,256]{1,0:T(8,128)(2,1)S(1)}, u32[]{:S(2)}, u32[]{:S(2)}) %collective-permute-start) | collective-permute-done | bytes 524320 | tf_op jit(solution)/shard_map/ppermute | solution.py:32
  18.8 3.0 %collective-permute-done.2.refs_7_ = bf16[1024,256]{1,0:T(8,128)(2,1)S(1)} collective-permute-done((bf16[1024,256]{1,0:T(8,128)(2,1)}, bf16[1024,256]{1,0:T(8,128)(2,1)S(1)}, u32[]{:S(2)}, u32[]{:S(2)}) %collective-permute-start.2) | collective-permute-done | bytes 524320 | tf_op jit(solution)/shard_map/ppermute | solution.py:32
  21.8 1.5 collective-permute-start.8
  23.8 9.3 %collective-permute-done.5.refs_6_ = bf16[1024,256]{1,0:T(8,128)(2,1)} collective-permute-done((bf16[1024,256]{1,0:T(8,128)(2,1)}, bf16[1024,256]{1,0:T(8,128)(2,1)}, u32[]{:S(2)}, u32[]{:S(2)}) %collective-permute-start.5) | collective-permute-done | bytes 524320 | tf_op jit(solution)/shard_map/ppermute | solution.py:32
  33.8 2.5 %dynamic-slice_bitcast_fusion = (bf16[192,2560]{1,0:T(8,128)(2,1)S(1)}, bf16[192,2560]{1,0:T(8,128)(2,1)S(1)}, bf16[192,2560]{1,0:T(8,128)(2,1)S(1)}, bf16[192,2560]{1,0:T(8,128)(2,1)S(1)}) fusion(bf16[1,192,16384]{2,1,0:T(8,128)(2,1)} %param.7, s32[]{:T(128)S(6)} %select_n.42, s32[]{:T(128)S(6)} %select_n.40, s32[]{:T(128)S(6)} %select_n.39, s32[]{:T(128)S(6)} %select_n.41), kind=kLoop, calls=%fused_computation.1 | loop fusion | bytes 7864336 | tf_op jit(solution)/shard_map/dynamic_slice | solution.py:465
  37.8 3.2 %project.2.refs_0_ = f32[192,256]{1,0:T(8,128)S(1)} custom-call(s32[3]{0:T(128)S(1)} %pad_add_fusion.ids, bf16[192,16384]{1,0:T(8,128)(2,1)S(1)} %bitcast.19, bf16[4096,128]{1,0:T(8,128)(2,1)S(1)} %copy-done, bf16[4096,128]{1,0:T(8,128)(2,1)S(1)} %copy-done.1, bf16[1024,256]{1,0:T(8,128)(2,1)S(1)} %collective-permute-done.refs_2_, ...), custom_call_target="tpu_custom_call" | custom-call | bytes 16777216 | tf_op jit(solution)/shard_map/project/pallas_call | solution.py:48
  41.0 1.8 %collective-permute-done.8.refs_1_ = bf16[1024,256]{1,0:T(8,128)(2,1)S(1)} collective-permute-done((bf16[1024,256]{1,0:T(8,128)(2,1)S(1)}, bf16[1024,256]{1,0:T(8,128)(2,1)S(1)}, u32[]{:S(2)}, u32[]{:S(2)}) %collective-permute-start.8) | collective-permute-done | bytes 524320 | tf_op jit(solution)/shard_map/ppermute | solution.py:32
  43.4 1.5 collective-permute-start.20
  45.5 1.1 project.3.refs_0_
  46.7 3.7 %collective-permute-start.14 = (bf16[192,256]{1,0:T(8,128)(2,1)S(1)}, bf16[192,256]{1,0:T(8,128)(2,1)S(1)}, u32[]{:S(2)}, u32[]{:S(2)}) collective-permute-start(bf16[192,256]{1,0:T(8,128)(2,1)S(1)} %project.3.refs_0_), channel_id=1, source_target_pairs={{0,6},{1,7},{2,4},{3,5},{4,2},{5,3},{6,0},{7,1},{8,14},{9,15},{10,... | collective-permute-start | bytes 294920 | tf_op jit(solution)/shard_map/ppermute | solution.py:32
  51.1 3.1 %collective-permute-done.14.refs_6_ = bf16[192,256]{1,0:T(8,128)(2,1)S(1)} collective-permute-done((bf16[192,256]{1,0:T(8,128)(2,1)S(1)}, bf16[192,256]{1,0:T(8,128)(2,1)S(1)}, u32[]{:S(2)}, u32[]{:S(2)}) %collective-permute-start.14) | collective-permute-done | bytes 98336 | tf_op jit(solution)/shard_map/ppermute | solution.py:32
  54.3 4.6 %collective-permute-done.13.refs_4_ = bf16[192,256]{1,0:T(8,128)(2,1)S(1)} collective-permute-done((bf16[192,256]{1,0:T(8,128)(2,1)S(1)}, bf16[192,256]{1,0:T(8,128)(2,1)S(1)}, u32[]{:S(2)}, u32[]{:S(2)}) %collective-permute-start.13) | collective-permute-done | bytes 98336 | tf_op jit(solution)/shard_map/ppermute | solution.py:32
  58.9 2.0 %collective-permute-start.26 = (bf16[192,2560]{1,0:T(8,128)(2,1)S(1)}, bf16[192,2560]{1,0:T(8,128)(2,1)S(1)}, u32[]{:S(2)}, u32[]{:S(2)}) collective-permute-start(bf16[192,2560]{1,0:T(8,128)(2,1)S(1)} %get-tuple-element.77), channel_id=1, source_target_pairs={{0,24},{8,16},{16,8},{24,0},{1,25},{9,17},{17,9},{25,1},{2,26},{10... | collective-permute-start | bytes 2949128 | tf_op jit(solution)/shard_map/ppermute | solution.py:32
  63.7 8.5 %attention.1 = (bf16[192,1024]{1,0:T(8,128)(2,1)}, f32[768,256]{1,0:T(8,128)S(1)}, bf16[768,256]{1,0:T(8,128)(2,1)S(1)}) custom-call(s32[1]{0:T(128)} %bitcast.ids, s32[16]{0:T(128)S(1)} %copy-done.4, s32[8]{0:T(128)S(1)} %bitcast.24, bf16[192,1024]{1,0:T(8,128)(2,1)S(1)} %bitcast.22, bf16[192,1024]{1,0:T(8,128)(2,1)S(1)} %bitcast.23, ...), custom_call_target="tpu_custom_call" | custom-call | tf_op jit(solution)/shard_map/attention/pallas_call | solution.py:171
  72.5 1.4 collective-permute-done.21.came
  74.5 2.5 %collective-permute-start.23 = (bf16[192,256]{1,0:T(8,128)(2,1)S(1)}, bf16[192,256]{1,0:T(8,128)(2,1)S(1)}, u32[]{:S(2)}, u32[]{:S(2)}) collective-permute-start(bf16[192,256]{1,0:T(8,128)(2,1)S(1)} %get-tuple-element.74), channel_id=1, source_target_pairs={{0,4},{1,5},{2,6},{3,7},{4,0},{5,1},{6,2},{7,3},{8,12},{9,13},{10,... | collective-permute-start | bytes 294920 | tf_op jit(solution)/shard_map/ppermute | solution.py:32
  77.1 1.3 collective-permute-start.24
  78.4 2.2 %collective-permute-done.22.refs_1_ = bf16[192,256]{1,0:T(8,128)(2,1)S(1)} collective-permute-done((bf16[192,256]{1,0:T(8,128)(2,1)S(1)}, bf16[192,256]{1,0:T(8,128)(2,1)S(1)}, u32[]{:S(2)}, u32[]{:S(2)}) %collective-permute-start.22) | collective-permute-done | bytes 98336 | tf_op jit(solution)/shard_map/ppermute | solution.py:32
  80.6 4.8 %collective-permute-done.23.refs_2_ = bf16[192,256]{1,0:T(8,128)(2,1)S(1)} collective-permute-done((bf16[192,256]{1,0:T(8,128)(2,1)S(1)}, bf16[192,256]{1,0:T(8,128)(2,1)S(1)}, u32[]{:S(2)}, u32[]{:S(2)}) %collective-permute-start.23) | collective-permute-done | bytes 98336 | tf_op jit(solution)/shard_map/ppermute | solution.py:32
  85.4 1.1 collective-permute-start.25
  86.5 0.9 collective-permute-start.28
  87.5 1.5 collective-permute-start.27
  89.0 2.5 %collective-permute-done.26.refs_3_ = bf16[192,2560]{1,0:T(8,128)(2,1)S(1)} collective-permute-done((bf16[192,2560]{1,0:T(8,128)(2,1)S(1)}, bf16[192,2560]{1,0:T(8,128)(2,1)S(1)}, u32[]{:S(2)}, u32[]{:S(2)}) %collective-permute-start.26) | collective-permute-done | bytes 983072 | tf_op jit(solution)/shard_map/ppermute | solution.py:32
  91.5 1.2 collective-permute-done.25.refs_5_
  92.7 1.7 %weight_rows.5 = (bf16[3072,256]{1,0:T(8,128)(2,1)S(1)}, bf16[3072,256]{1,0:T(8,128)(2,1)S(1)}) custom-call(s32[3]{0:T(128)S(1)} %pad_add_fusion.ids, bf16[192,16384]{1,0:T(8,128)(2,1)S(1)} %bitcast.21, bf16[192,256]{1,0:T(8,128)(2,1)S(1)} %total.1.refs_4_.refs_1_), custom_call_target="tpu_custom_call" | custom-call | tf_op jit(solution)/shard_map/weight_rows/pallas_call | solution.py:48
  94.9 1.3 weight_rows.3
  96.8 1.6 %weight_rows.4 = (bf16[768,256]{1,0:T(8,128)(2,1)S(1)}, bf16[768,256]{1,0:T(8,128)(2,1)S(1)}) custom-call(s32[3]{0:T(128)S(1)} %pad_add_fusion.ids, bf16[192,2560]{1,0:T(8,128)(2,1)S(1)} %get-tuple-element.101.refs_0_, bf16[192,2560]{1,0:T(8,128)(2,1)S(1)} %collective-permute-done.19.refs_1_, bf16[192,2560]{1,0:T(8,128)(2,1)S(1)} %collective-permute-done.20.refs_2_, ...), custom_call_target="tpu_custom_call" | custom-call | tf_op jit(solution)/shard_map/weight_rows/pallas_call | solution.py:48
  98.7 1.6 %collective-permute-start.30 = (bf16[256,256]{1,0:T(8,128)(2,1)S(1)}, bf16[256,256]{1,0:T(8,128)(2,1)S(1)}, u32[]{:S(2)}, u32[]{:S(2)}) collective-permute-start(bf16[256,256]{1,0:T(8,128)(2,1)S(1)} %slice.75), channel_id=1, source_target_pairs={{0,2},{1,3},{2,0},{3,1},{4,6},{5,7},{6,4},{7,5},{8,10},{9,11},{10,... | collective-permute-start | bytes 393224 | tf_op jit(solution)/shard_map/ppermute | solution.py:32
  101.1 3.4 %collective-permute-done.30 = bf16[256,256]{1,0:T(8,128)(2,1)S(1)} collective-permute-done((bf16[256,256]{1,0:T(8,128)(2,1)S(1)}, bf16[256,256]{1,0:T(8,128)(2,1)S(1)}, u32[]{:S(2)}, u32[]{:S(2)}) %collective-permute-start.30) | collective-permute-done | bytes 131104 | tf_op jit(solution)/shard_map/ppermute | solution.py:32
  104.5 2.6 %collective-permute-start.33 = (bf16[256,256]{1,0:T(8,128)(2,1)S(1)}, bf16[256,256]{1,0:T(8,128)(2,1)S(1)}, u32[]{:S(2)}, u32[]{:S(2)}) collective-permute-start(bf16[256,256]{1,0:T(8,128)(2,1)S(1)} %fusion.2), channel_id=1, source_target_pairs={{0,4},{1,5},{2,6},{3,7},{4,0},{5,1},{6,2},{7,3},{8,12},{9,13},{10,... | collective-permute-start | bytes 393224 | tf_op jit(solution)/shard_map/ppermute | solution.py:32
  107.7 1.0 collective-permute-start.43
  108.7 2.0 %collective-permute-start.44 = (bf16[768,256]{1,0:T(8,128)(2,1)S(1)}, bf16[768,256]{1,0:T(8,128)(2,1)S(1)}, u32[]{:S(2)}, u32[]{:S(2)}) collective-permute-start(bf16[768,256]{1,0:T(8,128)(2,1)S(1)} %get-tuple-element.91), channel_id=1, source_target_pairs={{0,24},{8,16},{16,8},{24,0},{1,25},{9,17},{17,9},{25,1},{2,26},{10... | collective-permute-start | bytes 1179656 | tf_op jit(solution)/shard_map/ppermute | solution.py:32
  110.7 1.7 %collective-permute-start.37 = (bf16[384,256]{1,0:T(8,128)(2,1)S(1)}, bf16[384,256]{1,0:T(8,128)(2,1)S(1)}, u32[]{:S(2)}, u32[]{:S(2)}) collective-permute-start(bf16[384,256]{1,0:T(8,128)(2,1)S(1)} %slice.74), channel_id=1, source_target_pairs={{0,2},{1,3},{2,0},{3,1},{4,6},{5,7},{6,4},{7,5},{8,10},{9,11},{10,... | collective-permute-start | bytes 589832 | tf_op jit(solution)/shard_map/ppermute | solution.py:32
  112.3 1.0 collective-permute-done.33
  114.0 4.6 %collective-permute-done.37 = bf16[384,256]{1,0:T(8,128)(2,1)S(1)} collective-permute-done((bf16[384,256]{1,0:T(8,128)(2,1)S(1)}, bf16[384,256]{1,0:T(8,128)(2,1)S(1)}, u32[]{:S(2)}, u32[]{:S(2)}) %collective-permute-start.37) | collective-permute-done | bytes 196640 | tf_op jit(solution)/shard_map/ppermute | solution.py:32
  119.3 7.0 %collective-permute-done.44 = bf16[768,256]{1,0:T(8,128)(2,1)S(1)} collective-permute-done((bf16[768,256]{1,0:T(8,128)(2,1)S(1)}, bf16[768,256]{1,0:T(8,128)(2,1)S(1)}, u32[]{:S(2)}, u32[]{:S(2)}) %collective-permute-start.44) | collective-permute-done | bytes 393248 | tf_op jit(solution)/shard_map/ppermute | solution.py:32
  126.5 1.7 %collective-permute-start.45 = (bf16[384,256]{1,0:T(8,128)(2,1)S(1)}, bf16[384,256]{1,0:T(8,128)(2,1)S(1)}, u32[]{:S(2)}, u32[]{:S(2)}) collective-permute-start(bf16[384,256]{1,0:T(8,128)(2,1)S(1)} %slice.73), channel_id=1, source_target_pairs={{0,2},{1,3},{2,0},{3,1},{4,6},{5,7},{6,4},{7,5},{8,10},{9,11},{10,... | collective-permute-start | bytes 589832 | tf_op jit(solution)/shard_map/ppermute | solution.py:32
  128.7 5.7 %collective-permute-done.45 = bf16[384,256]{1,0:T(8,128)(2,1)S(1)} collective-permute-done((bf16[384,256]{1,0:T(8,128)(2,1)S(1)}, bf16[384,256]{1,0:T(8,128)(2,1)S(1)}, u32[]{:S(2)}, u32[]{:S(2)}) %collective-permute-start.45) | collective-permute-done | bytes 196640 | tf_op jit(solution)/shard_map/ppermute | solution.py:32
  135.2 3.8 %collective-permute-done.39.refs_5_ = bf16[384,256]{1,0:T(8,128)(2,1)S(1)} collective-permute-done((bf16[384,256]{1,0:T(8,128)(2,1)S(1)}, bf16[384,256]{1,0:T(8,128)(2,1)S(1)}, u32[]{:S(2)}, u32[]{:S(2)}) %collective-permute-start.39) | collective-permute-done | bytes 196640 | tf_op jit(solution)/shard_map/ppermute | solution.py:32
  138.9 4.3 %collective-permute-done.46 = bf16[384,256]{1,0:T(8,128)(2,1)S(1)} collective-permute-done((bf16[384,256]{1,0:T(8,128)(2,1)S(1)}, bf16[384,256]{1,0:T(8,128)(2,1)S(1)}, u32[]{:S(2)}, u32[]{:S(2)}) %collective-permute-start.46) | collective-permute-done | bytes 196640 | tf_op jit(solution)/shard_map/ppermute | solution.py:32
  143.5 2.2 %assemble.2 = (f32[4096,128]{1,0:T(8,128)}, f32[4096,128]{1,0:T(8,128)}) custom-call(s32[3]{0:T(128)S(1)} %pad_add_fusion.ids, bf16[256,256]{1,0:T(8,128)(2,1)S(1)} %add_convert_fusion.2.refs_0_, bf16[256,256]{1,0:T(8,128)(2,1)S(1)} %collective-permute-done.34.refs_1_, bf16[256,256]{1,0:T(8,128)(2,1)S(1)} %collective-permute-done.35.refs_2_, ...), custom_call_target="tpu_custom_call" | custom-call | tf_op jit(solution)/shard_map/assemble/pallas_call | solution.py:394
  145.6 3.4 %collective-permute-done.47.refs_3_ = bf16[384,256]{1,0:T(8,128)(2,1)S(1)} collective-permute-done((bf16[384,256]{1,0:T(8,128)(2,1)S(1)}, bf16[384,256]{1,0:T(8,128)(2,1)S(1)}, u32[]{:S(2)}, u32[]{:S(2)}) %collective-permute-start.47) | collective-permute-done | bytes 196640 | tf_op jit(solution)/shard_map/ppermute | solution.py:32
  149.0 1.4 collective-permute-done.49.refs_5_
  150.5 1.8 %assemble.3 = (f32[4096,128]{1,0:T(8,128)}, f32[4096,128]{1,0:T(8,128)}) custom-call(s32[3]{0:T(128)S(1)} %pad_add_fusion.ids, f32[4096,128]{1,0:T(8,128)} %get-tuple-element.94.refs_0_, f32[4096,128]{1,0:T(8,128)} %get-tuple-element.95.refs_1_, bf16[384,256]{1,0:T(8,128)(2,1)S(1)} %add_convert_fusion.refs_2_, ...), custom_call_target="tpu_custom_call", output_to_operand_aliasing={{0}: (1, {}), {1}: (2, {})} | custom-call | tf_op jit(solution)/shard_map/assemble/pallas_call | solution.py:394
  (99 shorter events, 15.9 us)
Async XLA Ops:
  2.9 15.9 %collective-permute-start = (bf16[1024,256]{1,0:T(8,128)(2,1)}, bf16[1024,256]{1,0:T(8,128)(2,1)S(1)}, u32[]{:S(2)}, u32[]{:S(2)}) collective-permute-start(bf16[1024,256]{1,0:T(8,128)(2,1)} %pad_maximum_fusion), channel_id=1, source_target_pairs={{0,8},{8,0},{16,24},{24,16},{1,9},{9,1},{17,25},{25,17},{2,10},{10... | collective-permute-start | bytes 1572872 | tf_op jit(solution)/shard_map/ppermute | solution.py:32
  6.7 15.1 %collective-permute-start.2 = (bf16[1024,256]{1,0:T(8,128)(2,1)}, bf16[1024,256]{1,0:T(8,128)(2,1)S(1)}, u32[]{:S(2)}, u32[]{:S(2)}) collective-permute-start(bf16[1024,256]{1,0:T(8,128)(2,1)} %pad_maximum_fusion.1), channel_id=1, source_target_pairs={{0,16},{8,24},{16,0},{24,8},{1,17},{9,25},{17,1},{25,9},{2,18},{10... | collective-permute-start | bytes 1572872 | tf_op jit(solution)/shard_map/ppermute | solution.py:32
  8.2 24.9 %collective-permute-start.5 = (bf16[1024,256]{1,0:T(8,128)(2,1)}, bf16[1024,256]{1,0:T(8,128)(2,1)}, u32[]{:S(2)}, u32[]{:S(2)}) collective-permute-start(bf16[1024,256]{1,0:T(8,128)(2,1)} %pad_maximum_fusion), channel_id=1, source_target_pairs={{0,16},{8,24},{16,0},{24,8},{1,17},{9,25},{17,1},{25,9},{2,18},{10... | collective-permute-start | bytes 1572872 | tf_op jit(solution)/shard_map/ppermute | solution.py:32
  8.7 24.4 %collective-permute-start.1 = (bf16[1024,256]{1,0:T(8,128)(2,1)}, bf16[1024,256]{1,0:T(8,128)(2,1)}, u32[]{:S(2)}, u32[]{:S(2)}) collective-permute-start(bf16[1024,256]{1,0:T(8,128)(2,1)} %pad_maximum_fusion.1), channel_id=1, source_target_pairs={{0,8},{8,0},{16,24},{24,16},{1,9},{9,1},{17,25},{25,17},{2,10},{10... | collective-permute-start | bytes 1572872 | tf_op jit(solution)/shard_map/ppermute | solution.py:32
  21.8 11.9 %collective-permute-start.3 = (bf16[1024,256]{1,0:T(8,128)(2,1)S(1)}, bf16[1024,256]{1,0:T(8,128)(2,1)}, u32[]{:S(2)}, u32[]{:S(2)}) collective-permute-start(bf16[1024,256]{1,0:T(8,128)(2,1)S(1)} %collective-permute-done.refs_2_), channel_id=1, source_target_pairs={{0,1},{1,0},{2,3},{3,2},{4,5},{5,4},{6,7},{7,6},{8,9},{9,8},{10,11... | collective-permute-start | bytes 1572872 | tf_op jit(solution)/shard_map/ppermute | solution.py:32
  21.8 21.0 %collective-permute-start.8 = (bf16[1024,256]{1,0:T(8,128)(2,1)S(1)}, bf16[1024,256]{1,0:T(8,128)(2,1)S(1)}, u32[]{:S(2)}, u32[]{:S(2)}) collective-permute-start(bf16[1024,256]{1,0:T(8,128)(2,1)S(1)} %collective-permute-done.refs_2_), channel_id=1, source_target_pairs={{0,16},{8,24},{16,0},{24,8},{1,17},{9,25},{17,1},{25,9},{2,18},{10... | collective-permute-start | bytes 1572872 | tf_op jit(solution)/shard_map/ppermute | solution.py:32
  23.3 19.5 %collective-permute-start.9 = (bf16[1024,256]{1,0:T(8,128)(2,1)S(1)}, bf16[1024,256]{1,0:T(8,128)(2,1)S(1)}, u32[]{:S(2)}, u32[]{:S(2)}) collective-permute-start(bf16[1024,256]{1,0:T(8,128)(2,1)S(1)} %collective-permute-done.2.refs_7_), channel_id=1, source_target_pairs={{0,8},{8,0},{16,24},{24,16},{1,9},{9,1},{17,25},{25,17},{2,10},{10... | collective-permute-start | bytes 1572872 | tf_op jit(solution)/shard_map/ppermute | solution.py:32
  33.1 3.2 %collective-permute-start.6 = (bf16[1024,256]{1,0:T(8,128)(2,1)}, bf16[1024,256]{1,0:T(8,128)(2,1)S(1)}, u32[]{:S(2)}, u32[]{:S(2)}) collective-permute-start(bf16[1024,256]{1,0:T(8,128)(2,1)} %collective-permute-done.5.refs_6_), channel_id=1, source_target_pairs={{0,1},{1,0},{2,3},{3,2},{4,5},{5,4},{6,7},{7,6},{8,9},{9,8},{10,11... | collective-permute-start | bytes 1572872 | tf_op jit(solution)/shard_map/ppermute | solution.py:32
  33.1 3.6 %collective-permute-start.4 = (bf16[1024,256]{1,0:T(8,128)(2,1)}, bf16[1024,256]{1,0:T(8,128)(2,1)S(1)}, u32[]{:S(2)}, u32[]{:S(2)}) collective-permute-start(bf16[1024,256]{1,0:T(8,128)(2,1)} %collective-permute-done.1.refs_3_), channel_id=1, source_target_pairs={{0,1},{1,0},{2,3},{3,2},{4,5},{5,4},{6,7},{7,6},{8,9},{9,8},{10,11... | collective-permute-start | bytes 1572872 | tf_op jit(solution)/shard_map/ppermute | solution.py:32
  33.6 3.1 %collective-permute-start.7 = (bf16[1024,256]{1,0:T(8,128)(2,1)S(1)}, bf16[1024,256]{1,0:T(8,128)(2,1)S(1)}, u32[]{:S(2)}, u32[]{:S(2)}) collective-permute-start(bf16[1024,256]{1,0:T(8,128)(2,1)S(1)} %collective-permute-done.2.refs_7_), channel_id=1, source_target_pairs={{0,1},{1,0},{2,3},{3,2},{4,5},{5,4},{6,7},{7,6},{8,9},{9,8},{10,11... | collective-permute-start | bytes 1572872 | tf_op jit(solution)/shard_map/ppermute | solution.py:32
  42.8 2.1 %collective-permute-start.10 = (bf16[1024,256]{1,0:T(8,128)(2,1)S(1)}, bf16[1024,256]{1,0:T(8,128)(2,1)S(1)}, u32[]{:S(2)}, u32[]{:S(2)}) collective-permute-start(bf16[1024,256]{1,0:T(8,128)(2,1)S(1)} %collective-permute-done.8.refs_1_), channel_id=1, source_target_pairs={{0,1},{1,0},{2,3},{3,2},{4,5},{5,4},{6,7},{7,6},{8,9},{9,8},{10,11... | collective-permute-start | bytes 1572872 | tf_op jit(solution)/shard_map/ppermute | solution.py:32
  42.9 2.6 %collective-permute-start.11 = (bf16[1024,256]{1,0:T(8,128)(2,1)S(1)}, bf16[1024,256]{1,0:T(8,128)(2,1)S(1)}, u32[]{:S(2)}, u32[]{:S(2)}) collective-permute-start(bf16[1024,256]{1,0:T(8,128)(2,1)S(1)} %collective-permute-done.9.refs_2_), channel_id=1, source_target_pairs={{0,1},{1,0},{2,3},{3,2},{4,5},{5,4},{6,7},{7,6},{8,9},{9,8},{10,11... | collective-permute-start | bytes 1572872 | tf_op jit(solution)/shard_map/ppermute | solution.py:32
  43.4 28.7 %collective-permute-start.20 = (bf16[192,2560]{1,0:T(8,128)(2,1)S(1)}, bf16[192,2560]{1,0:T(8,128)(2,1)S(1)}, u32[]{:S(2)}, u32[]{:S(2)}) collective-permute-start(bf16[192,2560]{1,0:T(8,128)(2,1)S(1)} %get-tuple-element.67), channel_id=1, source_target_pairs={{0,16},{8,24},{16,0},{24,8},{1,17},{9,25},{17,1},{25,9},{2,18},{10... | collective-permute-start | bytes 2949128 | tf_op jit(solution)/shard_map/ppermute | solution.py:32
  44.9 27.2 %collective-permute-start.19 = (bf16[192,2560]{1,0:T(8,128)(2,1)S(1)}, bf16[192,2560]{1,0:T(8,128)(2,1)S(1)}, u32[]{:S(2)}, u32[]{:S(2)}) collective-permute-start(bf16[192,2560]{1,0:T(8,128)(2,1)S(1)} %get-tuple-element.66), channel_id=1, source_target_pairs={{0,8},{8,0},{16,24},{24,16},{1,9},{9,1},{17,25},{25,17},{2,10},{10... | collective-permute-start | bytes 2949128 | tf_op jit(solution)/shard_map/ppermute | solution.py:32
  46.7 7.6 %collective-permute-start.14 = (bf16[192,256]{1,0:T(8,128)(2,1)S(1)}, bf16[192,256]{1,0:T(8,128)(2,1)S(1)}, u32[]{:S(2)}, u32[]{:S(2)}) collective-permute-start(bf16[192,256]{1,0:T(8,128)(2,1)S(1)} %project.3.refs_0_), channel_id=1, source_target_pairs={{0,6},{1,7},{2,4},{3,5},{4,2},{5,3},{6,0},{7,1},{8,14},{9,15},{10,... | collective-permute-start | bytes 294920 | tf_op jit(solution)/shard_map/ppermute | solution.py:32
  50.3 8.6 %collective-permute-start.13 = (bf16[192,256]{1,0:T(8,128)(2,1)S(1)}, bf16[192,256]{1,0:T(8,128)(2,1)S(1)}, u32[]{:S(2)}, u32[]{:S(2)}) collective-permute-start(bf16[192,256]{1,0:T(8,128)(2,1)S(1)} %project.3.refs_0_), channel_id=1, source_target_pairs={{0,4},{1,5},{2,6},{3,7},{4,0},{5,1},{6,2},{7,3},{8,12},{9,13},{10,... | collective-permute-start | bytes 294920 | tf_op jit(solution)/shard_map/ppermute | solution.py:32
  50.4 8.6 %collective-permute-start.12 = (bf16[192,256]{1,0:T(8,128)(2,1)S(1)}, bf16[192,256]{1,0:T(8,128)(2,1)S(1)}, u32[]{:S(2)}, u32[]{:S(2)}) collective-permute-start(bf16[192,256]{1,0:T(8,128)(2,1)S(1)} %project.3.refs_0_), channel_id=1, source_target_pairs={{0,2},{1,3},{2,0},{3,1},{4,6},{5,7},{6,4},{7,5},{8,10},{9,11},{10,... | collective-permute-start | bytes 294920 | tf_op jit(solution)/shard_map/ppermute | solution.py:32
  58.9 32.5 %collective-permute-start.26 = (bf16[192,2560]{1,0:T(8,128)(2,1)S(1)}, bf16[192,2560]{1,0:T(8,128)(2,1)S(1)}, u32[]{:S(2)}, u32[]{:S(2)}) collective-permute-start(bf16[192,2560]{1,0:T(8,128)(2,1)S(1)} %get-tuple-element.77), channel_id=1, source_target_pairs={{0,24},{8,16},{16,8},{24,0},{1,25},{9,17},{17,9},{25,1},{2,26},{10... | collective-permute-start | bytes 2949128 | tf_op jit(solution)/shard_map/ppermute | solution.py:32
  60.9 1.5 collective-permute-start.16
  62.3 1.3 collective-permute-start.18
  72.1 1.7 %collective-permute-start.21 = (bf16[768,256]{1,0:T(8,128)(2,1)S(1)}, bf16[768,256]{1,0:T(8,128)(2,1)S(1)}, u32[]{:S(2)}, u32[]{:S(2)}) collective-permute-start(bf16[768,256]{1,0:T(8,128)(2,1)S(1)} %get-tuple-element.71), channel_id=1, source_target_pairs={{0,1},{1,0},{2,3},{3,2},{4,5},{5,4},{6,7},{7,6},{8,9},{9,8},{10,11... | collective-permute-start | bytes 1179656 | tf_op jit(solution)/shard_map/ppermute | solution.py:32
  73.9 6.6 %collective-permute-start.22 = (bf16[192,256]{1,0:T(8,128)(2,1)S(1)}, bf16[192,256]{1,0:T(8,128)(2,1)S(1)}, u32[]{:S(2)}, u32[]{:S(2)}) collective-permute-start(bf16[192,256]{1,0:T(8,128)(2,1)S(1)} %get-tuple-element.73), channel_id=1, source_target_pairs={{0,2},{1,3},{2,0},{3,1},{4,6},{5,7},{6,4},{7,5},{8,10},{9,11},{10,... | collective-permute-start | bytes 294920 | tf_op jit(solution)/shard_map/ppermute | solution.py:32
  74.5 10.8 %collective-permute-start.23 = (bf16[192,256]{1,0:T(8,128)(2,1)S(1)}, bf16[192,256]{1,0:T(8,128)(2,1)S(1)}, u32[]{:S(2)}, u32[]{:S(2)}) collective-permute-start(bf16[192,256]{1,0:T(8,128)(2,1)S(1)} %get-tuple-element.74), channel_id=1, source_target_pairs={{0,4},{1,5},{2,6},{3,7},{4,0},{5,1},{6,2},{7,3},{8,12},{9,13},{10,... | collective-permute-start | bytes 294920 | tf_op jit(solution)/shard_map/ppermute | solution.py:32
  77.1 8.3 %collective-permute-start.24 = (bf16[192,256]{1,0:T(8,128)(2,1)S(1)}, bf16[192,256]{1,0:T(8,128)(2,1)S(1)}, u32[]{:S(2)}, u32[]{:S(2)}) collective-permute-start(bf16[192,256]{1,0:T(8,128)(2,1)S(1)} %get-tuple-element.75), channel_id=1, source_target_pairs={{0,6},{1,7},{2,4},{3,5},{4,2},{5,3},{6,0},{7,1},{8,14},{9,15},{10,... | collective-permute-start | bytes 294920 | tf_op jit(solution)/shard_map/ppermute | solution.py:32
  85.4 7.3 %collective-permute-start.25 = (bf16[192,256]{1,0:T(8,128)(2,1)S(1)}, bf16[192,256]{1,0:T(8,128)(2,1)S(1)}, u32[]{:S(2)}, u32[]{:S(2)}) collective-permute-start(bf16[192,256]{1,0:T(8,128)(2,1)S(1)} %total.1.refs_4_.refs_1_), channel_id=1, source_target_pairs={{0,8},{8,0},{16,24},{24,16},{1,9},{9,1},{17,25},{25,17},{2,10},{10... | collective-permute-start | bytes 294920 | tf_op jit(solution)/shard_map/ppermute | solution.py:32
  86.5 8.4 %collective-permute-start.28 = (bf16[192,256]{1,0:T(8,128)(2,1)S(1)}, bf16[192,256]{1,0:T(8,128)(2,1)S(1)}, u32[]{:S(2)}, u32[]{:S(2)}) collective-permute-start(bf16[192,256]{1,0:T(8,128)(2,1)S(1)} %total.1.refs_4_.refs_1_), channel_id=1, source_target_pairs={{0,24},{8,16},{16,8},{24,0},{1,25},{9,17},{17,9},{25,1},{2,26},{10... | collective-permute-start | bytes 294920 | tf_op jit(solution)/shard_map/ppermute | solution.py:32
  87.5 7.4 %collective-permute-start.27 = (bf16[192,256]{1,0:T(8,128)(2,1)S(1)}, bf16[192,256]{1,0:T(8,128)(2,1)S(1)}, u32[]{:S(2)}, u32[]{:S(2)}) collective-permute-start(bf16[192,256]{1,0:T(8,128)(2,1)S(1)} %total.1.refs_4_.refs_1_), channel_id=1, source_target_pairs={{0,16},{8,24},{16,0},{24,8},{1,17},{9,25},{17,1},{25,9},{2,18},{10... | collective-permute-start | bytes 294920 | tf_op jit(solution)/shard_map/ppermute | solution.py:32
  94.9 5.6 %collective-permute-start.32 = (bf16[3072,256]{1,0:T(8,128)(2,1)S(1)}, bf16[3072,256]{1,0:T(8,128)(2,1)S(1)}, u32[]{:S(2)}, u32[]{:S(2)}) collective-permute-start(bf16[3072,256]{1,0:T(8,128)(2,1)S(1)} %get-tuple-element.87), channel_id=1, source_target_pairs={{0,1},{1,0},{2,3},{3,2},{4,5},{5,4},{6,7},{7,6},{8,9},{9,8},{10,11... | collective-permute-start | bytes 4718600 | tf_op jit(solution)/shard_map/ppermute | solution.py:32
  96.2 2.5 %collective-permute-start.29 = (bf16[512,256]{1,0:T(8,128)(2,1)S(1)}, bf16[512,256]{1,0:T(8,128)(2,1)S(1)}, u32[]{:S(2)}, u32[]{:S(2)}) collective-permute-start(bf16[512,256]{1,0:T(8,128)(2,1)S(1)} %get-tuple-element.81), channel_id=1, source_target_pairs={{0,1},{1,0},{2,3},{3,2},{4,5},{5,4},{6,7},{7,6},{8,9},{9,8},{10,11... | collective-permute-start | bytes 786440 | tf_op jit(solution)/shard_map/ppermute | solution.py:32
  98.4 2.0 %collective-permute-start.31 = (bf16[768,256]{1,0:T(8,128)(2,1)S(1)}, bf16[768,256]{1,0:T(8,128)(2,1)S(1)}, u32[]{:S(2)}, u32[]{:S(2)}) collective-permute-start(bf16[768,256]{1,0:T(8,128)(2,1)S(1)} %get-tuple-element.83), channel_id=1, source_target_pairs={{0,1},{1,0},{2,3},{3,2},{4,5},{5,4},{6,7},{7,6},{8,9},{9,8},{10,11... | collective-permute-start | bytes 1179656 | tf_op jit(solution)/shard_map/ppermute | solution.py:32
  98.7 5.8 %collective-permute-start.30 = (bf16[256,256]{1,0:T(8,128)(2,1)S(1)}, bf16[256,256]{1,0:T(8,128)(2,1)S(1)}, u32[]{:S(2)}, u32[]{:S(2)}) collective-permute-start(bf16[256,256]{1,0:T(8,128)(2,1)S(1)} %slice.75), channel_id=1, source_target_pairs={{0,2},{1,3},{2,0},{3,1},{4,6},{5,7},{6,4},{7,5},{8,10},{9,11},{10,... | collective-permute-start | bytes 393224 | tf_op jit(solution)/shard_map/ppermute | solution.py:32
  104.5 8.8 %collective-permute-start.33 = (bf16[256,256]{1,0:T(8,128)(2,1)S(1)}, bf16[256,256]{1,0:T(8,128)(2,1)S(1)}, u32[]{:S(2)}, u32[]{:S(2)}) collective-permute-start(bf16[256,256]{1,0:T(8,128)(2,1)S(1)} %fusion.2), channel_id=1, source_target_pairs={{0,4},{1,5},{2,6},{3,7},{4,0},{5,1},{6,2},{7,3},{8,12},{9,13},{10,... | collective-permute-start | bytes 393224 | tf_op jit(solution)/shard_map/ppermute | solution.py:32
  107.1 12.1 %collective-permute-start.42 = (bf16[768,256]{1,0:T(8,128)(2,1)S(1)}, bf16[768,256]{1,0:T(8,128)(2,1)S(1)}, u32[]{:S(2)}, u32[]{:S(2)}) collective-permute-start(bf16[768,256]{1,0:T(8,128)(2,1)S(1)} %get-tuple-element.89), channel_id=1, source_target_pairs={{0,8},{8,0},{16,24},{24,16},{1,9},{9,1},{17,25},{25,17},{2,10},{10... | collective-permute-start | bytes 1179656 | tf_op jit(solution)/shard_map/ppermute | solution.py:32
  107.7 11.6 %collective-permute-start.43 = (bf16[768,256]{1,0:T(8,128)(2,1)S(1)}, bf16[768,256]{1,0:T(8,128)(2,1)S(1)}, u32[]{:S(2)}, u32[]{:S(2)}) collective-permute-start(bf16[768,256]{1,0:T(8,128)(2,1)S(1)} %get-tuple-element.90), channel_id=1, source_target_pairs={{0,16},{8,24},{16,0},{24,8},{1,17},{9,25},{17,1},{25,9},{2,18},{10... | collective-permute-start | bytes 1179656 | tf_op jit(solution)/shard_map/ppermute | solution.py:32
  108.7 17.6 %collective-permute-start.44 = (bf16[768,256]{1,0:T(8,128)(2,1)S(1)}, bf16[768,256]{1,0:T(8,128)(2,1)S(1)}, u32[]{:S(2)}, u32[]{:S(2)}) collective-permute-start(bf16[768,256]{1,0:T(8,128)(2,1)S(1)} %get-tuple-element.91), channel_id=1, source_target_pairs={{0,24},{8,16},{16,8},{24,0},{1,25},{9,17},{17,9},{25,1},{2,26},{10... | collective-permute-start | bytes 1179656 | tf_op jit(solution)/shard_map/ppermute | solution.py:32
  110.7 7.9 %collective-permute-start.37 = (bf16[384,256]{1,0:T(8,128)(2,1)S(1)}, bf16[384,256]{1,0:T(8,128)(2,1)S(1)}, u32[]{:S(2)}, u32[]{:S(2)}) collective-permute-start(bf16[384,256]{1,0:T(8,128)(2,1)S(1)} %slice.74), channel_id=1, source_target_pairs={{0,2},{1,3},{2,0},{3,1},{4,6},{5,7},{6,4},{7,5},{8,10},{9,11},{10,... | collective-permute-start | bytes 589832 | tf_op jit(solution)/shard_map/ppermute | solution.py:32
  113.3 21.2 %collective-permute-start.34 = (bf16[256,256]{1,0:T(8,128)(2,1)S(1)}, bf16[256,256]{1,0:T(8,128)(2,1)S(1)}, u32[]{:S(2)}, u32[]{:S(2)}) collective-permute-start(bf16[256,256]{1,0:T(8,128)(2,1)S(1)} %add_convert_fusion.2.refs_0_), channel_id=1, source_target_pairs={{0,2},{1,3},{2,0},{3,1},{4,6},{5,7},{6,4},{7,5},{8,10},{9,11},{10,... | collective-permute-start | bytes 393224 | tf_op jit(solution)/shard_map/ppermute | solution.py:32
  118.6 9.9 %collective-permute-start.38 = (bf16[384,256]{1,0:T(8,128)(2,1)S(1)}, bf16[384,256]{1,0:T(8,128)(2,1)S(1)}, u32[]{:S(2)}, u32[]{:S(2)}) collective-permute-start(bf16[384,256]{1,0:T(8,128)(2,1)S(1)} %fusion), channel_id=1, source_target_pairs={{0,4},{1,5},{2,6},{3,7},{4,0},{5,1},{6,2},{7,3},{8,12},{9,13},{10,... | collective-permute-start | bytes 589832 | tf_op jit(solution)/shard_map/ppermute | solution.py:32
  126.5 7.9 %collective-permute-start.45 = (bf16[384,256]{1,0:T(8,128)(2,1)S(1)}, bf16[384,256]{1,0:T(8,128)(2,1)S(1)}, u32[]{:S(2)}, u32[]{:S(2)}) collective-permute-start(bf16[384,256]{1,0:T(8,128)(2,1)S(1)} %slice.73), channel_id=1, source_target_pairs={{0,2},{1,3},{2,0},{3,1},{4,6},{5,7},{6,4},{7,5},{8,10},{9,11},{10,... | collective-permute-start | bytes 589832 | tf_op jit(solution)/shard_map/ppermute | solution.py:32
  128.6 10.4 %collective-permute-start.39 = (bf16[384,256]{1,0:T(8,128)(2,1)S(1)}, bf16[384,256]{1,0:T(8,128)(2,1)S(1)}, u32[]{:S(2)}, u32[]{:S(2)}) collective-permute-start(bf16[384,256]{1,0:T(8,128)(2,1)S(1)} %add_convert_fusion.1.refs_4_), channel_id=1, source_target_pairs={{0,2},{1,3},{2,0},{3,1},{4,6},{5,7},{6,4},{7,5},{8,10},{9,11},{10,... | collective-permute-start | bytes 589832 | tf_op jit(solution)/shard_map/ppermute | solution.py:32
  134.4 8.8 %collective-permute-start.46 = (bf16[384,256]{1,0:T(8,128)(2,1)S(1)}, bf16[384,256]{1,0:T(8,128)(2,1)S(1)}, u32[]{:S(2)}, u32[]{:S(2)}) collective-permute-start(bf16[384,256]{1,0:T(8,128)(2,1)S(1)} %fusion.1), channel_id=1, source_target_pairs={{0,4},{1,5},{2,6},{3,7},{4,0},{5,1},{6,2},{7,3},{8,12},{9,13},{10,... | collective-permute-start | bytes 589832 | tf_op jit(solution)/shard_map/ppermute | solution.py:32
  134.5 4.4 %collective-permute-start.35 = (bf16[256,256]{1,0:T(8,128)(2,1)S(1)}, bf16[256,256]{1,0:T(8,128)(2,1)S(1)}, u32[]{:S(2)}, u32[]{:S(2)}) collective-permute-start(bf16[256,256]{1,0:T(8,128)(2,1)S(1)} %add_convert_fusion.2.refs_0_), channel_id=1, source_target_pairs={{0,1},{1,0},{2,3},{3,2},{4,5},{5,4},{6,7},{7,6},{8,9},{9,8},{10,11... | collective-permute-start | bytes 393224 | tf_op jit(solution)/shard_map/ppermute | solution.py:32
  134.6 4.4 %collective-permute-start.36 = (bf16[256,256]{1,0:T(8,128)(2,1)S(1)}, bf16[256,256]{1,0:T(8,128)(2,1)S(1)}, u32[]{:S(2)}, u32[]{:S(2)}) collective-permute-start(bf16[256,256]{1,0:T(8,128)(2,1)S(1)} %collective-permute-done.34.refs_1_), channel_id=1, source_target_pairs={{0,1},{1,0},{2,3},{3,2},{4,5},{5,4},{6,7},{7,6},{8,9},{9,8},{10,11... | collective-permute-start | bytes 393224 | tf_op jit(solution)/shard_map/ppermute | solution.py:32
  135.1 8.4 %collective-permute-start.40 = (bf16[384,256]{1,0:T(8,128)(2,1)S(1)}, bf16[384,256]{1,0:T(8,128)(2,1)S(1)}, u32[]{:S(2)}, u32[]{:S(2)}) collective-permute-start(bf16[384,256]{1,0:T(8,128)(2,1)S(1)} %add_convert_fusion.1.refs_4_), channel_id=1, source_target_pairs={{0,1},{1,0},{2,3},{3,2},{4,5},{5,4},{6,7},{7,6},{8,9},{9,8},{10,11... | collective-permute-start | bytes 589832 | tf_op jit(solution)/shard_map/ppermute | solution.py:32
  138.9 4.5 %collective-permute-start.41 = (bf16[384,256]{1,0:T(8,128)(2,1)S(1)}, bf16[384,256]{1,0:T(8,128)(2,1)S(1)}, u32[]{:S(2)}, u32[]{:S(2)}) collective-permute-start(bf16[384,256]{1,0:T(8,128)(2,1)S(1)} %collective-permute-done.39.refs_5_), channel_id=1, source_target_pairs={{0,1},{1,0},{2,3},{3,2},{4,5},{5,4},{6,7},{7,6},{8,9},{9,8},{10,11... | collective-permute-start | bytes 589832 | tf_op jit(solution)/shard_map/ppermute | solution.py:32
  143.3 5.7 %collective-permute-start.47 = (bf16[384,256]{1,0:T(8,128)(2,1)S(1)}, bf16[384,256]{1,0:T(8,128)(2,1)S(1)}, u32[]{:S(2)}, u32[]{:S(2)}) collective-permute-start(bf16[384,256]{1,0:T(8,128)(2,1)S(1)} %add_convert_fusion.refs_2_), channel_id=1, source_target_pairs={{0,2},{1,3},{2,0},{3,1},{4,6},{5,7},{6,4},{7,5},{8,10},{9,11},{10,... | collective-permute-start | bytes 589832 | tf_op jit(solution)/shard_map/ppermute | solution.py:32
  143.4 5.7 %collective-permute-start.48 = (bf16[384,256]{1,0:T(8,128)(2,1)S(1)}, bf16[384,256]{1,0:T(8,128)(2,1)S(1)}, u32[]{:S(2)}, u32[]{:S(2)}) collective-permute-start(bf16[384,256]{1,0:T(8,128)(2,1)S(1)} %add_convert_fusion.refs_2_), channel_id=1, source_target_pairs={{0,1},{1,0},{2,3},{3,2},{4,5},{5,4},{6,7},{7,6},{8,9},{9,8},{10,11... | collective-permute-start | bytes 589832 | tf_op jit(solution)/shard_map/ppermute | solution.py:32
  149.0 1.4 collective-permute-start.49
  (10 other events, 133.1 us)
